TPU v7x, 32 devices: a whole 2x2x4 slice. The times are simulated.
32 devices in a mesh: dp: 16 (over z, y, core), tensor: 2 (over x).
Axes of the slice: x: 2, y: 2, z: 4, core: 2. Of those that a mesh axis runs over, the one named last changes fastest.
Arguments:
- block_input: bfloat16 [4096, 2048], P(('dp', 'tensor')), may hold values from -6 to 6
- segments: int32 [16, 256], P('dp'), may hold values from 0 to 3, never falling along the last dimension, each value on 1 to 128 neighbouring positions
- counts: int32 [16], P('dp'), may hold values from 128 to 256, as said below
- routes: int32 [4096, 6], P('dp'), may hold values from 0 to 15, all different within a row; in each aligned block of 256 rows (0 to 255, 256 to 511, ...) at most 192 rows name the same one
- attn_gain: bfloat16 [2048], P('dp'), may hold values from 0.5 to 1.5
- w_query: bfloat16 [2048, 3072], P('dp', 'tensor'), may hold values from -0.125 to 0.125
- w_latent: bfloat16 [2048, 576], P('dp'), may hold values from -0.125 to 0.125
- latent_gain: bfloat16 [512], P('dp'), may hold values from 0.5 to 1.5
- w_keyval: bfloat16 [512, 4096], P('dp', 'tensor'), may hold values from -0.25 to 0.25
- w_output: bfloat16 [2048, 2048], P('tensor', 'dp'), may hold values from -1.25 to 1.25
- ffn_gain: bfloat16 [2048], P('dp'), may hold values from 0.5 to 1.5
- w_router: bfloat16 [2048, 16], P('dp'), may hold values from -0.15625 to 0.15625
- shared_gate_up: bfloat16 [2, 2048, 2816], P(None, 'dp', 'tensor'), may hold values from -0.125 to 0.125
- shared_down: bfloat16 [2816, 2048], P('tensor', 'dp'), may hold values from -0.109375 to 0.109375
- expert_gate_up: bfloat16 [16, 2, 2048, 1408], P('dp', None, None, 'tensor'), may hold values from -0.125 to 0.125
- expert_down: bfloat16 [16, 1408, 2048], P('dp', 'tensor'), may hold values from -3 to 3
- cotangent: bfloat16 [4096, 2048], P(('dp', 'tensor')), may hold values from -6 to 6
Outputs:
- block_output: float32 [4096, 2048], P(('dp', 'tensor'))
- grad_input: float32 [4096, 2048], P(('dp', 'tensor'))
- grad_attn_gain: float32 [2048], P('dp')
- grad_w_query: float32 [2048, 3072], P('dp', 'tensor')
- grad_w_latent: float32 [2048, 576], P('dp')
- grad_latent_gain: float32 [512], P('dp')
- grad_w_keyval: float32 [512, 4096], P('dp', 'tensor')
- grad_w_output: float32 [2048, 2048], P('tensor', 'dp')
- grad_ffn_gain: float32 [2048], P('dp')
- grad_w_router: float32 [2048, 16], P('dp')
- grad_shared_gate_up: float32 [2, 2048, 2816], P(None, 'dp', 'tensor')
- grad_shared_down: float32 [2816, 2048], P('tensor', 'dp')
- grad_expert_gate_up: float32 [16, 2, 2048, 1408], P('dp', None, None, 'tensor')
- grad_expert_down: float32 [16, 1408, 2048], P('dp', 'tensor')
Inputs may be any that keep to these rules, and one draw needn't show every extreme that they name: `routes`: each row names 6 different experts; in each aligned block of 256 rows no expert is named by more than 192 rows, a bound that some block reaches. `segments`: along a row the ids never fall; every id of the range is used in every row. `counts`: some block has all 256 slots live.
All inputs are finite; a program needn't handle non-finite values.
Results may differ from a plain program's by a relative error of at most 0.018.
Values may be sent and summed in bfloat16 or wider, within the bound.
No kernel may reach another device: no remote copies, remote signals or barrier semaphores. Data moves between devices by JAX's collectives and lax.ppermute only.
A program may use at most 384 MiB of HBM per device.

v0:
```python
import math

import jax
import jax.numpy as jnp
from jax import lax
from jax.sharding import PartitionSpec as P

D = 2048
NOPE = 128
ROPE = 64
VD = 128
KVR = 512
TOP = 6


EPSILON = 1e-06


def rms_scale(values):
    return lax.rsqrt(jnp.mean(values * values, axis=-1, keepdims=True) + EPSILON)


def rms_back(grad_unit, unit_rows, row_scale):
    return row_scale * (
        grad_unit - unit_rows * jnp.mean(grad_unit * unit_rows, axis=-1, keepdims=True)
    )


def rotary_tables(segment_row, width):
    count = segment_row.shape[0]
    position = jnp.arange(count, dtype=jnp.int32)
    same = segment_row[:, None] == segment_row[None, :]
    start = jnp.min(jnp.where(same, position[None, :], count), axis=1)
    offset = (position - start).astype(jnp.float32)
    freq = jnp.exp(jnp.arange(width // 2, dtype=jnp.float32) * (-2.0 * math.log(10000.0) / width))
    angle = offset[:, None] * freq[None, :]
    return (jnp.cos(angle), jnp.sin(angle))


def rotate(values, cosine, sine):
    half = values.shape[-1] // 2
    first = values[..., :half]
    second = values[..., half:]
    return jnp.concatenate(
        [first * cosine - second * sine, second * cosine + first * sine], axis=-1
    )


def rotate_back(grads, cosine, sine):
    half = grads.shape[-1] // 2
    first = grads[..., :half]
    second = grads[..., half:]
    return jnp.concatenate(
        [first * cosine + second * sine, second * cosine - first * sine], axis=-1
    )


def allowed_pairs(segment_row, count):
    position = jnp.arange(segment_row.shape[0], dtype=jnp.int32)
    live = position < count
    same = segment_row[:, None] == segment_row[None, :]
    causal = position[None, :] <= position[:, None]
    return same & causal & live[:, None] & live[None, :] | (position[:, None] == position[None, :])


def attention_scores(query_rows, key_nope, key_rope, allowed, scale):
    scores = jnp.einsum(
        "ihd,jhd->hij", query_rows[..., :NOPE], key_nope, preferred_element_type=jnp.float32
    )
    scores = scores + jnp.einsum(
        "ihd,jd->hij", query_rows[..., NOPE:], key_rope, preferred_element_type=jnp.float32
    )
    return jnp.where(allowed[None], scores * scale, -1e30)


def swiglu_back(gate, upper, grad_hidden, axis):
    sigmoid = jax.nn.sigmoid(gate)
    grad_gate = grad_hidden * upper * sigmoid * (1.0 + gate * (1.0 - sigmoid))
    grad_upper = grad_hidden * gate * sigmoid
    return jnp.stack([grad_gate, grad_upper], axis=axis)


def slot_layout(routes, experts, capacity):
    tokens = routes.shape[0]
    flat = routes.reshape(-1)
    onehot = (flat[:, None] == jnp.arange(experts, dtype=jnp.int32)[None, :]).astype(jnp.int32)
    before = jnp.cumsum(onehot, axis=0) - onehot
    slot_index = jnp.sum(before * onehot, axis=1)
    target = flat * capacity + slot_index
    token_ids = jnp.arange(flat.shape[0], dtype=jnp.int32) // routes.shape[1]
    owner = jnp.full((experts * capacity,), tokens, jnp.int32).at[target].set(token_ids)
    return (slot_index, target, owner)


def to_expert_major(arrived, groups, local_experts):
    capacity = arrived.shape[1]
    width = arrived.shape[2]
    return (
        arrived.reshape(groups, local_experts, capacity, width)
        .transpose(1, 0, 2, 3)
        .reshape(local_experts, groups * capacity, width)
    )


def from_expert_major(results, groups):
    local_experts = results.shape[0]
    width = results.shape[2]
    capacity = results.shape[1] // groups
    return (
        results.reshape(local_experts, groups, capacity, width)
        .transpose(1, 0, 2, 3)
        .reshape(groups * local_experts, capacity, width)
    )


def body(
    block_input,
    segments,
    counts,
    routes,
    attn_gain,
    w_query,
    w_latent,
    latent_gain,
    w_keyval,
    w_output,
    ffn_gain,
    w_router,
    shared_gate_up,
    shared_down,
    expert_gate_up,
    expert_down,
    cotangent,
):
    gathered = (
        lax.all_gather(attn_gain, "dp", axis=0, tiled=True),
        lax.all_gather(w_query, "dp", axis=0, tiled=True),
        lax.all_gather(w_latent, "dp", axis=0, tiled=True),
        lax.all_gather(latent_gain, "dp", axis=0, tiled=True),
        lax.all_gather(w_keyval, "dp", axis=0, tiled=True),
        lax.all_gather(w_output, "dp", axis=1, tiled=True),
        lax.all_gather(ffn_gain, "dp", axis=0, tiled=True),
        lax.all_gather(w_router, "dp", axis=0, tiled=True),
        lax.all_gather(shared_gate_up, "dp", axis=1, tiled=True),
        lax.all_gather(shared_down, "dp", axis=1, tiled=True),
    )
    (
        full_attn_gain,
        query_weight,
        latent_weight,
        full_latent_gain,
        keyval_weight,
        output_weight,
        full_ffn_gain,
        router_weight,
        shared_in,
        shared_out,
    ) = gathered
    tensor_rank = lax.axis_index("tensor")
    dp_size = lax.axis_size("dp")
    rows_all = lax.all_gather(block_input, "tensor", axis=0, tiled=True)
    tokens = rows_all.shape[0]
    local_rows = block_input.shape[0]
    heads = query_weight.shape[1] // (NOPE + ROPE)
    experts = router_weight.shape[1]
    local_experts = expert_gate_up.shape[0]
    capacity = 2 * tokens * TOP // experts
    scale = (NOPE + ROPE) ** (-0.5)
    start = tensor_rank * local_rows
    cosine, sine = rotary_tables(segments[0], ROPE)
    allowed = allowed_pairs(segments[0], counts[0])
    attn_gain_wide = full_attn_gain.astype(jnp.float32)
    latent_gain_wide = full_latent_gain.astype(jnp.float32)
    ffn_gain_wide = full_ffn_gain.astype(jnp.float32)
    inputs = rows_all.astype(jnp.float32)
    first_scale = rms_scale(inputs)
    first_unit = inputs * first_scale
    first_normed = (first_unit * attn_gain_wide).astype(jnp.bfloat16)
    query = jnp.dot(first_normed, query_weight, preferred_element_type=jnp.float32).reshape(
        tokens, heads, NOPE + ROPE
    )
    query_rows = jnp.concatenate(
        [query[..., :NOPE], rotate(query[..., NOPE:], cosine[:, None, :], sine[:, None, :])],
        axis=-1,
    ).astype(jnp.bfloat16)
    latent_all = jnp.dot(first_normed, latent_weight, preferred_element_type=jnp.float32)
    latent = latent_all[:, :KVR]
    key_rope = rotate(latent_all[:, KVR:], cosine, sine).astype(jnp.bfloat16)
    latent_scale = rms_scale(latent)
    latent_unit = latent * latent_scale
    latent_normed = (latent_unit * latent_gain_wide).astype(jnp.bfloat16)
    keyval = (
        jnp.dot(latent_normed, keyval_weight, preferred_element_type=jnp.float32)
        .astype(jnp.bfloat16)
        .reshape(tokens, heads, NOPE + VD)
    )
    key_nope = keyval[..., :NOPE]
    values = keyval[..., NOPE:]
    scores = attention_scores(query_rows, key_nope, key_rope, allowed, scale)
    row_max = jnp.max(scores, axis=-1, keepdims=True)
    log_total = row_max + jnp.log(jnp.sum(jnp.exp(scores - row_max), axis=-1, keepdims=True))
    weights_low = jnp.exp(scores - log_total).astype(jnp.bfloat16)
    attended = (
        jnp.einsum("hij,jhd->ihd", weights_low, values, preferred_element_type=jnp.float32)
        .astype(jnp.bfloat16)
        .reshape(tokens, heads * VD)
    )
    attn_part = jnp.dot(attended, output_weight, preferred_element_type=jnp.float32)
    mixed = inputs + lax.psum(attn_part, "tensor")
    second_scale = rms_scale(mixed)
    second_unit = mixed * second_scale
    second_normed = (second_unit * ffn_gain_wide).astype(jnp.bfloat16)
    logits = jnp.dot(second_normed, router_weight, preferred_element_type=jnp.float32)
    probabilities = jax.nn.softmax(logits, axis=-1)
    gate_values = jnp.take_along_axis(probabilities, routes, axis=1)
    shared_pre = jnp.einsum(
        "td,gdf->tgf", second_normed, shared_in, preferred_element_type=jnp.float32
    )
    shared_hidden = (jax.nn.silu(shared_pre[:, 0]) * shared_pre[:, 1]).astype(jnp.bfloat16)
    shared_part = jnp.dot(shared_hidden, shared_out, preferred_element_type=jnp.float32)
    slot_index, target, owner = slot_layout(routes, experts, capacity)
    owner_grid = owner.reshape(experts, capacity)
    padded_rows = jnp.concatenate([second_normed, jnp.zeros((1, D), jnp.bfloat16)], axis=0)
    outgoing = padded_rows[owner_grid]
    arrived = lax.all_to_all(outgoing, "dp", split_axis=0, concat_axis=0, tiled=True)
    expert_rows = to_expert_major(arrived, dp_size, local_experts)
    expert_pre = jnp.einsum(
        "erd,egdf->ergf", expert_rows, expert_gate_up, preferred_element_type=jnp.float32
    )
    expert_hidden = (jax.nn.silu(expert_pre[:, :, 0]) * expert_pre[:, :, 1]).astype(jnp.bfloat16)
    expert_result = jnp.einsum(
        "erf,efd->erd", expert_hidden, expert_down, preferred_element_type=jnp.float32
    )
    returning = from_expert_major(expert_result, dp_size)
    returned = lax.all_to_all(
        returning.astype(jnp.bfloat16), "dp", split_axis=0, concat_axis=0, tiled=True
    ).astype(returning.dtype)
    padded_back = jnp.concatenate([returned.reshape(-1, D), jnp.zeros((1, D), jnp.float32)], axis=0)
    picked = padded_back[target].reshape(tokens, TOP, D)
    routed_part = jnp.sum(gate_values[:, :, None] * picked, axis=1)
    branch_sum = lax.psum_scatter(
        (shared_part + routed_part).astype(jnp.bfloat16), "tensor", scatter_dimension=0, tiled=True
    ).astype(jnp.float32)
    block_output = lax.dynamic_slice_in_dim(mixed, start, local_rows, 0) + branch_sum
    grad_rows = lax.all_gather(cotangent, "tensor", axis=0, tiled=True)
    grad_out = grad_rows.astype(jnp.float32)
    grad_shared_hidden = jnp.dot(grad_rows, shared_out.T, preferred_element_type=jnp.float32)
    grad_shared_out = jnp.dot(shared_hidden.T, grad_rows, preferred_element_type=jnp.float32)
    grad_shared_pre = swiglu_back(shared_pre[:, 0], shared_pre[:, 1], grad_shared_hidden, 1).astype(
        jnp.bfloat16
    )
    grad_shared_in = jnp.einsum(
        "td,tgf->gdf", second_normed, grad_shared_pre, preferred_element_type=jnp.float32
    )
    grad_second = jnp.einsum(
        "tgf,gdf->td", grad_shared_pre, shared_in, preferred_element_type=jnp.float32
    )
    gate_by_slot = (
        jnp.zeros((experts * capacity + 1,), jnp.float32).at[target].set(gate_values.reshape(-1))
    )
    slot_ids = jnp.arange(experts * capacity, dtype=jnp.int32).reshape(experts, capacity)
    padded_grad = jnp.concatenate([grad_out, jnp.zeros((1, D), jnp.float32)], axis=0)
    grad_outgoing = (gate_by_slot[slot_ids][..., None] * padded_grad[owner_grid]).astype(
        jnp.bfloat16
    )
    grad_arrived = lax.all_to_all(grad_outgoing, "dp", split_axis=0, concat_axis=0, tiled=True)
    grad_expert_rows = to_expert_major(grad_arrived, dp_size, local_experts)
    grad_expert_hidden = jnp.einsum(
        "erd,efd->erf", grad_expert_rows, expert_down, preferred_element_type=jnp.float32
    )
    grad_expert_down = jnp.einsum(
        "erf,erd->efd", expert_hidden, grad_expert_rows, preferred_element_type=jnp.float32
    )
    grad_expert_pre = swiglu_back(
        expert_pre[:, :, 0], expert_pre[:, :, 1], grad_expert_hidden, 2
    ).astype(jnp.bfloat16)
    grad_expert_gate_up = jnp.einsum(
        "erd,ergf->egdf", expert_rows, grad_expert_pre, preferred_element_type=jnp.float32
    )
    grad_expert_input = jnp.einsum(
        "ergf,egdf->erd", grad_expert_pre, expert_gate_up, preferred_element_type=jnp.float32
    )
    grad_returning = from_expert_major(grad_expert_input, dp_size)
    grad_returned = lax.all_to_all(
        grad_returning.astype(jnp.bfloat16), "dp", split_axis=0, concat_axis=0, tiled=True
    ).astype(grad_returning.dtype)
    padded_grad_back = jnp.concatenate(
        [grad_returned.reshape(-1, D), jnp.zeros((1, D), jnp.float32)], axis=0
    )
    grad_second = grad_second + jnp.sum(padded_grad_back[target].reshape(tokens, TOP, D), axis=1)
    grad_gates = jnp.sum(grad_out[:, None, :] * picked, axis=-1)
    grad_second, grad_gates = (
        lax.psum(grad_second.astype(jnp.bfloat16), "tensor").astype(jnp.float32),
        lax.psum(grad_gates.astype(jnp.bfloat16), "tensor").astype(jnp.float32),
    )
    chosen = (routes[:, :, None] == jnp.arange(experts, dtype=jnp.int32)[None, None, :]).astype(
        jnp.float32
    )
    grad_probabilities = jnp.sum(chosen * grad_gates[:, :, None], axis=1)
    grad_logits = probabilities * (
        grad_probabilities - jnp.sum(probabilities * grad_probabilities, axis=-1, keepdims=True)
    )
    grad_logits_low = grad_logits.astype(jnp.bfloat16)
    grad_router = jnp.dot(second_normed.T, grad_logits_low, preferred_element_type=jnp.float32)
    grad_second = grad_second + jnp.dot(
        grad_logits_low, router_weight.T, preferred_element_type=jnp.float32
    )
    gain_ffn_grad = jnp.sum(grad_second * second_unit, axis=0)
    grad_mixed = grad_out + rms_back(grad_second * ffn_gain_wide, second_unit, second_scale)
    grad_attn_low = grad_mixed.astype(jnp.bfloat16)
    grad_output_weight = jnp.dot(attended.T, grad_attn_low, preferred_element_type=jnp.float32)
    grad_attended = (
        jnp.dot(grad_attn_low, output_weight.T, preferred_element_type=jnp.float32)
        .astype(jnp.bfloat16)
        .reshape(tokens, heads, VD)
    )
    scores = attention_scores(query_rows, key_nope, key_rope, allowed, scale)
    weights = jnp.exp(scores - log_total)
    weights_low = weights.astype(jnp.bfloat16)
    grad_weights = jnp.einsum(
        "ihd,jhd->hij", grad_attended, values, preferred_element_type=jnp.float32
    )
    grad_values = jnp.einsum(
        "hij,ihd->jhd", weights_low, grad_attended, preferred_element_type=jnp.float32
    )
    grad_scores = (
        weights * (grad_weights - jnp.sum(weights * grad_weights, axis=-1, keepdims=True))
    ).astype(jnp.bfloat16)
    grad_query_nope = (
        jnp.einsum("hij,jhd->ihd", grad_scores, key_nope, preferred_element_type=jnp.float32)
        * scale
    )
    grad_query_rope = (
        jnp.einsum("hij,jd->ihd", grad_scores, key_rope, preferred_element_type=jnp.float32) * scale
    )
    grad_key_nope = (
        jnp.einsum(
            "hij,ihd->jhd", grad_scores, query_rows[..., :NOPE], preferred_element_type=jnp.float32
        )
        * scale
    )
    grad_key_rope = (
        jnp.einsum(
            "hij,ihd->jd", grad_scores, query_rows[..., NOPE:], preferred_element_type=jnp.float32
        )
        * scale
    )
    grad_query = (
        jnp.concatenate(
            [grad_query_nope, rotate_back(grad_query_rope, cosine[:, None, :], sine[:, None, :])],
            axis=-1,
        )
        .astype(jnp.bfloat16)
        .reshape(tokens, heads * (NOPE + ROPE))
    )
    grad_query_weight = jnp.dot(first_normed.T, grad_query, preferred_element_type=jnp.float32)
    grad_first = jnp.dot(grad_query, query_weight.T, preferred_element_type=jnp.float32)
    grad_keyval = (
        jnp.concatenate([grad_key_nope, grad_values], axis=-1)
        .astype(jnp.bfloat16)
        .reshape(tokens, heads * (NOPE + VD))
    )
    grad_keyval_weight = jnp.dot(latent_normed.T, grad_keyval, preferred_element_type=jnp.float32)
    grad_latent_normed = jnp.dot(grad_keyval, keyval_weight.T, preferred_element_type=jnp.float32)
    gain_latent_part = jnp.sum(grad_latent_normed * latent_unit, axis=0)
    grad_latent = rms_back(grad_latent_normed * latent_gain_wide, latent_unit, latent_scale)
    grad_latent_all = jnp.concatenate(
        [grad_latent, rotate_back(grad_key_rope, cosine, sine)], axis=-1
    )
    grad_first, grad_latent_all, gain_latent_grad = (
        lax.psum(grad_first.astype(jnp.bfloat16), "tensor").astype(jnp.float32),
        lax.psum(grad_latent_all.astype(jnp.bfloat16), "tensor").astype(jnp.float32),
        lax.psum(gain_latent_part.astype(jnp.bfloat16), "tensor").astype(jnp.float32),
    )
    grad_latent_low = grad_latent_all.astype(jnp.bfloat16)
    grad_latent_weight = jnp.dot(
        first_normed.T, grad_latent_low, preferred_element_type=jnp.float32
    )
    grad_first = grad_first + jnp.dot(
        grad_latent_low, latent_weight.T, preferred_element_type=jnp.float32
    )
    gain_attn_grad = jnp.sum(grad_first * first_unit, axis=0)
    grad_inputs = grad_mixed + rms_back(grad_first * attn_gain_wide, first_unit, first_scale)
    grad_local = lax.dynamic_slice_in_dim(grad_inputs, start, local_rows, 0)
    summed = (
        lax.psum_scatter(gain_attn_grad, "dp", scatter_dimension=0, tiled=True),
        lax.psum_scatter(grad_query_weight, "dp", scatter_dimension=0, tiled=True),
        lax.psum_scatter(grad_latent_weight, "dp", scatter_dimension=0, tiled=True),
        lax.psum_scatter(gain_latent_grad, "dp", scatter_dimension=0, tiled=True),
        lax.psum_scatter(grad_keyval_weight, "dp", scatter_dimension=0, tiled=True),
        lax.psum_scatter(grad_output_weight, "dp", scatter_dimension=1, tiled=True),
        lax.psum_scatter(gain_ffn_grad, "dp", scatter_dimension=0, tiled=True),
        lax.psum_scatter(grad_router, "dp", scatter_dimension=0, tiled=True),
        lax.psum_scatter(grad_shared_in, "dp", scatter_dimension=1, tiled=True),
        lax.psum_scatter(grad_shared_out, "dp", scatter_dimension=1, tiled=True),
    )
    return (
        block_output,
        grad_local,
        summed[0],
        summed[1],
        summed[2],
        summed[3],
        summed[4],
        summed[5],
        summed[6],
        summed[7],
        summed[8],
        summed[9],
        grad_expert_gate_up,
        grad_expert_down,
    )


def solution(mesh):
    in_specs = (
        P(("dp", "tensor"), None),
        P("dp", None),
        P("dp"),
        P("dp", None),
        P("dp"),
        P("dp", "tensor"),
        P("dp", None),
        P("dp"),
        P("dp", "tensor"),
        P("tensor", "dp"),
        P("dp"),
        P("dp", None),
        P(None, "dp", "tensor"),
        P("tensor", "dp"),
        P("dp", None, None, "tensor"),
        P("dp", "tensor", None),
        P(("dp", "tensor"), None),
    )
    out_specs = (
        P(("dp", "tensor"), None),
        P(("dp", "tensor"), None),
        P("dp"),
        P("dp", "tensor"),
        P("dp", None),
        P("dp"),
        P("dp", "tensor"),
        P("tensor", "dp"),
        P("dp"),
        P("dp", None),
        P(None, "dp", "tensor"),
        P("tensor", "dp"),
        P("dp", None, None, "tensor"),
        P("dp", "tensor", None),
    )
    return jax.shard_map(body, mesh=mesh, in_specs=in_specs, out_specs=out_specs, check_vma=False)
```

profile of v0, /device:TPU:0, one launch (start us, length us, event | category | flops | bytes accessed | tf_op | source)
XLA Modules:
  0.0 2705.8 jit_solution(12535031807572591685)
XLA Ops:
  10.6 23.2 all-gather
  36.7 30.0 %all-reduce.4 = bf16[512]{0:T(512)(128)(2,1)S(1)} all-reduce(bf16[512]{0:T(512)(128)(2,1)S(1)} %dynamic-update-slice), channel_id=1, replica_groups=mesh['dp'=16,'tensor'=2] {'dp'}, use_global_device_ids=true, to_apply=%add.4 | all-reduce | flops 512 | bytes 2048
  81.5 39.4 %all-gather.15.cloned.1.call-done = bf16[512,2048]{1,0:T(8,128)(2,1)} async-done(((bf16[32,2048]{1,0:T(8,128)(2,1)}), bf16[512,2048]{1,0:T(8,128)(2,1)}) %all-gather.15.cloned.1.call-update) | async-done | bytes 2097168 | tf_op jit(solution)/shard_map/all_gather | solution.py:140
  128.3 55.4 %all-gather.17.cloned.1.call-done = bf16[2048,1536]{1,0:T(8,128)(2,1)} async-done(((bf16[128,1536]{1,0:T(8,128)(2,1)}), bf16[2048,1536]{1,0:T(8,128)(2,1)}) %all-gather.17.cloned.1.call-update) | async-done | bytes 6291472 | tf_op jit(solution)/shard_map/all_gather | solution.py:137
  194.0 43.5 %all-gather.19.cloned.1.call-done = bf16[1024,2048]{1,0:T(8,128)(2,1)} async-done(((bf16[1024,128]{1,0:T(8,128)(2,1)}), bf16[1024,2048]{1,0:T(8,128)(2,1)}) %all-gather.19.cloned.1.call-update) | async-done | bytes 4194320 | tf_op jit(solution)/shard_map/all_gather | solution.py:141
  242.9 18.5 all-gather.1
  273.8 29.8 %all-reduce.14.cloned.1.call-done = f32[256,2048]{1,0:T(8,128)} async-done(((f32[256,2048]{1,0:T(8,128)}), f32[256,2048]{1,0:T(8,128)}) %all-reduce.14.cloned.1.call-update) | async-done | bytes 2097168 | tf_op jit(solution)/shard_map/psum | solution.py:209
  309.4 25.2 gather_fusion
  341.5 218.2 %all_gather.46 = bf16[2048,16]{0,1:T(8,128)(2,1)S(1)} all-gather(bf16[128,16]{0,1:T(8,128)(2,1)S(1)} %copy-done.76), channel_id=1, replica_groups=mesh['dp'=16,'tensor'=2] {'dp'}, dimensions={0}, use_global_device_ids=true | all-gather | bytes 69632 | tf_op jit(solution)/shard_map/all_gather | solution.py:143
  562.6 25.7 gather_fusion.3
  641.8 67.8 %all-to-all-start.2 = ((bf16[16,192,2048]{2,1,0:T(8,128)(2,1)}), bf16[16,192,2048]{2,1,0:T(8,128)(2,1)}, u32[]{:S(2)}, u32[]{:S(2)}) async-start(bf16[16,192,2048]{2,1,0:T(8,128)(2,1)} %multiply_convert_fusion), calls=%async_computation.3 | async-start | bytes 25165824 | tf_op jit(solution)/shard_map/all_to_all | solution.py:266
  709.6 24.6 convolution_bitcast_fusion.1
  734.2 199.2 %all-to-all-done.2 = bf16[16,192,2048]{2,1,0:T(8,128)(2,1)} async-done(((bf16[16,192,2048]{2,1,0:T(8,128)(2,1)}), bf16[16,192,2048]{2,1,0:T(8,128)(2,1)}, u32[]{:S(2)}, u32[]{:S(2)}) %all-to-all-start.2) | async-done | bytes 12582944 | tf_op jit(solution)/shard_map/all_to_all | solution.py:266
  933.3 20.8 fusion.17
  974.2 25.8 bitcast_convert_fusion
  1000.0 54.2 %all-to-all-start.3 = ((bf16[16,192,2048]{2,1,0:T(8,128)(2,1)}), bf16[16,192,2048]{2,1,0:T(8,128)(2,1)}, u32[]{:S(2)}, u32[]{:S(2)}) async-start(bf16[16,192,2048]{2,1,0:T(8,128)(2,1)} %bitcast_convert_fusion), calls=%async_computation.4 | async-start | bytes 25165824 | tf_op jit(solution)/shard_map/all_to_all | solution.py:284
  1085.2 262.2 %all-to-all-done.3 = bf16[16,192,2048]{2,1,0:T(8,128)(2,1)} async-done(((bf16[16,192,2048]{2,1,0:T(8,128)(2,1)}), bf16[16,192,2048]{2,1,0:T(8,128)(2,1)}, u32[]{:S(2)}, u32[]{:S(2)}) %all-to-all-start.3) | async-done | bytes 12582944 | tf_op jit(solution)/shard_map/all_to_all | solution.py:284
  1347.4 53.3 %all-to-all-start.1 = ((bf16[16,192,2048]{2,1,0:T(8,128)(2,1)}), bf16[16,192,2048]{2,1,0:T(8,128)(2,1)}, u32[]{:S(2)}, u32[]{:S(2)}) async-start(bf16[16,192,2048]{2,1,0:T(8,128)(2,1)} %convolution_convert_fusion), calls=%async_computation.1 | async-start | bytes 25165824 | tf_op jit(solution)/shard_map/all_to_all | solution.py:235
  1412.6 211.0 %all-gather.23.cloned.1.call-done = bf16[1408,2048]{1,0:T(8,128)(2,1)} async-done(((bf16[1408,128]{1,0:T(8,128)(2,1)}), bf16[1408,2048]{1,0:T(8,128)(2,1)}) %all-gather.23.cloned.1.call-update) | async-done | bytes 5767184 | tf_op jit(solution)/shard_map/all_gather | solution.py:145
  1645.1 20.7 gather_fusion.4
  1712.4 20.8 gather_fusion.1
  1814.2 40.4 %all-reduce.18.cloned.1.call-done = (bf16[256,576]{0,1:T(8,128)(2,1)}, bf16[256,2048]{1,0:T(8,128)(2,1)}) async-done(((bf16[256,576]{0,1:T(8,128)(2,1)}, bf16[256,2048]{1,0:T(8,128)(2,1)}), (bf16[256,576]{0,1:T(8,128)(2,1)}, bf16[256,2048]{1,0:T(8,128)(2,1)})) %all-reduce.18.cloned.1.call-update) | async-done | bytes 1343504 | tf_op jit(solution)/shard_map/psum | solution.py:372
  1879.1 17.6 fusion.18
  1896.7 23.8 fusion.13
  1920.5 165.0 %reduce-scatter.21.cloned.1.call-done = f32[2,128,1408]{1,2,0:T(8,128)} async-done(((f32[2,2048,1408]{1,2,0:T(8,128)}), f32[2,128,1408]{1,2,0:T(8,128)}) %reduce-scatter.21.cloned.1.call-update) | async-done | bytes 1441808 | tf_op jit(solution)/shard_map/reduce_scatter | solution.py:394
  2115.1 63.3 %all-reduce.8 = (f32[2048]{0:T(1024)S(1)}, f32[512]{0:T(512)S(1)}, f32[2048]{0:T(1024)S(1)}) all-reduce(f32[2048]{0:T(1024)S(1)} %get-tuple-element.104, bf16[512]{0:T(512)(128)(2,1)S(1)} %psum.47, f32[2048]{0:T(1024)S(1)} %get-tuple-element.100), channel_id=3, replica_groups=mesh['dp'=16,'tensor'=2] {'dp'}, use_global_device_ids=true, to_apply=%region_29.30.clone | all-reduce | flops 4608 | bytes 35840
  2183.4 55.9 %reduce-scatter.23.cloned.1.call-done = f32[1408,128]{1,0:T(8,128)} async-done(((f32[1408,2048]{1,0:T(8,128)}), f32[1408,128]{1,0:T(8,128)}) %reduce-scatter.23.cloned.1.call-update) | async-done | bytes 720912 | tf_op jit(solution)/shard_map/reduce_scatter | solution.py:395
  2239.3 55.8 %reduce-scatter.19.cloned.1.call-done = f32[128,16]{0,1:T(8,128)} async-done(((f32[2048,16]{0,1:T(8,128)}), f32[128,16]{0,1:T(8,128)}) %reduce-scatter.19.cloned.1.call-update) | async-done | bytes 8208 | tf_op jit(solution)/shard_map/reduce_scatter | solution.py:393
  2295.1 76.3 %reduce-scatter.15.cloned.1.call-done = f32[32,2048]{1,0:T(8,128)} async-done(((f32[512,2048]{1,0:T(8,128)}), f32[32,2048]{1,0:T(8,128)}) %reduce-scatter.15.cloned.1.call-update) | async-done | bytes 262160 | tf_op jit(solution)/shard_map/reduce_scatter | solution.py:390
  2371.4 78.8 %reduce-scatter.13.cloned.1.call-done = f32[128,576]{0,1:T(8,128)} async-done(((f32[2048,576]{0,1:T(8,128)}), f32[128,576]{0,1:T(8,128)}) %reduce-scatter.13.cloned.1.call-update) | async-done | bytes 294928 | tf_op jit(solution)/shard_map/reduce_scatter | solution.py:388
  2450.3 109.0 %reduce-scatter.17.cloned.1.call-done = f32[1024,128]{1,0:T(8,128)} async-done(((f32[1024,2048]{1,0:T(8,128)}), f32[1024,128]{1,0:T(8,128)}) %reduce-scatter.17.cloned.1.call-update) | async-done | bytes 524304 | tf_op jit(solution)/shard_map/reduce_scatter | solution.py:391
  2559.2 139.7 %reduce-scatter.11.cloned.1.call-done = f32[128,1536]{1,0:T(8,128)} async-done(((f32[2048,1536]{1,0:T(8,128)}), f32[128,1536]{1,0:T(8,128)}) %reduce-scatter.11.cloned.1.call-update) | async-done | bytes 786448 | tf_op jit(solution)/shard_map/reduce_scatter | solution.py:387
  (351 shorter events, 392.7 us)
Async XLA Ops:
  7.2 926.2 %copy-start = (bf16[1,704,2048]{2,1,0:T(8,128)(2,1)S(1)}, bf16[1,704,2048]{2,1,0:T(8,128)(2,1)}, u32[]{:S(2)}) copy-start(bf16[1,704,2048]{2,1,0:T(8,128)(2,1)} %param.32) | copy-start | bytes 8650756
  7.2 63.1 %all-gather.11.cloned.1.call-start = ((), (), s32[]{:S(2)}) async-start(), calls=%async_computation.12 | async-start | bytes 1572864 | tf_op jit(solution)/shard_map/all_gather | solution.py:161
  7.9 70.5 %all-gather.13.cloned.1.call-start = ((), (), s32[]{:S(2)}) async-start(), calls=%async_computation.13 | async-start | bytes 2506752 | tf_op jit(solution)/shard_map/all_gather | solution.py:138
  8.7 112.2 %all-gather.15.cloned.1.call-start = ((), (), s32[]{:S(2)}) async-start(), calls=%async_computation.14 | async-start | bytes 2228224 | tf_op jit(solution)/shard_map/all_gather | solution.py:140
  9.4 174.3 %all-gather.17.cloned.1.call-start = ((), (), s32[]{:S(2)}) async-start(), calls=%async_computation.15 | async-start | bytes 6684672 | tf_op jit(solution)/shard_map/all_gather | solution.py:137
  10.0 227.5 %all-gather.19.cloned.1.call-start = ((), (), s32[]{:S(2)}) async-start(), calls=%async_computation.16 | async-start | bytes 4456448 | tf_op jit(solution)/shard_map/all_gather | solution.py:141
  10.6 292.9 %all-reduce.14.cloned.1.call-start = ((), (), s32[]{:S(2)}) async-start(), calls=%async_computation.17 | async-start | bytes 4194304 | tf_op jit(solution)/shard_map/psum | solution.py:209
  33.8 149.9 %copy-start.52 = (f32[16,1,128]{2,1,0:T(1,128)}, f32[16,1,128]{2,1,0:T(1,128)S(1)}, u32[]{:S(2)}) copy-start(f32[16,1,128]{2,1,0:T(1,128)S(1)} %convert_element_type.181) | copy-start | bytes 24580
  71.9 111.8 %copy-start.64 = (f32[256]{0:T(256)}, f32[256]{0:T(256)S(1)}, u32[]{:S(2)}) copy-start(f32[256]{0:T(256)S(1)} %add_rsqrt_fusion.2) | copy-start | bytes 3076
  267.2 337.7 %copy-start.62 = (s32[1536]{0:T(1024)}, s32[1536]{0:T(1024)S(1)}, u32[]{:S(2)}) copy-start(s32[1536]{0:T(1024)S(1)} %get-tuple-element.106) | copy-start | bytes 18436
  334.5 307.3 %all-to-all-start = ((bf16[16,192,2048]{2,1,0:T(8,128)(2,1)}), bf16[16,192,2048]{2,1,0:T(8,128)(2,1)}, u32[]{:S(2)}, u32[]{:S(2)}) async-start(bf16[16,192,2048]{2,1,0:T(8,128)(2,1)} %bitcast.231), calls=%async_computation | async-start | bytes 25165824 | tf_op jit(solution)/shard_map/all_to_all | solution.py:225
  340.4 219.4 %all-gather.25.cloned.1.call-start = ((), (), s32[]{:S(2)}) async-start(), calls=%async_computation.21 | async-start | bytes 1572864 | tf_op jit(solution)/shard_map/all_gather | solution.py:245
  641.8 291.5 %all-to-all-start.2 = ((bf16[16,192,2048]{2,1,0:T(8,128)(2,1)}), bf16[16,192,2048]{2,1,0:T(8,128)(2,1)}, u32[]{:S(2)}, u32[]{:S(2)}) async-start(bf16[16,192,2048]{2,1,0:T(8,128)(2,1)} %multiply_convert_fusion), calls=%async_computation.3 | async-start | bytes 25165824 | tf_op jit(solution)/shard_map/all_to_all | solution.py:266
  1000.0 347.5 %all-to-all-start.3 = ((bf16[16,192,2048]{2,1,0:T(8,128)(2,1)}), bf16[16,192,2048]{2,1,0:T(8,128)(2,1)}, u32[]{:S(2)}, u32[]{:S(2)}) async-start(bf16[16,192,2048]{2,1,0:T(8,128)(2,1)} %bitcast_convert_fusion), calls=%async_computation.4 | async-start | bytes 25165824 | tf_op jit(solution)/shard_map/all_to_all | solution.py:284
  1054.2 349.5 %all-gather.21.cloned.1.call-start = ((), (), s32[]{:S(2)}) async-start(), calls=%async_computation.18 | async-start | bytes 12255232 | tf_op jit(solution)/shard_map/all_gather | solution.py:144
  1085.2 316.8 %copy-start.63 = (s32[1536]{0:T(1024)S(1)}, s32[1536]{0:T(1024)}, u32[]{:S(2)}) copy-start(s32[1536]{0:T(1024)} %copy-done.62) | copy-start | bytes 18436
  1085.2 316.8 %copy-start.11 = (bf16[256,2048]{1,0:T(8,128)(2,1)S(1)}, bf16[256,2048]{1,0:T(8,128)(2,1)}, u32[]{:S(2)}) copy-start(bf16[256,2048]{1,0:T(8,128)(2,1)} %all-gather.25.cloned.1.call-done) | copy-start | bytes 3145732
  1347.4 350.6 %all-to-all-start.1 = ((bf16[16,192,2048]{2,1,0:T(8,128)(2,1)}), bf16[16,192,2048]{2,1,0:T(8,128)(2,1)}, u32[]{:S(2)}, u32[]{:S(2)}) async-start(bf16[16,192,2048]{2,1,0:T(8,128)(2,1)} %convolution_convert_fusion), calls=%async_computation.1 | async-start | bytes 25165824 | tf_op jit(solution)/shard_map/all_to_all | solution.py:235
  1400.8 222.8 %all-gather.23.cloned.1.call-start = ((), (), s32[]{:S(2)}) async-start(), calls=%async_computation.19 | async-start | bytes 6127616 | tf_op jit(solution)/shard_map/all_gather | solution.py:145
  1401.5 364.4 %all-reduce.16.cloned.1.call-start = ((), (), s32[]{:S(2)}) async-start(), calls=%async_computation.22 | async-start | bytes 2097152 | tf_op jit(solution)/shard_map/psum | solution.py:293
  1698.0 156.6 %all-reduce.18.cloned.1.call-start = ((), (), s32[]{:S(2)}) async-start(), calls=%async_computation.30 | async-start | bytes 2686976 | tf_op jit(solution)/shard_map/psum | solution.py:372
  1785.7 299.8 %reduce-scatter.21.cloned.1.call-start = ((), (), s32[]{:S(2)}) async-start(), calls=%async_computation.28 | async-start | bytes 24510464 | tf_op jit(solution)/shard_map/reduce_scatter | solution.py:394
  1796.6 311.2 %reduce-scatter.9.cloned.1.call-start = ((), (), s32[]{:S(2)}) async-start(), calls=%async_computation.20 | async-start | bytes 1572864 | tf_op jit(solution)/shard_map/reduce_scatter | solution.py:241
  1803.0 436.3 %reduce-scatter.23.cloned.1.call-start = ((), (), s32[]{:S(2)}) async-start(), calls=%async_computation.29 | async-start | bytes 12255232 | tf_op jit(solution)/shard_map/reduce_scatter | solution.py:395
  1810.2 484.9 %reduce-scatter.19.cloned.1.call-start = ((), (), s32[]{:S(2)}) async-start(), calls=%async_computation.27 | async-start | bytes 139264 | tf_op jit(solution)/shard_map/reduce_scatter | solution.py:393
  1811.2 560.2 %reduce-scatter.15.cloned.1.call-start = ((), (), s32[]{:S(2)}) async-start(), calls=%async_computation.25 | async-start | bytes 4456448 | tf_op jit(solution)/shard_map/reduce_scatter | solution.py:390
  1814.2 636.1 %reduce-scatter.13.cloned.1.call-start = ((), (), s32[]{:S(2)}) async-start(), calls=%async_computation.24 | async-start | bytes 5013504 | tf_op jit(solution)/shard_map/reduce_scatter | solution.py:388
  1858.7 700.6 %reduce-scatter.17.cloned.1.call-start = ((), (), s32[]{:S(2)}) async-start(), calls=%async_computation.26 | async-start | bytes 8912896 | tf_op jit(solution)/shard_map/reduce_scatter | solution.py:391
  1866.7 832.2 %reduce-scatter.11.cloned.1.call-start = ((), (), s32[]{:S(2)}) async-start(), calls=%async_computation.23 | async-start | bytes 13369344 | tf_op jit(solution)/shard_map/reduce_scatter | solution.py:387
  1920.5 187.3 %copy-start.6 = (f32[256,2048]{1,0:T(8,128)S(1)}, f32[256,2048]{1,0:T(8,128)}, u32[]{:S(2)}) copy-start(f32[256,2048]{1,0:T(8,128)} %copy-done.4) | copy-start | bytes 6291460
  1920.5 189.6 %copy-start.30 = (bf16[256,576]{0,1:T(8,128)(2,1)S(1)}, bf16[256,576]{0,1:T(8,128)(2,1)}, u32[]{:S(2)}) copy-start(bf16[256,576]{0,1:T(8,128)(2,1)} %get-tuple-element.111) | copy-start | bytes 884740
  2110.0 588.9 %copy-start.1 = (bf16[1,704,2048]{2,1,0:T(8,128)(2,1)S(1)}, bf16[1,704,2048]{2,1,0:T(8,128)(2,1)}, u32[]{:S(2)}) copy-start(bf16[1,704,2048]{2,1,0:T(8,128)(2,1)} %param.32) | copy-start | bytes 8650756
  (75 other events, 1035.8 us)
Sparse Core Ops, SparseCore 0:
  9.6 23.9 all-gather.10
  35.8 42.6 all-gather.12
  80.6 40.2 all-gather.14
  123.0 60.6 all-gather.16
  185.7 51.7 all-gather.18
  242.4 61.0 all-reduce.13
  342.8 21.6 all-gather.24
  1057.6 261.9 all-gather.20
  1404.0 219.5 all-gather.22
  1698.2 62.0 all-reduce.15
  1785.9 68.7 all-reduce.17
  1858.6 226.8 reduce-scatter.20
  2088.3 19.3 reduce-scatter.8
  2112.8 126.4 reduce-scatter.22
  2243.1 51.9 reduce-scatter.18
  2299.9 71.4 reduce-scatter.14
  2375.7 74.5 reduce-scatter.12
  2455.3 103.8 reduce-scatter.16
  2564.4 134.4 reduce-scatter.10
where the time goes:
time: 2720 us; the launch traced here: 2710 us
  waiting for transfers between devices  1590 us (58%)
  blocking collectives  363 us (13%)
  matrix products  235 us (9%)
  local copies, waits for them, and re-layouts  216 us (8%)
  starting transfers between devices  182 us (7%)
  other arithmetic  103 us (4%)
    all_to_all x1, waiting for transfers between devices, body(): lax.all_to_all(grad_returning.astype(jnp.bfloat16), 'dp', split_axis=0, c...  262 us
    all_gather x1, blocking collectives, body(): lax.all_gather(w_router, 'dp', axis=0, tiled=True)  218 us
    all_gather x1, waiting for transfers between devices, body(): lax.all_gather(shared_down, 'dp', axis=1, tiled=True)  211 us
    all_to_all x1, waiting for transfers between devices, body(): lax.all_to_all(grad_outgoing, 'dp', split_axis=0, concat_axis=0, tiled=True)  199 us
    reduce_scatter x1, waiting for transfers between devices, body(): lax.psum_scatter(grad_shared_in, 'dp', scatter_dimension=1, tiled=True)  165 us
    reduce_scatter x1, waiting for transfers between devices, body(): lax.psum_scatter(grad_query_weight, 'dp', scatter_dimension=0, tiled=True)  140 us
    reduce_scatter x1, waiting for transfers between devices, body(): lax.psum_scatter(grad_output_weight, 'dp', scatter_dimension=1, tiled=True)  109 us
    unnamed x2, blocking collectives  93.4 us
  transfers between devices with their start and end apart: 23, of which 17 were waited for; matrix products, arithmetic and copies ran while one was open for 16% of the time, Pallas kernels for 0%

commit v1 on v0

--- a/solution.py
+++ b/solution.py
@@ -1,8 +1,11 @@
+import functools
 import math
 
 import jax
 import jax.numpy as jnp
 from jax import lax
+from jax.experimental import pallas as pl
+from jax.experimental.pallas import tpu as pltpu
 from jax.sharding import PartitionSpec as P
 
 D = 2048
@@ -84,7 +87,11 @@
     tokens = routes.shape[0]
     flat = routes.reshape(-1)
     onehot = (flat[:, None] == jnp.arange(experts, dtype=jnp.int32)[None, :]).astype(jnp.int32)
-    before = jnp.cumsum(onehot, axis=0) - onehot
+    rank = jnp.arange(flat.shape[0], dtype=jnp.int32)
+    earlier = (rank[None, :] < rank[:, None]).astype(jnp.bfloat16)
+    before = jnp.dot(
+        earlier, onehot.astype(jnp.bfloat16), preferred_element_type=jnp.float32
+    ).astype(jnp.int32)
     slot_index = jnp.sum(before * onehot, axis=1)
     target = flat * capacity + slot_index
     token_ids = jnp.arange(flat.shape[0], dtype=jnp.int32) // routes.shape[1]
@@ -113,7 +120,7 @@
     )
 
 
-def body(
+def exchange_body(
     block_input,
     segments,
     counts,
@@ -412,6 +419,578 @@
     )
 
 
+RINGS = 4
+
+
+def ring_step(values):
+    return lax.ppermute(values, "dp", [(i, (i + RINGS) % 16) for i in range(16)])
+
+
+def other_y(values):
+    return lax.ppermute(values, "dp", [(i, i ^ 2) for i in range(16)])
+
+
+def other_core(values):
+    return lax.ppermute(values, "dp", [(i, i ^ 1) for i in range(16)])
+
+
+def other_x(values):
+    return lax.ppermute(values, "tensor", [(0, 1), (1, 0)])
+
+
+def gather_rows(rows):
+    half = rows.shape[0] // 2
+    planes = []
+    current = rows
+    for distance in range(RINGS):
+        if distance:
+            current = ring_step(current)
+        beside = other_y(current)
+        across = other_x(current)
+        plane = jnp.concatenate(
+            [current, beside, across, other_y(across[:half]), other_x(beside[half:])], axis=0
+        )
+        planes.append((plane, other_core(plane)))
+    return planes
+
+
+def add_low(first, second):
+    return (first.astype(jnp.float32) + second.astype(jnp.float32)).astype(jnp.bfloat16)
+
+
+def plane_sum(mine, theirs):
+    size = mine.shape[0] // 4
+    half = size // 2
+    total = add_low(mine, other_core(theirs))
+    own, beside, across = total[:size], total[size : 2 * size], total[2 * size : 3 * size]
+    corner_y = other_y(total[3 * size : 3 * size + half])
+    corner_x = other_x(total[3 * size + half :])
+    across = jnp.concatenate([add_low(across[:half], corner_y), across[half:]], axis=0)
+    beside = jnp.concatenate([beside[:half], add_low(beside[half:], corner_x)], axis=0)
+    return (
+        own.astype(jnp.float32)
+        + other_x(across).astype(jnp.float32)
+        + other_y(beside).astype(jnp.float32)
+    )
+
+
+def ring_sum(parts):
+    moving = parts[1]
+    for distance in (2, 3, 0):
+        moving = ring_step(moving.astype(jnp.bfloat16)).astype(jnp.float32) + parts[distance]
+    return moving
+
+
+def gather_weight(shard):
+    chunks = []
+    current = shard
+    for distance in range(RINGS):
+        if distance:
+            current = ring_step(current)
+        beside = other_y(current)
+        for flip_y, chunk in ((0, current), (1, beside)):
+            for flip_core, piece in ((0, chunk), (1, other_core(chunk))):
+                chunks.append(((distance, flip_y, flip_core), piece))
+    return chunks
+
+
+def place_of(coords, key):
+    z, y, core = coords
+    distance, flip_y, flip_core = key
+    return (
+        lax.rem(z + RINGS - distance, RINGS) * 4
+        + (1 - y if flip_y else y) * 2
+        + (1 - core if flip_core else core)
+    )
+
+
+def place_kernel(keys, moves, coords_ref, *refs):
+    chunks = refs[: len(keys)]
+    outs = refs[len(keys) : -1]
+    semaphores = refs[-1]
+    coords = (coords_ref[0], coords_ref[1], coords_ref[2])
+    copies = []
+    for key, chunk in zip(keys, chunks):
+        block = place_of(coords, key)
+        for source_rows, source_columns, out, rows, columns in moves:
+            start = pl.multiple_of(block * rows, rows)
+            copies.append(
+                pltpu.make_async_copy(
+                    chunk.at[source_rows, source_columns],
+                    outs[out].at[pl.ds(start, rows), columns],
+                    semaphores.at[len(copies)],
+                )
+            )
+    for copy in copies:
+        copy.start()
+    for copy in copies:
+        copy.wait()
+
+
+def place_chunks(coords, chunks, moves, shapes):
+    keys = [key for key, _ in chunks]
+    anywhere = pl.BlockSpec(memory_space=pl.ANY)
+    return pl.pallas_call(
+        functools.partial(place_kernel, keys, moves),
+        out_shape=[jax.ShapeDtypeStruct(shape, jnp.bfloat16) for shape in shapes],
+        in_specs=[pl.BlockSpec(memory_space=pltpu.SMEM)] + [anywhere] * len(chunks),
+        out_specs=[anywhere] * len(shapes),
+        scratch_shapes=[pltpu.SemaphoreType.DMA((len(chunks) * len(moves),))],
+        cost_estimate=pl.CostEstimate(
+            flops=0,
+            bytes_accessed=4 * sum(shape[0] * shape[1] for shape in shapes),
+            transcendentals=0,
+        ),
+    )(coords, *[piece for _, piece in chunks])
+
+
+def weight_keys():
+    return [
+        (distance, flip_y, flip_core)
+        for flip_core in (0, 1)
+        for flip_y in (0, 1)
+        for distance in range(RINGS)
+    ]
+
+
+def scatter_weight(grads):
+    half = grads.shape[0] // 2
+    total = add_low(grads[:half], other_core(grads[half:]))
+    quarter = half // 2
+    total = total[:quarter].astype(jnp.float32) + other_y(total[quarter:]).astype(jnp.float32)
+    size = quarter // RINGS
+    return ring_sum([total[r * size : (r + 1) * size] for r in range(RINGS)])
+
+
+def attend_forward(query_rows, key_nope, key_rope, values, allowed, scale):
+    scores = attention_scores(query_rows, key_nope, key_rope, allowed, scale)
+    row_max = jnp.max(scores, axis=-1, keepdims=True)
+    log_total = row_max + jnp.log(jnp.sum(jnp.exp(scores - row_max), axis=-1, keepdims=True))
+    weights_low = jnp.exp(scores - log_total).astype(jnp.bfloat16)
+    attended = jnp.einsum("hij,jhd->ihd", weights_low, values, preferred_element_type=jnp.float32)
+    return attended.astype(jnp.bfloat16), log_total
+
+
+def wide_dot(left, right):
+    return jnp.dot(left, right, preferred_element_type=jnp.float32)
+
+
+def dot_turned(left, right):
+    return lax.dot_general(left, right, (((1,), (1,)), ((), ())), preferred_element_type=jnp.float32)
+
+
+def dot_rows(left, right):
+    return lax.dot_general(left, right, (((0,), (0,)), ((), ())), preferred_element_type=jnp.float32)
+
+
+def mlp_rows(rows, grad_rows, routed, expert, sizes, gate_weight, up_weight, down_weight):
+    units, shared, experts = sizes
+    width = gate_weight.shape[1]
+    pre_gate = wide_dot(rows, gate_weight)
+    pre_up = wide_dot(rows, up_weight)
+    down_grad = dot_turned(grad_rows, down_weight)
+    column = lax.broadcasted_iota(jnp.int32, (1, width), 1)
+    logits = pre_gate[:, units + shared : units + shared + experts]
+    probabilities = jax.nn.softmax(logits, axis=-1)
+    mine = lax.broadcasted_iota(jnp.int32, (1, experts), 1) == expert
+    gate = routed[:, None] * jnp.sum(jnp.where(mine, probabilities, 0.0), axis=1, keepdims=True)
+    sigmoid = jax.nn.sigmoid(pre_gate)
+    hidden = (pre_gate * sigmoid * pre_up).astype(jnp.bfloat16).astype(jnp.float32)
+    scale = jnp.where(column < units, gate, jnp.where(column < units + shared, 1.0, 0.0))
+    scaled_hidden = (scale * hidden).astype(jnp.bfloat16)
+    grad_gate_value = jnp.sum(
+        jnp.where(column < units, hidden * down_grad, 0.0), axis=1, keepdims=True
+    )
+    grad_hidden = scale * down_grad
+    grad_gate = grad_hidden * pre_up * sigmoid * (1.0 + pre_gate * (1.0 - sigmoid))
+    grad_up = (grad_hidden * pre_gate * sigmoid).astype(jnp.bfloat16)
+    grad_logits = (gate * grad_gate_value) * (jnp.where(mine, 1.0, 0.0) - probabilities)
+    grad_logits = jnp.pad(
+        grad_logits, ((0, 0), (units + shared, width - units - shared - experts))
+    )
+    router_column = (column >= units + shared) & (column < units + shared + experts)
+    grad_gate = jnp.where(router_column, grad_logits, grad_gate).astype(jnp.bfloat16)
+    out = wide_dot(scaled_hidden, down_weight).astype(jnp.bfloat16)
+    grad_input = (dot_turned(grad_gate, gate_weight) + dot_turned(grad_up, up_weight)).astype(
+        jnp.bfloat16
+    )
+    return scaled_hidden, grad_gate, grad_up, out, grad_input
+
+
+def gather_body(
+    block_input,
+    segments,
+    counts,
+    routes,
+    attn_gain,
+    w_query,
+    w_latent,
+    latent_gain,
+    w_keyval,
+    w_output,
+    ffn_gain,
+    w_router,
+    shared_gate_up,
+    shared_down,
+    expert_gate_up,
+    expert_down,
+    cotangent,
+):
+    f32 = jnp.float32
+    bf16 = jnp.bfloat16
+    blocks = 16
+    index = lax.axis_index("dp")
+    x = lax.axis_index("tensor")
+    coords = jnp.stack([index // 4, (index // 2) % 2, index % 2]).astype(jnp.int32)
+    z, y, core = coords[0], coords[1], coords[2]
+    local_rows = block_input.shape[0]
+    tokens = 2 * local_rows
+    depth = w_query.shape[0]
+    query_width = w_query.shape[1]
+    heads = query_width // (NOPE + ROPE)
+    experts = w_router.shape[1]
+    units = expert_gate_up.shape[3]
+    shared = shared_gate_up.shape[2] // blocks
+    width = -(-(units + shared + experts) // 128) * 128
+    latent_depth = w_keyval.shape[0]
+    scale = (NOPE + ROPE) ** (-0.5)
+
+    def both_halves(own, other):
+        return jnp.concatenate(
+            [jnp.where(x == 0, own, other), jnp.where(x == 0, other, own)], axis=0
+        )
+
+    small = jnp.concatenate(
+        [
+            attn_gain[:, None],
+            ffn_gain[:, None],
+            w_router,
+            jnp.pad(latent_gain, (0, depth - latent_depth))[:, None],
+            routes.reshape(depth, -1).astype(bf16),
+        ],
+        axis=1,
+    )
+    small = lax.all_gather(small, "dp", axis=0, tiled=True)
+    attn_gain_wide = small[:, 0].astype(f32)
+    ffn_gain_wide = small[:, 1].astype(f32)
+    router_weight = small[:, 2 : 2 + experts]
+    latent_gain_wide = (
+        small[:, 2 + experts].reshape(blocks, depth)[:, :latent_depth].reshape(-1).astype(f32)
+    )
+    routes_all = small[:, 3 + experts :].reshape(blocks * tokens, TOP)
+    routed_all = jnp.any(routes_all == index.astype(bf16), axis=1).astype(f32)
+    order = jnp.stack(
+        [
+            place_of(coords, (distance, flip_y, flip_core)) * 2 + (1 - x if flip_x else x)
+            for distance in range(RINGS)
+            for flip_core in (0, 1)
+            for flip_x, flip_y in ((0, 0), (0, 1), (1, 0), (1, 1))
+        ]
+    )
+    routed = routed_all.reshape(blocks * 2, local_rows)[order].reshape(
+        RINGS, 2, 4 * local_rows
+    )
+
+    rows_all = both_halves(block_input, other_x(block_input))
+    first_chunks = gather_weight(jnp.concatenate([w_query, w_latent], axis=1))
+    parts = depth // latent_depth
+    keyval_part = w_keyval.shape[1] // parts
+    keyval_packed = (
+        w_keyval.reshape(latent_depth, parts, keyval_part).transpose(1, 0, 2).reshape(depth, -1)
+    )
+    second_chunks = gather_weight(jnp.concatenate([keyval_packed, w_output.T], axis=1))
+    (first_weight,) = place_chunks(
+        coords,
+        first_chunks,
+        [(pl.ds(0, depth), pl.ds(0, query_width + KVR + ROPE), 0, depth, pl.ds(0, query_width + KVR + ROPE))],
+        [(D, query_width + KVR + ROPE)],
+    )
+    keyval_weight, output_turned = place_chunks(
+        coords,
+        second_chunks,
+        [
+            (
+                pl.ds(k * latent_depth, latent_depth),
+                pl.ds(0, keyval_part),
+                0,
+                latent_depth,
+                pl.ds(k * keyval_part, keyval_part),
+            )
+            for k in range(parts)
+        ]
+        + [
+            (
+                pl.ds(0, depth),
+                pl.ds(keyval_part, w_output.shape[0]),
+                1,
+                depth,
+                pl.ds(0, w_output.shape[0]),
+            )
+        ],
+        [(KVR, w_keyval.shape[1]), (D, w_output.shape[0])],
+    )
+
+    shared_in = lax.all_to_all(
+        shared_gate_up.reshape(2, depth, blocks, shared).transpose(2, 0, 1, 3).reshape(
+            blocks, 2 * depth, shared
+        ),
+        "dp",
+        split_axis=0,
+        concat_axis=0,
+        tiled=True,
+    ).reshape(blocks, 2, depth, shared)
+    shared_out = lax.all_to_all(
+        shared_down.reshape(blocks, shared, depth),
+        "dp",
+        split_axis=0,
+        concat_axis=0,
+        tiled=True,
+    )
+    shared_gate = shared_in[:, 0].reshape(D, shared)
+    shared_up = shared_in[:, 1].reshape(D, shared)
+    spare = width - units - shared
+    gate_weight = jnp.concatenate(
+        [
+            expert_gate_up[0, 0],
+            shared_gate,
+            router_weight,
+            jnp.zeros((D, spare - experts), bf16),
+        ],
+        axis=1,
+    )
+    up_weight = jnp.concatenate(
+        [expert_gate_up[0, 1], shared_up, jnp.zeros((D, spare), bf16)], axis=1
+    )
+    down_weight = jnp.concatenate(
+        [
+            expert_down[0],
+            shared_out.transpose(1, 0, 2).reshape(shared, D),
+            jnp.zeros((spare, D), bf16),
+        ],
+        axis=0,
+    )
+
+    cosine, sine = rotary_tables(segments[0], ROPE)
+    allowed = allowed_pairs(segments[0], counts[0])
+    inputs = rows_all.astype(f32)
+    first_scale = rms_scale(inputs)
+    first_unit = inputs * first_scale
+    first_normed = (first_unit * attn_gain_wide).astype(bf16)
+    projected = wide_dot(first_normed, first_weight)
+    query = projected[:, :query_width].reshape(tokens, heads, NOPE + ROPE)
+    query_rows = jnp.concatenate(
+        [query[..., :NOPE], rotate(query[..., NOPE:], cosine[:, None, :], sine[:, None, :])],
+        axis=-1,
+    ).astype(bf16)
+    latent = projected[:, query_width : query_width + KVR]
+    key_rope = rotate(projected[:, query_width + KVR :], cosine, sine).astype(bf16)
+    latent_scale = rms_scale(latent)
+    latent_unit = latent * latent_scale
+    latent_normed = (latent_unit * latent_gain_wide).astype(bf16)
+    keyval = wide_dot(latent_normed, keyval_weight).astype(bf16).reshape(tokens, heads, NOPE + VD)
+    key_nope = keyval[..., :NOPE]
+    values = keyval[..., NOPE:]
+    attended, log_total = attend_forward(query_rows, key_nope, key_rope, values, allowed, scale)
+    attended = attended.reshape(tokens, heads * VD)
+    attn_part = dot_turned(attended, output_turned)
+    low_rows, high_rows = attn_part[:local_rows], attn_part[local_rows:]
+    own_part = jnp.where(x == 0, low_rows, high_rows)
+    sent_part = jnp.where(x == 0, high_rows, low_rows).astype(bf16)
+    mixed = block_input.astype(f32) + own_part + other_x(sent_part).astype(f32)
+    second_scale = rms_scale(mixed)
+    second_unit = mixed * second_scale
+    second_normed = (second_unit * ffn_gain_wide).astype(bf16)
+
+    grad_planes = gather_rows(cotangent)
+    row_planes = gather_rows(second_normed)
+    hiddens, gate_grads, up_grads, grad_sums, out_sums = [], [], [], [], []
+    for distance in range(RINGS):
+        results = [
+            mlp_rows(
+                row_planes[distance][side],
+                grad_planes[distance][side],
+                routed[distance, side],
+                index,
+                (units, shared, experts),
+                gate_weight,
+                up_weight,
+                down_weight,
+            )
+            for side in (0, 1)
+        ]
+        for side in (0, 1):
+            hiddens.append(results[side][0])
+            gate_grads.append(results[side][1])
+            up_grads.append(results[side][2])
+        out_sums.append(plane_sum(results[0][3], results[1][3]))
+        grad_sums.append(plane_sum(results[0][4], results[1][4]))
+    grad_second = ring_sum(grad_sums)
+    block_output = mixed + ring_sum(out_sums)
+
+    every_row = jnp.concatenate([plane for pair in row_planes for plane in pair], axis=0)
+    every_grad = jnp.concatenate([plane for pair in grad_planes for plane in pair], axis=0)
+    every_hidden = jnp.concatenate(hiddens, axis=0)
+    every_gate_grad = jnp.concatenate(gate_grads, axis=0)
+    every_up_grad = jnp.concatenate(up_grads, axis=0)
+    grad_expert_gate_up = jnp.stack(
+        [
+            dot_rows(every_row, every_gate_grad[:, :units]),
+            dot_rows(every_row, every_up_grad[:, :units]),
+        ]
+    )[None]
+    side_grads = dot_rows(
+        every_row, jnp.concatenate([every_gate_grad[:, units:], every_up_grad[:, units:]], axis=1)
+    )
+    spare_width = width - units
+    grad_router = side_grads[:, shared : shared + experts]
+    shared_in_grads = jnp.stack(
+        [side_grads[:, :shared], side_grads[:, spare_width : spare_width + shared]]
+    )
+    grad_expert_down = dot_rows(every_hidden[:, :units], every_grad)[None]
+    shared_down_grads = dot_rows(every_hidden[:, units:], every_grad)[:shared]
+    grad_shared_in = (
+        lax.all_to_all(
+            shared_in_grads.astype(bf16)
+            .reshape(2, blocks, depth, shared)
+            .transpose(1, 0, 2, 3)
+            .reshape(blocks, 2 * depth, shared),
+            "dp",
+            split_axis=0,
+            concat_axis=0,
+            tiled=True,
+        )
+        .astype(f32)
+        .reshape(blocks, 2, depth, shared)
+        .transpose(1, 2, 0, 3)
+        .reshape(2, depth, blocks * shared)
+    )
+    grad_shared_down = (
+        lax.all_to_all(
+            shared_down_grads.astype(bf16).reshape(shared, blocks, depth).transpose(1, 0, 2),
+            "dp",
+            split_axis=0,
+            concat_axis=0,
+            tiled=True,
+        )
+        .astype(f32)
+        .reshape(blocks * shared, depth)
+    )
+
+    gain_ffn_part = jnp.sum(grad_second * second_unit, axis=0)
+    grad_mixed = cotangent.astype(f32) + rms_back(
+        grad_second * ffn_gain_wide, second_unit, second_scale
+    )
+    grad_mixed_low = grad_mixed.astype(bf16)
+    grad_attn = both_halves(grad_mixed_low, other_x(grad_mixed_low))
+
+    keys = weight_keys()
+    places = [place_of(coords, key) for key in keys]
+
+    def in_key_order(values):
+        return jnp.concatenate(
+            [lax.dynamic_slice_in_dim(values, place * depth, depth, 1) for place in places], axis=1
+        )
+
+    grad_output_weight = scatter_weight(
+        dot_rows(in_key_order(grad_attn), attended).astype(bf16)
+    ).T
+    grad_attended = (
+        wide_dot(grad_attn, output_turned).astype(bf16).reshape(tokens, heads, VD)
+    )
+    scores = attention_scores(query_rows, key_nope, key_rope, allowed, scale)
+    weights = jnp.exp(scores - log_total)
+    weights_low = weights.astype(bf16)
+    grad_weights = jnp.einsum("ihd,jhd->hij", grad_attended, values, preferred_element_type=f32)
+    grad_values = jnp.einsum("hij,ihd->jhd", weights_low, grad_attended, preferred_element_type=f32)
+    grad_scores = (
+        weights * (grad_weights - jnp.sum(weights * grad_weights, axis=-1, keepdims=True))
+    ).astype(bf16)
+    grad_query_nope = scale * jnp.einsum(
+        "hij,jhd->ihd", grad_scores, key_nope, preferred_element_type=f32
+    )
+    grad_query_rope = scale * jnp.einsum(
+        "hij,jd->ihd", grad_scores, key_rope, preferred_element_type=f32
+    )
+    grad_key_nope = scale * jnp.einsum(
+        "hij,ihd->jhd", grad_scores, query_rows[..., :NOPE], preferred_element_type=f32
+    )
+    grad_key_rope = scale * jnp.einsum(
+        "hij,ihd->jd", grad_scores, query_rows[..., NOPE:], preferred_element_type=f32
+    )
+    grad_query = (
+        jnp.concatenate(
+            [grad_query_nope, rotate_back(grad_query_rope, cosine[:, None, :], sine[:, None, :])],
+            axis=-1,
+        )
+        .astype(bf16)
+        .reshape(tokens, heads * (NOPE + ROPE))
+    )
+    grad_keyval = (
+        jnp.concatenate([grad_key_nope, grad_values], axis=-1)
+        .astype(bf16)
+        .reshape(tokens, heads * (NOPE + VD))
+    )
+    key_order = jnp.stack(places)
+    latent_column = jnp.arange(KVR, dtype=jnp.int32)
+    wanted = key_order[latent_column // latent_depth] * latent_depth + latent_column % latent_depth
+    shuffle = (latent_column[:, None] == wanted[None, :]).astype(bf16)
+    latent_in_order = wide_dot(latent_normed, shuffle).astype(bf16)
+    grad_keyval_weight = scatter_weight(dot_rows(latent_in_order, grad_keyval).astype(bf16))
+    grad_latent_normed = dot_turned(grad_keyval, keyval_weight)
+    gain_latent_part = jnp.sum(grad_latent_normed * latent_unit, axis=0)
+    grad_latent = rms_back(grad_latent_normed * latent_gain_wide, latent_unit, latent_scale)
+    grad_latent_all = jnp.concatenate(
+        [grad_latent, rotate_back(grad_key_rope, cosine, sine)], axis=-1
+    ).astype(bf16)
+    grad_projected = jnp.concatenate([grad_query, grad_latent_all], axis=1)
+    grad_first_weight = scatter_weight(
+        dot_rows(in_key_order(first_normed), grad_projected).astype(bf16)
+    )
+    grad_latent_part = grad_first_weight[:, query_width:]
+    grad_latent_weight = grad_latent_part + other_x(grad_latent_part)
+    grad_first_part = dot_turned(grad_projected, first_weight)
+    low_rows, high_rows = grad_first_part[:local_rows], grad_first_part[local_rows:]
+    sent_part = jnp.where(x == 0, high_rows, low_rows).astype(bf16)
+    grad_first = jnp.where(x == 0, low_rows, high_rows) + other_x(sent_part).astype(f32)
+    own_inputs = block_input.astype(f32)
+    own_scale = rms_scale(own_inputs)
+    own_unit = own_inputs * own_scale
+    gain_attn_part = jnp.sum(grad_first * own_unit, axis=0)
+    grad_input = grad_mixed + rms_back(grad_first * attn_gain_wide, own_unit, own_scale)
+
+    small_grads = jnp.concatenate(
+        [
+            gain_attn_part.reshape(blocks, 1, depth),
+            gain_ffn_part.reshape(blocks, 1, depth),
+            grad_router.reshape(blocks, experts, depth),
+            jnp.pad(
+                gain_latent_part.reshape(blocks, 1, latent_depth),
+                ((0, 0), (0, 0), (0, depth - latent_depth)),
+            ),
+        ],
+        axis=1,
+    )
+    small_grads = lax.dynamic_index_in_dim(
+        lax.psum(small_grads, ("dp", "tensor")), index, 0, keepdims=False
+    )
+    return (
+        block_output,
+        grad_input,
+        small_grads[0],
+        grad_first_weight[:, :query_width],
+        grad_latent_weight,
+        small_grads[2 + experts, :latent_depth],
+        grad_keyval_weight,
+        grad_output_weight,
+        small_grads[1],
+        small_grads[2 : 2 + experts].reshape(depth, experts),
+        grad_shared_in,
+        grad_shared_down,
+        grad_expert_gate_up,
+        grad_expert_down,
+    )
+
+
 def solution(mesh):
     in_specs = (
         P(("dp", "tensor"), None),
@@ -448,4 +1027,5 @@
         P("dp", None, None, "tensor"),
         P("dp", "tensor", None),
     )
+    body = gather_body if mesh.shape["dp"] == 16 else exchange_body
     return jax.shard_map(body, mesh=mesh, in_specs=in_specs, out_specs=out_specs, check_vma=False)

time: 2720 us -> 1650 us (0.61)
  waiting for transfers between devices: 1590 us -> 379 us
  Pallas kernels: 0 us -> 465 us
  blocking collectives: 363 us -> 27.8 us
  matrix products: 235 us -> 303 us
  starting transfers between devices: 182 us -> 146 us
  local copies, waits for them, and re-layouts: 216 us -> 188 us
    reduce_scatter x8 -> x0, waiting for transfers between devices: 695 us -> none  [the longest x1 165 us: body(): lax.psum_scatter(grad_shared_in, 'dp', scatter_dimension=1, tiled=True)]
    pallas_call x0 -> x2, Pallas kernels: none -> 465 us  [place_chunks(): pl.pallas_call(functools.partial(place_kernel, keys, moves), out_shape=[j...]
    all_to_all x4, waiting for transfers between devices: 461 us -> 0.01 us  [the longest x1 0.01 us: gather_body(): lax.all_to_all(shared_down.reshape(blocks, shared, depth), 'dp', split_ax...]
    all_gather x8 -> x0, waiting for transfers between devices: 356 us -> none  [the longest x1 211 us: body(): lax.all_gather(shared_down, 'dp', axis=1, tiled=True)]
    ppermute x0 -> x142, waiting for transfers between devices: none -> 266 us  [the longest x27 112 us: ring_step(): lax.ppermute(values, 'dp', [(i, (i + RINGS) % 16) for i in range(16)])]
    all_gather x3 -> x1, blocking collectives: 260 us -> 27.8 us  [gather_body(): small = lax.all_gather(small, 'dp', axis=0, tiled=True)]
    all_to_all x4, starting transfers between devices: 181 us -> 16.3 us  [the longest x1 4.29 us: gather_body(): lax.all_to_all(shared_in_grads.astype(bf16).reshape(2, blocks, depth, sha...]
    ppermute x0 -> x142, starting transfers between devices: none -> 129 us  [the longest x43 43.4 us: other_y(): return lax.ppermute(values, 'dp', [(i, i ^ 2) for i in range(16)])]
  transfers between devices with their start and end apart: 23 -> 147, of which waited for: 17 -> 45; matrix products, arithmetic and copies ran while one was open for 16% -> 25% of each run, Pallas kernels for 0% -> 28%
where the time goes in v1:
time: 1650 us; the launch traced here: 1640 us
  Pallas kernels  465 us (28%)
  waiting for transfers between devices  379 us (23%)
  matrix products  303 us (18%)
  local copies, waits for them, and re-layouts  188 us (11%)
  starting transfers between devices  146 us (9%)
  other arithmetic  113 us (7%)
  blocking collectives  27.8 us (2%)
  between operations  18.2 us (1%)
    pallas_call x2, Pallas kernels, place_chunks(): pl.pallas_call(functools.partial(place_kernel, keys, moves), out_shape=[j...  465 us
    psum x1, waiting for transfers between devices, gather_body(): lax.psum(small_grads, ('dp', 'tensor'))  113 us
    ppermute x27, waiting for transfers between devices, ring_step(): lax.ppermute(values, 'dp', [(i, (i + RINGS) % 16) for i in range(16)])  112 us
    dot_general x27, matrix products, wide_dot(): return jnp.dot(left, right, preferred_element_type=jnp.float32)  105 us
    ppermute x43, waiting for transfers between devices, other_y(): return lax.ppermute(values, 'dp', [(i, i ^ 2) for i in range(16)])  103 us
    dot_general x27, matrix products, dot_turned(): lax.dot_general(left, right, (((1,), (1,)), ((), ())), preferred_element_...  102 us
    unnamed x437, local copies, waits for them, and re-layouts  95.4 us
    dot_general x8, matrix products, dot_rows(): lax.dot_general(left, right, (((0,), (0,)), ((), ())), preferred_element_...  91.1 us
  transfers between devices with their start and end apart: 147, of which 45 were waited for; matrix products, arithmetic and copies ran while one was open for 25% of the time, Pallas kernels for 28%

profile of v1, /device:TPU:0, one launch (start us, length us, event | category | flops | bytes accessed | tf_op | source)
XLA Modules:
  0.0 1640.4 jit_solution(9900771589193516555)
XLA Ops:
  25.3 27.8 %all_gather.3 = bf16[2048,31]{0,1:T(8,128)(2,1)S(1)} all-gather(bf16[128,31]{0,1:T(8,128)(2,1)S(1)} %concatenate.170), channel_id=1, replica_groups=mesh['dp'=16,'tensor'=2] {'dp'}, dimensions={0}, use_global_device_ids=true | all-gather | bytes 134912 | tf_op jit(solution)/shard_map/all_gather | solution.py:673
  81.0 7.1 collective-permute-done.78
  91.6 8.1 collective-permute-done.4
  105.9 9.7 collective-permute-done.116
  122.3 10.2 collective-permute-done.90
  150.8 19.1 %collective-permute-done.27.refs_12_ = bf16[128,1536]{1,0:T(8,128)(2,1)S(1)} collective-permute-done((bf16[128,1536]{1,0:T(8,128)(2,1)}, bf16[128,1536]{1,0:T(8,128)(2,1)S(1)}, u32[]{:S(2)}, u32[]{:S(2)}) %collective-permute-start.27) | collective-permute-done | bytes 393248 | tf_op jit(solution)/shard_map/ppermute | solution.py:426
  188.1 7.1 collective-permute-done.29.refs_14_
  223.1 6.3 maximum_maximum_fusion
  241.1 193.1 %shard_map.273 = (bf16[512,2048]{1,0:T(8,128)(2,1)}, bf16[2048,1024]{1,0:T(8,128)(2,1)}) custom-call(s32[3]{0:T(128)} %pad_add_fusion.coords_ref, bf16[128,1536]{1,0:T(8,128)(2,1)} %pad_maximum_fusion.23.refs_0_, bf16[128,1536]{1,0:T(8,128)(2,1)} %collective-permute-done.16.refs_1_, bf16[128,1536]{1,0:T(8,128)(2,1)} %collective-permute-done.17.refs_2_, ...), custom_call_target="tpu_custom_call" | custom-call | bytes 12582912 | tf_op jit(solution)/shard_map/pallas_call | solution.py:533
  449.9 272.0 %shard_map.272 = bf16[2048,2112]{1,0:T(8,128)(2,1)} custom-call(s32[3]{0:T(128)} %pad_add_fusion.coords_ref, bf16[128,2112]{1,0:T(8,128)(2,1)} %copy-done.19, bf16[128,2112]{1,0:T(8,128)(2,1)} %copy.236.refs_1_, bf16[128,2112]{1,0:T(8,128)(2,1)} %copy.237.refs_2_, bf16[128,2112]{1,0:T(8,128)(2,1)} %copy.238.refs_3_, bf16[128,2112]{1,0:T(8,128)(2,1)} %copy.239.refs_4_, ...), custom_call_target="tpu_custom_call" | custom-call | bytes 17301504 | tf_op jit(solution)/shard_map/pallas_call | solution.py:533
  721.9 7.2 fusion.176
  797.1 8.1 collective-permute-done.46
  904.3 6.0 constant_dynamic-update-slice_fusion.119
  922.4 6.2 constant_dynamic-update-slice_fusion.116
  946.4 10.3 fusion.22
  956.7 19.3 %fusion.6 = f32[1,704,2048]{2,1,0:T(8,128)} fusion(bf16[4096,2048]{1,0:T(8,128)(2,1)} %constant_dynamic-update-slice_fusion.120, bf16[4096,896]{1,0:T(8,128)(2,1)} %get-tuple-element.124), kind=kOutput, calls=%fused_computation.32 | convolution fusion | flops 11811160064 | bytes 28835840 | tf_op jit(solution)/shard_map/dot_general | solution.py:583
  991.2 7.6 fusion.27
  1036.2 20.2 %fusion.12 = f32[1,2048,704]{1,2,0:T(8,128)} fusion(bf16[4096,2048]{1,0:T(8,128)(2,1)} %constant_dynamic-update-slice_fusion.40, bf16[4096,896]{1,0:T(8,128)(2,1)} %get-tuple-element.156), kind=kOutput, calls=%fused_computation.34 | convolution fusion | flops 11811160064 | bytes 28835840 | tf_op jit(solution)/shard_map/dot_general | solution.py:583
  1058.8 17.5 %fusion.9 = f32[1,2048,704]{1,2,0:T(8,128)} fusion(bf16[4096,2048]{1,0:T(8,128)(2,1)} %constant_dynamic-update-slice_fusion.40, bf16[4096,896]{1,0:T(8,128)(2,1)S(1)} %bitcast.309), kind=kOutput, calls=%fused_computation.33 | convolution fusion | flops 11811160064 | bytes 28835840 | tf_op jit(solution)/shard_map/dot_general | solution.py:583
  1127.4 8.7 maximum_bitcast_fusion
  1136.1 15.1 fusion.175
  1234.9 25.9 %collective-permute-done.88 = bf16[128,2048]{1,0:T(8,128)(2,1)S(1)} collective-permute-done((bf16[128,2048]{1,0:T(8,128)(2,1)S(1)}, bf16[128,2048]{1,0:T(8,128)(2,1)S(1)}, u32[]{:S(2)}, u32[]{:S(2)}) %collective-permute-start.88) | collective-permute-done | bytes 524320 | tf_op jit(solution)/shard_map/ppermute | solution.py:430
  1265.7 8.3 collective-permute-done.100
  1275.5 8.6 collective-permute-done.98
  1290.4 16.0 collective-permute-done.112
  1319.8 9.4 collective-permute-done.123
  1332.6 8.3 collective-permute-done.67
  1426.7 113.2 %all-reduce.12.cloned.1.call-done = f32[16,19,128]{2,1,0:T(8,128)} async-done(((f32[16,19,128]{2,1,0:T(8,128)}), f32[16,19,128]{2,1,0:T(8,128)}) %all-reduce.12.cloned.1.call-update) | async-done | bytes 155664 | tf_op jit(solution)/shard_map/psum | solution.py:974
  1564.3 17.2 %collective-permute-done.138 = bf16[512,1024]{1,0:T(8,128)(2,1)S(1)} collective-permute-done((bf16[512,1024]{1,0:T(8,128)(2,1)S(1)}, bf16[512,1024]{1,0:T(8,128)(2,1)S(1)}, u32[]{:S(2)}, u32[]{:S(2)}) %collective-permute-start.138) | collective-permute-done | bytes 1048608 | tf_op jit(solution)/shard_map/ppermute | solution.py:430
  1586.6 6.4 collective-permute-done.139
  1593.4 11.2 collective-permute-done.129
  1613.4 11.2 collective-permute-done.130
  (1043 shorter events, 699.8 us)
Async XLA Ops:
  10.1 69.4 %collective-permute-start.19 = (bf16[128,1536]{1,0:T(8,128)(2,1)}, bf16[128,1536]{1,0:T(8,128)(2,1)}, u32[]{:S(2)}, u32[]{:S(2)}) collective-permute-start(bf16[128,1536]{1,0:T(8,128)(2,1)} %pad_maximum_fusion.23.refs_0_), channel_id=1, source_target_pairs={{0,8},{2,10},{4,12},{6,14},{8,16},{10,18},{12,20},{14,22},{16,24},... | collective-permute-start | bytes 1179656 | tf_op jit(solution)/shard_map/ppermute | solution.py:426
  13.1 66.4 %collective-permute-start.17 = (bf16[128,1536]{1,0:T(8,128)(2,1)}, bf16[128,1536]{1,0:T(8,128)(2,1)}, u32[]{:S(2)}, u32[]{:S(2)}) collective-permute-start(bf16[128,1536]{1,0:T(8,128)(2,1)} %pad_maximum_fusion.23.refs_0_), channel_id=1, source_target_pairs={{0,4},{2,6},{4,0},{6,2},{8,12},{10,14},{12,8},{14,10},{16,20},{18,... | collective-permute-start | bytes 1179656 | tf_op jit(solution)/shard_map/ppermute | solution.py:430
  14.6 65.0 %collective-permute-start.16 = (bf16[128,1536]{1,0:T(8,128)(2,1)}, bf16[128,1536]{1,0:T(8,128)(2,1)}, u32[]{:S(2)}, u32[]{:S(2)}) collective-permute-start(bf16[128,1536]{1,0:T(8,128)(2,1)} %pad_maximum_fusion.23.refs_0_), channel_id=1, source_target_pairs={{0,2},{2,0},{4,6},{6,4},{8,10},{10,8},{12,14},{14,12},{16,18},{18,... | collective-permute-start | bytes 1179656 | tf_op jit(solution)/shard_map/ppermute | solution.py:434
  14.6 125.4 %all-to-all-start.1 = ((bf16[16,88,128]{2,1,0:T(8,128)(2,1)}), bf16[16,88,128]{2,1,0:T(8,128)(2,1)}, u32[]{:S(2)}, u32[]{:S(2)}) async-start(bf16[16,88,128]{2,1,0:T(8,128)(2,1)} %bitcast.314), calls=%async_computation.1 | async-start | bytes 720896 | tf_op jit(solution)/shard_map/all_to_all | solution.py:742
  18.9 52.4 %collective-permute-start = (bf16[128,2048]{1,0:T(8,128)(2,1)S(1)}, bf16[128,2048]{1,0:T(8,128)(2,1)}, u32[]{:S(2)}, u32[]{:S(2)}) collective-permute-start(bf16[128,2048]{1,0:T(8,128)(2,1)S(1)} %copy-done.13), channel_id=1, source_target_pairs={{0,1},{1,0},{2,3},{3,2},{4,5},{5,4},{6,7},{7,6},{8,9},{9,8},{10,11... | collective-permute-start | bytes 1572872 | tf_op jit(solution)/shard_map/ppermute | solution.py:438
  20.4 54.7 %collective-permute-start.114 = (bf16[128,2048]{1,0:T(8,128)(2,1)}, bf16[128,2048]{1,0:T(8,128)(2,1)}, u32[]{:S(2)}, u32[]{:S(2)}) collective-permute-start(bf16[128,2048]{1,0:T(8,128)(2,1)} %param.33), channel_id=1, source_target_pairs={{0,4},{2,6},{4,0},{6,2},{8,12},{10,14},{12,8},{14,10},{16,20},{18,... | collective-permute-start | bytes 1572872 | tf_op jit(solution)/shard_map/ppermute | solution.py:430
  140.1 75.3 %all-to-all-start = ((bf16[16,256,88]{1,2,0:T(8,128)(2,1)}), bf16[16,256,88]{1,2,0:T(8,128)(2,1)}, u32[]{:S(2)}, u32[]{:S(2)}) async-start(bf16[16,256,88]{1,2,0:T(8,128)(2,1)} %bitcast.299), calls=%async_computation | async-start | bytes 1441792 | tf_op jit(solution)/shard_map/all_to_all | solution.py:733
  186.6 35.2 %collective-permute-start.10 = (bf16[128,2112]{0,1:T(8,128)(2,1)}, bf16[128,2112]{0,1:T(8,128)(2,1)}, u32[]{:S(2)}, u32[]{:S(2)}) collective-permute-start(bf16[128,2112]{0,1:T(8,128)(2,1)} %collective-permute-done.8), channel_id=1, source_target_pairs={{0,4},{2,6},{4,0},{6,2},{8,12},{10,14},{12,8},{14,10},{16,20},{18,... | collective-permute-start | bytes 1622024 | tf_op jit(solution)/shard_map/ppermute | solution.py:430
  221.8 212.3 %collective-permute-start.104 = (bf16[128,2048]{1,0:T(8,128)(2,1)}, bf16[128,2048]{1,0:T(8,128)(2,1)}, u32[]{:S(2)}, u32[]{:S(2)}) collective-permute-start(bf16[128,2048]{1,0:T(8,128)(2,1)} %collective-permute-done.102), channel_id=1, source_target_pairs={{0,1},{1,0},{2,3},{3,2},{4,5},{5,4},{6,7},{7,6},{8,9},{9,8},{10,11... | collective-permute-start | bytes 1572872 | tf_op jit(solution)/shard_map/ppermute | solution.py:438
  222.4 213.9 %collective-permute-start.103 = (bf16[128,2048]{1,0:T(8,128)(2,1)}, bf16[128,2048]{1,0:T(8,128)(2,1)}, u32[]{:S(2)}, u32[]{:S(2)}) collective-permute-start(bf16[128,2048]{1,0:T(8,128)(2,1)} %collective-permute-done.102), channel_id=1, source_target_pairs={{0,4},{2,6},{4,0},{6,2},{8,12},{10,14},{12,8},{14,10},{16,20},{18,... | collective-permute-start | bytes 1572872 | tf_op jit(solution)/shard_map/ppermute | solution.py:430
  222.5 219.5 %collective-permute-start.13 = (bf16[128,2112]{0,1:T(8,128)(2,1)}, bf16[128,2112]{0,1:T(8,128)(2,1)}, u32[]{:S(2)}, u32[]{:S(2)}) collective-permute-start(bf16[128,2112]{0,1:T(8,128)(2,1)} %collective-permute-done.12), channel_id=1, source_target_pairs={{0,2},{2,0},{4,6},{6,4},{8,10},{10,8},{12,14},{14,12},{16,18},{18,... | collective-permute-start | bytes 1622024 | tf_op jit(solution)/shard_map/ppermute | solution.py:434
  222.5 223.1 %collective-permute-start.11 = (bf16[128,2112]{0,1:T(8,128)(2,1)}, bf16[128,2112]{0,1:T(8,128)(2,1)}, u32[]{:S(2)}, u32[]{:S(2)}) collective-permute-start(bf16[128,2112]{0,1:T(8,128)(2,1)} %collective-permute-done.10), channel_id=1, source_target_pairs={{0,2},{2,0},{4,6},{6,4},{8,10},{10,8},{12,14},{14,12},{16,18},{18,... | collective-permute-start | bytes 1622024 | tf_op jit(solution)/shard_map/ppermute | solution.py:434
  223.0 224.7 %collective-permute-start.15 = (bf16[128,2112]{0,1:T(8,128)(2,1)}, bf16[128,2112]{0,1:T(8,128)(2,1)}, u32[]{:S(2)}, u32[]{:S(2)}) collective-permute-start(bf16[128,2112]{0,1:T(8,128)(2,1)} %collective-permute-done.14), channel_id=1, source_target_pairs={{0,2},{2,0},{4,6},{6,4},{8,10},{10,8},{12,14},{14,12},{16,18},{18,... | collective-permute-start | bytes 1622024 | tf_op jit(solution)/shard_map/ppermute | solution.py:434
  434.2 309.3 %collective-permute-start.118 = (bf16[512,2048]{1,0:T(8,128)(2,1)}, bf16[512,2048]{1,0:T(8,128)(2,1)}, u32[]{:S(2)}, u32[]{:S(2)}) collective-permute-start(bf16[512,2048]{1,0:T(8,128)(2,1)} %get-tuple-element.322), channel_id=1, source_target_pairs={{0,2},{2,0},{4,6},{6,4},{8,10},{10,8},{12,14},{14,12},{16,18},{18,... | collective-permute-start | bytes 6291464 | tf_op jit(solution)/shard_map/ppermute | solution.py:434
  436.3 316.1 %collective-permute-start.81 = (bf16[64,2048]{1,0:T(8,128)(2,1)}, bf16[64,2048]{1,0:T(8,128)(2,1)}, u32[]{:S(2)}, u32[]{:S(2)}) collective-permute-start(bf16[64,2048]{1,0:T(8,128)(2,1)} %slice.781), channel_id=1, source_target_pairs={{0,4},{2,6},{4,0},{6,2},{8,12},{10,14},{12,8},{14,10},{16,20},{18,... | collective-permute-start | bytes 786440 | tf_op jit(solution)/shard_map/ppermute | solution.py:430
  442.0 312.1 %collective-permute-start.82 = (bf16[64,2048]{1,0:T(8,128)(2,1)}, bf16[64,2048]{1,0:T(8,128)(2,1)}, u32[]{:S(2)}, u32[]{:S(2)}) collective-permute-start(bf16[64,2048]{1,0:T(8,128)(2,1)} %slice.782), channel_id=1, source_target_pairs={{0,1},{1,0},{2,3},{3,2},{4,5},{5,4},{6,7},{7,6},{8,9},{9,8},{10,11... | collective-permute-start | bytes 786440 | tf_op jit(solution)/shard_map/ppermute | solution.py:438
  755.8 50.6 %collective-permute-start.83 = (bf16[512,2048]{1,0:T(8,128)(2,1)S(1)}, bf16[512,2048]{1,0:T(8,128)(2,1)S(1)}, u32[]{:S(2)}, u32[]{:S(2)}) collective-permute-start(bf16[512,2048]{1,0:T(8,128)(2,1)S(1)} %get-tuple-element.318), channel_id=1, source_target_pairs={{0,2},{2,0},{4,6},{6,4},{8,10},{10,8},{12,14},{14,12},{16,18},{18,... | collective-permute-start | bytes 6291464 | tf_op jit(solution)/shard_map/ppermute | solution.py:434
  805.2 57.3 %collective-permute-start.105 = (bf16[64,2048]{1,0:T(8,128)(2,1)S(1)}, bf16[64,2048]{1,0:T(8,128)(2,1)S(1)}, u32[]{:S(2)}, u32[]{:S(2)}) collective-permute-start(bf16[64,2048]{1,0:T(8,128)(2,1)S(1)} %copy-done.122), channel_id=1, source_target_pairs={{0,4},{2,6},{4,0},{6,2},{8,12},{10,14},{12,8},{14,10},{16,20},{18,... | collective-permute-start | bytes 786440 | tf_op jit(solution)/shard_map/ppermute | solution.py:430
  816.2 47.3 %collective-permute-start.106 = (bf16[64,2048]{1,0:T(8,128)(2,1)S(1)}, bf16[64,2048]{1,0:T(8,128)(2,1)S(1)}, u32[]{:S(2)}, u32[]{:S(2)}) collective-permute-start(bf16[64,2048]{1,0:T(8,128)(2,1)S(1)} %copy-done.121), channel_id=1, source_target_pairs={{0,1},{1,0},{2,3},{3,2},{4,5},{5,4},{6,7},{7,6},{8,9},{9,8},{10,11... | collective-permute-start | bytes 786440 | tf_op jit(solution)/shard_map/ppermute | solution.py:438
  1076.3 74.9 %collective-permute-start.73 = (bf16[512,2048]{1,0:T(8,128)(2,1)}, bf16[512,2048]{1,0:T(8,128)(2,1)}, u32[]{:S(2)}, u32[]{:S(2)}) collective-permute-start(bf16[512,2048]{1,0:T(8,128)(2,1)} %convolution_convert_fusion.3), channel_id=1, source_target_pairs={{0,2},{2,0},{4,6},{6,4},{8,10},{10,8},{12,14},{14,12},{16,18},{18,... | collective-permute-start | bytes 6291464 | tf_op jit(solution)/shard_map/ppermute | solution.py:434
  1076.6 79.0 %collective-permute-start.38 = (bf16[512,2048]{1,0:T(8,128)(2,1)}, bf16[512,2048]{1,0:T(8,128)(2,1)}, u32[]{:S(2)}, u32[]{:S(2)}) collective-permute-start(bf16[512,2048]{1,0:T(8,128)(2,1)} %convolution_convert_fusion.9), channel_id=1, source_target_pairs={{0,2},{2,0},{4,6},{6,4},{8,10},{10,8},{12,14},{14,12},{16,18},{18,... | collective-permute-start | bytes 6291464 | tf_op jit(solution)/shard_map/ppermute | solution.py:434
  1076.8 84.1 %collective-permute-start.50 = (bf16[512,2048]{1,0:T(8,128)(2,1)}, bf16[512,2048]{1,0:T(8,128)(2,1)}, u32[]{:S(2)}, u32[]{:S(2)}) collective-permute-start(bf16[512,2048]{1,0:T(8,128)(2,1)} %convolution_convert_fusion.7), channel_id=1, source_target_pairs={{0,2},{2,0},{4,6},{6,4},{8,10},{10,8},{12,14},{14,12},{16,18},{18,... | collective-permute-start | bytes 6291464 | tf_op jit(solution)/shard_map/ppermute | solution.py:434
  1077.1 89.1 %collective-permute-start.62 = (bf16[512,2048]{1,0:T(8,128)(2,1)}, bf16[512,2048]{1,0:T(8,128)(2,1)}, u32[]{:S(2)}, u32[]{:S(2)}) collective-permute-start(bf16[512,2048]{1,0:T(8,128)(2,1)} %convolution_convert_fusion.5), channel_id=1, source_target_pairs={{0,2},{2,0},{4,6},{6,4},{8,10},{10,8},{12,14},{14,12},{16,18},{18,... | collective-permute-start | bytes 6291464 | tf_op jit(solution)/shard_map/ppermute | solution.py:434
  1078.1 272.8 %all-to-all-start.3 = ((bf16[16,88,128]{2,1,0:T(8,128)(2,1)}), bf16[16,88,128]{2,1,0:T(8,128)(2,1)S(1)}, u32[]{:S(2)}, u32[]{:S(2)}) async-start(bf16[16,88,128]{2,1,0:T(8,128)(2,1)} %bitcast_bitcast_fusion), calls=%async_computation.3 | async-start | bytes 720896 | tf_op jit(solution)/shard_map/all_to_all | solution.py:868
  1090.5 81.4 %collective-permute-start.108 = (bf16[512,2048]{1,0:T(8,128)(2,1)}, bf16[512,2048]{1,0:T(8,128)(2,1)}, u32[]{:S(2)}, u32[]{:S(2)}) collective-permute-start(bf16[512,2048]{1,0:T(8,128)(2,1)} %add_convert_fusion.6), channel_id=1, source_target_pairs={{0,2},{2,0},{4,6},{6,4},{8,10},{10,8},{12,14},{14,12},{16,18},{18,... | collective-permute-start | bytes 6291464 | tf_op jit(solution)/shard_map/ppermute | solution.py:434
  1222.2 40.8 %collective-permute-start.42 = (bf16[128,2048]{1,0:T(8,128)(2,1)S(1)}, bf16[128,2048]{1,0:T(8,128)(2,1)S(1)}, u32[]{:S(2)}, u32[]{:S(2)}) collective-permute-start(bf16[128,2048]{1,0:T(8,128)(2,1)S(1)} %pad_maximum_fusion.8), channel_id=1, source_target_pairs={{0,4},{2,6},{4,0},{6,2},{8,12},{10,14},{12,8},{14,10},{16,20},{18,... | collective-permute-start | bytes 1572872 | tf_op jit(solution)/shard_map/ppermute | solution.py:430
  1223.4 40.5 %collective-permute-start.40 = (bf16[128,2048]{1,0:T(8,128)(2,1)S(1)}, bf16[128,2048]{1,0:T(8,128)(2,1)S(1)}, u32[]{:S(2)}, u32[]{:S(2)}) collective-permute-start(bf16[128,2048]{1,0:T(8,128)(2,1)S(1)} %pad_maximum_fusion.7), channel_id=1, source_target_pairs={{0,1},{1,0},{2,3},{3,2},{4,5},{5,4},{6,7},{7,6},{8,9},{9,8},{10,11... | collective-permute-start | bytes 1572872 | tf_op jit(solution)/shard_map/ppermute | solution.py:438
  1227.8 58.6 %collective-permute-start.54 = (bf16[128,2048]{1,0:T(8,128)(2,1)S(1)}, bf16[128,2048]{1,0:T(8,128)(2,1)S(1)}, u32[]{:S(2)}, u32[]{:S(2)}) collective-permute-start(bf16[128,2048]{1,0:T(8,128)(2,1)S(1)} %pad_maximum_fusion.10), channel_id=1, source_target_pairs={{0,4},{2,6},{4,0},{6,2},{8,12},{10,14},{12,8},{14,10},{16,20},{18,... | collective-permute-start | bytes 1572872 | tf_op jit(solution)/shard_map/ppermute | solution.py:430
  1355.2 184.8 %all-reduce.12.cloned.1.call-start = ((), (), s32[]{:S(2)}) async-start(), calls=%async_computation.4 | async-start | bytes 393216 | tf_op jit(solution)/shard_map/psum | solution.py:974
  1404.7 139.2 %collective-permute-start.132 = (bf16[256,2048]{1,0:T(8,128)(2,1)}, bf16[256,2048]{1,0:T(8,128)(2,1)}, u32[]{:S(2)}, u32[]{:S(2)}) collective-permute-start(bf16[256,2048]{1,0:T(8,128)(2,1)} %slice.838), channel_id=1, source_target_pairs={{0,2},{2,0},{4,6},{6,4},{8,10},{10,8},{12,14},{14,12},{16,18},{18,... | collective-permute-start | bytes 3145736 | tf_op jit(solution)/shard_map/ppermute | solution.py:434
  1411.2 136.2 %collective-permute-start.137 = (bf16[1024,1024]{1,0:T(8,128)(2,1)}, bf16[1024,1024]{1,0:T(8,128)(2,1)}, u32[]{:S(2)}, u32[]{:S(2)}) collective-permute-start(bf16[1024,1024]{1,0:T(8,128)(2,1)} %slice.846), channel_id=1, source_target_pairs={{0,2},{2,0},{4,6},{6,4},{8,10},{10,8},{12,14},{14,12},{16,18},{18,... | collective-permute-start | bytes 6291464 | tf_op jit(solution)/shard_map/ppermute | solution.py:434
  1423.6 127.3 %collective-permute-start.127 = (bf16[512,2112]{0,1:T(8,128)(2,1)}, bf16[512,2112]{0,1:T(8,128)(2,1)}, u32[]{:S(2)}, u32[]{:S(2)}) collective-permute-start(bf16[512,2112]{0,1:T(8,128)(2,1)} %slice.829), channel_id=1, source_target_pairs={{0,4},{2,6},{4,0},{6,2},{8,12},{10,14},{12,8},{14,10},{16,20},{18,... | collective-permute-start | bytes 6488072 | tf_op jit(solution)/shard_map/ppermute | solution.py:430
  (296 other events, 4081.8 us)
Sparse Core Ops, SparseCore 0:
  1415.1 124.7 all-reduce.11

commit v2 on v1

--- a/solution.py
+++ b/solution.py
@@ -439,7 +439,6 @@
 
 
 def gather_rows(rows):
-    half = rows.shape[0] // 2
     planes = []
     current = rows
     for distance in range(RINGS):
@@ -447,10 +446,8 @@
             current = ring_step(current)
         beside = other_y(current)
         across = other_x(current)
-        plane = jnp.concatenate(
-            [current, beside, across, other_y(across[:half]), other_x(beside[half:])], axis=0
-        )
-        planes.append((plane, other_core(plane)))
+        corner = other_x(beside) if distance % 2 else other_y(across)
+        planes.append((current, beside, across, corner))
     return planes
 
 
@@ -458,26 +455,26 @@
     return (first.astype(jnp.float32) + second.astype(jnp.float32)).astype(jnp.bfloat16)
 
 
-def plane_sum(mine, theirs):
-    size = mine.shape[0] // 4
-    half = size // 2
-    total = add_low(mine, other_core(theirs))
-    own, beside, across = total[:size], total[size : 2 * size], total[2 * size : 3 * size]
-    corner_y = other_y(total[3 * size : 3 * size + half])
-    corner_x = other_x(total[3 * size + half :])
-    across = jnp.concatenate([add_low(across[:half], corner_y), across[half:]], axis=0)
-    beside = jnp.concatenate([beside[:half], add_low(beside[half:], corner_x)], axis=0)
-    return (
-        own.astype(jnp.float32)
-        + other_x(across).astype(jnp.float32)
-        + other_y(beside).astype(jnp.float32)
-    )
-
-
-def ring_sum(parts):
+def scatter_rows(planes):
+    moving = None
+    for distance in (1, 2, 3, 0):
+        own, beside, across, corner = planes[distance]
+        if distance % 2:
+            beside = add_low(beside, other_x(corner))
+        else:
+            across = add_low(across, other_y(corner))
+        total = own.astype(jnp.float32)
+        total = total + other_x(across).astype(jnp.float32) + other_y(beside).astype(jnp.float32)
+        if moving is not None:
+            total = total + ring_step(moving).astype(jnp.float32)
+        moving = total.astype(jnp.bfloat16)
+    return total
+
+
+def ring_sum(parts, low):
     moving = parts[1]
     for distance in (2, 3, 0):
-        moving = ring_step(moving.astype(jnp.bfloat16)).astype(jnp.float32) + parts[distance]
+        moving = ring_step(moving.astype(low)).astype(jnp.float32) + parts[distance]
     return moving
 
 
@@ -534,8 +531,9 @@
         functools.partial(place_kernel, keys, moves),
         out_shape=[jax.ShapeDtypeStruct(shape, jnp.bfloat16) for shape in shapes],
         in_specs=[pl.BlockSpec(memory_space=pltpu.SMEM)] + [anywhere] * len(chunks),
-        out_specs=[anywhere] * len(shapes),
+        out_specs=[pl.BlockSpec(memory_space=pltpu.VMEM)] * len(shapes),
         scratch_shapes=[pltpu.SemaphoreType.DMA((len(chunks) * len(moves),))],
+        compiler_params=pltpu.CompilerParams(vmem_limit_bytes=24 * 1024 * 1024),
         cost_estimate=pl.CostEstimate(
             flops=0,
             bytes_accessed=4 * sum(shape[0] * shape[1] for shape in shapes),
@@ -553,13 +551,21 @@
     ]
 
 
-def scatter_weight(grads):
+def scatter_blocks(grads, low):
     half = grads.shape[0] // 2
-    total = add_low(grads[:half], other_core(grads[half:]))
+    total = grads[:half].astype(jnp.float32) + other_core(grads[half:].astype(low)).astype(
+        jnp.float32
+    )
     quarter = half // 2
-    total = total[:quarter].astype(jnp.float32) + other_y(total[quarter:]).astype(jnp.float32)
+    total = total[:quarter] + other_y(total[quarter:].astype(low)).astype(jnp.float32)
     size = quarter // RINGS
-    return ring_sum([total[r * size : (r + 1) * size] for r in range(RINGS)])
+    return ring_sum([total[r * size : (r + 1) * size] for r in range(RINGS)], low)
+
+
+def pick_blocks(values, order):
+    chosen = order[:, None] == jnp.arange(values.shape[0], dtype=jnp.int32)[None, :]
+    chosen = chosen.reshape(chosen.shape + (1,) * (values.ndim - 1))
+    return jnp.sum(jnp.where(chosen, values[None], 0.0), axis=1)
 
 
 def attend_forward(query_rows, key_nope, key_rope, values, allowed, scale):
@@ -583,38 +589,147 @@
     return lax.dot_general(left, right, (((0,), (0,)), ((), ())), preferred_element_type=jnp.float32)
 
 
-def mlp_rows(rows, grad_rows, routed, expert, sizes, gate_weight, up_weight, down_weight):
-    units, shared, experts = sizes
-    width = gate_weight.shape[1]
-    pre_gate = wide_dot(rows, gate_weight)
-    pre_up = wide_dot(rows, up_weight)
-    down_grad = dot_turned(grad_rows, down_weight)
-    column = lax.broadcasted_iota(jnp.int32, (1, width), 1)
-    logits = pre_gate[:, units + shared : units + shared + experts]
-    probabilities = jax.nn.softmax(logits, axis=-1)
-    mine = lax.broadcasted_iota(jnp.int32, (1, experts), 1) == expert
-    gate = routed[:, None] * jnp.sum(jnp.where(mine, probabilities, 0.0), axis=1, keepdims=True)
-    sigmoid = jax.nn.sigmoid(pre_gate)
-    hidden = (pre_gate * sigmoid * pre_up).astype(jnp.bfloat16).astype(jnp.float32)
-    scale = jnp.where(column < units, gate, jnp.where(column < units + shared, 1.0, 0.0))
-    scaled_hidden = (scale * hidden).astype(jnp.bfloat16)
-    grad_gate_value = jnp.sum(
-        jnp.where(column < units, hidden * down_grad, 0.0), axis=1, keepdims=True
-    )
-    grad_hidden = scale * down_grad
-    grad_gate = grad_hidden * pre_up * sigmoid * (1.0 + pre_gate * (1.0 - sigmoid))
-    grad_up = (grad_hidden * pre_gate * sigmoid).astype(jnp.bfloat16)
-    grad_logits = (gate * grad_gate_value) * (jnp.where(mine, 1.0, 0.0) - probabilities)
-    grad_logits = jnp.pad(
-        grad_logits, ((0, 0), (units + shared, width - units - shared - experts))
-    )
-    router_column = (column >= units + shared) & (column < units + shared + experts)
-    grad_gate = jnp.where(router_column, grad_logits, grad_gate).astype(jnp.bfloat16)
-    out = wide_dot(scaled_hidden, down_weight).astype(jnp.bfloat16)
-    grad_input = (dot_turned(grad_gate, gate_weight) + dot_turned(grad_up, up_weight)).astype(
-        jnp.bfloat16
-    )
-    return scaled_hidden, grad_gate, grad_up, out, grad_input
+TILE = 256
+
+
+def mlp_kernel(tiles, steps, pieces, *refs):
+    experts_ref, routed_ref = refs[:2]
+    row_refs = refs[2 : 2 + pieces]
+    cot_refs = refs[2 + pieces : 2 + 2 * pieces]
+    router_ref, gate_col, up_col, down_row, gate_row, up_row, down_col = refs[
+        2 + 2 * pieces : 9 + 2 * pieces
+    ]
+    outs = refs[9 + 2 * pieces + 6 :]
+    grad_refs, out_refs = outs[:pieces], outs[pieces : 2 * pieces]
+    rows_out, cots_out, hidden_out, gate_out, up_out, logit_out = outs[2 * pieces : 2 * pieces + 6]
+    hidden_all, gate_all, up_all, prob_ref, scale_ref, sum_ref = outs[2 * pieces + 6 :]
+    step = pl.program_id(0)
+    third = tiles // 2
+    size = row_refs[0].shape[0]
+    lane = lax.broadcasted_iota(jnp.int32, (1, router_ref.shape[1]), 1)
+
+    @pl.when(step == 0)
+    def _():
+        for k in range(pieces):
+            rows_out[k * size : (k + 1) * size, :] = row_refs[k][...]
+            cots_out[k * size : (k + 1) * size, :] = cot_refs[k][...]
+        logits = wide_dot(rows_out[...], router_ref[...])
+        logits = jnp.where(lane < experts_ref[2], logits, -1e30)
+        raised = jnp.exp(logits - jnp.max(logits, axis=1, keepdims=True))
+        chances = raised / jnp.sum(raised, axis=1, keepdims=True)
+        prob_ref[...] = chances
+        for k in (0, 1):
+            chance = jnp.sum(jnp.where(lane == experts_ref[k], chances, 0.0), axis=1, keepdims=True)
+            scale_ref[k] = routed_ref[:, k : k + 1] * chance
+        scale_ref[2] = jnp.ones_like(scale_ref[2])
+        sum_ref[...] = jnp.zeros_like(sum_ref)
+
+    @pl.when(step < tiles)
+    def _():
+        pre_gate = wide_dot(rows_out[...], gate_col[...])
+        pre_up = wide_dot(rows_out[...], up_col[...])
+        down_grad = dot_turned(cots_out[...], down_row[...])
+        part = step // third
+        scale = scale_ref[part]
+        sigmoid = 1.0 / (1.0 + jnp.exp(-pre_gate))
+        silu = pre_gate * sigmoid
+        hidden = (silu * pre_up).astype(jnp.bfloat16).astype(jnp.float32)
+        sum_ref[part] += jnp.sum(hidden * down_grad, axis=1, keepdims=True)
+        grad_hidden = scale * down_grad
+        columns = pl.ds(pl.multiple_of(step * TILE, TILE), TILE)
+        low_hidden = (scale * hidden).astype(jnp.bfloat16)
+        low_gate = (grad_hidden * pre_up * (sigmoid + silu * (1.0 - sigmoid))).astype(jnp.bfloat16)
+        low_up = (grad_hidden * silu).astype(jnp.bfloat16)
+        hidden_all[:, columns] = low_hidden
+        gate_all[:, columns] = low_gate
+        up_all[:, columns] = low_up
+        hidden_out[...] = low_hidden
+        gate_out[...] = low_gate
+        up_out[...] = low_up
+
+    @pl.when(step == tiles - 1)
+    def _():
+        grad_logits = jnp.zeros_like(prob_ref)
+        for k in (0, 1):
+            own = jnp.where(lane == experts_ref[k], 1.0, 0.0)
+            grad_logits += scale_ref[k] * sum_ref[k] * (own - prob_ref[...])
+        logit_out[...] = grad_logits.astype(jnp.bfloat16)
+
+    @pl.when(step >= tiles)
+    def _():
+        some = pl.ds(pl.multiple_of((step - tiles) * TILE, TILE), TILE)
+        grads = dot_turned(gate_all[...], gate_row[...]) + dot_turned(up_all[...], up_row[...])
+        grads += dot_turned(logit_out[...], router_ref[some, :])
+        grads = grads.astype(jnp.bfloat16)
+        result = wide_dot(hidden_all[...], down_col[...]).astype(jnp.bfloat16)
+        for k in range(pieces):
+            grad_refs[k][...] = grads[k * size : (k + 1) * size]
+            out_refs[k][...] = result[k * size : (k + 1) * size]
+
+
+def mlp_plane(distance, experts, routed, rows, cots, router, gate, up, down, kept):
+    pieces = len(rows)
+    size, depth = rows[0].shape
+    width = gate.shape[1]
+    tiles, columns = width // TILE, depth // TILE
+    total = pieces * size
+
+    def whole(array):
+        return pl.BlockSpec(array.shape, lambda i: (0,) * array.ndim)
+
+    def early(i):
+        return jnp.minimum(i, tiles - 1)
+
+    def late(i):
+        return jnp.maximum(i - tiles, 0)
+
+    low = jnp.bfloat16
+    piece_spec = pl.BlockSpec((size, TILE), lambda i: (0, late(i)))
+    tile_spec = pl.BlockSpec((total, TILE), lambda i: (distance, early(i)))
+    kept_specs = [
+        pl.BlockSpec((total, depth), lambda i: (distance, 0)),
+        pl.BlockSpec((total, depth), lambda i: (distance, 0)),
+        tile_spec,
+        tile_spec,
+        tile_spec,
+        pl.BlockSpec((total, router.shape[1]), lambda i: (distance, 0)),
+    ]
+    first_kept = 9 + 2 * pieces
+    aliases = {first_kept + k: 2 * pieces + k for k in range(6)}
+    results = pl.pallas_call(
+        functools.partial(mlp_kernel, tiles, tiles + columns, pieces),
+        grid=(tiles + columns,),
+        in_specs=[pl.BlockSpec(memory_space=pltpu.SMEM), whole(routed)]
+        + [whole(piece) for piece in rows]
+        + [whole(piece) for piece in cots]
+        + [
+            whole(router),
+            pl.BlockSpec((depth, TILE), lambda i: (0, early(i))),
+            pl.BlockSpec((depth, TILE), lambda i: (0, early(i))),
+            pl.BlockSpec((TILE, depth), lambda i: (early(i), 0)),
+            pl.BlockSpec((TILE, width), lambda i: (late(i), 0)),
+            pl.BlockSpec((TILE, width), lambda i: (late(i), 0)),
+            pl.BlockSpec((width, TILE), lambda i: (0, late(i))),
+        ]
+        + [pl.BlockSpec(memory_space=pl.ANY)] * 6,
+        out_specs=[piece_spec] * (2 * pieces) + kept_specs,
+        out_shape=[jax.ShapeDtypeStruct((size, depth), low)] * (2 * pieces)
+        + [jax.ShapeDtypeStruct(array.shape, array.dtype) for array in kept],
+        scratch_shapes=[pltpu.VMEM((total, width), low)] * 3
+        + [
+            pltpu.VMEM((total, router.shape[1]), jnp.float32),
+            pltpu.VMEM((3, total, 1), jnp.float32),
+            pltpu.VMEM((3, total, 1), jnp.float32),
+        ],
+        input_output_aliases=aliases,
+        compiler_params=pltpu.CompilerParams(vmem_limit_bytes=60 * 1024 * 1024),
+        cost_estimate=pl.CostEstimate(
+            flops=2 * total * depth * width * 6,
+            bytes_accessed=2 * (6 * depth * width + 6 * total * depth + 3 * total * width),
+            transcendentals=total * width,
+        ),
+    )(experts, routed, *rows, *cots, router, gate, up, down, gate, up, down, *kept)
+    return results[:pieces], results[pieces : 2 * pieces], results[2 * pieces :]
 
 
 def gather_body(
@@ -651,7 +766,6 @@
     experts = w_router.shape[1]
     units = expert_gate_up.shape[3]
     shared = shared_gate_up.shape[2] // blocks
-    width = -(-(units + shared + experts) // 128) * 128
     latent_depth = w_keyval.shape[0]
     scale = (NOPE + ROPE) ** (-0.5)
 
@@ -670,40 +784,52 @@
         ],
         axis=1,
     )
-    small = lax.all_gather(small, "dp", axis=0, tiled=True)
+    rows_all = both_halves(block_input, other_x(block_input))
+    used = query_width + KVR + ROPE
+    first_width = -(-(used + small.shape[1]) // 128) * 128
+    first_chunks = gather_weight(
+        jnp.pad(
+            jnp.concatenate([w_query, w_latent, small], axis=1),
+            ((0, 0), (0, first_width - used - small.shape[1])),
+        )
+    )
+    parts = depth // latent_depth
+    keyval_part = w_keyval.shape[1] // parts
+    keyval_packed = (
+        w_keyval.reshape(latent_depth, parts, keyval_part).transpose(1, 0, 2).reshape(depth, -1)
+    )
+    second_chunks = gather_weight(jnp.concatenate([keyval_packed, w_output.T], axis=1))
+    (first_weight,) = place_chunks(
+        coords,
+        first_chunks,
+        [(pl.ds(0, depth), pl.ds(0, first_width), 0, depth, pl.ds(0, first_width))],
+        [(D, first_width)],
+    )
+    small = first_weight[:, used:]
     attn_gain_wide = small[:, 0].astype(f32)
     ffn_gain_wide = small[:, 1].astype(f32)
     router_weight = small[:, 2 : 2 + experts]
     latent_gain_wide = (
         small[:, 2 + experts].reshape(blocks, depth)[:, :latent_depth].reshape(-1).astype(f32)
     )
-    routes_all = small[:, 3 + experts :].reshape(blocks * tokens, TOP)
-    routed_all = jnp.any(routes_all == index.astype(bf16), axis=1).astype(f32)
+    routes_all = small[:, 3 + experts : 3 + experts + 2 * TOP].reshape(blocks * tokens, TOP)
+    chip_experts = jnp.stack([index, index + 1 - 2 * core])
+    routed_all = jnp.any(
+        routes_all[None] == chip_experts[:, None, None].astype(bf16), axis=2
+    ).astype(f32)
     order = jnp.stack(
         [
-            place_of(coords, (distance, flip_y, flip_core)) * 2 + (1 - x if flip_x else x)
+            place_of(coords, (distance, flip_y, 0)) * 2 + (1 - x if flip_x else x)
             for distance in range(RINGS)
-            for flip_core in (0, 1)
             for flip_x, flip_y in ((0, 0), (0, 1), (1, 0), (1, 1))
         ]
     )
-    routed = routed_all.reshape(blocks * 2, local_rows)[order].reshape(
-        RINGS, 2, 4 * local_rows
-    )
-
-    rows_all = both_halves(block_input, other_x(block_input))
-    first_chunks = gather_weight(jnp.concatenate([w_query, w_latent], axis=1))
-    parts = depth // latent_depth
-    keyval_part = w_keyval.shape[1] // parts
-    keyval_packed = (
-        w_keyval.reshape(latent_depth, parts, keyval_part).transpose(1, 0, 2).reshape(depth, -1)
-    )
-    second_chunks = gather_weight(jnp.concatenate([keyval_packed, w_output.T], axis=1))
-    (first_weight,) = place_chunks(
-        coords,
-        first_chunks,
-        [(pl.ds(0, depth), pl.ds(0, query_width + KVR + ROPE), 0, depth, pl.ds(0, query_width + KVR + ROPE))],
-        [(D, query_width + KVR + ROPE)],
+    routed = jnp.stack(
+        [
+            pick_blocks(one.reshape(blocks * 2, local_rows), order).reshape(RINGS, -1)
+            for one in routed_all
+        ],
+        axis=2,
     )
     keyval_weight, output_turned = place_chunks(
         coords,
@@ -746,29 +872,41 @@
         concat_axis=0,
         tiled=True,
     )
-    shared_gate = shared_in[:, 0].reshape(D, shared)
-    shared_up = shared_in[:, 1].reshape(D, shared)
-    spare = width - units - shared
-    gate_weight = jnp.concatenate(
-        [
-            expert_gate_up[0, 0],
-            shared_gate,
-            router_weight,
-            jnp.zeros((D, spare - experts), bf16),
-        ],
-        axis=1,
-    )
-    up_weight = jnp.concatenate(
-        [expert_gate_up[0, 1], shared_up, jnp.zeros((D, spare), bf16)], axis=1
-    )
+    shared_other = other_core(shared_in)
+    shared_out_other = other_core(shared_out)
+    expert_in_other = other_core(expert_gate_up[0])
+    expert_out_other = other_core(expert_down[0])
+    hole = -(-units // TILE) * TILE - units
+
+    def side_columns(k):
+        return jnp.concatenate(
+            [
+                expert_gate_up[0, k],
+                jnp.zeros((D, hole), bf16),
+                expert_in_other[k],
+                jnp.zeros((D, hole), bf16),
+                shared_in[:, k].reshape(D, shared),
+                shared_other[:, k].reshape(D, shared),
+                jnp.zeros((D, TILE - 2 * shared), bf16),
+            ],
+            axis=1,
+        )
+
+    gate_weight = side_columns(0)
+    up_weight = side_columns(1)
     down_weight = jnp.concatenate(
         [
             expert_down[0],
+            jnp.zeros((hole, D), bf16),
+            expert_out_other,
+            jnp.zeros((hole, D), bf16),
             shared_out.transpose(1, 0, 2).reshape(shared, D),
-            jnp.zeros((spare, D), bf16),
+            shared_out_other.transpose(1, 0, 2).reshape(shared, D),
+            jnp.zeros((TILE - 2 * shared, D), bf16),
         ],
         axis=0,
     )
+    router_wide = jnp.pad(router_weight, ((0, 0), (0, 128 - experts)))
 
     cosine, sine = rotary_tables(segments[0], ROPE)
     allowed = allowed_pairs(segments[0], counts[0])
@@ -783,7 +921,7 @@
         axis=-1,
     ).astype(bf16)
     latent = projected[:, query_width : query_width + KVR]
-    key_rope = rotate(projected[:, query_width + KVR :], cosine, sine).astype(bf16)
+    key_rope = rotate(projected[:, query_width + KVR : used], cosine, sine).astype(bf16)
     latent_scale = rms_scale(latent)
     latent_unit = latent * latent_scale
     latent_normed = (latent_unit * latent_gain_wide).astype(bf16)
@@ -803,51 +941,64 @@
 
     grad_planes = gather_rows(cotangent)
     row_planes = gather_rows(second_normed)
-    hiddens, gate_grads, up_grads, grad_sums, out_sums = [], [], [], [], []
+    width = gate_weight.shape[1]
+    total_rows = 16 * local_rows
+    kept = [
+        jnp.zeros((total_rows, columns), bf16)
+        for columns in (D, D, width, width, width, router_wide.shape[1])
+    ]
+    expert_ids = jnp.concatenate([chip_experts, jnp.array([experts], jnp.int32)])
+    grad_parts, out_parts = [], []
     for distance in range(RINGS):
-        results = [
-            mlp_rows(
-                row_planes[distance][side],
-                grad_planes[distance][side],
-                routed[distance, side],
-                index,
-                (units, shared, experts),
-                gate_weight,
-                up_weight,
-                down_weight,
-            )
-            for side in (0, 1)
-        ]
-        for side in (0, 1):
-            hiddens.append(results[side][0])
-            gate_grads.append(results[side][1])
-            up_grads.append(results[side][2])
-        out_sums.append(plane_sum(results[0][3], results[1][3]))
-        grad_sums.append(plane_sum(results[0][4], results[1][4]))
-    grad_second = ring_sum(grad_sums)
-    block_output = mixed + ring_sum(out_sums)
-
-    every_row = jnp.concatenate([plane for pair in row_planes for plane in pair], axis=0)
-    every_grad = jnp.concatenate([plane for pair in grad_planes for plane in pair], axis=0)
-    every_hidden = jnp.concatenate(hiddens, axis=0)
-    every_gate_grad = jnp.concatenate(gate_grads, axis=0)
-    every_up_grad = jnp.concatenate(up_grads, axis=0)
-    grad_expert_gate_up = jnp.stack(
-        [
-            dot_rows(every_row, every_gate_grad[:, :units]),
-            dot_rows(every_row, every_up_grad[:, :units]),
-        ]
+        grads, outs, kept = mlp_plane(
+            distance,
+            expert_ids,
+            routed[distance],
+            row_planes[distance],
+            grad_planes[distance],
+            router_wide,
+            gate_weight,
+            up_weight,
+            down_weight,
+            kept,
+        )
+        grad_parts.append(grads)
+        out_parts.append(outs)
+    grad_second = scatter_rows(grad_parts)
+    block_output = mixed + scatter_rows(out_parts)
+
+    every_row, every_grad, every_hidden, every_gate_grad, every_up_grad, logit_grads = kept
+    far = units + hole
+
+    def both_in(grads):
+        sent = other_core(dot_rows(every_row, grads[:, far : far + units]).astype(bf16))
+        return dot_rows(every_row, grads[:, :units]) + sent.astype(f32)
+
+    grad_expert_gate_up = jnp.stack([both_in(every_gate_grad), both_in(every_up_grad)])[None]
+    sent_down = other_core(dot_rows(every_hidden[:, far : far + units], every_grad).astype(bf16))
+    grad_expert_down = (
+        dot_rows(every_hidden[:, :units], every_grad) + sent_down.astype(f32)
     )[None]
     side_grads = dot_rows(
-        every_row, jnp.concatenate([every_gate_grad[:, units:], every_up_grad[:, units:]], axis=1)
-    )
-    spare_width = width - units
-    grad_router = side_grads[:, shared : shared + experts]
+        every_row,
+        jnp.concatenate(
+            [every_gate_grad[:, 2 * far :], every_up_grad[:, 2 * far :], logit_grads], axis=1
+        ),
+    )
+    grad_router = side_grads[:, 2 * TILE : 2 * TILE + experts]
     shared_in_grads = jnp.stack(
-        [side_grads[:, :shared], side_grads[:, spare_width : spare_width + shared]]
-    )
-    grad_expert_down = dot_rows(every_hidden[:, :units], every_grad)[None]
-    shared_down_grads = dot_rows(every_hidden[:, units:], every_grad)[:shared]
+        [
+            side_grads[:, k * TILE : k * TILE + shared]
+            + other_core(
+                side_grads[:, k * TILE + shared : k * TILE + 2 * shared].astype(bf16)
+            ).astype(f32)
+            for k in (0, 1)
+        ]
+    )
+    side_down = dot_rows(every_hidden[:, 2 * far :], every_grad)
+    shared_down_grads = side_down[:shared] + other_core(
+        side_down[shared : 2 * shared].astype(bf16)
+    ).astype(f32)
     grad_shared_in = (
         lax.all_to_all(
             shared_in_grads.astype(bf16)
@@ -891,8 +1042,8 @@
             [lax.dynamic_slice_in_dim(values, place * depth, depth, 1) for place in places], axis=1
         )
 
-    grad_output_weight = scatter_weight(
-        dot_rows(in_key_order(grad_attn), attended).astype(bf16)
+    grad_output_weight = scatter_blocks(
+        dot_rows(in_key_order(grad_attn), attended).astype(bf16), bf16
     ).T
     grad_attended = (
         wide_dot(grad_attn, output_turned).astype(bf16).reshape(tokens, heads, VD)
@@ -935,7 +1086,7 @@
     wanted = key_order[latent_column // latent_depth] * latent_depth + latent_column % latent_depth
     shuffle = (latent_column[:, None] == wanted[None, :]).astype(bf16)
     latent_in_order = wide_dot(latent_normed, shuffle).astype(bf16)
-    grad_keyval_weight = scatter_weight(dot_rows(latent_in_order, grad_keyval).astype(bf16))
+    grad_keyval_weight = scatter_blocks(dot_rows(latent_in_order, grad_keyval).astype(bf16), bf16)
     grad_latent_normed = dot_turned(grad_keyval, keyval_weight)
     gain_latent_part = jnp.sum(grad_latent_normed * latent_unit, axis=0)
     grad_latent = rms_back(grad_latent_normed * latent_gain_wide, latent_unit, latent_scale)
@@ -943,12 +1094,12 @@
         [grad_latent, rotate_back(grad_key_rope, cosine, sine)], axis=-1
     ).astype(bf16)
     grad_projected = jnp.concatenate([grad_query, grad_latent_all], axis=1)
-    grad_first_weight = scatter_weight(
-        dot_rows(in_key_order(first_normed), grad_projected).astype(bf16)
+    grad_first_weight = scatter_blocks(
+        dot_rows(in_key_order(first_normed), grad_projected).astype(bf16), bf16
     )
     grad_latent_part = grad_first_weight[:, query_width:]
     grad_latent_weight = grad_latent_part + other_x(grad_latent_part)
-    grad_first_part = dot_turned(grad_projected, first_weight)
+    grad_first_part = dot_turned(grad_projected, first_weight[:, :used])
     low_rows, high_rows = grad_first_part[:local_rows], grad_first_part[local_rows:]
     sent_part = jnp.where(x == 0, high_rows, low_rows).astype(bf16)
     grad_first = jnp.where(x == 0, low_rows, high_rows) + other_x(sent_part).astype(f32)
@@ -970,9 +1121,8 @@
         ],
         axis=1,
     )
-    small_grads = lax.dynamic_index_in_dim(
-        lax.psum(small_grads, ("dp", "tensor")), index, 0, keepdims=False
-    )
+    small_grads = scatter_blocks(pick_blocks(small_grads, key_order), f32)[0]
+    small_grads = small_grads + other_x(small_grads)
     return (
         block_output,
         grad_input,

time: 1650 us -> 986 us (0.60)
  Pallas kernels: 465 us -> 163 us
  matrix products: 303 us -> 97.4 us
  waiting for transfers between devices: 379 us -> 306 us
  other arithmetic: 113 us -> 77.5 us
  blocking collectives: 27.8 us -> 0 us
    pallas_call x2, Pallas kernels: 465 us -> 7.34 us  [place_chunks(): pl.pallas_call(functools.partial(place_kernel, keys, moves), out_shape=[j...]
    pallas_call x0 -> x4, Pallas kernels: none -> 155 us  [mlp_plane(): pl.pallas_call(functools.partial(mlp_kernel, tiles, tiles + columns, piec...]
    psum x1 -> x0, waiting for transfers between devices: 113 us -> none  [gather_body(): lax.psum(small_grads, ('dp', 'tensor'))]
    dot_general x27 -> x3, matrix products: 105 us -> 6.49 us  [wide_dot(): return jnp.dot(left, right, preferred_element_type=jnp.float32)]
    dot_general x27 -> x3, matrix products: 102 us -> 8.35 us  [dot_turned(): lax.dot_general(left, right, (((1,), (1,)), ((), ())), preferred_element_...]
    ppermute x43 -> x36, waiting for transfers between devices: 103 us -> 167 us  [other_y(): return lax.ppermute(values, 'dp', [(i, i ^ 2) for i in range(16)])]
    ppermute x15 -> x0, local copies, waits for them, and re-layouts: 31.4 us -> none  [the longest x8 16.8 us: other_core(): return lax.ppermute(values, 'dp', [(i, i ^ 1) for i in range(16)])]
    all_gather x1 -> x0, blocking collectives: 27.8 us -> none  [gather_body(): small = lax.all_gather(small, 'dp', axis=0, tiled=True)]
  transfers between devices with their start and end apart: 147 -> 130, of which waited for: 45 -> 46; matrix products, arithmetic and copies ran while one was open for 25% -> 31% of each run, Pallas kernels for 28% -> 17%
where the time goes in v2:
time: 986 us; the launch traced here: 974 us
  waiting for transfers between devices  306 us (31%)
  local copies, waits for them, and re-layouts  179 us (18%)
  Pallas kernels  163 us (17%)
  starting transfers between devices  147 us (15%)
  matrix products  97.4 us (10%)
  other arithmetic  77.5 us (8%)
    ppermute x36, waiting for transfers between devices, other_y(): return lax.ppermute(values, 'dp', [(i, i ^ 2) for i in range(16)])  167 us
    pallas_call x4, Pallas kernels, mlp_plane(): pl.pallas_call(functools.partial(mlp_kernel, tiles, tiles + columns, piec...  155 us
    ppermute x30, waiting for transfers between devices, ring_step(): lax.ppermute(values, 'dp', [(i, (i + RINGS) % 16) for i in range(16)])  97.8 us
    dot_general x11, matrix products, dot_rows(): lax.dot_general(left, right, (((0,), (0,)), ((), ())), preferred_element_...  77.1 us
    unnamed x357, local copies, waits for them, and re-layouts  71.3 us
    ppermute x30, starting transfers between devices, ring_step(): lax.ppermute(values, 'dp', [(i, (i + RINGS) % 16) for i in range(16)])  51 us
    ppermute x36, starting transfers between devices, other_y(): return lax.ppermute(values, 'dp', [(i, i ^ 2) for i in range(16)])  41.5 us
    ppermute x30, waiting for transfers between devices, other_x(): return lax.ppermute(values, 'tensor', [(0, 1), (1, 0)])  40.8 us
  transfers between devices with their start and end apart: 130, of which 46 were waited for; matrix products, arithmetic and copies ran while one was open for 31% of the time, Pallas kernels for 17%

profile of v2, /device:TPU:0, one launch (start us, length us, event | category | flops | bytes accessed | tf_op | source)
XLA Modules:
  0.0 974.5 jit_solution(10645709180826131897)
XLA Ops:
  37.5 9.3 collective-permute-done
  69.0 9.5 collective-permute-done.8.refs_8_
  109.9 13.0 %collective-permute-done.10.refs_10_ = bf16[128,2176]{1,0:T(8,128)(2,1)} collective-permute-done((bf16[128,2176]{1,0:T(8,128)(2,1)}, bf16[128,2176]{1,0:T(8,128)(2,1)}, u32[]{:S(2)}, u32[]{:S(2)}) %collective-permute-start.10) | collective-permute-done | bytes 557088 | tf_op jit(solution)/shard_map/ppermute | solution.py:430
  125.0 9.2 collective-permute-done.14.refs_14_
  216.3 12.0 %collective-permute-start.52 = (bf16[128,2048]{1,0:T(8,128)(2,1)}, bf16[128,2048]{1,0:T(8,128)(2,1)}, u32[]{:S(2)}, u32[]{:S(2)}) collective-permute-start(bf16[128,2048]{1,0:T(8,128)(2,1)} %collective-permute-done.51.refs_6_), channel_id=1, source_target_pairs={{0,8},{2,10},{4,12},{6,14},{8,16},{10,18},{12,20},{14,22},{16,24},... | collective-permute-start | bytes 1572872 | tf_op jit(solution)/shard_map/ppermute | solution.py:426
  231.1 10.4 %collective-permute-done.52.refs_6_ = bf16[128,2048]{1,0:T(8,128)(2,1)} collective-permute-done((bf16[128,2048]{1,0:T(8,128)(2,1)}, bf16[128,2048]{1,0:T(8,128)(2,1)}, u32[]{:S(2)}, u32[]{:S(2)}) %collective-permute-start.52) | collective-permute-done | bytes 524320 | tf_op jit(solution)/shard_map/ppermute | solution.py:426
  271.7 12.4 %concatenate.73.refs_11_.refs_14_ = bf16[2048,1792]{1,0:T(8,128)(2,1)} concatenate(bf16[2048,704]{1,0:T(8,128)(2,1)} %bitcast.219, bf16[2048,64]{1,0:T(8,128)(2,1)S(1)} %broadcast.322, bf16[2048,704]{1,0:T(8,128)(2,1)} %bitcast.221, bf16[2048,64]{1,0:T(8,128)(2,1)S(1)} %broadcast.322, bf16[2048,88]{1,0:T(8,128)(2,1)} %bitcast.239, bf16[2048,88]{1,0:T(8,128)(2,1)} %bitcast.241, ...), dimensions={1} | concatenate | bytes 14680064 | tf_op jit(solution)/shard_map/concatenate | solution.py:882
  284.1 12.3 %concatenate.74.refs_12_.refs_15_ = bf16[2048,1792]{1,0:T(8,128)(2,1)} concatenate(bf16[2048,704]{1,0:T(8,128)(2,1)} %bitcast.218, bf16[2048,64]{1,0:T(8,128)(2,1)S(1)} %broadcast.322, bf16[2048,704]{1,0:T(8,128)(2,1)} %bitcast.220, bf16[2048,64]{1,0:T(8,128)(2,1)S(1)} %broadcast.322, bf16[2048,88]{1,0:T(8,128)(2,1)S(1)} %bitcast.238, bf16[2048,88]{1,0:T(8,128)(2,1)S(1)} %bitcast.240, ...), dimensions={1} | concatenate | bytes 14680064 | tf_op jit(solution)/shard_map/concatenate | solution.py:882
  324.1 38.7 %shard_map.283 = (bf16[128,2048]{1,0:T(8,128)(2,1)}, bf16[128,2048]{1,0:T(8,128)(2,1)}, bf16[128,2048]{1,0:T(8,128)(2,1)}, bf16[128,2048]{1,0:T(8,128)(2,1)}, bf...) custom-call(s32[3]{0:T(128)} %pad_add_fusion.1.refs_0_, ...), custom_call_target="tpu_custom_call", output_to_operand_aliasing={{8}: (17, {}), {9}: (18, {}), {10}: (19, {}), {11}: (20, {}... | custom-call | flops 22548578304 | bytes 62128128 | tf_op jit(solution)/shard_map/pallas_call | solution.py:699
  368.0 38.7 %shard_map.284 = (bf16[128,2048]{1,0:T(8,128)(2,1)}, bf16[128,2048]{1,0:T(8,128)(2,1)}, bf16[128,2048]{1,0:T(8,128)(2,1)}, bf16[128,2048]{1,0:T(8,128)(2,1)}, bf...) custom-call(s32[3]{0:T(128)} %pad_add_fusion.1.refs_0_, ...), custom_call_target="tpu_custom_call", output_to_operand_aliasing={{8}: (17, {}), {9}: (18, {}), {10}: (19, {}), {11}: (20, {}... | custom-call | flops 22548578304 | bytes 62128128 | tf_op jit(solution)/shard_map/pallas_call | solution.py:699
  414.3 39.1 %shard_map.285 = (bf16[128,2048]{1,0:T(8,128)(2,1)}, bf16[128,2048]{1,0:T(8,128)(2,1)}, bf16[128,2048]{1,0:T(8,128)(2,1)}, bf16[128,2048]{1,0:T(8,128)(2,1)}, bf...) custom-call(s32[3]{0:T(128)} %pad_add_fusion.1.refs_0_, ...), custom_call_target="tpu_custom_call", output_to_operand_aliasing={{8}: (17, {}), {9}: (18, {}), {10}: (19, {}), {11}: (20, {}... | custom-call | flops 22548578304 | bytes 62128128 | tf_op jit(solution)/shard_map/pallas_call | solution.py:699
  454.3 38.8 %shard_map.286 = (bf16[128,2048]{1,0:T(8,128)(2,1)}, bf16[128,2048]{1,0:T(8,128)(2,1)}, bf16[128,2048]{1,0:T(8,128)(2,1)}, bf16[128,2048]{1,0:T(8,128)(2,1)}, bf...) custom-call(s32[3]{0:T(128)} %pad_add_fusion.1.refs_0_, ...), custom_call_target="tpu_custom_call", output_to_operand_aliasing={{8}: (17, {}), {9}: (18, {}), {10}: (19, {}), {11}: (20, {}... | custom-call | flops 22548578304 | bytes 62128128 | tf_op jit(solution)/shard_map/pallas_call | solution.py:699
  495.9 10.9 %convolution_convert_fusion.3 = bf16[2048,704]{0,1:T(8,128)(2,1)} fusion(bf16[2048,2048]{1,0:T(8,128)(2,1)} %get-tuple-element.124, bf16[2048,1792]{1,0:T(8,128)(2,1)} %get-tuple-element.126), kind=kOutput, calls=%fused_computation.13 | convolution fusion | flops 5907021824 | bytes 14417920 | tf_op jit(solution)/shard_map/dot_general | solution.py:589
  506.8 9.9 %convolution_convert_fusion.4 = bf16[2048,704]{0,1:T(8,128)(2,1)} fusion(bf16[2048,2048]{1,0:T(8,128)(2,1)S(1)} %bitcast.211, bf16[2048,1792]{1,0:T(8,128)(2,1)} %get-tuple-element.125), kind=kOutput, calls=%fused_computation.14 | convolution fusion | flops 5907021824 | bytes 14417920 | tf_op jit(solution)/shard_map/dot_general | solution.py:589
  516.7 7.6 fusion.119
  528.8 7.8 convolution_convert_fusion.2
  557.5 10.6 %collective-permute-done.87 = bf16[128,2048]{1,0:T(8,128)(2,1)} collective-permute-done((bf16[128,2048]{1,0:T(8,128)(2,1)}, bf16[128,2048]{1,0:T(8,128)(2,1)}, u32[]{:S(2)}, u32[]{:S(2)}) %collective-permute-start.87) | collective-permute-done | bytes 524320 | tf_op jit(solution)/shard_map/ppermute | solution.py:430
  570.8 8.5 collective-permute-done.81
  583.5 10.9 %collective-permute-done.72 = bf16[128,2048]{1,0:T(8,128)(2,1)S(1)} collective-permute-done((bf16[128,2048]{1,0:T(8,128)(2,1)}, bf16[128,2048]{1,0:T(8,128)(2,1)S(1)}, u32[]{:S(2)}, u32[]{:S(2)}) %collective-permute-start.72) | collective-permute-done | bytes 524320 | tf_op jit(solution)/shard_map/ppermute | solution.py:430
  595.9 8.1 collective-permute-done.42
  608.2 10.5 %collective-permute-done.92 = bf16[128,2048]{1,0:T(8,128)(2,1)S(1)} collective-permute-done((bf16[128,2048]{1,0:T(8,128)(2,1)S(1)}, bf16[128,2048]{1,0:T(8,128)(2,1)S(1)}, u32[]{:S(2)}, u32[]{:S(2)}) %collective-permute-start.92) | collective-permute-done | bytes 524320 | tf_op jit(solution)/shard_map/ppermute | solution.py:430
  622.2 7.8 collective-permute-done.77
  648.5 7.6 collective-permute-done.73
  725.2 12.2 %add_bitcast_fusion.1 = f32[1,2048,704]{1,2,0:T(8,128)} fusion(bf16[2048,704]{0,1:T(8,128)(2,1)} %collective-permute-done.124, bf16[2048,2048]{1,0:T(8,128)(2,1)} %get-tuple-element.124, bf16[2048,1792]{1,0:T(8,128)(2,1)} %get-tuple-element.126), kind=kOutput, calls=%fused_computation.6 | convolution fusion | flops 5908463616 | bytes 20185088 | tf_op jit(solution)/shard_map/dot_general | solution.py:589
  737.5 10.5 %add_bitcast_fusion.2 = f32[1,2048,704]{1,2,0:T(8,128)} fusion(bf16[2048,704]{0,1:T(8,128)(2,1)} %collective-permute-done.123, bf16[2048,2048]{1,0:T(8,128)(2,1)S(1)} %bitcast.213, bf16[2048,1792]{1,0:T(8,128)(2,1)} %get-tuple-element.125), kind=kOutput, calls=%fused_computation.7 | convolution fusion | flops 5908463616 | bytes 20185088 | tf_op jit(solution)/shard_map/dot_general | solution.py:589
  748.0 9.6 add_bitcast_fusion
  757.6 10.8 %maximum_bitcast_fusion = f32[1,2,2048,704]{2,3,1,0:T(8,128)} fusion(f32[1,2048,704]{1,2,0:T(8,128)} %add_bitcast_fusion.1, f32[1,2048,704]{1,2,0:T(8,128)} %add_bitcast_fusion.2), kind=kLoop, calls=%fused_computation | loop fusion | flops 2883584 | bytes 23068672 | tf_op jit(solution)/shard_map/broadcast_in_dim | solution.py:977
  854.5 36.4 %collective-permute-done.105 = bf16[512,2112]{0,1:T(8,128)(2,1)} collective-permute-done((bf16[512,2112]{0,1:T(8,128)(2,1)}, bf16[512,2112]{0,1:T(8,128)(2,1)}, u32[]{:S(2)}, u32[]{:S(2)}) %collective-permute-start.105) | collective-permute-done | bytes 2162720 | tf_op jit(solution)/shard_map/ppermute | solution.py:430
  893.9 8.2 collective-permute-done.111
  902.5 20.0 %collective-permute-done.116 = bf16[512,1024]{1,0:T(8,128)(2,1)S(1)} collective-permute-done((bf16[512,1024]{1,0:T(8,128)(2,1)S(1)}, bf16[512,1024]{1,0:T(8,128)(2,1)S(1)}, u32[]{:S(2)}, u32[]{:S(2)}) %collective-permute-start.116) | collective-permute-done | bytes 1048608 | tf_op jit(solution)/shard_map/ppermute | solution.py:430
  934.1 11.4 %collective-permute-done.107 = bf16[128,2112]{0,1:T(8,128)(2,1)S(1)} collective-permute-done((bf16[128,2112]{0,1:T(8,128)(2,1)S(1)}, bf16[128,2112]{0,1:T(8,128)(2,1)S(1)}, u32[]{:S(2)}, u32[]{:S(2)}) %collective-permute-start.107) | collective-permute-done | bytes 540704 | tf_op jit(solution)/shard_map/ppermute | solution.py:426
  954.1 11.4 %collective-permute-done.108 = bf16[128,2112]{0,1:T(8,128)(2,1)S(1)} collective-permute-done((bf16[128,2112]{0,1:T(8,128)(2,1)S(1)}, bf16[128,2112]{0,1:T(8,128)(2,1)S(1)}, u32[]{:S(2)}, u32[]{:S(2)}) %collective-permute-start.108) | collective-permute-done | bytes 540704 | tf_op jit(solution)/shard_map/ppermute | solution.py:426
  (820 shorter events, 496.5 us)
Async XLA Ops:
  18.8 79.8 %all-to-all-start = ((bf16[16,256,88]{1,2,0:T(8,128)(2,1)}), bf16[16,256,88]{1,2,0:T(8,128)(2,1)}, u32[]{:S(2)}, u32[]{:S(2)}) async-start(bf16[16,256,88]{1,2,0:T(8,128)(2,1)} %bitcast.236), calls=%async_computation | async-start | bytes 1441792 | tf_op jit(solution)/shard_map/all_to_all | solution.py:859
  98.6 105.5 %all-to-all-start.1 = ((bf16[16,88,128]{2,1,0:T(8,128)(2,1)}), bf16[16,88,128]{2,1,0:T(8,128)(2,1)}, u32[]{:S(2)}, u32[]{:S(2)}) async-start(bf16[16,88,128]{2,1,0:T(8,128)(2,1)} %bitcast.49), calls=%async_computation.1 | async-start | bytes 720896 | tf_op jit(solution)/shard_map/all_to_all | solution.py:868
  109.6 50.8 %collective-permute-start.9 = (bf16[128,2176]{1,0:T(8,128)(2,1)}, bf16[128,2176]{1,0:T(8,128)(2,1)}, u32[]{:S(2)}, u32[]{:S(2)}) collective-permute-start(bf16[128,2176]{1,0:T(8,128)(2,1)} %collective-permute-done.8.refs_8_), channel_id=1, source_target_pairs={{0,2},{2,0},{4,6},{6,4},{8,10},{10,8},{12,14},{14,12},{16,18},{18,... | collective-permute-start | bytes 1671176 | tf_op jit(solution)/shard_map/ppermute | solution.py:434
  158.1 45.9 %collective-permute-start.51 = (bf16[128,2048]{1,0:T(8,128)(2,1)}, bf16[128,2048]{1,0:T(8,128)(2,1)}, u32[]{:S(2)}, u32[]{:S(2)}) collective-permute-start(bf16[128,2048]{1,0:T(8,128)(2,1)} %refs_6_.1), channel_id=1, source_target_pairs={{0,8},{2,10},{4,12},{6,14},{8,16},{10,18},{12,20},{14,22},{16,24},... | collective-permute-start | bytes 1572872 | tf_op jit(solution)/shard_map/ppermute | solution.py:426
  160.4 55.2 %collective-permute-start.35 = (bf16[128,2048]{1,0:T(8,128)(2,1)}, bf16[128,2048]{1,0:T(8,128)(2,1)}, u32[]{:S(2)}, u32[]{:S(2)}) collective-permute-start(bf16[128,2048]{1,0:T(8,128)(2,1)} %refs_6_.1), channel_id=1, source_target_pairs={{0,4},{2,6},{4,0},{6,2},{8,12},{10,14},{12,8},{14,10},{16,20},{18,... | collective-permute-start | bytes 1572872 | tf_op jit(solution)/shard_map/ppermute | solution.py:430
  161.4 54.8 %collective-permute-start.36 = (bf16[128,2048]{1,0:T(8,128)(2,1)}, bf16[128,2048]{1,0:T(8,128)(2,1)}, u32[]{:S(2)}, u32[]{:S(2)}) collective-permute-start(bf16[128,2048]{1,0:T(8,128)(2,1)} %refs_6_.1), channel_id=1, source_target_pairs={{0,1},{1,0},{2,3},{3,2},{4,5},{5,4},{6,7},{7,6},{8,9},{9,8},{10,11... | collective-permute-start | bytes 1572872 | tf_op jit(solution)/shard_map/ppermute | solution.py:438
  162.9 95.3 %collective-permute-start.38 = (bf16[2,2048,704]{1,2,0:T(8,128)(2,1)}, bf16[2,2048,704]{1,2,0:T(8,128)(2,1)}, u32[]{:S(2)}, u32[]{:S(2)}) collective-permute-start(bf16[2,2048,704]{1,2,0:T(8,128)(2,1)} %bitcast.227), channel_id=1, source_target_pairs={{0,2},{2,0},{4,6},{6,4},{8,10},{10,8},{12,14},{14,12},{16,18},{18,... | collective-permute-start | bytes 17301512 | tf_op jit(solution)/shard_map/ppermute | solution.py:434
  246.0 50.3 %collective-permute-start.61 = (bf16[128,2048]{1,0:T(8,128)(2,1)}, bf16[128,2048]{1,0:T(8,128)(2,1)}, u32[]{:S(2)}, u32[]{:S(2)}) collective-permute-start(bf16[128,2048]{1,0:T(8,128)(2,1)} %collective-permute-done.52.refs_6_), channel_id=1, source_target_pairs={{0,1},{1,0},{2,3},{3,2},{4,5},{5,4},{6,7},{7,6},{8,9},{9,8},{10,11... | collective-permute-start | bytes 1572872 | tf_op jit(solution)/shard_map/ppermute | solution.py:438
  258.3 44.6 %collective-permute-start.34 = (bf16[128,2048]{1,0:T(8,128)(2,1)}, bf16[128,2048]{1,0:T(8,128)(2,1)}, u32[]{:S(2)}, u32[]{:S(2)}) collective-permute-start(bf16[128,2048]{1,0:T(8,128)(2,1)} %collective-permute-done.33.refs_4_), channel_id=1, source_target_pairs={{0,4},{2,6},{4,0},{6,2},{8,12},{10,14},{12,8},{14,10},{16,20},{18,... | collective-permute-start | bytes 1572872 | tf_op jit(solution)/shard_map/ppermute | solution.py:430
  296.3 66.5 %collective-permute-start.53 = (bf16[128,2048]{1,0:T(8,128)(2,1)}, bf16[128,2048]{1,0:T(8,128)(2,1)S(1)}, u32[]{:S(2)}, u32[]{:S(2)}) collective-permute-start(bf16[128,2048]{1,0:T(8,128)(2,1)} %collective-permute-done.52.refs_6_), channel_id=1, source_target_pairs={{0,8},{2,10},{4,12},{6,14},{8,16},{10,18},{12,20},{14,22},{16,24},... | collective-permute-start | bytes 1572872 | tf_op jit(solution)/shard_map/ppermute | solution.py:426
  297.0 66.9 %collective-permute-start.64 = (bf16[128,2048]{1,0:T(8,128)(2,1)}, bf16[128,2048]{1,0:T(8,128)(2,1)S(1)}, u32[]{:S(2)}, u32[]{:S(2)}) collective-permute-start(bf16[128,2048]{1,0:T(8,128)(2,1)} %collective-permute-done.45.refs_2_), channel_id=1, source_target_pairs={{0,1},{1,0},{2,3},{3,2},{4,5},{5,4},{6,7},{7,6},{8,9},{9,8},{10,11... | collective-permute-start | bytes 1572872 | tf_op jit(solution)/shard_map/ppermute | solution.py:438
  298.4 67.5 %collective-permute-start.58 = (bf16[128,2048]{1,0:T(8,128)(2,1)}, bf16[128,2048]{1,0:T(8,128)(2,1)S(1)}, u32[]{:S(2)}, u32[]{:S(2)}) collective-permute-start(bf16[128,2048]{1,0:T(8,128)(2,1)} %collective-permute-done.46.refs_2_), channel_id=1, source_target_pairs={{0,1},{1,0},{2,3},{3,2},{4,5},{5,4},{6,7},{7,6},{8,9},{9,8},{10,11... | collective-permute-start | bytes 1572872 | tf_op jit(solution)/shard_map/ppermute | solution.py:438
  299.0 67.9 %collective-permute-start.47 = (bf16[128,2048]{1,0:T(8,128)(2,1)}, bf16[128,2048]{1,0:T(8,128)(2,1)S(1)}, u32[]{:S(2)}, u32[]{:S(2)}) collective-permute-start(bf16[128,2048]{1,0:T(8,128)(2,1)} %collective-permute-done.46.refs_2_), channel_id=1, source_target_pairs={{0,8},{2,10},{4,12},{6,14},{8,16},{10,18},{12,20},{14,22},{16,24},... | collective-permute-start | bytes 1572872 | tf_op jit(solution)/shard_map/ppermute | solution.py:426
  302.9 62.0 %collective-permute-start.65 = (bf16[128,2048]{1,0:T(8,128)(2,1)}, bf16[128,2048]{1,0:T(8,128)(2,1)S(1)}, u32[]{:S(2)}, u32[]{:S(2)}) collective-permute-start(bf16[128,2048]{1,0:T(8,128)(2,1)} %collective-permute-done.63.refs_3_), channel_id=1, source_target_pairs={{0,1},{1,0},{2,3},{3,2},{4,5},{5,4},{6,7},{7,6},{8,9},{9,8},{10,11... | collective-permute-start | bytes 1572872 | tf_op jit(solution)/shard_map/ppermute | solution.py:438
  362.8 43.9 %collective-permute-start.62 = (bf16[128,2048]{1,0:T(8,128)(2,1)}, bf16[128,2048]{1,0:T(8,128)(2,1)S(1)}, u32[]{:S(2)}, u32[]{:S(2)}) collective-permute-start(bf16[128,2048]{1,0:T(8,128)(2,1)} %collective-permute-done.61.refs_8_), channel_id=1, source_target_pairs={{0,4},{2,6},{4,0},{6,2},{8,12},{10,14},{12,8},{14,10},{16,20},{18,... | collective-permute-start | bytes 1572872 | tf_op jit(solution)/shard_map/ppermute | solution.py:430
  364.9 43.9 %collective-permute-start.57 = (bf16[128,2048]{1,0:T(8,128)(2,1)}, bf16[128,2048]{1,0:T(8,128)(2,1)}, u32[]{:S(2)}, u32[]{:S(2)}) collective-permute-start(bf16[128,2048]{1,0:T(8,128)(2,1)} %collective-permute-done.46.refs_2_), channel_id=1, source_target_pairs={{0,4},{2,6},{4,0},{6,2},{8,12},{10,14},{12,8},{14,10},{16,20},{18,... | collective-permute-start | bytes 1572872 | tf_op jit(solution)/shard_map/ppermute | solution.py:430
  365.9 47.1 %collective-permute-start.59 = (bf16[128,2048]{1,0:T(8,128)(2,1)S(1)}, bf16[128,2048]{1,0:T(8,128)(2,1)}, u32[]{:S(2)}, u32[]{:S(2)}) collective-permute-start(bf16[128,2048]{1,0:T(8,128)(2,1)S(1)} %collective-permute-done.58.refs_4_), channel_id=1, source_target_pairs={{0,4},{2,6},{4,0},{6,2},{8,12},{10,14},{12,8},{14,10},{16,20},{18,... | collective-permute-start | bytes 1572872 | tf_op jit(solution)/shard_map/ppermute | solution.py:430
  366.9 45.3 %collective-permute-start.48 = (bf16[128,2048]{1,0:T(8,128)(2,1)S(1)}, bf16[128,2048]{1,0:T(8,128)(2,1)S(1)}, u32[]{:S(2)}, u32[]{:S(2)}) collective-permute-start(bf16[128,2048]{1,0:T(8,128)(2,1)S(1)} %collective-permute-done.47.refs_2_), channel_id=1, source_target_pairs={{0,4},{2,6},{4,0},{6,2},{8,12},{10,14},{12,8},{14,10},{16,20},{18,... | collective-permute-start | bytes 1572872 | tf_op jit(solution)/shard_map/ppermute | solution.py:430
  406.7 46.8 %collective-permute-start.55 = (bf16[128,2048]{1,0:T(8,128)(2,1)S(1)}, bf16[128,2048]{1,0:T(8,128)(2,1)S(1)}, u32[]{:S(2)}, u32[]{:S(2)}) collective-permute-start(bf16[128,2048]{1,0:T(8,128)(2,1)S(1)} %collective-permute-done.53.refs_6_), channel_id=1, source_target_pairs={{0,1},{1,0},{2,3},{3,2},{4,5},{5,4},{6,7},{7,6},{8,9},{9,8},{10,11... | collective-permute-start | bytes 1572872 | tf_op jit(solution)/shard_map/ppermute | solution.py:438
  407.4 46.9 %collective-permute-start.56 = (bf16[128,2048]{1,0:T(8,128)(2,1)S(1)}, bf16[128,2048]{1,0:T(8,128)(2,1)}, u32[]{:S(2)}, u32[]{:S(2)}) collective-permute-start(bf16[128,2048]{1,0:T(8,128)(2,1)S(1)} %collective-permute-done.54.refs_7_), channel_id=1, source_target_pairs={{0,1},{1,0},{2,3},{3,2},{4,5},{5,4},{6,7},{7,6},{8,9},{9,8},{10,11... | collective-permute-start | bytes 1572872 | tf_op jit(solution)/shard_map/ppermute | solution.py:438
  408.8 45.5 %collective-permute-start.49 = (bf16[128,2048]{1,0:T(8,128)(2,1)S(1)}, bf16[128,2048]{1,0:T(8,128)(2,1)}, u32[]{:S(2)}, u32[]{:S(2)}) collective-permute-start(bf16[128,2048]{1,0:T(8,128)(2,1)S(1)} %collective-permute-done.47.refs_2_), channel_id=1, source_target_pairs={{0,1},{1,0},{2,3},{3,2},{4,5},{5,4},{6,7},{7,6},{8,9},{9,8},{10,11... | collective-permute-start | bytes 1572872 | tf_op jit(solution)/shard_map/ppermute | solution.py:438
  413.0 141.9 %collective-permute-start.91 = (bf16[128,2048]{1,0:T(8,128)(2,1)}, bf16[128,2048]{1,0:T(8,128)(2,1)}, u32[]{:S(2)}, u32[]{:S(2)}) collective-permute-start(bf16[128,2048]{1,0:T(8,128)(2,1)} %get-tuple-element.123), channel_id=1, source_target_pairs={{0,1},{1,0},{2,3},{3,2},{4,5},{5,4},{6,7},{7,6},{8,9},{9,8},{10,11... | collective-permute-start | bytes 1572872 | tf_op jit(solution)/shard_map/ppermute | solution.py:438
  453.5 153.5 %collective-permute-start.90 = (bf16[128,2048]{1,0:T(8,128)(2,1)}, bf16[128,2048]{1,0:T(8,128)(2,1)}, u32[]{:S(2)}, u32[]{:S(2)}) collective-permute-start(bf16[128,2048]{1,0:T(8,128)(2,1)} %get-tuple-element.121), channel_id=1, source_target_pairs={{0,1},{1,0},{2,3},{3,2},{4,5},{5,4},{6,7},{7,6},{8,9},{9,8},{10,11... | collective-permute-start | bytes 1572872 | tf_op jit(solution)/shard_map/ppermute | solution.py:438
  538.9 94.4 %collective-permute-start.89 = (bf16[128,2048]{1,0:T(8,128)(2,1)}, bf16[128,2048]{1,0:T(8,128)(2,1)S(1)}, u32[]{:S(2)}, u32[]{:S(2)}) collective-permute-start(bf16[128,2048]{1,0:T(8,128)(2,1)} %get-tuple-element.119), channel_id=1, source_target_pairs={{0,4},{2,6},{4,0},{6,2},{8,12},{10,14},{12,8},{14,10},{16,20},{18,... | collective-permute-start | bytes 1572872 | tf_op jit(solution)/shard_map/ppermute | solution.py:430
  549.9 111.5 %all-to-all-start.3 = ((bf16[16,88,128]{2,1,0:T(8,128)(2,1)}), bf16[16,88,128]{2,1,0:T(8,128)(2,1)S(1)}, u32[]{:S(2)}, u32[]{:S(2)}) async-start(bf16[16,88,128]{2,1,0:T(8,128)(2,1)} %bitcast_bitcast_fusion), calls=%async_computation.3 | async-start | bytes 720896 | tf_op jit(solution)/shard_map/all_to_all | solution.py:1019
  568.1 53.3 %collective-permute-start.75 = (bf16[128,2048]{1,0:T(8,128)(2,1)}, bf16[128,2048]{1,0:T(8,128)(2,1)S(1)}, u32[]{:S(2)}, u32[]{:S(2)}) collective-permute-start(bf16[128,2048]{1,0:T(8,128)(2,1)} %get-tuple-element.105), channel_id=1, source_target_pairs={{0,1},{1,0},{2,3},{3,2},{4,5},{5,4},{6,7},{7,6},{8,9},{9,8},{10,11... | collective-permute-start | bytes 1572872 | tf_op jit(solution)/shard_map/ppermute | solution.py:438
  648.5 76.7 %collective-permute-start.124 = (bf16[2048,704]{0,1:T(8,128)(2,1)}, bf16[2048,704]{0,1:T(8,128)(2,1)}, u32[]{:S(2)}, u32[]{:S(2)}) collective-permute-start(bf16[2048,704]{0,1:T(8,128)(2,1)} %convolution_convert_fusion.3), channel_id=1, source_target_pairs={{0,2},{2,0},{4,6},{6,4},{8,10},{10,8},{12,14},{14,12},{16,18},{18,... | collective-permute-start | bytes 8650760 | tf_op jit(solution)/shard_map/ppermute | solution.py:434
  723.9 44.6 %collective-permute-start.96 = (bf16[128,2048]{1,0:T(8,128)(2,1)S(1)}, bf16[128,2048]{1,0:T(8,128)(2,1)S(1)}, u32[]{:S(2)}, u32[]{:S(2)}) collective-permute-start(bf16[128,2048]{1,0:T(8,128)(2,1)S(1)} %get-tuple-element.225), channel_id=1, source_target_pairs={{0,1},{1,0},{2,3},{3,2},{4,5},{5,4},{6,7},{7,6},{8,9},{9,8},{10,11... | collective-permute-start | bytes 1572872 | tf_op jit(solution)/shard_map/ppermute | solution.py:438
  801.6 46.0 %collective-permute-start.110 = (bf16[256,2048]{1,0:T(8,128)(2,1)}, bf16[256,2048]{1,0:T(8,128)(2,1)}, u32[]{:S(2)}, u32[]{:S(2)}) collective-permute-start(bf16[256,2048]{1,0:T(8,128)(2,1)} %slice.462), channel_id=1, source_target_pairs={{0,2},{2,0},{4,6},{6,4},{8,10},{10,8},{12,14},{14,12},{16,18},{18,... | collective-permute-start | bytes 3145736 | tf_op jit(solution)/shard_map/ppermute | solution.py:434
  840.6 50.3 %collective-permute-start.105 = (bf16[512,2112]{0,1:T(8,128)(2,1)}, bf16[512,2112]{0,1:T(8,128)(2,1)}, u32[]{:S(2)}, u32[]{:S(2)}) collective-permute-start(bf16[512,2112]{0,1:T(8,128)(2,1)} %slice.603), channel_id=1, source_target_pairs={{0,4},{2,6},{4,0},{6,2},{8,12},{10,14},{12,8},{14,10},{16,20},{18,... | collective-permute-start | bytes 6488072 | tf_op jit(solution)/shard_map/ppermute | solution.py:430
  849.5 52.6 %collective-permute-start.111 = (bf16[128,2048]{1,0:T(8,128)(2,1)S(1)}, bf16[128,2048]{1,0:T(8,128)(2,1)S(1)}, u32[]{:S(2)}, u32[]{:S(2)}) collective-permute-start(bf16[128,2048]{1,0:T(8,128)(2,1)S(1)} %slice.606), channel_id=1, source_target_pairs={{0,4},{2,6},{4,0},{6,2},{8,12},{10,14},{12,8},{14,10},{16,20},{18,... | collective-permute-start | bytes 1572872 | tf_op jit(solution)/shard_map/ppermute | solution.py:430
  853.0 69.5 %collective-permute-start.116 = (bf16[512,1024]{1,0:T(8,128)(2,1)S(1)}, bf16[512,1024]{1,0:T(8,128)(2,1)S(1)}, u32[]{:S(2)}, u32[]{:S(2)}) collective-permute-start(bf16[512,1024]{1,0:T(8,128)(2,1)S(1)} %slice.604), channel_id=1, source_target_pairs={{0,4},{2,6},{4,0},{6,2},{8,12},{10,14},{12,8},{14,10},{16,20},{18,... | collective-permute-start | bytes 3145736 | tf_op jit(solution)/shard_map/ppermute | solution.py:430
  (256 other events, 4371.0 us)

commit v3 on v2

--- a/solution.py
+++ b/solution.py
@@ -438,7 +438,22 @@
     return lax.ppermute(values, "tensor", [(0, 1), (1, 0)])
 
 
-def gather_rows(rows):
+def fence_kernel(*refs):
+    pass
+
+
+def after(values, *others):
+    anywhere = pl.BlockSpec(memory_space=pl.ANY)
+    return pl.pallas_call(
+        fence_kernel,
+        out_shape=jax.ShapeDtypeStruct(values.shape, values.dtype),
+        in_specs=[anywhere] * (1 + len(others)),
+        out_specs=anywhere,
+        input_output_aliases={0: 0},
+    )(values, *others)
+
+
+def gather_rows(rows, corners):
     planes = []
     current = rows
     for distance in range(RINGS):
@@ -446,7 +461,7 @@
             current = ring_step(current)
         beside = other_y(current)
         across = other_x(current)
-        corner = other_x(beside) if distance % 2 else other_y(across)
+        corner = other_x(beside) if corners[distance] == "x" else other_y(across)
         planes.append((current, beside, across, corner))
     return planes
 
@@ -455,16 +470,23 @@
     return (first.astype(jnp.float32) + second.astype(jnp.float32)).astype(jnp.bfloat16)
 
 
-def scatter_rows(planes):
+def turn_corner(plane, direction):
+    own, beside, across, corner = plane
+    if direction == "x":
+        return own, add_low(beside, other_x(corner)), across
+    return own, beside, add_low(across, other_y(corner))
+
+
+def close_plane(turned):
+    own, beside, across = turned
+    return own, other_y(beside), other_x(across)
+
+
+def ring_rows(closed):
     moving = None
     for distance in (1, 2, 3, 0):
-        own, beside, across, corner = planes[distance]
-        if distance % 2:
-            beside = add_low(beside, other_x(corner))
-        else:
-            across = add_low(across, other_y(corner))
-        total = own.astype(jnp.float32)
-        total = total + other_x(across).astype(jnp.float32) + other_y(beside).astype(jnp.float32)
+        own, from_y, from_x = closed[distance]
+        total = own.astype(jnp.float32) + from_y.astype(jnp.float32) + from_x.astype(jnp.float32)
         if moving is not None:
             total = total + ring_step(moving).astype(jnp.float32)
         moving = total.astype(jnp.bfloat16)
@@ -478,12 +500,16 @@
     return moving
 
 
-def gather_weight(shard):
+def ring_shards(shard):
+    held = [shard]
+    for _ in range(RINGS - 1):
+        held.append(ring_step(held[-1]))
+    return held
+
+
+def gather_weight(held):
     chunks = []
-    current = shard
-    for distance in range(RINGS):
-        if distance:
-            current = ring_step(current)
+    for distance, current in enumerate(held):
         beside = other_y(current)
         for flip_y, chunk in ((0, current), (1, beside)):
             for flip_core, piece in ((0, chunk), (1, other_core(chunk))):
@@ -501,9 +527,9 @@
     )
 
 
-def place_kernel(keys, moves, coords_ref, *refs):
+def place_kernel(keys, moves, outputs, coords_ref, *refs):
     chunks = refs[: len(keys)]
-    outs = refs[len(keys) : -1]
+    outs = refs[-1 - outputs : -1]
     semaphores = refs[-1]
     coords = (coords_ref[0], coords_ref[1], coords_ref[2])
     copies = []
@@ -524,13 +550,13 @@
         copy.wait()
 
 
-def place_chunks(coords, chunks, moves, shapes):
+def place_chunks(coords, chunks, moves, shapes, others=()):
     keys = [key for key, _ in chunks]
     anywhere = pl.BlockSpec(memory_space=pl.ANY)
     return pl.pallas_call(
-        functools.partial(place_kernel, keys, moves),
+        functools.partial(place_kernel, keys, moves, len(shapes)),
         out_shape=[jax.ShapeDtypeStruct(shape, jnp.bfloat16) for shape in shapes],
-        in_specs=[pl.BlockSpec(memory_space=pltpu.SMEM)] + [anywhere] * len(chunks),
+        in_specs=[pl.BlockSpec(memory_space=pltpu.SMEM)] + [anywhere] * (len(chunks) + len(others)),
         out_specs=[pl.BlockSpec(memory_space=pltpu.VMEM)] * len(shapes),
         scratch_shapes=[pltpu.SemaphoreType.DMA((len(chunks) * len(moves),))],
         compiler_params=pltpu.CompilerParams(vmem_limit_bytes=24 * 1024 * 1024),
@@ -539,7 +565,7 @@
             bytes_accessed=4 * sum(shape[0] * shape[1] for shape in shapes),
             transcendentals=0,
         ),
-    )(coords, *[piece for _, piece in chunks])
+    )(coords, *[piece for _, piece in chunks], *others)
 
 
 def weight_keys():
@@ -592,27 +618,109 @@
 TILE = 256
 
 
-def mlp_kernel(tiles, steps, pieces, *refs):
-    experts_ref, routed_ref = refs[:2]
-    row_refs = refs[2 : 2 + pieces]
-    cot_refs = refs[2 + pieces : 2 + 2 * pieces]
-    router_ref, gate_col, up_col, down_row, gate_row, up_row, down_col = refs[
-        2 + 2 * pieces : 9 + 2 * pieces
+def whole(array):
+    return pl.BlockSpec(array.shape, lambda i: (0,) * array.ndim)
+
+
+def load_pieces(pieces, target, semaphores):
+    size = pieces[0].shape[0]
+    copies = [
+        pltpu.make_async_copy(piece, target.at[pl.ds(k * size, size)], semaphores.at[k])
+        for k, piece in enumerate(pieces)
     ]
-    outs = refs[9 + 2 * pieces + 6 :]
-    grad_refs, out_refs = outs[:pieces], outs[pieces : 2 * pieces]
-    rows_out, cots_out, hidden_out, gate_out, up_out, logit_out = outs[2 * pieces : 2 * pieces + 6]
-    hidden_all, gate_all, up_all, prob_ref, scale_ref, sum_ref = outs[2 * pieces + 6 :]
+    for copy in copies:
+        copy.start()
+    for copy in copies:
+        copy.wait()
+
+
+def down_kernel(count, *refs):
+    pieces, (weight_ref, grads_ref, rows_ref, semaphores) = refs[:count], refs[count:]
+
+    @pl.when(pl.program_id(0) == 0)
+    def _():
+        load_pieces(pieces, rows_ref, semaphores)
+
+    size = rows_ref.shape[0] // 4
+    for k in range(4):
+        part = slice(k * size, (k + 1) * size)
+        grads_ref[part, :] = dot_turned(rows_ref[part, :], weight_ref[...]).astype(jnp.bfloat16)
+
+
+def down_grads(pieces, down):
+    count = len(pieces)
+    size, depth = pieces[0].shape
+    width = down.shape[0]
+    rows = count * size
+    return pl.pallas_call(
+        functools.partial(down_kernel, count),
+        grid=(width // TILE,),
+        in_specs=[pl.BlockSpec(memory_space=pl.ANY)] * count
+        + [pl.BlockSpec((TILE, depth), lambda i: (i, 0))],
+        out_specs=[
+            pl.BlockSpec((rows, TILE), lambda i: (0, i)),
+            pl.BlockSpec((rows, depth), lambda i: (0, 0)),
+        ],
+        out_shape=[
+            jax.ShapeDtypeStruct((rows, width), jnp.bfloat16),
+            jax.ShapeDtypeStruct((rows, depth), jnp.bfloat16),
+        ],
+        scratch_shapes=[pltpu.SemaphoreType.DMA((count,))],
+        compiler_params=pltpu.CompilerParams(vmem_limit_bytes=48 * 1024 * 1024),
+        cost_estimate=pl.CostEstimate(
+            flops=2 * rows * depth * width,
+            bytes_accessed=2 * (2 * rows * depth + depth * width + rows * width),
+            transcendentals=0,
+        ),
+    )(*pieces, down)
+
+
+def out_kernel(count, *refs):
+    hidden_ref, weight_ref = refs[:2]
+    outs = refs[2:]
+    size = outs[0].shape[0]
+    for k in range(0, count, 4):
+        part = hidden_ref[k * size : (k + 4) * size, :]
+        result = wide_dot(part, weight_ref[...]).astype(jnp.bfloat16)
+        for j in range(4):
+            outs[k + j][...] = result[j * size : (j + 1) * size]
+
+
+def out_rows(count, hidden, down):
+    rows, width = hidden.shape
+    depth = down.shape[1]
+    size = rows // count
+    return pl.pallas_call(
+        functools.partial(out_kernel, count),
+        grid=(depth // TILE,),
+        in_specs=[whole(hidden), pl.BlockSpec((width, TILE), lambda i: (0, i))],
+        out_specs=[pl.BlockSpec((size, TILE), lambda i: (0, i))] * count,
+        out_shape=[jax.ShapeDtypeStruct((size, depth), jnp.bfloat16)] * count,
+        compiler_params=pltpu.CompilerParams(vmem_limit_bytes=48 * 1024 * 1024),
+        cost_estimate=pl.CostEstimate(
+            flops=2 * rows * depth * width,
+            bytes_accessed=2 * (rows * depth + depth * width + rows * width),
+            transcendentals=0,
+        ),
+    )(hidden, down)
+
+
+def mlp_kernel(tiles, pieces, others, experts_ref, routed_ref, *refs):
+    row_refs = refs[:pieces]
+    router_ref, gate_col, up_col, down_grad, gate_row, up_row = refs[pieces : pieces + 6]
+    outs = refs[pieces + 6 + others :]
+    grad_refs = outs[:pieces]
+    rows_out, hidden_out, gate_out, up_out, logit_out = outs[pieces : pieces + 5]
+    gate_all, up_all, prob_ref, scale_ref, sum_ref, semaphores = outs[pieces + 5 :]
     step = pl.program_id(0)
     third = tiles // 2
-    size = row_refs[0].shape[0]
+    total = rows_out.shape[0]
+    size = total // pieces
     lane = lax.broadcasted_iota(jnp.int32, (1, router_ref.shape[1]), 1)
 
     @pl.when(step == 0)
     def _():
-        for k in range(pieces):
-            rows_out[k * size : (k + 1) * size, :] = row_refs[k][...]
-            cots_out[k * size : (k + 1) * size, :] = cot_refs[k][...]
+        load_pieces(row_refs, rows_out, semaphores)
         logits = wide_dot(rows_out[...], router_ref[...])
         logits = jnp.where(lane < experts_ref[2], logits, -1e30)
         raised = jnp.exp(logits - jnp.max(logits, axis=1, keepdims=True))
@@ -626,26 +734,29 @@
 
     @pl.when(step < tiles)
     def _():
-        pre_gate = wide_dot(rows_out[...], gate_col[...])
-        pre_up = wide_dot(rows_out[...], up_col[...])
-        down_grad = dot_turned(cots_out[...], down_row[...])
-        part = step // third
-        scale = scale_ref[part]
-        sigmoid = 1.0 / (1.0 + jnp.exp(-pre_gate))
-        silu = pre_gate * sigmoid
-        hidden = (silu * pre_up).astype(jnp.bfloat16).astype(jnp.float32)
-        sum_ref[part] += jnp.sum(hidden * down_grad, axis=1, keepdims=True)
-        grad_hidden = scale * down_grad
         columns = pl.ds(pl.multiple_of(step * TILE, TILE), TILE)
-        low_hidden = (scale * hidden).astype(jnp.bfloat16)
-        low_gate = (grad_hidden * pre_up * (sigmoid + silu * (1.0 - sigmoid))).astype(jnp.bfloat16)
-        low_up = (grad_hidden * silu).astype(jnp.bfloat16)
-        hidden_all[:, columns] = low_hidden
-        gate_all[:, columns] = low_gate
-        up_all[:, columns] = low_up
-        hidden_out[...] = low_hidden
-        gate_out[...] = low_gate
-        up_out[...] = low_up
+        kind = step // third
+        half = total // 2
+        for k in (0, 1):
+            part = slice(k * half, (k + 1) * half)
+            pre_gate = wide_dot(rows_out[part, :], gate_col[...])
+            pre_up = wide_dot(rows_out[part, :], up_col[...])
+            grads = down_grad[part, :].astype(jnp.float32)
+            scale = scale_ref[kind, part, :]
+            sigmoid = 1.0 / (1.0 + jnp.exp(-pre_gate))
+            silu = pre_gate * sigmoid
+            hidden = (silu * pre_up).astype(jnp.bfloat16).astype(jnp.float32)
+            sum_ref[kind, part, :] += jnp.sum(hidden * grads, axis=1, keepdims=True)
+            grad_hidden = scale * grads
+            low_gate = (grad_hidden * pre_up * (sigmoid + silu * (1.0 - sigmoid))).astype(
+                jnp.bfloat16
+            )
+            low_up = (grad_hidden * silu).astype(jnp.bfloat16)
+            gate_all[part, columns] = low_gate
+            up_all[part, columns] = low_up
+            hidden_out[part, :] = (scale * hidden).astype(jnp.bfloat16)
+            gate_out[part, :] = low_gate
+            up_out[part, :] = low_up
 
     @pl.when(step == tiles - 1)
     def _():
@@ -661,21 +772,17 @@
         grads = dot_turned(gate_all[...], gate_row[...]) + dot_turned(up_all[...], up_row[...])
         grads += dot_turned(logit_out[...], router_ref[some, :])
         grads = grads.astype(jnp.bfloat16)
-        result = wide_dot(hidden_all[...], down_col[...]).astype(jnp.bfloat16)
         for k in range(pieces):
             grad_refs[k][...] = grads[k * size : (k + 1) * size]
-            out_refs[k][...] = result[k * size : (k + 1) * size]
-
-
-def mlp_plane(distance, experts, routed, rows, cots, router, gate, up, down, kept):
+
+
+def mlp_plane(distance, experts, routed, rows, down_grad, router, gate, up, kept, others):
     pieces = len(rows)
     size, depth = rows[0].shape
     width = gate.shape[1]
     tiles, columns = width // TILE, depth // TILE
     total = pieces * size
-
-    def whole(array):
-        return pl.BlockSpec(array.shape, lambda i: (0,) * array.ndim)
+    low = jnp.bfloat16
 
     def early(i):
         return jnp.minimum(i, tiles - 1)
@@ -683,53 +790,52 @@
     def late(i):
         return jnp.maximum(i - tiles, 0)
 
-    low = jnp.bfloat16
-    piece_spec = pl.BlockSpec((size, TILE), lambda i: (0, late(i)))
     tile_spec = pl.BlockSpec((total, TILE), lambda i: (distance, early(i)))
-    kept_specs = [
-        pl.BlockSpec((total, depth), lambda i: (distance, 0)),
-        pl.BlockSpec((total, depth), lambda i: (distance, 0)),
-        tile_spec,
-        tile_spec,
-        tile_spec,
-        pl.BlockSpec((total, router.shape[1]), lambda i: (distance, 0)),
-    ]
-    first_kept = 9 + 2 * pieces
-    aliases = {first_kept + k: 2 * pieces + k for k in range(6)}
+    anywhere = pl.BlockSpec(memory_space=pl.ANY)
+    first_kept = 2 + pieces + 6
     results = pl.pallas_call(
-        functools.partial(mlp_kernel, tiles, tiles + columns, pieces),
+        functools.partial(mlp_kernel, tiles, pieces, len(kept) + len(others)),
         grid=(tiles + columns,),
         in_specs=[pl.BlockSpec(memory_space=pltpu.SMEM), whole(routed)]
-        + [whole(piece) for piece in rows]
-        + [whole(piece) for piece in cots]
+        + [anywhere] * pieces
         + [
             whole(router),
             pl.BlockSpec((depth, TILE), lambda i: (0, early(i))),
             pl.BlockSpec((depth, TILE), lambda i: (0, early(i))),
-            pl.BlockSpec((TILE, depth), lambda i: (early(i), 0)),
+            tile_spec,
             pl.BlockSpec((TILE, width), lambda i: (late(i), 0)),
             pl.BlockSpec((TILE, width), lambda i: (late(i), 0)),
-            pl.BlockSpec((width, TILE), lambda i: (0, late(i))),
         ]
-        + [pl.BlockSpec(memory_space=pl.ANY)] * 6,
-        out_specs=[piece_spec] * (2 * pieces) + kept_specs,
-        out_shape=[jax.ShapeDtypeStruct((size, depth), low)] * (2 * pieces)
-        + [jax.ShapeDtypeStruct(array.shape, array.dtype) for array in kept],
-        scratch_shapes=[pltpu.VMEM((total, width), low)] * 3
+        + [anywhere] * (len(kept) + len(others)),
+        out_specs=[pl.BlockSpec((size, TILE), lambda i: (0, late(i)))] * pieces
+        + [
+            pl.BlockSpec((total, depth), lambda i: (distance, 0)),
+            tile_spec,
+            tile_spec,
+            tile_spec,
+            pl.BlockSpec((total, router.shape[1]), lambda i: (distance, 0)),
+        ],
+        out_shape=[jax.ShapeDtypeStruct((size, depth), low)] * pieces
+        + [
+            jax.ShapeDtypeStruct((RINGS * total, many), low)
+            for many in (depth, width, width, width, router.shape[1])
+        ],
+        scratch_shapes=[pltpu.VMEM((total, width), low)] * 2
         + [
             pltpu.VMEM((total, router.shape[1]), jnp.float32),
             pltpu.VMEM((3, total, 1), jnp.float32),
             pltpu.VMEM((3, total, 1), jnp.float32),
+            pltpu.SemaphoreType.DMA((pieces,)),
         ],
-        input_output_aliases=aliases,
-        compiler_params=pltpu.CompilerParams(vmem_limit_bytes=60 * 1024 * 1024),
+        input_output_aliases={first_kept + k: pieces + k for k in range(len(kept))},
+        compiler_params=pltpu.CompilerParams(vmem_limit_bytes=48 * 1024 * 1024),
         cost_estimate=pl.CostEstimate(
-            flops=2 * total * depth * width * 6,
-            bytes_accessed=2 * (6 * depth * width + 6 * total * depth + 3 * total * width),
+            flops=2 * total * depth * width * 4,
+            bytes_accessed=2 * (4 * depth * width + 3 * total * depth + 4 * total * width),
             transcendentals=total * width,
         ),
-    )(experts, routed, *rows, *cots, router, gate, up, down, gate, up, down, *kept)
-    return results[:pieces], results[pieces : 2 * pieces], results[2 * pieces :]
+    )(experts, routed, *rows, router, gate, up, down_grad, gate, up, *kept, *others)
+    return results[:pieces], results[pieces:]
 
 
 def gather_body(
@@ -787,23 +893,82 @@
     rows_all = both_halves(block_input, other_x(block_input))
     used = query_width + KVR + ROPE
     first_width = -(-(used + small.shape[1]) // 128) * 128
-    first_chunks = gather_weight(
+    first_held = ring_shards(
         jnp.pad(
             jnp.concatenate([w_query, w_latent, small], axis=1),
             ((0, 0), (0, first_width - used - small.shape[1])),
         )
     )
+    first_chunks = gather_weight(first_held)
     parts = depth // latent_depth
     keyval_part = w_keyval.shape[1] // parts
     keyval_packed = (
         w_keyval.reshape(latent_depth, parts, keyval_part).transpose(1, 0, 2).reshape(depth, -1)
     )
-    second_chunks = gather_weight(jnp.concatenate([keyval_packed, w_output.T], axis=1))
+    second_held = ring_shards(
+        after(jnp.concatenate([keyval_packed, w_output.T], axis=1), first_held[3])
+    )
+    second_chunks = gather_weight(second_held)
+    grad_planes = gather_rows(after(cotangent, second_held[3]), "xxxx")
+    shared_in = lax.all_to_all(
+        after(
+            shared_gate_up.reshape(2, depth, blocks, shared)
+            .transpose(2, 0, 1, 3)
+            .reshape(blocks, 2 * depth, shared),
+            first_held[1],
+        ),
+        "dp",
+        split_axis=0,
+        concat_axis=0,
+        tiled=True,
+    ).reshape(blocks, 2, depth, shared)
+    shared_out = lax.all_to_all(
+        after(shared_down.reshape(blocks, shared, depth), first_held[1]),
+        "dp",
+        split_axis=0,
+        concat_axis=0,
+        tiled=True,
+    )
+    shared_other = other_core(shared_in)
+    shared_out_other = other_core(shared_out)
+    expert_in_other = other_core(expert_gate_up[0])
+    expert_out_other = other_core(expert_down[0])
+    hole = -(-units // TILE) * TILE - units
+
+    def side_columns(k):
+        return jnp.concatenate(
+            [
+                expert_gate_up[0, k],
+                jnp.zeros((D, hole), bf16),
+                expert_in_other[k],
+                jnp.zeros((D, hole), bf16),
+                shared_in[:, k].reshape(D, shared),
+                shared_other[:, k].reshape(D, shared),
+                jnp.zeros((D, TILE - 2 * shared), bf16),
+            ],
+            axis=1,
+        )
+
+    gate_weight = side_columns(0)
+    up_weight = side_columns(1)
+    down_weight = jnp.concatenate(
+        [
+            expert_down[0],
+            jnp.zeros((hole, D), bf16),
+            expert_out_other,
+            jnp.zeros((hole, D), bf16),
+            shared_out.transpose(1, 0, 2).reshape(shared, D),
+            shared_out_other.transpose(1, 0, 2).reshape(shared, D),
+            jnp.zeros((TILE - 2 * shared, D), bf16),
+        ],
+        axis=0,
+    )
     (first_weight,) = place_chunks(
         coords,
         first_chunks,
         [(pl.ds(0, depth), pl.ds(0, first_width), 0, depth, pl.ds(0, first_width))],
         [(D, first_width)],
+        (gate_weight, up_weight, down_weight),
     )
     small = first_weight[:, used:]
     attn_gain_wide = small[:, 0].astype(f32)
@@ -856,56 +1021,6 @@
         [(KVR, w_keyval.shape[1]), (D, w_output.shape[0])],
     )
 
-    shared_in = lax.all_to_all(
-        shared_gate_up.reshape(2, depth, blocks, shared).transpose(2, 0, 1, 3).reshape(
-            blocks, 2 * depth, shared
-        ),
-        "dp",
-        split_axis=0,
-        concat_axis=0,
-        tiled=True,
-    ).reshape(blocks, 2, depth, shared)
-    shared_out = lax.all_to_all(
-        shared_down.reshape(blocks, shared, depth),
-        "dp",
-        split_axis=0,
-        concat_axis=0,
-        tiled=True,
-    )
-    shared_other = other_core(shared_in)
-    shared_out_other = other_core(shared_out)
-    expert_in_other = other_core(expert_gate_up[0])
-    expert_out_other = other_core(expert_down[0])
-    hole = -(-units // TILE) * TILE - units
-
-    def side_columns(k):
-        return jnp.concatenate(
-            [
-                expert_gate_up[0, k],
-                jnp.zeros((D, hole), bf16),
-                expert_in_other[k],
-                jnp.zeros((D, hole), bf16),
-                shared_in[:, k].reshape(D, shared),
-                shared_other[:, k].reshape(D, shared),
-                jnp.zeros((D, TILE - 2 * shared), bf16),
-            ],
-            axis=1,
-        )
-
-    gate_weight = side_columns(0)
-    up_weight = side_columns(1)
-    down_weight = jnp.concatenate(
-        [
-            expert_down[0],
-            jnp.zeros((hole, D), bf16),
-            expert_out_other,
-            jnp.zeros((hole, D), bf16),
-            shared_out.transpose(1, 0, 2).reshape(shared, D),
-            shared_out_other.transpose(1, 0, 2).reshape(shared, D),
-            jnp.zeros((TILE - 2 * shared, D), bf16),
-        ],
-        axis=0,
-    )
     router_wide = jnp.pad(router_weight, ((0, 0), (0, 128 - experts)))
 
     cosine, sine = rotary_tables(segments[0], ROPE)
@@ -939,35 +1054,42 @@
     second_unit = mixed * second_scale
     second_normed = (second_unit * ffn_gain_wide).astype(bf16)
 
-    grad_planes = gather_rows(cotangent)
-    row_planes = gather_rows(second_normed)
-    width = gate_weight.shape[1]
-    total_rows = 16 * local_rows
-    kept = [
-        jnp.zeros((total_rows, columns), bf16)
-        for columns in (D, D, width, width, width, router_wide.shape[1])
-    ]
+    down_grad, every_grad = down_grads(
+        [piece for plane in grad_planes for piece in plane], down_weight
+    )
+    row_planes = gather_rows(second_normed, "yxyx")
     expert_ids = jnp.concatenate([chip_experts, jnp.array([experts], jnp.int32)])
-    grad_parts, out_parts = [], []
+    kept = []
+    turned, closed = [], []
     for distance in range(RINGS):
-        grads, outs, kept = mlp_plane(
+        others = list(turned[distance - 2][1:]) if distance > 1 else []
+        if distance > 2:
+            others += list(closed[distance - 3][1:])
+        grads, kept = mlp_plane(
             distance,
             expert_ids,
             routed[distance],
             row_planes[distance],
-            grad_planes[distance],
+            down_grad,
             router_wide,
             gate_weight,
             up_weight,
-            down_weight,
             kept,
+            others,
         )
-        grad_parts.append(grads)
-        out_parts.append(outs)
-    grad_second = scatter_rows(grad_parts)
-    block_output = mixed + scatter_rows(out_parts)
-
-    every_row, every_grad, every_hidden, every_gate_grad, every_up_grad, logit_grads = kept
+        turned.append(turn_corner(grads, "yxyx"[distance]))
+        closed.append(close_plane(turned[distance]))
+    grad_second = ring_rows(closed)
+    every_row, every_hidden, every_gate_grad, every_up_grad, logit_grads = kept
+    out_pieces = out_rows(4 * RINGS, every_hidden, down_weight)
+    out_closed = []
+    for distance in range(RINGS):
+        plane = list(out_pieces[4 * distance : 4 * distance + 4])
+        plane[3] = after(plane[3], grad_second)
+        plane[2] = after(plane[2], grad_second)
+        out_closed.append(close_plane(turn_corner(plane, "x")))
+    block_output = mixed + ring_rows(out_closed)
+
     far = units + hole
 
     def both_in(grads):

time: 986 us -> 1020 us (1.034)
  matrix products: 97.4 us -> 123 us
    ppermute x36 -> x32, waiting for transfers between devices: 167 us -> 129 us  [other_y(): return lax.ppermute(values, 'dp', [(i, i ^ 2) for i in range(16)])]
    another operation x8 -> x3, local copies, waits for them, and re-layouts: 20 us -> 0.98 us
    ppermute x30 -> x34, waiting for transfers between devices: 40.8 us -> 57.9 us  [other_x(): return lax.ppermute(values, 'tensor', [(0, 1), (1, 0)])]
    dot_general x11, matrix products: 77.1 us -> 92.9 us  [dot_rows(): lax.dot_general(left, right, (((0,), (0,)), ((), ())), preferred_element_...]
    unnamed x357 -> x353, local copies, waits for them, and re-layouts: 71.3 us -> 87 us
    ppermute x30, starting transfers between devices: 51 us -> 38.8 us  [ring_step(): lax.ppermute(values, 'dp', [(i, (i + RINGS) % 16) for i in range(16)])]
    ppermute x30 -> x34, starting transfers between devices: 32.5 us -> 43.5 us  [other_x(): return lax.ppermute(values, 'tensor', [(0, 1), (1, 0)])]
    all_to_all x1, waiting for transfers between devices: 0.01 us -> 10.7 us  [gather_body(): lax.all_to_all(shared_in_grads.astype(bf16).reshape(2, blocks, depth, sha...]
  transfers between devices with their start and end apart: 130 -> 130, of which waited for: 46 -> 40; matrix products, arithmetic and copies ran while one was open for 31% -> 34% of each run, Pallas kernels for 17% -> 17%
where the time goes in v3:
time: 1020 us; the launch traced here: 1010 us
  waiting for transfers between devices  296 us (29%)
  local copies, waits for them, and re-layouts  182 us (18%)
  Pallas kernels  172 us (17%)
  starting transfers between devices  145 us (14%)
  matrix products  123 us (12%)
  other arithmetic  85.5 us (8%)
    ppermute x32, waiting for transfers between devices, other_y(): return lax.ppermute(values, 'dp', [(i, i ^ 2) for i in range(16)])  129 us
    pallas_call x4, Pallas kernels, mlp_plane(): pl.pallas_call(functools.partial(mlp_kernel, tiles, pieces, len(kept) + l...  117 us
    ppermute x30, waiting for transfers between devices, ring_step(): lax.ppermute(values, 'dp', [(i, (i + RINGS) % 16) for i in range(16)])  97.4 us
    dot_general x11, matrix products, dot_rows(): lax.dot_general(left, right, (((0,), (0,)), ((), ())), preferred_element_...  92.9 us
    unnamed x353, local copies, waits for them, and re-layouts  87 us
    ppermute x34, waiting for transfers between devices, other_x(): return lax.ppermute(values, 'tensor', [(0, 1), (1, 0)])  57.9 us
    ppermute x34, starting transfers between devices, other_x(): return lax.ppermute(values, 'tensor', [(0, 1), (1, 0)])  43.5 us
    ppermute x30, starting transfers between devices, ring_step(): lax.ppermute(values, 'dp', [(i, (i + RINGS) % 16) for i in range(16)])  38.8 us
  transfers between devices with their start and end apart: 130, of which 40 were waited for; matrix products, arithmetic and copies ran while one was open for 34% of the time, Pallas kernels for 17%

profile of v3, /device:TPU:0, one launch (start us, length us, event | category | flops | bytes accessed | tf_op | source)
XLA Modules:
  0.0 1007.1 jit_solution(15016014244050964402)
XLA Ops:
  38.5 16.6 %collective-permute-done.8.refs_8_ = bf16[128,2176]{1,0:T(8,128)(2,1)S(1)} collective-permute-done((bf16[128,2176]{1,0:T(8,128)(2,1)}, bf16[128,2176]{1,0:T(8,128)(2,1)S(1)}, u32[]{:S(2)}, u32[]{:S(2)}) %collective-permute-start.8) | collective-permute-done | bytes 557088 | tf_op jit(solution)/shard_map/ppermute | solution.py:426
  76.1 12.8 %collective-permute-done.6.refs_6_ = bf16[128,2176]{1,0:T(8,128)(2,1)} collective-permute-done((bf16[128,2176]{1,0:T(8,128)(2,1)S(1)}, bf16[128,2176]{1,0:T(8,128)(2,1)}, u32[]{:S(2)}, u32[]{:S(2)}) %collective-permute-start.6) | collective-permute-done | bytes 557088 | tf_op jit(solution)/shard_map/ppermute | solution.py:430
  160.3 10.9 %collective-permute-start.45 = (bf16[128,2048]{1,0:T(8,128)(2,1)S(1)}, bf16[128,2048]{1,0:T(8,128)(2,1)}, u32[]{:S(2)}, u32[]{:S(2)}) collective-permute-start(bf16[128,2048]{1,0:T(8,128)(2,1)S(1)} %copy-done.11), channel_id=1, source_target_pairs={{0,8},{2,10},{4,12},{6,14},{8,16},{10,18},{12,20},{14,22},{16,24},... | collective-permute-start | bytes 1572872 | tf_op jit(solution)/shard_map/ppermute | solution.py:426
  202.0 12.5 %concatenate.69.refs_16_.refs_5_.refs_8_ = bf16[2048,1792]{1,0:T(8,128)(2,1)} concatenate(bf16[2048,704]{1,0:T(8,128)(2,1)} %bitcast.223, bf16[2048,64]{1,0:T(8,128)(2,1)S(1)} %broadcast.316, bf16[2048,704]{1,0:T(8,128)(2,1)} %bitcast.225, bf16[2048,64]{1,0:T(8,128)(2,1)S(1)} %broadcast.316, bf16[2048,88]{1,0:T(8,128)(2,1)} %bitcast.244, bf16[2048,88]{1,0:T(8,128)(2,1)} %bitcast.242, ...), dimensions={1} | concatenate | bytes 14680064 | tf_op jit(solution)/shard_map/concatenate | solution.py:939
  214.5 12.5 %concatenate.70.refs_17_.refs_6_.refs_9_ = bf16[2048,1792]{1,0:T(8,128)(2,1)} concatenate(bf16[2048,704]{1,0:T(8,128)(2,1)} %bitcast.222, bf16[2048,64]{1,0:T(8,128)(2,1)S(1)} %broadcast.316, bf16[2048,704]{1,0:T(8,128)(2,1)} %bitcast.224, bf16[2048,64]{1,0:T(8,128)(2,1)S(1)} %broadcast.316, bf16[2048,88]{1,0:T(8,128)(2,1)} %bitcast.243, bf16[2048,88]{1,0:T(8,128)(2,1)} %bitcast.241, ...), dimensions={1} | concatenate | bytes 14680064 | tf_op jit(solution)/shard_map/concatenate | solution.py:939
  278.7 9.0 collective-permute-done.50.refs_9_
  303.0 21.1 %collective-permute-done.52.refs_11_ = bf16[128,2048]{1,0:T(8,128)(2,1)S(1)} collective-permute-done((bf16[128,2048]{1,0:T(8,128)(2,1)S(1)}, bf16[128,2048]{1,0:T(8,128)(2,1)S(1)}, u32[]{:S(2)}, u32[]{:S(2)}) %collective-permute-start.52) | collective-permute-done | bytes 524320 | tf_op jit(solution)/shard_map/ppermute | solution.py:438
  324.0 11.2 %collective-permute-done.56.refs_15_ = bf16[128,2048]{1,0:T(8,128)(2,1)S(1)} collective-permute-done((bf16[128,2048]{1,0:T(8,128)(2,1)S(1)}, bf16[128,2048]{1,0:T(8,128)(2,1)S(1)}, u32[]{:S(2)}, u32[]{:S(2)}) %collective-permute-start.56) | collective-permute-done | bytes 524320 | tf_op jit(solution)/shard_map/ppermute | solution.py:438
  336.1 22.8 %shard_map.287 = (bf16[2048,1792]{1,0:T(8,128)(2,1)}, bf16[2048,2048]{1,0:T(8,128)(2,1)}) custom-call(bf16[128,2048]{1,0:T(8,128)(2,1)S(1)} %copy-done.11, bf16[128,2048]{1,0:T(8,128)(2,1)} %collective-permute-done.42.refs_1_, bf16[128,2048]{1,0:T(8,128)(2,1)} %collective-permute-done.43.refs_2_, bf16[128,2048]{1,0:T(8,128)(2,1)} %collective-permute-done.44.refs_3_, ...), custom_call_target="tpu_custom_call" | custom-call | flops 15032385536 | bytes 31457280 | tf_op jit(solution)/shard_map/pallas_call | solution.py:655
  368.8 9.7 collective-permute-done.36.refs_0_
  401.0 30.4 %shard_map.288 = (bf16[128,2048]{1,0:T(8,128)(2,1)S(1)}, bf16[128,2048]{1,0:T(8,128)(2,1)S(1)}, bf16[128,2048]{1,0:T(8,128)(2,1)S(1)}, bf16[128,2048]{1,0:T(8,12...) custom-call(s32[3]{0:T(128)S(1)} %pad_add_fusion.1.experts_ref, ...), custom_call_target="tpu_custom_call" | custom-call | flops 15032385536 | bytes 42991616 | tf_op jit(solution)/shard_map/pallas_call | solution.py:796
  436.3 28.9 %shard_map.289 = (bf16[128,2048]{1,0:T(8,128)(2,1)S(1)}, bf16[128,2048]{1,0:T(8,128)(2,1)S(1)}, bf16[128,2048]{1,0:T(8,128)(2,1)S(1)}, bf16[128,2048]{1,0:T(8,12...) custom-call(s32[3]{0:T(128)S(1)} %pad_add_fusion.1.experts_ref, ...), custom_call_target="tpu_custom_call", output_to_operand_aliasing={{4}: (12, {}), {5}: (13, {}), {6}: (14, {}), {7}: (15, {}),... | custom-call | flops 15032385536 | bytes 42991616 | tf_op jit(solution)/shard_map/pallas_call | solution.py:796
  470.2 7.9 collective-permute-done.59.refs_3_
  486.0 28.9 %shard_map.290 = (bf16[128,2048]{1,0:T(8,128)(2,1)S(1)}, bf16[128,2048]{1,0:T(8,128)(2,1)S(1)}, bf16[128,2048]{1,0:T(8,128)(2,1)S(1)}, bf16[128,2048]{1,0:T(8,12...) custom-call(s32[3]{0:T(128)S(1)} %pad_add_fusion.1.experts_ref, ...), custom_call_target="tpu_custom_call", output_to_operand_aliasing={{4}: (12, {}), {5}: (13, {}), {6}: (14, {}), {7}: (15, {}),... | custom-call | flops 15032385536 | bytes 42991616 | tf_op jit(solution)/shard_map/pallas_call | solution.py:796
  518.0 29.0 %shard_map.291 = (bf16[128,2048]{1,0:T(8,128)(2,1)S(1)}, bf16[128,2048]{1,0:T(8,128)(2,1)S(1)}, bf16[128,2048]{1,0:T(8,128)(2,1)S(1)}, bf16[128,2048]{1,0:T(8,12...) custom-call(s32[3]{0:T(128)S(1)} %pad_add_fusion.1.experts_ref, ...), custom_call_target="tpu_custom_call", output_to_operand_aliasing={{4}: (12, {}), {5}: (13, {}), {6}: (14, {}), {7}: (15, {}),... | custom-call | flops 15032385536 | bytes 42991616 | tf_op jit(solution)/shard_map/pallas_call | solution.py:796
  547.0 10.7 %convolution_convert_fusion.3 = bf16[2048,704]{0,1:T(8,128)(2,1)} fusion(bf16[2048,2048]{1,0:T(8,128)(2,1)} %get-tuple-element.121, bf16[2048,1792]{1,0:T(8,128)(2,1)} %get-tuple-element.123), kind=kOutput, calls=%fused_computation.13 | convolution fusion | flops 5907021824 | bytes 14417920 | tf_op jit(solution)/shard_map/dot_general | solution.py:615
  557.8 10.9 %convolution_convert_fusion.4 = bf16[2048,704]{0,1:T(8,128)(2,1)} fusion(bf16[2048,2048]{1,0:T(8,128)(2,1)} %get-tuple-element.121, bf16[2048,1792]{1,0:T(8,128)(2,1)} %get-tuple-element.122), kind=kOutput, calls=%fused_computation.14 | convolution fusion | flops 5907021824 | bytes 14417920 | tf_op jit(solution)/shard_map/dot_general | solution.py:615
  575.8 10.2 %convolution_convert_fusion.2 = bf16[704,2048]{1,0:T(8,128)(2,1)} fusion(bf16[2048,2048]{1,0:T(8,128)(2,1)} %get-tuple-element.125, bf16[2048,1792]{1,0:T(8,128)(2,1)S(1)} %bitcast.213), kind=kOutput, calls=%fused_computation.12 | convolution fusion | flops 5907021824 | bytes 14417920 | tf_op jit(solution)/shard_map/dot_general | solution.py:615
  586.1 9.5 fusion.119
  620.9 21.7 %shard_map.292 = (bf16[128,2048]{1,0:T(8,128)(2,1)S(1)}, bf16[128,2048]{1,0:T(8,128)(2,1)S(1)}, bf16[128,2048]{1,0:T(8,128)(2,1)S(1)}, bf16[128,2048]{1,0:T(8,12...) custom-call(bf16[2048,1792]{1,0:T(8,128)(2,1)} %get-tuple-element.94, ...), custom_call_target="tpu_custom_call" | custom-call | flops 15032385536 | bytes 23068672 | tf_op jit(solution)/shard_map/pallas_call | solution.py:693
  662.4 8.6 all-to-all-start.2
  677.9 10.7 %all-to-all-done.2 = bf16[16,256,88]{1,2,0:T(8,128)(2,1)} async-done(((bf16[16,256,88]{1,2,0:T(8,128)(2,1)}), bf16[16,256,88]{1,2,0:T(8,128)(2,1)}, u32[]{:S(2)}, u32[]{:S(2)}) %all-to-all-start.2) | async-done | bytes 720928 | tf_op jit(solution)/shard_map/all_to_all | solution.py:1125
  733.5 8.5 collective-permute-done.84
  807.4 12.4 %add_bitcast_fusion.1 = f32[1,2048,704]{1,2,0:T(8,128)} fusion(bf16[2048,704]{0,1:T(8,128)(2,1)} %collective-permute-done.124, bf16[2048,2048]{1,0:T(8,128)(2,1)} %get-tuple-element.121, bf16[2048,1792]{1,0:T(8,128)(2,1)} %get-tuple-element.123), kind=kOutput, calls=%fused_computation.6 | convolution fusion | flops 5908463616 | bytes 20185088 | tf_op jit(solution)/shard_map/dot_general | solution.py:615
  820.7 10.8 %add_bitcast_fusion.2 = f32[1,2048,704]{1,2,0:T(8,128)} fusion(bf16[2048,704]{0,1:T(8,128)(2,1)} %collective-permute-done.123, bf16[2048,2048]{1,0:T(8,128)(2,1)S(1)} %bitcast.217, bf16[2048,1792]{1,0:T(8,128)(2,1)} %get-tuple-element.122), kind=kOutput, calls=%fused_computation.7 | convolution fusion | flops 5908463616 | bytes 20185088 | tf_op jit(solution)/shard_map/dot_general | solution.py:615
  831.6 9.6 add_bitcast_fusion
  861.8 10.8 %maximum_bitcast_fusion = f32[1,2,2048,704]{2,3,1,0:T(8,128)} fusion(f32[1,2048,704]{1,2,0:T(8,128)} %add_bitcast_fusion.1, f32[1,2048,704]{1,2,0:T(8,128)} %add_bitcast_fusion.2), kind=kLoop, calls=%fused_computation | loop fusion | flops 2883584 | bytes 23068672 | tf_op jit(solution)/shard_map/broadcast_in_dim | solution.py:1099
  884.0 32.8 %collective-permute-done.105 = bf16[512,2112]{0,1:T(8,128)(2,1)} collective-permute-done((bf16[512,2112]{0,1:T(8,128)(2,1)}, bf16[512,2112]{0,1:T(8,128)(2,1)}, u32[]{:S(2)}, u32[]{:S(2)}) %collective-permute-start.105) | collective-permute-done | bytes 2162720 | tf_op jit(solution)/shard_map/ppermute | solution.py:430
  920.9 28.7 %collective-permute-done.116 = bf16[512,1024]{1,0:T(8,128)(2,1)S(1)} collective-permute-done((bf16[512,1024]{1,0:T(8,128)(2,1)S(1)}, bf16[512,1024]{1,0:T(8,128)(2,1)S(1)}, u32[]{:S(2)}, u32[]{:S(2)}) %collective-permute-start.116) | collective-permute-done | bytes 1048608 | tf_op jit(solution)/shard_map/ppermute | solution.py:430
  963.5 11.1 %collective-permute-done.107 = bf16[128,2112]{0,1:T(8,128)(2,1)S(1)} collective-permute-done((bf16[128,2112]{0,1:T(8,128)(2,1)S(1)}, bf16[128,2112]{0,1:T(8,128)(2,1)S(1)}, u32[]{:S(2)}, u32[]{:S(2)}) %collective-permute-start.107) | collective-permute-done | bytes 540704 | tf_op jit(solution)/shard_map/ppermute | solution.py:426
  977.5 8.1 collective-permute-done.118
  985.7 10.2 %collective-permute-done.108 = bf16[128,2112]{0,1:T(8,128)(2,1)S(1)} collective-permute-done((bf16[128,2112]{0,1:T(8,128)(2,1)S(1)}, bf16[128,2112]{0,1:T(8,128)(2,1)S(1)}, u32[]{:S(2)}, u32[]{:S(2)}) %collective-permute-start.108) | collective-permute-done | bytes 540704 | tf_op jit(solution)/shard_map/ppermute | solution.py:426
  (822 shorter events, 513.5 us)
Async XLA Ops:
  12.0 52.2 %collective-permute-start.2 = (bf16[128,2176]{1,0:T(8,128)(2,1)S(1)}, bf16[128,2176]{1,0:T(8,128)(2,1)S(1)}, u32[]{:S(2)}, u32[]{:S(2)}) collective-permute-start(bf16[128,2176]{1,0:T(8,128)(2,1)S(1)} %pad.17.refs_0_), channel_id=1, source_target_pairs={{0,4},{2,6},{4,0},{6,2},{8,12},{10,14},{12,8},{14,10},{16,20},{18,... | collective-permute-start | bytes 1671176 | tf_op jit(solution)/shard_map/ppermute | solution.py:430
  13.5 173.1 %collective-permute-start.16 = (bf16[2,2048,704]{1,2,0:T(8,128)(2,1)}, bf16[2,2048,704]{1,2,0:T(8,128)(2,1)}, u32[]{:S(2)}, u32[]{:S(2)}) collective-permute-start(bf16[2,2048,704]{1,2,0:T(8,128)(2,1)} %bitcast.230), channel_id=1, source_target_pairs={{0,2},{2,0},{4,6},{6,4},{8,10},{10,8},{12,14},{14,12},{16,18},{18,... | collective-permute-start | bytes 17301512 | tf_op jit(solution)/shard_map/ppermute | solution.py:434
  13.5 123.2 %collective-permute-start.18 = (bf16[704,2048]{1,0:T(8,128)(2,1)}, bf16[704,2048]{1,0:T(8,128)(2,1)}, u32[]{:S(2)}, u32[]{:S(2)}) collective-permute-start(bf16[704,2048]{1,0:T(8,128)(2,1)} %bitcast.240), channel_id=1, source_target_pairs={{0,2},{2,0},{4,6},{6,4},{8,10},{10,8},{12,14},{14,12},{16,18},{18,... | collective-permute-start | bytes 8650760 | tf_op jit(solution)/shard_map/ppermute | solution.py:434
  14.0 49.7 %collective-permute-start = (bf16[128,2048]{1,0:T(8,128)(2,1)S(1)}, bf16[128,2048]{1,0:T(8,128)(2,1)}, u32[]{:S(2)}, u32[]{:S(2)}) collective-permute-start(bf16[128,2048]{1,0:T(8,128)(2,1)S(1)} %copy-done.56), channel_id=1, source_target_pairs={{0,1},{1,0},{2,3},{3,2},{4,5},{5,4},{6,7},{7,6},{8,9},{9,8},{10,11... | collective-permute-start | bytes 1572872 | tf_op jit(solution)/shard_map/ppermute | solution.py:438
  55.1 48.5 %all-to-all-start = ((bf16[16,256,88]{1,2,0:T(8,128)(2,1)}), bf16[16,256,88]{1,2,0:T(8,128)(2,1)}, u32[]{:S(2)}, u32[]{:S(2)}) async-start(bf16[16,256,88]{1,2,0:T(8,128)(2,1)} %copy.284), calls=%async_computation | async-start | bytes 1441792 | tf_op jit(solution)/shard_map/all_to_all | solution.py:913
  177.9 49.7 %collective-permute-start.13 = (bf16[128,2176]{1,0:T(8,128)(2,1)S(1)}, bf16[128,2176]{1,0:T(8,128)(2,1)}, u32[]{:S(2)}, u32[]{:S(2)}) collective-permute-start(bf16[128,2176]{1,0:T(8,128)(2,1)S(1)} %copy-done.7), channel_id=1, source_target_pairs={{0,2},{2,0},{4,6},{6,4},{8,10},{10,8},{12,14},{14,12},{16,18},{18,... | collective-permute-start | bytes 1671176 | tf_op jit(solution)/shard_map/ppermute | solution.py:434
  177.9 49.1 %collective-permute-start.11 = (bf16[128,2176]{1,0:T(8,128)(2,1)}, bf16[128,2176]{1,0:T(8,128)(2,1)}, u32[]{:S(2)}, u32[]{:S(2)}) collective-permute-start(bf16[128,2176]{1,0:T(8,128)(2,1)} %collective-permute-done.10.refs_10_), channel_id=1, source_target_pairs={{0,2},{2,0},{4,6},{6,4},{8,10},{10,8},{12,14},{14,12},{16,18},{18,... | collective-permute-start | bytes 1671176 | tf_op jit(solution)/shard_map/ppermute | solution.py:434
  227.6 49.1 %collective-permute-start.46 = (bf16[128,2048]{1,0:T(8,128)(2,1)}, bf16[128,2048]{1,0:T(8,128)(2,1)}, u32[]{:S(2)}, u32[]{:S(2)}) collective-permute-start(bf16[128,2048]{1,0:T(8,128)(2,1)} %collective-permute-done.45.refs_4_), channel_id=1, source_target_pairs={{0,4},{2,6},{4,0},{6,2},{8,12},{10,14},{12,8},{14,10},{16,20},{18,... | collective-permute-start | bytes 1572872 | tf_op jit(solution)/shard_map/ppermute | solution.py:430
  229.0 48.3 %collective-permute-start.47 = (bf16[128,2048]{1,0:T(8,128)(2,1)}, bf16[128,2048]{1,0:T(8,128)(2,1)}, u32[]{:S(2)}, u32[]{:S(2)}) collective-permute-start(bf16[128,2048]{1,0:T(8,128)(2,1)} %collective-permute-done.45.refs_4_), channel_id=1, source_target_pairs={{0,1},{1,0},{2,3},{3,2},{4,5},{5,4},{6,7},{7,6},{8,9},{9,8},{10,11... | collective-permute-start | bytes 1572872 | tf_op jit(solution)/shard_map/ppermute | solution.py:438
  301.6 59.7 %collective-permute-start.35 = (bf16[128,2048]{1,0:T(8,128)(2,1)}, bf16[128,2048]{1,0:T(8,128)(2,1)}, u32[]{:S(2)}, u32[]{:S(2)}) collective-permute-start(bf16[128,2048]{1,0:T(8,128)(2,1)} %select_convert_fusion.1), channel_id=1, source_target_pairs={{0,1},{1,0},{2,3},{3,2},{4,5},{5,4},{6,7},{7,6},{8,9},{9,8},{10,11... | collective-permute-start | bytes 1572872 | tf_op jit(solution)/shard_map/ppermute | solution.py:438
  432.2 82.9 %collective-permute-start.68 = (bf16[128,2048]{1,0:T(8,128)(2,1)S(1)}, bf16[128,2048]{1,0:T(8,128)(2,1)S(1)}, u32[]{:S(2)}, u32[]{:S(2)}) collective-permute-start(bf16[128,2048]{1,0:T(8,128)(2,1)S(1)} %get-tuple-element.83.refs_15_), channel_id=1, source_target_pairs={{0,4},{2,6},{4,0},{6,2},{8,12},{10,14},{12,8},{14,10},{16,20},{18,... | collective-permute-start | bytes 1572872 | tf_op jit(solution)/shard_map/ppermute | solution.py:430
  435.5 48.2 %collective-permute-start.39 = (bf16[128,2048]{1,0:T(8,128)(2,1)S(1)}, bf16[128,2048]{1,0:T(8,128)(2,1)S(1)}, u32[]{:S(2)}, u32[]{:S(2)}) collective-permute-start(bf16[128,2048]{1,0:T(8,128)(2,1)S(1)} %collective-permute-done.38.refs_0_), channel_id=1, source_target_pairs={{0,4},{2,6},{4,0},{6,2},{8,12},{10,14},{12,8},{14,10},{16,20},{18,... | collective-permute-start | bytes 1572872 | tf_op jit(solution)/shard_map/ppermute | solution.py:430
  465.2 49.7 %collective-permute-start.67 = (bf16[128,2048]{1,0:T(8,128)(2,1)S(1)}, bf16[128,2048]{1,0:T(8,128)(2,1)S(1)}, u32[]{:S(2)}, u32[]{:S(2)}) collective-permute-start(bf16[128,2048]{1,0:T(8,128)(2,1)S(1)} %get-tuple-element.92), channel_id=1, source_target_pairs={{0,1},{1,0},{2,3},{3,2},{4,5},{5,4},{6,7},{7,6},{8,9},{9,8},{10,11... | collective-permute-start | bytes 1572872 | tf_op jit(solution)/shard_map/ppermute | solution.py:438
  468.8 48.4 %collective-permute-start.69 = (bf16[128,2048]{1,0:T(8,128)(2,1)S(1)}, bf16[128,2048]{1,0:T(8,128)(2,1)S(1)}, u32[]{:S(2)}, u32[]{:S(2)}) collective-permute-start(bf16[128,2048]{1,0:T(8,128)(2,1)S(1)} %add_convert_fusion.13.refs_16_), channel_id=1, source_target_pairs={{0,1},{1,0},{2,3},{3,2},{4,5},{5,4},{6,7},{7,6},{8,9},{9,8},{10,11... | collective-permute-start | bytes 1572872 | tf_op jit(solution)/shard_map/ppermute | solution.py:438
  514.9 56.4 %collective-permute-start.77 = (bf16[128,2048]{1,0:T(8,128)(2,1)S(1)}, bf16[128,2048]{1,0:T(8,128)(2,1)S(1)}, u32[]{:S(2)}, u32[]{:S(2)}) collective-permute-start(bf16[128,2048]{1,0:T(8,128)(2,1)S(1)} %get-tuple-element.93.refs_16_), channel_id=1, source_target_pairs={{0,1},{1,0},{2,3},{3,2},{4,5},{5,4},{6,7},{7,6},{8,9},{9,8},{10,11... | collective-permute-start | bytes 1572872 | tf_op jit(solution)/shard_map/ppermute | solution.py:438
  515.1 56.1 %collective-permute-start.76 = (bf16[128,2048]{1,0:T(8,128)(2,1)S(1)}, bf16[128,2048]{1,0:T(8,128)(2,1)S(1)}, u32[]{:S(2)}, u32[]{:S(2)}) collective-permute-start(bf16[128,2048]{1,0:T(8,128)(2,1)S(1)} %add_convert_fusion.12.refs_15_), channel_id=1, source_target_pairs={{0,4},{2,6},{4,0},{6,2},{8,12},{10,14},{12,8},{14,10},{16,20},{18,... | collective-permute-start | bytes 1572872 | tf_op jit(solution)/shard_map/ppermute | solution.py:430
  515.5 56.1 %collective-permute-start.74 = (bf16[128,2048]{1,0:T(8,128)(2,1)S(1)}, bf16[128,2048]{1,0:T(8,128)(2,1)S(1)}, u32[]{:S(2)}, u32[]{:S(2)}) collective-permute-start(bf16[128,2048]{1,0:T(8,128)(2,1)S(1)} %get-tuple-element.106), channel_id=1, source_target_pairs={{0,4},{2,6},{4,0},{6,2},{8,12},{10,14},{12,8},{14,10},{16,20},{18,... | collective-permute-start | bytes 1572872 | tf_op jit(solution)/shard_map/ppermute | solution.py:430
  517.2 84.2 %collective-permute-start.73 = (bf16[128,2048]{1,0:T(8,128)(2,1)S(1)}, bf16[128,2048]{1,0:T(8,128)(2,1)S(1)}, u32[]{:S(2)}, u32[]{:S(2)}) collective-permute-start(bf16[128,2048]{1,0:T(8,128)(2,1)S(1)} %get-tuple-element.104), channel_id=1, source_target_pairs={{0,4},{2,6},{4,0},{6,2},{8,12},{10,14},{12,8},{14,10},{16,20},{18,... | collective-permute-start | bytes 1572872 | tf_op jit(solution)/shard_map/ppermute | solution.py:430
  605.1 48.8 %collective-permute-start.120 = (bf16[2048,88]{0,1:T(8,128)(2,1)}, bf16[2048,88]{0,1:T(8,128)(2,1)}, u32[]{:S(2)}, u32[]{:S(2)}) collective-permute-start(bf16[2048,88]{0,1:T(8,128)(2,1)} %get-tuple-element.216), channel_id=1, source_target_pairs={{0,2},{2,0},{4,6},{6,4},{8,10},{10,8},{12,14},{14,12},{16,18},{18,... | collective-permute-start | bytes 1081352 | tf_op jit(solution)/shard_map/ppermute | solution.py:434
  605.3 48.6 %collective-permute-start.121 = (bf16[2048,88]{0,1:T(8,128)(2,1)}, bf16[2048,88]{0,1:T(8,128)(2,1)}, u32[]{:S(2)}, u32[]{:S(2)}) collective-permute-start(bf16[2048,88]{0,1:T(8,128)(2,1)} %get-tuple-element.217), channel_id=1, source_target_pairs={{0,2},{2,0},{4,6},{6,4},{8,10},{10,8},{12,14},{14,12},{16,18},{18,... | collective-permute-start | bytes 1081352 | tf_op jit(solution)/shard_map/ppermute | solution.py:434
  606.4 56.0 %all-to-all-start.3 = ((bf16[16,88,128]{2,1,0:T(8,128)(2,1)}), bf16[16,88,128]{2,1,0:T(8,128)(2,1)S(1)}, u32[]{:S(2)}, u32[]{:S(2)}) async-start(bf16[16,88,128]{2,1,0:T(8,128)(2,1)} %bitcast_bitcast_fusion), calls=%async_computation.3 | async-start | bytes 720896 | tf_op jit(solution)/shard_map/all_to_all | solution.py:1141
  620.9 50.2 %collective-permute-start.80 = (bf16[128,2048]{1,0:T(8,128)(2,1)}, bf16[128,2048]{1,0:T(8,128)(2,1)}, u32[]{:S(2)}, u32[]{:S(2)}) collective-permute-start(bf16[128,2048]{1,0:T(8,128)(2,1)} %add_convert_fusion.7), channel_id=1, source_target_pairs={{0,8},{2,10},{4,12},{6,14},{8,16},{10,18},{12,20},{14,22},{16,24},... | collective-permute-start | bytes 1572872 | tf_op jit(solution)/shard_map/ppermute | solution.py:426
  653.4 154.0 %collective-permute-start.124 = (bf16[2048,704]{0,1:T(8,128)(2,1)}, bf16[2048,704]{0,1:T(8,128)(2,1)}, u32[]{:S(2)}, u32[]{:S(2)}) collective-permute-start(bf16[2048,704]{0,1:T(8,128)(2,1)} %convolution_convert_fusion.3), channel_id=1, source_target_pairs={{0,2},{2,0},{4,6},{6,4},{8,10},{10,8},{12,14},{14,12},{16,18},{18,... | collective-permute-start | bytes 8650760 | tf_op jit(solution)/shard_map/ppermute | solution.py:434
  653.4 166.5 %collective-permute-start.123 = (bf16[2048,704]{0,1:T(8,128)(2,1)}, bf16[2048,704]{0,1:T(8,128)(2,1)}, u32[]{:S(2)}, u32[]{:S(2)}) collective-permute-start(bf16[2048,704]{0,1:T(8,128)(2,1)} %convolution_convert_fusion.4), channel_id=1, source_target_pairs={{0,2},{2,0},{4,6},{6,4},{8,10},{10,8},{12,14},{14,12},{16,18},{18,... | collective-permute-start | bytes 8650760 | tf_op jit(solution)/shard_map/ppermute | solution.py:434
  675.8 114.2 %collective-permute-start.92 = (bf16[128,2048]{1,0:T(8,128)(2,1)}, bf16[128,2048]{1,0:T(8,128)(2,1)}, u32[]{:S(2)}, u32[]{:S(2)}) collective-permute-start(bf16[128,2048]{1,0:T(8,128)(2,1)} %shard_map.300), channel_id=1, source_target_pairs={{0,1},{1,0},{2,3},{3,2},{4,5},{5,4},{6,7},{7,6},{8,9},{9,8},{10,11... | collective-permute-start | bytes 1572872 | tf_op jit(solution)/shard_map/ppermute | solution.py:438
  677.7 49.4 %collective-permute-start.90 = (bf16[128,2048]{1,0:T(8,128)(2,1)}, bf16[128,2048]{1,0:T(8,128)(2,1)}, u32[]{:S(2)}, u32[]{:S(2)}) collective-permute-start(bf16[128,2048]{1,0:T(8,128)(2,1)} %shard_map.299), channel_id=1, source_target_pairs={{0,1},{1,0},{2,3},{3,2},{4,5},{5,4},{6,7},{7,6},{8,9},{9,8},{10,11... | collective-permute-start | bytes 1572872 | tf_op jit(solution)/shard_map/ppermute | solution.py:438
  790.0 62.2 %collective-permute-start.89 = (bf16[128,2048]{1,0:T(8,128)(2,1)S(1)}, bf16[128,2048]{1,0:T(8,128)(2,1)}, u32[]{:S(2)}, u32[]{:S(2)}) collective-permute-start(bf16[128,2048]{1,0:T(8,128)(2,1)S(1)} %copy-done.33), channel_id=1, source_target_pairs={{0,1},{1,0},{2,3},{3,2},{4,5},{5,4},{6,7},{7,6},{8,9},{9,8},{10,11... | collective-permute-start | bytes 1572872 | tf_op jit(solution)/shard_map/ppermute | solution.py:438
  804.7 49.3 %collective-permute-start.88 = (bf16[128,2048]{1,0:T(8,128)(2,1)}, bf16[128,2048]{1,0:T(8,128)(2,1)}, u32[]{:S(2)}, u32[]{:S(2)}) collective-permute-start(bf16[128,2048]{1,0:T(8,128)(2,1)} %add_convert_fusion.4), channel_id=1, source_target_pairs={{0,4},{2,6},{4,0},{6,2},{8,12},{10,14},{12,8},{14,10},{16,20},{18,... | collective-permute-start | bytes 1572872 | tf_op jit(solution)/shard_map/ppermute | solution.py:430
  857.6 59.3 %collective-permute-start.105 = (bf16[512,2112]{0,1:T(8,128)(2,1)}, bf16[512,2112]{0,1:T(8,128)(2,1)}, u32[]{:S(2)}, u32[]{:S(2)}) collective-permute-start(bf16[512,2112]{0,1:T(8,128)(2,1)} %slice.603), channel_id=1, source_target_pairs={{0,4},{2,6},{4,0},{6,2},{8,12},{10,14},{12,8},{14,10},{16,20},{18,... | collective-permute-start | bytes 6488072 | tf_op jit(solution)/shard_map/ppermute | solution.py:430
  874.0 124.7 %collective-permute-start.83 = (bf16[128,2048]{1,0:T(8,128)(2,1)S(1)}, bf16[128,2048]{1,0:T(8,128)(2,1)S(1)}, u32[]{:S(2)}, u32[]{:S(2)}) collective-permute-start(bf16[128,2048]{1,0:T(8,128)(2,1)S(1)} %copy-done.31), channel_id=1, source_target_pairs={{0,1},{1,0},{2,3},{3,2},{4,5},{5,4},{6,7},{7,6},{8,9},{9,8},{10,11... | collective-permute-start | bytes 1572872 | tf_op jit(solution)/shard_map/ppermute | solution.py:438
  875.8 122.9 %collective-permute-start.82 = (bf16[128,2048]{1,0:T(8,128)(2,1)}, bf16[128,2048]{1,0:T(8,128)(2,1)S(1)}, u32[]{:S(2)}, u32[]{:S(2)}) collective-permute-start(bf16[128,2048]{1,0:T(8,128)(2,1)} %add_convert_fusion.6), channel_id=1, source_target_pairs={{0,4},{2,6},{4,0},{6,2},{8,12},{10,14},{12,8},{14,10},{16,20},{18,... | collective-permute-start | bytes 1572872 | tf_op jit(solution)/shard_map/ppermute | solution.py:430
  879.7 119.0 %collective-permute-start.95 = (bf16[128,2048]{1,0:T(8,128)(2,1)S(1)}, bf16[128,2048]{1,0:T(8,128)(2,1)S(1)}, u32[]{:S(2)}, u32[]{:S(2)}) collective-permute-start(bf16[128,2048]{1,0:T(8,128)(2,1)S(1)} %add_convert_fusion), channel_id=1, source_target_pairs={{0,8},{2,10},{4,12},{6,14},{8,16},{10,18},{12,20},{14,22},{16,24},... | collective-permute-start | bytes 1572872 | tf_op jit(solution)/shard_map/ppermute | solution.py:426
  (252 other events, 4140.8 us)

commit v4 on v3

--- a/solution.py
+++ b/solution.py
@@ -507,10 +507,10 @@
     return held
 
 
-def gather_weight(held):
+def gather_weight(held, others):
     chunks = []
     for distance, current in enumerate(held):
-        beside = other_y(current)
+        beside = other_y(after(current, *others) if distance == RINGS - 1 else current)
         for flip_y, chunk in ((0, current), (1, beside)):
             for flip_core, piece in ((0, chunk), (1, other_core(chunk))):
                 chunks.append(((distance, flip_y, flip_core), piece))
@@ -527,47 +527,6 @@
     )
 
 
-def place_kernel(keys, moves, outputs, coords_ref, *refs):
-    chunks = refs[: len(keys)]
-    outs = refs[-1 - outputs : -1]
-    semaphores = refs[-1]
-    coords = (coords_ref[0], coords_ref[1], coords_ref[2])
-    copies = []
-    for key, chunk in zip(keys, chunks):
-        block = place_of(coords, key)
-        for source_rows, source_columns, out, rows, columns in moves:
-            start = pl.multiple_of(block * rows, rows)
-            copies.append(
-                pltpu.make_async_copy(
-                    chunk.at[source_rows, source_columns],
-                    outs[out].at[pl.ds(start, rows), columns],
-                    semaphores.at[len(copies)],
-                )
-            )
-    for copy in copies:
-        copy.start()
-    for copy in copies:
-        copy.wait()
-
-
-def place_chunks(coords, chunks, moves, shapes, others=()):
-    keys = [key for key, _ in chunks]
-    anywhere = pl.BlockSpec(memory_space=pl.ANY)
-    return pl.pallas_call(
-        functools.partial(place_kernel, keys, moves, len(shapes)),
-        out_shape=[jax.ShapeDtypeStruct(shape, jnp.bfloat16) for shape in shapes],
-        in_specs=[pl.BlockSpec(memory_space=pltpu.SMEM)] + [anywhere] * (len(chunks) + len(others)),
-        out_specs=[pl.BlockSpec(memory_space=pltpu.VMEM)] * len(shapes),
-        scratch_shapes=[pltpu.SemaphoreType.DMA((len(chunks) * len(moves),))],
-        compiler_params=pltpu.CompilerParams(vmem_limit_bytes=24 * 1024 * 1024),
-        cost_estimate=pl.CostEstimate(
-            flops=0,
-            bytes_accessed=4 * sum(shape[0] * shape[1] for shape in shapes),
-            transcendentals=0,
-        ),
-    )(coords, *[piece for _, piece in chunks], *others)
-
-
 def weight_keys():
     return [
         (distance, flip_y, flip_core)
@@ -594,15 +553,6 @@
     return jnp.sum(jnp.where(chosen, values[None], 0.0), axis=1)
 
 
-def attend_forward(query_rows, key_nope, key_rope, values, allowed, scale):
-    scores = attention_scores(query_rows, key_nope, key_rope, allowed, scale)
-    row_max = jnp.max(scores, axis=-1, keepdims=True)
-    log_total = row_max + jnp.log(jnp.sum(jnp.exp(scores - row_max), axis=-1, keepdims=True))
-    weights_low = jnp.exp(scores - log_total).astype(jnp.bfloat16)
-    attended = jnp.einsum("hij,jhd->ihd", weights_low, values, preferred_element_type=jnp.float32)
-    return attended.astype(jnp.bfloat16), log_total
-
-
 def wide_dot(left, right):
     return jnp.dot(left, right, preferred_element_type=jnp.float32)
 
@@ -619,7 +569,497 @@
 
 
 def whole(array):
-    return pl.BlockSpec(array.shape, lambda i: (0,) * array.ndim)
+    return pl.BlockSpec(array.shape, lambda *i: (0,) * array.ndim)
+
+
+def in_vmem(count):
+    return [pl.BlockSpec(memory_space=pltpu.VMEM)] * count
+
+
+def in_place(count):
+    return [pl.BlockSpec(memory_space=pl.ANY)] * count
+
+
+def head_scores(heads, h, nope_ref, turned_ref, keyval_ref, key_ref, masks):
+    span = ROPE // 2 * heads
+    column = pl.ds(pl.multiple_of(h * NOPE, NOPE), NOPE)
+    key_column = pl.ds(pl.multiple_of(h * (NOPE + VD), NOPE), NOPE)
+    scores = dot_turned(nope_ref[:, column], keyval_ref[:, key_column])
+    for k in (0, 1):
+        part = turned_ref[:, k * span : (k + 1) * span]
+        part = jnp.where(masks, part, jnp.zeros_like(part))
+        scores += dot_turned(part, key_ref[:, k * span : (k + 1) * span])
+    return scores * (NOPE + ROPE) ** (-0.5)
+
+
+def head_lanes(heads, h):
+    span = ROPE // 2 * heads
+    lane = lax.broadcasted_iota(jnp.int32, (1, span), 1)
+    return (lane >= h * (ROPE // 2)) & (lane < (h + 1) * (ROPE // 2))
+
+
+def allowed_rows(count, segment_row, segment_column):
+    tokens = segment_row.shape[1]
+    column = lax.broadcasted_iota(jnp.int32, (tokens, tokens), 0)
+    row = lax.broadcasted_iota(jnp.int32, (tokens, tokens), 1)
+    live = (column < count) & (row < count) & (row <= column)
+    return (segment_row == segment_column) & live | (column == row)
+
+
+def attend_kernel(
+    keys,
+    heads,
+    sizes,
+    place_ref,
+    segment_row_ref,
+    segment_column_ref,
+    cosine_ref,
+    sine_ref,
+    own_ref,
+    other_ref,
+    *refs,
+):
+    depth, query_width, used, latent_depth, keyval_part, first_width = sizes
+    chunks = refs[: len(keys)]
+    (
+        own_out,
+        sent_out,
+        first_ref,
+        keyval_weight_ref,
+        output_ref,
+        normed_ref,
+        nope_ref,
+        turned_ref,
+        latent_ref,
+        key_ref,
+        keyval_ref,
+        total_ref,
+        attended_ref,
+        gains_ref,
+        latent_gain_ref,
+        semaphores,
+    ) = refs[len(keys) :]
+    f32, bf16 = jnp.float32, jnp.bfloat16
+    local_rows = own_ref.shape[0]
+    tokens = 2 * local_rows
+    coords = (place_ref[0], place_ref[1], place_ref[2])
+    x = place_ref[3]
+    copies = []
+    parts = depth // latent_depth
+    for key, chunk in zip(keys, chunks):
+        block = place_of(coords, key)
+        rows = pl.ds(pl.multiple_of(block * depth, depth), depth)
+        small_rows = pl.ds(pl.multiple_of(block * latent_depth, latent_depth), latent_depth)
+        moves = [(chunk.at[:, pl.ds(0, first_width)], first_ref.at[rows])]
+        for k in range(parts):
+            moves.append(
+                (
+                    chunk.at[
+                        pl.ds(k * latent_depth, latent_depth), pl.ds(first_width, keyval_part)
+                    ],
+                    keyval_weight_ref.at[small_rows, pl.ds(k * keyval_part, keyval_part)],
+                )
+            )
+        moves.append(
+            (
+                chunk.at[:, pl.ds(first_width + keyval_part, heads * VD)],
+                output_ref.at[rows],
+            )
+        )
+        for source, target in moves:
+            copies.append(pltpu.make_async_copy(source, target, semaphores.at[len(copies)]))
+    for copy in copies:
+        copy.start()
+    for copy in copies:
+        copy.wait()
+
+    edge = query_width + KVR
+    spread = jnp.transpose(first_ref[:, edge:].astype(f32))[used - edge : used - edge + 8]
+    gains_ref[...] = spread
+    gain = spread[0:1]
+    source = lax.broadcasted_iota(jnp.int32, (D, KVR), 0)
+    target = lax.broadcasted_iota(jnp.int32, (D, KVR), 1)
+    wanted = target // latent_depth * depth + target % latent_depth
+    chosen = jnp.where(source == wanted, 1.0, 0.0).astype(bf16)
+    latent_gain = wide_dot(spread.astype(bf16), chosen)[2:3]
+    latent_gain_ref[...] = latent_gain
+    for ref, start in ((own_ref, x * local_rows), (other_ref, (1 - x) * local_rows)):
+        rows = ref[...].astype(f32)
+        unit = rows * lax.rsqrt(jnp.mean(rows * rows, axis=1, keepdims=True) + EPSILON)
+        normed_ref[pl.ds(pl.multiple_of(start, local_rows), local_rows), :] = (unit * gain).astype(
+            bf16
+        )
+    nope_width = heads * NOPE
+    span = heads * (ROPE // 2)
+    half = nope_width // 2
+    for k in (0, 1):
+        nope_ref[:, k * half : (k + 1) * half] = wide_dot(
+            normed_ref[...], first_ref[:, k * half : (k + 1) * half]
+        ).astype(bf16)
+    turning = wide_dot(normed_ref[...], first_ref[:, nope_width : nope_width + 2 * span])
+    cosine, sine = cosine_ref[...], sine_ref[...]
+    first, second = turning[:, :span], turning[:, span:]
+    turned_ref[:, :span] = (first * cosine - second * sine).astype(bf16)
+    turned_ref[:, span:] = (second * cosine + first * sine).astype(bf16)
+    latent = wide_dot(normed_ref[...], first_ref[:, query_width : query_width + KVR])
+    latent_ref[...] = latent
+    tail = wide_dot(normed_ref[...], first_ref[:, query_width + KVR :])
+    lane = lax.broadcasted_iota(jnp.int32, (1, tail.shape[1]), 1)
+    swapped = jnp.where(
+        lane < ROPE // 2,
+        -pltpu.roll(tail, tail.shape[1] - ROPE // 2, 1),
+        pltpu.roll(tail, ROPE // 2, 1),
+    )
+    width = tail.shape[1]
+    turned_key = tail * cosine[:, :width] + swapped * sine[:, :width]
+    turned_key = jnp.where(lane < ROPE, turned_key, 0.0).astype(bf16)
+    source = lax.broadcasted_iota(jnp.int32, (width, 2 * span), 0)
+    target = lax.broadcasted_iota(jnp.int32, (width, 2 * span), 1)
+    wanted = target % (ROPE // 2) + jnp.where(target < span, 0, ROPE // 2)
+    key_ref[...] = wide_dot(turned_key, (source == wanted).astype(bf16)).astype(bf16)
+    unit = latent * lax.rsqrt(jnp.mean(latent * latent, axis=1, keepdims=True) + EPSILON)
+    latent_normed = (unit * latent_gain).astype(bf16)
+    half = keyval_ref.shape[1] // 4
+    for k in range(4):
+        keyval_ref[:, k * half : (k + 1) * half] = wide_dot(
+            latent_normed, keyval_weight_ref[:, k * half : (k + 1) * half]
+        ).astype(bf16)
+    allowed = allowed_rows(place_ref[4], segment_row_ref[...], segment_column_ref[...])
+    total_lane = lax.broadcasted_iota(jnp.int32, total_ref.shape, 1)
+    total_ref[...] = jnp.zeros_like(total_ref)
+
+    def one_head(h, _):
+        scores = head_scores(
+            heads, h, nope_ref, turned_ref, keyval_ref, key_ref, head_lanes(heads, h)
+        )
+        scores = jnp.where(allowed, scores, -1e30)
+        most = jnp.max(scores, axis=1, keepdims=True)
+        total = most + jnp.log(jnp.sum(jnp.exp(scores - most), axis=1, keepdims=True))
+        weights = jnp.exp(scores - total).astype(bf16)
+        total_ref[...] += jnp.where(total_lane == h, total, 0.0)
+        value_column = pl.ds(pl.multiple_of(h * (NOPE + VD) + NOPE, NOPE), VD)
+        attended_ref[:, pl.ds(pl.multiple_of(h * VD, VD), VD)] = wide_dot(
+            weights, keyval_ref[:, value_column]
+        ).astype(bf16)
+        return 0
+
+    lax.fori_loop(0, heads, one_head, 0)
+    own = pl.ds(pl.multiple_of(x * local_rows, local_rows), local_rows)
+    other = pl.ds(pl.multiple_of((1 - x) * local_rows, local_rows), local_rows)
+    pieces = 4
+    size = output_ref.shape[0] // pieces
+    for k in range(pieces):
+        columns = slice(k * size, (k + 1) * size)
+        own_out[:, columns] = dot_turned(attended_ref[own, :], output_ref[columns, :])
+        sent_out[:, columns] = dot_turned(attended_ref[other, :], output_ref[columns, :]).astype(
+            bf16
+        )
+
+
+def attend_forward(place, segments, cosine, sine, own, other, chunks, heads, sizes):
+    depth, query_width, used, latent_depth, keyval_part, first_width = sizes
+    f32, bf16 = jnp.float32, jnp.bfloat16
+    keys = [key for key, _ in chunks]
+    local_rows = own.shape[0]
+    tokens = 2 * local_rows
+    span = heads * (ROPE // 2)
+    shapes = [
+        ((local_rows, D), f32),
+        ((local_rows, D), bf16),
+        ((D, first_width), bf16),
+        ((KVR, heads * (NOPE + VD)), bf16),
+        ((D, heads * VD), bf16),
+        ((tokens, D), bf16),
+        ((tokens, heads * NOPE), bf16),
+        ((tokens, 2 * span), bf16),
+        ((tokens, KVR), f32),
+        ((tokens, 2 * span), bf16),
+        ((tokens, heads * (NOPE + VD)), bf16),
+        ((tokens, 128), f32),
+        ((tokens, heads * VD), bf16),
+        ((8, D), f32),
+        ((1, KVR), f32),
+    ]
+    return pl.pallas_call(
+        functools.partial(attend_kernel, keys, heads, sizes),
+        out_shape=[jax.ShapeDtypeStruct(*shape) for shape in shapes],
+        in_specs=[pl.BlockSpec(memory_space=pltpu.SMEM)] + in_vmem(6) + in_place(len(chunks)),
+        out_specs=in_vmem(len(shapes)),
+        scratch_shapes=[
+            pltpu.SemaphoreType.DMA((len(chunks) * (2 + depth // latent_depth),))
+        ],
+        compiler_params=pltpu.CompilerParams(vmem_limit_bytes=48 * 1024 * 1024),
+        cost_estimate=pl.CostEstimate(
+            flops=2 * tokens * D * (first_width + heads * VD + 1024),
+            bytes_accessed=4 * D * (first_width + 1536),
+            transcendentals=2 * heads * tokens * tokens,
+        ),
+    )(place, segments, segments.T, cosine, sine, own, other, *[piece for _, piece in chunks])
+
+
+def attend_back_kernel(
+    heads,
+    place_ref,
+    segment_row_ref,
+    segment_column_ref,
+    cosine_ref,
+    sine_ref,
+    own_ref,
+    other_ref,
+    keyval_weight_ref,
+    output_ref,
+    nope_ref,
+    turned_ref,
+    latent_ref,
+    key_ref,
+    keyval_ref,
+    total_ref,
+    latent_gain_ref,
+    projected_ref,
+    keyval_grad_ref,
+    latent_out,
+    gain_ref,
+    grad_ref,
+    turn_ref,
+    back_ref,
+):
+    f32, bf16 = jnp.float32, jnp.bfloat16
+    local_rows = own_ref.shape[0]
+    x = place_ref[3]
+    span = heads * (ROPE // 2)
+    nope_width = heads * NOPE
+    query_width = nope_width + 2 * span
+    scale = (NOPE + ROPE) ** (-0.5)
+    for ref, start in ((own_ref, x * local_rows), (other_ref, (1 - x) * local_rows)):
+        rows = pl.ds(pl.multiple_of(start, local_rows), local_rows)
+        for k in (0, 1):
+            half = slice(k * nope_width // 2, (k + 1) * nope_width // 2)
+            grad_ref[rows, half] = wide_dot(ref[...], output_ref[:, half]).astype(bf16)
+    allowed = allowed_rows(place_ref[4], segment_row_ref[...], segment_column_ref[...])
+    total_lane = lax.broadcasted_iota(jnp.int32, total_ref.shape, 1)
+    turn_ref[...] = jnp.zeros_like(turn_ref)
+    back_ref[...] = jnp.zeros_like(back_ref)
+
+    def one_head(h, _):
+        mask = head_lanes(heads, h)
+        scores = head_scores(heads, h, nope_ref, turned_ref, keyval_ref, key_ref, mask)
+        total = jnp.sum(jnp.where(total_lane == h, total_ref[...], 0.0), axis=1, keepdims=True)
+        weights = jnp.exp(jnp.where(allowed, scores, -1e30) - total)
+        weights_low = weights.astype(bf16)
+        column = pl.ds(pl.multiple_of(h * NOPE, NOPE), NOPE)
+        key_column = pl.ds(pl.multiple_of(h * (NOPE + VD), NOPE), NOPE)
+        value_column = pl.ds(pl.multiple_of(h * (NOPE + VD) + NOPE, NOPE), VD)
+        grads = grad_ref[:, column]
+        grad_weights = dot_turned(grads, keyval_ref[:, value_column])
+        keyval_grad_ref[:, value_column] = dot_rows(weights_low, grads).astype(bf16)
+        grad_scores = (
+            weights * (grad_weights - jnp.sum(weights * grad_weights, axis=1, keepdims=True))
+        ).astype(bf16)
+        projected_ref[:, column] = (
+            scale * wide_dot(grad_scores, keyval_ref[:, key_column])
+        ).astype(bf16)
+        keyval_grad_ref[:, key_column] = (
+            scale * dot_rows(grad_scores, nope_ref[:, column])
+        ).astype(bf16)
+        for k in (0, 1):
+            part = slice(k * span, (k + 1) * span)
+            turn = wide_dot(grad_scores, key_ref[:, part])
+            turn_ref[:, part] += jnp.where(mask, turn, 0.0)
+            own = turned_ref[:, part]
+            own = jnp.where(mask, own, jnp.zeros_like(own))
+            back_ref[:, part] += dot_rows(grad_scores, own)
+        return 0
+
+    lax.fori_loop(0, heads, one_head, 0)
+    cosine, sine = cosine_ref[...], sine_ref[...]
+    first, second = scale * turn_ref[:, :span], scale * turn_ref[:, span:]
+    projected_ref[:, nope_width : nope_width + span] = (first * cosine + second * sine).astype(bf16)
+    projected_ref[:, nope_width + span : query_width] = (second * cosine - first * sine).astype(
+        bf16
+    )
+    folded = []
+    for k in (0, 1):
+        part = scale * back_ref[:, k * span : (k + 1) * span]
+        shift = span // 2
+        while shift >= ROPE // 2:
+            part = part + pltpu.roll(part, shift, 1)
+            shift //= 2
+        folded.append(part)
+    width = projected_ref.shape[1] - query_width - KVR
+    lane = lax.broadcasted_iota(jnp.int32, (1, width), 1)
+    first = (folded[0] * cosine + folded[1] * sine)[:, :width]
+    second = (folded[1] * cosine - folded[0] * sine)[:, :width]
+    projected_ref[:, query_width + KVR :] = jnp.where(
+        lane < ROPE // 2, first, jnp.where(lane < ROPE, second, 0.0)
+    ).astype(bf16)
+    gain = latent_gain_ref[...]
+    latent = latent_ref[...]
+    row_scale = lax.rsqrt(jnp.mean(latent * latent, axis=1, keepdims=True) + EPSILON)
+    unit = latent * row_scale
+    latent_out[...] = (unit * gain).astype(bf16)
+    grad_normed = dot_turned(keyval_grad_ref[...], keyval_weight_ref[...])
+    gain_ref[...] = jnp.sum(grad_normed * unit, axis=0, keepdims=True)
+    grad_unit = grad_normed * gain
+    projected_ref[:, query_width : query_width + KVR] = (
+        row_scale * (grad_unit - unit * jnp.mean(grad_unit * unit, axis=1, keepdims=True))
+    ).astype(bf16)
+
+
+def attend_back(place, segments, cosine, sine, own, other, saved, heads, first_width):
+    f32, bf16 = jnp.float32, jnp.bfloat16
+    keyval = saved[6]
+    tokens = 2 * own.shape[0]
+    span = heads * (ROPE // 2)
+    return pl.pallas_call(
+        functools.partial(attend_back_kernel, heads),
+        out_shape=[
+            jax.ShapeDtypeStruct((tokens, first_width), bf16),
+            jax.ShapeDtypeStruct((tokens, keyval.shape[1]), bf16),
+            jax.ShapeDtypeStruct((tokens, KVR), bf16),
+            jax.ShapeDtypeStruct((1, KVR), f32),
+        ],
+        in_specs=[pl.BlockSpec(memory_space=pltpu.SMEM)] + in_vmem(15),
+        out_specs=in_vmem(4),
+        scratch_shapes=[
+            pltpu.VMEM((tokens, heads * NOPE), bf16),
+            pltpu.VMEM((tokens, 2 * span), f32),
+            pltpu.VMEM((tokens, 2 * span), f32),
+        ],
+        compiler_params=pltpu.CompilerParams(vmem_limit_bytes=48 * 1024 * 1024),
+        cost_estimate=pl.CostEstimate(
+            flops=2 * tokens * D * 3000,
+            bytes_accessed=2 * D * 1536,
+            transcendentals=heads * tokens * tokens,
+        ),
+    )(
+        place,
+        segments,
+        segments.T,
+        cosine,
+        sine,
+        own,
+        other,
+        *saved,
+    )
+
+
+def block_grads_kernel(places_ref, left_ref, right_ref, *refs):
+    result = dot_rows(left_ref[...], right_ref[...])
+    if len(refs) > 1:
+        result += refs[0][...].astype(jnp.float32)
+    refs[-1][...] = result.astype(jnp.bfloat16)
+
+
+def block_grads(left, right, places, first, count, arrived=None, others=()):
+    rows, width = right.shape
+    size = left.shape[1] // places.shape[0]
+    block = pl.BlockSpec((size, width), lambda i, where: (i, 0))
+    extra = [] if arrived is None else [arrived]
+    return pl.pallas_call(
+        lambda places_ref, left_ref, right_ref, *refs: block_grads_kernel(
+            places_ref, left_ref, right_ref, *refs[: len(extra)], refs[-1]
+        ),
+        grid_spec=pltpu.PrefetchScalarGridSpec(
+            num_scalar_prefetch=1,
+            grid=(count,),
+            in_specs=[
+                pl.BlockSpec((rows, size), lambda i, where: (0, where[first + i])),
+                pl.BlockSpec((rows, width), lambda i, where: (0, 0)),
+            ]
+            + [pl.BlockSpec((size, width), lambda i, where: (first + i, 0))] * len(extra)
+            + [pl.BlockSpec(memory_space=pl.ANY)] * len(others),
+            out_specs=block,
+        ),
+        out_shape=jax.ShapeDtypeStruct((count * size, width), jnp.bfloat16),
+        cost_estimate=pl.CostEstimate(
+            flops=2 * rows * count * size * width,
+            bytes_accessed=2 * (count * size * width + rows * width),
+            transcendentals=0,
+        ),
+    )(places, left, right, *extra, *others)
+
+
+def close_ring(near, arrived):
+    size = near.shape[0] // RINGS
+    total = near.astype(jnp.float32) + arrived.astype(jnp.float32)
+    return ring_sum([total[r * size : (r + 1) * size] for r in range(RINGS)], jnp.bfloat16)
+
+
+def scatter_product(left, right, places):
+    sent = block_grads(left, right, places, 2 * RINGS, 2 * RINGS)
+    arrived = other_core(sent)
+    far = block_grads(left, right, places, RINGS, RINGS, arrived)
+    from_y = other_y(far)
+    near = block_grads(left, right, places, 0, RINGS, arrived)
+    return close_ring(near, from_y)
+
+
+def latent_blocks_kernel(places_ref, left_ref, right_ref, out_ref, whole_ref):
+    blocks = places_ref.shape[0]
+    size = left_ref.shape[1] // blocks
+    pieces = 4
+    part = right_ref.shape[1] // pieces
+    for k in range(pieces):
+        columns = slice(k * part, (k + 1) * part)
+        whole_ref[:, columns] = dot_rows(left_ref[...], right_ref[:, columns])
+    for k in range(blocks):
+        start = pl.multiple_of(places_ref[k] * size, size)
+        out_ref[k * size : (k + 1) * size, :] = whole_ref[pl.ds(start, size), :].astype(
+            jnp.bfloat16
+        )
+
+
+def latent_blocks(left, right, places):
+    shape = (left.shape[1], right.shape[1])
+    return pl.pallas_call(
+        latent_blocks_kernel,
+        out_shape=jax.ShapeDtypeStruct(shape, jnp.bfloat16),
+        in_specs=[pl.BlockSpec(memory_space=pltpu.SMEM)] + in_vmem(2),
+        out_specs=pl.BlockSpec(memory_space=pltpu.VMEM),
+        scratch_shapes=[pltpu.VMEM(shape, jnp.float32)],
+        compiler_params=pltpu.CompilerParams(vmem_limit_bytes=32 * 1024 * 1024),
+    )(places, left, right)
+
+
+def pack_kernel(heads, query_ref, latent_ref, small_ref, keyval_ref, output_ref, out_ref):
+    half = ROPE // 2
+    head = NOPE + ROPE
+    nope_width = heads * NOPE
+    for h in range(heads):
+        start = h * head
+        out_ref[:, h * NOPE : (h + 1) * NOPE] = query_ref[:, start : start + NOPE]
+        for k in (0, 1):
+            to = nope_width + k * heads * half + h * half
+            out_ref[:, to : to + half] = query_ref[
+                :, start + NOPE + k * half : start + NOPE + (k + 1) * half
+            ]
+    at = heads * head
+    edge = at + KVR
+    out_ref[:, at:edge] = latent_ref[:, :KVR]
+    out_ref[:, edge : edge + 128] = jnp.concatenate([latent_ref[:, KVR:], small_ref[...]], axis=1)
+    at = edge + 128
+    size = keyval_ref.shape[0]
+    parts = out_ref.shape[0] // size
+    part = keyval_ref.shape[1] // parts
+    for k in range(parts):
+        out_ref[k * size : (k + 1) * size, at : at + part] = keyval_ref[
+            :, k * part : (k + 1) * part
+        ]
+    out_ref[:, at + part :] = jnp.transpose(output_ref[...].astype(jnp.float32)).astype(
+        jnp.bfloat16
+    )
+
+
+def pack_weights(query, latent, small, keyval, output):
+    depth, query_width = query.shape
+    heads = query_width // (NOPE + ROPE)
+    width = query_width + KVR + 128 + keyval.size // depth + output.shape[0]
+    return pl.pallas_call(
+        functools.partial(pack_kernel, heads),
+        out_shape=jax.ShapeDtypeStruct((depth, width), jnp.bfloat16),
+        in_specs=in_vmem(5),
+        out_specs=pl.BlockSpec(memory_space=pltpu.VMEM),
+    )(query, latent, small, keyval, output)
 
 
 def load_pieces(pieces, target, semaphores):
@@ -632,6 +1072,109 @@
         copy.start()
     for copy in copies:
         copy.wait()
+
+
+def pack_sides_kernel(units, shared, own_ref, other_ref, near_ref, far_ref, *refs):
+    gate_out, up_out = refs[-2:]
+    hole = -(-units // TILE) * TILE
+    rows = gate_out.shape[0]
+    gap = -(-shared // 32) * 32
+    for k, out in ((0, gate_out), (1, up_out)):
+        part = slice(k * rows, (k + 1) * rows)
+        out[:, :units] = own_ref[0, k]
+        out[:, units:hole] = jnp.zeros((rows, hole - units), jnp.bfloat16)
+        out[:, hole : hole + units] = other_ref[0, k]
+        out[:, hole + units : 2 * hole] = jnp.zeros((rows, hole - units), jnp.bfloat16)
+        out[:, 2 * hole :] = jnp.zeros((rows, TILE), jnp.bfloat16)
+        out[:, 2 * hole : 2 * hole + shared] = near_ref[0, part]
+        out[:, 2 * hole + gap : 2 * hole + gap + shared] = far_ref[0, part]
+
+
+def pack_sides(own, other, near, far, others):
+    depth, units = own.shape[2:]
+    blocks, rows, shared = near.shape
+    rows //= 2
+    width = 2 * (-(-units // TILE) * TILE) + TILE
+    wide = pl.BlockSpec((1, 2, rows, units), lambda i: (0, 0, i, 0))
+    narrow = pl.BlockSpec((1, 2 * rows, shared), lambda i: (i, 0, 0))
+    out = pl.BlockSpec((rows, width), lambda i: (i, 0))
+    return pl.pallas_call(
+        functools.partial(pack_sides_kernel, units, shared),
+        grid=(blocks,),
+        in_specs=[wide, wide, narrow, narrow] + in_place(len(others)),
+        out_specs=[out, out],
+        out_shape=[jax.ShapeDtypeStruct((depth, width), jnp.bfloat16)] * 2,
+        compiler_params=pltpu.CompilerParams(vmem_limit_bytes=32 * 1024 * 1024),
+    )(own, other, near, far, *others)
+
+
+def pack_down_kernel(units, shared, own_ref, other_ref, near_ref, far_ref, *refs):
+    out = refs[-1]
+    hole = -(-units // TILE) * TILE
+    columns = out.shape[1]
+    gap = -(-shared // 32) * 32
+    out[:units] = own_ref[0]
+    out[units:hole] = jnp.zeros((hole - units, columns), jnp.bfloat16)
+    out[hole : hole + units] = other_ref[0]
+    out[hole + units : 2 * hole] = jnp.zeros((hole - units, columns), jnp.bfloat16)
+    out[2 * hole :] = jnp.zeros((TILE, columns), jnp.bfloat16)
+    size = near_ref.shape[2]
+    for k in range(columns // size):
+        part = slice(k * size, (k + 1) * size)
+        out[2 * hole : 2 * hole + shared, part] = near_ref[k]
+        out[2 * hole + gap : 2 * hole + gap + shared, part] = far_ref[k]
+
+
+def pack_down(own, other, near, far, others):
+    units, depth = own.shape[1:]
+    blocks, shared, size = near.shape
+    height = 2 * (-(-units // TILE) * TILE) + TILE
+    columns = 4 * size
+    wide = pl.BlockSpec((1, units, columns), lambda i: (0, 0, i))
+    narrow = pl.BlockSpec((4, shared, size), lambda i: (i, 0, 0))
+    return pl.pallas_call(
+        functools.partial(pack_down_kernel, units, shared),
+        grid=(depth // columns,),
+        in_specs=[wide, wide, narrow, narrow] + in_place(len(others)),
+        out_specs=pl.BlockSpec((height, columns), lambda i: (0, i)),
+        out_shape=jax.ShapeDtypeStruct((height, depth), jnp.bfloat16),
+        compiler_params=pltpu.CompilerParams(vmem_limit_bytes=32 * 1024 * 1024),
+    )(own, other, near, far, *others)
+
+
+def expert_grads_kernel(units, extra, rows_ref, gate_ref, up_ref, *refs):
+    out = refs[-1]
+    for k, grads in ((0, gate_ref), (1, up_ref)):
+
+        @pl.when(pl.program_id(0) == k)
+        def _():
+            result = dot_rows(rows_ref[...], grads[...])[:, :units]
+            if extra:
+                result += refs[0][0, 0].astype(jnp.float32)
+            out[0, 0] = result.astype(out.dtype)
+
+
+def expert_grads(rows, gate, up, units, column, arrived, kind, others=()):
+    total, depth = rows.shape
+    wide = -(-units // TILE) * TILE
+    extra = [] if arrived is None else [arrived]
+    out = pl.BlockSpec((1, 1, 2 * TILE, units), lambda k, i: (0, k, i, 0))
+    side = pl.BlockSpec((total, wide), lambda k, i: (0, column))
+    return pl.pallas_call(
+        functools.partial(expert_grads_kernel, units, len(extra)),
+        grid=(2, depth // (2 * TILE)),
+        in_specs=[pl.BlockSpec((total, 2 * TILE), lambda k, i: (0, i)), side, side]
+        + [out] * len(extra)
+        + in_place(len(others)),
+        out_specs=out,
+        out_shape=jax.ShapeDtypeStruct((1, 2, depth, units), kind),
+        compiler_params=pltpu.CompilerParams(vmem_limit_bytes=48 * 1024 * 1024),
+        cost_estimate=pl.CostEstimate(
+            flops=4 * total * depth * wide,
+            bytes_accessed=4 * total * (depth + wide) + 8 * depth * units,
+            transcendentals=0,
+        ),
+    )(rows, gate, up, *extra, *others)
 
 
 def down_kernel(count, *refs):
@@ -716,13 +1259,13 @@
     third = tiles // 2
     total = rows_out.shape[0]
     size = total // pieces
-    lane = lax.broadcasted_iota(jnp.int32, (1, router_ref.shape[1]), 1)
+    lane = lax.broadcasted_iota(jnp.int32, (1, router_ref.shape[1]), 1) - experts_ref[3]
 
     @pl.when(step == 0)
     def _():
         load_pieces(row_refs, rows_out, semaphores)
         logits = wide_dot(rows_out[...], router_ref[...])
-        logits = jnp.where(lane < experts_ref[2], logits, -1e30)
+        logits = jnp.where((lane >= 0) & (lane < experts_ref[2]), logits, -1e30)
         raised = jnp.exp(logits - jnp.max(logits, axis=1, keepdims=True))
         chances = raised / jnp.sum(raised, axis=1, keepdims=True)
         prob_ref[...] = chances
@@ -768,7 +1311,7 @@
 
     @pl.when(step >= tiles)
     def _():
-        some = pl.ds(pl.multiple_of((step - tiles) * TILE, TILE), TILE)
+        some = pl.ds(pl.multiple_of((step - tiles) * 2 * TILE, TILE), 2 * TILE)
         grads = dot_turned(gate_all[...], gate_row[...]) + dot_turned(up_all[...], up_row[...])
         grads += dot_turned(logit_out[...], router_ref[some, :])
         grads = grads.astype(jnp.bfloat16)
@@ -780,7 +1323,7 @@
     pieces = len(rows)
     size, depth = rows[0].shape
     width = gate.shape[1]
-    tiles, columns = width // TILE, depth // TILE
+    tiles, columns = width // TILE, depth // (2 * TILE)
     total = pieces * size
     low = jnp.bfloat16
 
@@ -799,30 +1342,30 @@
         in_specs=[pl.BlockSpec(memory_space=pltpu.SMEM), whole(routed)]
         + [anywhere] * pieces
         + [
-            whole(router),
+            pl.BlockSpec((depth, 128), lambda i: (0, router.shape[1] // 128 - 1)),
             pl.BlockSpec((depth, TILE), lambda i: (0, early(i))),
             pl.BlockSpec((depth, TILE), lambda i: (0, early(i))),
             tile_spec,
-            pl.BlockSpec((TILE, width), lambda i: (late(i), 0)),
-            pl.BlockSpec((TILE, width), lambda i: (late(i), 0)),
+            pl.BlockSpec((2 * TILE, width), lambda i: (late(i), 0)),
+            pl.BlockSpec((2 * TILE, width), lambda i: (late(i), 0)),
         ]
         + [anywhere] * (len(kept) + len(others)),
-        out_specs=[pl.BlockSpec((size, TILE), lambda i: (0, late(i)))] * pieces
+        out_specs=[pl.BlockSpec((size, 2 * TILE), lambda i: (0, late(i)))] * pieces
         + [
             pl.BlockSpec((total, depth), lambda i: (distance, 0)),
             tile_spec,
             tile_spec,
             tile_spec,
-            pl.BlockSpec((total, router.shape[1]), lambda i: (distance, 0)),
+            pl.BlockSpec((total, 128), lambda i: (distance, 0)),
         ],
         out_shape=[jax.ShapeDtypeStruct((size, depth), low)] * pieces
         + [
             jax.ShapeDtypeStruct((RINGS * total, many), low)
-            for many in (depth, width, width, width, router.shape[1])
+            for many in (depth, width, width, width, 128)
         ],
         scratch_shapes=[pltpu.VMEM((total, width), low)] * 2
         + [
-            pltpu.VMEM((total, router.shape[1]), jnp.float32),
+            pltpu.VMEM((total, 128), jnp.float32),
             pltpu.VMEM((3, total, 1), jnp.float32),
             pltpu.VMEM((3, total, 1), jnp.float32),
             pltpu.SemaphoreType.DMA((pieces,)),
@@ -863,7 +1406,8 @@
     index = lax.axis_index("dp")
     x = lax.axis_index("tensor")
     coords = jnp.stack([index // 4, (index // 2) % 2, index % 2]).astype(jnp.int32)
-    z, y, core = coords[0], coords[1], coords[2]
+    core = coords[2]
+    place = jnp.concatenate([coords, x.astype(jnp.int32)[None], counts])
     local_rows = block_input.shape[0]
     tokens = 2 * local_rows
     depth = w_query.shape[0]
@@ -873,112 +1417,86 @@
     units = expert_gate_up.shape[3]
     shared = shared_gate_up.shape[2] // blocks
     latent_depth = w_keyval.shape[0]
-    scale = (NOPE + ROPE) ** (-0.5)
-
-    def both_halves(own, other):
-        return jnp.concatenate(
-            [jnp.where(x == 0, own, other), jnp.where(x == 0, other, own)], axis=0
-        )
-
+
+    used = query_width + KVR + ROPE
     small = jnp.concatenate(
         [
             attn_gain[:, None],
             ffn_gain[:, None],
+            jnp.pad(latent_gain, (0, depth - latent_depth))[:, None],
             w_router,
-            jnp.pad(latent_gain, (0, depth - latent_depth))[:, None],
             routes.reshape(depth, -1).astype(bf16),
+            jnp.zeros((depth, 128 - ROPE - 3 - experts - 2 * TOP), bf16),
         ],
         axis=1,
     )
-    rows_all = both_halves(block_input, other_x(block_input))
-    used = query_width + KVR + ROPE
-    first_width = -(-(used + small.shape[1]) // 128) * 128
-    first_held = ring_shards(
-        jnp.pad(
-            jnp.concatenate([w_query, w_latent, small], axis=1),
-            ((0, 0), (0, first_width - used - small.shape[1])),
-        )
-    )
-    first_chunks = gather_weight(first_held)
-    parts = depth // latent_depth
-    keyval_part = w_keyval.shape[1] // parts
-    keyval_packed = (
-        w_keyval.reshape(latent_depth, parts, keyval_part).transpose(1, 0, 2).reshape(depth, -1)
-    )
-    second_held = ring_shards(
-        after(jnp.concatenate([keyval_packed, w_output.T], axis=1), first_held[3])
-    )
-    second_chunks = gather_weight(second_held)
-    grad_planes = gather_rows(after(cotangent, second_held[3]), "xxxx")
+    first_width = query_width + KVR + 128
+    shards = pack_weights(w_query, w_latent, small, w_keyval, w_output)
+    held = ring_shards(shards)
+    other_input = other_x(block_input)
+    expert_in_other = other_core(expert_gate_up)
+    expert_out_other = other_core(expert_down)
+
     shared_in = lax.all_to_all(
         after(
             shared_gate_up.reshape(2, depth, blocks, shared)
             .transpose(2, 0, 1, 3)
             .reshape(blocks, 2 * depth, shared),
-            first_held[1],
+            held[1],
         ),
         "dp",
         split_axis=0,
         concat_axis=0,
         tiled=True,
-    ).reshape(blocks, 2, depth, shared)
+    )
     shared_out = lax.all_to_all(
-        after(shared_down.reshape(blocks, shared, depth), first_held[1]),
+        after(shared_down.reshape(blocks, shared, depth), held[1]),
         "dp",
         split_axis=0,
         concat_axis=0,
         tiled=True,
     )
-    shared_other = other_core(shared_in)
-    shared_out_other = other_core(shared_out)
-    expert_in_other = other_core(expert_gate_up[0])
-    expert_out_other = other_core(expert_down[0])
-    hole = -(-units // TILE) * TILE - units
-
-    def side_columns(k):
-        return jnp.concatenate(
-            [
-                expert_gate_up[0, k],
-                jnp.zeros((D, hole), bf16),
-                expert_in_other[k],
-                jnp.zeros((D, hole), bf16),
-                shared_in[:, k].reshape(D, shared),
-                shared_other[:, k].reshape(D, shared),
-                jnp.zeros((D, TILE - 2 * shared), bf16),
-            ],
-            axis=1,
-        )
-
-    gate_weight = side_columns(0)
-    up_weight = side_columns(1)
-    down_weight = jnp.concatenate(
-        [
-            expert_down[0],
-            jnp.zeros((hole, D), bf16),
-            expert_out_other,
-            jnp.zeros((hole, D), bf16),
-            shared_out.transpose(1, 0, 2).reshape(shared, D),
-            shared_out_other.transpose(1, 0, 2).reshape(shared, D),
-            jnp.zeros((TILE - 2 * shared, D), bf16),
-        ],
-        axis=0,
-    )
-    (first_weight,) = place_chunks(
-        coords,
-        first_chunks,
-        [(pl.ds(0, depth), pl.ds(0, first_width), 0, depth, pl.ds(0, first_width))],
-        [(D, first_width)],
-        (gate_weight, up_weight, down_weight),
-    )
-    small = first_weight[:, used:]
-    attn_gain_wide = small[:, 0].astype(f32)
-    ffn_gain_wide = small[:, 1].astype(f32)
-    router_weight = small[:, 2 : 2 + experts]
-    latent_gain_wide = (
-        small[:, 2 + experts].reshape(blocks, depth)[:, :latent_depth].reshape(-1).astype(f32)
-    )
-    routes_all = small[:, 3 + experts : 3 + experts + 2 * TOP].reshape(blocks * tokens, TOP)
-    chip_experts = jnp.stack([index, index + 1 - 2 * core])
+    gate_weight, up_weight = pack_sides(
+        expert_gate_up, expert_in_other, shared_in, other_core(shared_in), (held[2],)
+    )
+    down_weight = pack_down(
+        expert_down, expert_out_other, shared_out, other_core(shared_out), (held[2],)
+    )
+    chunks = gather_weight(held, (gate_weight, up_weight, down_weight))
+    grad_planes = gather_rows(after(cotangent, held[3]), "xyxy")
+
+    cosine, sine = rotary_tables(segments[0], ROPE)
+    cosine = jnp.tile(cosine, (1, heads))
+    sine = jnp.tile(sine, (1, heads))
+    sizes = (depth, query_width, used, latent_depth, w_keyval.shape[1] * latent_depth // depth, first_width)
+    (
+        own_part,
+        sent_part,
+        first_weight,
+        keyval_weight,
+        output_turned,
+        first_normed,
+        nope,
+        turned_query,
+        latent,
+        key,
+        keyval,
+        total,
+        attended,
+        gains,
+        latent_gain_row,
+    ) = attend_forward(
+        place, segments, cosine, sine, block_input, other_input, chunks, heads, sizes
+    )
+    attn_gain_wide, ffn_gain_wide = gains[0], gains[1]
+    mixed = block_input.astype(f32) + own_part + other_x(sent_part).astype(f32)
+    second_scale = rms_scale(mixed)
+    second_unit = mixed * second_scale
+    second_normed = (second_unit * ffn_gain_wide).astype(bf16)
+
+    routes_at = used + 3 + experts
+    routes_all = first_weight[:, routes_at : routes_at + 2 * TOP].reshape(blocks * tokens, TOP)
+    chip_experts = jnp.stack([index, index + 1 - 2 * core]).astype(jnp.int32)
     routed_all = jnp.any(
         routes_all[None] == chip_experts[:, None, None].astype(bf16), axis=2
     ).astype(f32)
@@ -996,69 +1514,15 @@
         ],
         axis=2,
     )
-    keyval_weight, output_turned = place_chunks(
-        coords,
-        second_chunks,
-        [
-            (
-                pl.ds(k * latent_depth, latent_depth),
-                pl.ds(0, keyval_part),
-                0,
-                latent_depth,
-                pl.ds(k * keyval_part, keyval_part),
-            )
-            for k in range(parts)
-        ]
-        + [
-            (
-                pl.ds(0, depth),
-                pl.ds(keyval_part, w_output.shape[0]),
-                1,
-                depth,
-                pl.ds(0, w_output.shape[0]),
-            )
-        ],
-        [(KVR, w_keyval.shape[1]), (D, w_output.shape[0])],
-    )
-
-    router_wide = jnp.pad(router_weight, ((0, 0), (0, 128 - experts)))
-
-    cosine, sine = rotary_tables(segments[0], ROPE)
-    allowed = allowed_pairs(segments[0], counts[0])
-    inputs = rows_all.astype(f32)
-    first_scale = rms_scale(inputs)
-    first_unit = inputs * first_scale
-    first_normed = (first_unit * attn_gain_wide).astype(bf16)
-    projected = wide_dot(first_normed, first_weight)
-    query = projected[:, :query_width].reshape(tokens, heads, NOPE + ROPE)
-    query_rows = jnp.concatenate(
-        [query[..., :NOPE], rotate(query[..., NOPE:], cosine[:, None, :], sine[:, None, :])],
-        axis=-1,
-    ).astype(bf16)
-    latent = projected[:, query_width : query_width + KVR]
-    key_rope = rotate(projected[:, query_width + KVR : used], cosine, sine).astype(bf16)
-    latent_scale = rms_scale(latent)
-    latent_unit = latent * latent_scale
-    latent_normed = (latent_unit * latent_gain_wide).astype(bf16)
-    keyval = wide_dot(latent_normed, keyval_weight).astype(bf16).reshape(tokens, heads, NOPE + VD)
-    key_nope = keyval[..., :NOPE]
-    values = keyval[..., NOPE:]
-    attended, log_total = attend_forward(query_rows, key_nope, key_rope, values, allowed, scale)
-    attended = attended.reshape(tokens, heads * VD)
-    attn_part = dot_turned(attended, output_turned)
-    low_rows, high_rows = attn_part[:local_rows], attn_part[local_rows:]
-    own_part = jnp.where(x == 0, low_rows, high_rows)
-    sent_part = jnp.where(x == 0, high_rows, low_rows).astype(bf16)
-    mixed = block_input.astype(f32) + own_part + other_x(sent_part).astype(f32)
-    second_scale = rms_scale(mixed)
-    second_unit = mixed * second_scale
-    second_normed = (second_unit * ffn_gain_wide).astype(bf16)
 
     down_grad, every_grad = down_grads(
         [piece for plane in grad_planes for piece in plane], down_weight
     )
-    row_planes = gather_rows(second_normed, "yxyx")
-    expert_ids = jnp.concatenate([chip_experts, jnp.array([experts], jnp.int32)])
+    corners = "yxyx"
+    row_planes = gather_rows(second_normed, corners)
+    expert_ids = jnp.concatenate(
+        [chip_experts, jnp.array([experts, used + 3 - query_width - KVR], jnp.int32)]
+    )
     kept = []
     turned, closed = [], []
     for distance in range(RINGS):
@@ -1071,17 +1535,20 @@
             routed[distance],
             row_planes[distance],
             down_grad,
-            router_wide,
+            first_weight,
             gate_weight,
             up_weight,
             kept,
             others,
         )
-        turned.append(turn_corner(grads, "yxyx"[distance]))
-        closed.append(close_plane(turned[distance]))
-    grad_second = ring_rows(closed)
+        turned.append(turn_corner(grads, corners[distance]))
+        if distance < RINGS - 1:
+            closed.append(close_plane(turned[distance]))
     every_row, every_hidden, every_gate_grad, every_up_grad, logit_grads = kept
     out_pieces = out_rows(4 * RINGS, every_hidden, down_weight)
+    own, beside, across = turned[3]
+    closed.append(close_plane((own, after(beside, out_pieces[0]), after(across, out_pieces[0]))))
+    grad_second = ring_rows(closed)
     out_closed = []
     for distance in range(RINGS):
         plane = list(out_pieces[4 * distance : 4 * distance + 4])
@@ -1090,36 +1557,34 @@
         out_closed.append(close_plane(turn_corner(plane, "x")))
     block_output = mixed + ring_rows(out_closed)
 
-    far = units + hole
-
-    def both_in(grads):
-        sent = other_core(dot_rows(every_row, grads[:, far : far + units]).astype(bf16))
-        return dot_rows(every_row, grads[:, :units]) + sent.astype(f32)
-
-    grad_expert_gate_up = jnp.stack([both_in(every_gate_grad), both_in(every_up_grad)])[None]
-    sent_down = other_core(dot_rows(every_hidden[:, far : far + units], every_grad).astype(bf16))
-    grad_expert_down = (
-        dot_rows(every_hidden[:, :units], every_grad) + sent_down.astype(f32)
-    )[None]
+    wide = -(-units // TILE) * TILE
+    arrived_in = other_core(
+        expert_grads(every_row, every_gate_grad, every_up_grad, units, 1, None, bf16)
+    )
+    arrived_down = other_core(
+        dot_rows(every_hidden[:, wide : wide + units], every_grad).astype(bf16)
+    )
     side_grads = dot_rows(
         every_row,
         jnp.concatenate(
-            [every_gate_grad[:, 2 * far :], every_up_grad[:, 2 * far :], logit_grads], axis=1
+            [every_gate_grad[:, 2 * wide :], every_up_grad[:, 2 * wide :], logit_grads], axis=1
         ),
     )
-    grad_router = side_grads[:, 2 * TILE : 2 * TILE + experts]
+    router_at = 2 * TILE + used + 3 - query_width - KVR
+    grad_router = side_grads[:, router_at : router_at + experts]
+    gap = -(-shared // 32) * 32
     shared_in_grads = jnp.stack(
         [
             side_grads[:, k * TILE : k * TILE + shared]
             + other_core(
-                side_grads[:, k * TILE + shared : k * TILE + 2 * shared].astype(bf16)
+                side_grads[:, k * TILE + gap : k * TILE + gap + shared].astype(bf16)
             ).astype(f32)
             for k in (0, 1)
         ]
     )
-    side_down = dot_rows(every_hidden[:, 2 * far :], every_grad)
+    side_down = dot_rows(every_hidden[:, 2 * wide :], every_grad)
     shared_down_grads = side_down[:shared] + other_core(
-        side_down[shared : 2 * shared].astype(bf16)
+        side_down[gap : gap + shared].astype(bf16)
     ).astype(f32)
     grad_shared_in = (
         lax.all_to_all(
@@ -1154,77 +1619,60 @@
         grad_second * ffn_gain_wide, second_unit, second_scale
     )
     grad_mixed_low = grad_mixed.astype(bf16)
-    grad_attn = both_halves(grad_mixed_low, other_x(grad_mixed_low))
-
-    keys = weight_keys()
-    places = [place_of(coords, key) for key in keys]
-
-    def in_key_order(values):
-        return jnp.concatenate(
-            [lax.dynamic_slice_in_dim(values, place * depth, depth, 1) for place in places], axis=1
-        )
-
-    grad_output_weight = scatter_blocks(
-        dot_rows(in_key_order(grad_attn), attended).astype(bf16), bf16
-    ).T
-    grad_attended = (
-        wide_dot(grad_attn, output_turned).astype(bf16).reshape(tokens, heads, VD)
-    )
-    scores = attention_scores(query_rows, key_nope, key_rope, allowed, scale)
-    weights = jnp.exp(scores - log_total)
-    weights_low = weights.astype(bf16)
-    grad_weights = jnp.einsum("ihd,jhd->hij", grad_attended, values, preferred_element_type=f32)
-    grad_values = jnp.einsum("hij,ihd->jhd", weights_low, grad_attended, preferred_element_type=f32)
-    grad_scores = (
-        weights * (grad_weights - jnp.sum(weights * grad_weights, axis=-1, keepdims=True))
-    ).astype(bf16)
-    grad_query_nope = scale * jnp.einsum(
-        "hij,jhd->ihd", grad_scores, key_nope, preferred_element_type=f32
-    )
-    grad_query_rope = scale * jnp.einsum(
-        "hij,jd->ihd", grad_scores, key_rope, preferred_element_type=f32
-    )
-    grad_key_nope = scale * jnp.einsum(
-        "hij,ihd->jhd", grad_scores, query_rows[..., :NOPE], preferred_element_type=f32
-    )
-    grad_key_rope = scale * jnp.einsum(
-        "hij,ihd->jd", grad_scores, query_rows[..., NOPE:], preferred_element_type=f32
-    )
-    grad_query = (
-        jnp.concatenate(
-            [grad_query_nope, rotate_back(grad_query_rope, cosine[:, None, :], sine[:, None, :])],
-            axis=-1,
-        )
-        .astype(bf16)
-        .reshape(tokens, heads * (NOPE + ROPE))
-    )
-    grad_keyval = (
-        jnp.concatenate([grad_key_nope, grad_values], axis=-1)
-        .astype(bf16)
-        .reshape(tokens, heads * (NOPE + VD))
-    )
-    key_order = jnp.stack(places)
-    latent_column = jnp.arange(KVR, dtype=jnp.int32)
-    wanted = key_order[latent_column // latent_depth] * latent_depth + latent_column % latent_depth
-    shuffle = (latent_column[:, None] == wanted[None, :]).astype(bf16)
-    latent_in_order = wide_dot(latent_normed, shuffle).astype(bf16)
-    grad_keyval_weight = scatter_blocks(dot_rows(latent_in_order, grad_keyval).astype(bf16), bf16)
-    grad_latent_normed = dot_turned(grad_keyval, keyval_weight)
-    gain_latent_part = jnp.sum(grad_latent_normed * latent_unit, axis=0)
-    grad_latent = rms_back(grad_latent_normed * latent_gain_wide, latent_unit, latent_scale)
-    grad_latent_all = jnp.concatenate(
-        [grad_latent, rotate_back(grad_key_rope, cosine, sine)], axis=-1
-    ).astype(bf16)
-    grad_projected = jnp.concatenate([grad_query, grad_latent_all], axis=1)
-    grad_first_weight = scatter_blocks(
-        dot_rows(in_key_order(first_normed), grad_projected).astype(bf16), bf16
-    )
-    grad_latent_part = grad_first_weight[:, query_width:]
+    other_grad = other_x(grad_mixed_low)
+
+    places = jnp.stack([place_of(coords, key_of) for key_of in weight_keys()]).astype(jnp.int32)
+    projected_grad, keyval_grad, latent_normed, gain_latent_part = attend_back(
+        place,
+        segments,
+        cosine,
+        sine,
+        grad_mixed_low,
+        other_grad,
+        (keyval_weight, output_turned, nope, turned_query, latent, key, keyval, total, latent_gain_row),
+        heads,
+        first_width,
+    )
+    grad_attn = jnp.concatenate(
+        [
+            jnp.where(x == 0, grad_mixed_low, other_grad),
+            jnp.where(x == 0, other_grad, grad_mixed_low),
+        ],
+        axis=0,
+    )
+    grad_output_weight = scatter_product(grad_attn, attended, places).T
+    grad_keyval_weight = scatter_blocks(latent_blocks(latent_normed, keyval_grad, places), bf16)
+
+    sent = block_grads(first_normed, projected_grad, places, 2 * RINGS, 2 * RINGS)
+    arrived = other_core(sent)
+    far = block_grads(first_normed, projected_grad, places, RINGS, RINGS, arrived)
+    from_y = other_y(far)
+    grad_expert_gate_up = expert_grads(
+        every_row, every_gate_grad, every_up_grad, units, 0, arrived_in, f32, (arrived,)
+    )
+    grad_expert_down = (
+        dot_rows(every_hidden[:, :units], every_grad) + arrived_down.astype(f32)
+    )[None]
+    near = block_grads(
+        first_normed, projected_grad, places, 0, RINGS, arrived, (grad_expert_gate_up,)
+    )
+    grad_first_weight = close_ring(near, from_y)
+    nope_width = heads * NOPE
+    span = heads * (ROPE // 2)
+    grad_query_weight = jnp.concatenate(
+        [
+            grad_first_weight[:, :nope_width].reshape(depth, heads, NOPE),
+            grad_first_weight[:, nope_width : nope_width + span].reshape(depth, heads, -1),
+            grad_first_weight[:, nope_width + span : query_width].reshape(depth, heads, -1),
+        ],
+        axis=2,
+    ).reshape(depth, query_width)
+    grad_latent_part = grad_first_weight[:, query_width:used]
     grad_latent_weight = grad_latent_part + other_x(grad_latent_part)
-    grad_first_part = dot_turned(grad_projected, first_weight[:, :used])
+    grad_first_part = dot_turned(projected_grad, first_weight)
     low_rows, high_rows = grad_first_part[:local_rows], grad_first_part[local_rows:]
-    sent_part = jnp.where(x == 0, high_rows, low_rows).astype(bf16)
-    grad_first = jnp.where(x == 0, low_rows, high_rows) + other_x(sent_part).astype(f32)
+    sent_rows = jnp.where(x == 0, high_rows, low_rows).astype(bf16)
+    grad_first = jnp.where(x == 0, low_rows, high_rows) + other_x(sent_rows).astype(f32)
     own_inputs = block_input.astype(f32)
     own_scale = rms_scale(own_inputs)
     own_unit = own_inputs * own_scale
@@ -1243,13 +1691,13 @@
         ],
         axis=1,
     )
-    small_grads = scatter_blocks(pick_blocks(small_grads, key_order), f32)[0]
+    small_grads = scatter_blocks(pick_blocks(small_grads, places), f32)[0]
     small_grads = small_grads + other_x(small_grads)
     return (
         block_output,
         grad_input,
         small_grads[0],
-        grad_first_weight[:, :query_width],
+        grad_query_weight,
         grad_latent_weight,
         small_grads[2 + experts, :latent_depth],
         grad_keyval_weight,

time: 1020 us -> 989 us (0.970)
  Pallas kernels: 172 us -> 289 us
  matrix products: 123 us -> 40.2 us
  local copies, waits for them, and re-layouts: 182 us -> 141 us
  starting transfers between devices: 145 us -> 110 us
  waiting for transfers between devices: 296 us -> 331 us
  other arithmetic: 85.5 us -> 64.3 us
    pallas_call x2 -> x14, Pallas kernels: 9.88 us -> 127 us  [the longest x2 40.9 us: expert_grads(): pl.pallas_call(functools.partial(expert_grads_kernel, units, len(extra)),...]
    dot_general x11 -> x4, matrix products: 92.9 us -> 34.3 us  [dot_rows(): lax.dot_general(left, right, (((0,), (0,)), ((), ())), preferred_element_...]
    ppermute x30 -> x27, waiting for transfers between devices: 97.4 us -> 140 us  [ring_step(): lax.ppermute(values, 'dp', [(i, (i + RINGS) % 16) for i in range(16)])]
    ppermute x32 -> x30, waiting for transfers between devices: 129 us -> 91.4 us  [other_y(): return lax.ppermute(values, 'dp', [(i, i ^ 2) for i in range(16)])]
    slice x22 -> x15, local copies, waits for them, and re-layouts: 36.8 us -> 8.99 us  [the longest x1 2.02 us: gather_body(): side_grads[:, k * TILE + gap:k * TILE + gap + shared].astype(bf16)]
    concatenate x5 -> x2, local copies, waits for them, and re-layouts: 26.9 us -> 0.83 us  [the longest x1 0.75 us: gather_body(): jnp.concatenate([attn_gain[:, None], ffn_gain[:, None], jnp.pad(latent_ga...]
    dot_general x12 -> x0, matrix products: 20 us -> none  [the longest x3 12.2 us: wide_dot(): return jnp.dot(left, right, preferred_element_type=jnp.float32)]
    ppermute x0 -> x3, local copies, waits for them, and re-layouts: none -> 19.2 us  [other_core(): return lax.ppermute(values, 'dp', [(i, i ^ 1) for i in range(16)])]
  transfers between devices with their start and end apart: 130 -> 114, of which waited for: 40 -> 40; matrix products, arithmetic and copies ran while one was open for 34% -> 20% of each run, Pallas kernels for 17% -> 27%
where the time goes in v4:
time: 989 us; the launch traced here: 980 us
  waiting for transfers between devices  331 us (33%)
  Pallas kernels  289 us (29%)
  local copies, waits for them, and re-layouts  141 us (14%)
  starting transfers between devices  110 us (11%)
  other arithmetic  64.3 us (7%)
  matrix products  40.2 us (4%)
    ppermute x27, waiting for transfers between devices, ring_step(): lax.ppermute(values, 'dp', [(i, (i + RINGS) % 16) for i in range(16)])  140 us
    pallas_call x4, Pallas kernels, mlp_plane(): pl.pallas_call(functools.partial(mlp_kernel, tiles, pieces, len(kept) + l...  116 us
    ppermute x30, waiting for transfers between devices, other_y(): return lax.ppermute(values, 'dp', [(i, i ^ 2) for i in range(16)])  91.4 us
    unnamed x238, local copies, waits for them, and re-layouts  82.7 us
    ppermute x32, waiting for transfers between devices, other_x(): return lax.ppermute(values, 'tensor', [(0, 1), (1, 0)])  74.7 us
    pallas_call x2, Pallas kernels, expert_grads(): pl.pallas_call(functools.partial(expert_grads_kernel, units, len(extra)),...  40.9 us
    pallas_call x6, Pallas kernels, block_grads(): pl.pallas_call(lambda places_ref, left_ref, right_ref, *refs: block_grads...  35.5 us
    ppermute x32, starting transfers between devices, other_x(): return lax.ppermute(values, 'tensor', [(0, 1), (1, 0)])  35.1 us
  transfers between devices with their start and end apart: 114, of which 40 were waited for; matrix products, arithmetic and copies ran while one was open for 20% of the time, Pallas kernels for 27%

profile of v4, /device:TPU:0, one launch (start us, length us, event | category | flops | bytes accessed | tf_op | source)
XLA Modules:
  0.0 979.9 jit_solution(17617923818444372124)
XLA Ops:
  17.7 21.0 %collective-permute-done.4.refs_1_.refs_4_ = bf16[128,3712]{1,0:T(8,128)(2,1)} collective-permute-done((bf16[128,3712]{1,0:T(8,128)(2,1)}, bf16[128,3712]{1,0:T(8,128)(2,1)}, u32[]{:S(2)}, u32[]{:S(2)}) %collective-permute-start.4) | collective-permute-done | bytes 950304 | tf_op jit(solution)/shard_map/ppermute | solution.py:426
  51.8 18.9 %all-to-all-done.1.near_ref = bf16[16,88,128]{2,1,0:T(8,128)(2,1)S(1)} async-done(((bf16[16,88,128]{2,1,0:T(8,128)(2,1)}), bf16[16,88,128]{2,1,0:T(8,128)(2,1)S(1)}, u32[]{:S(2)}, u32[]{:S(2)}) %all-to-all-start.1) | async-done | bytes 360480 | tf_op jit(solution)/shard_map/all_to_all | solution.py:1452
  78.9 33.2 %collective-permute-done.12.refs_12_.refs_1_ = bf16[128,3712]{1,0:T(8,128)(2,1)} collective-permute-done((bf16[128,3712]{1,0:T(8,128)(2,1)S(1)}, bf16[128,3712]{1,0:T(8,128)(2,1)}, u32[]{:S(2)}, u32[]{:S(2)}) %collective-permute-start.12) | collective-permute-done | bytes 950304 | tf_op jit(solution)/shard_map/ppermute | solution.py:426
  115.3 14.1 %collective-permute-done.30.refs_4_ = bf16[128,2048]{1,0:T(8,128)(2,1)} collective-permute-done((bf16[128,2048]{1,0:T(8,128)(2,1)}, bf16[128,2048]{1,0:T(8,128)(2,1)}, u32[]{:S(2)}, u32[]{:S(2)}) %collective-permute-start.30) | collective-permute-done | bytes 524320 | tf_op jit(solution)/shard_map/ppermute | solution.py:426
  132.9 12.2 %collective-permute-done.34.refs_8_ = bf16[128,2048]{1,0:T(8,128)(2,1)} collective-permute-done((bf16[128,2048]{1,0:T(8,128)(2,1)}, bf16[128,2048]{1,0:T(8,128)(2,1)}, u32[]{:S(2)}, u32[]{:S(2)}) %collective-permute-start.34) | collective-permute-done | bytes 524320 | tf_op jit(solution)/shard_map/ppermute | solution.py:426
  163.1 8.5 copy.157.own_ref
  186.7 8.5 copy.158.other_ref
  221.6 10.2 %collective-permute-done.36.refs_10_ = bf16[128,2048]{1,0:T(8,128)(2,1)S(1)} collective-permute-done((bf16[128,2048]{1,0:T(8,128)(2,1)}, bf16[128,2048]{1,0:T(8,128)(2,1)S(1)}, u32[]{:S(2)}, u32[]{:S(2)}) %collective-permute-start.36) | collective-permute-done | bytes 524320 | tf_op jit(solution)/shard_map/ppermute | solution.py:438
  239.1 9.1 collective-permute-done.39.refs_13_
  257.6 24.4 %shard_map.289 = (bf16[2048,1792]{1,0:T(8,128)(2,1)}, bf16[2048,2048]{1,0:T(8,128)(2,1)}) custom-call(bf16[128,2048]{1,0:T(8,128)(2,1)S(1)} %copy-done.13, bf16[128,2048]{1,0:T(8,128)(2,1)} %collective-permute-done.27.refs_1_, bf16[128,2048]{1,0:T(8,128)(2,1)S(1)} %copy-done.54, bf16[128,2048]{1,0:T(8,128)(2,1)} %collective-permute-done.29.refs_3_, ...), custom_call_target="tpu_custom_call" | custom-call | flops 15032385536 | bytes 31457280 | tf_op jit(solution)/shard_map/pallas_call | solution.py:1198
  284.8 22.0 %shard_map.287 = (f32[128,2048]{1,0:T(8,128)}, bf16[128,2048]{1,0:T(8,128)(2,1)S(1)}, bf16[2048,2176]{1,0:T(8,128)(2,1)}, bf16[512,2048]{1,0:T(8,128)(2,1)}, bf1...) custom-call(s32[5]{0:T(128)S(1)} %concatenate.29.place_ref, ...), custom_call_target="tpu_custom_call" | custom-call | flops 4429185024 | bytes 30408704 | tf_op jit(solution)/shard_map/pallas_call | solution.py:783
  329.4 13.3 %collective-permute-done.21.refs_0_ = bf16[128,2048]{1,0:T(8,128)(2,1)S(1)} collective-permute-done((bf16[128,2048]{1,0:T(8,128)(2,1)S(1)}, bf16[128,2048]{1,0:T(8,128)(2,1)S(1)}, u32[]{:S(2)}, u32[]{:S(2)}) %collective-permute-start.21) | collective-permute-done | bytes 524320 | tf_op jit(solution)/shard_map/ppermute | solution.py:426
  346.2 11.5 %collective-permute-done.45.refs_1_ = bf16[128,2048]{1,0:T(8,128)(2,1)} collective-permute-done((bf16[128,2048]{1,0:T(8,128)(2,1)S(1)}, bf16[128,2048]{1,0:T(8,128)(2,1)}, u32[]{:S(2)}, u32[]{:S(2)}) %collective-permute-start.45) | collective-permute-done | bytes 524320 | tf_op jit(solution)/shard_map/ppermute | solution.py:430
  366.9 29.7 %shard_map.290 = (bf16[128,2048]{1,0:T(8,128)(2,1)S(1)}, bf16[128,2048]{1,0:T(8,128)(2,1)S(1)}, bf16[128,2048]{1,0:T(8,128)(2,1)S(1)}, bf16[128,2048]{1,0:T(8,12...) custom-call(s32[4]{0:T(128)S(1)} %pad_add_fusion.experts_ref, ...), custom_call_target="tpu_custom_call" | custom-call | flops 15032385536 | bytes 42991616 | tf_op jit(solution)/shard_map/pallas_call | solution.py:1339
  401.1 29.9 %shard_map.291 = (bf16[128,2048]{1,0:T(8,128)(2,1)S(1)}, bf16[128,2048]{1,0:T(8,128)(2,1)S(1)}, bf16[128,2048]{1,0:T(8,128)(2,1)S(1)}, bf16[128,2048]{1,0:T(8,12...) custom-call(s32[4]{0:T(128)S(1)} %pad_add_fusion.experts_ref, ...), custom_call_target="tpu_custom_call", output_to_operand_aliasing={{4}: (12, {}), {5}: (13, {}), {6}: (14, {}), {7}: (15, {}),... | custom-call | flops 15032385536 | bytes 42991616 | tf_op jit(solution)/shard_map/pallas_call | solution.py:1339
  434.8 28.3 %shard_map.292 = (bf16[128,2048]{1,0:T(8,128)(2,1)S(1)}, bf16[128,2048]{1,0:T(8,128)(2,1)}, bf16[128,2048]{1,0:T(8,128)(2,1)S(1)}, bf16[128,2048]{1,0:T(8,128)(2...) custom-call(s32[4]{0:T(128)S(1)} %pad_add_fusion.experts_ref, ...), custom_call_target="tpu_custom_call", output_to_operand_aliasing={{4}: (12, {}), {5}: (13, {}), {6}: (14, {}), {7}: (15, {}),... | custom-call | flops 15032385536 | bytes 42991616 | tf_op jit(solution)/shard_map/pallas_call | solution.py:1339
  468.5 9.5 collective-permute-done.59
  479.4 9.8 collective-permute-done.61
  490.8 9.6 collective-permute-done.53.refs_17_
  502.4 28.5 %shard_map.293 = (bf16[128,2048]{1,0:T(8,128)(2,1)S(1)}, bf16[128,2048]{1,0:T(8,128)(2,1)S(1)}, bf16[128,2048]{1,0:T(8,128)(2,1)S(1)}, bf16[128,2048]{1,0:T(8,12...) custom-call(s32[4]{0:T(128)S(1)} %pad_add_fusion.experts_ref, ...), custom_call_target="tpu_custom_call", output_to_operand_aliasing={{4}: (12, {}), {5}: (13, {}), {6}: (14, {}), {7}: (15, {}),... | custom-call | flops 15032385536 | bytes 42991616 | tf_op jit(solution)/shard_map/pallas_call | solution.py:1339
  533.3 21.8 %shard_map.294 = (bf16[128,2048]{1,0:T(8,128)(2,1)S(1)}, bf16[128,2048]{1,0:T(8,128)(2,1)S(1)}, bf16[128,2048]{1,0:T(8,128)(2,1)S(1)}, bf16[128,2048]{1,0:T(8,12...) custom-call(bf16[2048,1792]{1,0:T(8,128)(2,1)} %get-tuple-element.11, ...), custom_call_target="tpu_custom_call" | custom-call | flops 15032385536 | bytes 23068672 | tf_op jit(solution)/shard_map/pallas_call | solution.py:1236
  564.7 10.9 %convolution_convert_fusion = bf16[704,2048]{1,0:T(8,128)(2,1)} fusion(bf16[2048,2048]{1,0:T(8,128)(2,1)} %get-tuple-element.163, bf16[2048,1792]{1,0:T(8,128)(2,1)} %get-tuple-element.117.refs_0_), kind=kOutput, calls=%fused_computation.2 | convolution fusion | flops 5907021824 | bytes 14417920 | tf_op jit(solution)/shard_map/dot_general | solution.py:565
  613.6 19.4 %shard_map.307 = bf16[1,2,2048,704]{3,2,1,0:T(8,128)(2,1)} custom-call(bf16[2048,2048]{1,0:T(8,128)(2,1)} %get-tuple-element.154.rows_ref, bf16[2048,1792]{1,0:T(8,128)(2,1)} %get-tuple-element.155.gate_ref, bf16[2048,1792]{1,0:T(8,128)(2,1)} %get-tuple-element.156.up_ref), custom_call_target="tpu_custom_call" | custom-call | flops 12884901888 | bytes 34603008 | tf_op jit(solution)/shard_map/pallas_call | solution.py:1163
  684.9 13.3 %shard_map.305 = (bf16[256,2176]{1,0:T(8,128)(2,1)}, bf16[256,2048]{1,0:T(8,128)(2,1)S(1)}, bf16[256,512]{1,0:T(8,128)(2,1)S(1)}, f32[1,512]{1,0:T(1,128)S(1)}) custom-call(s32[5]{0:T(128)S(1)} %copy-done.47, s32[1,256]{1,0:T(1,128)S(1)} %copy-done.45, s32[256,1]{1,0:T(8,128)S(1)} %copy-done.19, f32[256,256]{1,0:T(8,128)S(1)} %copy.162.cosine_ref, ...), custom_call_target="tpu_custom_call" | custom-call | flops 3145728000 | bytes 6291456 | tf_op jit(solution)/shard_map/pallas_call | solution.py:913
  728.0 16.0 %collective-permute-done.82 = bf16[128,2048]{1,0:T(8,128)(2,1)} collective-permute-done((bf16[128,2048]{1,0:T(8,128)(2,1)}, bf16[128,2048]{1,0:T(8,128)(2,1)}, u32[]{:S(2)}, u32[]{:S(2)}) %collective-permute-start.82) | collective-permute-done | bytes 524320 | tf_op jit(solution)/shard_map/ppermute | solution.py:438
  807.2 11.6 %add_bitcast_fusion = f32[1,704,2048]{2,1,0:T(8,128)} fusion(bf16[704,2048]{1,0:T(8,128)(2,1)} %collective-permute-done.109, bf16[2048,2048]{1,0:T(8,128)(2,1)} %get-tuple-element.163, bf16[2048,1792]{1,0:T(8,128)(2,1)} %get-tuple-element.117.refs_0_), kind=kOutput, calls=%fused_computation | convolution fusion | flops 5908463616 | bytes 20185088 | tf_op jit(solution)/shard_map/dot_general | solution.py:565
  851.1 8.8 collective-permute-done.102
  864.6 8.5 copy.177.refs_0_
  873.1 21.5 %shard_map.308.refs_1_ = f32[1,2,2048,704]{3,2,1,0:T(8,128)} custom-call(bf16[2048,2048]{1,0:T(8,128)(2,1)} %get-tuple-element.154.rows_ref, bf16[2048,1792]{1,0:T(8,128)(2,1)} %get-tuple-element.155.gate_ref, bf16[2048,1792]{1,0:T(8,128)(2,1)} %get-tuple-element.156.up_ref, bf16[1,2,2048,704]{3,2,1,0:T(8,128)(2,1)} %copy.177.refs_0_, ...), custom_call_target="tpu_custom_call" | custom-call | flops 12884901888 | bytes 34603008 | tf_op jit(solution)/shard_map/pallas_call | solution.py:1163
  918.4 10.6 %collective-permute-done.92 = bf16[128,2176]{1,0:T(8,128)(2,1)S(1)} collective-permute-done((bf16[128,2176]{1,0:T(8,128)(2,1)S(1)}, bf16[128,2176]{1,0:T(8,128)(2,1)S(1)}, u32[]{:S(2)}, u32[]{:S(2)}) %collective-permute-start.92) | collective-permute-done | bytes 557088 | tf_op jit(solution)/shard_map/ppermute | solution.py:426
  940.1 11.8 %collective-permute-done.93 = bf16[128,2176]{1,0:T(8,128)(2,1)S(1)} collective-permute-done((bf16[128,2176]{1,0:T(8,128)(2,1)S(1)}, bf16[128,2176]{1,0:T(8,128)(2,1)S(1)}, u32[]{:S(2)}, u32[]{:S(2)}) %collective-permute-start.93) | collective-permute-done | bytes 557088 | tf_op jit(solution)/shard_map/ppermute | solution.py:426
  957.8 12.2 %copy.190 = f32[1,2,2048,704]{2,3,1,0:T(8,128)} copy(f32[1,2,2048,704]{3,2,1,0:T(8,128)} %shard_map.308.refs_1_) | data formatting | bytes 23068672
  (606 shorter events, 458.2 us)
Async XLA Ops:
  2.5 159.1 %collective-permute-start.14 = (bf16[1,2,2048,704]{2,3,1,0:T(8,128)(2,1)}, bf16[1,2,2048,704]{2,3,1,0:T(8,128)(2,1)}, u32[]{:S(2)}, u32[]{:S(2)}) collective-permute-start(bf16[1,2,2048,704]{2,3,1,0:T(8,128)(2,1)} %param.32), channel_id=1, source_target_pairs={{0,2},{2,0},{4,6},{6,4},{8,10},{10,8},{12,14},{14,12},{16,18},{18,... | collective-permute-start | bytes 17301512 | tf_op jit(solution)/shard_map/ppermute | solution.py:434
  38.8 92.1 %collective-permute-start.16 = (bf16[1,704,2048]{2,1,0:T(8,128)(2,1)}, bf16[1,704,2048]{2,1,0:T(8,128)(2,1)}, u32[]{:S(2)}, u32[]{:S(2)}) collective-permute-start(bf16[1,704,2048]{2,1,0:T(8,128)(2,1)} %own_ref.3), channel_id=1, source_target_pairs={{0,2},{2,0},{4,6},{6,4},{8,10},{10,8},{12,14},{14,12},{16,18},{18,... | collective-permute-start | bytes 8650760 | tf_op jit(solution)/shard_map/ppermute | solution.py:434
  70.7 44.3 %all-to-all-start = ((bf16[16,256,88]{1,2,0:T(8,128)(2,1)}), bf16[16,256,88]{1,2,0:T(8,128)(2,1)}, u32[]{:S(2)}, u32[]{:S(2)}) async-start(bf16[16,256,88]{1,2,0:T(8,128)(2,1)} %copy.156), calls=%async_computation | async-start | bytes 1441792 | tf_op jit(solution)/shard_map/all_to_all | solution.py:1440
  78.3 51.0 %collective-permute-start.10 = (bf16[128,3712]{1,0:T(8,128)(2,1)S(1)}, bf16[128,3712]{1,0:T(8,128)(2,1)}, u32[]{:S(2)}, u32[]{:S(2)}) collective-permute-start(bf16[128,3712]{1,0:T(8,128)(2,1)S(1)} %collective-permute-done.8.refs_0_.refs_8_), channel_id=1, source_target_pairs={{0,4},{2,6},{4,0},{6,2},{8,12},{10,14},{12,8},{14,10},{16,20},{18,... | collective-permute-start | bytes 2850824 | tf_op jit(solution)/shard_map/ppermute | solution.py:430
  145.3 67.3 %collective-permute-start.29 = (bf16[128,2048]{1,0:T(8,128)(2,1)}, bf16[128,2048]{1,0:T(8,128)(2,1)}, u32[]{:S(2)}, u32[]{:S(2)}) collective-permute-start(bf16[128,2048]{1,0:T(8,128)(2,1)} %collective-permute-done.27.refs_1_), channel_id=1, source_target_pairs={{0,1},{1,0},{2,3},{3,2},{4,5},{5,4},{6,7},{7,6},{8,9},{9,8},{10,11... | collective-permute-start | bytes 1572872 | tf_op jit(solution)/shard_map/ppermute | solution.py:438
  147.9 68.8 %collective-permute-start.31 = (bf16[128,2048]{1,0:T(8,128)(2,1)}, bf16[128,2048]{1,0:T(8,128)(2,1)}, u32[]{:S(2)}, u32[]{:S(2)}) collective-permute-start(bf16[128,2048]{1,0:T(8,128)(2,1)} %collective-permute-done.30.refs_4_), channel_id=1, source_target_pairs={{0,4},{2,6},{4,0},{6,2},{8,12},{10,14},{12,8},{14,10},{16,20},{18,... | collective-permute-start | bytes 1572872 | tf_op jit(solution)/shard_map/ppermute | solution.py:430
  157.3 61.4 %collective-permute-start.35 = (bf16[128,2048]{1,0:T(8,128)(2,1)}, bf16[128,2048]{1,0:T(8,128)(2,1)}, u32[]{:S(2)}, u32[]{:S(2)}) collective-permute-start(bf16[128,2048]{1,0:T(8,128)(2,1)} %collective-permute-done.34.refs_8_), channel_id=1, source_target_pairs={{0,4},{2,6},{4,0},{6,2},{8,12},{10,14},{12,8},{14,10},{16,20},{18,... | collective-permute-start | bytes 1572872 | tf_op jit(solution)/shard_map/ppermute | solution.py:430
  160.1 57.1 %collective-permute-start.33 = (bf16[128,2048]{1,0:T(8,128)(2,1)}, bf16[128,2048]{1,0:T(8,128)(2,1)}, u32[]{:S(2)}, u32[]{:S(2)}) collective-permute-start(bf16[128,2048]{1,0:T(8,128)(2,1)} %collective-permute-done.32.refs_6_), channel_id=1, source_target_pairs={{0,4},{2,6},{4,0},{6,2},{8,12},{10,14},{12,8},{14,10},{16,20},{18,... | collective-permute-start | bytes 1572872 | tf_op jit(solution)/shard_map/ppermute | solution.py:430
  161.6 58.6 %collective-permute-start.40 = (bf16[128,2048]{1,0:T(8,128)(2,1)}, bf16[128,2048]{1,0:T(8,128)(2,1)}, u32[]{:S(2)}, u32[]{:S(2)}) collective-permute-start(bf16[128,2048]{1,0:T(8,128)(2,1)} %collective-permute-done.38.refs_12_), channel_id=1, source_target_pairs={{0,1},{1,0},{2,3},{3,2},{4,5},{5,4},{6,7},{7,6},{8,9},{9,8},{10,11... | collective-permute-start | bytes 1572872 | tf_op jit(solution)/shard_map/ppermute | solution.py:438
  212.7 43.1 %collective-permute-start.18 = (bf16[128,3712]{1,0:T(8,128)(2,1)}, bf16[128,3712]{1,0:T(8,128)(2,1)}, u32[]{:S(2)}, u32[]{:S(2)}) collective-permute-start(bf16[128,3712]{1,0:T(8,128)(2,1)} %shard_map.286), channel_id=1, source_target_pairs={{0,4},{2,6},{4,0},{6,2},{8,12},{10,14},{12,8},{14,10},{16,20},{18,... | collective-permute-start | bytes 2850824 | tf_op jit(solution)/shard_map/ppermute | solution.py:430
  231.8 50.2 %collective-permute-start.9 = (bf16[128,3712]{1,0:T(8,128)(2,1)S(1)}, bf16[128,3712]{1,0:T(8,128)(2,1)S(1)}, u32[]{:S(2)}, u32[]{:S(2)}) collective-permute-start(bf16[128,3712]{1,0:T(8,128)(2,1)S(1)} %collective-permute-done.8.refs_0_.refs_8_), channel_id=1, source_target_pairs={{0,2},{2,0},{4,6},{6,4},{8,10},{10,8},{12,14},{14,12},{16,18},{18,... | collective-permute-start | bytes 2850824 | tf_op jit(solution)/shard_map/ppermute | solution.py:434
  239.0 42.9 %collective-permute-start.7 = (bf16[128,3712]{1,0:T(8,128)(2,1)}, bf16[128,3712]{1,0:T(8,128)(2,1)S(1)}, u32[]{:S(2)}, u32[]{:S(2)}) collective-permute-start(bf16[128,3712]{1,0:T(8,128)(2,1)} %collective-permute-done.6.refs_6_), channel_id=1, source_target_pairs={{0,2},{2,0},{4,6},{6,4},{8,10},{10,8},{12,14},{14,12},{16,18},{18,... | collective-permute-start | bytes 2850824 | tf_op jit(solution)/shard_map/ppermute | solution.py:434
  345.6 53.8 %collective-permute-start.46 = (bf16[128,2048]{1,0:T(8,128)(2,1)S(1)}, bf16[128,2048]{1,0:T(8,128)(2,1)S(1)}, u32[]{:S(2)}, u32[]{:S(2)}) collective-permute-start(bf16[128,2048]{1,0:T(8,128)(2,1)S(1)} %collective-permute-done.21.refs_0_), channel_id=1, source_target_pairs={{0,1},{1,0},{2,3},{3,2},{4,5},{5,4},{6,7},{7,6},{8,9},{9,8},{10,11... | collective-permute-start | bytes 1572872 | tf_op jit(solution)/shard_map/ppermute | solution.py:438
  357.7 42.4 %collective-permute-start.47 = (bf16[128,2048]{1,0:T(8,128)(2,1)}, bf16[128,2048]{1,0:T(8,128)(2,1)S(1)}, u32[]{:S(2)}, u32[]{:S(2)}) collective-permute-start(bf16[128,2048]{1,0:T(8,128)(2,1)} %collective-permute-done.45.refs_1_), channel_id=1, source_target_pairs={{0,1},{1,0},{2,3},{3,2},{4,5},{5,4},{6,7},{7,6},{8,9},{9,8},{10,11... | collective-permute-start | bytes 1572872 | tf_op jit(solution)/shard_map/ppermute | solution.py:438
  358.2 41.2 %collective-permute-start.43 = (bf16[128,2048]{1,0:T(8,128)(2,1)S(1)}, bf16[128,2048]{1,0:T(8,128)(2,1)S(1)}, u32[]{:S(2)}, u32[]{:S(2)}) collective-permute-start(bf16[128,2048]{1,0:T(8,128)(2,1)S(1)} %collective-permute-done.22.refs_0_), channel_id=1, source_target_pairs={{0,1},{1,0},{2,3},{3,2},{4,5},{5,4},{6,7},{7,6},{8,9},{9,8},{10,11... | collective-permute-start | bytes 1572872 | tf_op jit(solution)/shard_map/ppermute | solution.py:438
  489.2 99.1 %collective-permute-start.58 = (bf16[128,2048]{1,0:T(8,128)(2,1)}, bf16[128,2048]{1,0:T(8,128)(2,1)}, u32[]{:S(2)}, u32[]{:S(2)}) collective-permute-start(bf16[128,2048]{1,0:T(8,128)(2,1)} %get-tuple-element.127), channel_id=1, source_target_pairs={{0,4},{2,6},{4,0},{6,2},{8,12},{10,14},{12,8},{14,10},{16,20},{18,... | collective-permute-start | bytes 1572872 | tf_op jit(solution)/shard_map/ppermute | solution.py:430
  500.4 87.9 %collective-permute-start.63 = (bf16[128,2048]{1,0:T(8,128)(2,1)}, bf16[128,2048]{1,0:T(8,128)(2,1)}, u32[]{:S(2)}, u32[]{:S(2)}) collective-permute-start(bf16[128,2048]{1,0:T(8,128)(2,1)} %add_convert_fusion.9), channel_id=1, source_target_pairs={{0,8},{2,10},{4,12},{6,14},{8,16},{10,18},{12,20},{14,22},{16,24},... | collective-permute-start | bytes 1572872 | tf_op jit(solution)/shard_map/ppermute | solution.py:426
  500.5 87.9 %collective-permute-start.60 = (bf16[128,2048]{1,0:T(8,128)(2,1)}, bf16[128,2048]{1,0:T(8,128)(2,1)}, u32[]{:S(2)}, u32[]{:S(2)}) collective-permute-start(bf16[128,2048]{1,0:T(8,128)(2,1)} %add_convert_fusion.10), channel_id=1, source_target_pairs={{0,1},{1,0},{2,3},{3,2},{4,5},{5,4},{6,7},{7,6},{8,9},{9,8},{10,11... | collective-permute-start | bytes 1572872 | tf_op jit(solution)/shard_map/ppermute | solution.py:438
  559.9 44.3 %collective-permute-start.57 = (bf16[128,2048]{1,0:T(8,128)(2,1)}, bf16[128,2048]{1,0:T(8,128)(2,1)}, u32[]{:S(2)}, u32[]{:S(2)}) collective-permute-start(bf16[128,2048]{1,0:T(8,128)(2,1)} %shard_map.296), channel_id=1, source_target_pairs={{0,1},{1,0},{2,3},{3,2},{4,5},{5,4},{6,7},{7,6},{8,9},{9,8},{10,11... | collective-permute-start | bytes 1572872 | tf_op jit(solution)/shard_map/ppermute | solution.py:438
  597.5 46.0 %collective-permute-start.106 = (bf16[2048,88]{0,1:T(8,128)(2,1)}, bf16[2048,88]{0,1:T(8,128)(2,1)}, u32[]{:S(2)}, u32[]{:S(2)}) collective-permute-start(bf16[2048,88]{0,1:T(8,128)(2,1)} %get-tuple-element.232), channel_id=1, source_target_pairs={{0,2},{2,0},{4,6},{6,4},{8,10},{10,8},{12,14},{14,12},{16,18},{18,... | collective-permute-start | bytes 1081352 | tf_op jit(solution)/shard_map/ppermute | solution.py:434
  597.5 46.0 %collective-permute-start.107 = (bf16[2048,88]{0,1:T(8,128)(2,1)}, bf16[2048,88]{0,1:T(8,128)(2,1)}, u32[]{:S(2)}, u32[]{:S(2)}) collective-permute-start(bf16[2048,88]{0,1:T(8,128)(2,1)} %get-tuple-element.233), channel_id=1, source_target_pairs={{0,2},{2,0},{4,6},{6,4},{8,10},{10,8},{12,14},{14,12},{16,18},{18,... | collective-permute-start | bytes 1081352 | tf_op jit(solution)/shard_map/ppermute | solution.py:434
  600.0 52.0 %all-to-all-start.3 = ((bf16[16,88,128]{2,1,0:T(8,128)(2,1)}), bf16[16,88,128]{2,1,0:T(8,128)(2,1)}, u32[]{:S(2)}, u32[]{:S(2)}) async-start(bf16[16,88,128]{2,1,0:T(8,128)(2,1)} %bitcast_bitcast_fusion), calls=%async_computation.3 | async-start | bytes 720896 | tf_op jit(solution)/shard_map/all_to_all | solution.py:1606
  612.7 44.0 %collective-permute-start.65 = (bf16[128,2048]{1,0:T(8,128)(2,1)}, bf16[128,2048]{1,0:T(8,128)(2,1)}, u32[]{:S(2)}, u32[]{:S(2)}) collective-permute-start(bf16[128,2048]{1,0:T(8,128)(2,1)} %add_convert_fusion.7), channel_id=1, source_target_pairs={{0,8},{2,10},{4,12},{6,14},{8,16},{10,18},{12,20},{14,22},{16,24},... | collective-permute-start | bytes 1572872 | tf_op jit(solution)/shard_map/ppermute | solution.py:426
  643.0 220.4 %collective-permute-start.90 = (bf16[1,2,2048,704]{2,3,1,0:T(8,128)(2,1)}, bf16[1,2,2048,704]{2,3,1,0:T(8,128)(2,1)}, u32[]{:S(2)}, u32[]{:S(2)}) collective-permute-start(bf16[1,2,2048,704]{2,3,1,0:T(8,128)(2,1)} %copy.176), channel_id=1, source_target_pairs={{0,2},{2,0},{4,6},{6,4},{8,10},{10,8},{12,14},{14,12},{16,18},{18,... | collective-permute-start | bytes 17301512 | tf_op jit(solution)/shard_map/ppermute | solution.py:434
  643.0 162.7 %collective-permute-start.109 = (bf16[704,2048]{1,0:T(8,128)(2,1)}, bf16[704,2048]{1,0:T(8,128)(2,1)}, u32[]{:S(2)}, u32[]{:S(2)}) collective-permute-start(bf16[704,2048]{1,0:T(8,128)(2,1)} %convolution_convert_fusion), channel_id=1, source_target_pairs={{0,2},{2,0},{4,6},{6,4},{8,10},{10,8},{12,14},{14,12},{16,18},{18,... | collective-permute-start | bytes 8650760 | tf_op jit(solution)/shard_map/ppermute | solution.py:434
  666.0 114.5 %collective-permute-start.77 = (bf16[128,2048]{1,0:T(8,128)(2,1)}, bf16[128,2048]{1,0:T(8,128)(2,1)}, u32[]{:S(2)}, u32[]{:S(2)}) collective-permute-start(bf16[128,2048]{1,0:T(8,128)(2,1)} %shard_map.304), channel_id=1, source_target_pairs={{0,1},{1,0},{2,3},{3,2},{4,5},{5,4},{6,7},{7,6},{8,9},{9,8},{10,11... | collective-permute-start | bytes 1572872 | tf_op jit(solution)/shard_map/ppermute | solution.py:438
  780.5 49.6 %collective-permute-start.89 = (bf16[1024,2176]{1,0:T(8,128)(2,1)}, bf16[1024,2176]{1,0:T(8,128)(2,1)}, u32[]{:S(2)}, u32[]{:S(2)}) collective-permute-start(bf16[1024,2176]{1,0:T(8,128)(2,1)} %shard_map.306), channel_id=1, source_target_pairs={{0,2},{2,0},{4,6},{6,4},{8,10},{10,8},{12,14},{14,12},{16,18},{18,... | collective-permute-start | bytes 13369352 | tf_op jit(solution)/shard_map/ppermute | solution.py:434
  836.6 116.4 %collective-permute-start.68 = (bf16[128,2048]{1,0:T(8,128)(2,1)S(1)}, bf16[128,2048]{1,0:T(8,128)(2,1)}, u32[]{:S(2)}, u32[]{:S(2)}) collective-permute-start(bf16[128,2048]{1,0:T(8,128)(2,1)S(1)} %copy-done.38), channel_id=1, source_target_pairs={{0,1},{1,0},{2,3},{3,2},{4,5},{5,4},{6,7},{7,6},{8,9},{9,8},{10,11... | collective-permute-start | bytes 1572872 | tf_op jit(solution)/shard_map/ppermute | solution.py:438
  838.8 69.0 %collective-permute-start.91 = (bf16[512,2176]{1,0:T(8,128)(2,1)}, bf16[512,2176]{1,0:T(8,128)(2,1)}, u32[]{:S(2)}, u32[]{:S(2)}) collective-permute-start(bf16[512,2176]{1,0:T(8,128)(2,1)} %shard_map.310), channel_id=1, source_target_pairs={{0,4},{2,6},{4,0},{6,2},{8,12},{10,14},{12,8},{14,10},{16,20},{18,... | collective-permute-start | bytes 6684680 | tf_op jit(solution)/shard_map/ppermute | solution.py:430
  844.2 108.9 %collective-permute-start.67 = (bf16[128,2048]{1,0:T(8,128)(2,1)}, bf16[128,2048]{1,0:T(8,128)(2,1)}, u32[]{:S(2)}, u32[]{:S(2)}) collective-permute-start(bf16[128,2048]{1,0:T(8,128)(2,1)} %add_convert_fusion.6), channel_id=1, source_target_pairs={{0,4},{2,6},{4,0},{6,2},{8,12},{10,14},{12,8},{14,10},{16,20},{18,... | collective-permute-start | bytes 1572872 | tf_op jit(solution)/shard_map/ppermute | solution.py:430
  860.9 92.2 %collective-permute-start.80 = (bf16[128,2048]{1,0:T(8,128)(2,1)}, bf16[128,2048]{1,0:T(8,128)(2,1)}, u32[]{:S(2)}, u32[]{:S(2)}) collective-permute-start(bf16[128,2048]{1,0:T(8,128)(2,1)} %add_convert_fusion), channel_id=1, source_target_pairs={{0,8},{2,10},{4,12},{6,14},{8,16},{10,18},{12,20},{14,22},{16,24},... | collective-permute-start | bytes 1572872 | tf_op jit(solution)/shard_map/ppermute | solution.py:426
  863.4 47.7 %collective-permute-start.99 = (bf16[32,2048]{1,0:T(8,128)(2,1)S(1)}, bf16[32,2048]{1,0:T(8,128)(2,1)}, u32[]{:S(2)}, u32[]{:S(2)}) collective-permute-start(bf16[32,2048]{1,0:T(8,128)(2,1)S(1)} %fusion.32), channel_id=1, source_target_pairs={{0,8},{2,10},{4,12},{6,14},{8,16},{10,18},{12,20},{14,22},{16,24},... | collective-permute-start | bytes 393224 | tf_op jit(solution)/shard_map/ppermute | solution.py:426
  (191 other events, 3797.4 us)

commit v5 on v4

--- a/solution.py
+++ b/solution.py
@@ -507,10 +507,10 @@
     return held
 
 
-def gather_weight(held, others):
+def gather_weight(held):
     chunks = []
     for distance, current in enumerate(held):
-        beside = other_y(after(current, *others) if distance == RINGS - 1 else current)
+        beside = other_y(current)
         for flip_y, chunk in ((0, current), (1, beside)):
             for flip_core, piece in ((0, chunk), (1, other_core(chunk))):
                 chunks.append(((distance, flip_y, flip_core), piece))
@@ -608,6 +608,7 @@
 
 def attend_kernel(
     keys,
+    extra,
     heads,
     sizes,
     place_ref,
@@ -638,7 +639,7 @@
         gains_ref,
         latent_gain_ref,
         semaphores,
-    ) = refs[len(keys) :]
+    ) = refs[len(keys) + extra :]
     f32, bf16 = jnp.float32, jnp.bfloat16
     local_rows = own_ref.shape[0]
     tokens = 2 * local_rows
@@ -756,7 +757,7 @@
         )
 
 
-def attend_forward(place, segments, cosine, sine, own, other, chunks, heads, sizes):
+def attend_forward(place, segments, cosine, sine, own, other, chunks, heads, sizes, others):
     depth, query_width, used, latent_depth, keyval_part, first_width = sizes
     f32, bf16 = jnp.float32, jnp.bfloat16
     keys = [key for key, _ in chunks]
@@ -781,9 +782,11 @@
         ((1, KVR), f32),
     ]
     return pl.pallas_call(
-        functools.partial(attend_kernel, keys, heads, sizes),
+        functools.partial(attend_kernel, keys, len(others), heads, sizes),
         out_shape=[jax.ShapeDtypeStruct(*shape) for shape in shapes],
-        in_specs=[pl.BlockSpec(memory_space=pltpu.SMEM)] + in_vmem(6) + in_place(len(chunks)),
+        in_specs=[pl.BlockSpec(memory_space=pltpu.SMEM)]
+        + in_vmem(6)
+        + in_place(len(chunks) + len(others)),
         out_specs=in_vmem(len(shapes)),
         scratch_shapes=[
             pltpu.SemaphoreType.DMA((len(chunks) * (2 + depth // latent_depth),))
@@ -794,7 +797,17 @@
             bytes_accessed=4 * D * (first_width + 1536),
             transcendentals=2 * heads * tokens * tokens,
         ),
-    )(place, segments, segments.T, cosine, sine, own, other, *[piece for _, piece in chunks])
+    )(
+        place,
+        segments,
+        segments.T,
+        cosine,
+        sine,
+        own,
+        other,
+        *[piece for _, piece in chunks],
+        *others,
+    )
 
 
 def attend_back_kernel(
@@ -985,8 +998,8 @@
     return ring_sum([total[r * size : (r + 1) * size] for r in range(RINGS)], jnp.bfloat16)
 
 
-def scatter_product(left, right, places):
-    sent = block_grads(left, right, places, 2 * RINGS, 2 * RINGS)
+def scatter_product(left, right, places, others):
+    sent = block_grads(left, right, places, 2 * RINGS, 2 * RINGS, None, others)
     arrived = other_core(sent)
     far = block_grads(left, right, places, RINGS, RINGS, arrived)
     from_y = other_y(far)
@@ -1009,16 +1022,18 @@
         )
 
 
-def latent_blocks(left, right, places):
+def latent_blocks(left, right, places, others):
     shape = (left.shape[1], right.shape[1])
     return pl.pallas_call(
-        latent_blocks_kernel,
+        lambda places_ref, left_ref, right_ref, *refs: latent_blocks_kernel(
+            places_ref, left_ref, right_ref, *refs[len(others) :]
+        ),
         out_shape=jax.ShapeDtypeStruct(shape, jnp.bfloat16),
-        in_specs=[pl.BlockSpec(memory_space=pltpu.SMEM)] + in_vmem(2),
+        in_specs=[pl.BlockSpec(memory_space=pltpu.SMEM)] + in_vmem(2) + in_place(len(others)),
         out_specs=pl.BlockSpec(memory_space=pltpu.VMEM),
         scratch_shapes=[pltpu.VMEM(shape, jnp.float32)],
         compiler_params=pltpu.CompilerParams(vmem_limit_bytes=32 * 1024 * 1024),
-    )(places, left, right)
+    )(places, left, right, *others)
 
 
 def pack_kernel(heads, query_ref, latent_ref, small_ref, keyval_ref, output_ref, out_ref):
@@ -1074,123 +1089,199 @@
         copy.wait()
 
 
-def pack_sides_kernel(units, shared, own_ref, other_ref, near_ref, far_ref, *refs):
-    gate_out, up_out = refs[-2:]
+def shared_stride(shared):
+    return -(-shared // 32) * 32
+
+
+def pack_shared_kernel(blocks, shared, in_ref, down_ref, out_ref):
+    stride = shared_stride(shared)
+    out_ref[...] = jnp.zeros_like(out_ref)
+    for k in range(3):
+        if k < 2:
+            units = jnp.transpose(in_ref[k].astype(jnp.float32)).astype(jnp.bfloat16)
+        else:
+            units = down_ref[...]
+        for b in range(blocks):
+            out_ref[b, k * stride : k * stride + shared] = units[b * shared : (b + 1) * shared]
+
+
+def pack_shared(shared_in, shared_down, blocks, others):
+    depth = shared_in.shape[1]
+    shared = shared_down.shape[0] // blocks
+    return pl.pallas_call(
+        lambda in_ref, down_ref, *refs: pack_shared_kernel(
+            blocks, shared, in_ref, down_ref, refs[-1]
+        ),
+        out_shape=jax.ShapeDtypeStruct((blocks, 3 * shared_stride(shared), depth), jnp.bfloat16),
+        in_specs=in_vmem(2) + in_place(len(others)),
+        out_specs=pl.BlockSpec(memory_space=pltpu.VMEM),
+    )(shared_in, shared_down, *others)
+
+
+def unpack_shared_kernel(shared, packed_ref, in_ref, down_ref, units_ref):
+    stride = shared_stride(shared)
+    blocks = packed_ref.shape[0]
+    for k in range(3):
+        target = down_ref if k == 2 else units_ref
+        for b in range(blocks):
+            target[b * shared : (b + 1) * shared, :] = packed_ref[
+                b, k * stride : k * stride + shared
+            ].astype(jnp.float32)
+        if k < 2:
+            in_ref[k] = jnp.transpose(units_ref[...])
+
+
+def unpack_shared(packed, shared):
+    blocks, _, depth = packed.shape
+    return pl.pallas_call(
+        functools.partial(unpack_shared_kernel, shared),
+        out_shape=[
+            jax.ShapeDtypeStruct((2, depth, blocks * shared), jnp.float32),
+            jax.ShapeDtypeStruct((blocks * shared, depth), jnp.float32),
+        ],
+        in_specs=in_vmem(1),
+        out_specs=in_vmem(2),
+        scratch_shapes=[pltpu.VMEM((blocks * shared, depth), jnp.float32)],
+    )(packed)
+
+
+def pack_units_kernel(units, shared, own_in, other_in, own_down, other_down, near, far, *refs):
+    outs = refs[-3:]
     hole = -(-units // TILE) * TILE
-    rows = gate_out.shape[0]
-    gap = -(-shared // 32) * 32
-    for k, out in ((0, gate_out), (1, up_out)):
-        part = slice(k * rows, (k + 1) * rows)
-        out[:, :units] = own_ref[0, k]
-        out[:, units:hole] = jnp.zeros((rows, hole - units), jnp.bfloat16)
-        out[:, hole : hole + units] = other_ref[0, k]
-        out[:, hole + units : 2 * hole] = jnp.zeros((rows, hole - units), jnp.bfloat16)
-        out[:, 2 * hole :] = jnp.zeros((rows, TILE), jnp.bfloat16)
-        out[:, 2 * hole : 2 * hole + shared] = near_ref[0, part]
-        out[:, 2 * hole + gap : 2 * hole + gap + shared] = far_ref[0, part]
-
-
-def pack_sides(own, other, near, far, others):
-    depth, units = own.shape[2:]
-    blocks, rows, shared = near.shape
-    rows //= 2
-    width = 2 * (-(-units // TILE) * TILE) + TILE
-    wide = pl.BlockSpec((1, 2, rows, units), lambda i: (0, 0, i, 0))
-    narrow = pl.BlockSpec((1, 2 * rows, shared), lambda i: (i, 0, 0))
-    out = pl.BlockSpec((rows, width), lambda i: (i, 0))
+    stride = shared_stride(shared)
+    columns = outs[0].shape[1]
+    size = near.shape[2]
+    for k, out in enumerate(outs):
+        first = own_in[0, k] if k < 2 else own_down[0]
+        second = other_in[0, k] if k < 2 else other_down[0]
+        out[:units] = first
+        out[units:hole] = jnp.zeros((hole - units, columns), jnp.bfloat16)
+        out[hole : hole + units] = second
+        out[hole + units : 2 * hole] = jnp.zeros((hole - units, columns), jnp.bfloat16)
+        out[2 * hole :] = jnp.zeros((TILE, columns), jnp.bfloat16)
+        for b in range(columns // size):
+            part = slice(b * size, (b + 1) * size)
+            for at, ref in ((2 * hole, near), (2 * hole + stride, far)):
+                out[at : at + shared, part] = ref[b, k * stride : k * stride + shared]
+
+
+def pack_units(own_in, other_in, own_down, other_down, near, far, shared, others):
+    units, depth = own_down.shape[1:]
+    size = near.shape[2]
+    height = 2 * (-(-units // TILE) * TILE) + TILE
+    columns = 2 * size
+    in_spec = pl.BlockSpec((1, 2, units, columns), lambda i: (0, 0, 0, i))
+    down_spec = pl.BlockSpec((1, units, columns), lambda i: (0, 0, i))
+    narrow = pl.BlockSpec((2,) + near.shape[1:], lambda i: (i, 0, 0))
     return pl.pallas_call(
-        functools.partial(pack_sides_kernel, units, shared),
-        grid=(blocks,),
-        in_specs=[wide, wide, narrow, narrow] + in_place(len(others)),
-        out_specs=[out, out],
-        out_shape=[jax.ShapeDtypeStruct((depth, width), jnp.bfloat16)] * 2,
+        functools.partial(pack_units_kernel, units, shared),
+        grid=(depth // columns,),
+        in_specs=[in_spec, in_spec, down_spec, down_spec, narrow, narrow]
+        + in_place(len(others)),
+        out_specs=[pl.BlockSpec((height, columns), lambda i: (0, i))] * 3,
+        out_shape=[jax.ShapeDtypeStruct((height, depth), jnp.bfloat16)] * 3,
         compiler_params=pltpu.CompilerParams(vmem_limit_bytes=32 * 1024 * 1024),
-    )(own, other, near, far, *others)
-
-
-def pack_down_kernel(units, shared, own_ref, other_ref, near_ref, far_ref, *refs):
+        cost_estimate=pl.CostEstimate(
+            flops=0, bytes_accessed=12 * height * depth, transcendentals=0
+        ),
+    )(own_in, other_in, own_down, other_down, near, far, *others)
+
+
+def expert_grads_kernel(units, count, extra, right_ref, *refs):
     out = refs[-1]
-    hole = -(-units // TILE) * TILE
-    columns = out.shape[1]
-    gap = -(-shared // 32) * 32
-    out[:units] = own_ref[0]
-    out[units:hole] = jnp.zeros((hole - units, columns), jnp.bfloat16)
-    out[hole : hole + units] = other_ref[0]
-    out[hole + units : 2 * hole] = jnp.zeros((hole - units, columns), jnp.bfloat16)
-    out[2 * hole :] = jnp.zeros((TILE, columns), jnp.bfloat16)
-    size = near_ref.shape[2]
-    for k in range(columns // size):
-        part = slice(k * size, (k + 1) * size)
-        out[2 * hole : 2 * hole + shared, part] = near_ref[k]
-        out[2 * hole + gap : 2 * hole + gap + shared, part] = far_ref[k]
-
-
-def pack_down(own, other, near, far, others):
-    units, depth = own.shape[1:]
-    blocks, shared, size = near.shape
-    height = 2 * (-(-units // TILE) * TILE) + TILE
-    columns = 4 * size
-    wide = pl.BlockSpec((1, units, columns), lambda i: (0, 0, i))
-    narrow = pl.BlockSpec((4, shared, size), lambda i: (i, 0, 0))
-    return pl.pallas_call(
-        functools.partial(pack_down_kernel, units, shared),
-        grid=(depth // columns,),
-        in_specs=[wide, wide, narrow, narrow] + in_place(len(others)),
-        out_specs=pl.BlockSpec((height, columns), lambda i: (0, i)),
-        out_shape=jax.ShapeDtypeStruct((height, depth), jnp.bfloat16),
-        compiler_params=pltpu.CompilerParams(vmem_limit_bytes=32 * 1024 * 1024),
-    )(own, other, near, far, *others)
-
-
-def expert_grads_kernel(units, extra, rows_ref, gate_ref, up_ref, *refs):
-    out = refs[-1]
-    for k, grads in ((0, gate_ref), (1, up_ref)):
+    for k in range(count):
 
         @pl.when(pl.program_id(0) == k)
         def _():
-            result = dot_rows(rows_ref[...], grads[...])[:, :units]
+            result = dot_rows(refs[k][...], right_ref[...])[:units]
             if extra:
-                result += refs[0][0, 0].astype(jnp.float32)
+                result += refs[count][0, 0].astype(jnp.float32)
             out[0, 0] = result.astype(out.dtype)
 
 
-def expert_grads(rows, gate, up, units, column, arrived, kind, others=()):
-    total, depth = rows.shape
+def expert_grads(lefts, right, units, column, arrived, kind, others=()):
+    total, depth = right.shape
     wide = -(-units // TILE) * TILE
     extra = [] if arrived is None else [arrived]
-    out = pl.BlockSpec((1, 1, 2 * TILE, units), lambda k, i: (0, k, i, 0))
+    out = pl.BlockSpec((1, 1, units, 2 * TILE), lambda k, i: (0, k, 0, i))
     side = pl.BlockSpec((total, wide), lambda k, i: (0, column))
     return pl.pallas_call(
-        functools.partial(expert_grads_kernel, units, len(extra)),
-        grid=(2, depth // (2 * TILE)),
-        in_specs=[pl.BlockSpec((total, 2 * TILE), lambda k, i: (0, i)), side, side]
+        functools.partial(expert_grads_kernel, units, len(lefts), len(extra)),
+        grid=(len(lefts), depth // (2 * TILE)),
+        in_specs=[pl.BlockSpec((total, 2 * TILE), lambda k, i: (0, i))]
+        + [side] * len(lefts)
         + [out] * len(extra)
         + in_place(len(others)),
         out_specs=out,
-        out_shape=jax.ShapeDtypeStruct((1, 2, depth, units), kind),
+        out_shape=jax.ShapeDtypeStruct((1, len(lefts), units, depth), kind),
         compiler_params=pltpu.CompilerParams(vmem_limit_bytes=48 * 1024 * 1024),
         cost_estimate=pl.CostEstimate(
-            flops=4 * total * depth * wide,
-            bytes_accessed=4 * total * (depth + wide) + 8 * depth * units,
+            flops=2 * len(lefts) * total * depth * wide,
+            bytes_accessed=2 * len(lefts) * total * (depth + wide) + 8 * depth * units,
             transcendentals=0,
         ),
-    )(rows, gate, up, *extra, *others)
+    )(right, *lefts, *extra, *others)
+
+
+def side_grads_kernel(shared, rows_ref, cots_ref, gate_ref, up_ref, hidden_ref, logit_ref, *outs):
+    kept_ref, sent_ref, router_ref = outs
+    stride = shared_stride(shared)
+    size = kept_ref.shape[2]
+    for k, (left, right) in enumerate(
+        ((gate_ref, rows_ref), (up_ref, rows_ref), (hidden_ref, cots_ref))
+    ):
+        result = dot_rows(left[...], right[...])
+        for b in range(kept_ref.shape[0]):
+            part = slice(b * size, (b + 1) * size)
+            kept_ref[b, k * stride : (k + 1) * stride] = result[:stride, part]
+            sent_ref[b, k * stride : (k + 1) * stride] = result[
+                stride : 2 * stride, part
+            ].astype(jnp.bfloat16)
+    router_ref[...] = dot_rows(logit_ref[...], rows_ref[...])
+
+
+def side_grads(rows, cots, gate, up, hidden, logits, shared, blocks):
+    total, depth = rows.shape
+    column = gate.shape[1] // TILE - 1
+    size = depth // blocks
+    stride = shared_stride(shared)
+    wide = pl.BlockSpec((total, 2 * TILE), lambda i: (0, i))
+    side = pl.BlockSpec((total, TILE), lambda i: (0, column))
+    packed = pl.BlockSpec((2 * TILE // size, 3 * stride, size), lambda i: (i, 0, 0))
+    return pl.pallas_call(
+        functools.partial(side_grads_kernel, shared),
+        grid=(depth // (2 * TILE),),
+        in_specs=[wide, wide, side, side, side, whole(logits)],
+        out_specs=[packed, packed, pl.BlockSpec((logits.shape[1], 2 * TILE), lambda i: (0, i))],
+        out_shape=[
+            jax.ShapeDtypeStruct((blocks, 3 * stride, size), jnp.float32),
+            jax.ShapeDtypeStruct((blocks, 3 * stride, size), jnp.bfloat16),
+            jax.ShapeDtypeStruct((logits.shape[1], depth), jnp.float32),
+        ],
+        compiler_params=pltpu.CompilerParams(vmem_limit_bytes=48 * 1024 * 1024),
+        cost_estimate=pl.CostEstimate(
+            flops=8 * total * depth * TILE,
+            bytes_accessed=4 * total * depth,
+            transcendentals=0,
+        ),
+    )(rows, cots, gate, up, hidden, logits)
 
 
 def down_kernel(count, *refs):
-    pieces, (weight_ref, grads_ref, rows_ref, semaphores) = refs[:count], refs[count:]
+    pieces, weight_ref = refs[:count], refs[count]
+    grads_ref, rows_ref, semaphores = refs[-3:]
 
     @pl.when(pl.program_id(0) == 0)
     def _():
         load_pieces(pieces, rows_ref, semaphores)
 
-    size = rows_ref.shape[0] // 4
-    for k in range(4):
+    size = rows_ref.shape[0] // 2
+    for k in range(2):
         part = slice(k * size, (k + 1) * size)
         grads_ref[part, :] = dot_turned(rows_ref[part, :], weight_ref[...]).astype(jnp.bfloat16)
 
 
-def down_grads(pieces, down):
+def down_grads(part, pieces, down, kept, others):
     count = len(pieces)
     size, depth = pieces[0].shape
     width = down.shape[0]
@@ -1198,24 +1289,26 @@
     return pl.pallas_call(
         functools.partial(down_kernel, count),
         grid=(width // TILE,),
-        in_specs=[pl.BlockSpec(memory_space=pl.ANY)] * count
-        + [pl.BlockSpec((TILE, depth), lambda i: (i, 0))],
+        in_specs=in_place(count)
+        + [pl.BlockSpec((TILE, depth), lambda i: (i, 0))]
+        + in_place(len(kept) + len(others)),
         out_specs=[
-            pl.BlockSpec((rows, TILE), lambda i: (0, i)),
-            pl.BlockSpec((rows, depth), lambda i: (0, 0)),
+            pl.BlockSpec((rows, TILE), lambda i: (part, i)),
+            pl.BlockSpec((rows, depth), lambda i: (part, 0)),
         ],
         out_shape=[
-            jax.ShapeDtypeStruct((rows, width), jnp.bfloat16),
-            jax.ShapeDtypeStruct((rows, depth), jnp.bfloat16),
+            jax.ShapeDtypeStruct((2 * rows, width), jnp.bfloat16),
+            jax.ShapeDtypeStruct((2 * rows, depth), jnp.bfloat16),
         ],
         scratch_shapes=[pltpu.SemaphoreType.DMA((count,))],
+        input_output_aliases={count + 1 + k: k for k in range(len(kept))},
         compiler_params=pltpu.CompilerParams(vmem_limit_bytes=48 * 1024 * 1024),
         cost_estimate=pl.CostEstimate(
             flops=2 * rows * depth * width,
             bytes_accessed=2 * (2 * rows * depth + depth * width + rows * width),
             transcendentals=0,
         ),
-    )(*pieces, down)
+    )(*pieces, down, *kept, *others)
 
 
 def out_kernel(count, *refs):
@@ -1282,8 +1375,8 @@
         half = total // 2
         for k in (0, 1):
             part = slice(k * half, (k + 1) * half)
-            pre_gate = wide_dot(rows_out[part, :], gate_col[...])
-            pre_up = wide_dot(rows_out[part, :], up_col[...])
+            pre_gate = dot_turned(rows_out[part, :], gate_col[...])
+            pre_up = dot_turned(rows_out[part, :], up_col[...])
             grads = down_grad[part, :].astype(jnp.float32)
             scale = scale_ref[kind, part, :]
             sigmoid = 1.0 / (1.0 + jnp.exp(-pre_gate))
@@ -1312,7 +1405,7 @@
     @pl.when(step >= tiles)
     def _():
         some = pl.ds(pl.multiple_of((step - tiles) * 2 * TILE, TILE), 2 * TILE)
-        grads = dot_turned(gate_all[...], gate_row[...]) + dot_turned(up_all[...], up_row[...])
+        grads = wide_dot(gate_all[...], gate_row[...]) + wide_dot(up_all[...], up_row[...])
         grads += dot_turned(logit_out[...], router_ref[some, :])
         grads = grads.astype(jnp.bfloat16)
         for k in range(pieces):
@@ -1322,7 +1415,7 @@
 def mlp_plane(distance, experts, routed, rows, down_grad, router, gate, up, kept, others):
     pieces = len(rows)
     size, depth = rows[0].shape
-    width = gate.shape[1]
+    width = gate.shape[0]
     tiles, columns = width // TILE, depth // (2 * TILE)
     total = pieces * size
     low = jnp.bfloat16
@@ -1343,11 +1436,11 @@
         + [anywhere] * pieces
         + [
             pl.BlockSpec((depth, 128), lambda i: (0, router.shape[1] // 128 - 1)),
-            pl.BlockSpec((depth, TILE), lambda i: (0, early(i))),
-            pl.BlockSpec((depth, TILE), lambda i: (0, early(i))),
+            pl.BlockSpec((TILE, depth), lambda i: (early(i), 0)),
+            pl.BlockSpec((TILE, depth), lambda i: (early(i), 0)),
             tile_spec,
-            pl.BlockSpec((2 * TILE, width), lambda i: (late(i), 0)),
-            pl.BlockSpec((2 * TILE, width), lambda i: (late(i), 0)),
+            pl.BlockSpec((width, 2 * TILE), lambda i: (0, late(i))),
+            pl.BlockSpec((width, 2 * TILE), lambda i: (0, late(i))),
         ]
         + [anywhere] * (len(kept) + len(others)),
         out_specs=[pl.BlockSpec((size, 2 * TILE), lambda i: (0, late(i)))] * pieces
@@ -1434,36 +1527,20 @@
     shards = pack_weights(w_query, w_latent, small, w_keyval, w_output)
     held = ring_shards(shards)
     other_input = other_x(block_input)
-    expert_in_other = other_core(expert_gate_up)
-    expert_out_other = other_core(expert_down)
-
-    shared_in = lax.all_to_all(
-        after(
-            shared_gate_up.reshape(2, depth, blocks, shared)
-            .transpose(2, 0, 1, 3)
-            .reshape(blocks, 2 * depth, shared),
-            held[1],
-        ),
+    expert_in = expert_gate_up.swapaxes(2, 3)
+    expert_in_other = other_core(expert_in)
+    expert_down_other = other_core(expert_down)
+    chunks = gather_weight(held)
+    grad_planes = gather_rows(after(cotangent, held[3]), "xyxy")
+
+    shared_near = lax.all_to_all(
+        pack_shared(shared_gate_up, shared_down, blocks, (held[3],)),
         "dp",
         split_axis=0,
         concat_axis=0,
         tiled=True,
     )
-    shared_out = lax.all_to_all(
-        after(shared_down.reshape(blocks, shared, depth), held[1]),
-        "dp",
-        split_axis=0,
-        concat_axis=0,
-        tiled=True,
-    )
-    gate_weight, up_weight = pack_sides(
-        expert_gate_up, expert_in_other, shared_in, other_core(shared_in), (held[2],)
-    )
-    down_weight = pack_down(
-        expert_down, expert_out_other, shared_out, other_core(shared_out), (held[2],)
-    )
-    chunks = gather_weight(held, (gate_weight, up_weight, down_weight))
-    grad_planes = gather_rows(after(cotangent, held[3]), "xyxy")
+    shared_far = other_core(shared_near)
 
     cosine, sine = rotary_tables(segments[0], ROPE)
     cosine = jnp.tile(cosine, (1, heads))
@@ -1486,7 +1563,16 @@
         gains,
         latent_gain_row,
     ) = attend_forward(
-        place, segments, cosine, sine, block_input, other_input, chunks, heads, sizes
+        place,
+        segments,
+        cosine,
+        sine,
+        block_input,
+        other_input,
+        chunks,
+        heads,
+        sizes,
+        (grad_planes[1][0], grad_planes[0][2]),
     )
     attn_gain_wide, ffn_gain_wide = gains[0], gains[1]
     mixed = block_input.astype(f32) + own_part + other_x(sent_part).astype(f32)
@@ -1515,11 +1601,28 @@
         axis=2,
     )
 
-    down_grad, every_grad = down_grads(
-        [piece for plane in grad_planes for piece in plane], down_weight
-    )
     corners = "yxyx"
     row_planes = gather_rows(second_normed, corners)
+    gate_weight, up_weight, down_weight = pack_units(
+        expert_in,
+        expert_in_other,
+        expert_down,
+        expert_down_other,
+        shared_near,
+        shared_far,
+        shared,
+        (second_normed,),
+    )
+    half_kept = down_grads(
+        0, [piece for plane in grad_planes[:2] for piece in plane], down_weight, (), ()
+    )
+    down_grad, every_grad = down_grads(
+        1,
+        [piece for plane in grad_planes[2:] for piece in plane],
+        down_weight,
+        half_kept,
+        (row_planes[1][0],),
+    )
     expert_ids = jnp.concatenate(
         [chip_experts, jnp.array([experts, used + 3 - query_width - KVR], jnp.int32)]
     )
@@ -1557,61 +1660,31 @@
         out_closed.append(close_plane(turn_corner(plane, "x")))
     block_output = mixed + ring_rows(out_closed)
 
-    wide = -(-units // TILE) * TILE
     arrived_in = other_core(
-        expert_grads(every_row, every_gate_grad, every_up_grad, units, 1, None, bf16)
-    )
-    arrived_down = other_core(
-        dot_rows(every_hidden[:, wide : wide + units], every_grad).astype(bf16)
-    )
-    side_grads = dot_rows(
+        expert_grads((every_gate_grad, every_up_grad), every_row, units, 1, None, bf16)
+    )
+    arrived_down = other_core(expert_grads((every_hidden,), every_grad, units, 1, None, bf16))
+    shared_kept, shared_sent, logit_rows = side_grads(
         every_row,
-        jnp.concatenate(
-            [every_gate_grad[:, 2 * wide :], every_up_grad[:, 2 * wide :], logit_grads], axis=1
-        ),
-    )
-    router_at = 2 * TILE + used + 3 - query_width - KVR
-    grad_router = side_grads[:, router_at : router_at + experts]
-    gap = -(-shared // 32) * 32
-    shared_in_grads = jnp.stack(
-        [
-            side_grads[:, k * TILE : k * TILE + shared]
-            + other_core(
-                side_grads[:, k * TILE + gap : k * TILE + gap + shared].astype(bf16)
-            ).astype(f32)
-            for k in (0, 1)
-        ]
-    )
-    side_down = dot_rows(every_hidden[:, 2 * wide :], every_grad)
-    shared_down_grads = side_down[:shared] + other_core(
-        side_down[gap : gap + shared].astype(bf16)
-    ).astype(f32)
-    grad_shared_in = (
+        every_grad,
+        every_gate_grad,
+        every_up_grad,
+        every_hidden,
+        logit_grads,
+        shared,
+        blocks,
+    )
+    router_at = used + 3 - query_width - KVR
+    grad_router = logit_rows[router_at : router_at + experts].reshape(experts, blocks, depth)
+    grad_shared_in, grad_shared_down = unpack_shared(
         lax.all_to_all(
-            shared_in_grads.astype(bf16)
-            .reshape(2, blocks, depth, shared)
-            .transpose(1, 0, 2, 3)
-            .reshape(blocks, 2 * depth, shared),
+            add_low(shared_kept, other_core(shared_sent)),
             "dp",
             split_axis=0,
             concat_axis=0,
             tiled=True,
-        )
-        .astype(f32)
-        .reshape(blocks, 2, depth, shared)
-        .transpose(1, 2, 0, 3)
-        .reshape(2, depth, blocks * shared)
-    )
-    grad_shared_down = (
-        lax.all_to_all(
-            shared_down_grads.astype(bf16).reshape(shared, blocks, depth).transpose(1, 0, 2),
-            "dp",
-            split_axis=0,
-            concat_axis=0,
-            tiled=True,
-        )
-        .astype(f32)
-        .reshape(blocks * shared, depth)
+        ),
+        shared,
     )
 
     gain_ffn_part = jnp.sum(grad_second * second_unit, axis=0)
@@ -1640,23 +1713,37 @@
         ],
         axis=0,
     )
-    grad_output_weight = scatter_product(grad_attn, attended, places).T
-    grad_keyval_weight = scatter_blocks(latent_blocks(latent_normed, keyval_grad, places), bf16)
-
-    sent = block_grads(first_normed, projected_grad, places, 2 * RINGS, 2 * RINGS)
-    arrived = other_core(sent)
-    far = block_grads(first_normed, projected_grad, places, RINGS, RINGS, arrived)
-    from_y = other_y(far)
-    grad_expert_gate_up = expert_grads(
-        every_row, every_gate_grad, every_up_grad, units, 0, arrived_in, f32, (arrived,)
-    )
-    grad_expert_down = (
-        dot_rows(every_hidden[:, :units], every_grad) + arrived_down.astype(f32)
-    )[None]
-    near = block_grads(
-        first_normed, projected_grad, places, 0, RINGS, arrived, (grad_expert_gate_up,)
-    )
-    grad_first_weight = close_ring(near, from_y)
+    middle = heads * NOPE
+    edges = ((0, middle), (middle, first_width))
+    parts = [projected_grad[:, start:end] for start, end in edges]
+    arrived = [
+        other_core(block_grads(first_normed, part, places, 2 * RINGS, 2 * RINGS))
+        for part in parts
+    ]
+    far = [
+        block_grads(first_normed, part, places, RINGS, RINGS, came)
+        for part, came in zip(parts, arrived)
+    ]
+    from_y = [other_y(far[0]), other_y(far[1])]
+    grad_expert_in = expert_grads(
+        (every_gate_grad, every_up_grad), every_row, units, 0, arrived_in, f32, tuple(far)
+    )
+    near = [
+        block_grads(first_normed, part, places, 0, RINGS, came)
+        for part, came in zip(parts, arrived)
+    ]
+    first_closed = close_ring(after(near[0], grad_expert_in), from_y[0])
+    grad_expert_down = expert_grads(
+        (every_hidden,), every_grad, units, 0, arrived_down, f32, (from_y[0],)
+    )
+    second_closed = close_ring(near[1], from_y[1])
+    grad_expert_gate_up = grad_expert_in.swapaxes(2, 3)
+    grad_expert_down = grad_expert_down[0]
+    grad_output_weight = scatter_product(grad_attn, attended, places, (arrived[1],)).T
+    grad_keyval_weight = scatter_blocks(
+        latent_blocks(latent_normed, keyval_grad, places, (arrived[1],)), bf16
+    )
+    grad_first_weight = jnp.concatenate([first_closed, second_closed], axis=1)
     nope_width = heads * NOPE
     span = heads * (ROPE // 2)
     grad_query_weight = jnp.concatenate(
@@ -1683,7 +1770,7 @@
         [
             gain_attn_part.reshape(blocks, 1, depth),
             gain_ffn_part.reshape(blocks, 1, depth),
-            grad_router.reshape(blocks, experts, depth),
+            grad_router.swapaxes(0, 1),
             jnp.pad(
                 gain_latent_part.reshape(blocks, 1, latent_depth),
                 ((0, 0), (0, 0), (0, depth - latent_depth)),
@@ -1691,7 +1778,9 @@
         ],
         axis=1,
     )
-    small_grads = scatter_blocks(pick_blocks(small_grads, places), f32)[0]
+    small_grads = scatter_blocks(
+        pick_blocks(after(small_grads, far[1]), places), f32
+    )[0]
     small_grads = small_grads + other_x(small_grads)
     return (
         block_output,
@@ -1703,7 +1792,7 @@
         grad_keyval_weight,
         grad_output_weight,
         small_grads[1],
-        small_grads[2 : 2 + experts].reshape(depth, experts),
+        small_grads[2 : 2 + experts].T,
         grad_shared_in,
         grad_shared_down,
         grad_expert_gate_up,

time: 989 us -> 838 us (0.85)
  waiting for transfers between devices: 331 us -> 231 us
  local copies, waits for them, and re-layouts: 141 us -> 64.4 us
  Pallas kernels: 289 us -> 345 us
  matrix products: 40.2 us -> 5.95 us
    pallas_call x6 -> x10, Pallas kernels: 75.6 us -> 117 us  [the longest x4 62.7 us: expert_grads(): pl.pallas_call(functools.partial(expert_grads_kernel, units, len(lefts),...]
    unnamed x238 -> x229, local copies, waits for them, and re-layouts: 82.7 us -> 43.6 us
    ppermute x27 -> x30, waiting for transfers between devices: 140 us -> 101 us  [ring_step(): lax.ppermute(values, 'dp', [(i, (i + RINGS) % 16) for i in range(16)])]
    dot_general x4 -> x0, matrix products: 34.3 us -> none  [dot_rows(): lax.dot_general(left, right, (((0,), (0,)), ((), ())), preferred_element_...]
    all_to_all x4 -> x2, waiting for transfers between devices: 25.2 us -> 0.01 us  [the longest x1 0.01 us: gather_body(): lax.all_to_all(pack_shared(shared_gate_up, shared_down, blocks, (held[3],...]
    ppermute x30 -> x31, waiting for transfers between devices: 91.4 us -> 68.1 us  [other_y(): return lax.ppermute(values, 'dp', [(i, i ^ 2) for i in range(16)])]
    ppermute x3 -> x0, local copies, waits for them, and re-layouts: 19.2 us -> none  [other_core(): return lax.ppermute(values, 'dp', [(i, i ^ 1) for i in range(16)])]
    ppermute x27 -> x30, starting transfers between devices: 21.2 us -> 36.5 us  [ring_step(): lax.ppermute(values, 'dp', [(i, (i + RINGS) % 16) for i in range(16)])]
  transfers between devices with their start and end apart: 114 -> 114, of which waited for: 40 -> 35; matrix products, arithmetic and copies ran while one was open for 20% -> 11% of each run, Pallas kernels for 27% -> 41%
where the time goes in v5:
time: 838 us; the launch traced here: 830 us
  Pallas kernels  345 us (41%)
  waiting for transfers between devices  231 us (28%)
  starting transfers between devices  119 us (14%)
  local copies, waits for them, and re-layouts  64.4 us (8%)
  other arithmetic  60.7 us (7%)
    pallas_call x4, Pallas kernels, mlp_plane(): pl.pallas_call(functools.partial(mlp_kernel, tiles, pieces, len(kept) + l...  113 us
    ppermute x30, waiting for transfers between devices, ring_step(): lax.ppermute(values, 'dp', [(i, (i + RINGS) % 16) for i in range(16)])  101 us
    ppermute x31, waiting for transfers between devices, other_y(): return lax.ppermute(values, 'dp', [(i, i ^ 2) for i in range(16)])  68.1 us
    pallas_call x4, Pallas kernels, expert_grads(): pl.pallas_call(functools.partial(expert_grads_kernel, units, len(lefts),...  62.7 us
    ppermute x32, waiting for transfers between devices, other_x(): return lax.ppermute(values, 'tensor', [(0, 1), (1, 0)])  61.7 us
    pallas_call x9, Pallas kernels, block_grads(): pl.pallas_call(lambda places_ref, left_ref, right_ref, *refs: block_grads...  50 us
    unnamed x229, local copies, waits for them, and re-layouts  43.6 us
    ppermute x30, starting transfers between devices, ring_step(): lax.ppermute(values, 'dp', [(i, (i + RINGS) % 16) for i in range(16)])  36.5 us
  transfers between devices with their start and end apart: 114, of which 35 were waited for; matrix products, arithmetic and copies ran while one was open for 11% of the time, Pallas kernels for 41%

profile of v5, /device:TPU:0, one launch (start us, length us, event | category | flops | bytes accessed | tf_op | source)
XLA Modules:
  0.0 829.6 jit_solution(16771925016597069890)
XLA Ops:
  14.5 21.8 %collective-permute-done.4.refs_4_ = bf16[128,3712]{1,0:T(8,128)(2,1)S(1)} collective-permute-done((bf16[128,3712]{1,0:T(8,128)(2,1)}, bf16[128,3712]{1,0:T(8,128)(2,1)S(1)}, u32[]{:S(2)}, u32[]{:S(2)}) %collective-permute-start.4) | collective-permute-done | bytes 950304 | tf_op jit(solution)/shard_map/ppermute | solution.py:426
  39.4 10.1 %collective-permute-done.other_ref = bf16[128,2048]{1,0:T(8,128)(2,1)S(1)} collective-permute-done((bf16[128,2048]{1,0:T(8,128)(2,1)S(1)}, bf16[128,2048]{1,0:T(8,128)(2,1)S(1)}, u32[]{:S(2)}, u32[]{:S(2)}) %collective-permute-start) | collective-permute-done | bytes 524320 | tf_op jit(solution)/shard_map/ppermute | solution.py:438
  51.3 9.2 %collective-permute-done.8.refs_8_ = bf16[128,3712]{1,0:T(8,128)(2,1)} collective-permute-done((bf16[128,3712]{1,0:T(8,128)(2,1)S(1)}, bf16[128,3712]{1,0:T(8,128)(2,1)}, u32[]{:S(2)}, u32[]{:S(2)}) %collective-permute-start.8) | collective-permute-done | bytes 950304 | tf_op jit(solution)/shard_map/ppermute | solution.py:426
  62.2 21.5 %collective-permute-done.12.refs_1_.refs_12_.refs_0_ = bf16[128,3712]{1,0:T(8,128)(2,1)S(1)} collective-permute-done((bf16[128,3712]{1,0:T(8,128)(2,1)}, bf16[128,3712]{1,0:T(8,128)(2,1)S(1)}, u32[]{:S(2)}, u32[]{:S(2)}) %collective-permute-start.12) | collective-permute-done | bytes 950304 | tf_op jit(solution)/shard_map/ppermute | solution.py:426
  87.6 11.0 %collective-permute-done.16.refs_16_.refs_4_ = bf16[128,2048]{1,0:T(8,128)(2,1)} collective-permute-done((bf16[128,2048]{1,0:T(8,128)(2,1)}, bf16[128,2048]{1,0:T(8,128)(2,1)}, u32[]{:S(2)}, u32[]{:S(2)}) %collective-permute-start.16) | collective-permute-done | bytes 524320 | tf_op jit(solution)/shard_map/ppermute | solution.py:426
  120.7 22.2 %shard_map.283 = (f32[128,2048]{1,0:T(8,128)}, bf16[128,2048]{1,0:T(8,128)(2,1)S(1)}, bf16[2048,2176]{1,0:T(8,128)(2,1)}, bf16[512,2048]{1,0:T(8,128)(2,1)}, bf1...) custom-call(s32[5]{0:T(128)S(1)} %concatenate.24.place_ref, ...), custom_call_target="tpu_custom_call" | custom-call | flops 4429185024 | bytes 30408704 | tf_op jit(solution)/shard_map/pallas_call | solution.py:784
  157.1 10.9 %collective-permute-done.18 = bf16[128,2048]{1,0:T(8,128)(2,1)} collective-permute-done((bf16[128,2048]{1,0:T(8,128)(2,1)}, bf16[128,2048]{1,0:T(8,128)(2,1)}, u32[]{:S(2)}, u32[]{:S(2)}) %collective-permute-start.18) | collective-permute-done | bytes 524320 | tf_op jit(solution)/shard_map/ppermute | solution.py:438
  176.3 13.7 %collective-permute-done.37.refs_3_ = bf16[128,2048]{1,0:T(8,128)(2,1)} collective-permute-done((bf16[128,2048]{1,0:T(8,128)(2,1)}, bf16[128,2048]{1,0:T(8,128)(2,1)}, u32[]{:S(2)}, u32[]{:S(2)}) %collective-permute-start.37) | collective-permute-done | bytes 524320 | tf_op jit(solution)/shard_map/ppermute | solution.py:438
  198.0 13.0 %shard_map.285 = (bf16[1792,2048]{1,0:T(8,128)(2,1)}, bf16[1792,2048]{1,0:T(8,128)(2,1)}, bf16[1792,2048]{1,0:T(8,128)(2,1)}) custom-call(bf16[1,2,704,2048]{3,2,1,0:T(8,128)(2,1)S(1)} %bitcast.85, bf16[1,2,704,2048]{3,2,1,0:T(8,128)(2,1)} %collective-permute-done.25.other_in, bf16[1,704,2048]{2,1,0:T(8,128)(2,1)} %own_down.1, ...), custom_call_target="tpu_custom_call" | custom-call | bytes 44040192 | tf_op jit(solution)/shard_map/pallas_call | solution.py:1176
  229.0 14.2 %shard_map.286 = (bf16[2048,1792]{1,0:T(8,128)(2,1)}, bf16[2048,2048]{1,0:T(8,128)(2,1)}) custom-call(bf16[128,2048]{1,0:T(8,128)(2,1)S(1)} %copy-done.9, bf16[128,2048]{1,0:T(8,128)(2,1)} %collective-permute-done.36.refs_1_, bf16[128,2048]{1,0:T(8,128)(2,1)S(1)} %copy-done.22, bf16[128,2048]{1,0:T(8,128)(2,1)} %collective-permute-done.37.refs_3_, ...), custom_call_target="tpu_custom_call" | custom-call | flops 7516192768 | bytes 19398656 | tf_op jit(solution)/shard_map/pallas_call | solution.py:1289
  254.9 13.0 %shard_map.287 = (bf16[2048,1792]{1,0:T(8,128)(2,1)}, bf16[2048,2048]{1,0:T(8,128)(2,1)}) custom-call(bf16[128,2048]{1,0:T(8,128)(2,1)} %collective-permute-done.28.refs_0_, bf16[128,2048]{1,0:T(8,128)(2,1)S(1)} %collective-permute-done.29.refs_1_, ...), custom_call_target="tpu_custom_call", output_to_operand_aliasing={{0}: (9, {}), {1}: (10, {})} | custom-call | flops 7516192768 | bytes 19398656 | tf_op jit(solution)/shard_map/pallas_call | solution.py:1289
  274.5 7.8 collective-permute-done.49.refs_3_
  282.3 28.3 %shard_map.288 = (bf16[128,2048]{1,0:T(8,128)(2,1)S(1)}, bf16[128,2048]{1,0:T(8,128)(2,1)S(1)}, bf16[128,2048]{1,0:T(8,128)(2,1)S(1)}, bf16[128,2048]{1,0:T(8,12...) custom-call(s32[4]{0:T(128)S(1)} %pad_add_fusion.experts_ref, ...), custom_call_target="tpu_custom_call" | custom-call | flops 15032385536 | bytes 42991616 | tf_op jit(solution)/shard_map/pallas_call | solution.py:1432
  317.0 28.2 %shard_map.289 = (bf16[128,2048]{1,0:T(8,128)(2,1)S(1)}, bf16[128,2048]{1,0:T(8,128)(2,1)S(1)}, bf16[128,2048]{1,0:T(8,128)(2,1)S(1)}, bf16[128,2048]{1,0:T(8,12...) custom-call(s32[4]{0:T(128)S(1)} %pad_add_fusion.experts_ref, ...), custom_call_target="tpu_custom_call", output_to_operand_aliasing={{4}: (12, {}), {5}: (13, {}), {6}: (14, {}), {7}: (15, {}),... | custom-call | flops 15032385536 | bytes 42991616 | tf_op jit(solution)/shard_map/pallas_call | solution.py:1432
  347.8 28.2 %shard_map.290 = (bf16[128,2048]{1,0:T(8,128)(2,1)S(1)}, bf16[128,2048]{1,0:T(8,128)(2,1)}, bf16[128,2048]{1,0:T(8,128)(2,1)S(1)}, bf16[128,2048]{1,0:T(8,128)(2...) custom-call(s32[4]{0:T(128)S(1)} %pad_add_fusion.experts_ref, ...), custom_call_target="tpu_custom_call", output_to_operand_aliasing={{4}: (12, {}), {5}: (13, {}), {6}: (14, {}), {7}: (15, {}),... | custom-call | flops 15032385536 | bytes 42991616 | tf_op jit(solution)/shard_map/pallas_call | solution.py:1432
  382.2 8.8 %collective-permute-done.58 = bf16[128,2048]{1,0:T(8,128)(2,1)S(1)} collective-permute-done((bf16[128,2048]{1,0:T(8,128)(2,1)S(1)}, bf16[128,2048]{1,0:T(8,128)(2,1)S(1)}, u32[]{:S(2)}, u32[]{:S(2)}) %collective-permute-start.58) | collective-permute-done | bytes 524320 | tf_op jit(solution)/shard_map/ppermute | solution.py:430
  393.4 8.8 %collective-permute-done.60 = bf16[128,2048]{1,0:T(8,128)(2,1)S(1)} collective-permute-done((bf16[128,2048]{1,0:T(8,128)(2,1)S(1)}, bf16[128,2048]{1,0:T(8,128)(2,1)S(1)}, u32[]{:S(2)}, u32[]{:S(2)}) %collective-permute-start.60) | collective-permute-done | bytes 524320 | tf_op jit(solution)/shard_map/ppermute | solution.py:430
  405.0 8.5 %collective-permute-done.52.refs_17_ = bf16[128,2048]{1,0:T(8,128)(2,1)S(1)} collective-permute-done((bf16[128,2048]{1,0:T(8,128)(2,1)S(1)}, bf16[128,2048]{1,0:T(8,128)(2,1)S(1)}, u32[]{:S(2)}, u32[]{:S(2)}) %collective-permute-start.52) | collective-permute-done | bytes 524320 | tf_op jit(solution)/shard_map/ppermute | solution.py:430
  417.5 28.3 %shard_map.291 = (bf16[128,2048]{1,0:T(8,128)(2,1)S(1)}, bf16[128,2048]{1,0:T(8,128)(2,1)S(1)}, bf16[128,2048]{1,0:T(8,128)(2,1)S(1)}, bf16[128,2048]{1,0:T(8,12...) custom-call(s32[4]{0:T(128)S(1)} %pad_add_fusion.experts_ref, ...), custom_call_target="tpu_custom_call", output_to_operand_aliasing={{4}: (12, {}), {5}: (13, {}), {6}: (14, {}), {7}: (15, {}),... | custom-call | flops 15032385536 | bytes 42991616 | tf_op jit(solution)/shard_map/pallas_call | solution.py:1432
  447.4 21.9 %shard_map.292 = (bf16[128,2048]{1,0:T(8,128)(2,1)S(1)}, bf16[128,2048]{1,0:T(8,128)(2,1)S(1)}, bf16[128,2048]{1,0:T(8,128)(2,1)S(1)}, bf16[128,2048]{1,0:T(8,12...) custom-call(bf16[2048,1792]{1,0:T(8,128)(2,1)} %get-tuple-element.12, ...), custom_call_target="tpu_custom_call" | custom-call | flops 15032385536 | bytes 23068672 | tf_op jit(solution)/shard_map/pallas_call | solution.py:1329
  478.5 18.8 %shard_map.310 = bf16[1,2,704,2048]{3,2,1,0:T(8,128)(2,1)S(1)} custom-call(bf16[2048,2048]{1,0:T(8,128)(2,1)} %get-tuple-element.165.rows_ref.right_ref, bf16[2048,1792]{1,0:T(8,128)(2,1)} %get-tuple-element.167.gate_ref.refs_0_, bf16[2048,1792]{1,0:T(8,128)(2,1)} %get-tuple-element.168.up_ref.refs_1_), custom_call_target="tpu_custom_call" | custom-call | flops 12884901888 | bytes 34603008 | tf_op jit(solution)/shard_map/pallas_call | solution.py:1208
  506.4 11.8 %shard_map.304 = (f32[16,288,128]{2,1,0:T(8,128)S(1)}, bf16[16,288,128]{2,1,0:T(8,128)(2,1)S(1)}, f32[128,2048]{1,0:T(8,128)S(1)}) custom-call(bf16[2048,2048]{1,0:T(8,128)(2,1)} %get-tuple-element.165.rows_ref.right_ref, bf16[2048,2048]{1,0:T(8,128)(2,1)} %get-tuple-element.166.cots_ref.right_ref, bf16[2048,1792]{1,0:T(8,128)(2,1)} %get-tuple-element.167.gate_ref.refs_0_, ...), custom_call_target="tpu_custom_call" | custom-call | flops 8589934592 | bytes 16777216 | tf_op jit(solution)/shard_map/pallas_call | solution.py:1251
  520.1 11.0 %shard_map.320 = bf16[1,1,704,2048]{3,2,1,0:T(8,128)(2,1)} custom-call(bf16[2048,2048]{1,0:T(8,128)(2,1)} %get-tuple-element.166.cots_ref.right_ref, bf16[2048,1792]{1,0:T(8,128)(2,1)} %get-tuple-element.128.refs_0_.hidden_ref), custom_call_target="tpu_custom_call" | custom-call | flops 6442450944 | bytes 23068672 | tf_op jit(solution)/shard_map/pallas_call | solution.py:1208
  556.2 13.1 %shard_map.303 = (bf16[256,2176]{1,0:T(8,128)(2,1)}, bf16[256,2048]{1,0:T(8,128)(2,1)S(1)}, bf16[256,512]{1,0:T(8,128)(2,1)S(1)}, f32[1,512]{1,0:T(1,128)S(1)}) custom-call(s32[5]{0:T(128)S(1)} %concatenate.24.place_ref, s32[1,256]{1,0:T(1,128)S(1)} %copy-done.48, s32[256,1]{1,0:T(8,128)S(1)} %copy-done.20, f32[256,256]{1,0:T(8,128)S(1)} %copy-done.11, ...), custom_call_target="tpu_custom_call" | custom-call | flops 3145728000 | bytes 6291456 | tf_op jit(solution)/shard_map/pallas_call | solution.py:926
  578.2 7.1 shard_map.305
  589.6 7.4 collective-permute-done.71
  602.2 7.0 shard_map.308
  643.7 9.3 %collective-permute-done.70 = bf16[128,2048]{1,0:T(8,128)(2,1)S(1)} collective-permute-done((bf16[128,2048]{1,0:T(8,128)(2,1)S(1)}, bf16[128,2048]{1,0:T(8,128)(2,1)S(1)}, u32[]{:S(2)}, u32[]{:S(2)}) %collective-permute-start.70) | collective-permute-done | bytes 524320 | tf_op jit(solution)/shard_map/ppermute | solution.py:438
  705.3 11.8 %shard_map.321 = f32[1,1,704,2048]{3,2,1,0:T(8,128)} custom-call(bf16[2048,2048]{1,0:T(8,128)(2,1)} %get-tuple-element.166.cots_ref.right_ref, bf16[2048,1792]{1,0:T(8,128)(2,1)} %get-tuple-element.128.refs_0_.hidden_ref, bf16[1,1,704,2048]{3,2,1,0:T(8,128)(2,1)} %collective-permute-done.111.refs_1_, bf16[512,1024]{1,0:T(8,128)(2,1)} %collective-permute-done.91.refs_2_), custom_call_target="tpu_custom_call" | custom-call | flops 6442450944 | bytes 23068672 | tf_op jit(solution)/shard_map/pallas_call | solution.py:1208
  718.7 7.4 collective-permute-done.95
  729.8 21.2 %shard_map.312.refs_1_ = f32[1,2,704,2048]{3,2,1,0:T(8,128)} custom-call(bf16[2048,2048]{1,0:T(8,128)(2,1)} %get-tuple-element.165.rows_ref.right_ref, bf16[2048,1792]{1,0:T(8,128)(2,1)} %get-tuple-element.167.gate_ref.refs_0_, bf16[2048,1792]{1,0:T(8,128)(2,1)} %get-tuple-element.168.up_ref.refs_1_, ...), custom_call_target="tpu_custom_call" | custom-call | flops 12884901888 | bytes 34603008 | tf_op jit(solution)/shard_map/pallas_call | solution.py:1208
  766.2 8.4 %collective-permute-done.102 = bf16[32,2048]{1,0:T(8,128)(2,1)S(1)} collective-permute-done((bf16[32,2048]{1,0:T(8,128)(2,1)S(1)}, bf16[32,2048]{1,0:T(8,128)(2,1)S(1)}, u32[]{:S(2)}, u32[]{:S(2)}) %collective-permute-start.102) | collective-permute-done | bytes 131104 | tf_op jit(solution)/shard_map/ppermute | solution.py:426
  (583 shorter events, 362.7 us)
Async XLA Ops:
  14.5 35.8 %collective-permute-start.1 = (bf16[128,3712]{1,0:T(8,128)(2,1)}, bf16[128,3712]{1,0:T(8,128)(2,1)S(1)}, u32[]{:S(2)}, u32[]{:S(2)}) collective-permute-start(bf16[128,3712]{1,0:T(8,128)(2,1)} %shard_map.281.refs_0_), channel_id=1, source_target_pairs={{0,2},{2,0},{4,6},{6,4},{8,10},{10,8},{12,14},{14,12},{16,18},{18,... | collective-permute-start | bytes 2850824 | tf_op jit(solution)/shard_map/ppermute | solution.py:434
  50.3 143.2 %collective-permute-start.25 = (bf16[1,2,704,2048]{3,2,1,0:T(8,128)(2,1)}, bf16[1,2,704,2048]{3,2,1,0:T(8,128)(2,1)}, u32[]{:S(2)}, u32[]{:S(2)}) collective-permute-start(bf16[1,2,704,2048]{3,2,1,0:T(8,128)(2,1)} %bitcast.84), channel_id=1, source_target_pairs={{0,2},{2,0},{4,6},{6,4},{8,10},{10,8},{12,14},{14,12},{16,18},{18,... | collective-permute-start | bytes 17301512 | tf_op jit(solution)/shard_map/ppermute | solution.py:434
  87.5 65.4 %collective-permute-start.26 = (bf16[1,704,2048]{2,1,0:T(8,128)(2,1)}, bf16[1,704,2048]{2,1,0:T(8,128)(2,1)}, u32[]{:S(2)}, u32[]{:S(2)}) collective-permute-start(bf16[1,704,2048]{2,1,0:T(8,128)(2,1)} %own_down.1), channel_id=1, source_target_pairs={{0,2},{2,0},{4,6},{6,4},{8,10},{10,8},{12,14},{14,12},{16,18},{18,... | collective-permute-start | bytes 8650760 | tf_op jit(solution)/shard_map/ppermute | solution.py:434
  109.2 43.6 %all-to-all-start = ((bf16[16,288,128]{2,1,0:T(8,128)(2,1)}), bf16[16,288,128]{2,1,0:T(8,128)(2,1)S(1)}, u32[]{:S(2)}, u32[]{:S(2)}) async-start(bf16[16,288,128]{2,1,0:T(8,128)(2,1)} %shard_map.284), calls=%async_computation | async-start | bytes 2359296 | tf_op jit(solution)/shard_map/all_to_all | solution.py:1536
  116.0 39.1 %collective-permute-start.36 = (bf16[128,2048]{1,0:T(8,128)(2,1)S(1)}, bf16[128,2048]{1,0:T(8,128)(2,1)}, u32[]{:S(2)}, u32[]{:S(2)}) collective-permute-start(bf16[128,2048]{1,0:T(8,128)(2,1)S(1)} %copy-done.9), channel_id=1, source_target_pairs={{0,4},{2,6},{4,0},{6,2},{8,12},{10,14},{12,8},{14,10},{16,20},{18,... | collective-permute-start | bytes 1572872 | tf_op jit(solution)/shard_map/ppermute | solution.py:430
  117.9 37.7 %collective-permute-start.28 = (bf16[128,2048]{1,0:T(8,128)(2,1)}, bf16[128,2048]{1,0:T(8,128)(2,1)}, u32[]{:S(2)}, u32[]{:S(2)}) collective-permute-start(bf16[128,2048]{1,0:T(8,128)(2,1)} %collective-permute-done.16.refs_16_.refs_4_), channel_id=1, source_target_pairs={{0,8},{2,10},{4,12},{6,14},{8,16},{10,18},{12,20},{14,22},{16,24},... | collective-permute-start | bytes 1572872 | tf_op jit(solution)/shard_map/ppermute | solution.py:426
  152.8 41.9 %collective-permute-start.27 = (bf16[16,288,128]{2,1,0:T(8,128)(2,1)S(1)}, bf16[16,288,128]{2,1,0:T(8,128)(2,1)S(1)}, u32[]{:S(2)}, u32[]{:S(2)}) collective-permute-start(bf16[16,288,128]{2,1,0:T(8,128)(2,1)S(1)} %all-to-all-done.near), channel_id=1, source_target_pairs={{0,2},{2,0},{4,6},{6,4},{8,10},{10,8},{12,14},{14,12},{16,18},{18,... | collective-permute-start | bytes 3538952 | tf_op jit(solution)/shard_map/ppermute | solution.py:434
  155.1 36.1 %collective-permute-start.39 = (bf16[128,2048]{1,0:T(8,128)(2,1)}, bf16[128,2048]{1,0:T(8,128)(2,1)}, u32[]{:S(2)}, u32[]{:S(2)}) collective-permute-start(bf16[128,2048]{1,0:T(8,128)(2,1)} %collective-permute-done.16.refs_16_.refs_4_), channel_id=1, source_target_pairs={{0,1},{1,0},{2,3},{3,2},{4,5},{5,4},{6,7},{7,6},{8,9},{9,8},{10,11... | collective-permute-start | bytes 1572872 | tf_op jit(solution)/shard_map/ppermute | solution.py:438
  245.4 67.4 %collective-permute-start.45 = (bf16[128,2048]{1,0:T(8,128)(2,1)S(1)}, bf16[128,2048]{1,0:T(8,128)(2,1)S(1)}, u32[]{:S(2)}, u32[]{:S(2)}) collective-permute-start(bf16[128,2048]{1,0:T(8,128)(2,1)S(1)} %collective-permute-done.19.refs_11_.refs_0_), channel_id=1, source_target_pairs={{0,1},{1,0},{2,3},{3,2},{4,5},{5,4},{6,7},{7,6},{8,9},{9,8},{10,11... | collective-permute-start | bytes 1572872 | tf_op jit(solution)/shard_map/ppermute | solution.py:438
  272.5 44.6 %collective-permute-start.46 = (bf16[128,2048]{1,0:T(8,128)(2,1)S(1)}, bf16[128,2048]{1,0:T(8,128)(2,1)S(1)}, u32[]{:S(2)}, u32[]{:S(2)}) collective-permute-start(bf16[128,2048]{1,0:T(8,128)(2,1)S(1)} %collective-permute-done.44.refs_1_), channel_id=1, source_target_pairs={{0,1},{1,0},{2,3},{3,2},{4,5},{5,4},{6,7},{7,6},{8,9},{9,8},{10,11... | collective-permute-start | bytes 1572872 | tf_op jit(solution)/shard_map/ppermute | solution.py:438
  274.0 41.3 %collective-permute-start.42 = (bf16[128,2048]{1,0:T(8,128)(2,1)S(1)}, bf16[128,2048]{1,0:T(8,128)(2,1)S(1)}, u32[]{:S(2)}, u32[]{:S(2)}) collective-permute-start(bf16[128,2048]{1,0:T(8,128)(2,1)S(1)} %collective-permute-done.20.refs_0_), channel_id=1, source_target_pairs={{0,1},{1,0},{2,3},{3,2},{4,5},{5,4},{6,7},{7,6},{8,9},{9,8},{10,11... | collective-permute-start | bytes 1572872 | tf_op jit(solution)/shard_map/ppermute | solution.py:438
  310.6 36.2 %collective-permute-start.50 = (bf16[128,2048]{1,0:T(8,128)(2,1)S(1)}, bf16[128,2048]{1,0:T(8,128)(2,1)S(1)}, u32[]{:S(2)}, u32[]{:S(2)}) collective-permute-start(bf16[128,2048]{1,0:T(8,128)(2,1)S(1)} %get-tuple-element.119), channel_id=1, source_target_pairs={{0,4},{2,6},{4,0},{6,2},{8,12},{10,14},{12,8},{14,10},{16,20},{18,... | collective-permute-start | bytes 1572872 | tf_op jit(solution)/shard_map/ppermute | solution.py:430
  311.4 36.4 %collective-permute-start.41 = (bf16[128,2048]{1,0:T(8,128)(2,1)S(1)}, bf16[128,2048]{1,0:T(8,128)(2,1)S(1)}, u32[]{:S(2)}, u32[]{:S(2)}) collective-permute-start(bf16[128,2048]{1,0:T(8,128)(2,1)S(1)} %collective-permute-done.20.refs_0_), channel_id=1, source_target_pairs={{0,4},{2,6},{4,0},{6,2},{8,12},{10,14},{12,8},{14,10},{16,20},{18,... | collective-permute-start | bytes 1572872 | tf_op jit(solution)/shard_map/ppermute | solution.py:430
  312.7 34.6 %collective-permute-start.21 = (bf16[128,2048]{1,0:T(8,128)(2,1)S(1)}, bf16[128,2048]{1,0:T(8,128)(2,1)S(1)}, u32[]{:S(2)}, u32[]{:S(2)}) collective-permute-start(bf16[128,2048]{1,0:T(8,128)(2,1)S(1)} %collective-permute-done.20.refs_0_), channel_id=1, source_target_pairs={{0,8},{2,10},{4,12},{6,14},{8,16},{10,18},{12,20},{14,22},{16,24},... | collective-permute-start | bytes 1572872 | tf_op jit(solution)/shard_map/ppermute | solution.py:426
  345.3 34.9 %collective-permute-start.61 = (bf16[128,2048]{1,0:T(8,128)(2,1)S(1)}, bf16[128,2048]{1,0:T(8,128)(2,1)S(1)}, u32[]{:S(2)}, u32[]{:S(2)}) collective-permute-start(bf16[128,2048]{1,0:T(8,128)(2,1)S(1)} %get-tuple-element.127.refs_16_), channel_id=1, source_target_pairs={{0,1},{1,0},{2,3},{3,2},{4,5},{5,4},{6,7},{7,6},{8,9},{9,8},{10,11... | collective-permute-start | bytes 1572872 | tf_op jit(solution)/shard_map/ppermute | solution.py:438
  378.4 35.1 %collective-permute-start.52 = (bf16[128,2048]{1,0:T(8,128)(2,1)S(1)}, bf16[128,2048]{1,0:T(8,128)(2,1)S(1)}, u32[]{:S(2)}, u32[]{:S(2)}) collective-permute-start(bf16[128,2048]{1,0:T(8,128)(2,1)S(1)} %get-tuple-element.117.refs_15_), channel_id=1, source_target_pairs={{0,4},{2,6},{4,0},{6,2},{8,12},{10,14},{12,8},{14,10},{16,20},{18,... | collective-permute-start | bytes 1572872 | tf_op jit(solution)/shard_map/ppermute | solution.py:430
  380.1 36.6 %collective-permute-start.53 = (bf16[128,2048]{1,0:T(8,128)(2,1)S(1)}, bf16[128,2048]{1,0:T(8,128)(2,1)S(1)}, u32[]{:S(2)}, u32[]{:S(2)}) collective-permute-start(bf16[128,2048]{1,0:T(8,128)(2,1)S(1)} %add_convert_fusion.14.refs_16_), channel_id=1, source_target_pairs={{0,1},{1,0},{2,3},{3,2},{4,5},{5,4},{6,7},{7,6},{8,9},{9,8},{10,11... | collective-permute-start | bytes 1572872 | tf_op jit(solution)/shard_map/ppermute | solution.py:438
  402.2 97.6 %collective-permute-start.57 = (bf16[128,2048]{1,0:T(8,128)(2,1)}, bf16[128,2048]{1,0:T(8,128)(2,1)}, u32[]{:S(2)}, u32[]{:S(2)}) collective-permute-start(bf16[128,2048]{1,0:T(8,128)(2,1)} %get-tuple-element.138), channel_id=1, source_target_pairs={{0,4},{2,6},{4,0},{6,2},{8,12},{10,14},{12,8},{14,10},{16,20},{18,... | collective-permute-start | bytes 1572872 | tf_op jit(solution)/shard_map/ppermute | solution.py:430
  413.4 86.4 %collective-permute-start.62 = (bf16[128,2048]{1,0:T(8,128)(2,1)}, bf16[128,2048]{1,0:T(8,128)(2,1)}, u32[]{:S(2)}, u32[]{:S(2)}) collective-permute-start(bf16[128,2048]{1,0:T(8,128)(2,1)} %add_convert_fusion.10), channel_id=1, source_target_pairs={{0,8},{2,10},{4,12},{6,14},{8,16},{10,18},{12,20},{14,22},{16,24},... | collective-permute-start | bytes 1572872 | tf_op jit(solution)/shard_map/ppermute | solution.py:426
  415.2 84.6 %collective-permute-start.59 = (bf16[128,2048]{1,0:T(8,128)(2,1)}, bf16[128,2048]{1,0:T(8,128)(2,1)}, u32[]{:S(2)}, u32[]{:S(2)}) collective-permute-start(bf16[128,2048]{1,0:T(8,128)(2,1)} %add_convert_fusion.11), channel_id=1, source_target_pairs={{0,1},{1,0},{2,3},{3,2},{4,5},{5,4},{6,7},{7,6},{8,9},{9,8},{10,11... | collective-permute-start | bytes 1572872 | tf_op jit(solution)/shard_map/ppermute | solution.py:438
  476.5 41.8 %collective-permute-start.56 = (bf16[128,2048]{1,0:T(8,128)(2,1)}, bf16[128,2048]{1,0:T(8,128)(2,1)}, u32[]{:S(2)}, u32[]{:S(2)}) collective-permute-start(bf16[128,2048]{1,0:T(8,128)(2,1)} %shard_map.294), channel_id=1, source_target_pairs={{0,1},{1,0},{2,3},{3,2},{4,5},{5,4},{6,7},{7,6},{8,9},{9,8},{10,11... | collective-permute-start | bytes 1572872 | tf_op jit(solution)/shard_map/ppermute | solution.py:438
  539.6 123.7 %all-to-all-start.1 = ((bf16[16,288,128]{2,1,0:T(8,128)(2,1)}), bf16[16,288,128]{2,1,0:T(8,128)(2,1)}, u32[]{:S(2)}, u32[]{:S(2)}) async-start(bf16[16,288,128]{2,1,0:T(8,128)(2,1)} %add_convert_fusion), calls=%async_computation.1 | async-start | bytes 2359296 | tf_op jit(solution)/shard_map/all_to_all | solution.py:1680
  544.0 69.6 %collective-permute-start.76 = (bf16[128,2048]{1,0:T(8,128)(2,1)}, bf16[128,2048]{1,0:T(8,128)(2,1)}, u32[]{:S(2)}, u32[]{:S(2)}) collective-permute-start(bf16[128,2048]{1,0:T(8,128)(2,1)} %shard_map.302), channel_id=1, source_target_pairs={{0,1},{1,0},{2,3},{3,2},{4,5},{5,4},{6,7},{7,6},{8,9},{9,8},{10,11... | collective-permute-start | bytes 1572872 | tf_op jit(solution)/shard_map/ppermute | solution.py:438
  545.6 39.8 %collective-permute-start.74 = (bf16[128,2048]{1,0:T(8,128)(2,1)}, bf16[128,2048]{1,0:T(8,128)(2,1)}, u32[]{:S(2)}, u32[]{:S(2)}) collective-permute-start(bf16[128,2048]{1,0:T(8,128)(2,1)} %shard_map.301), channel_id=1, source_target_pairs={{0,1},{1,0},{2,3},{3,2},{4,5},{5,4},{6,7},{7,6},{8,9},{9,8},{10,11... | collective-permute-start | bytes 1572872 | tf_op jit(solution)/shard_map/ppermute | solution.py:438
  546.1 83.3 %collective-permute-start.73 = (bf16[128,2048]{1,0:T(8,128)(2,1)}, bf16[128,2048]{1,0:T(8,128)(2,1)}, u32[]{:S(2)}, u32[]{:S(2)}) collective-permute-start(bf16[128,2048]{1,0:T(8,128)(2,1)} %shard_map.300), channel_id=1, source_target_pairs={{0,1},{1,0},{2,3},{3,2},{4,5},{5,4},{6,7},{7,6},{8,9},{9,8},{10,11... | collective-permute-start | bytes 1572872 | tf_op jit(solution)/shard_map/ppermute | solution.py:438
  547.6 49.4 %collective-permute-start.71 = (bf16[128,2048]{1,0:T(8,128)(2,1)}, bf16[128,2048]{1,0:T(8,128)(2,1)}, u32[]{:S(2)}, u32[]{:S(2)}) collective-permute-start(bf16[128,2048]{1,0:T(8,128)(2,1)} %shard_map.299), channel_id=1, source_target_pairs={{0,1},{1,0},{2,3},{3,2},{4,5},{5,4},{6,7},{7,6},{8,9},{9,8},{10,11... | collective-permute-start | bytes 1572872 | tf_op jit(solution)/shard_map/ppermute | solution.py:438
  615.6 42.3 %collective-permute-start.89 = (bf16[1024,1024]{1,0:T(8,128)(2,1)}, bf16[1024,1024]{1,0:T(8,128)(2,1)}, u32[]{:S(2)}, u32[]{:S(2)}) collective-permute-start(bf16[1024,1024]{1,0:T(8,128)(2,1)} %shard_map.308), channel_id=1, source_target_pairs={{0,2},{2,0},{4,6},{6,4},{8,10},{10,8},{12,14},{14,12},{16,18},{18,... | collective-permute-start | bytes 6291464 | tf_op jit(solution)/shard_map/ppermute | solution.py:434
  629.4 100.3 %collective-permute-start.90 = (bf16[1,2,704,2048]{3,2,1,0:T(8,128)(2,1)}, bf16[1,2,704,2048]{3,2,1,0:T(8,128)(2,1)}, u32[]{:S(2)}, u32[]{:S(2)}) collective-permute-start(bf16[1,2,704,2048]{3,2,1,0:T(8,128)(2,1)} %copy-done.49), channel_id=1, source_target_pairs={{0,2},{2,0},{4,6},{6,4},{8,10},{10,8},{12,14},{14,12},{16,18},{18,... | collective-permute-start | bytes 17301512 | tf_op jit(solution)/shard_map/ppermute | solution.py:434
  653.0 51.8 %collective-permute-start.111 = (bf16[1,1,704,2048]{3,2,1,0:T(8,128)(2,1)}, bf16[1,1,704,2048]{3,2,1,0:T(8,128)(2,1)}, u32[]{:S(2)}, u32[]{:S(2)}) collective-permute-start(bf16[1,1,704,2048]{3,2,1,0:T(8,128)(2,1)} %shard_map.320), channel_id=1, source_target_pairs={{0,2},{2,0},{4,6},{6,4},{8,10},{10,8},{12,14},{14,12},{16,18},{18,... | collective-permute-start | bytes 8650760 | tf_op jit(solution)/shard_map/ppermute | solution.py:434
  682.5 43.5 %collective-permute-start.95 = (bf16[512,1152]{1,0:T(8,128)(2,1)S(1)}, bf16[512,1152]{1,0:T(8,128)(2,1)}, u32[]{:S(2)}, u32[]{:S(2)}) collective-permute-start(bf16[512,1152]{1,0:T(8,128)(2,1)S(1)} %copy-done.8), channel_id=1, source_target_pairs={{0,4},{2,6},{4,0},{6,2},{8,12},{10,14},{12,8},{14,10},{16,20},{18,... | collective-permute-start | bytes 3538952 | tf_op jit(solution)/shard_map/ppermute | solution.py:430
  704.8 72.3 %collective-permute-start.105 = (bf16[1024,1024]{1,0:T(8,128)(2,1)}, bf16[1024,1024]{1,0:T(8,128)(2,1)S(1)}, u32[]{:S(2)}, u32[]{:S(2)}) collective-permute-start(bf16[1024,1024]{1,0:T(8,128)(2,1)} %shard_map.316), channel_id=1, source_target_pairs={{0,2},{2,0},{4,6},{6,4},{8,10},{10,8},{12,14},{14,12},{16,18},{18,... | collective-permute-start | bytes 6291464 | tf_op jit(solution)/shard_map/ppermute | solution.py:434
  718.4 42.1 %collective-permute-start.101 = (bf16[128,2048]{1,0:T(8,128)(2,1)}, bf16[128,2048]{1,0:T(8,128)(2,1)}, u32[]{:S(2)}, u32[]{:S(2)}) collective-permute-start(bf16[128,2048]{1,0:T(8,128)(2,1)} %slice.288), channel_id=1, source_target_pairs={{0,4},{2,6},{4,0},{6,2},{8,12},{10,14},{12,8},{14,10},{16,20},{18,... | collective-permute-start | bytes 1572872 | tf_op jit(solution)/shard_map/ppermute | solution.py:430
  (191 other events, 3119.2 us)

commit v6 on v5

--- a/solution.py
+++ b/solution.py
@@ -482,14 +482,10 @@
     return own, other_y(beside), other_x(across)
 
 
-def ring_rows(closed):
-    moving = None
-    for distance in (1, 2, 3, 0):
-        own, from_y, from_x = closed[distance]
-        total = own.astype(jnp.float32) + from_y.astype(jnp.float32) + from_x.astype(jnp.float32)
-        if moving is not None:
-            total = total + ring_step(moving).astype(jnp.float32)
-        moving = total.astype(jnp.bfloat16)
+def wide_sum(*values):
+    total = values[0].astype(jnp.float32)
+    for value in values[1:]:
+        total = total + value.astype(jnp.float32)
     return total
 
 
@@ -509,8 +505,9 @@
 
 def gather_weight(held):
     chunks = []
+    beside = None
     for distance, current in enumerate(held):
-        beside = other_y(current)
+        beside = other_y(current if beside is None else after(current, beside))
         for flip_y, chunk in ((0, current), (1, beside)):
             for flip_core, piece in ((0, chunk), (1, other_core(chunk))):
                 chunks.append(((distance, flip_y, flip_core), piece))
@@ -956,22 +953,19 @@
     )
 
 
-def block_grads_kernel(places_ref, left_ref, right_ref, *refs):
+def block_grads_kernel(extra, places_ref, left_ref, right_ref, *refs):
     result = dot_rows(left_ref[...], right_ref[...])
-    if len(refs) > 1:
+    if extra:
         result += refs[0][...].astype(jnp.float32)
     refs[-1][...] = result.astype(jnp.bfloat16)
 
 
-def block_grads(left, right, places, first, count, arrived=None, others=()):
-    rows, width = right.shape
+def block_grads(left, right, width, places, first, count, arrived=None):
+    rows = right.shape[0]
     size = left.shape[1] // places.shape[0]
-    block = pl.BlockSpec((size, width), lambda i, where: (i, 0))
     extra = [] if arrived is None else [arrived]
     return pl.pallas_call(
-        lambda places_ref, left_ref, right_ref, *refs: block_grads_kernel(
-            places_ref, left_ref, right_ref, *refs[: len(extra)], refs[-1]
-        ),
+        functools.partial(block_grads_kernel, len(extra)),
         grid_spec=pltpu.PrefetchScalarGridSpec(
             num_scalar_prefetch=1,
             grid=(count,),
@@ -979,9 +973,8 @@
                 pl.BlockSpec((rows, size), lambda i, where: (0, where[first + i])),
                 pl.BlockSpec((rows, width), lambda i, where: (0, 0)),
             ]
-            + [pl.BlockSpec((size, width), lambda i, where: (first + i, 0))] * len(extra)
-            + [pl.BlockSpec(memory_space=pl.ANY)] * len(others),
-            out_specs=block,
+            + [pl.BlockSpec((size, width), lambda i, where: (first + i, 0))] * len(extra),
+            out_specs=pl.BlockSpec((size, width), lambda i, where: (i, 0)),
         ),
         out_shape=jax.ShapeDtypeStruct((count * size, width), jnp.bfloat16),
         cost_estimate=pl.CostEstimate(
@@ -989,51 +982,132 @@
             bytes_accessed=2 * (count * size * width + rows * width),
             transcendentals=0,
         ),
-    )(places, left, right, *extra, *others)
+    )(places, left, right, *extra)
+
+
+def mixed_grads_kernel(first, extra, places_ref, *refs):
+    normed_ref, right_ref, small_ref, latent_ref, keyval_ref, grad_ref, attended_ref = refs[:7]
+    out_ref, keyval_all = refs[-2:]
+    step = pl.program_id(0)
+    size = normed_ref.shape[1]
+    blocks = places_ref.shape[0]
+    latent_size = latent_ref.shape[1] // blocks
+    parts = size // latent_size
+    columns = keyval_ref.shape[1] // parts
+
+    @pl.when(step == 0)
+    def _():
+        for k in range(parts):
+            some = slice(k * columns, (k + 1) * columns)
+            keyval_all[:, some] = dot_rows(latent_ref[...], keyval_ref[:, some])
+
+    low = jnp.bfloat16
+    at = right_ref.shape[1]
+    result = dot_rows(normed_ref[...], right_ref[...])
+    small = jnp.transpose(small_ref[...])
+    result = result + jnp.concatenate(
+        [jnp.zeros((size, at - small.shape[1]), jnp.float32), small], axis=1
+    )
+    start = pl.multiple_of(places_ref[first + step] * latent_size, latent_size)
+    strip = keyval_all[pl.ds(start, latent_size), :]
+    keyval = jnp.concatenate([strip[:, k * columns : (k + 1) * columns] for k in range(parts)], axis=0)
+    output = dot_rows(grad_ref[...], attended_ref[...])
+    for value, begin in ((result, 0), (keyval, at), (output, at + columns)):
+        end = begin + value.shape[1]
+        if extra:
+            value = value + refs[7][:, begin:end].astype(jnp.float32)
+        out_ref[:, begin:end] = value.astype(low)
+
+
+def mixed_grads(normed, right, small, latent, keyval, grad, attended, places, first, count, arrived=None):
+    rows, width = right.shape
+    blocks = places.shape[0]
+    size = normed.shape[1] // blocks
+    parts = size // (latent.shape[1] // blocks)
+    total = width + keyval.shape[1] // parts + attended.shape[1]
+    extra = [] if arrived is None else [arrived]
+
+    def block(i, where):
+        return (0, where[first + i])
+
+    def still(array):
+        return pl.BlockSpec(array.shape, lambda i, where: (0, 0))
+
+    return pl.pallas_call(
+        functools.partial(mixed_grads_kernel, first, len(extra)),
+        grid_spec=pltpu.PrefetchScalarGridSpec(
+            num_scalar_prefetch=1,
+            grid=(count,),
+            in_specs=[
+                pl.BlockSpec((rows, size), block),
+                still(right),
+                pl.BlockSpec((small.shape[0], size), block),
+                still(latent),
+                still(keyval),
+                pl.BlockSpec((rows, size), block),
+                still(attended),
+            ]
+            + [pl.BlockSpec((size, total), lambda i, where: (first + i, 0))] * len(extra),
+            out_specs=pl.BlockSpec((size, total), lambda i, where: (i, 0)),
+            scratch_shapes=[pltpu.VMEM((latent.shape[1], keyval.shape[1]), jnp.float32)],
+        ),
+        out_shape=jax.ShapeDtypeStruct((count * size, total), jnp.bfloat16),
+        compiler_params=pltpu.CompilerParams(vmem_limit_bytes=32 * 1024 * 1024),
+        cost_estimate=pl.CostEstimate(
+            flops=2 * rows * count * size * total,
+            bytes_accessed=2 * (count * size * total + rows * total),
+            transcendentals=0,
+        ),
+    )(places, normed, right, small, latent, keyval, grad, attended, *extra)
+
+
+def first_back_kernel(place_ref, own_ref, other_ref, grad_ref, weight_ref, own_out, sent_out, gain_ref):
+    local_rows = own_ref.shape[0]
+    x = place_ref[3]
+    size = weight_ref.shape[0] // 4
+    for ref, start, out in (
+        (own_ref, x * local_rows, own_out),
+        (other_ref, (1 - x) * local_rows, sent_out),
+    ):
+        rows = ref[...].astype(jnp.float32)
+        unit = rows * lax.rsqrt(jnp.mean(rows * rows, axis=1, keepdims=True) + EPSILON)
+        grads = grad_ref[pl.ds(pl.multiple_of(start, local_rows), local_rows), :]
+        for k in range(4):
+            some = slice(k * size, (k + 1) * size)
+            part = dot_turned(grads, weight_ref[some, :])
+            out[:, some] = part.astype(out.dtype)
+            gain = jnp.sum(part * unit[:, some], axis=0, keepdims=True)
+            if ref is own_ref:
+                gain_ref[:, some] = gain
+            else:
+                gain_ref[:, some] += gain
+
+
+def first_back(place, own, other, grads, weight):
+    f32, bf16 = jnp.float32, jnp.bfloat16
+    depth = weight.shape[0]
+    return pl.pallas_call(
+        first_back_kernel,
+        out_shape=[
+            jax.ShapeDtypeStruct(own.shape, f32),
+            jax.ShapeDtypeStruct(own.shape, bf16),
+            jax.ShapeDtypeStruct((1, depth), f32),
+        ],
+        in_specs=[pl.BlockSpec(memory_space=pltpu.SMEM)] + in_vmem(4),
+        out_specs=in_vmem(3),
+        compiler_params=pltpu.CompilerParams(vmem_limit_bytes=32 * 1024 * 1024),
+        cost_estimate=pl.CostEstimate(
+            flops=4 * own.shape[0] * weight.shape[0] * weight.shape[1],
+            bytes_accessed=2 * weight.shape[0] * weight.shape[1],
+            transcendentals=0,
+        ),
+    )(place, own, other, grads, weight)
 
 
 def close_ring(near, arrived):
     size = near.shape[0] // RINGS
     total = near.astype(jnp.float32) + arrived.astype(jnp.float32)
     return ring_sum([total[r * size : (r + 1) * size] for r in range(RINGS)], jnp.bfloat16)
-
-
-def scatter_product(left, right, places, others):
-    sent = block_grads(left, right, places, 2 * RINGS, 2 * RINGS, None, others)
-    arrived = other_core(sent)
-    far = block_grads(left, right, places, RINGS, RINGS, arrived)
-    from_y = other_y(far)
-    near = block_grads(left, right, places, 0, RINGS, arrived)
-    return close_ring(near, from_y)
-
-
-def latent_blocks_kernel(places_ref, left_ref, right_ref, out_ref, whole_ref):
-    blocks = places_ref.shape[0]
-    size = left_ref.shape[1] // blocks
-    pieces = 4
-    part = right_ref.shape[1] // pieces
-    for k in range(pieces):
-        columns = slice(k * part, (k + 1) * part)
-        whole_ref[:, columns] = dot_rows(left_ref[...], right_ref[:, columns])
-    for k in range(blocks):
-        start = pl.multiple_of(places_ref[k] * size, size)
-        out_ref[k * size : (k + 1) * size, :] = whole_ref[pl.ds(start, size), :].astype(
-            jnp.bfloat16
-        )
-
-
-def latent_blocks(left, right, places, others):
-    shape = (left.shape[1], right.shape[1])
-    return pl.pallas_call(
-        lambda places_ref, left_ref, right_ref, *refs: latent_blocks_kernel(
-            places_ref, left_ref, right_ref, *refs[len(others) :]
-        ),
-        out_shape=jax.ShapeDtypeStruct(shape, jnp.bfloat16),
-        in_specs=[pl.BlockSpec(memory_space=pltpu.SMEM)] + in_vmem(2) + in_place(len(others)),
-        out_specs=pl.BlockSpec(memory_space=pltpu.VMEM),
-        scratch_shapes=[pltpu.VMEM(shape, jnp.float32)],
-        compiler_params=pltpu.CompilerParams(vmem_limit_bytes=32 * 1024 * 1024),
-    )(places, left, right, *others)
 
 
 def pack_kernel(heads, query_ref, latent_ref, small_ref, keyval_ref, output_ref, out_ref):
@@ -1311,43 +1385,14 @@
     )(*pieces, down, *kept, *others)
 
 
-def out_kernel(count, *refs):
-    hidden_ref, weight_ref = refs[:2]
-    outs = refs[2:]
-    size = outs[0].shape[0]
-    for k in range(0, count, 4):
-        part = hidden_ref[k * size : (k + 4) * size, :]
-        result = wide_dot(part, weight_ref[...]).astype(jnp.bfloat16)
-        for j in range(4):
-            outs[k + j][...] = result[j * size : (j + 1) * size]
-
-
-def out_rows(count, hidden, down):
-    rows, width = hidden.shape
-    depth = down.shape[1]
-    size = rows // count
-    return pl.pallas_call(
-        functools.partial(out_kernel, count),
-        grid=(depth // TILE,),
-        in_specs=[whole(hidden), pl.BlockSpec((width, TILE), lambda i: (0, i))],
-        out_specs=[pl.BlockSpec((size, TILE), lambda i: (0, i))] * count,
-        out_shape=[jax.ShapeDtypeStruct((size, depth), jnp.bfloat16)] * count,
-        compiler_params=pltpu.CompilerParams(vmem_limit_bytes=48 * 1024 * 1024),
-        cost_estimate=pl.CostEstimate(
-            flops=2 * rows * depth * width,
-            bytes_accessed=2 * (rows * depth + depth * width + rows * width),
-            transcendentals=0,
-        ),
-    )(hidden, down)
-
-
-def mlp_kernel(tiles, pieces, others, experts_ref, routed_ref, *refs):
+def mlp_kernel(tiles, columns, joined, pieces, others, experts_ref, routed_ref, *refs):
     row_refs = refs[:pieces]
-    router_ref, gate_col, up_col, down_grad, gate_row, up_row = refs[pieces : pieces + 6]
-    outs = refs[pieces + 6 + others :]
-    grad_refs = outs[:pieces]
-    rows_out, hidden_out, gate_out, up_out, logit_out = outs[pieces : pieces + 5]
-    gate_all, up_all, prob_ref, scale_ref, sum_ref, semaphores = outs[pieces + 5 :]
+    router_ref, gate_col, up_col, down_grad, gate_row, up_row, down_row = refs[pieces : pieces + 7]
+    outs = refs[pieces + 7 + others :]
+    grad_refs, out_refs = outs[:pieces], outs[:pieces] if joined else outs[pieces : 2 * pieces]
+    outs = outs[pieces if joined else 2 * pieces :]
+    rows_out, hidden_out, gate_out, up_out, logit_out = outs[:5]
+    hidden_all, gate_all, up_all, prob_ref, scale_ref, sum_ref, semaphores = outs[5:]
     step = pl.program_id(0)
     third = tiles // 2
     total = rows_out.shape[0]
@@ -1370,7 +1415,7 @@
 
     @pl.when(step < tiles)
     def _():
-        columns = pl.ds(pl.multiple_of(step * TILE, TILE), TILE)
+        columns_here = pl.ds(pl.multiple_of(step * TILE, TILE), TILE)
         kind = step // third
         half = total // 2
         for k in (0, 1):
@@ -1388,9 +1433,11 @@
                 jnp.bfloat16
             )
             low_up = (grad_hidden * silu).astype(jnp.bfloat16)
-            gate_all[part, columns] = low_gate
-            up_all[part, columns] = low_up
-            hidden_out[part, :] = (scale * hidden).astype(jnp.bfloat16)
+            gate_all[part, columns_here] = low_gate
+            up_all[part, columns_here] = low_up
+            low_hidden = (scale * hidden).astype(jnp.bfloat16)
+            hidden_all[part, columns_here] = low_hidden
+            hidden_out[part, :] = low_hidden
             gate_out[part, :] = low_gate
             up_out[part, :] = low_up
 
@@ -1402,7 +1449,7 @@
             grad_logits += scale_ref[k] * sum_ref[k] * (own - prob_ref[...])
         logit_out[...] = grad_logits.astype(jnp.bfloat16)
 
-    @pl.when(step >= tiles)
+    @pl.when((step >= tiles) & (step < tiles + columns))
     def _():
         some = pl.ds(pl.multiple_of((step - tiles) * 2 * TILE, TILE), 2 * TILE)
         grads = wide_dot(gate_all[...], gate_row[...]) + wide_dot(up_all[...], up_row[...])
@@ -1411,8 +1458,15 @@
         for k in range(pieces):
             grad_refs[k][...] = grads[k * size : (k + 1) * size]
 
-
-def mlp_plane(distance, experts, routed, rows, down_grad, router, gate, up, kept, others):
+    @pl.when(step >= tiles + columns)
+    def _():
+        result = wide_dot(hidden_all[...], down_row[...]).astype(jnp.bfloat16)
+        for k in range(pieces):
+            out_refs[k][...] = result[k * size : (k + 1) * size]
+
+
+def mlp_plane(distance, joined, experts, routed, rows, down_grad, router, weights, kept, others):
+    gate, up, down = weights
     pieces = len(rows)
     size, depth = rows[0].shape
     width = gate.shape[0]
@@ -1424,26 +1478,42 @@
         return jnp.minimum(i, tiles - 1)
 
     def late(i):
-        return jnp.maximum(i - tiles, 0)
+        return jnp.clip(i - tiles, 0, columns - 1)
+
+    def last(i):
+        return jnp.maximum(i - tiles - columns, 0)
 
     tile_spec = pl.BlockSpec((total, TILE), lambda i: (distance, early(i)))
-    anywhere = pl.BlockSpec(memory_space=pl.ANY)
-    first_kept = 2 + pieces + 6
+    weight_tile = pl.BlockSpec((TILE, depth), lambda i: (early(i), 0))
+    if joined:
+        result_specs = [
+            pl.BlockSpec((size, 2 * TILE), lambda i: (0, jnp.maximum(i - tiles, 0)))
+        ] * pieces
+        result_shapes = [jax.ShapeDtypeStruct((size, 2 * depth), low)] * pieces
+    else:
+        result_specs = [pl.BlockSpec((size, 2 * TILE), lambda i: (0, late(i)))] * pieces + [
+            pl.BlockSpec((size, 2 * TILE), lambda i: (0, last(i)))
+        ] * pieces
+        result_shapes = [jax.ShapeDtypeStruct((size, depth), low)] * (2 * pieces)
+    first_kept = 2 + pieces + 7
     results = pl.pallas_call(
-        functools.partial(mlp_kernel, tiles, pieces, len(kept) + len(others)),
-        grid=(tiles + columns,),
+        functools.partial(
+            mlp_kernel, tiles, columns, joined, pieces, len(kept) + len(others)
+        ),
+        grid=(tiles + 2 * columns,),
         in_specs=[pl.BlockSpec(memory_space=pltpu.SMEM), whole(routed)]
-        + [anywhere] * pieces
+        + in_place(pieces)
         + [
             pl.BlockSpec((depth, 128), lambda i: (0, router.shape[1] // 128 - 1)),
-            pl.BlockSpec((TILE, depth), lambda i: (early(i), 0)),
-            pl.BlockSpec((TILE, depth), lambda i: (early(i), 0)),
+            weight_tile,
+            weight_tile,
             tile_spec,
             pl.BlockSpec((width, 2 * TILE), lambda i: (0, late(i))),
             pl.BlockSpec((width, 2 * TILE), lambda i: (0, late(i))),
+            pl.BlockSpec((width, 2 * TILE), lambda i: (0, last(i))),
         ]
-        + [anywhere] * (len(kept) + len(others)),
-        out_specs=[pl.BlockSpec((size, 2 * TILE), lambda i: (0, late(i)))] * pieces
+        + in_place(len(kept) + len(others)),
+        out_specs=result_specs
         + [
             pl.BlockSpec((total, depth), lambda i: (distance, 0)),
             tile_spec,
@@ -1451,27 +1521,30 @@
             tile_spec,
             pl.BlockSpec((total, 128), lambda i: (distance, 0)),
         ],
-        out_shape=[jax.ShapeDtypeStruct((size, depth), low)] * pieces
+        out_shape=result_shapes
         + [
             jax.ShapeDtypeStruct((RINGS * total, many), low)
             for many in (depth, width, width, width, 128)
         ],
-        scratch_shapes=[pltpu.VMEM((total, width), low)] * 2
+        scratch_shapes=[pltpu.VMEM((total, width), low)] * 3
         + [
             pltpu.VMEM((total, 128), jnp.float32),
             pltpu.VMEM((3, total, 1), jnp.float32),
             pltpu.VMEM((3, total, 1), jnp.float32),
             pltpu.SemaphoreType.DMA((pieces,)),
         ],
-        input_output_aliases={first_kept + k: pieces + k for k in range(len(kept))},
-        compiler_params=pltpu.CompilerParams(vmem_limit_bytes=48 * 1024 * 1024),
+        input_output_aliases={
+            first_kept + k: len(result_shapes) + k for k in range(len(kept))
+        },
+        compiler_params=pltpu.CompilerParams(vmem_limit_bytes=56 * 1024 * 1024),
         cost_estimate=pl.CostEstimate(
-            flops=2 * total * depth * width * 4,
-            bytes_accessed=2 * (4 * depth * width + 3 * total * depth + 4 * total * width),
+            flops=2 * total * depth * width * 5,
+            bytes_accessed=2 * (5 * depth * width + 4 * total * depth + 4 * total * width),
             transcendentals=total * width,
         ),
-    )(experts, routed, *rows, router, gate, up, down_grad, gate, up, *kept, *others)
-    return results[:pieces], results[pieces:]
+    )(experts, routed, *rows, router, gate, up, down_grad, gate, up, down, *kept, *others)
+    count = len(result_shapes)
+    return results[:pieces], results[pieces:count], results[count:]
 
 
 def gather_body(
@@ -1572,7 +1645,7 @@
         chunks,
         heads,
         sizes,
-        (grad_planes[1][0], grad_planes[0][2]),
+        (grad_planes[2][0], grad_planes[0][1], grad_planes[0][2], grad_planes[1][2], shared_near),
     )
     attn_gain_wide, ffn_gain_wide = gains[0], gains[1]
     mixed = block_input.astype(f32) + own_part + other_x(sent_part).astype(f32)
@@ -1614,14 +1687,18 @@
         (second_normed,),
     )
     half_kept = down_grads(
-        0, [piece for plane in grad_planes[:2] for piece in plane], down_weight, (), ()
+        0,
+        [piece for plane in grad_planes[:2] for piece in plane],
+        down_weight,
+        (),
+        (row_planes[1][0], row_planes[0][1], row_planes[0][2]),
     )
     down_grad, every_grad = down_grads(
         1,
         [piece for plane in grad_planes[2:] for piece in plane],
         down_weight,
         half_kept,
-        (row_planes[1][0],),
+        (row_planes[2][0], row_planes[0][3]),
     )
     expert_ids = jnp.concatenate(
         [chip_experts, jnp.array([experts, used + 3 - query_width - KVR], jnp.int32)]
@@ -1629,18 +1706,20 @@
     kept = []
     turned, closed = [], []
     for distance in range(RINGS):
-        others = list(turned[distance - 2][1:]) if distance > 1 else []
-        if distance > 2:
-            others += list(closed[distance - 3][1:])
-        grads, kept = mlp_plane(
+        others = [row_planes[3][0]] if distance == 0 else []
+        if distance == 2:
+            others = list(turned[0][1:])
+        elif distance == 3:
+            others = list(turned[1][1:]) + list(closed[0][1:])
+        grads, outs, kept = mlp_plane(
             distance,
+            distance < RINGS - 1,
             expert_ids,
             routed[distance],
             row_planes[distance],
             down_grad,
             first_weight,
-            gate_weight,
-            up_weight,
+            (gate_weight, up_weight, down_weight),
             kept,
             others,
         )
@@ -1648,22 +1727,6 @@
         if distance < RINGS - 1:
             closed.append(close_plane(turned[distance]))
     every_row, every_hidden, every_gate_grad, every_up_grad, logit_grads = kept
-    out_pieces = out_rows(4 * RINGS, every_hidden, down_weight)
-    own, beside, across = turned[3]
-    closed.append(close_plane((own, after(beside, out_pieces[0]), after(across, out_pieces[0]))))
-    grad_second = ring_rows(closed)
-    out_closed = []
-    for distance in range(RINGS):
-        plane = list(out_pieces[4 * distance : 4 * distance + 4])
-        plane[3] = after(plane[3], grad_second)
-        plane[2] = after(plane[2], grad_second)
-        out_closed.append(close_plane(turn_corner(plane, "x")))
-    block_output = mixed + ring_rows(out_closed)
-
-    arrived_in = other_core(
-        expert_grads((every_gate_grad, every_up_grad), every_row, units, 1, None, bf16)
-    )
-    arrived_down = other_core(expert_grads((every_hidden,), every_grad, units, 1, None, bf16))
     shared_kept, shared_sent, logit_rows = side_grads(
         every_row,
         every_grad,
@@ -1674,8 +1737,28 @@
         shared,
         blocks,
     )
+    sent_down = expert_grads((every_hidden,), every_grad, units, 1, None, bf16)
+    moving = ring_step(wide_sum(*closed[1]).astype(bf16))
+    moving = ring_step(wide_sum(moving, *closed[2]).astype(bf16))
+    own, beside, across = turned[3]
+    grad_close = close_plane((own, after(beside, shared_sent), across))
+    grad_second = wide_sum(
+        ring_step(
+            after(wide_sum(moving[:, :D], *grad_close).astype(bf16), sent_down)
+        ),
+        *[part[:, :D] for part in closed[0]],
+    )
+    outs = list(outs)
+    outs[3] = after(outs[3], grad_close[1])
+    out_close = close_plane(turn_corner(outs, corners[3]))
+    block_output = mixed + wide_sum(
+        ring_step(wide_sum(moving[:, D:], *out_close).astype(bf16)),
+        *[part[:, D:] for part in closed[0]],
+    )
+
+    arrived_down = other_core(sent_down)
     router_at = used + 3 - query_width - KVR
-    grad_router = logit_rows[router_at : router_at + experts].reshape(experts, blocks, depth)
+    grad_router = logit_rows[router_at : router_at + experts]
     grad_shared_in, grad_shared_down = unpack_shared(
         lax.all_to_all(
             add_low(shared_kept, other_core(shared_sent)),
@@ -1713,86 +1796,97 @@
         ],
         axis=0,
     )
-    middle = heads * NOPE
-    edges = ((0, middle), (middle, first_width))
-    parts = [projected_grad[:, start:end] for start, end in edges]
-    arrived = [
-        other_core(block_grads(first_normed, part, places, 2 * RINGS, 2 * RINGS))
-        for part in parts
+    cut = (query_width + KVR) // TILE * TILE - TILE
+    arrived = [other_core(block_grads(first_normed, projected_grad, cut, places, 8, 8))]
+    own_first, sent_first, gain_attn_part = first_back(
+        place, block_input, other_input, projected_grad, first_weight
+    )
+    grad_first = own_first + other_x(sent_first).astype(f32)
+    small_rows = jnp.concatenate(
+        [
+            jnp.zeros((ROPE, D), f32),
+            gain_attn_part,
+            gain_ffn_part[None],
+            jnp.pad(
+                gain_latent_part.reshape(blocks, latent_depth),
+                ((0, 0), (0, depth - latent_depth)),
+            ).reshape(1, D),
+            grad_router,
+            jnp.zeros((128 - ROPE - 3 - experts, D), f32),
+        ],
+        axis=0,
+    )
+    mixed_parts = (
+        first_normed,
+        projected_grad[:, cut:],
+        small_rows,
+        latent_normed,
+        keyval_grad,
+        grad_attn,
+        attended,
+        places,
+    )
+    arrived.append(other_core(mixed_grads(*mixed_parts, 8, 8)))
+    far = [
+        block_grads(first_normed, projected_grad, cut, places, 4, 4, arrived[0]),
+        mixed_grads(*mixed_parts, 4, 4, arrived[1]),
     ]
-    far = [
-        block_grads(first_normed, part, places, RINGS, RINGS, came)
-        for part, came in zip(parts, arrived)
+    from_y = [other_y(part) for part in far]
+    arrived_in = other_core(
+        expert_grads((every_gate_grad, every_up_grad), every_row, units, 1, None, bf16, (far[1],))
+    )
+    near = [
+        block_grads(first_normed, projected_grad, cut, places, 0, 4, arrived[0]),
+        mixed_grads(*mixed_parts, 0, 4, arrived[1]),
     ]
-    from_y = [other_y(far[0]), other_y(far[1])]
+    grad_expert_down = expert_grads(
+        (every_hidden,), every_grad, units, 0, arrived_down, f32, (near[1],)
+    )
+    first_closed = close_ring(near[0], from_y[0])
     grad_expert_in = expert_grads(
-        (every_gate_grad, every_up_grad), every_row, units, 0, arrived_in, f32, tuple(far)
-    )
-    near = [
-        block_grads(first_normed, part, places, 0, RINGS, came)
-        for part, came in zip(parts, arrived)
-    ]
-    first_closed = close_ring(after(near[0], grad_expert_in), from_y[0])
-    grad_expert_down = expert_grads(
-        (every_hidden,), every_grad, units, 0, arrived_down, f32, (from_y[0],)
-    )
-    second_closed = close_ring(near[1], from_y[1])
+        (every_gate_grad, every_up_grad), every_row, units, 0, arrived_in, f32
+    )
+    second_closed = close_ring(after(near[1], grad_expert_in), from_y[1])
     grad_expert_gate_up = grad_expert_in.swapaxes(2, 3)
     grad_expert_down = grad_expert_down[0]
-    grad_output_weight = scatter_product(grad_attn, attended, places, (arrived[1],)).T
-    grad_keyval_weight = scatter_blocks(
-        latent_blocks(latent_normed, keyval_grad, places, (arrived[1],)), bf16
-    )
-    grad_first_weight = jnp.concatenate([first_closed, second_closed], axis=1)
     nope_width = heads * NOPE
     span = heads * (ROPE // 2)
     grad_query_weight = jnp.concatenate(
         [
-            grad_first_weight[:, :nope_width].reshape(depth, heads, NOPE),
-            grad_first_weight[:, nope_width : nope_width + span].reshape(depth, heads, -1),
-            grad_first_weight[:, nope_width + span : query_width].reshape(depth, heads, -1),
+            first_closed[:, :nope_width].reshape(depth, heads, NOPE),
+            first_closed[:, nope_width : nope_width + span].reshape(depth, heads, -1),
+            first_closed[:, nope_width + span : query_width].reshape(depth, heads, -1),
         ],
         axis=2,
     ).reshape(depth, query_width)
-    grad_latent_part = grad_first_weight[:, query_width:used]
-    grad_latent_weight = grad_latent_part + other_x(grad_latent_part)
-    grad_first_part = dot_turned(projected_grad, first_weight)
-    low_rows, high_rows = grad_first_part[:local_rows], grad_first_part[local_rows:]
-    sent_rows = jnp.where(x == 0, high_rows, low_rows).astype(bf16)
-    grad_first = jnp.where(x == 0, low_rows, high_rows) + other_x(sent_rows).astype(f32)
+    at = first_width - cut
+    both = jnp.concatenate([first_closed[:, query_width:], second_closed[:, :at]], axis=1)
+    both = both + other_x(both)
+    grad_latent_weight = both[:, : KVR + ROPE]
+    small_grads = both[:, KVR + ROPE :].T
+    keyval_columns = w_keyval.shape[1] * latent_depth // depth
+    grad_keyval_weight = (
+        second_closed[:, at : at + keyval_columns]
+        .reshape(-1, latent_depth, keyval_columns)
+        .transpose(1, 0, 2)
+        .reshape(latent_depth, -1)
+    )
+    grad_output_weight = second_closed[:, at + keyval_columns :].T
     own_inputs = block_input.astype(f32)
     own_scale = rms_scale(own_inputs)
     own_unit = own_inputs * own_scale
-    gain_attn_part = jnp.sum(grad_first * own_unit, axis=0)
     grad_input = grad_mixed + rms_back(grad_first * attn_gain_wide, own_unit, own_scale)
-
-    small_grads = jnp.concatenate(
-        [
-            gain_attn_part.reshape(blocks, 1, depth),
-            gain_ffn_part.reshape(blocks, 1, depth),
-            grad_router.swapaxes(0, 1),
-            jnp.pad(
-                gain_latent_part.reshape(blocks, 1, latent_depth),
-                ((0, 0), (0, 0), (0, depth - latent_depth)),
-            ),
-        ],
-        axis=1,
-    )
-    small_grads = scatter_blocks(
-        pick_blocks(after(small_grads, far[1]), places), f32
-    )[0]
-    small_grads = small_grads + other_x(small_grads)
     return (
         block_output,
         grad_input,
         small_grads[0],
         grad_query_weight,
         grad_latent_weight,
-        small_grads[2 + experts, :latent_depth],
+        small_grads[2, :latent_depth],
         grad_keyval_weight,
         grad_output_weight,
         small_grads[1],
-        small_grads[2 : 2 + experts].T,
+        small_grads[3 : 3 + experts].T,
         grad_shared_in,
         grad_shared_down,
         grad_expert_gate_up,

time: 838 us -> 894 us (1.067)
  waiting for transfers between devices: 231 us -> 303 us
  local copies, waits for them, and re-layouts: 64.4 us -> 103 us
  starting transfers between devices: 119 us -> 88.9 us
  other arithmetic: 60.7 us -> 40.3 us
    ppermute x30 -> x19, waiting for transfers between devices: 101 us -> 156 us  [ring_step(): lax.ppermute(values, 'dp', [(i, (i + RINGS) % 16) for i in range(16)])]
    unnamed x229 -> x269, local copies, waits for them, and re-layouts: 43.6 us -> 72.7 us
    all_to_all x1, waiting for transfers between devices: 0.01 us -> 16.6 us  [gather_body(): lax.all_to_all(add_low(shared_kept, other_core(shared_sent)), 'dp', split...]
    ppermute x30 -> x19, starting transfers between devices: 36.5 us -> 22.7 us  [ring_step(): lax.ppermute(values, 'dp', [(i, (i + RINGS) % 16) for i in range(16)])]
    ppermute x32 -> x25, starting transfers between devices: 34.5 us -> 26 us  [other_x(): return lax.ppermute(values, 'tensor', [(0, 1), (1, 0)])]
    ppermute x31 -> x25, starting transfers between devices: 35 us -> 28.9 us  [other_y(): return lax.ppermute(values, 'dp', [(i, i ^ 2) for i in range(16)])]
    ppermute x32 -> x25, waiting for transfers between devices: 61.7 us -> 60.5 us  [other_x(): return lax.ppermute(values, 'tensor', [(0, 1), (1, 0)])]
    pallas_call x15 -> x11, Pallas kernels: 186 us -> 187 us  [the longest x4 146 us: mlp_plane(): pl.pallas_call(functools.partial(mlp_kernel, tiles, columns, joined, piec...]
  transfers between devices with their start and end apart: 114 -> 87, of which waited for: 35 -> 28; matrix products, arithmetic and copies ran while one was open for 11% -> 7% of each run, Pallas kernels for 41% -> 36%
where the time goes in v6:
time: 894 us; the launch traced here: 885 us
  Pallas kernels  348 us (39%)
  waiting for transfers between devices  303 us (34%)
  local copies, waits for them, and re-layouts  103 us (12%)
  starting transfers between devices  88.9 us (10%)
  other arithmetic  40.3 us (5%)
    ppermute x19, waiting for transfers between devices, ring_step(): lax.ppermute(values, 'dp', [(i, (i + RINGS) % 16) for i in range(16)])  156 us
    pallas_call x4, Pallas kernels, mlp_plane(): pl.pallas_call(functools.partial(mlp_kernel, tiles, columns, joined, piec...  146 us
    unnamed x269, local copies, waits for them, and re-layouts  72.7 us
    ppermute x25, waiting for transfers between devices, other_y(): return lax.ppermute(values, 'dp', [(i, i ^ 2) for i in range(16)])  69 us
    pallas_call x4, Pallas kernels, expert_grads(): pl.pallas_call(functools.partial(expert_grads_kernel, units, len(lefts),...  63.8 us
    ppermute x25, waiting for transfers between devices, other_x(): return lax.ppermute(values, 'tensor', [(0, 1), (1, 0)])  60.5 us
    ppermute x25, starting transfers between devices, other_y(): return lax.ppermute(values, 'dp', [(i, i ^ 2) for i in range(16)])  28.9 us
    pallas_call x2, Pallas kernels, down_grads(): pl.pallas_call(functools.partial(down_kernel, count), grid=(width // TILE...  27.6 us
  transfers between devices with their start and end apart: 87, of which 28 were waited for; matrix products, arithmetic and copies ran while one was open for 7% of the time, Pallas kernels for 36%

profile of v6, /device:TPU:0, one launch (start us, length us, event | category | flops | bytes accessed | tf_op | source)
XLA Modules:
  0.0 884.9 jit_solution(3161419070607140707)
XLA Ops:
  14.4 21.9 %collective-permute-done.4.refs_4_ = bf16[128,3712]{1,0:T(8,128)(2,1)} collective-permute-done((bf16[128,3712]{1,0:T(8,128)(2,1)}, bf16[128,3712]{1,0:T(8,128)(2,1)}, u32[]{:S(2)}, u32[]{:S(2)}) %collective-permute-start.4) | collective-permute-done | bytes 950304 | tf_op jit(solution)/shard_map/ppermute | solution.py:426
  41.6 19.1 %collective-permute-done.8.refs_8_ = bf16[128,3712]{1,0:T(8,128)(2,1)} collective-permute-done((bf16[128,3712]{1,0:T(8,128)(2,1)}, bf16[128,3712]{1,0:T(8,128)(2,1)}, u32[]{:S(2)}, u32[]{:S(2)}) %collective-permute-start.8) | collective-permute-done | bytes 950304 | tf_op jit(solution)/shard_map/ppermute | solution.py:426
  64.1 8.7 collective-permute-done.other_ref
  74.4 9.6 %collective-permute-done.12.refs_1_.refs_0_.refs_12_ = bf16[128,3712]{1,0:T(8,128)(2,1)S(1)} collective-permute-done((bf16[128,3712]{1,0:T(8,128)(2,1)}, bf16[128,3712]{1,0:T(8,128)(2,1)S(1)}, u32[]{:S(2)}, u32[]{:S(2)}) %collective-permute-start.12) | collective-permute-done | bytes 950304 | tf_op jit(solution)/shard_map/ppermute | solution.py:426
  99.2 27.5 %collective-permute-done.16.refs_4_ = bf16[128,2048]{1,0:T(8,128)(2,1)} collective-permute-done((bf16[128,2048]{1,0:T(8,128)(2,1)}, bf16[128,2048]{1,0:T(8,128)(2,1)}, u32[]{:S(2)}, u32[]{:S(2)}) %collective-permute-start.16) | collective-permute-done | bytes 524320 | tf_op jit(solution)/shard_map/ppermute | solution.py:426
  128.2 10.4 %collective-permute-done.14.refs_14_ = bf16[128,3712]{1,0:T(8,128)(2,1)} collective-permute-done((bf16[128,3712]{1,0:T(8,128)(2,1)}, bf16[128,3712]{1,0:T(8,128)(2,1)}, u32[]{:S(2)}, u32[]{:S(2)}) %collective-permute-start.14) | collective-permute-done | bytes 950304 | tf_op jit(solution)/shard_map/ppermute | solution.py:430
  160.8 22.6 %shard_map.287 = (f32[128,2048]{1,0:T(8,128)}, bf16[128,2048]{1,0:T(8,128)(2,1)}, bf16[2048,2176]{1,0:T(8,128)(2,1)}, bf16[512,2048]{1,0:T(8,128)(2,1)}, bf16[20...) custom-call(s32[5]{0:T(128)S(1)} %concatenate.27.place_ref, ...), custom_call_target="tpu_custom_call" | custom-call | flops 4429185024 | bytes 30408704 | tf_op jit(solution)/shard_map/pallas_call | solution.py:781
  209.8 12.1 %collective-permute-done.32.refs_4_ = bf16[128,2048]{1,0:T(8,128)(2,1)} collective-permute-done((bf16[128,2048]{1,0:T(8,128)(2,1)S(1)}, bf16[128,2048]{1,0:T(8,128)(2,1)}, u32[]{:S(2)}, u32[]{:S(2)}) %collective-permute-start.32) | collective-permute-done | bytes 524320 | tf_op jit(solution)/shard_map/ppermute | solution.py:426
  244.3 12.4 %shard_map.288 = (bf16[1792,2048]{1,0:T(8,128)(2,1)}, bf16[1792,2048]{1,0:T(8,128)(2,1)}, bf16[1792,2048]{1,0:T(8,128)(2,1)}) custom-call(bf16[1,2,704,2048]{3,2,1,0:T(8,128)(2,1)S(1)} %bitcast.76, bf16[1,2,704,2048]{3,2,1,0:T(8,128)(2,1)} %collective-permute-done.26.other_in, bf16[1,704,2048]{2,1,0:T(8,128)(2,1)S(1)} %copy-done.28, ...), custom_call_target="tpu_custom_call" | custom-call | bytes 44040192 | tf_op jit(solution)/shard_map/pallas_call | solution.py:1250
  261.5 14.4 %shard_map.289 = (bf16[2048,1792]{1,0:T(8,128)(2,1)}, bf16[2048,2048]{1,0:T(8,128)(2,1)}) custom-call(bf16[128,2048]{1,0:T(8,128)(2,1)S(1)} %copy-done.39, bf16[128,2048]{1,0:T(8,128)(2,1)} %collective-permute-done.18.refs_17_.refs_1_, bf16[128,2048]{1,0:T(8,128)(2,1)S(1)} %copy-done.53, bf16[128,2048]{1,0:T(8,128)(2,1)} %collective-permute-done.36.refs_3_, ...), custom_call_target="tpu_custom_call" | custom-call | flops 7516192768 | bytes 19398656 | tf_op jit(solution)/shard_map/pallas_call | solution.py:1363
  281.3 11.4 %collective-permute-done.42.refs_12_.refs_3_ = bf16[128,2048]{1,0:T(8,128)(2,1)S(1)} collective-permute-done((bf16[128,2048]{1,0:T(8,128)(2,1)}, bf16[128,2048]{1,0:T(8,128)(2,1)S(1)}, u32[]{:S(2)}, u32[]{:S(2)}) %collective-permute-start.42) | collective-permute-done | bytes 524320 | tf_op jit(solution)/shard_map/ppermute | solution.py:430
  295.0 13.2 %shard_map.290 = (bf16[2048,1792]{1,0:T(8,128)(2,1)}, bf16[2048,2048]{1,0:T(8,128)(2,1)}) custom-call(bf16[128,2048]{1,0:T(8,128)(2,1)S(1)} %collective-permute-done.17.refs_16_.refs_0_, bf16[128,2048]{1,0:T(8,128)(2,1)S(1)} %copy-done.45, bf16[128,2048]{1,0:T(8,128)(2,1)S(1)} %copy-done.47, ...), custom_call_target="tpu_custom_call", output_to_operand_aliasing={{0}: (9, {}), {1}: (10, {})} | custom-call | flops 7516192768 | bytes 19398656 | tf_op jit(solution)/shard_map/pallas_call | solution.py:1363
  309.1 36.2 %shard_map.291 = (bf16[128,4096]{1,0:T(8,128)(2,1)}, bf16[128,4096]{1,0:T(8,128)(2,1)}, bf16[128,4096]{1,0:T(8,128)(2,1)}, bf16[128,4096]{1,0:T(8,128)(2,1)}, bf...) custom-call(s32[4]{0:T(128)} %pad_add_fusion.experts_ref, ...), custom_call_target="tpu_custom_call" | custom-call | flops 18790481920 | bytes 52428800 | tf_op jit(solution)/shard_map/pallas_call | solution.py:1499
  347.0 36.4 %shard_map.292 = (bf16[128,4096]{1,0:T(8,128)(2,1)}, bf16[128,4096]{1,0:T(8,128)(2,1)}, bf16[128,4096]{1,0:T(8,128)(2,1)}, bf16[128,4096]{1,0:T(8,128)(2,1)}, bf...) custom-call(s32[4]{0:T(128)} %pad_add_fusion.experts_ref, ...), custom_call_target="tpu_custom_call", output_to_operand_aliasing={{4}: (13, {}), {5}: (14, {}), {6}: (15, {}), {7}: (16, {}),... | custom-call | flops 18790481920 | bytes 52428800 | tf_op jit(solution)/shard_map/pallas_call | solution.py:1499
  389.3 32.6 %collective-permute-done.50.refs_3_ = bf16[128,2048]{1,0:T(8,128)(2,1)S(1)} collective-permute-done((bf16[128,2048]{1,0:T(8,128)(2,1)}, bf16[128,2048]{1,0:T(8,128)(2,1)S(1)}, u32[]{:S(2)}, u32[]{:S(2)}) %collective-permute-start.50) | collective-permute-done | bytes 524320 | tf_op jit(solution)/shard_map/ppermute | solution.py:430
  422.9 36.7 %shard_map.293 = (bf16[128,4096]{1,0:T(8,128)(2,1)}, bf16[128,4096]{1,0:T(8,128)(2,1)}, bf16[128,4096]{1,0:T(8,128)(2,1)}, bf16[128,4096]{1,0:T(8,128)(2,1)}, bf...) custom-call(s32[4]{0:T(128)} %pad_add_fusion.experts_ref, ...), custom_call_target="tpu_custom_call", output_to_operand_aliasing={{4}: (13, {}), {5}: (14, {}), {6}: (15, {}), {7}: (16, {}),... | custom-call | flops 18790481920 | bytes 52428800 | tf_op jit(solution)/shard_map/pallas_call | solution.py:1499
  477.7 36.5 %shard_map.294 = (bf16[128,2048]{1,0:T(8,128)(2,1)}, bf16[128,2048]{1,0:T(8,128)(2,1)}, bf16[128,2048]{1,0:T(8,128)(2,1)}, bf16[128,2048]{1,0:T(8,128)(2,1)}, bf...) custom-call(s32[4]{0:T(128)} %pad_add_fusion.experts_ref, ...), custom_call_target="tpu_custom_call", output_to_operand_aliasing={{8}: (13, {}), {9}: (14, {}), {10}: (15, {}), {11}: (16, {}... | custom-call | flops 18790481920 | bytes 52428800 | tf_op jit(solution)/shard_map/pallas_call | solution.py:1499
  520.7 12.5 %shard_map.295 = (f32[16,288,128]{2,1,0:T(8,128)S(1)}, bf16[16,288,128]{2,1,0:T(8,128)(2,1)}, f32[128,2048]{1,0:T(8,128)S(1)}) custom-call(bf16[2048,2048]{1,0:T(8,128)(2,1)} %get-tuple-element.129.rows_ref.right_ref, bf16[2048,2048]{1,0:T(8,128)(2,1)} %get-tuple-element.130.cots_ref.right_ref, bf16[2048,1792]{1,0:T(8,128)(2,1)} %get-tuple-element.131.gate_ref.refs_0_, ...), custom_call_target="tpu_custom_call" | custom-call | flops 8589934592 | bytes 16777216 | tf_op jit(solution)/shard_map/pallas_call | solution.py:1325
  537.2 7.7 collective-permute-done.62.refs_1_
  554.5 19.3 %collective-permute-done.63 = bf16[128,2048]{1,0:T(8,128)(2,1)S(1)} collective-permute-done((bf16[128,2048]{1,0:T(8,128)(2,1)}, bf16[128,2048]{1,0:T(8,128)(2,1)S(1)}, u32[]{:S(2)}, u32[]{:S(2)}) %collective-permute-start.63) | collective-permute-done | bytes 524320 | tf_op jit(solution)/shard_map/ppermute | solution.py:438
  574.7 10.8 %shard_map.298.refs_1_ = bf16[1,1,704,2048]{3,2,1,0:T(8,128)(2,1)} custom-call(bf16[2048,2048]{1,0:T(8,128)(2,1)} %get-tuple-element.130.cots_ref.right_ref, bf16[2048,1792]{1,0:T(8,128)(2,1)} %get-tuple-element.133.hidden_ref.refs_0_), custom_call_target="tpu_custom_call" | custom-call | flops 6442450944 | bytes 23068672 | tf_op jit(solution)/shard_map/pallas_call | solution.py:1282
  590.5 9.1 %collective-permute-done.68 = bf16[128,2048]{1,0:T(8,128)(2,1)S(1)} collective-permute-done((bf16[128,2048]{1,0:T(8,128)(2,1)}, bf16[128,2048]{1,0:T(8,128)(2,1)S(1)}, u32[]{:S(2)}, u32[]{:S(2)}) %collective-permute-start.68) | collective-permute-done | bytes 524320 | tf_op jit(solution)/shard_map/ppermute | solution.py:426
  625.8 13.4 %shard_map.300 = (bf16[256,2176]{1,0:T(8,128)(2,1)}, bf16[256,2048]{1,0:T(8,128)(2,1)S(1)}, bf16[256,512]{1,0:T(8,128)(2,1)S(1)}, f32[1,512]{1,0:T(1,128)S(1)}) custom-call(s32[5]{0:T(128)S(1)} %concatenate.27.place_ref, s32[1,256]{1,0:T(1,128)S(1)} %copy-done.58, s32[256,1]{1,0:T(8,128)S(1)} %copy-done.50, f32[256,256]{1,0:T(8,128)S(1)} %copy.120.cosine_ref, ...), custom_call_target="tpu_custom_call" | custom-call | flops 3145728000 | bytes 6291456 | tf_op jit(solution)/shard_map/pallas_call | solution.py:923
  688.5 19.4 %shard_map.308 = bf16[1,2,704,2048]{3,2,1,0:T(8,128)(2,1)} custom-call(bf16[2048,2048]{1,0:T(8,128)(2,1)} %get-tuple-element.129.rows_ref.right_ref, bf16[2048,1792]{1,0:T(8,128)(2,1)} %get-tuple-element.131.gate_ref.refs_0_, bf16[2048,1792]{1,0:T(8,128)(2,1)} %get-tuple-element.132.up_ref.refs_1_, bf16[512,1920]{1,0:T(8,128)(2,1)} %shard_map.307.refs_2_), custom_call_target="tpu_custom_call" | custom-call | flops 12884901888 | bytes 34603008 | tf_op jit(solution)/shard_map/pallas_call | solution.py:1282
  724.2 16.6 %all-to-all-done.1.packed_ref = bf16[16,288,128]{2,1,0:T(8,128)(2,1)} async-done(((bf16[16,288,128]{2,1,0:T(8,128)(2,1)}), bf16[16,288,128]{2,1,0:T(8,128)(2,1)}, u32[]{:S(2)}, u32[]{:S(2)}) %all-to-all-start.1) | async-done | bytes 1179680 | tf_op jit(solution)/shard_map/all_to_all | solution.py:1763
  766.1 12.5 %shard_map.312 = f32[1,1,704,2048]{3,2,1,0:T(8,128)} custom-call(bf16[2048,2048]{1,0:T(8,128)(2,1)} %get-tuple-element.130.cots_ref.right_ref, bf16[2048,1792]{1,0:T(8,128)(2,1)} %get-tuple-element.133.hidden_ref.refs_0_, bf16[1,1,704,2048]{3,2,1,0:T(8,128)(2,1)} %collective-permute-done.84.refs_1_, bf16[512,1920]{1,0:T(8,128)(2,1)S(1)} %shard_map.306.refs_0_.refs_2_), custom_call_target="tpu_custom_call" | custom-call | flops 6442450944 | bytes 23068672 | tf_op jit(solution)/shard_map/pallas_call | solution.py:1282
  786.2 21.1 %shard_map.309.refs_1_ = f32[1,2,704,2048]{3,2,1,0:T(8,128)} custom-call(bf16[2048,2048]{1,0:T(8,128)(2,1)} %get-tuple-element.129.rows_ref.right_ref, bf16[2048,1792]{1,0:T(8,128)(2,1)} %get-tuple-element.131.gate_ref.refs_0_, bf16[2048,1792]{1,0:T(8,128)(2,1)} %get-tuple-element.132.up_ref.refs_1_, bf16[1,2,704,2048]{3,2,1,0:T(8,128)(2,1)} %collective-permute-done.77.refs_2_), custom_call_target="tpu_custom_call" | custom-call | flops 12884901888 | bytes 34603008 | tf_op jit(solution)/shard_map/pallas_call | solution.py:1282
  819.6 12.4 %collective-permute-done.79 = bf16[128,1920]{1,0:T(8,128)(2,1)S(1)} collective-permute-done((bf16[128,1920]{1,0:T(8,128)(2,1)S(1)}, bf16[128,1920]{1,0:T(8,128)(2,1)S(1)}, u32[]{:S(2)}, u32[]{:S(2)}) %collective-permute-start.79) | collective-permute-done | bytes 491552 | tf_op jit(solution)/shard_map/ppermute | solution.py:426
  833.5 8.4 collective-permute-done.74
  843.3 9.1 %collective-permute-done.80 = bf16[128,1920]{1,0:T(8,128)(2,1)S(1)} collective-permute-done((bf16[128,1920]{1,0:T(8,128)(2,1)S(1)}, bf16[128,1920]{1,0:T(8,128)(2,1)S(1)}, u32[]{:S(2)}, u32[]{:S(2)}) %collective-permute-start.80) | collective-permute-done | bytes 491552 | tf_op jit(solution)/shard_map/ppermute | solution.py:426
  854.5 7.7 collective-permute-done.75
  862.8 8.7 collective-permute-done.81
  (535 shorter events, 331.5 us)
Async XLA Ops:
  84.0 141.0 %collective-permute-start.26 = (bf16[1,2,704,2048]{3,2,1,0:T(8,128)(2,1)}, bf16[1,2,704,2048]{3,2,1,0:T(8,128)(2,1)}, u32[]{:S(2)}, u32[]{:S(2)}) collective-permute-start(bf16[1,2,704,2048]{3,2,1,0:T(8,128)(2,1)} %bitcast.75), channel_id=1, source_target_pairs={{0,2},{2,0},{4,6},{6,4},{8,10},{10,8},{12,14},{14,12},{16,18},{18,... | collective-permute-start | bytes 17301512 | tf_op jit(solution)/shard_map/ppermute | solution.py:434
  87.5 69.3 %all-to-all-start = ((bf16[16,288,128]{2,1,0:T(8,128)(2,1)}), bf16[16,288,128]{2,1,0:T(8,128)(2,1)S(1)}, u32[]{:S(2)}, u32[]{:S(2)}) async-start(bf16[16,288,128]{2,1,0:T(8,128)(2,1)} %shard_map.286), calls=%async_computation | async-start | bytes 2359296 | tf_op jit(solution)/shard_map/all_to_all | solution.py:1609
  92.1 34.6 %collective-permute-start.16 = (bf16[128,2048]{1,0:T(8,128)(2,1)}, bf16[128,2048]{1,0:T(8,128)(2,1)}, u32[]{:S(2)}, u32[]{:S(2)}) collective-permute-start(bf16[128,2048]{1,0:T(8,128)(2,1)} %shard_map.285.refs_0_), channel_id=1, source_target_pairs={{0,8},{2,10},{4,12},{6,14},{8,16},{10,18},{12,20},{14,22},{16,24},... | collective-permute-start | bytes 1572872 | tf_op jit(solution)/shard_map/ppermute | solution.py:426
  97.6 41.0 %collective-permute-start.14 = (bf16[128,3712]{1,0:T(8,128)(2,1)}, bf16[128,3712]{1,0:T(8,128)(2,1)}, u32[]{:S(2)}, u32[]{:S(2)}) collective-permute-start(bf16[128,3712]{1,0:T(8,128)(2,1)} %shard_map.284), channel_id=1, source_target_pairs={{0,4},{2,6},{4,0},{6,2},{8,12},{10,14},{12,8},{14,10},{16,20},{18,... | collective-permute-start | bytes 2850824 | tf_op jit(solution)/shard_map/ppermute | solution.py:430
  128.0 66.8 %collective-permute-start.27 = (bf16[1,704,2048]{2,1,0:T(8,128)(2,1)}, bf16[1,704,2048]{2,1,0:T(8,128)(2,1)}, u32[]{:S(2)}, u32[]{:S(2)}) collective-permute-start(bf16[1,704,2048]{2,1,0:T(8,128)(2,1)} %own_down.1), channel_id=1, source_target_pairs={{0,2},{2,0},{4,6},{6,4},{8,10},{10,8},{12,14},{14,12},{16,18},{18,... | collective-permute-start | bytes 8650760 | tf_op jit(solution)/shard_map/ppermute | solution.py:434
  155.2 50.4 %collective-permute-start.37 = (bf16[128,2048]{1,0:T(8,128)(2,1)}, bf16[128,2048]{1,0:T(8,128)(2,1)}, u32[]{:S(2)}, u32[]{:S(2)}) collective-permute-start(bf16[128,2048]{1,0:T(8,128)(2,1)} %collective-permute-done.16.refs_4_), channel_id=1, source_target_pairs={{0,4},{2,6},{4,0},{6,2},{8,12},{10,14},{12,8},{14,10},{16,20},{18,... | collective-permute-start | bytes 1572872 | tf_op jit(solution)/shard_map/ppermute | solution.py:430
  155.9 50.0 %collective-permute-start.36 = (bf16[128,2048]{1,0:T(8,128)(2,1)}, bf16[128,2048]{1,0:T(8,128)(2,1)}, u32[]{:S(2)}, u32[]{:S(2)}) collective-permute-start(bf16[128,2048]{1,0:T(8,128)(2,1)} %collective-permute-done.18.refs_17_.refs_1_), channel_id=1, source_target_pairs={{0,1},{1,0},{2,3},{3,2},{4,5},{5,4},{6,7},{7,6},{8,9},{9,8},{10,11... | collective-permute-start | bytes 1572872 | tf_op jit(solution)/shard_map/ppermute | solution.py:438
  221.8 34.9 %collective-permute-start.34 = (bf16[128,2048]{1,0:T(8,128)(2,1)}, bf16[128,2048]{1,0:T(8,128)(2,1)}, u32[]{:S(2)}, u32[]{:S(2)}) collective-permute-start(bf16[128,2048]{1,0:T(8,128)(2,1)} %collective-permute-done.32.refs_4_), channel_id=1, source_target_pairs={{0,1},{1,0},{2,3},{3,2},{4,5},{5,4},{6,7},{7,6},{8,9},{9,8},{10,11... | collective-permute-start | bytes 1572872 | tf_op jit(solution)/shard_map/ppermute | solution.py:438
  222.9 34.9 %collective-permute-start.33 = (bf16[128,2048]{1,0:T(8,128)(2,1)}, bf16[128,2048]{1,0:T(8,128)(2,1)}, u32[]{:S(2)}, u32[]{:S(2)}) collective-permute-start(bf16[128,2048]{1,0:T(8,128)(2,1)} %collective-permute-done.32.refs_4_), channel_id=1, source_target_pairs={{0,4},{2,6},{4,0},{6,2},{8,12},{10,14},{12,8},{14,10},{16,20},{18,... | collective-permute-start | bytes 1572872 | tf_op jit(solution)/shard_map/ppermute | solution.py:430
  276.0 70.1 %collective-permute-start.24 = (bf16[128,2048]{1,0:T(8,128)(2,1)}, bf16[128,2048]{1,0:T(8,128)(2,1)S(1)}, u32[]{:S(2)}, u32[]{:S(2)}) collective-permute-start(bf16[128,2048]{1,0:T(8,128)(2,1)} %collective-permute-done.22.refs_9_.refs_0_), channel_id=1, source_target_pairs={{0,1},{1,0},{2,3},{3,2},{4,5},{5,4},{6,7},{7,6},{8,9},{9,8},{10,11... | collective-permute-start | bytes 1572872 | tf_op jit(solution)/shard_map/ppermute | solution.py:438
  280.3 105.7 %collective-permute-start.49 = (bf16[128,2048]{1,0:T(8,128)(2,1)S(1)}, bf16[128,2048]{1,0:T(8,128)(2,1)}, u32[]{:S(2)}, u32[]{:S(2)}) collective-permute-start(bf16[128,2048]{1,0:T(8,128)(2,1)S(1)} %collective-permute-done.41.refs_11_.refs_0_), channel_id=1, source_target_pairs={{0,1},{1,0},{2,3},{3,2},{4,5},{5,4},{6,7},{7,6},{8,9},{9,8},{10,11... | collective-permute-start | bytes 1572872 | tf_op jit(solution)/shard_map/ppermute | solution.py:438
  292.7 95.2 %collective-permute-start.48 = (bf16[128,2048]{1,0:T(8,128)(2,1)S(1)}, bf16[128,2048]{1,0:T(8,128)(2,1)}, u32[]{:S(2)}, u32[]{:S(2)}) collective-permute-start(bf16[128,2048]{1,0:T(8,128)(2,1)S(1)} %collective-permute-done.41.refs_11_.refs_0_), channel_id=1, source_target_pairs={{0,4},{2,6},{4,0},{6,2},{8,12},{10,14},{12,8},{14,10},{16,20},{18,... | collective-permute-start | bytes 1572872 | tf_op jit(solution)/shard_map/ppermute | solution.py:430
  294.0 52.0 %collective-permute-start.25 = (bf16[128,2048]{1,0:T(8,128)(2,1)S(1)}, bf16[128,2048]{1,0:T(8,128)(2,1)S(1)}, u32[]{:S(2)}, u32[]{:S(2)}) collective-permute-start(bf16[128,2048]{1,0:T(8,128)(2,1)S(1)} %collective-permute-done.23.refs_1_), channel_id=1, source_target_pairs={{0,1},{1,0},{2,3},{3,2},{4,5},{5,4},{6,7},{7,6},{8,9},{9,8},{10,11... | collective-permute-start | bytes 1572872 | tf_op jit(solution)/shard_map/ppermute | solution.py:438
  345.3 41.6 %collective-permute-start.51 = (bf16[128,4096]{1,0:T(8,128)(2,1)}, bf16[128,4096]{1,0:T(8,128)(2,1)S(1)}, u32[]{:S(2)}, u32[]{:S(2)}) collective-permute-start(bf16[128,4096]{1,0:T(8,128)(2,1)} %get-tuple-element.114), channel_id=1, source_target_pairs={{0,4},{2,6},{4,0},{6,2},{8,12},{10,14},{12,8},{14,10},{16,20},{18,... | collective-permute-start | bytes 3145736 | tf_op jit(solution)/shard_map/ppermute | solution.py:430
  383.5 77.3 %collective-permute-start.44 = (bf16[128,4096]{1,0:T(8,128)(2,1)}, bf16[128,4096]{1,0:T(8,128)(2,1)S(1)}, u32[]{:S(2)}, u32[]{:S(2)}) collective-permute-start(bf16[128,4096]{1,0:T(8,128)(2,1)} %get-tuple-element.105), channel_id=1, source_target_pairs={{0,1},{1,0},{2,3},{3,2},{4,5},{5,4},{6,7},{7,6},{8,9},{9,8},{10,11... | collective-permute-start | bytes 3145736 | tf_op jit(solution)/shard_map/ppermute | solution.py:438
  384.6 86.5 %collective-permute-start.59 = (bf16[128,4096]{1,0:T(8,128)(2,1)S(1)}, bf16[128,4096]{1,0:T(8,128)(2,1)S(1)}, u32[]{:S(2)}, u32[]{:S(2)}) collective-permute-start(bf16[128,4096]{1,0:T(8,128)(2,1)S(1)} %copy-done.94), channel_id=1, source_target_pairs={{0,4},{2,6},{4,0},{6,2},{8,12},{10,14},{12,8},{14,10},{16,20},{18,... | collective-permute-start | bytes 3145736 | tf_op jit(solution)/shard_map/ppermute | solution.py:430
  385.9 129.4 %collective-permute-start.46 = (bf16[128,4096]{1,0:T(8,128)(2,1)}, bf16[128,4096]{1,0:T(8,128)(2,1)}, u32[]{:S(2)}, u32[]{:S(2)}) collective-permute-start(bf16[128,4096]{1,0:T(8,128)(2,1)} %get-tuple-element.106.refs_17_), channel_id=1, source_target_pairs={{0,1},{1,0},{2,3},{3,2},{4,5},{5,4},{6,7},{7,6},{8,9},{9,8},{10,11... | collective-permute-start | bytes 3145736 | tf_op jit(solution)/shard_map/ppermute | solution.py:438
  386.9 35.0 %collective-permute-start.50 = (bf16[128,2048]{1,0:T(8,128)(2,1)}, bf16[128,2048]{1,0:T(8,128)(2,1)S(1)}, u32[]{:S(2)}, u32[]{:S(2)}) collective-permute-start(bf16[128,2048]{1,0:T(8,128)(2,1)} %collective-permute-done.49.refs_2_), channel_id=1, source_target_pairs={{0,4},{2,6},{4,0},{6,2},{8,12},{10,14},{12,8},{14,10},{16,20},{18,... | collective-permute-start | bytes 1572872 | tf_op jit(solution)/shard_map/ppermute | solution.py:430
  387.9 71.8 %collective-permute-start.56 = (bf16[128,2048]{1,0:T(8,128)(2,1)S(1)}, bf16[128,2048]{1,0:T(8,128)(2,1)S(1)}, u32[]{:S(2)}, u32[]{:S(2)}) collective-permute-start(bf16[128,2048]{1,0:T(8,128)(2,1)S(1)} %copy-done.102), channel_id=1, source_target_pairs={{0,4},{2,6},{4,0},{6,2},{8,12},{10,14},{12,8},{14,10},{16,20},{18,... | collective-permute-start | bytes 1572872 | tf_op jit(solution)/shard_map/ppermute | solution.py:430
  421.9 54.7 %collective-permute-start.60 = (bf16[128,4096]{1,0:T(8,128)(2,1)S(1)}, bf16[128,4096]{1,0:T(8,128)(2,1)S(1)}, u32[]{:S(2)}, u32[]{:S(2)}) collective-permute-start(bf16[128,4096]{1,0:T(8,128)(2,1)S(1)} %add_convert_fusion.3.refs_17_), channel_id=1, source_target_pairs={{0,1},{1,0},{2,3},{3,2},{4,5},{5,4},{6,7},{7,6},{8,9},{9,8},{10,11... | collective-permute-start | bytes 3145736 | tf_op jit(solution)/shard_map/ppermute | solution.py:438
  469.7 45.6 %collective-permute-start.45 = (bf16[128,4096]{1,0:T(8,128)(2,1)S(1)}, bf16[128,4096]{1,0:T(8,128)(2,1)}, u32[]{:S(2)}, u32[]{:S(2)}) collective-permute-start(bf16[128,4096]{1,0:T(8,128)(2,1)S(1)} %add_convert_fusion.5.refs_16_), channel_id=1, source_target_pairs={{0,4},{2,6},{4,0},{6,2},{8,12},{10,14},{12,8},{14,10},{16,20},{18,... | collective-permute-start | bytes 3145736 | tf_op jit(solution)/shard_map/ppermute | solution.py:430
  471.1 47.4 %collective-permute-start.53 = (bf16[128,4096]{1,0:T(8,128)(2,1)}, bf16[128,4096]{1,0:T(8,128)(2,1)S(1)}, u32[]{:S(2)}, u32[]{:S(2)}) collective-permute-start(bf16[128,4096]{1,0:T(8,128)(2,1)} %get-tuple-element.118), channel_id=1, source_target_pairs={{0,4},{2,6},{4,0},{6,2},{8,12},{10,14},{12,8},{14,10},{16,20},{18,... | collective-permute-start | bytes 3145736 | tf_op jit(solution)/shard_map/ppermute | solution.py:430
  475.3 70.7 %collective-permute-start.52 = (bf16[128,4096]{1,0:T(8,128)(2,1)}, bf16[128,4096]{1,0:T(8,128)(2,1)}, u32[]{:S(2)}, u32[]{:S(2)}) collective-permute-start(bf16[128,4096]{1,0:T(8,128)(2,1)} %get-tuple-element.116), channel_id=1, source_target_pairs={{0,4},{2,6},{4,0},{6,2},{8,12},{10,14},{12,8},{14,10},{16,20},{18,... | collective-permute-start | bytes 3145736 | tf_op jit(solution)/shard_map/ppermute | solution.py:430
  536.2 49.3 %collective-permute-start.65 = (bf16[128,2048]{1,0:T(8,128)(2,1)}, bf16[128,2048]{1,0:T(8,128)(2,1)}, u32[]{:S(2)}, u32[]{:S(2)}) collective-permute-start(bf16[128,2048]{1,0:T(8,128)(2,1)} %get-tuple-element.136), channel_id=1, source_target_pairs={{0,1},{1,0},{2,3},{3,2},{4,5},{5,4},{6,7},{7,6},{8,9},{9,8},{10,11... | collective-permute-start | bytes 1572872 | tf_op jit(solution)/shard_map/ppermute | solution.py:438
  544.9 40.5 %collective-permute-start.67 = (bf16[128,2048]{1,0:T(8,128)(2,1)}, bf16[128,2048]{1,0:T(8,128)(2,1)}, u32[]{:S(2)}, u32[]{:S(2)}) collective-permute-start(bf16[128,2048]{1,0:T(8,128)(2,1)} %get-tuple-element.139), channel_id=1, source_target_pairs={{0,1},{1,0},{2,3},{3,2},{4,5},{5,4},{6,7},{7,6},{8,9},{9,8},{10,11... | collective-permute-start | bytes 1572872 | tf_op jit(solution)/shard_map/ppermute | solution.py:438
  671.4 36.9 %collective-permute-start.83 = (bf16[16,288,128]{2,1,0:T(8,128)(2,1)}, bf16[16,288,128]{2,1,0:T(8,128)(2,1)}, u32[]{:S(2)}, u32[]{:S(2)}) collective-permute-start(bf16[16,288,128]{2,1,0:T(8,128)(2,1)} %get-tuple-element.135.refs_1_), channel_id=1, source_target_pairs={{0,2},{2,0},{4,6},{6,4},{8,10},{10,8},{12,14},{14,12},{16,18},{18,... | collective-permute-start | bytes 3538952 | tf_op jit(solution)/shard_map/ppermute | solution.py:434
  679.5 37.6 %collective-permute-start.71 = (bf16[1024,1792]{1,0:T(8,128)(2,1)}, bf16[1024,1792]{1,0:T(8,128)(2,1)}, u32[]{:S(2)}, u32[]{:S(2)}) collective-permute-start(bf16[1024,1792]{1,0:T(8,128)(2,1)} %shard_map.302), channel_id=1, source_target_pairs={{0,2},{2,0},{4,6},{6,4},{8,10},{10,8},{12,14},{14,12},{16,18},{18,... | collective-permute-start | bytes 11010056 | tf_op jit(solution)/shard_map/ppermute | solution.py:434
  707.9 78.3 %collective-permute-start.77 = (bf16[1,2,704,2048]{3,2,1,0:T(8,128)(2,1)}, bf16[1,2,704,2048]{3,2,1,0:T(8,128)(2,1)}, u32[]{:S(2)}, u32[]{:S(2)}) collective-permute-start(bf16[1,2,704,2048]{3,2,1,0:T(8,128)(2,1)} %shard_map.308), channel_id=1, source_target_pairs={{0,2},{2,0},{4,6},{6,4},{8,10},{10,8},{12,14},{14,12},{16,18},{18,... | collective-permute-start | bytes 17301512 | tf_op jit(solution)/shard_map/ppermute | solution.py:434
  715.6 50.5 %collective-permute-start.84 = (bf16[1,1,704,2048]{3,2,1,0:T(8,128)(2,1)}, bf16[1,1,704,2048]{3,2,1,0:T(8,128)(2,1)}, u32[]{:S(2)}, u32[]{:S(2)}) collective-permute-start(bf16[1,1,704,2048]{3,2,1,0:T(8,128)(2,1)} %shard_map.298.refs_1_), channel_id=1, source_target_pairs={{0,2},{2,0},{4,6},{6,4},{8,10},{10,8},{12,14},{14,12},{16,18},{18,... | collective-permute-start | bytes 8650760 | tf_op jit(solution)/shard_map/ppermute | solution.py:434
  722.4 56.2 %collective-permute-start.72 = (bf16[512,1792]{1,0:T(8,128)(2,1)}, bf16[512,1792]{1,0:T(8,128)(2,1)}, u32[]{:S(2)}, u32[]{:S(2)}) collective-permute-start(bf16[512,1792]{1,0:T(8,128)(2,1)} %shard_map.304), channel_id=1, source_target_pairs={{0,4},{2,6},{4,0},{6,2},{8,12},{10,14},{12,8},{14,10},{16,20},{18,... | collective-permute-start | bytes 5505032 | tf_op jit(solution)/shard_map/ppermute | solution.py:430
  753.7 59.8 %collective-permute-start.78 = (bf16[512,1920]{1,0:T(8,128)(2,1)}, bf16[512,1920]{1,0:T(8,128)(2,1)}, u32[]{:S(2)}, u32[]{:S(2)}) collective-permute-start(bf16[512,1920]{1,0:T(8,128)(2,1)} %shard_map.307.refs_2_), channel_id=1, source_target_pairs={{0,4},{2,6},{4,0},{6,2},{8,12},{10,14},{12,8},{14,10},{16,20},{18,... | collective-permute-start | bytes 5898248 | tf_op jit(solution)/shard_map/ppermute | solution.py:430
  782.4 36.7 %collective-permute-start.73 = (bf16[128,1792]{1,0:T(8,128)(2,1)S(1)}, bf16[128,1792]{1,0:T(8,128)(2,1)S(1)}, u32[]{:S(2)}, u32[]{:S(2)}) collective-permute-start(bf16[128,1792]{1,0:T(8,128)(2,1)S(1)} %slice.216), channel_id=1, source_target_pairs={{0,8},{2,10},{4,12},{6,14},{8,16},{10,18},{12,20},{14,22},{16,24},... | collective-permute-start | bytes 1376264 | tf_op jit(solution)/shard_map/ppermute | solution.py:426
  (182 other events, 2702.6 us)

commit v7 on v6

--- a/solution.py
+++ b/solution.py
@@ -453,10 +453,12 @@
     )(values, *others)
 
 
-def gather_rows(rows, corners):
+def gather_rows(rows, corners, eager=False):
     planes = []
     current = rows
     for distance in range(RINGS):
+        if distance > 1 and eager:
+            current = after(current, *planes[distance - 2][1:3])
         if distance:
             current = ring_step(current)
         beside = other_y(current)
@@ -492,7 +494,9 @@
 def ring_sum(parts, low):
     moving = parts[1]
     for distance in (2, 3, 0):
-        moving = ring_step(moving.astype(low)).astype(jnp.float32) + parts[distance]
+        moving = ring_step(moving.astype(low)).astype(jnp.float32) + parts[distance].astype(
+            jnp.float32
+        )
     return moving
 
 
@@ -953,45 +957,25 @@
     )
 
 
-def block_grads_kernel(extra, places_ref, left_ref, right_ref, *refs):
+def first_grads_kernel(extra, places_ref, left_ref, right_ref, small_ref, *refs):
+    out_ref = refs[-1]
+    size = left_ref.shape[1]
+    edge = right_ref.shape[1] - small_ref.shape[0]
     result = dot_rows(left_ref[...], right_ref[...])
-    if extra:
-        result += refs[0][...].astype(jnp.float32)
-    refs[-1][...] = result.astype(jnp.bfloat16)
-
-
-def block_grads(left, right, width, places, first, count, arrived=None):
-    rows = right.shape[0]
-    size = left.shape[1] // places.shape[0]
-    extra = [] if arrived is None else [arrived]
-    return pl.pallas_call(
-        functools.partial(block_grads_kernel, len(extra)),
-        grid_spec=pltpu.PrefetchScalarGridSpec(
-            num_scalar_prefetch=1,
-            grid=(count,),
-            in_specs=[
-                pl.BlockSpec((rows, size), lambda i, where: (0, where[first + i])),
-                pl.BlockSpec((rows, width), lambda i, where: (0, 0)),
-            ]
-            + [pl.BlockSpec((size, width), lambda i, where: (first + i, 0))] * len(extra),
-            out_specs=pl.BlockSpec((size, width), lambda i, where: (i, 0)),
-        ),
-        out_shape=jax.ShapeDtypeStruct((count * size, width), jnp.bfloat16),
-        cost_estimate=pl.CostEstimate(
-            flops=2 * rows * count * size * width,
-            bytes_accessed=2 * (count * size * width + rows * width),
-            transcendentals=0,
-        ),
-    )(places, left, right, *extra)
-
-
-def mixed_grads_kernel(first, extra, places_ref, *refs):
-    normed_ref, right_ref, small_ref, latent_ref, keyval_ref, grad_ref, attended_ref = refs[:7]
+    for value, some in (
+        (result[:, :edge], slice(0, edge)),
+        (result[:, edge:] + jnp.transpose(small_ref[...]), slice(edge, right_ref.shape[1])),
+    ):
+        if extra:
+            value = value + refs[0][:, some].astype(jnp.float32)
+        out_ref[:, some] = value.astype(jnp.bfloat16)
+
+
+def other_grads_kernel(first, extra, places_ref, latent_ref, keyval_ref, grad_ref, attended_ref, *refs):
     out_ref, keyval_all = refs[-2:]
     step = pl.program_id(0)
-    size = normed_ref.shape[1]
-    blocks = places_ref.shape[0]
-    latent_size = latent_ref.shape[1] // blocks
+    size = grad_ref.shape[1]
+    latent_size = latent_ref.shape[1] // places_ref.shape[0]
     parts = size // latent_size
     columns = keyval_ref.shape[1] // parts
 
@@ -1001,64 +985,83 @@
             some = slice(k * columns, (k + 1) * columns)
             keyval_all[:, some] = dot_rows(latent_ref[...], keyval_ref[:, some])
 
-    low = jnp.bfloat16
-    at = right_ref.shape[1]
-    result = dot_rows(normed_ref[...], right_ref[...])
-    small = jnp.transpose(small_ref[...])
-    result = result + jnp.concatenate(
-        [jnp.zeros((size, at - small.shape[1]), jnp.float32), small], axis=1
-    )
     start = pl.multiple_of(places_ref[first + step] * latent_size, latent_size)
     strip = keyval_all[pl.ds(start, latent_size), :]
     keyval = jnp.concatenate([strip[:, k * columns : (k + 1) * columns] for k in range(parts)], axis=0)
     output = dot_rows(grad_ref[...], attended_ref[...])
-    for value, begin in ((result, 0), (keyval, at), (output, at + columns)):
-        end = begin + value.shape[1]
+    for value, some in (
+        (keyval, slice(0, columns)),
+        (output, slice(columns, columns + output.shape[1])),
+    ):
         if extra:
-            value = value + refs[7][:, begin:end].astype(jnp.float32)
-        out_ref[:, begin:end] = value.astype(low)
-
-
-def mixed_grads(normed, right, small, latent, keyval, grad, attended, places, first, count, arrived=None):
-    rows, width = right.shape
-    blocks = places.shape[0]
-    size = normed.shape[1] // blocks
-    parts = size // (latent.shape[1] // blocks)
-    total = width + keyval.shape[1] // parts + attended.shape[1]
+            value = value + refs[0][:, some].astype(jnp.float32)
+        out_ref[:, some] = value.astype(jnp.bfloat16)
+
+
+def still(array):
+    return pl.BlockSpec(array.shape, lambda i, where: (0, 0))
+
+
+def grads_call(kernel, specs, operands, scratch, size, width, places, first, count, arrived):
     extra = [] if arrived is None else [arrived]
-
-    def block(i, where):
-        return (0, where[first + i])
-
-    def still(array):
-        return pl.BlockSpec(array.shape, lambda i, where: (0, 0))
-
     return pl.pallas_call(
-        functools.partial(mixed_grads_kernel, first, len(extra)),
+        functools.partial(kernel, len(extra)),
         grid_spec=pltpu.PrefetchScalarGridSpec(
             num_scalar_prefetch=1,
             grid=(count,),
-            in_specs=[
-                pl.BlockSpec((rows, size), block),
-                still(right),
-                pl.BlockSpec((small.shape[0], size), block),
-                still(latent),
-                still(keyval),
-                pl.BlockSpec((rows, size), block),
-                still(attended),
-            ]
-            + [pl.BlockSpec((size, total), lambda i, where: (first + i, 0))] * len(extra),
-            out_specs=pl.BlockSpec((size, total), lambda i, where: (i, 0)),
-            scratch_shapes=[pltpu.VMEM((latent.shape[1], keyval.shape[1]), jnp.float32)],
+            in_specs=specs
+            + [pl.BlockSpec((size, width), lambda i, where: (first + i, 0))] * len(extra),
+            out_specs=pl.BlockSpec((size, width), lambda i, where: (i, 0)),
+            scratch_shapes=scratch,
         ),
-        out_shape=jax.ShapeDtypeStruct((count * size, total), jnp.bfloat16),
+        out_shape=jax.ShapeDtypeStruct((count * size, width), jnp.bfloat16),
         compiler_params=pltpu.CompilerParams(vmem_limit_bytes=32 * 1024 * 1024),
         cost_estimate=pl.CostEstimate(
-            flops=2 * rows * count * size * total,
-            bytes_accessed=2 * (count * size * total + rows * total),
+            flops=1024 * count * size * width,
+            bytes_accessed=4 * count * size * width,
             transcendentals=0,
         ),
-    )(places, normed, right, small, latent, keyval, grad, attended, *extra)
+    )(places, *operands, *extra)
+
+
+def first_grads(left, right, small, places, first, count, arrived=None):
+    rows, width = right.shape
+    size = left.shape[1] // places.shape[0]
+    specs = [
+        pl.BlockSpec((rows, size), lambda i, where: (0, where[first + i])),
+        still(right),
+        pl.BlockSpec((small.shape[0], size), lambda i, where: (0, where[first + i])),
+    ]
+    return grads_call(
+        first_grads_kernel, specs, (left, right, small), [], size, width, places, first, count, arrived
+    )
+
+
+def other_grads(latent, keyval, grad, attended, places, first, count, arrived=None):
+    rows = grad.shape[0]
+    blocks = places.shape[0]
+    size = grad.shape[1] // blocks
+    parts = size // (latent.shape[1] // blocks)
+    width = keyval.shape[1] // parts + attended.shape[1]
+    specs = [
+        still(latent),
+        still(keyval),
+        pl.BlockSpec((rows, size), lambda i, where: (0, where[first + i])),
+        still(attended),
+    ]
+    scratch = [pltpu.VMEM((latent.shape[1], keyval.shape[1]), jnp.float32)]
+    return grads_call(
+        functools.partial(other_grads_kernel, first),
+        specs,
+        (latent, keyval, grad, attended),
+        scratch,
+        size,
+        width,
+        places,
+        first,
+        count,
+        arrived,
+    )
 
 
 def first_back_kernel(place_ref, own_ref, other_ref, grad_ref, weight_ref, own_out, sent_out, gain_ref):
@@ -1205,18 +1208,18 @@
             in_ref[k] = jnp.transpose(units_ref[...])
 
 
-def unpack_shared(packed, shared):
+def unpack_shared(packed, shared, others):
     blocks, _, depth = packed.shape
     return pl.pallas_call(
-        functools.partial(unpack_shared_kernel, shared),
+        lambda packed_ref, *refs: unpack_shared_kernel(shared, packed_ref, *refs[len(others) :]),
         out_shape=[
             jax.ShapeDtypeStruct((2, depth, blocks * shared), jnp.float32),
             jax.ShapeDtypeStruct((blocks * shared, depth), jnp.float32),
         ],
-        in_specs=in_vmem(1),
+        in_specs=in_vmem(1) + in_place(len(others)),
         out_specs=in_vmem(2),
         scratch_shapes=[pltpu.VMEM((blocks * shared, depth), jnp.float32)],
-    )(packed)
+    )(packed, *others)
 
 
 def pack_units_kernel(units, shared, own_in, other_in, own_down, other_down, near, far, *refs):
@@ -1604,10 +1607,10 @@
     expert_in_other = other_core(expert_in)
     expert_down_other = other_core(expert_down)
     chunks = gather_weight(held)
-    grad_planes = gather_rows(after(cotangent, held[3]), "xyxy")
+    grad_planes = gather_rows(cotangent, "xxxx")
 
     shared_near = lax.all_to_all(
-        pack_shared(shared_gate_up, shared_down, blocks, (held[3],)),
+        pack_shared(shared_gate_up, shared_down, blocks, ()),
         "dp",
         split_axis=0,
         concat_axis=0,
@@ -1615,6 +1618,30 @@
     )
     shared_far = other_core(shared_near)
 
+    gate_weight, up_weight, down_weight = pack_units(
+        expert_in,
+        expert_in_other,
+        expert_down,
+        expert_down_other,
+        shared_near,
+        shared_far,
+        shared,
+        (),
+    )
+    half_kept = down_grads(
+        0,
+        [piece for plane in grad_planes[:2] for piece in plane],
+        down_weight,
+        (),
+        (),
+    )
+    down_grad, every_grad = down_grads(
+        1,
+        [piece for plane in grad_planes[2:] for piece in plane],
+        down_weight,
+        half_kept,
+        (),
+    )
     cosine, sine = rotary_tables(segments[0], ROPE)
     cosine = jnp.tile(cosine, (1, heads))
     sine = jnp.tile(sine, (1, heads))
@@ -1645,7 +1672,7 @@
         chunks,
         heads,
         sizes,
-        (grad_planes[2][0], grad_planes[0][1], grad_planes[0][2], grad_planes[1][2], shared_near),
+        (down_grad,),
     )
     attn_gain_wide, ffn_gain_wide = gains[0], gains[1]
     mixed = block_input.astype(f32) + own_part + other_x(sent_part).astype(f32)
@@ -1675,31 +1702,7 @@
     )
 
     corners = "yxyx"
-    row_planes = gather_rows(second_normed, corners)
-    gate_weight, up_weight, down_weight = pack_units(
-        expert_in,
-        expert_in_other,
-        expert_down,
-        expert_down_other,
-        shared_near,
-        shared_far,
-        shared,
-        (second_normed,),
-    )
-    half_kept = down_grads(
-        0,
-        [piece for plane in grad_planes[:2] for piece in plane],
-        down_weight,
-        (),
-        (row_planes[1][0], row_planes[0][1], row_planes[0][2]),
-    )
-    down_grad, every_grad = down_grads(
-        1,
-        [piece for plane in grad_planes[2:] for piece in plane],
-        down_weight,
-        half_kept,
-        (row_planes[2][0], row_planes[0][3]),
-    )
+    row_planes = gather_rows(second_normed, corners, True)
     expert_ids = jnp.concatenate(
         [chip_experts, jnp.array([experts, used + 3 - query_width - KVR], jnp.int32)]
     )
@@ -1737,16 +1740,17 @@
         shared,
         blocks,
     )
+    sent_in = expert_grads((every_gate_grad, every_up_grad), every_row, units, 1, None, bf16)
     sent_down = expert_grads((every_hidden,), every_grad, units, 1, None, bf16)
     moving = ring_step(wide_sum(*closed[1]).astype(bf16))
     moving = ring_step(wide_sum(moving, *closed[2]).astype(bf16))
     own, beside, across = turned[3]
+    own = after(own, sent_in)
     grad_close = close_plane((own, after(beside, shared_sent), across))
     grad_second = wide_sum(
-        ring_step(
-            after(wide_sum(moving[:, :D], *grad_close).astype(bf16), sent_down)
-        ),
-        *[part[:, :D] for part in closed[0]],
+        ring_step(wide_sum(moving[:, :D], *grad_close).astype(bf16)),
+        after(closed[0][0], sent_down)[:, :D],
+        *[part[:, :D] for part in closed[0][1:]],
     )
     outs = list(outs)
     outs[3] = after(outs[3], grad_close[1])
@@ -1756,18 +1760,12 @@
         *[part[:, D:] for part in closed[0]],
     )
 
+    arrived_in = other_core(sent_in)
     arrived_down = other_core(sent_down)
     router_at = used + 3 - query_width - KVR
     grad_router = logit_rows[router_at : router_at + experts]
-    grad_shared_in, grad_shared_down = unpack_shared(
-        lax.all_to_all(
-            add_low(shared_kept, other_core(shared_sent)),
-            "dp",
-            split_axis=0,
-            concat_axis=0,
-            tiled=True,
-        ),
-        shared,
+    shared_grads = lax.all_to_all(
+        add_low(shared_kept, other_core(shared_sent)), "dp", split_axis=0, concat_axis=0, tiled=True
     )
 
     gain_ffn_part = jnp.sum(grad_second * second_unit, axis=0)
@@ -1796,8 +1794,9 @@
         ],
         axis=0,
     )
-    cut = (query_width + KVR) // TILE * TILE - TILE
-    arrived = [other_core(block_grads(first_normed, projected_grad, cut, places, 8, 8))]
+    ring_places = places.reshape(2, 2, RINGS).swapaxes(1, 2).reshape(-1)
+    other_parts = (latent_normed, keyval_grad, grad_attn, attended, ring_places)
+    other_arrived = other_core(other_grads(*other_parts, 8, 8))
     own_first, sent_first, gain_attn_part = first_back(
         place, block_input, other_input, projected_grad, first_weight
     )
@@ -1816,37 +1815,24 @@
         ],
         axis=0,
     )
-    mixed_parts = (
-        first_normed,
-        projected_grad[:, cut:],
-        small_rows,
-        latent_normed,
-        keyval_grad,
-        grad_attn,
-        attended,
-        places,
-    )
-    arrived.append(other_core(mixed_grads(*mixed_parts, 8, 8)))
-    far = [
-        block_grads(first_normed, projected_grad, cut, places, 4, 4, arrived[0]),
-        mixed_grads(*mixed_parts, 4, 4, arrived[1]),
-    ]
-    from_y = [other_y(part) for part in far]
-    arrived_in = other_core(
-        expert_grads((every_gate_grad, every_up_grad), every_row, units, 1, None, bf16, (far[1],))
-    )
-    near = [
-        block_grads(first_normed, projected_grad, cut, places, 0, 4, arrived[0]),
-        mixed_grads(*mixed_parts, 0, 4, arrived[1]),
-    ]
+    first_parts = (first_normed, projected_grad, small_rows, places)
+    first_arrived = other_core(first_grads(*first_parts, 8, 8))
+    other_kept = other_grads(*other_parts, 0, 8, other_arrived)
+    far = first_grads(*first_parts, 4, 4, first_arrived)
+    from_y = other_y(far)
+    near = first_grads(*first_parts, 0, 4, first_arrived)
+    other_summed = ring_sum(
+        [other_kept[2 * r * depth : 2 * (r + 1) * depth] for r in range(RINGS)], bf16
+    )
+    other_closed = other_summed[:depth] + other_y(other_summed[depth:].astype(bf16)).astype(f32)
     grad_expert_down = expert_grads(
-        (every_hidden,), every_grad, units, 0, arrived_down, f32, (near[1],)
-    )
-    first_closed = close_ring(near[0], from_y[0])
+        (every_hidden,), every_grad, units, 0, arrived_down, f32, (near,)
+    )
+    first_closed = close_ring(near, from_y)
     grad_expert_in = expert_grads(
-        (every_gate_grad, every_up_grad), every_row, units, 0, arrived_in, f32
-    )
-    second_closed = close_ring(after(near[1], grad_expert_in), from_y[1])
+        (every_gate_grad, every_up_grad), every_row, units, 0, arrived_in, f32, (from_y,)
+    )
+    grad_shared_in, grad_shared_down = unpack_shared(shared_grads, shared, (from_y,))
     grad_expert_gate_up = grad_expert_in.swapaxes(2, 3)
     grad_expert_down = grad_expert_down[0]
     nope_width = heads * NOPE
@@ -1859,19 +1845,18 @@
         ],
         axis=2,
     ).reshape(depth, query_width)
-    at = first_width - cut
-    both = jnp.concatenate([first_closed[:, query_width:], second_closed[:, :at]], axis=1)
+    both = first_closed[:, query_width:]
     both = both + other_x(both)
     grad_latent_weight = both[:, : KVR + ROPE]
     small_grads = both[:, KVR + ROPE :].T
     keyval_columns = w_keyval.shape[1] * latent_depth // depth
     grad_keyval_weight = (
-        second_closed[:, at : at + keyval_columns]
+        other_closed[:, :keyval_columns]
         .reshape(-1, latent_depth, keyval_columns)
         .transpose(1, 0, 2)
         .reshape(latent_depth, -1)
     )
-    grad_output_weight = second_closed[:, at + keyval_columns :].T
+    grad_output_weight = other_closed[:, keyval_columns:].T
     own_inputs = block_input.astype(f32)
     own_scale = rms_scale(own_inputs)
     own_unit = own_inputs * own_scale

time: 894 us -> 845 us (0.945)
  local copies, waits for them, and re-layouts: 103 us -> 80.4 us
  waiting for transfers between devices: 303 us -> 288 us
  Pallas kernels: 348 us -> 336 us
    ppermute x25 -> x27, waiting for transfers between devices: 60.5 us -> 95.1 us  [other_x(): return lax.ppermute(values, 'tensor', [(0, 1), (1, 0)])]
    ppermute x19, waiting for transfers between devices: 156 us -> 127 us  [ring_step(): lax.ppermute(values, 'dp', [(i, (i + RINGS) % 16) for i in range(16)])]
    unnamed x269 -> x207, local copies, waits for them, and re-layouts: 72.7 us -> 56 us
    all_to_all x1, waiting for transfers between devices: 16.6 us -> 0.01 us  [gather_body(): lax.all_to_all(add_low(shared_kept, other_core(shared_sent)), 'dp', split...]
    pallas_call x7 -> x6, Pallas kernels: 37.9 us -> 25.4 us  [the longest x5 22.5 us: grads_call(): pl.pallas_call(functools.partial(kernel, len(extra)), grid_spec=pltpu.Pre...]
    ppermute x25 -> x23, waiting for transfers between devices: 69 us -> 61 us  [other_y(): return lax.ppermute(values, 'dp', [(i, i ^ 2) for i in range(16)])]
    ppermute x25 -> x27, starting transfers between devices: 26 us -> 31.4 us  [other_x(): return lax.ppermute(values, 'tensor', [(0, 1), (1, 0)])]
    ppermute x25 -> x23, starting transfers between devices: 28.9 us -> 26 us  [other_y(): return lax.ppermute(values, 'dp', [(i, i ^ 2) for i in range(16)])]
  transfers between devices with their start and end apart: 87 -> 87, of which waited for: 28 -> 35; matrix products, arithmetic and copies ran while one was open for 7% -> 7% of each run, Pallas kernels for 36% -> 34%
where the time goes in v7:
time: 845 us; the launch traced here: 837 us
  Pallas kernels  336 us (40%)
  waiting for transfers between devices  288 us (34%)
  starting transfers between devices  89.5 us (11%)
  local copies, waits for them, and re-layouts  80.4 us (10%)
  other arithmetic  40.8 us (5%)
    pallas_call x4, Pallas kernels, mlp_plane(): pl.pallas_call(functools.partial(mlp_kernel, tiles, columns, joined, piec...  146 us
    ppermute x19, waiting for transfers between devices, ring_step(): lax.ppermute(values, 'dp', [(i, (i + RINGS) % 16) for i in range(16)])  127 us
    ppermute x27, waiting for transfers between devices, other_x(): return lax.ppermute(values, 'tensor', [(0, 1), (1, 0)])  95.1 us
    pallas_call x4, Pallas kernels, expert_grads(): pl.pallas_call(functools.partial(expert_grads_kernel, units, len(lefts),...  64.9 us
    ppermute x23, waiting for transfers between devices, other_y(): return lax.ppermute(values, 'dp', [(i, i ^ 2) for i in range(16)])  61 us
    unnamed x207, local copies, waits for them, and re-layouts  56 us
    ppermute x27, starting transfers between devices, other_x(): return lax.ppermute(values, 'tensor', [(0, 1), (1, 0)])  31.4 us
    pallas_call x2, Pallas kernels, down_grads(): pl.pallas_call(functools.partial(down_kernel, count), grid=(width // TILE...  28.2 us
  transfers between devices with their start and end apart: 87, of which 35 were waited for; matrix products, arithmetic and copies ran while one was open for 7% of the time, Pallas kernels for 34%

profile of v7, /device:TPU:0, one launch (start us, length us, event | category | flops | bytes accessed | tf_op | source)
XLA Modules:
  0.0 837.2 jit_solution(12338402709558826724)
XLA Ops:
  21.9 10.4 %collective-permute-done.other_ref = bf16[128,2048]{1,0:T(8,128)(2,1)S(1)} collective-permute-done((bf16[128,2048]{1,0:T(8,128)(2,1)S(1)}, bf16[128,2048]{1,0:T(8,128)(2,1)S(1)}, u32[]{:S(2)}, u32[]{:S(2)}) %collective-permute-start) | collective-permute-done | bytes 524320 | tf_op jit(solution)/shard_map/ppermute | solution.py:438
  33.7 6.9 collective-permute-done.4.refs_4_
  66.8 8.9 %collective-permute-done.33.refs_7_ = bf16[128,2048]{1,0:T(8,128)(2,1)} collective-permute-done((bf16[128,2048]{1,0:T(8,128)(2,1)}, bf16[128,2048]{1,0:T(8,128)(2,1)}, u32[]{:S(2)}, u32[]{:S(2)}) %collective-permute-start.33) | collective-permute-done | bytes 524320 | tf_op jit(solution)/shard_map/ppermute | solution.py:438
  75.7 14.7 %collective-permute-done.21.refs_4_ = bf16[128,2048]{1,0:T(8,128)(2,1)S(1)} collective-permute-done((bf16[128,2048]{1,0:T(8,128)(2,1)}, bf16[128,2048]{1,0:T(8,128)(2,1)S(1)}, u32[]{:S(2)}, u32[]{:S(2)}) %collective-permute-start.21) | collective-permute-done | bytes 524320 | tf_op jit(solution)/shard_map/ppermute | solution.py:426
  92.0 18.3 %collective-permute-done.8.refs_8_ = bf16[128,3712]{1,0:T(8,128)(2,1)S(1)} collective-permute-done((bf16[128,3712]{1,0:T(8,128)(2,1)}, bf16[128,3712]{1,0:T(8,128)(2,1)S(1)}, u32[]{:S(2)}, u32[]{:S(2)}) %collective-permute-start.8) | collective-permute-done | bytes 950304 | tf_op jit(solution)/shard_map/ppermute | solution.py:426
  114.6 9.4 %collective-permute-done.19.refs_2_ = bf16[128,2048]{1,0:T(8,128)(2,1)} collective-permute-done((bf16[128,2048]{1,0:T(8,128)(2,1)}, bf16[128,2048]{1,0:T(8,128)(2,1)}, u32[]{:S(2)}, u32[]{:S(2)}) %collective-permute-start.19) | collective-permute-done | bytes 524320 | tf_op jit(solution)/shard_map/ppermute | solution.py:438
  128.4 7.2 collective-permute-done.10.refs_1_.refs_10_
  137.1 10.8 %collective-permute-done.12.refs_12_ = bf16[128,3712]{1,0:T(8,128)(2,1)} collective-permute-done((bf16[128,3712]{1,0:T(8,128)(2,1)}, bf16[128,3712]{1,0:T(8,128)(2,1)}, u32[]{:S(2)}, u32[]{:S(2)}) %collective-permute-start.12) | collective-permute-done | bytes 950304 | tf_op jit(solution)/shard_map/ppermute | solution.py:426
  166.9 12.4 %shard_map.286 = (bf16[1792,2048]{1,0:T(8,128)(2,1)}, bf16[1792,2048]{1,0:T(8,128)(2,1)}, bf16[1792,2048]{1,0:T(8,128)(2,1)}) custom-call(bf16[1,2,704,2048]{3,2,1,0:T(8,128)(2,1)S(1)} %bitcast.77, bf16[1,2,704,2048]{3,2,1,0:T(8,128)(2,1)} %collective-permute-done.25.other_in, bf16[1,704,2048]{2,1,0:T(8,128)(2,1)S(1)} %copy-done.16, ...), custom_call_target="tpu_custom_call" | custom-call | bytes 44040192 | tf_op jit(solution)/shard_map/pallas_call | solution.py:1253
  179.9 9.5 %collective-permute-done.24.refs_7_ = bf16[128,2048]{1,0:T(8,128)(2,1)} collective-permute-done((bf16[128,2048]{1,0:T(8,128)(2,1)}, bf16[128,2048]{1,0:T(8,128)(2,1)}, u32[]{:S(2)}, u32[]{:S(2)}) %collective-permute-start.24) | collective-permute-done | bytes 524320 | tf_op jit(solution)/shard_map/ppermute | solution.py:438
  189.9 14.5 %shard_map.287 = (bf16[2048,1792]{1,0:T(8,128)(2,1)}, bf16[2048,2048]{1,0:T(8,128)(2,1)}) custom-call(bf16[128,2048]{1,0:T(8,128)(2,1)S(1)} %copy-done.20, bf16[128,2048]{1,0:T(8,128)(2,1)S(1)} %copy-done.41, bf16[128,2048]{1,0:T(8,128)(2,1)S(1)} %copy-done.43, bf16[128,2048]{1,0:T(8,128)(2,1)} %collective-permute-done.30.refs_3_, ...), custom_call_target="tpu_custom_call" | custom-call | flops 7516192768 | bytes 19398656 | tf_op jit(solution)/shard_map/pallas_call | solution.py:1366
  204.5 13.7 %shard_map.288 = (bf16[2048,1792]{1,0:T(8,128)(2,1)}, bf16[2048,2048]{1,0:T(8,128)(2,1)}) custom-call(bf16[128,2048]{1,0:T(8,128)(2,1)} %collective-permute-done.17.refs_0_, bf16[128,2048]{1,0:T(8,128)(2,1)S(1)} %copy-done.47, bf16[128,2048]{1,0:T(8,128)(2,1)} %collective-permute-done.19.refs_2_, ...), custom_call_target="tpu_custom_call", output_to_operand_aliasing={{0}: (9, {}), {1}: (10, {})} | custom-call | flops 7516192768 | bytes 19398656 | tf_op jit(solution)/shard_map/pallas_call | solution.py:1366
  220.5 22.1 %shard_map.289 = (f32[128,2048]{1,0:T(8,128)}, bf16[128,2048]{1,0:T(8,128)(2,1)S(1)}, bf16[2048,2176]{1,0:T(8,128)(2,1)}, bf16[512,2048]{1,0:T(8,128)(2,1)}, bf1...) custom-call(s32[5]{0:T(128)S(1)} %concatenate.24.place_ref, ...), custom_call_target="tpu_custom_call" | custom-call | flops 4429185024 | bytes 30408704 | tf_op jit(solution)/shard_map/pallas_call | solution.py:785
  248.0 11.4 %collective-permute-done.34 = bf16[128,2048]{1,0:T(8,128)(2,1)S(1)} collective-permute-done((bf16[128,2048]{1,0:T(8,128)(2,1)S(1)}, bf16[128,2048]{1,0:T(8,128)(2,1)S(1)}, u32[]{:S(2)}, u32[]{:S(2)}) %collective-permute-start.34) | collective-permute-done | bytes 524320 | tf_op jit(solution)/shard_map/ppermute | solution.py:438
  285.8 9.8 %collective-permute-done.42.refs_0_ = bf16[128,2048]{1,0:T(8,128)(2,1)S(1)} collective-permute-done((bf16[128,2048]{1,0:T(8,128)(2,1)}, bf16[128,2048]{1,0:T(8,128)(2,1)S(1)}, u32[]{:S(2)}, u32[]{:S(2)}) %collective-permute-start.42) | collective-permute-done | bytes 524320 | tf_op jit(solution)/shard_map/ppermute | solution.py:426
  311.5 36.3 %shard_map.292 = (bf16[128,4096]{1,0:T(8,128)(2,1)}, bf16[128,4096]{1,0:T(8,128)(2,1)}, bf16[128,4096]{1,0:T(8,128)(2,1)}, bf16[128,4096]{1,0:T(8,128)(2,1)}, bf...) custom-call(s32[4]{0:T(128)} %pad_add_fusion.experts_ref, ...), custom_call_target="tpu_custom_call" | custom-call | flops 18790481920 | bytes 52428800 | tf_op jit(solution)/shard_map/pallas_call | solution.py:1502
  349.3 36.4 %shard_map.293 = (bf16[128,4096]{1,0:T(8,128)(2,1)}, bf16[128,4096]{1,0:T(8,128)(2,1)}, bf16[128,4096]{1,0:T(8,128)(2,1)}, bf16[128,4096]{1,0:T(8,128)(2,1)}, bf...) custom-call(s32[4]{0:T(128)} %pad_add_fusion.experts_ref, ...), custom_call_target="tpu_custom_call", output_to_operand_aliasing={{4}: (13, {}), {5}: (14, {}), {6}: (15, {}), {7}: (16, {}),... | custom-call | flops 18790481920 | bytes 52428800 | tf_op jit(solution)/shard_map/pallas_call | solution.py:1502
  392.8 32.1 %collective-permute-done.50.refs_3_ = bf16[128,2048]{1,0:T(8,128)(2,1)S(1)} collective-permute-done((bf16[128,2048]{1,0:T(8,128)(2,1)S(1)}, bf16[128,2048]{1,0:T(8,128)(2,1)S(1)}, u32[]{:S(2)}, u32[]{:S(2)}) %collective-permute-start.50) | collective-permute-done | bytes 524320 | tf_op jit(solution)/shard_map/ppermute | solution.py:430
  425.6 36.6 %shard_map.294 = (bf16[128,4096]{1,0:T(8,128)(2,1)}, bf16[128,4096]{1,0:T(8,128)(2,1)}, bf16[128,4096]{1,0:T(8,128)(2,1)}, bf16[128,4096]{1,0:T(8,128)(2,1)}, bf...) custom-call(s32[4]{0:T(128)} %pad_add_fusion.experts_ref, ...), custom_call_target="tpu_custom_call", output_to_operand_aliasing={{4}: (13, {}), {5}: (14, {}), {6}: (15, {}), {7}: (16, {}),... | custom-call | flops 18790481920 | bytes 52428800 | tf_op jit(solution)/shard_map/pallas_call | solution.py:1502
  479.7 36.6 %shard_map.295 = (bf16[128,2048]{1,0:T(8,128)(2,1)}, bf16[128,2048]{1,0:T(8,128)(2,1)}, bf16[128,2048]{1,0:T(8,128)(2,1)}, bf16[128,2048]{1,0:T(8,128)(2,1)}, bf...) custom-call(s32[4]{0:T(128)} %pad_add_fusion.experts_ref, ...), custom_call_target="tpu_custom_call", output_to_operand_aliasing={{8}: (13, {}), {9}: (14, {}), {10}: (15, {}), {11}: (16, {}... | custom-call | flops 18790481920 | bytes 52428800 | tf_op jit(solution)/shard_map/pallas_call | solution.py:1502
  522.6 11.9 %shard_map.296 = (f32[16,288,128]{2,1,0:T(8,128)S(1)}, bf16[16,288,128]{2,1,0:T(8,128)(2,1)S(1)}, f32[128,2048]{1,0:T(8,128)S(1)}) custom-call(bf16[2048,2048]{1,0:T(8,128)(2,1)} %get-tuple-element.129.rows_ref.right_ref, bf16[2048,2048]{1,0:T(8,128)(2,1)} %get-tuple-element.130.cots_ref.right_ref, bf16[2048,1792]{1,0:T(8,128)(2,1)} %get-tuple-element.131.gate_ref.refs_0_, ...), custom_call_target="tpu_custom_call" | custom-call | flops 8589934592 | bytes 16777216 | tf_op jit(solution)/shard_map/pallas_call | solution.py:1328
  541.6 6.8 collective-permute-done.62.refs_1_
  554.4 19.9 %collective-permute-done.63 = bf16[128,2048]{1,0:T(8,128)(2,1)S(1)} collective-permute-done((bf16[128,2048]{1,0:T(8,128)(2,1)}, bf16[128,2048]{1,0:T(8,128)(2,1)S(1)}, u32[]{:S(2)}, u32[]{:S(2)}) %collective-permute-start.63) | collective-permute-done | bytes 524320 | tf_op jit(solution)/shard_map/ppermute | solution.py:438
  575.7 19.3 %shard_map.299.refs_1_ = bf16[1,2,704,2048]{3,2,1,0:T(8,128)(2,1)} custom-call(bf16[2048,2048]{1,0:T(8,128)(2,1)} %get-tuple-element.129.rows_ref.right_ref, bf16[2048,1792]{1,0:T(8,128)(2,1)} %get-tuple-element.131.gate_ref.refs_0_, bf16[2048,1792]{1,0:T(8,128)(2,1)} %get-tuple-element.132.up_ref.refs_1_), custom_call_target="tpu_custom_call" | custom-call | flops 12884901888 | bytes 34603008 | tf_op jit(solution)/shard_map/pallas_call | solution.py:1285
  598.5 11.2 %shard_map.301.refs_1_ = bf16[1,1,704,2048]{3,2,1,0:T(8,128)(2,1)} custom-call(bf16[2048,2048]{1,0:T(8,128)(2,1)} %get-tuple-element.130.cots_ref.right_ref, bf16[2048,1792]{1,0:T(8,128)(2,1)} %get-tuple-element.133.hidden_ref.refs_0_), custom_call_target="tpu_custom_call" | custom-call | flops 6442450944 | bytes 23068672 | tf_op jit(solution)/shard_map/pallas_call | solution.py:1285
  636.1 13.1 %shard_map.303 = (bf16[256,2176]{1,0:T(8,128)(2,1)}, bf16[256,2048]{1,0:T(8,128)(2,1)S(1)}, bf16[256,512]{1,0:T(8,128)(2,1)S(1)}, f32[1,512]{1,0:T(1,128)S(1)}) custom-call(s32[5]{0:T(128)S(1)} %concatenate.24.place_ref, s32[1,256]{1,0:T(1,128)S(1)} %copy-done.31, s32[256,1]{1,0:T(8,128)S(1)} %copy-done.29, f32[256,256]{1,0:T(8,128)S(1)} %copy-done.25, ...), custom_call_target="tpu_custom_call" | custom-call | flops 3145728000 | bytes 6291456 | tf_op jit(solution)/shard_map/pallas_call | solution.py:927
  657.0 7.1 shard_map.304
  725.5 26.3 %collective-permute-done.79 = bf16[256,1536]{1,0:T(8,128)(2,1)S(1)} collective-permute-done((bf16[256,1536]{1,0:T(8,128)(2,1)S(1)}, bf16[256,1536]{1,0:T(8,128)(2,1)S(1)}, u32[]{:S(2)}, u32[]{:S(2)}) %collective-permute-start.79) | collective-permute-done | bytes 786464 | tf_op jit(solution)/shard_map/ppermute | solution.py:426
  754.3 7.6 collective-permute-done.72.refs_0_.refs_3_
  764.1 13.2 %shard_map.312 = f32[1,1,704,2048]{3,2,1,0:T(8,128)} custom-call(bf16[2048,2048]{1,0:T(8,128)(2,1)} %get-tuple-element.130.cots_ref.right_ref, bf16[2048,1792]{1,0:T(8,128)(2,1)} %get-tuple-element.133.hidden_ref.refs_0_, bf16[1,1,704,2048]{3,2,1,0:T(8,128)(2,1)} %collective-permute-done.84.refs_1_, bf16[512,2176]{1,0:T(8,128)(2,1)S(1)} %shard_map.306.refs_2_), custom_call_target="tpu_custom_call" | custom-call | flops 6442450944 | bytes 23068672 | tf_op jit(solution)/shard_map/pallas_call | solution.py:1285
  789.0 10.6 %collective-permute-done.74 = bf16[128,2176]{1,0:T(8,128)(2,1)S(1)} collective-permute-done((bf16[128,2176]{1,0:T(8,128)(2,1)S(1)}, bf16[128,2176]{1,0:T(8,128)(2,1)S(1)}, u32[]{:S(2)}, u32[]{:S(2)}) %collective-permute-start.74) | collective-permute-done | bytes 557088 | tf_op jit(solution)/shard_map/ppermute | solution.py:426
  801.0 21.2 %shard_map.311 = f32[1,2,704,2048]{3,2,1,0:T(8,128)} custom-call(bf16[2048,2048]{1,0:T(8,128)(2,1)} %get-tuple-element.129.rows_ref.right_ref, bf16[2048,1792]{1,0:T(8,128)(2,1)} %get-tuple-element.131.gate_ref.refs_0_, bf16[2048,1792]{1,0:T(8,128)(2,1)} %get-tuple-element.132.up_ref.refs_1_, bf16[1,2,704,2048]{3,2,1,0:T(8,128)(2,1)} %collective-permute-done.83.refs_2_, ...), custom_call_target="tpu_custom_call" | custom-call | flops 12884901888 | bytes 34603008 | tf_op jit(solution)/shard_map/pallas_call | solution.py:1285
  (475 shorter events, 308.5 us)
Async XLA Ops:
  0.7 153.9 %collective-permute-start.25 = (bf16[1,2,704,2048]{3,2,1,0:T(8,128)(2,1)}, bf16[1,2,704,2048]{3,2,1,0:T(8,128)(2,1)}, u32[]{:S(2)}, u32[]{:S(2)}) collective-permute-start(bf16[1,2,704,2048]{3,2,1,0:T(8,128)(2,1)} %bitcast.76), channel_id=1, source_target_pairs={{0,2},{2,0},{4,6},{6,4},{8,10},{10,8},{12,14},{14,12},{16,18},{18,... | collective-permute-start | bytes 17301512 | tf_op jit(solution)/shard_map/ppermute | solution.py:434
  49.3 79.0 %all-to-all-start = ((bf16[16,288,128]{2,1,0:T(8,128)(2,1)}), bf16[16,288,128]{2,1,0:T(8,128)(2,1)S(1)}, u32[]{:S(2)}, u32[]{:S(2)}) async-start(bf16[16,288,128]{2,1,0:T(8,128)(2,1)} %shard_map.285), calls=%async_computation | async-start | bytes 2359296 | tf_op jit(solution)/shard_map/all_to_all | solution.py:1612
  58.6 33.4 %collective-permute-start.6 = (bf16[128,3712]{1,0:T(8,128)(2,1)}, bf16[128,3712]{1,0:T(8,128)(2,1)}, u32[]{:S(2)}, u32[]{:S(2)}) collective-permute-start(bf16[128,3712]{1,0:T(8,128)(2,1)} %shard_map.282), channel_id=1, source_target_pairs={{0,4},{2,6},{4,0},{6,2},{8,12},{10,14},{12,8},{14,10},{16,20},{18,... | collective-permute-start | bytes 2850824 | tf_op jit(solution)/shard_map/ppermute | solution.py:430
  66.8 85.7 %collective-permute-start.26 = (bf16[1,704,2048]{2,1,0:T(8,128)(2,1)}, bf16[1,704,2048]{2,1,0:T(8,128)(2,1)}, u32[]{:S(2)}, u32[]{:S(2)}) collective-permute-start(bf16[1,704,2048]{2,1,0:T(8,128)(2,1)} %own_down.1), channel_id=1, source_target_pairs={{0,2},{2,0},{4,6},{6,4},{8,10},{10,8},{12,14},{14,12},{16,18},{18,... | collective-permute-start | bytes 8650760 | tf_op jit(solution)/shard_map/ppermute | solution.py:434
  75.7 34.6 %collective-permute-start.8 = (bf16[128,3712]{1,0:T(8,128)(2,1)}, bf16[128,3712]{1,0:T(8,128)(2,1)S(1)}, u32[]{:S(2)}, u32[]{:S(2)}) collective-permute-start(bf16[128,3712]{1,0:T(8,128)(2,1)} %copy-done.63), channel_id=1, source_target_pairs={{0,8},{2,10},{4,12},{6,14},{8,16},{10,18},{12,20},{14,22},{16,24},... | collective-permute-start | bytes 2850824 | tf_op jit(solution)/shard_map/ppermute | solution.py:426
  92.0 36.4 %collective-permute-start.5 = (bf16[128,3712]{1,0:T(8,128)(2,1)}, bf16[128,3712]{1,0:T(8,128)(2,1)}, u32[]{:S(2)}, u32[]{:S(2)}) collective-permute-start(bf16[128,3712]{1,0:T(8,128)(2,1)} %copy-done.63), channel_id=1, source_target_pairs={{0,2},{2,0},{4,6},{6,4},{8,10},{10,8},{12,14},{14,12},{16,18},{18,... | collective-permute-start | bytes 2850824 | tf_op jit(solution)/shard_map/ppermute | solution.py:434
  150.1 39.2 %collective-permute-start.14 = (bf16[128,3712]{1,0:T(8,128)(2,1)}, bf16[128,3712]{1,0:T(8,128)(2,1)}, u32[]{:S(2)}, u32[]{:S(2)}) collective-permute-start(bf16[128,3712]{1,0:T(8,128)(2,1)} %shard_map.284), channel_id=1, source_target_pairs={{0,4},{2,6},{4,0},{6,2},{8,12},{10,14},{12,8},{14,10},{16,20},{18,... | collective-permute-start | bytes 2850824 | tf_op jit(solution)/shard_map/ppermute | solution.py:430
  154.5 34.8 %collective-permute-start.24 = (bf16[128,2048]{1,0:T(8,128)(2,1)}, bf16[128,2048]{1,0:T(8,128)(2,1)}, u32[]{:S(2)}, u32[]{:S(2)}) collective-permute-start(bf16[128,2048]{1,0:T(8,128)(2,1)} %collective-permute-done.22.refs_5_), channel_id=1, source_target_pairs={{0,1},{1,0},{2,3},{3,2},{4,5},{5,4},{6,7},{7,6},{8,9},{9,8},{10,11... | collective-permute-start | bytes 1572872 | tf_op jit(solution)/shard_map/ppermute | solution.py:438
  179.3 39.0 %collective-permute-start.7 = (bf16[128,3712]{1,0:T(8,128)(2,1)}, bf16[128,3712]{1,0:T(8,128)(2,1)S(1)}, u32[]{:S(2)}, u32[]{:S(2)}) collective-permute-start(bf16[128,3712]{1,0:T(8,128)(2,1)} %collective-permute-done.6.refs_1_.refs_6_), channel_id=1, source_target_pairs={{0,2},{2,0},{4,6},{6,4},{8,10},{10,8},{12,14},{14,12},{16,18},{18,... | collective-permute-start | bytes 2850824 | tf_op jit(solution)/shard_map/ppermute | solution.py:434
  179.3 39.0 %collective-permute-start.9 = (bf16[128,3712]{1,0:T(8,128)(2,1)S(1)}, bf16[128,3712]{1,0:T(8,128)(2,1)S(1)}, u32[]{:S(2)}, u32[]{:S(2)}) collective-permute-start(bf16[128,3712]{1,0:T(8,128)(2,1)S(1)} %copy-done.65), channel_id=1, source_target_pairs={{0,2},{2,0},{4,6},{6,4},{8,10},{10,8},{12,14},{14,12},{16,18},{18,... | collective-permute-start | bytes 2850824 | tf_op jit(solution)/shard_map/ppermute | solution.py:434
  179.8 38.5 %collective-permute-start.11 = (bf16[128,3712]{1,0:T(8,128)(2,1)}, bf16[128,3712]{1,0:T(8,128)(2,1)S(1)}, u32[]{:S(2)}, u32[]{:S(2)}) collective-permute-start(bf16[128,3712]{1,0:T(8,128)(2,1)} %collective-permute-done.10.refs_1_.refs_10_), channel_id=1, source_target_pairs={{0,2},{2,0},{4,6},{6,4},{8,10},{10,8},{12,14},{14,12},{16,18},{18,... | collective-permute-start | bytes 2850824 | tf_op jit(solution)/shard_map/ppermute | solution.py:434
  303.3 45.1 %collective-permute-start.38 = (bf16[128,2048]{1,0:T(8,128)(2,1)}, bf16[128,2048]{1,0:T(8,128)(2,1)S(1)}, u32[]{:S(2)}, u32[]{:S(2)}) collective-permute-start(bf16[128,2048]{1,0:T(8,128)(2,1)} %copy-done.68), channel_id=1, source_target_pairs={{0,1},{1,0},{2,3},{3,2},{4,5},{5,4},{6,7},{7,6},{8,9},{9,8},{10,11... | collective-permute-start | bytes 1572872 | tf_op jit(solution)/shard_map/ppermute | solution.py:438
  305.1 83.8 %collective-permute-start.49 = (bf16[128,2048]{1,0:T(8,128)(2,1)S(1)}, bf16[128,2048]{1,0:T(8,128)(2,1)S(1)}, u32[]{:S(2)}, u32[]{:S(2)}) collective-permute-start(bf16[128,2048]{1,0:T(8,128)(2,1)S(1)} %collective-permute-done.42.refs_0_), channel_id=1, source_target_pairs={{0,1},{1,0},{2,3},{3,2},{4,5},{5,4},{6,7},{7,6},{8,9},{9,8},{10,11... | collective-permute-start | bytes 1572872 | tf_op jit(solution)/shard_map/ppermute | solution.py:438
  305.4 86.3 %collective-permute-start.48 = (bf16[128,2048]{1,0:T(8,128)(2,1)S(1)}, bf16[128,2048]{1,0:T(8,128)(2,1)}, u32[]{:S(2)}, u32[]{:S(2)}) collective-permute-start(bf16[128,2048]{1,0:T(8,128)(2,1)S(1)} %collective-permute-done.42.refs_0_), channel_id=1, source_target_pairs={{0,4},{2,6},{4,0},{6,2},{8,12},{10,14},{12,8},{14,10},{16,20},{18,... | collective-permute-start | bytes 1572872 | tf_op jit(solution)/shard_map/ppermute | solution.py:430
  347.8 41.4 %collective-permute-start.51 = (bf16[128,4096]{1,0:T(8,128)(2,1)}, bf16[128,4096]{1,0:T(8,128)(2,1)S(1)}, u32[]{:S(2)}, u32[]{:S(2)}) collective-permute-start(bf16[128,4096]{1,0:T(8,128)(2,1)} %get-tuple-element.114), channel_id=1, source_target_pairs={{0,4},{2,6},{4,0},{6,2},{8,12},{10,14},{12,8},{14,10},{16,20},{18,... | collective-permute-start | bytes 3145736 | tf_op jit(solution)/shard_map/ppermute | solution.py:430
  385.7 77.9 %collective-permute-start.44 = (bf16[128,4096]{1,0:T(8,128)(2,1)}, bf16[128,4096]{1,0:T(8,128)(2,1)S(1)}, u32[]{:S(2)}, u32[]{:S(2)}) collective-permute-start(bf16[128,4096]{1,0:T(8,128)(2,1)} %get-tuple-element.105), channel_id=1, source_target_pairs={{0,1},{1,0},{2,3},{3,2},{4,5},{5,4},{6,7},{7,6},{8,9},{9,8},{10,11... | collective-permute-start | bytes 3145736 | tf_op jit(solution)/shard_map/ppermute | solution.py:438
  387.4 85.6 %collective-permute-start.59 = (bf16[128,4096]{1,0:T(8,128)(2,1)}, bf16[128,4096]{1,0:T(8,128)(2,1)S(1)}, u32[]{:S(2)}, u32[]{:S(2)}) collective-permute-start(bf16[128,4096]{1,0:T(8,128)(2,1)} %get-tuple-element.112.refs_16_), channel_id=1, source_target_pairs={{0,4},{2,6},{4,0},{6,2},{8,12},{10,14},{12,8},{14,10},{16,20},{18,... | collective-permute-start | bytes 3145736 | tf_op jit(solution)/shard_map/ppermute | solution.py:430
  388.9 128.7 %collective-permute-start.46 = (bf16[128,4096]{1,0:T(8,128)(2,1)}, bf16[128,4096]{1,0:T(8,128)(2,1)}, u32[]{:S(2)}, u32[]{:S(2)}) collective-permute-start(bf16[128,4096]{1,0:T(8,128)(2,1)} %get-tuple-element.106.refs_17_), channel_id=1, source_target_pairs={{0,1},{1,0},{2,3},{3,2},{4,5},{5,4},{6,7},{7,6},{8,9},{9,8},{10,11... | collective-permute-start | bytes 3145736 | tf_op jit(solution)/shard_map/ppermute | solution.py:438
  389.2 35.7 %collective-permute-start.50 = (bf16[128,2048]{1,0:T(8,128)(2,1)S(1)}, bf16[128,2048]{1,0:T(8,128)(2,1)S(1)}, u32[]{:S(2)}, u32[]{:S(2)}) collective-permute-start(bf16[128,2048]{1,0:T(8,128)(2,1)S(1)} %collective-permute-done.49.refs_2_), channel_id=1, source_target_pairs={{0,4},{2,6},{4,0},{6,2},{8,12},{10,14},{12,8},{14,10},{16,20},{18,... | collective-permute-start | bytes 1572872 | tf_op jit(solution)/shard_map/ppermute | solution.py:430
  391.7 70.5 %collective-permute-start.56 = (bf16[128,2048]{1,0:T(8,128)(2,1)S(1)}, bf16[128,2048]{1,0:T(8,128)(2,1)}, u32[]{:S(2)}, u32[]{:S(2)}) collective-permute-start(bf16[128,2048]{1,0:T(8,128)(2,1)S(1)} %copy-done.83), channel_id=1, source_target_pairs={{0,4},{2,6},{4,0},{6,2},{8,12},{10,14},{12,8},{14,10},{16,20},{18,... | collective-permute-start | bytes 1572872 | tf_op jit(solution)/shard_map/ppermute | solution.py:430
  424.8 53.8 %collective-permute-start.60 = (bf16[128,4096]{1,0:T(8,128)(2,1)S(1)}, bf16[128,4096]{1,0:T(8,128)(2,1)S(1)}, u32[]{:S(2)}, u32[]{:S(2)}) collective-permute-start(bf16[128,4096]{1,0:T(8,128)(2,1)S(1)} %add_convert_fusion.3.refs_17_), channel_id=1, source_target_pairs={{0,1},{1,0},{2,3},{3,2},{4,5},{5,4},{6,7},{7,6},{8,9},{9,8},{10,11... | collective-permute-start | bytes 3145736 | tf_op jit(solution)/shard_map/ppermute | solution.py:438
  471.5 46.1 %collective-permute-start.45 = (bf16[128,4096]{1,0:T(8,128)(2,1)S(1)}, bf16[128,4096]{1,0:T(8,128)(2,1)}, u32[]{:S(2)}, u32[]{:S(2)}) collective-permute-start(bf16[128,4096]{1,0:T(8,128)(2,1)S(1)} %add_convert_fusion.5.refs_16_), channel_id=1, source_target_pairs={{0,4},{2,6},{4,0},{6,2},{8,12},{10,14},{12,8},{14,10},{16,20},{18,... | collective-permute-start | bytes 3145736 | tf_op jit(solution)/shard_map/ppermute | solution.py:430
  473.1 47.5 %collective-permute-start.53 = (bf16[128,4096]{1,0:T(8,128)(2,1)}, bf16[128,4096]{1,0:T(8,128)(2,1)S(1)}, u32[]{:S(2)}, u32[]{:S(2)}) collective-permute-start(bf16[128,4096]{1,0:T(8,128)(2,1)} %get-tuple-element.118), channel_id=1, source_target_pairs={{0,4},{2,6},{4,0},{6,2},{8,12},{10,14},{12,8},{14,10},{16,20},{18,... | collective-permute-start | bytes 3145736 | tf_op jit(solution)/shard_map/ppermute | solution.py:430
  477.1 72.5 %collective-permute-start.52 = (bf16[128,4096]{1,0:T(8,128)(2,1)}, bf16[128,4096]{1,0:T(8,128)(2,1)}, u32[]{:S(2)}, u32[]{:S(2)}) collective-permute-start(bf16[128,4096]{1,0:T(8,128)(2,1)} %get-tuple-element.116), channel_id=1, source_target_pairs={{0,4},{2,6},{4,0},{6,2},{8,12},{10,14},{12,8},{14,10},{16,20},{18,... | collective-permute-start | bytes 3145736 | tf_op jit(solution)/shard_map/ppermute | solution.py:430
  540.4 54.6 %collective-permute-start.65 = (bf16[128,2048]{1,0:T(8,128)(2,1)}, bf16[128,2048]{1,0:T(8,128)(2,1)}, u32[]{:S(2)}, u32[]{:S(2)}) collective-permute-start(bf16[128,2048]{1,0:T(8,128)(2,1)} %get-tuple-element.136), channel_id=1, source_target_pairs={{0,1},{1,0},{2,3},{3,2},{4,5},{5,4},{6,7},{7,6},{8,9},{9,8},{10,11... | collective-permute-start | bytes 1572872 | tf_op jit(solution)/shard_map/ppermute | solution.py:438
  548.4 46.6 %collective-permute-start.67 = (bf16[128,2048]{1,0:T(8,128)(2,1)}, bf16[128,2048]{1,0:T(8,128)(2,1)}, u32[]{:S(2)}, u32[]{:S(2)}) collective-permute-start(bf16[128,2048]{1,0:T(8,128)(2,1)} %get-tuple-element.139), channel_id=1, source_target_pairs={{0,1},{1,0},{2,3},{3,2},{4,5},{5,4},{6,7},{7,6},{8,9},{9,8},{10,11... | collective-permute-start | bytes 1572872 | tf_op jit(solution)/shard_map/ppermute | solution.py:438
  554.4 40.6 %collective-permute-start.55 = (bf16[128,4096]{1,0:T(8,128)(2,1)}, bf16[128,4096]{1,0:T(8,128)(2,1)S(1)}, u32[]{:S(2)}, u32[]{:S(2)}) collective-permute-start(bf16[128,4096]{1,0:T(8,128)(2,1)} %add_convert_fusion.1), channel_id=1, source_target_pairs={{0,8},{2,10},{4,12},{6,14},{8,16},{10,18},{12,20},{14,22},{16,24},... | collective-permute-start | bytes 3145736 | tf_op jit(solution)/shard_map/ppermute | solution.py:426
  694.5 69.6 %collective-permute-start.84 = (bf16[1,1,704,2048]{3,2,1,0:T(8,128)(2,1)}, bf16[1,1,704,2048]{3,2,1,0:T(8,128)(2,1)}, u32[]{:S(2)}, u32[]{:S(2)}) collective-permute-start(bf16[1,1,704,2048]{3,2,1,0:T(8,128)(2,1)} %shard_map.301.refs_1_), channel_id=1, source_target_pairs={{0,2},{2,0},{4,6},{6,4},{8,10},{10,8},{12,14},{14,12},{16,18},{18,... | collective-permute-start | bytes 8650760 | tf_op jit(solution)/shard_map/ppermute | solution.py:434
  694.7 106.4 %collective-permute-start.83 = (bf16[1,2,704,2048]{3,2,1,0:T(8,128)(2,1)}, bf16[1,2,704,2048]{3,2,1,0:T(8,128)(2,1)}, u32[]{:S(2)}, u32[]{:S(2)}) collective-permute-start(bf16[1,2,704,2048]{3,2,1,0:T(8,128)(2,1)} %shard_map.299.refs_1_), channel_id=1, source_target_pairs={{0,2},{2,0},{4,6},{6,4},{8,10},{10,8},{12,14},{14,12},{16,18},{18,... | collective-permute-start | bytes 17301512 | tf_op jit(solution)/shard_map/ppermute | solution.py:434
  700.8 61.1 %collective-permute-start.72 = (bf16[512,2176]{1,0:T(8,128)(2,1)}, bf16[512,2176]{1,0:T(8,128)(2,1)}, u32[]{:S(2)}, u32[]{:S(2)}) collective-permute-start(bf16[512,2176]{1,0:T(8,128)(2,1)} %shard_map.307), channel_id=1, source_target_pairs={{0,4},{2,6},{4,0},{6,2},{8,12},{10,14},{12,8},{14,10},{16,20},{18,... | collective-permute-start | bytes 6684680 | tf_op jit(solution)/shard_map/ppermute | solution.py:430
  702.8 119.4 %all-to-all-start.1 = ((bf16[16,288,128]{2,1,0:T(8,128)(2,1)}), bf16[16,288,128]{2,1,0:T(8,128)(2,1)}, u32[]{:S(2)}, u32[]{:S(2)}) async-start(bf16[16,288,128]{2,1,0:T(8,128)(2,1)} %add_convert_fusion), calls=%async_computation.1 | async-start | bytes 2359296 | tf_op jit(solution)/shard_map/all_to_all | solution.py:1767
  718.5 33.4 %collective-permute-start.79 = (bf16[256,1536]{1,0:T(8,128)(2,1)S(1)}, bf16[256,1536]{1,0:T(8,128)(2,1)S(1)}, u32[]{:S(2)}, u32[]{:S(2)}) collective-permute-start(bf16[256,1536]{1,0:T(8,128)(2,1)S(1)} %add_convert_fusion.7), channel_id=1, source_target_pairs={{0,8},{2,10},{4,12},{6,14},{8,16},{10,18},{12,20},{14,22},{16,24},... | collective-permute-start | bytes 2359304 | tf_op jit(solution)/shard_map/ppermute | solution.py:426
  (150 other events, 2034.9 us)

commit v8 on v7

--- a/solution.py
+++ b/solution.py
@@ -507,11 +507,13 @@
     return held
 
 
-def gather_weight(held):
+def gather_weight(held, early):
     chunks = []
     beside = None
     for distance, current in enumerate(held):
-        beside = other_y(current if beside is None else after(current, beside))
+        if distance:
+            current_after = after(current, beside, *(early if distance == 2 else ()))
+        beside = other_y(current_after if distance else current)
         for flip_y, chunk in ((0, current), (1, beside)):
             for flip_core, piece in ((0, chunk), (1, other_core(chunk))):
                 chunks.append(((distance, flip_y, flip_core), piece))
@@ -919,20 +921,20 @@
     ).astype(bf16)
 
 
-def attend_back(place, segments, cosine, sine, own, other, saved, heads, first_width):
+def attend_back(place, segments, cosine, sine, own, other, saved, heads, first_width, others):
     f32, bf16 = jnp.float32, jnp.bfloat16
     keyval = saved[6]
     tokens = 2 * own.shape[0]
     span = heads * (ROPE // 2)
     return pl.pallas_call(
-        functools.partial(attend_back_kernel, heads),
+        lambda *refs: attend_back_kernel(heads, *refs[:16], *refs[16 + len(others) :]),
         out_shape=[
             jax.ShapeDtypeStruct((tokens, first_width), bf16),
             jax.ShapeDtypeStruct((tokens, keyval.shape[1]), bf16),
             jax.ShapeDtypeStruct((tokens, KVR), bf16),
             jax.ShapeDtypeStruct((1, KVR), f32),
         ],
-        in_specs=[pl.BlockSpec(memory_space=pltpu.SMEM)] + in_vmem(15),
+        in_specs=[pl.BlockSpec(memory_space=pltpu.SMEM)] + in_vmem(15) + in_place(len(others)),
         out_specs=in_vmem(4),
         scratch_shapes=[
             pltpu.VMEM((tokens, heads * NOPE), bf16),
@@ -954,6 +956,7 @@
         own,
         other,
         *saved,
+        *others,
     )
 
 
@@ -1388,14 +1391,42 @@
     )(*pieces, down, *kept, *others)
 
 
-def mlp_kernel(tiles, columns, joined, pieces, others, experts_ref, routed_ref, *refs):
+def out_kernel(pieces, *refs):
+    hidden_ref, weight_ref = refs[:2]
+    outs = refs[2 : 2 + pieces]
+    size = hidden_ref.shape[0] // (RINGS * pieces)
+    for r in range(RINGS):
+        part = hidden_ref[r * pieces * size : (r + 1) * pieces * size, :]
+        result = wide_dot(part, weight_ref[...]).astype(jnp.bfloat16)
+        for k in range(pieces):
+            outs[k][r * size : (r + 1) * size, :] = result[k * size : (k + 1) * size]
+
+
+def out_rows(pieces, hidden, down):
+    rows, width = hidden.shape
+    depth = down.shape[1]
+    return pl.pallas_call(
+        functools.partial(out_kernel, pieces),
+        grid=(depth // TILE,),
+        in_specs=[whole(hidden), pl.BlockSpec((width, TILE), lambda i: (0, i))],
+        out_specs=[pl.BlockSpec((rows // pieces, TILE), lambda i: (0, i))] * pieces,
+        out_shape=[jax.ShapeDtypeStruct((rows // pieces, depth), jnp.bfloat16)] * pieces,
+        compiler_params=pltpu.CompilerParams(vmem_limit_bytes=48 * 1024 * 1024),
+        cost_estimate=pl.CostEstimate(
+            flops=2 * rows * depth * width,
+            bytes_accessed=2 * (rows * depth + depth * width + rows * width),
+            transcendentals=0,
+        ),
+    )(hidden, down)
+
+
+def mlp_kernel(tiles, pieces, others, experts_ref, routed_ref, *refs):
     row_refs = refs[:pieces]
-    router_ref, gate_col, up_col, down_grad, gate_row, up_row, down_row = refs[pieces : pieces + 7]
-    outs = refs[pieces + 7 + others :]
-    grad_refs, out_refs = outs[:pieces], outs[:pieces] if joined else outs[pieces : 2 * pieces]
-    outs = outs[pieces if joined else 2 * pieces :]
-    rows_out, hidden_out, gate_out, up_out, logit_out = outs[:5]
-    hidden_all, gate_all, up_all, prob_ref, scale_ref, sum_ref, semaphores = outs[5:]
+    router_ref, gate_col, up_col, down_grad, gate_row, up_row = refs[pieces : pieces + 6]
+    outs = refs[pieces + 6 + others :]
+    grad_refs = outs[:pieces]
+    rows_out, hidden_out, gate_out, up_out, logit_out = outs[pieces : pieces + 5]
+    gate_all, up_all, prob_ref, scale_ref, sum_ref, semaphores = outs[pieces + 5 :]
     step = pl.program_id(0)
     third = tiles // 2
     total = rows_out.shape[0]
@@ -1418,7 +1449,7 @@
 
     @pl.when(step < tiles)
     def _():
-        columns_here = pl.ds(pl.multiple_of(step * TILE, TILE), TILE)
+        columns = pl.ds(pl.multiple_of(step * TILE, TILE), TILE)
         kind = step // third
         half = total // 2
         for k in (0, 1):
@@ -1436,11 +1467,9 @@
                 jnp.bfloat16
             )
             low_up = (grad_hidden * silu).astype(jnp.bfloat16)
-            gate_all[part, columns_here] = low_gate
-            up_all[part, columns_here] = low_up
-            low_hidden = (scale * hidden).astype(jnp.bfloat16)
-            hidden_all[part, columns_here] = low_hidden
-            hidden_out[part, :] = low_hidden
+            gate_all[part, columns] = low_gate
+            up_all[part, columns] = low_up
+            hidden_out[part, :] = (scale * hidden).astype(jnp.bfloat16)
             gate_out[part, :] = low_gate
             up_out[part, :] = low_up
 
@@ -1452,7 +1481,7 @@
             grad_logits += scale_ref[k] * sum_ref[k] * (own - prob_ref[...])
         logit_out[...] = grad_logits.astype(jnp.bfloat16)
 
-    @pl.when((step >= tiles) & (step < tiles + columns))
+    @pl.when(step >= tiles)
     def _():
         some = pl.ds(pl.multiple_of((step - tiles) * 2 * TILE, TILE), 2 * TILE)
         grads = wide_dot(gate_all[...], gate_row[...]) + wide_dot(up_all[...], up_row[...])
@@ -1461,15 +1490,9 @@
         for k in range(pieces):
             grad_refs[k][...] = grads[k * size : (k + 1) * size]
 
-    @pl.when(step >= tiles + columns)
-    def _():
-        result = wide_dot(hidden_all[...], down_row[...]).astype(jnp.bfloat16)
-        for k in range(pieces):
-            out_refs[k][...] = result[k * size : (k + 1) * size]
-
-
-def mlp_plane(distance, joined, experts, routed, rows, down_grad, router, weights, kept, others):
-    gate, up, down = weights
+
+def mlp_plane(distance, experts, routed, rows, down_grad, router, weights, kept, others):
+    gate, up = weights
     pieces = len(rows)
     size, depth = rows[0].shape
     width = gate.shape[0]
@@ -1481,42 +1504,26 @@
         return jnp.minimum(i, tiles - 1)
 
     def late(i):
-        return jnp.clip(i - tiles, 0, columns - 1)
-
-    def last(i):
-        return jnp.maximum(i - tiles - columns, 0)
+        return jnp.maximum(i - tiles, 0)
 
     tile_spec = pl.BlockSpec((total, TILE), lambda i: (distance, early(i)))
-    weight_tile = pl.BlockSpec((TILE, depth), lambda i: (early(i), 0))
-    if joined:
-        result_specs = [
-            pl.BlockSpec((size, 2 * TILE), lambda i: (0, jnp.maximum(i - tiles, 0)))
-        ] * pieces
-        result_shapes = [jax.ShapeDtypeStruct((size, 2 * depth), low)] * pieces
-    else:
-        result_specs = [pl.BlockSpec((size, 2 * TILE), lambda i: (0, late(i)))] * pieces + [
-            pl.BlockSpec((size, 2 * TILE), lambda i: (0, last(i)))
-        ] * pieces
-        result_shapes = [jax.ShapeDtypeStruct((size, depth), low)] * (2 * pieces)
-    first_kept = 2 + pieces + 7
+    anywhere = pl.BlockSpec(memory_space=pl.ANY)
+    first_kept = 2 + pieces + 6
     results = pl.pallas_call(
-        functools.partial(
-            mlp_kernel, tiles, columns, joined, pieces, len(kept) + len(others)
-        ),
-        grid=(tiles + 2 * columns,),
+        functools.partial(mlp_kernel, tiles, pieces, len(kept) + len(others)),
+        grid=(tiles + columns,),
         in_specs=[pl.BlockSpec(memory_space=pltpu.SMEM), whole(routed)]
-        + in_place(pieces)
+        + [anywhere] * pieces
         + [
             pl.BlockSpec((depth, 128), lambda i: (0, router.shape[1] // 128 - 1)),
-            weight_tile,
-            weight_tile,
+            pl.BlockSpec((TILE, depth), lambda i: (early(i), 0)),
+            pl.BlockSpec((TILE, depth), lambda i: (early(i), 0)),
             tile_spec,
             pl.BlockSpec((width, 2 * TILE), lambda i: (0, late(i))),
             pl.BlockSpec((width, 2 * TILE), lambda i: (0, late(i))),
-            pl.BlockSpec((width, 2 * TILE), lambda i: (0, last(i))),
         ]
-        + in_place(len(kept) + len(others)),
-        out_specs=result_specs
+        + [anywhere] * (len(kept) + len(others)),
+        out_specs=[pl.BlockSpec((size, 2 * TILE), lambda i: (0, late(i)))] * pieces
         + [
             pl.BlockSpec((total, depth), lambda i: (distance, 0)),
             tile_spec,
@@ -1524,30 +1531,27 @@
             tile_spec,
             pl.BlockSpec((total, 128), lambda i: (distance, 0)),
         ],
-        out_shape=result_shapes
+        out_shape=[jax.ShapeDtypeStruct((size, depth), low)] * pieces
         + [
             jax.ShapeDtypeStruct((RINGS * total, many), low)
             for many in (depth, width, width, width, 128)
         ],
-        scratch_shapes=[pltpu.VMEM((total, width), low)] * 3
+        scratch_shapes=[pltpu.VMEM((total, width), low)] * 2
         + [
             pltpu.VMEM((total, 128), jnp.float32),
             pltpu.VMEM((3, total, 1), jnp.float32),
             pltpu.VMEM((3, total, 1), jnp.float32),
             pltpu.SemaphoreType.DMA((pieces,)),
         ],
-        input_output_aliases={
-            first_kept + k: len(result_shapes) + k for k in range(len(kept))
-        },
-        compiler_params=pltpu.CompilerParams(vmem_limit_bytes=56 * 1024 * 1024),
+        input_output_aliases={first_kept + k: pieces + k for k in range(len(kept))},
+        compiler_params=pltpu.CompilerParams(vmem_limit_bytes=48 * 1024 * 1024),
         cost_estimate=pl.CostEstimate(
-            flops=2 * total * depth * width * 5,
-            bytes_accessed=2 * (5 * depth * width + 4 * total * depth + 4 * total * width),
+            flops=2 * total * depth * width * 4,
+            bytes_accessed=2 * (4 * depth * width + 3 * total * depth + 4 * total * width),
             transcendentals=total * width,
         ),
-    )(experts, routed, *rows, router, gate, up, down_grad, gate, up, down, *kept, *others)
-    count = len(result_shapes)
-    return results[:pieces], results[pieces:count], results[count:]
+    )(experts, routed, *rows, router, gate, up, down_grad, gate, up, *kept, *others)
+    return results[:pieces], results[pieces:]
 
 
 def gather_body(
@@ -1606,9 +1610,6 @@
     expert_in = expert_gate_up.swapaxes(2, 3)
     expert_in_other = other_core(expert_in)
     expert_down_other = other_core(expert_down)
-    chunks = gather_weight(held)
-    grad_planes = gather_rows(cotangent, "xxxx")
-
     shared_near = lax.all_to_all(
         pack_shared(shared_gate_up, shared_down, blocks, ()),
         "dp",
@@ -1618,30 +1619,9 @@
     )
     shared_far = other_core(shared_near)
 
-    gate_weight, up_weight, down_weight = pack_units(
-        expert_in,
-        expert_in_other,
-        expert_down,
-        expert_down_other,
-        shared_near,
-        shared_far,
-        shared,
-        (),
-    )
-    half_kept = down_grads(
-        0,
-        [piece for plane in grad_planes[:2] for piece in plane],
-        down_weight,
-        (),
-        (),
-    )
-    down_grad, every_grad = down_grads(
-        1,
-        [piece for plane in grad_planes[2:] for piece in plane],
-        down_weight,
-        half_kept,
-        (),
-    )
+    chunks = gather_weight(held, (shared_near,))
+    grad_planes = gather_rows(after(cotangent, held[3]), "xyxy")
+
     cosine, sine = rotary_tables(segments[0], ROPE)
     cosine = jnp.tile(cosine, (1, heads))
     sine = jnp.tile(sine, (1, heads))
@@ -1672,7 +1652,13 @@
         chunks,
         heads,
         sizes,
-        (down_grad,),
+        (
+            grad_planes[3][0],
+            grad_planes[0][1],
+            grad_planes[0][2],
+            grad_planes[1][2],
+            grad_planes[2][2],
+        ),
     )
     attn_gain_wide, ffn_gain_wide = gains[0], gains[1]
     mixed = block_input.astype(f32) + own_part + other_x(sent_part).astype(f32)
@@ -1703,26 +1689,50 @@
 
     corners = "yxyx"
     row_planes = gather_rows(second_normed, corners, True)
+
+    gate_weight, up_weight, down_weight = pack_units(
+        expert_in,
+        expert_in_other,
+        expert_down,
+        expert_down_other,
+        shared_near,
+        shared_far,
+        shared,
+        (second_normed,),
+    )
+    half_kept = down_grads(
+        0,
+        [piece for plane in grad_planes[:2] for piece in plane],
+        down_weight,
+        (),
+        (row_planes[1][0],),
+    )
+    down_grad, every_grad = down_grads(
+        1,
+        [piece for plane in grad_planes[2:] for piece in plane],
+        down_weight,
+        half_kept,
+        (row_planes[2][0],),
+    )
     expert_ids = jnp.concatenate(
         [chip_experts, jnp.array([experts, used + 3 - query_width - KVR], jnp.int32)]
     )
     kept = []
     turned, closed = [], []
     for distance in range(RINGS):
-        others = [row_planes[3][0]] if distance == 0 else []
+        others = [row_planes[3][0]] if distance == 0 else [row_planes[2][3]]
         if distance == 2:
-            others = list(turned[0][1:])
+            others = list(turned[0][1:]) + [row_planes[3][3]]
         elif distance == 3:
             others = list(turned[1][1:]) + list(closed[0][1:])
-        grads, outs, kept = mlp_plane(
+        grads, kept = mlp_plane(
             distance,
-            distance < RINGS - 1,
             expert_ids,
             routed[distance],
             row_planes[distance],
             down_grad,
             first_weight,
-            (gate_weight, up_weight, down_weight),
+            (gate_weight, up_weight),
             kept,
             others,
         )
@@ -1745,21 +1755,13 @@
     moving = ring_step(wide_sum(*closed[1]).astype(bf16))
     moving = ring_step(wide_sum(moving, *closed[2]).astype(bf16))
     own, beside, across = turned[3]
-    own = after(own, sent_in)
+    own = after(own, sent_down)
     grad_close = close_plane((own, after(beside, shared_sent), across))
     grad_second = wide_sum(
-        ring_step(wide_sum(moving[:, :D], *grad_close).astype(bf16)),
-        after(closed[0][0], sent_down)[:, :D],
-        *[part[:, :D] for part in closed[0][1:]],
-    )
-    outs = list(outs)
-    outs[3] = after(outs[3], grad_close[1])
-    out_close = close_plane(turn_corner(outs, corners[3]))
-    block_output = mixed + wide_sum(
-        ring_step(wide_sum(moving[:, D:], *out_close).astype(bf16)),
-        *[part[:, D:] for part in closed[0]],
-    )
-
+        ring_step(wide_sum(moving, *grad_close).astype(bf16)),
+        after(closed[0][0], sent_in),
+        *closed[0][1:],
+    )
     arrived_in = other_core(sent_in)
     arrived_down = other_core(sent_down)
     router_at = used + 3 - query_width - KVR
@@ -1774,6 +1776,11 @@
     )
     grad_mixed_low = grad_mixed.astype(bf16)
     other_grad = other_x(grad_mixed_low)
+    outs = list(out_rows(4, every_hidden, down_weight))
+    outs[3] = after(outs[3], grad_close[2])
+    outs[2] = after(outs[2], other_grad)
+    out_own, out_beside, out_across = close_plane(turn_corner(outs, "x"))
+
 
     places = jnp.stack([place_of(coords, key_of) for key_of in weight_keys()]).astype(jnp.int32)
     projected_grad, keyval_grad, latent_normed, gain_latent_part = attend_back(
@@ -1786,6 +1793,7 @@
         (keyval_weight, output_turned, nope, turned_query, latent, key, keyval, total, latent_gain_row),
         heads,
         first_width,
+        (shared_grads,),
     )
     grad_attn = jnp.concatenate(
         [
@@ -1820,17 +1828,21 @@
     other_kept = other_grads(*other_parts, 0, 8, other_arrived)
     far = first_grads(*first_parts, 4, 4, first_arrived)
     from_y = other_y(far)
+    out_total = wide_sum(after(out_own, far), out_beside, out_across)
+    block_output = mixed + ring_sum(
+        [out_total[r * local_rows : (r + 1) * local_rows] for r in range(RINGS)], bf16
+    )
     near = first_grads(*first_parts, 0, 4, first_arrived)
     other_summed = ring_sum(
         [other_kept[2 * r * depth : 2 * (r + 1) * depth] for r in range(RINGS)], bf16
     )
     other_closed = other_summed[:depth] + other_y(other_summed[depth:].astype(bf16)).astype(f32)
     grad_expert_down = expert_grads(
-        (every_hidden,), every_grad, units, 0, arrived_down, f32, (near,)
+        (every_hidden,), every_grad, units, 0, arrived_down, f32, (from_y,)
     )
     first_closed = close_ring(near, from_y)
     grad_expert_in = expert_grads(
-        (every_gate_grad, every_up_grad), every_row, units, 0, arrived_in, f32, (from_y,)
+        (every_gate_grad, every_up_grad), every_row, units, 0, arrived_in, f32, (near,)
     )
     grad_shared_in, grad_shared_down = unpack_shared(shared_grads, shared, (from_y,))
     grad_expert_gate_up = grad_expert_in.swapaxes(2, 3)

time: 845 us -> 889 us (1.052); the launches traced: 837 us -> 871 us
  starting transfers between devices: 89.5 us -> 129 us
    ppermute x19 -> x21, starting transfers between devices: 18.3 us -> 54.3 us  [ring_step(): lax.ppermute(values, 'dp', [(i, (i + RINGS) % 16) for i in range(16)])]
    unnamed x207 -> x245, local copies, waits for them, and re-layouts: 56 us -> 65.8 us
    pallas_call x5 -> x6, Pallas kernels: 159 us -> 151 us  [the longest x4 116 us: mlp_plane(): pl.pallas_call(functools.partial(mlp_kernel, tiles, pieces, len(kept) + l...]
    ppermute x23 -> x25, starting transfers between devices: 26 us -> 32.2 us  [other_y(): return lax.ppermute(values, 'dp', [(i, i ^ 2) for i in range(16)])]
    ppermute x27 -> x25, waiting for transfers between devices: 95.1 us -> 89.9 us  [other_x(): return lax.ppermute(values, 'tensor', [(0, 1), (1, 0)])]
    ppermute x19 -> x21, waiting for transfers between devices: 127 us -> 123 us  [ring_step(): lax.ppermute(values, 'dp', [(i, (i + RINGS) % 16) for i in range(16)])]
    ppermute x27 -> x25, starting transfers between devices: 31.4 us -> 28.2 us  [other_x(): return lax.ppermute(values, 'tensor', [(0, 1), (1, 0)])]
    ppermute x23 -> x25, waiting for transfers between devices: 61 us -> 62 us  [other_y(): return lax.ppermute(values, 'dp', [(i, i ^ 2) for i in range(16)])]
  transfers between devices with their start and end apart: 87 -> 89, of which waited for: 35 -> 29; matrix products, arithmetic and copies ran while one was open for 7% -> 8% of each run, Pallas kernels for 34% -> 36%
where the time goes in v8:
time: 889 us; the launch traced here: 871 us
  Pallas kernels  331 us (37%)
  waiting for transfers between devices  281 us (32%)
  starting transfers between devices  129 us (15%)
  local copies, waits for them, and re-layouts  85 us (10%)
  other arithmetic  42.7 us (5%)
    ppermute x21, waiting for transfers between devices, ring_step(): lax.ppermute(values, 'dp', [(i, (i + RINGS) % 16) for i in range(16)])  123 us
    pallas_call x4, Pallas kernels, mlp_plane(): pl.pallas_call(functools.partial(mlp_kernel, tiles, pieces, len(kept) + l...  116 us
    ppermute x25, waiting for transfers between devices, other_x(): return lax.ppermute(values, 'tensor', [(0, 1), (1, 0)])  89.9 us
    unnamed x245, local copies, waits for them, and re-layouts  65.8 us
    pallas_call x4, Pallas kernels, expert_grads(): pl.pallas_call(functools.partial(expert_grads_kernel, units, len(lefts),...  62.5 us
    ppermute x25, waiting for transfers between devices, other_y(): return lax.ppermute(values, 'dp', [(i, i ^ 2) for i in range(16)])  62 us
    ppermute x21, starting transfers between devices, ring_step(): lax.ppermute(values, 'dp', [(i, (i + RINGS) % 16) for i in range(16)])  54.3 us
    ppermute x25, starting transfers between devices, other_y(): return lax.ppermute(values, 'dp', [(i, i ^ 2) for i in range(16)])  32.2 us
  transfers between devices with their start and end apart: 89, of which 29 were waited for; matrix products, arithmetic and copies ran while one was open for 8% of the time, Pallas kernels for 36%

profile of v8, /device:TPU:0, one launch (start us, length us, event | category | flops | bytes accessed | tf_op | source)
XLA Modules:
  0.0 871.4 jit_solution(3721242060667176599)
XLA Ops:
  22.4 14.9 %collective-permute-done.4.refs_4_ = bf16[128,3712]{1,0:T(8,128)(2,1)} collective-permute-done((bf16[128,3712]{1,0:T(8,128)(2,1)}, bf16[128,3712]{1,0:T(8,128)(2,1)}, u32[]{:S(2)}, u32[]{:S(2)}) %collective-permute-start.4) | collective-permute-done | bytes 950304 | tf_op jit(solution)/shard_map/ppermute | solution.py:426
  39.5 13.9 %collective-permute-done.2.refs_1_.refs_2_ = bf16[128,3712]{1,0:T(8,128)(2,1)S(1)} collective-permute-done((bf16[128,3712]{1,0:T(8,128)(2,1)}, bf16[128,3712]{1,0:T(8,128)(2,1)S(1)}, u32[]{:S(2)}, u32[]{:S(2)}) %collective-permute-start.2) | collective-permute-done | bytes 950304 | tf_op jit(solution)/shard_map/ppermute | solution.py:430
  58.3 17.5 %collective-permute-done.8.refs_8_ = bf16[128,3712]{1,0:T(8,128)(2,1)} collective-permute-done((bf16[128,3712]{1,0:T(8,128)(2,1)}, bf16[128,3712]{1,0:T(8,128)(2,1)}, u32[]{:S(2)}, u32[]{:S(2)}) %collective-permute-start.8) | collective-permute-done | bytes 950304 | tf_op jit(solution)/shard_map/ppermute | solution.py:426
  86.0 14.5 %collective-permute-done.12.refs_1_.refs_12_ = bf16[128,3712]{1,0:T(8,128)(2,1)S(1)} collective-permute-done((bf16[128,3712]{1,0:T(8,128)(2,1)}, bf16[128,3712]{1,0:T(8,128)(2,1)S(1)}, u32[]{:S(2)}, u32[]{:S(2)}) %collective-permute-start.12) | collective-permute-done | bytes 950304 | tf_op jit(solution)/shard_map/ppermute | solution.py:426
  121.4 23.9 %collective-permute-done.19.refs_17_.refs_1_ = bf16[128,2048]{1,0:T(8,128)(2,1)} collective-permute-done((bf16[128,2048]{1,0:T(8,128)(2,1)S(1)}, bf16[128,2048]{1,0:T(8,128)(2,1)}, u32[]{:S(2)}, u32[]{:S(2)}) %collective-permute-start.19) | collective-permute-done | bytes 524320 | tf_op jit(solution)/shard_map/ppermute | solution.py:430
  145.3 16.7 %collective-permute-start.17 = (bf16[128,2048]{1,0:T(8,128)(2,1)S(1)}, bf16[128,2048]{1,0:T(8,128)(2,1)S(1)}, u32[]{:S(2)}, u32[]{:S(2)}) collective-permute-start(bf16[128,2048]{1,0:T(8,128)(2,1)S(1)} %collective-permute-done.16.refs_4_), channel_id=1, source_target_pairs={{0,8},{2,10},{4,12},{6,14},{8,16},{10,18},{12,20},{14,22},{16,24},... | collective-permute-start | bytes 1572872 | tf_op jit(solution)/shard_map/ppermute | solution.py:426
  164.9 8.1 collective-permute-done.17.refs_0_
  177.8 9.7 %collective-permute-done.18.refs_16_.refs_4_ = bf16[128,2048]{1,0:T(8,128)(2,1)} collective-permute-done((bf16[128,2048]{1,0:T(8,128)(2,1)S(1)}, bf16[128,2048]{1,0:T(8,128)(2,1)}, u32[]{:S(2)}, u32[]{:S(2)}) %collective-permute-start.18) | collective-permute-done | bytes 524320 | tf_op jit(solution)/shard_map/ppermute | solution.py:426
  188.7 22.2 %shard_map.287 = (f32[128,2048]{1,0:T(8,128)}, bf16[128,2048]{1,0:T(8,128)(2,1)S(1)}, bf16[2048,2176]{1,0:T(8,128)(2,1)}, bf16[512,2048]{1,0:T(8,128)(2,1)}, bf1...) custom-call(s32[5]{0:T(128)S(1)} %concatenate.24.place_ref.refs_0_, ...), custom_call_target="tpu_custom_call" | custom-call | flops 4429185024 | bytes 30408704 | tf_op jit(solution)/shard_map/pallas_call | solution.py:787
  218.3 9.4 %collective-permute-done.23 = bf16[128,2048]{1,0:T(8,128)(2,1)S(1)} collective-permute-done((bf16[128,2048]{1,0:T(8,128)(2,1)S(1)}, bf16[128,2048]{1,0:T(8,128)(2,1)S(1)}, u32[]{:S(2)}, u32[]{:S(2)}) %collective-permute-start.23) | collective-permute-done | bytes 524320 | tf_op jit(solution)/shard_map/ppermute | solution.py:438
  248.8 9.6 %collective-permute-done.26.refs_2_ = bf16[128,2048]{1,0:T(8,128)(2,1)} collective-permute-done((bf16[128,2048]{1,0:T(8,128)(2,1)S(1)}, bf16[128,2048]{1,0:T(8,128)(2,1)}, u32[]{:S(2)}, u32[]{:S(2)}) %collective-permute-start.26) | collective-permute-done | bytes 524320 | tf_op jit(solution)/shard_map/ppermute | solution.py:438
  267.6 13.6 %shard_map.290 = (bf16[1792,2048]{1,0:T(8,128)(2,1)}, bf16[1792,2048]{1,0:T(8,128)(2,1)}, bf16[1792,2048]{1,0:T(8,128)(2,1)}) custom-call(bf16[1,2,704,2048]{3,2,1,0:T(8,128)(2,1)S(1)} %bitcast.77, bf16[1,2,704,2048]{3,2,1,0:T(8,128)(2,1)} %collective-permute-done.34.other_in, bf16[1,704,2048]{2,1,0:T(8,128)(2,1)} %own_down.1, ...), custom_call_target="tpu_custom_call" | custom-call | bytes 44040192 | tf_op jit(solution)/shard_map/pallas_call | solution.py:1256
  286.1 14.4 %shard_map.291 = (bf16[2048,1792]{1,0:T(8,128)(2,1)}, bf16[2048,2048]{1,0:T(8,128)(2,1)}) custom-call(bf16[128,2048]{1,0:T(8,128)(2,1)S(1)} %copy-done.48, bf16[128,2048]{1,0:T(8,128)(2,1)} %collective-permute-done.19.refs_17_.refs_1_, bf16[128,2048]{1,0:T(8,128)(2,1)S(1)} %copy-done.61, bf16[128,2048]{1,0:T(8,128)(2,1)} %collective-permute-done.42.refs_3_, ...), custom_call_target="tpu_custom_call" | custom-call | flops 7516192768 | bytes 19398656 | tf_op jit(solution)/shard_map/pallas_call | solution.py:1369
  301.3 13.5 %collective-permute-done.28.refs_1_ = bf16[128,2048]{1,0:T(8,128)(2,1)S(1)} collective-permute-done((bf16[128,2048]{1,0:T(8,128)(2,1)S(1)}, bf16[128,2048]{1,0:T(8,128)(2,1)S(1)}, u32[]{:S(2)}, u32[]{:S(2)}) %collective-permute-start.28) | collective-permute-done | bytes 524320 | tf_op jit(solution)/shard_map/ppermute | solution.py:430
  320.5 13.8 %shard_map.292 = (bf16[2048,1792]{1,0:T(8,128)(2,1)}, bf16[2048,2048]{1,0:T(8,128)(2,1)}) custom-call(bf16[128,2048]{1,0:T(8,128)(2,1)S(1)} %copy-done.89, bf16[128,2048]{1,0:T(8,128)(2,1)} %collective-permute-done.37.refs_1_, bf16[128,2048]{1,0:T(8,128)(2,1)S(1)} %copy-done.63, ...), custom_call_target="tpu_custom_call", output_to_operand_aliasing={{0}: (9, {}), {1}: (10, {})} | custom-call | flops 7516192768 | bytes 19398656 | tf_op jit(solution)/shard_map/pallas_call | solution.py:1369
  335.4 29.6 %shard_map.293 = (bf16[128,2048]{1,0:T(8,128)(2,1)S(1)}, bf16[128,2048]{1,0:T(8,128)(2,1)S(1)}, bf16[128,2048]{1,0:T(8,128)(2,1)S(1)}, bf16[128,2048]{1,0:T(8,12...) custom-call(s32[4]{0:T(128)S(1)} %pad_add_fusion.experts_ref, ...), custom_call_target="tpu_custom_call" | custom-call | flops 15032385536 | bytes 42991616 | tf_op jit(solution)/shard_map/pallas_call | solution.py:1512
  368.7 28.5 %shard_map.294 = (bf16[128,2048]{1,0:T(8,128)(2,1)S(1)}, bf16[128,2048]{1,0:T(8,128)(2,1)S(1)}, bf16[128,2048]{1,0:T(8,128)(2,1)S(1)}, bf16[128,2048]{1,0:T(8,12...) custom-call(s32[4]{0:T(128)S(1)} %pad_add_fusion.experts_ref, ...), custom_call_target="tpu_custom_call", output_to_operand_aliasing={{4}: (12, {}), {5}: (13, {}), {6}: (14, {}), {7}: (15, {}),... | custom-call | flops 15032385536 | bytes 42991616 | tf_op jit(solution)/shard_map/pallas_call | solution.py:1512
  418.3 18.9 %collective-permute-done.33.refs_17_.refs_3_ = bf16[128,2048]{1,0:T(8,128)(2,1)S(1)} collective-permute-done((bf16[128,2048]{1,0:T(8,128)(2,1)}, bf16[128,2048]{1,0:T(8,128)(2,1)S(1)}, u32[]{:S(2)}, u32[]{:S(2)}) %collective-permute-start.33) | collective-permute-done | bytes 524320 | tf_op jit(solution)/shard_map/ppermute | solution.py:438
  438.2 28.7 %shard_map.295 = (bf16[128,2048]{1,0:T(8,128)(2,1)S(1)}, bf16[128,2048]{1,0:T(8,128)(2,1)}, bf16[128,2048]{1,0:T(8,128)(2,1)S(1)}, bf16[128,2048]{1,0:T(8,128)(2...) custom-call(s32[4]{0:T(128)S(1)} %pad_add_fusion.experts_ref, ...), custom_call_target="tpu_custom_call", output_to_operand_aliasing={{4}: (12, {}), {5}: (13, {}), {6}: (14, {}), {7}: (15, {}),... | custom-call | flops 15032385536 | bytes 42991616 | tf_op jit(solution)/shard_map/pallas_call | solution.py:1512
  471.6 29.3 %shard_map.296 = (bf16[128,2048]{1,0:T(8,128)(2,1)S(1)}, bf16[128,2048]{1,0:T(8,128)(2,1)S(1)}, bf16[128,2048]{1,0:T(8,128)(2,1)}, bf16[128,2048]{1,0:T(8,128)(2...) custom-call(s32[4]{0:T(128)S(1)} %pad_add_fusion.experts_ref, ...), custom_call_target="tpu_custom_call", output_to_operand_aliasing={{4}: (12, {}), {5}: (13, {}), {6}: (14, {}), {7}: (15, {}),... | custom-call | flops 15032385536 | bytes 42991616 | tf_op jit(solution)/shard_map/pallas_call | solution.py:1512
  507.7 12.4 %shard_map.300 = (f32[16,288,128]{2,1,0:T(8,128)S(1)}, bf16[16,288,128]{2,1,0:T(8,128)(2,1)}, f32[128,2048]{1,0:T(8,128)S(1)}) custom-call(bf16[2048,2048]{1,0:T(8,128)(2,1)} %get-tuple-element.131.rows_ref.right_ref, bf16[2048,2048]{1,0:T(8,128)(2,1)} %get-tuple-element.128.right_ref.cots_ref, bf16[2048,1792]{1,0:T(8,128)(2,1)} %get-tuple-element.132.gate_ref.refs_0_, ...), custom_call_target="tpu_custom_call" | custom-call | flops 8589934592 | bytes 16777216 | tf_op jit(solution)/shard_map/pallas_call | solution.py:1331
  528.7 10.8 %shard_map.298.refs_1_ = bf16[1,1,704,2048]{3,2,1,0:T(8,128)(2,1)} custom-call(bf16[2048,2048]{1,0:T(8,128)(2,1)} %get-tuple-element.128.right_ref.cots_ref, bf16[2048,1792]{1,0:T(8,128)(2,1)} %get-tuple-element.119.refs_0_.hidden_ref), custom_call_target="tpu_custom_call" | custom-call | flops 6442450944 | bytes 23068672 | tf_op jit(solution)/shard_map/pallas_call | solution.py:1288
  545.1 18.8 %shard_map.302.refs_1_ = bf16[1,2,704,2048]{3,2,1,0:T(8,128)(2,1)S(1)} custom-call(bf16[2048,2048]{1,0:T(8,128)(2,1)} %get-tuple-element.131.rows_ref.right_ref, bf16[2048,1792]{1,0:T(8,128)(2,1)} %get-tuple-element.132.gate_ref.refs_0_, bf16[2048,1792]{1,0:T(8,128)(2,1)} %get-tuple-element.133.up_ref.refs_1_), custom_call_target="tpu_custom_call" | custom-call | flops 12884901888 | bytes 34603008 | tf_op jit(solution)/shard_map/pallas_call | solution.py:1288
  580.5 13.4 %collective-permute-done.65.refs_6_.refs_1_ = bf16[128,2048]{1,0:T(8,128)(2,1)S(1)} collective-permute-done((bf16[128,2048]{1,0:T(8,128)(2,1)S(1)}, bf16[128,2048]{1,0:T(8,128)(2,1)S(1)}, u32[]{:S(2)}, u32[]{:S(2)}) %collective-permute-start.65) | collective-permute-done | bytes 524320 | tf_op jit(solution)/shard_map/ppermute | solution.py:438
  605.6 13.2 %shard_map.304 = (bf16[256,2176]{1,0:T(8,128)(2,1)}, bf16[256,2048]{1,0:T(8,128)(2,1)S(1)}, bf16[256,512]{1,0:T(8,128)(2,1)S(1)}, f32[1,512]{1,0:T(1,128)S(1)}) custom-call(s32[5]{0:T(128)S(1)} %copy-done.87, s32[1,256]{1,0:T(1,128)S(1)} %copy-done.84, s32[256,1]{1,0:T(8,128)S(1)} %copy-done.50, f32[256,256]{1,0:T(8,128)S(1)} %copy-done.28, ...), custom_call_target="tpu_custom_call" | custom-call | flops 3145728000 | bytes 6291456 | tf_op jit(solution)/shard_map/pallas_call | solution.py:929
  625.4 21.2 %shard_map.297 = (bf16[512,2048]{1,0:T(8,128)(2,1)S(1)}, bf16[512,2048]{1,0:T(8,128)(2,1)S(1)}, bf16[512,2048]{1,0:T(8,128)(2,1)}, bf16[512,2048]{1,0:T(8,128)(2,1)}) custom-call(bf16[2048,1792]{1,0:T(8,128)(2,1)} %get-tuple-element.119.refs_0_.hidden_ref, bf16[1792,2048]{1,0:T(8,128)(2,1)} %get-tuple-element.94.refs_8_.refs_1_), custom_call_target="tpu_custom_call" | custom-call | flops 15032385536 | bytes 23068672 | tf_op jit(solution)/shard_map/pallas_call | solution.py:1408
  676.3 23.0 %collective-permute-done.68 = bf16[512,2048]{1,0:T(8,128)(2,1)} collective-permute-done((bf16[512,2048]{1,0:T(8,128)(2,1)}, bf16[512,2048]{1,0:T(8,128)(2,1)}, u32[]{:S(2)}, u32[]{:S(2)}) %collective-permute-start.68) | collective-permute-done | bytes 2097184 | tf_op jit(solution)/shard_map/ppermute | solution.py:438
  723.1 12.9 %collective-permute-done.81 = bf16[256,1536]{1,0:T(8,128)(2,1)S(1)} collective-permute-done((bf16[256,1536]{1,0:T(8,128)(2,1)S(1)}, bf16[256,1536]{1,0:T(8,128)(2,1)S(1)}, u32[]{:S(2)}, u32[]{:S(2)}) %collective-permute-start.81) | collective-permute-done | bytes 786464 | tf_op jit(solution)/shard_map/ppermute | solution.py:426
  771.8 21.2 %shard_map.315 = f32[1,2,704,2048]{3,2,1,0:T(8,128)} custom-call(bf16[2048,2048]{1,0:T(8,128)(2,1)} %get-tuple-element.131.rows_ref.right_ref, bf16[2048,1792]{1,0:T(8,128)(2,1)} %get-tuple-element.132.gate_ref.refs_0_, bf16[2048,1792]{1,0:T(8,128)(2,1)} %get-tuple-element.133.up_ref.refs_1_, bf16[1,2,704,2048]{3,2,1,0:T(8,128)(2,1)} %collective-permute-done.85.refs_2_, ...), custom_call_target="tpu_custom_call" | custom-call | flops 12884901888 | bytes 34603008 | tf_op jit(solution)/shard_map/pallas_call | solution.py:1288
  810.8 10.9 %collective-permute-done.76 = bf16[128,2176]{1,0:T(8,128)(2,1)S(1)} collective-permute-done((bf16[128,2176]{1,0:T(8,128)(2,1)S(1)}, bf16[128,2176]{1,0:T(8,128)(2,1)S(1)}, u32[]{:S(2)}, u32[]{:S(2)}) %collective-permute-start.76) | collective-permute-done | bytes 557088 | tf_op jit(solution)/shard_map/ppermute | solution.py:426
  823.7 9.3 %collective-permute-done.73 = bf16[128,2048]{1,0:T(8,128)(2,1)S(1)} collective-permute-done((bf16[128,2048]{1,0:T(8,128)(2,1)}, bf16[128,2048]{1,0:T(8,128)(2,1)S(1)}, u32[]{:S(2)}, u32[]{:S(2)}) %collective-permute-start.73) | collective-permute-done | bytes 524320 | tf_op jit(solution)/shard_map/ppermute | solution.py:426
  844.7 11.8 %shard_map.316 = f32[1,1,704,2048]{3,2,1,0:T(8,128)} custom-call(bf16[2048,2048]{1,0:T(8,128)(2,1)} %get-tuple-element.128.right_ref.cots_ref, bf16[2048,1792]{1,0:T(8,128)(2,1)} %get-tuple-element.119.refs_0_.hidden_ref, bf16[1,1,704,2048]{3,2,1,0:T(8,128)(2,1)} %collective-permute-done.86.refs_1_, bf16[512,2176]{1,0:T(8,128)(2,1)S(1)} %copy-done.2), custom_call_target="tpu_custom_call" | custom-call | flops 6442450944 | bytes 23068672 | tf_op jit(solution)/shard_map/pallas_call | solution.py:1288
  (526 shorter events, 339.1 us)
Async XLA Ops:
  15.5 67.5 %all-to-all-start = ((bf16[16,288,128]{2,1,0:T(8,128)(2,1)}), bf16[16,288,128]{2,1,0:T(8,128)(2,1)S(1)}, u32[]{:S(2)}, u32[]{:S(2)}) async-start(bf16[16,288,128]{2,1,0:T(8,128)(2,1)} %shard_map.283), calls=%async_computation | async-start | bytes 2359296 | tf_op jit(solution)/shard_map/all_to_all | solution.py:1613
  37.3 38.5 %collective-permute-start.8 = (bf16[128,3712]{1,0:T(8,128)(2,1)}, bf16[128,3712]{1,0:T(8,128)(2,1)}, u32[]{:S(2)}, u32[]{:S(2)}) collective-permute-start(bf16[128,3712]{1,0:T(8,128)(2,1)} %collective-permute-done.4.refs_4_), channel_id=1, source_target_pairs={{0,8},{2,10},{4,12},{6,14},{8,16},{10,18},{12,20},{14,22},{16,24},... | collective-permute-start | bytes 2850824 | tf_op jit(solution)/shard_map/ppermute | solution.py:426
  100.5 161.9 %collective-permute-start.34 = (bf16[1,2,704,2048]{3,2,1,0:T(8,128)(2,1)}, bf16[1,2,704,2048]{3,2,1,0:T(8,128)(2,1)}, u32[]{:S(2)}, u32[]{:S(2)}) collective-permute-start(bf16[1,2,704,2048]{3,2,1,0:T(8,128)(2,1)} %bitcast.76), channel_id=1, source_target_pairs={{0,2},{2,0},{4,6},{6,4},{8,10},{10,8},{12,14},{14,12},{16,18},{18,... | collective-permute-start | bytes 17301512 | tf_op jit(solution)/shard_map/ppermute | solution.py:434
  110.3 53.2 %collective-permute-start.13 = (bf16[128,3712]{1,0:T(8,128)(2,1)}, bf16[128,3712]{1,0:T(8,128)(2,1)}, u32[]{:S(2)}, u32[]{:S(2)}) collective-permute-start(bf16[128,3712]{1,0:T(8,128)(2,1)} %copy-done.98), channel_id=1, source_target_pairs={{0,2},{2,0},{4,6},{6,4},{8,10},{10,8},{12,14},{14,12},{16,18},{18,... | collective-permute-start | bytes 2850824 | tf_op jit(solution)/shard_map/ppermute | solution.py:434
  110.3 53.2 %collective-permute-start.14 = (bf16[128,3712]{1,0:T(8,128)(2,1)}, bf16[128,3712]{1,0:T(8,128)(2,1)}, u32[]{:S(2)}, u32[]{:S(2)}) collective-permute-start(bf16[128,3712]{1,0:T(8,128)(2,1)} %shard_map.285), channel_id=1, source_target_pairs={{0,4},{2,6},{4,0},{6,2},{8,12},{10,14},{12,8},{14,10},{16,20},{18,... | collective-permute-start | bytes 2850824 | tf_op jit(solution)/shard_map/ppermute | solution.py:430
  110.5 34.9 %collective-permute-start.19 = (bf16[128,2048]{1,0:T(8,128)(2,1)S(1)}, bf16[128,2048]{1,0:T(8,128)(2,1)}, u32[]{:S(2)}, u32[]{:S(2)}) collective-permute-start(bf16[128,2048]{1,0:T(8,128)(2,1)S(1)} %copy-done.47), channel_id=1, source_target_pairs={{0,4},{2,6},{4,0},{6,2},{8,12},{10,14},{12,8},{14,10},{16,20},{18,... | collective-permute-start | bytes 1572872 | tf_op jit(solution)/shard_map/ppermute | solution.py:430
  119.9 42.1 %collective-permute-start.20 = (bf16[128,2048]{1,0:T(8,128)(2,1)S(1)}, bf16[128,2048]{1,0:T(8,128)(2,1)S(1)}, u32[]{:S(2)}, u32[]{:S(2)}) collective-permute-start(bf16[128,2048]{1,0:T(8,128)(2,1)S(1)} %copy-done.47), channel_id=1, source_target_pairs={{0,1},{1,0},{2,3},{3,2},{4,5},{5,4},{6,7},{7,6},{8,9},{9,8},{10,11... | collective-permute-start | bytes 1572872 | tf_op jit(solution)/shard_map/ppermute | solution.py:438
  217.6 42.3 %collective-permute-start.35 = (bf16[1,704,2048]{2,1,0:T(8,128)(2,1)}, bf16[1,704,2048]{2,1,0:T(8,128)(2,1)}, u32[]{:S(2)}, u32[]{:S(2)}) collective-permute-start(bf16[1,704,2048]{2,1,0:T(8,128)(2,1)} %own_down.1), channel_id=1, source_target_pairs={{0,2},{2,0},{4,6},{6,4},{8,10},{10,8},{12,14},{14,12},{16,18},{18,... | collective-permute-start | bytes 8650760 | tf_op jit(solution)/shard_map/ppermute | solution.py:434
  281.2 36.2 %collective-permute-start.39 = (bf16[128,2048]{1,0:T(8,128)(2,1)}, bf16[128,2048]{1,0:T(8,128)(2,1)}, u32[]{:S(2)}, u32[]{:S(2)}) collective-permute-start(bf16[128,2048]{1,0:T(8,128)(2,1)} %collective-permute-done.18.refs_16_.refs_4_), channel_id=1, source_target_pairs={{0,4},{2,6},{4,0},{6,2},{8,12},{10,14},{12,8},{14,10},{16,20},{18,... | collective-permute-start | bytes 1572872 | tf_op jit(solution)/shard_map/ppermute | solution.py:430
  282.0 37.1 %collective-permute-start.38 = (bf16[128,2048]{1,0:T(8,128)(2,1)}, bf16[128,2048]{1,0:T(8,128)(2,1)}, u32[]{:S(2)}, u32[]{:S(2)}) collective-permute-start(bf16[128,2048]{1,0:T(8,128)(2,1)} %collective-permute-done.37.refs_1_), channel_id=1, source_target_pairs={{0,1},{1,0},{2,3},{3,2},{4,5},{5,4},{6,7},{7,6},{8,9},{9,8},{10,11... | collective-permute-start | bytes 1572872 | tf_op jit(solution)/shard_map/ppermute | solution.py:438
  283.5 35.9 %collective-permute-start.41 = (bf16[128,2048]{1,0:T(8,128)(2,1)}, bf16[128,2048]{1,0:T(8,128)(2,1)}, u32[]{:S(2)}, u32[]{:S(2)}) collective-permute-start(bf16[128,2048]{1,0:T(8,128)(2,1)} %collective-permute-done.40.refs_6_), channel_id=1, source_target_pairs={{0,4},{2,6},{4,0},{6,2},{8,12},{10,14},{12,8},{14,10},{16,20},{18,... | collective-permute-start | bytes 1572872 | tf_op jit(solution)/shard_map/ppermute | solution.py:430
  319.1 49.5 %collective-permute-start.48 = (bf16[128,2048]{1,0:T(8,128)(2,1)}, bf16[128,2048]{1,0:T(8,128)(2,1)S(1)}, u32[]{:S(2)}, u32[]{:S(2)}) collective-permute-start(bf16[128,2048]{1,0:T(8,128)(2,1)} %copy-done.33), channel_id=1, source_target_pairs={{0,1},{1,0},{2,3},{3,2},{4,5},{5,4},{6,7},{7,6},{8,9},{9,8},{10,11... | collective-permute-start | bytes 1572872 | tf_op jit(solution)/shard_map/ppermute | solution.py:438
  334.3 34.4 %collective-permute-start.47 = (bf16[128,2048]{1,0:T(8,128)(2,1)S(1)}, bf16[128,2048]{1,0:T(8,128)(2,1)S(1)}, u32[]{:S(2)}, u32[]{:S(2)}) collective-permute-start(bf16[128,2048]{1,0:T(8,128)(2,1)S(1)} %collective-permute-done.46.refs_2_), channel_id=1, source_target_pairs={{0,4},{2,6},{4,0},{6,2},{8,12},{10,14},{12,8},{14,10},{16,20},{18,... | collective-permute-start | bytes 1572872 | tf_op jit(solution)/shard_map/ppermute | solution.py:430
  366.6 38.1 %collective-permute-start.50 = (bf16[128,2048]{1,0:T(8,128)(2,1)}, bf16[128,2048]{1,0:T(8,128)(2,1)}, u32[]{:S(2)}, u32[]{:S(2)}) collective-permute-start(bf16[128,2048]{1,0:T(8,128)(2,1)} %get-tuple-element.110), channel_id=1, source_target_pairs={{0,4},{2,6},{4,0},{6,2},{8,12},{10,14},{12,8},{14,10},{16,20},{18,... | collective-permute-start | bytes 1572872 | tf_op jit(solution)/shard_map/ppermute | solution.py:430
  367.6 37.1 %collective-permute-start.31 = (bf16[128,2048]{1,0:T(8,128)(2,1)S(1)}, bf16[128,2048]{1,0:T(8,128)(2,1)}, u32[]{:S(2)}, u32[]{:S(2)}) collective-permute-start(bf16[128,2048]{1,0:T(8,128)(2,1)S(1)} %collective-permute-done.30.refs_10_.refs_0_), channel_id=1, source_target_pairs={{0,4},{2,6},{4,0},{6,2},{8,12},{10,14},{12,8},{14,10},{16,20},{18,... | collective-permute-start | bytes 1572872 | tf_op jit(solution)/shard_map/ppermute | solution.py:430
  403.4 64.3 %collective-permute-start.52 = (bf16[128,2048]{1,0:T(8,128)(2,1)}, bf16[128,2048]{1,0:T(8,128)(2,1)S(1)}, u32[]{:S(2)}, u32[]{:S(2)}) collective-permute-start(bf16[128,2048]{1,0:T(8,128)(2,1)} %copy-done.58), channel_id=1, source_target_pairs={{0,4},{2,6},{4,0},{6,2},{8,12},{10,14},{12,8},{14,10},{16,20},{18,... | collective-permute-start | bytes 1572872 | tf_op jit(solution)/shard_map/ppermute | solution.py:430
  404.7 64.0 %collective-permute-start.32 = (bf16[128,2048]{1,0:T(8,128)(2,1)S(1)}, bf16[128,2048]{1,0:T(8,128)(2,1)S(1)}, u32[]{:S(2)}, u32[]{:S(2)}) collective-permute-start(bf16[128,2048]{1,0:T(8,128)(2,1)S(1)} %collective-permute-done.30.refs_10_.refs_0_), channel_id=1, source_target_pairs={{0,1},{1,0},{2,3},{3,2},{4,5},{5,4},{6,7},{7,6},{8,9},{9,8},{10,11... | collective-permute-start | bytes 1572872 | tf_op jit(solution)/shard_map/ppermute | solution.py:438
  414.8 54.9 %collective-permute-start.53 = (bf16[128,2048]{1,0:T(8,128)(2,1)S(1)}, bf16[128,2048]{1,0:T(8,128)(2,1)S(1)}, u32[]{:S(2)}, u32[]{:S(2)}) collective-permute-start(bf16[128,2048]{1,0:T(8,128)(2,1)S(1)} %add_convert_fusion.10.refs_16_), channel_id=1, source_target_pairs={{0,1},{1,0},{2,3},{3,2},{4,5},{5,4},{6,7},{7,6},{8,9},{9,8},{10,11... | collective-permute-start | bytes 1572872 | tf_op jit(solution)/shard_map/ppermute | solution.py:438
  418.1 84.6 %collective-permute-start.55 = (bf16[128,2048]{1,0:T(8,128)(2,1)S(1)}, bf16[128,2048]{1,0:T(8,128)(2,1)S(1)}, u32[]{:S(2)}, u32[]{:S(2)}) collective-permute-start(bf16[128,2048]{1,0:T(8,128)(2,1)S(1)} %copy-done.57), channel_id=1, source_target_pairs={{0,1},{1,0},{2,3},{3,2},{4,5},{5,4},{6,7},{7,6},{8,9},{9,8},{10,11... | collective-permute-start | bytes 1572872 | tf_op jit(solution)/shard_map/ppermute | solution.py:438
  437.2 65.6 %collective-permute-start.54 = (bf16[128,2048]{1,0:T(8,128)(2,1)S(1)}, bf16[128,2048]{1,0:T(8,128)(2,1)S(1)}, u32[]{:S(2)}, u32[]{:S(2)}) collective-permute-start(bf16[128,2048]{1,0:T(8,128)(2,1)S(1)} %add_convert_fusion.9.refs_15_), channel_id=1, source_target_pairs={{0,4},{2,6},{4,0},{6,2},{8,12},{10,14},{12,8},{14,10},{16,20},{18,... | collective-permute-start | bytes 1572872 | tf_op jit(solution)/shard_map/ppermute | solution.py:430
  467.7 38.5 %collective-permute-start.58 = (bf16[128,2048]{1,0:T(8,128)(2,1)S(1)}, bf16[128,2048]{1,0:T(8,128)(2,1)S(1)}, u32[]{:S(2)}, u32[]{:S(2)}) collective-permute-start(bf16[128,2048]{1,0:T(8,128)(2,1)S(1)} %get-tuple-element.126), channel_id=1, source_target_pairs={{0,4},{2,6},{4,0},{6,2},{8,12},{10,14},{12,8},{14,10},{16,20},{18,... | collective-permute-start | bytes 1572872 | tf_op jit(solution)/shard_map/ppermute | solution.py:430
  468.7 54.8 %collective-permute-start.57 = (bf16[128,2048]{1,0:T(8,128)(2,1)}, bf16[128,2048]{1,0:T(8,128)(2,1)}, u32[]{:S(2)}, u32[]{:S(2)}) collective-permute-start(bf16[128,2048]{1,0:T(8,128)(2,1)} %get-tuple-element.124), channel_id=1, source_target_pairs={{0,4},{2,6},{4,0},{6,2},{8,12},{10,14},{12,8},{14,10},{16,20},{18,... | collective-permute-start | bytes 1572872 | tf_op jit(solution)/shard_map/ppermute | solution.py:430
  521.0 45.4 %collective-permute-start.66 = (bf16[16,288,128]{2,1,0:T(8,128)(2,1)}, bf16[16,288,128]{2,1,0:T(8,128)(2,1)}, u32[]{:S(2)}, u32[]{:S(2)}) collective-permute-start(bf16[16,288,128]{2,1,0:T(8,128)(2,1)} %get-tuple-element.135.refs_1_), channel_id=1, source_target_pairs={{0,2},{2,0},{4,6},{6,4},{8,10},{10,8},{12,14},{14,12},{16,18},{18,... | collective-permute-start | bytes 3538952 | tf_op jit(solution)/shard_map/ppermute | solution.py:434
  624.6 80.5 %collective-permute-start.80 = (bf16[1024,1536]{1,0:T(8,128)(2,1)}, bf16[1024,1536]{1,0:T(8,128)(2,1)}, u32[]{:S(2)}, u32[]{:S(2)}) collective-permute-start(bf16[1024,1536]{1,0:T(8,128)(2,1)} %shard_map.312), channel_id=1, source_target_pairs={{0,2},{2,0},{4,6},{6,4},{8,10},{10,8},{12,14},{14,12},{16,18},{18,... | collective-permute-start | bytes 9437192 | tf_op jit(solution)/shard_map/ppermute | solution.py:434
  650.4 48.9 %collective-permute-start.68 = (bf16[512,2048]{1,0:T(8,128)(2,1)}, bf16[512,2048]{1,0:T(8,128)(2,1)}, u32[]{:S(2)}, u32[]{:S(2)}) collective-permute-start(bf16[512,2048]{1,0:T(8,128)(2,1)} %shard_map.309), channel_id=1, source_target_pairs={{0,1},{1,0},{2,3},{3,2},{4,5},{5,4},{6,7},{7,6},{8,9},{9,8},{10,11... | collective-permute-start | bytes 6291464 | tf_op jit(solution)/shard_map/ppermute | solution.py:438
  675.0 61.2 %collective-permute-start.67 = (bf16[1024,2176]{1,0:T(8,128)(2,1)}, bf16[1024,2176]{1,0:T(8,128)(2,1)}, u32[]{:S(2)}, u32[]{:S(2)}) collective-permute-start(bf16[1024,2176]{1,0:T(8,128)(2,1)} %shard_map.306), channel_id=1, source_target_pairs={{0,2},{2,0},{4,6},{6,4},{8,10},{10,8},{12,14},{14,12},{16,18},{18,... | collective-permute-start | bytes 13369352 | tf_op jit(solution)/shard_map/ppermute | solution.py:434
  675.0 96.8 %collective-permute-start.85 = (bf16[1,2,704,2048]{3,2,1,0:T(8,128)(2,1)}, bf16[1,2,704,2048]{3,2,1,0:T(8,128)(2,1)}, u32[]{:S(2)}, u32[]{:S(2)}) collective-permute-start(bf16[1,2,704,2048]{3,2,1,0:T(8,128)(2,1)} %copy-done.15), channel_id=1, source_target_pairs={{0,2},{2,0},{4,6},{6,4},{8,10},{10,8},{12,14},{14,12},{16,18},{18,... | collective-permute-start | bytes 17301512 | tf_op jit(solution)/shard_map/ppermute | solution.py:434
  675.5 40.3 %collective-permute-start.74 = (bf16[128,2048]{1,0:T(8,128)(2,1)}, bf16[128,2048]{1,0:T(8,128)(2,1)}, u32[]{:S(2)}, u32[]{:S(2)}) collective-permute-start(bf16[128,2048]{1,0:T(8,128)(2,1)} %get-tuple-element.156), channel_id=1, source_target_pairs={{0,1},{1,0},{2,3},{3,2},{4,5},{5,4},{6,7},{7,6},{8,9},{9,8},{10,11... | collective-permute-start | bytes 1572872 | tf_op jit(solution)/shard_map/ppermute | solution.py:438
  702.9 46.5 %collective-permute-start.69 = (bf16[512,2048]{1,0:T(8,128)(2,1)}, bf16[512,2048]{1,0:T(8,128)(2,1)}, u32[]{:S(2)}, u32[]{:S(2)}) collective-permute-start(bf16[512,2048]{1,0:T(8,128)(2,1)} %add_convert_fusion), channel_id=1, source_target_pairs={{0,4},{2,6},{4,0},{6,2},{8,12},{10,14},{12,8},{14,10},{16,20},{18,... | collective-permute-start | bytes 6291464 | tf_op jit(solution)/shard_map/ppermute | solution.py:430
  705.1 49.4 %collective-permute-start.70 = (bf16[512,2048]{1,0:T(8,128)(2,1)}, bf16[512,2048]{1,0:T(8,128)(2,1)}, u32[]{:S(2)}, u32[]{:S(2)}) collective-permute-start(bf16[512,2048]{1,0:T(8,128)(2,1)} %shard_map.310), channel_id=1, source_target_pairs={{0,1},{1,0},{2,3},{3,2},{4,5},{5,4},{6,7},{7,6},{8,9},{9,8},{10,11... | collective-permute-start | bytes 6291464 | tf_op jit(solution)/shard_map/ppermute | solution.py:438
  736.0 108.8 %collective-permute-start.86 = (bf16[1,1,704,2048]{3,2,1,0:T(8,128)(2,1)}, bf16[1,1,704,2048]{3,2,1,0:T(8,128)(2,1)}, u32[]{:S(2)}, u32[]{:S(2)}) collective-permute-start(bf16[1,1,704,2048]{3,2,1,0:T(8,128)(2,1)} %shard_map.298.refs_1_), channel_id=1, source_target_pairs={{0,2},{2,0},{4,6},{6,4},{8,10},{10,8},{12,14},{14,12},{16,18},{18,... | collective-permute-start | bytes 8650760 | tf_op jit(solution)/shard_map/ppermute | solution.py:434
  749.4 49.9 %collective-permute-start.75 = (bf16[512,2176]{1,0:T(8,128)(2,1)}, bf16[512,2176]{1,0:T(8,128)(2,1)S(1)}, u32[]{:S(2)}, u32[]{:S(2)}) collective-permute-start(bf16[512,2176]{1,0:T(8,128)(2,1)} %copy-done.13), channel_id=1, source_target_pairs={{0,4},{2,6},{4,0},{6,2},{8,12},{10,14},{12,8},{14,10},{16,20},{18,... | collective-permute-start | bytes 6684680 | tf_op jit(solution)/shard_map/ppermute | solution.py:430
  (171 other events, 2719.7 us)

commit v9 on v8

--- a/solution.py
+++ b/solution.py
@@ -422,6 +422,14 @@
 RINGS = 4
 
 
+def cost(flops, bytes_accessed, transcendentals):
+    return pl.CostEstimate(
+        flops=flops // 16,
+        bytes_accessed=bytes_accessed // 16,
+        transcendentals=transcendentals // 16,
+    )
+
+
 def ring_step(values):
     return lax.ppermute(values, "dp", [(i, (i + RINGS) % 16) for i in range(16)])
 
@@ -453,19 +461,31 @@
     )(values, *others)
 
 
-def gather_rows(rows, corners, eager=False):
-    planes = []
-    current = rows
-    for distance in range(RINGS):
-        if distance > 1 and eager:
-            current = after(current, *planes[distance - 2][1:3])
-        if distance:
-            current = ring_step(current)
-        beside = other_y(current)
-        across = other_x(current)
-        corner = other_x(beside) if corners[distance] == "x" else other_y(across)
-        planes.append((current, beside, across, corner))
-    return planes
+def gather_whole(rows, early):
+    ring = [rows, ring_step(rows)]
+    ring.append(ring_step(ring[1]))
+    ring.append(ring_step(after(ring[2], early)))
+    over_x = [other_x(part) for part in ring]
+    groups = []
+    for k in (0, 2):
+        held = jnp.concatenate(ring[k : k + 2], axis=0)
+        across = jnp.concatenate(over_x[k : k + 2], axis=0)
+        beside = other_y(held)
+        groups.append((held, beside, across, other_x(beside) if k else other_y(across)))
+    return groups, ring, over_x
+
+
+def gather_rows(rows, corners):
+    held = [rows, ring_step(rows)]
+    first = (other_y(rows), other_x(rows))
+    held.append(ring_step(after(held[1], *first)))
+    held.append(ring_step(held[2]))
+    groups = []
+    for k, current in enumerate((held[0], held[1], jnp.concatenate(held[2:], axis=0))):
+        beside, across = (other_y(current), other_x(current)) if k else first
+        corner = other_x(beside) if corners[k] == "x" else other_y(across)
+        groups.append((current, beside, across, corner))
+    return held, groups
 
 
 def add_low(first, second):
@@ -507,17 +527,20 @@
     return held
 
 
-def gather_weight(held, early):
+def gather_weight(shard, early):
+    held, besides = [shard], []
+    for distance in range(RINGS):
+        beside = other_y(after(held[1], *early) if distance == 1 else held[distance])
+        besides.append(beside)
+        if distance < RINGS - 1:
+            source = after(held[distance], besides[distance - 1]) if distance else shard
+            held.append(ring_step(source))
     chunks = []
-    beside = None
-    for distance, current in enumerate(held):
-        if distance:
-            current_after = after(current, beside, *(early if distance == 2 else ()))
-        beside = other_y(current_after if distance else current)
+    for distance, (current, beside) in enumerate(zip(held, besides)):
         for flip_y, chunk in ((0, current), (1, beside)):
             for flip_core, piece in ((0, chunk), (1, other_core(chunk))):
                 chunks.append(((distance, flip_y, flip_core), piece))
-    return chunks
+    return chunks, held, besides
 
 
 def place_of(coords, key):
@@ -795,7 +818,7 @@
             pltpu.SemaphoreType.DMA((len(chunks) * (2 + depth // latent_depth),))
         ],
         compiler_params=pltpu.CompilerParams(vmem_limit_bytes=48 * 1024 * 1024),
-        cost_estimate=pl.CostEstimate(
+        cost_estimate=cost(
             flops=2 * tokens * D * (first_width + heads * VD + 1024),
             bytes_accessed=4 * D * (first_width + 1536),
             transcendentals=2 * heads * tokens * tokens,
@@ -942,7 +965,7 @@
             pltpu.VMEM((tokens, 2 * span), f32),
         ],
         compiler_params=pltpu.CompilerParams(vmem_limit_bytes=48 * 1024 * 1024),
-        cost_estimate=pl.CostEstimate(
+        cost_estimate=cost(
             flops=2 * tokens * D * 3000,
             bytes_accessed=2 * D * 1536,
             transcendentals=heads * tokens * tokens,
@@ -1019,7 +1042,7 @@
         ),
         out_shape=jax.ShapeDtypeStruct((count * size, width), jnp.bfloat16),
         compiler_params=pltpu.CompilerParams(vmem_limit_bytes=32 * 1024 * 1024),
-        cost_estimate=pl.CostEstimate(
+        cost_estimate=cost(
             flops=1024 * count * size * width,
             bytes_accessed=4 * count * size * width,
             transcendentals=0,
@@ -1102,7 +1125,7 @@
         in_specs=[pl.BlockSpec(memory_space=pltpu.SMEM)] + in_vmem(4),
         out_specs=in_vmem(3),
         compiler_params=pltpu.CompilerParams(vmem_limit_bytes=32 * 1024 * 1024),
-        cost_estimate=pl.CostEstimate(
+        cost_estimate=cost(
             flops=4 * own.shape[0] * weight.shape[0] * weight.shape[1],
             bytes_accessed=2 * weight.shape[0] * weight.shape[1],
             transcendentals=0,
@@ -1157,11 +1180,13 @@
     )(query, latent, small, keyval, output)
 
 
-def load_pieces(pieces, target, semaphores):
-    size = pieces[0].shape[0]
+def load_pieces(pieces, starts, target, semaphores):
+    size = target.shape[0] // len(pieces)
     copies = [
-        pltpu.make_async_copy(piece, target.at[pl.ds(k * size, size)], semaphores.at[k])
-        for k, piece in enumerate(pieces)
+        pltpu.make_async_copy(
+            piece.at[pl.ds(start, size)], target.at[pl.ds(k * size, size)], semaphores.at[k]
+        )
+        for k, (piece, start) in enumerate(zip(pieces, starts))
     ]
     for copy in copies:
         copy.start()
@@ -1261,7 +1286,7 @@
         out_specs=[pl.BlockSpec((height, columns), lambda i: (0, i))] * 3,
         out_shape=[jax.ShapeDtypeStruct((height, depth), jnp.bfloat16)] * 3,
         compiler_params=pltpu.CompilerParams(vmem_limit_bytes=32 * 1024 * 1024),
-        cost_estimate=pl.CostEstimate(
+        cost_estimate=cost(
             flops=0, bytes_accessed=12 * height * depth, transcendentals=0
         ),
     )(own_in, other_in, own_down, other_down, near, far, *others)
@@ -1295,7 +1320,7 @@
         out_specs=out,
         out_shape=jax.ShapeDtypeStruct((1, len(lefts), units, depth), kind),
         compiler_params=pltpu.CompilerParams(vmem_limit_bytes=48 * 1024 * 1024),
-        cost_estimate=pl.CostEstimate(
+        cost_estimate=cost(
             flops=2 * len(lefts) * total * depth * wide,
             bytes_accessed=2 * len(lefts) * total * (depth + wide) + 8 * depth * units,
             transcendentals=0,
@@ -1339,7 +1364,7 @@
             jax.ShapeDtypeStruct((logits.shape[1], depth), jnp.float32),
         ],
         compiler_params=pltpu.CompilerParams(vmem_limit_bytes=48 * 1024 * 1024),
-        cost_estimate=pl.CostEstimate(
+        cost_estimate=cost(
             flops=8 * total * depth * TILE,
             bytes_accessed=4 * total * depth,
             transcendentals=0,
@@ -1347,13 +1372,14 @@
     )(rows, cots, gate, up, hidden, logits)
 
 
-def down_kernel(count, *refs):
+def down_kernel(starts, *refs):
+    count = len(starts)
     pieces, weight_ref = refs[:count], refs[count]
     grads_ref, rows_ref, semaphores = refs[-3:]
 
     @pl.when(pl.program_id(0) == 0)
     def _():
-        load_pieces(pieces, rows_ref, semaphores)
+        load_pieces(pieces, starts, rows_ref, semaphores)
 
     size = rows_ref.shape[0] // 2
     for k in range(2):
@@ -1361,13 +1387,13 @@
         grads_ref[part, :] = dot_turned(rows_ref[part, :], weight_ref[...]).astype(jnp.bfloat16)
 
 
-def down_grads(part, pieces, down, kept, others):
+def down_grads(part, pieces, size, down, kept, others):
     count = len(pieces)
-    size, depth = pieces[0].shape
+    depth = down.shape[1]
     width = down.shape[0]
     rows = count * size
     return pl.pallas_call(
-        functools.partial(down_kernel, count),
+        functools.partial(down_kernel, tuple(start for _, start in pieces)),
         grid=(width // TILE,),
         in_specs=in_place(count)
         + [pl.BlockSpec((TILE, depth), lambda i: (i, 0))]
@@ -1383,12 +1409,12 @@
         scratch_shapes=[pltpu.SemaphoreType.DMA((count,))],
         input_output_aliases={count + 1 + k: k for k in range(len(kept))},
         compiler_params=pltpu.CompilerParams(vmem_limit_bytes=48 * 1024 * 1024),
-        cost_estimate=pl.CostEstimate(
+        cost_estimate=cost(
             flops=2 * rows * depth * width,
             bytes_accessed=2 * (2 * rows * depth + depth * width + rows * width),
             transcendentals=0,
         ),
-    )(*pieces, down, *kept, *others)
+    )(*[array for array, _ in pieces], down, *kept, *others)
 
 
 def out_kernel(pieces, *refs):
@@ -1412,7 +1438,7 @@
         out_specs=[pl.BlockSpec((rows // pieces, TILE), lambda i: (0, i))] * pieces,
         out_shape=[jax.ShapeDtypeStruct((rows // pieces, depth), jnp.bfloat16)] * pieces,
         compiler_params=pltpu.CompilerParams(vmem_limit_bytes=48 * 1024 * 1024),
-        cost_estimate=pl.CostEstimate(
+        cost_estimate=cost(
             flops=2 * rows * depth * width,
             bytes_accessed=2 * (rows * depth + depth * width + rows * width),
             transcendentals=0,
@@ -1420,7 +1446,8 @@
     )(hidden, down)
 
 
-def mlp_kernel(tiles, pieces, others, experts_ref, routed_ref, *refs):
+def mlp_kernel(tiles, starts, others, experts_ref, routed_ref, *refs):
+    pieces = len(starts)
     row_refs = refs[:pieces]
     router_ref, gate_col, up_col, down_grad, gate_row, up_row = refs[pieces : pieces + 6]
     outs = refs[pieces + 6 + others :]
@@ -1435,7 +1462,7 @@
 
     @pl.when(step == 0)
     def _():
-        load_pieces(row_refs, rows_out, semaphores)
+        load_pieces(row_refs, starts, rows_out, semaphores)
         logits = wide_dot(rows_out[...], router_ref[...])
         logits = jnp.where((lane >= 0) & (lane < experts_ref[2]), logits, -1e30)
         raised = jnp.exp(logits - jnp.max(logits, axis=1, keepdims=True))
@@ -1494,8 +1521,8 @@
 def mlp_plane(distance, experts, routed, rows, down_grad, router, weights, kept, others):
     gate, up = weights
     pieces = len(rows)
-    size, depth = rows[0].shape
-    width = gate.shape[0]
+    width, depth = gate.shape
+    size = routed.shape[0] // pieces
     tiles, columns = width // TILE, depth // (2 * TILE)
     total = pieces * size
     low = jnp.bfloat16
@@ -1510,7 +1537,9 @@
     anywhere = pl.BlockSpec(memory_space=pl.ANY)
     first_kept = 2 + pieces + 6
     results = pl.pallas_call(
-        functools.partial(mlp_kernel, tiles, pieces, len(kept) + len(others)),
+        functools.partial(
+            mlp_kernel, tiles, tuple(start for _, start in rows), len(kept) + len(others)
+        ),
         grid=(tiles + columns,),
         in_specs=[pl.BlockSpec(memory_space=pltpu.SMEM), whole(routed)]
         + [anywhere] * pieces
@@ -1545,12 +1574,12 @@
         ],
         input_output_aliases={first_kept + k: pieces + k for k in range(len(kept))},
         compiler_params=pltpu.CompilerParams(vmem_limit_bytes=48 * 1024 * 1024),
-        cost_estimate=pl.CostEstimate(
+        cost_estimate=cost(
             flops=2 * total * depth * width * 4,
             bytes_accessed=2 * (4 * depth * width + 3 * total * depth + 4 * total * width),
             transcendentals=total * width,
         ),
-    )(experts, routed, *rows, router, gate, up, down_grad, gate, up, *kept, *others)
+    )(experts, routed, *[array for array, _ in rows], router, gate, up, down_grad, gate, up, *kept, *others)
     return results[:pieces], results[pieces:]
 
 
@@ -1605,22 +1634,16 @@
     )
     first_width = query_width + KVR + 128
     shards = pack_weights(w_query, w_latent, small, w_keyval, w_output)
-    held = ring_shards(shards)
     other_input = other_x(block_input)
     expert_in = expert_gate_up.swapaxes(2, 3)
     expert_in_other = other_core(expert_in)
     expert_down_other = other_core(expert_down)
-    shared_near = lax.all_to_all(
-        pack_shared(shared_gate_up, shared_down, blocks, ()),
-        "dp",
-        split_axis=0,
-        concat_axis=0,
-        tiled=True,
-    )
-    shared_far = other_core(shared_near)
-
-    chunks = gather_weight(held, (shared_near,))
-    grad_planes = gather_rows(after(cotangent, held[3]), "xyxy")
+    chunks, held, besides = gather_weight(
+        shards, (expert_in_other, expert_down_other, other_input)
+    )
+    grad_groups, grad_ring, grad_across = gather_whole(
+        after(cotangent, held[3], besides[2]), besides[3]
+    )
 
     cosine, sine = rotary_tables(segments[0], ROPE)
     cosine = jnp.tile(cosine, (1, heads))
@@ -1652,13 +1675,7 @@
         chunks,
         heads,
         sizes,
-        (
-            grad_planes[3][0],
-            grad_planes[0][1],
-            grad_planes[0][2],
-            grad_planes[1][2],
-            grad_planes[2][2],
-        ),
+        (grad_ring[3], grad_across[2], grad_groups[0][1]),
     )
     attn_gain_wide, ffn_gain_wide = gains[0], gains[1]
     mixed = block_input.astype(f32) + own_part + other_x(sent_part).astype(f32)
@@ -1688,7 +1705,22 @@
     )
 
     corners = "yxyx"
-    row_planes = gather_rows(second_normed, corners, True)
+    row_ring, row_groups = gather_rows(second_normed, "yyx")
+    row_planes = [
+        [(array, 0) for array in row_groups[0]],
+        [(array, 0) for array in row_groups[1]],
+        [(array, 0) for array in row_groups[2]],
+        [(array, local_rows) for array in row_groups[2]],
+    ]
+
+    shared_near = lax.all_to_all(
+        after(pack_shared(shared_gate_up, shared_down, blocks, (held[1],)), sent_part),
+        "dp",
+        split_axis=0,
+        concat_axis=0,
+        tiled=True,
+    )
+    shared_far = other_core(shared_near)
 
     gate_weight, up_weight, down_weight = pack_units(
         expert_in,
@@ -1702,17 +1734,19 @@
     )
     half_kept = down_grads(
         0,
-        [piece for plane in grad_planes[:2] for piece in plane],
+        [(array, r * local_rows) for r in (0, 1) for array in grad_groups[0]],
+        local_rows,
         down_weight,
         (),
-        (row_planes[1][0],),
+        (row_ring[1],),
     )
     down_grad, every_grad = down_grads(
         1,
-        [piece for plane in grad_planes[2:] for piece in plane],
+        [(array, r * local_rows) for r in (0, 1) for array in grad_groups[1]],
+        local_rows,
         down_weight,
         half_kept,
-        (row_planes[2][0],),
+        (row_ring[2],),
     )
     expert_ids = jnp.concatenate(
         [chip_experts, jnp.array([experts, used + 3 - query_width - KVR], jnp.int32)]
@@ -1720,9 +1754,9 @@
     kept = []
     turned, closed = [], []
     for distance in range(RINGS):
-        others = [row_planes[3][0]] if distance == 0 else [row_planes[2][3]]
+        others = [row_ring[3]] if distance == 0 else list(row_groups[2][1:3])
         if distance == 2:
-            others = list(turned[0][1:]) + [row_planes[3][3]]
+            others = list(turned[0][1:])
         elif distance == 3:
             others = list(turned[1][1:]) + list(closed[0][1:])
         grads, kept = mlp_plane(
@@ -1750,7 +1784,7 @@
         shared,
         blocks,
     )
-    sent_in = expert_grads((every_gate_grad, every_up_grad), every_row, units, 1, None, bf16)
+    outs = list(out_rows(4, every_hidden, down_weight))
     sent_down = expert_grads((every_hidden,), every_grad, units, 1, None, bf16)
     moving = ring_step(wide_sum(*closed[1]).astype(bf16))
     moving = ring_step(wide_sum(moving, *closed[2]).astype(bf16))
@@ -1759,10 +1793,9 @@
     grad_close = close_plane((own, after(beside, shared_sent), across))
     grad_second = wide_sum(
         ring_step(wide_sum(moving, *grad_close).astype(bf16)),
-        after(closed[0][0], sent_in),
+        after(closed[0][0], outs[0]),
         *closed[0][1:],
     )
-    arrived_in = other_core(sent_in)
     arrived_down = other_core(sent_down)
     router_at = used + 3 - query_width - KVR
     grad_router = logit_rows[router_at : router_at + experts]
@@ -1776,7 +1809,6 @@
     )
     grad_mixed_low = grad_mixed.astype(bf16)
     other_grad = other_x(grad_mixed_low)
-    outs = list(out_rows(4, every_hidden, down_weight))
     outs[3] = after(outs[3], grad_close[2])
     outs[2] = after(outs[2], other_grad)
     out_own, out_beside, out_across = close_plane(turn_corner(outs, "x"))
@@ -1793,7 +1825,7 @@
         (keyval_weight, output_turned, nope, turned_query, latent, key, keyval, total, latent_gain_row),
         heads,
         first_width,
-        (shared_grads,),
+        (shared_grads, arrived_down),
     )
     grad_attn = jnp.concatenate(
         [
@@ -1828,6 +1860,9 @@
     other_kept = other_grads(*other_parts, 0, 8, other_arrived)
     far = first_grads(*first_parts, 4, 4, first_arrived)
     from_y = other_y(far)
+    arrived_in = other_core(
+        expert_grads((every_gate_grad, every_up_grad), every_row, units, 1, None, bf16, (far,))
+    )
     out_total = wide_sum(after(out_own, far), out_beside, out_across)
     block_output = mixed + ring_sum(
         [out_total[r * local_rows : (r + 1) * local_rows] for r in range(RINGS)], bf16
@@ -1840,10 +1875,10 @@
     grad_expert_down = expert_grads(
         (every_hidden,), every_grad, units, 0, arrived_down, f32, (from_y,)
     )
-    first_closed = close_ring(near, from_y)
     grad_expert_in = expert_grads(
         (every_gate_grad, every_up_grad), every_row, units, 0, arrived_in, f32, (near,)
     )
+    first_closed = close_ring(after(near, grad_expert_in), from_y)
     grad_shared_in, grad_shared_down = unpack_shared(shared_grads, shared, (from_y,))
     grad_expert_gate_up = grad_expert_in.swapaxes(2, 3)
     grad_expert_down = grad_expert_down[0]

time: 889 us -> 924 us (1.039)
  starting transfers between devices: 129 us -> 96 us
  waiting for transfers between devices: 281 us -> 314 us
  local copies, waits for them, and re-layouts: 85 us -> 104 us
  other arithmetic: 42.7 us -> 58.9 us
    ppermute x25 -> x22, waiting for transfers between devices: 89.9 us -> 123 us  [other_x(): return lax.ppermute(values, 'tensor', [(0, 1), (1, 0)])]
    ppermute x21, starting transfers between devices: 54.3 us -> 34.5 us  [ring_step(): lax.ppermute(values, 'dp', [(i, (i + RINGS) % 16) for i in range(16)])]
    ppermute x21, waiting for transfers between devices: 123 us -> 140 us  [ring_step(): lax.ppermute(values, 'dp', [(i, (i + RINGS) % 16) for i in range(16)])]
    ppermute x25 -> x21, waiting for transfers between devices: 62 us -> 51.1 us  [other_y(): return lax.ppermute(values, 'dp', [(i, i ^ 2) for i in range(16)])]
    ppermute x25 -> x21, starting transfers between devices: 32.2 us -> 24.4 us  [other_y(): return lax.ppermute(values, 'dp', [(i, i ^ 2) for i in range(16)])]
    unnamed x245 -> x253, local copies, waits for them, and re-layouts: 65.8 us -> 70.8 us
    ppermute x25 -> x22, starting transfers between devices: 28.2 us -> 24.2 us  [other_x(): return lax.ppermute(values, 'tensor', [(0, 1), (1, 0)])]
  transfers between devices with their start and end apart: 89 -> 82, of which waited for: 29 -> 25; matrix products, arithmetic and copies ran while one was open for 8% -> 12% of each run, Pallas kernels for 36% -> 28%
where the time goes in v9:
time: 924 us; the launch traced here: 910 us
  Pallas kernels  333 us (36%)
  waiting for transfers between devices  314 us (34%)
  local copies, waits for them, and re-layouts  104 us (11%)
  starting transfers between devices  96 us (10%)
  other arithmetic  58.9 us (6%)
    ppermute x21, waiting for transfers between devices, ring_step(): lax.ppermute(values, 'dp', [(i, (i + RINGS) % 16) for i in range(16)])  140 us
    ppermute x22, waiting for transfers between devices, other_x(): return lax.ppermute(values, 'tensor', [(0, 1), (1, 0)])  123 us
    pallas_call x4, Pallas kernels, mlp_plane(): pl.pallas_call(functools.partial(mlp_kernel, tiles, tuple((start for _, s...  119 us
    unnamed x253, local copies, waits for them, and re-layouts  70.8 us
    pallas_call x4, Pallas kernels, expert_grads(): pl.pallas_call(functools.partial(expert_grads_kernel, units, len(lefts),...  63.4 us
    ppermute x21, waiting for transfers between devices, other_y(): return lax.ppermute(values, 'dp', [(i, i ^ 2) for i in range(16)])  51.1 us
    ppermute x21, starting transfers between devices, ring_step(): lax.ppermute(values, 'dp', [(i, (i + RINGS) % 16) for i in range(16)])  34.5 us
    pallas_call x2, Pallas kernels, down_grads(): pl.pallas_call(functools.partial(down_kernel, tuple((start for _, start i...  27.8 us
  transfers between devices with their start and end apart: 82, of which 25 were waited for; matrix products, arithmetic and copies ran while one was open for 12% of the time, Pallas kernels for 28%

profile of v9, /device:TPU:0, one launch (start us, length us, event | category | flops | bytes accessed | tf_op | source)
XLA Modules:
  0.0 909.6 jit_solution(11123686808277492189)
XLA Ops:
  16.5 20.5 %collective-permute-done.4.refs_4_.refs_0_ = bf16[128,3712]{1,0:T(8,128)(2,1)S(1)} collective-permute-done((bf16[128,3712]{1,0:T(8,128)(2,1)}, bf16[128,3712]{1,0:T(8,128)(2,1)S(1)}, u32[]{:S(2)}, u32[]{:S(2)}) %collective-permute-start.4) | collective-permute-done | bytes 950304 | tf_op jit(solution)/shard_map/ppermute | solution.py:434
  42.2 21.3 %collective-permute-done.10.refs_8_ = bf16[128,3712]{1,0:T(8,128)(2,1)} collective-permute-done((bf16[128,3712]{1,0:T(8,128)(2,1)}, bf16[128,3712]{1,0:T(8,128)(2,1)}, u32[]{:S(2)}, u32[]{:S(2)}) %collective-permute-start.10) | collective-permute-done | bytes 950304 | tf_op jit(solution)/shard_map/ppermute | solution.py:434
  69.9 17.6 %collective-permute-done.12.refs_2_.refs_10_ = bf16[128,3712]{1,0:T(8,128)(2,1)S(1)} collective-permute-done((bf16[128,3712]{1,0:T(8,128)(2,1)}, bf16[128,3712]{1,0:T(8,128)(2,1)S(1)}, u32[]{:S(2)}, u32[]{:S(2)}) %collective-permute-start.12) | collective-permute-done | bytes 950304 | tf_op jit(solution)/shard_map/ppermute | solution.py:438
  91.7 12.5 %collective-permute-done.18 = bf16[128,2048]{1,0:T(8,128)(2,1)} collective-permute-done((bf16[128,2048]{1,0:T(8,128)(2,1)}, bf16[128,2048]{1,0:T(8,128)(2,1)}, u32[]{:S(2)}, u32[]{:S(2)}) %collective-permute-start.18) | collective-permute-done | bytes 524320 | tf_op jit(solution)/shard_map/ppermute | solution.py:434
  105.8 10.6 %collective-permute-done.19.refs_0_ = bf16[128,2048]{1,0:T(8,128)(2,1)S(1)} collective-permute-done((bf16[128,2048]{1,0:T(8,128)(2,1)}, bf16[128,2048]{1,0:T(8,128)(2,1)S(1)}, u32[]{:S(2)}, u32[]{:S(2)}) %collective-permute-start.19) | collective-permute-done | bytes 524320 | tf_op jit(solution)/shard_map/ppermute | solution.py:434
  119.8 8.8 collective-permute-done.16.refs_1_.refs_14_
  137.5 12.9 %collective-permute-done.22.refs_18_.refs_1_.refs_5_ = bf16[256,2048]{1,0:T(8,128)(2,1)S(1)} collective-permute-done((bf16[256,2048]{1,0:T(8,128)(2,1)S(1)}, bf16[256,2048]{1,0:T(8,128)(2,1)S(1)}, u32[]{:S(2)}, u32[]{:S(2)}) %collective-permute-start.22) | collective-permute-done | bytes 1048608 | tf_op jit(solution)/shard_map/ppermute | solution.py:438
  153.4 22.2 %shard_map.287 = (f32[128,2048]{1,0:T(8,128)}, bf16[128,2048]{1,0:T(8,128)(2,1)S(1)}, bf16[2048,2176]{1,0:T(8,128)(2,1)}, bf16[512,2048]{1,0:T(8,128)(2,1)}, bf1...) custom-call(s32[5]{0:T(128)S(1)} %concatenate.39.place_ref.refs_0_, ...), custom_call_target="tpu_custom_call" | custom-call | flops 276824064 | bytes 1900544 | tf_op jit(solution)/shard_map/pallas_call | solution.py:810
  201.9 22.3 %collective-permute-done.24.refs_9_.refs_0_ = bf16[128,2048]{1,0:T(8,128)(2,1)} collective-permute-done((bf16[128,2048]{1,0:T(8,128)(2,1)S(1)}, bf16[128,2048]{1,0:T(8,128)(2,1)}, u32[]{:S(2)}, u32[]{:S(2)}) %collective-permute-start.24) | collective-permute-done | bytes 524320 | tf_op jit(solution)/shard_map/ppermute | solution.py:434
  261.2 11.8 %collective-permute-done.38.refs_3_.refs_7_ = bf16[256,2048]{1,0:T(8,128)(2,1)} collective-permute-done((bf16[256,2048]{1,0:T(8,128)(2,1)}, bf16[256,2048]{1,0:T(8,128)(2,1)}, u32[]{:S(2)}, u32[]{:S(2)}) %collective-permute-start.38) | collective-permute-done | bytes 1048608 | tf_op jit(solution)/shard_map/ppermute | solution.py:438
  280.5 21.4 %collective-permute-done.40.refs_2_ = bf16[128,2048]{1,0:T(8,128)(2,1)} collective-permute-done((bf16[128,2048]{1,0:T(8,128)(2,1)}, bf16[128,2048]{1,0:T(8,128)(2,1)}, u32[]{:S(2)}, u32[]{:S(2)}) %collective-permute-start.40) | collective-permute-done | bytes 524320 | tf_op jit(solution)/shard_map/ppermute | solution.py:446
  314.0 12.9 %shard_map.291 = (bf16[1792,2048]{1,0:T(8,128)(2,1)}, bf16[1792,2048]{1,0:T(8,128)(2,1)}, bf16[1792,2048]{1,0:T(8,128)(2,1)}) custom-call(bf16[1,2,704,2048]{3,2,1,0:T(8,128)(2,1)S(1)} %bitcast.77, bf16[1,2,704,2048]{3,2,1,0:T(8,128)(2,1)} %collective-permute-done.6.refs_1_.other_in, bf16[1,704,2048]{2,1,0:T(8,128)(2,1)S(1)} %copy-done.41, ...), custom_call_target="tpu_custom_call" | custom-call | bytes 2752512 | tf_op jit(solution)/shard_map/pallas_call | solution.py:1281
  326.9 14.4 %shard_map.292 = (bf16[2048,1792]{1,0:T(8,128)(2,1)}, bf16[2048,2048]{1,0:T(8,128)(2,1)}) custom-call(bf16[256,2048]{1,0:T(8,128)(2,1)S(1)} %copy-done.13, bf16[256,2048]{1,0:T(8,128)(2,1)S(1)} %copy-done.11, bf16[256,2048]{1,0:T(8,128)(2,1)} %constant_dynamic-update-slice_fusion.6.refs_2_.refs_6_, ...), custom_call_target="tpu_custom_call" | custom-call | flops 469762048 | bytes 1212416 | tf_op jit(solution)/shard_map/pallas_call | solution.py:1395
  341.3 13.4 %shard_map.293 = (bf16[2048,1792]{1,0:T(8,128)(2,1)}, bf16[2048,2048]{1,0:T(8,128)(2,1)}) custom-call(bf16[256,2048]{1,0:T(8,128)(2,1)S(1)} %copy-done.21, bf16[256,2048]{1,0:T(8,128)(2,1)} %collective-permute-done.33.refs_1_.refs_5_, bf16[256,2048]{1,0:T(8,128)(2,1)S(1)} %pad_maximum_fusion.1.refs_2_.refs_6_, ...), custom_call_target="tpu_custom_call", output_to_operand_aliasing={{0}: (9, {}), {1}: (10, {})} | custom-call | flops 469762048 | bytes 1212416 | tf_op jit(solution)/shard_map/pallas_call | solution.py:1395
  354.8 29.3 %shard_map.294 = (bf16[128,2048]{1,0:T(8,128)(2,1)S(1)}, bf16[128,2048]{1,0:T(8,128)(2,1)S(1)}, bf16[128,2048]{1,0:T(8,128)(2,1)S(1)}, bf16[128,2048]{1,0:T(8,12...) custom-call(s32[4]{0:T(128)S(1)} %pad_add_fusion.experts_ref, ...), custom_call_target="tpu_custom_call" | custom-call | flops 939524096 | bytes 2686976 | tf_op jit(solution)/shard_map/pallas_call | solution.py:1539
  386.6 30.1 %shard_map.295 = (bf16[128,2048]{1,0:T(8,128)(2,1)S(1)}, bf16[128,2048]{1,0:T(8,128)(2,1)S(1)}, bf16[128,2048]{1,0:T(8,128)(2,1)S(1)}, bf16[128,2048]{1,0:T(8,12...) custom-call(s32[4]{0:T(128)S(1)} %pad_add_fusion.experts_ref, ...), custom_call_target="tpu_custom_call", output_to_operand_aliasing={{4}: (12, {}), {5}: (13, {}), {6}: (14, {}), {7}: (15, {}),... | custom-call | flops 939524096 | bytes 2686976 | tf_op jit(solution)/shard_map/pallas_call | solution.py:1539
  439.9 16.9 %collective-permute-done.31.refs_3_ = bf16[256,2048]{1,0:T(8,128)(2,1)} collective-permute-done((bf16[256,2048]{1,0:T(8,128)(2,1)S(1)}, bf16[256,2048]{1,0:T(8,128)(2,1)}, u32[]{:S(2)}, u32[]{:S(2)}) %collective-permute-start.31) | collective-permute-done | bytes 1048608 | tf_op jit(solution)/shard_map/ppermute | solution.py:446
  456.8 29.5 %shard_map.296 = (bf16[128,2048]{1,0:T(8,128)(2,1)S(1)}, bf16[128,2048]{1,0:T(8,128)(2,1)}, bf16[128,2048]{1,0:T(8,128)(2,1)S(1)}, bf16[128,2048]{1,0:T(8,128)(2...) custom-call(s32[4]{0:T(128)S(1)} %pad_add_fusion.experts_ref, ...), custom_call_target="tpu_custom_call", output_to_operand_aliasing={{4}: (12, {}), {5}: (13, {}), {6}: (14, {}), {7}: (15, {}),... | custom-call | flops 939524096 | bytes 2686976 | tf_op jit(solution)/shard_map/pallas_call | solution.py:1539
  492.0 29.8 %shard_map.297 = (bf16[128,2048]{1,0:T(8,128)(2,1)S(1)}, bf16[128,2048]{1,0:T(8,128)(2,1)S(1)}, bf16[128,2048]{1,0:T(8,128)(2,1)}, bf16[128,2048]{1,0:T(8,128)(2...) custom-call(s32[4]{0:T(128)S(1)} %pad_add_fusion.experts_ref, ...), custom_call_target="tpu_custom_call", output_to_operand_aliasing={{4}: (12, {}), {5}: (13, {}), {6}: (14, {}), {7}: (15, {}),... | custom-call | flops 939524096 | bytes 2686976 | tf_op jit(solution)/shard_map/pallas_call | solution.py:1539
  524.9 12.4 %shard_map.301 = (f32[16,288,128]{2,1,0:T(8,128)S(1)}, bf16[16,288,128]{2,1,0:T(8,128)(2,1)}, f32[128,2048]{1,0:T(8,128)S(1)}) custom-call(bf16[2048,2048]{1,0:T(8,128)(2,1)} %get-tuple-element.131.rows_ref.right_ref, bf16[2048,2048]{1,0:T(8,128)(2,1)} %get-tuple-element.128.right_ref.cots_ref, bf16[2048,1792]{1,0:T(8,128)(2,1)} %get-tuple-element.132.gate_ref.refs_0_, ...), custom_call_target="tpu_custom_call" | custom-call | flops 536870912 | bytes 1048576 | tf_op jit(solution)/shard_map/pallas_call | solution.py:1356
  545.2 11.2 %shard_map.299.refs_1_ = bf16[1,1,704,2048]{3,2,1,0:T(8,128)(2,1)} custom-call(bf16[2048,2048]{1,0:T(8,128)(2,1)} %get-tuple-element.128.right_ref.cots_ref, bf16[2048,1792]{1,0:T(8,128)(2,1)} %get-tuple-element.119.refs_0_.hidden_ref), custom_call_target="tpu_custom_call" | custom-call | flops 402653184 | bytes 1441792 | tf_op jit(solution)/shard_map/pallas_call | solution.py:1313
  569.1 21.2 %shard_map.298 = (bf16[512,2048]{1,0:T(8,128)(2,1)S(1)}, bf16[512,2048]{1,0:T(8,128)(2,1)S(1)}, bf16[512,2048]{1,0:T(8,128)(2,1)}, bf16[512,2048]{1,0:T(8,128)(2,1)}) custom-call(bf16[2048,1792]{1,0:T(8,128)(2,1)} %get-tuple-element.119.refs_0_.hidden_ref, bf16[1792,2048]{1,0:T(8,128)(2,1)} %get-tuple-element.94.refs_8_.refs_1_), custom_call_target="tpu_custom_call" | custom-call | flops 939524096 | bytes 1441792 | tf_op jit(solution)/shard_map/pallas_call | solution.py:1434
  593.0 7.2 collective-permute-done.57
  607.7 11.0 %collective-permute-done.58.refs_6_.refs_1_ = bf16[128,2048]{1,0:T(8,128)(2,1)S(1)} collective-permute-done((bf16[128,2048]{1,0:T(8,128)(2,1)S(1)}, bf16[128,2048]{1,0:T(8,128)(2,1)S(1)}, u32[]{:S(2)}, u32[]{:S(2)}) %collective-permute-start.58) | collective-permute-done | bytes 524320 | tf_op jit(solution)/shard_map/ppermute | solution.py:446
  625.0 13.2 %shard_map.304 = (bf16[256,2176]{1,0:T(8,128)(2,1)}, bf16[256,2048]{1,0:T(8,128)(2,1)S(1)}, bf16[256,512]{1,0:T(8,128)(2,1)S(1)}, f32[1,512]{1,0:T(1,128)S(1)}) custom-call(s32[5]{0:T(128)S(1)} %concatenate.39.place_ref.refs_0_, s32[1,256]{1,0:T(1,128)S(1)} %copy-done.86, s32[256,1]{1,0:T(8,128)S(1)} %copy.128.segment_column_ref.refs_2_, ...), custom_call_target="tpu_custom_call" | custom-call | flops 196608000 | bytes 393216 | tf_op jit(solution)/shard_map/pallas_call | solution.py:952
  683.0 19.4 %shard_map.312 = bf16[1,2,704,2048]{3,2,1,0:T(8,128)(2,1)} custom-call(bf16[2048,2048]{1,0:T(8,128)(2,1)} %get-tuple-element.131.rows_ref.right_ref, bf16[2048,1792]{1,0:T(8,128)(2,1)} %get-tuple-element.132.gate_ref.refs_0_, bf16[2048,1792]{1,0:T(8,128)(2,1)} %get-tuple-element.133.up_ref.refs_1_, bf16[512,2176]{1,0:T(8,128)(2,1)} %shard_map.307.refs_1_.refs_2_), custom_call_target="tpu_custom_call" | custom-call | flops 805306368 | bytes 2162688 | tf_op jit(solution)/shard_map/pallas_call | solution.py:1313
  703.6 21.1 %collective-permute-done.62 = bf16[512,2048]{1,0:T(8,128)(2,1)} collective-permute-done((bf16[512,2048]{1,0:T(8,128)(2,1)}, bf16[512,2048]{1,0:T(8,128)(2,1)}, u32[]{:S(2)}, u32[]{:S(2)}) %collective-permute-start.62) | collective-permute-done | bytes 2097184 | tf_op jit(solution)/shard_map/ppermute | solution.py:446
  742.7 37.2 %collective-permute-done.68 = bf16[128,2048]{1,0:T(8,128)(2,1)S(1)} collective-permute-done((bf16[128,2048]{1,0:T(8,128)(2,1)S(1)}, bf16[128,2048]{1,0:T(8,128)(2,1)S(1)}, u32[]{:S(2)}, u32[]{:S(2)}) %collective-permute-start.68) | collective-permute-done | bytes 524320 | tf_op jit(solution)/shard_map/ppermute | solution.py:446
  817.4 21.1 %shard_map.313.refs_1_ = f32[1,2,704,2048]{3,2,1,0:T(8,128)} custom-call(bf16[2048,2048]{1,0:T(8,128)(2,1)} %get-tuple-element.131.rows_ref.right_ref, bf16[2048,1792]{1,0:T(8,128)(2,1)} %get-tuple-element.132.gate_ref.refs_0_, bf16[2048,1792]{1,0:T(8,128)(2,1)} %get-tuple-element.133.up_ref.refs_1_, ...), custom_call_target="tpu_custom_call" | custom-call | flops 805306368 | bytes 2162688 | tf_op jit(solution)/shard_map/pallas_call | solution.py:1313
  849.8 8.7 collective-permute-done.71
  861.7 15.4 %collective-permute-done.72 = bf16[128,2176]{1,0:T(8,128)(2,1)S(1)} collective-permute-done((bf16[128,2176]{1,0:T(8,128)(2,1)S(1)}, bf16[128,2176]{1,0:T(8,128)(2,1)S(1)}, u32[]{:S(2)}, u32[]{:S(2)}) %collective-permute-start.72) | collective-permute-done | bytes 557088 | tf_op jit(solution)/shard_map/ppermute | solution.py:434
  885.2 11.7 %shard_map.318 = f32[1,1,704,2048]{3,2,1,0:T(8,128)} custom-call(bf16[2048,2048]{1,0:T(8,128)(2,1)} %get-tuple-element.128.right_ref.cots_ref, bf16[2048,1792]{1,0:T(8,128)(2,1)} %get-tuple-element.119.refs_0_.hidden_ref, bf16[1,1,704,2048]{3,2,1,0:T(8,128)(2,1)} %collective-permute-done.60.refs_17_.refs_1_, ...), custom_call_target="tpu_custom_call" | custom-call | flops 402653184 | bytes 1441792 | tf_op jit(solution)/shard_map/pallas_call | solution.py:1313
  (527 shorter events, 337.7 us)
Async XLA Ops:
  0.7 39.2 %collective-permute-start.6 = (bf16[1,2,704,2048]{3,2,1,0:T(8,128)(2,1)}, bf16[1,2,704,2048]{3,2,1,0:T(8,128)(2,1)}, u32[]{:S(2)}, u32[]{:S(2)}) collective-permute-start(bf16[1,2,704,2048]{3,2,1,0:T(8,128)(2,1)} %bitcast.76), channel_id=1, source_target_pairs={{0,2},{2,0},{4,6},{6,4},{8,10},{10,8},{12,14},{14,12},{16,18},{18,... | collective-permute-start | bytes 17301512 | tf_op jit(solution)/shard_map/ppermute | solution.py:442
  1.2 38.7 %collective-permute-start.7 = (bf16[1,704,2048]{2,1,0:T(8,128)(2,1)}, bf16[1,704,2048]{2,1,0:T(8,128)(2,1)}, u32[]{:S(2)}, u32[]{:S(2)}) collective-permute-start(bf16[1,704,2048]{2,1,0:T(8,128)(2,1)} %own_down.1), channel_id=1, source_target_pairs={{0,2},{2,0},{4,6},{6,4},{8,10},{10,8},{12,14},{14,12},{16,18},{18,... | collective-permute-start | bytes 8650760 | tf_op jit(solution)/shard_map/ppermute | solution.py:442
  68.0 36.3 %collective-permute-start.1 = (bf16[128,3712]{1,0:T(8,128)(2,1)}, bf16[128,3712]{1,0:T(8,128)(2,1)}, u32[]{:S(2)}, u32[]{:S(2)}) collective-permute-start(bf16[128,3712]{1,0:T(8,128)(2,1)} %shard_map.281.refs_0_), channel_id=1, source_target_pairs={{0,2},{2,0},{4,6},{6,4},{8,10},{10,8},{12,14},{14,12},{16,18},{18,... | collective-permute-start | bytes 2850824 | tf_op jit(solution)/shard_map/ppermute | solution.py:442
  183.6 90.6 %all-to-all-start = ((bf16[16,288,128]{2,1,0:T(8,128)(2,1)}), bf16[16,288,128]{2,1,0:T(8,128)(2,1)}, u32[]{:S(2)}, u32[]{:S(2)}) async-start(bf16[16,288,128]{2,1,0:T(8,128)(2,1)} %shard_map.290), calls=%async_computation | async-start | bytes 2359296 | tf_op jit(solution)/shard_map/all_to_all | solution.py:1716
  199.4 35.5 %collective-permute-start.37 = (bf16[128,2048]{1,0:T(8,128)(2,1)}, bf16[128,2048]{1,0:T(8,128)(2,1)}, u32[]{:S(2)}, u32[]{:S(2)}) collective-permute-start(bf16[128,2048]{1,0:T(8,128)(2,1)} %collective-permute-done.18), channel_id=1, source_target_pairs={{0,1},{1,0},{2,3},{3,2},{4,5},{5,4},{6,7},{7,6},{8,9},{9,8},{10,11... | collective-permute-start | bytes 1572872 | tf_op jit(solution)/shard_map/ppermute | solution.py:446
  236.9 36.1 %collective-permute-start.38 = (bf16[256,2048]{1,0:T(8,128)(2,1)}, bf16[256,2048]{1,0:T(8,128)(2,1)}, u32[]{:S(2)}, u32[]{:S(2)}) collective-permute-start(bf16[256,2048]{1,0:T(8,128)(2,1)} %constant_dynamic-update-slice_fusion.6.refs_2_.refs_6_), channel_id=1, source_target_pairs={{0,4},{2,6},{4,0},{6,2},{8,12},{10,14},{12,8},{14,10},{16,20},{18,... | collective-permute-start | bytes 3145736 | tf_op jit(solution)/shard_map/ppermute | solution.py:438
  256.0 46.5 %collective-permute-start.35 = (bf16[256,2048]{1,0:T(8,128)(2,1)}, bf16[256,2048]{1,0:T(8,128)(2,1)}, u32[]{:S(2)}, u32[]{:S(2)}) collective-permute-start(bf16[256,2048]{1,0:T(8,128)(2,1)} %collective-permute-done.33.refs_1_.refs_5_), channel_id=1, source_target_pairs={{0,1},{1,0},{2,3},{3,2},{4,5},{5,4},{6,7},{7,6},{8,9},{9,8},{10,11... | collective-permute-start | bytes 3145736 | tf_op jit(solution)/shard_map/ppermute | solution.py:446
  256.8 45.1 %collective-permute-start.40 = (bf16[128,2048]{1,0:T(8,128)(2,1)}, bf16[128,2048]{1,0:T(8,128)(2,1)}, u32[]{:S(2)}, u32[]{:S(2)}) collective-permute-start(bf16[128,2048]{1,0:T(8,128)(2,1)} %collective-permute-done.24.refs_9_.refs_0_), channel_id=1, source_target_pairs={{0,1},{1,0},{2,3},{3,2},{4,5},{5,4},{6,7},{7,6},{8,9},{9,8},{10,11... | collective-permute-start | bytes 1572872 | tf_op jit(solution)/shard_map/ppermute | solution.py:446
  260.5 126.0 %collective-permute-start.29 = (bf16[256,2048]{1,0:T(8,128)(2,1)S(1)}, bf16[256,2048]{1,0:T(8,128)(2,1)S(1)}, u32[]{:S(2)}, u32[]{:S(2)}) collective-permute-start(bf16[256,2048]{1,0:T(8,128)(2,1)S(1)} %constant_dynamic-update-slice_fusion.2.refs_0_), channel_id=1, source_target_pairs={{0,4},{2,6},{4,0},{6,2},{8,12},{10,14},{12,8},{14,10},{16,20},{18,... | collective-permute-start | bytes 3145736 | tf_op jit(solution)/shard_map/ppermute | solution.py:438
  272.9 113.6 %collective-permute-start.30 = (bf16[256,2048]{1,0:T(8,128)(2,1)S(1)}, bf16[256,2048]{1,0:T(8,128)(2,1)}, u32[]{:S(2)}, u32[]{:S(2)}) collective-permute-start(bf16[256,2048]{1,0:T(8,128)(2,1)S(1)} %constant_dynamic-update-slice_fusion.2.refs_0_), channel_id=1, source_target_pairs={{0,1},{1,0},{2,3},{3,2},{4,5},{5,4},{6,7},{7,6},{8,9},{9,8},{10,11... | collective-permute-start | bytes 3145736 | tf_op jit(solution)/shard_map/ppermute | solution.py:446
  301.9 52.9 %collective-permute-start.42 = (bf16[128,2048]{1,0:T(8,128)(2,1)}, bf16[128,2048]{1,0:T(8,128)(2,1)}, u32[]{:S(2)}, u32[]{:S(2)}) collective-permute-start(bf16[128,2048]{1,0:T(8,128)(2,1)} %copy-done.47), channel_id=1, source_target_pairs={{0,4},{2,6},{4,0},{6,2},{8,12},{10,14},{12,8},{14,10},{16,20},{18,... | collective-permute-start | bytes 1572872 | tf_op jit(solution)/shard_map/ppermute | solution.py:438
  302.5 84.0 %collective-permute-start.39 = (bf16[128,2048]{1,0:T(8,128)(2,1)}, bf16[128,2048]{1,0:T(8,128)(2,1)}, u32[]{:S(2)}, u32[]{:S(2)}) collective-permute-start(bf16[128,2048]{1,0:T(8,128)(2,1)} %collective-permute-done.24.refs_9_.refs_0_), channel_id=1, source_target_pairs={{0,4},{2,6},{4,0},{6,2},{8,12},{10,14},{12,8},{14,10},{16,20},{18,... | collective-permute-start | bytes 1572872 | tf_op jit(solution)/shard_map/ppermute | solution.py:438
  304.0 82.6 %collective-permute-start.41 = (bf16[128,2048]{1,0:T(8,128)(2,1)}, bf16[128,2048]{1,0:T(8,128)(2,1)}, u32[]{:S(2)}, u32[]{:S(2)}) collective-permute-start(bf16[128,2048]{1,0:T(8,128)(2,1)} %collective-permute-done.40.refs_2_), channel_id=1, source_target_pairs={{0,4},{2,6},{4,0},{6,2},{8,12},{10,14},{12,8},{14,10},{16,20},{18,... | collective-permute-start | bytes 1572872 | tf_op jit(solution)/shard_map/ppermute | solution.py:438
  420.4 36.4 %collective-permute-start.31 = (bf16[256,2048]{1,0:T(8,128)(2,1)S(1)}, bf16[256,2048]{1,0:T(8,128)(2,1)}, u32[]{:S(2)}, u32[]{:S(2)}) collective-permute-start(bf16[256,2048]{1,0:T(8,128)(2,1)S(1)} %collective-permute-done.29.refs_15_.refs_1_), channel_id=1, source_target_pairs={{0,1},{1,0},{2,3},{3,2},{4,5},{5,4},{6,7},{7,6},{8,9},{9,8},{10,11... | collective-permute-start | bytes 3145736 | tf_op jit(solution)/shard_map/ppermute | solution.py:446
  425.7 66.2 %collective-permute-start.45 = (bf16[128,2048]{1,0:T(8,128)(2,1)}, bf16[128,2048]{1,0:T(8,128)(2,1)S(1)}, u32[]{:S(2)}, u32[]{:S(2)}) collective-permute-start(bf16[128,2048]{1,0:T(8,128)(2,1)} %copy-done.65), channel_id=1, source_target_pairs={{0,4},{2,6},{4,0},{6,2},{8,12},{10,14},{12,8},{14,10},{16,20},{18,... | collective-permute-start | bytes 1572872 | tf_op jit(solution)/shard_map/ppermute | solution.py:438
  426.3 61.6 %collective-permute-start.48 = (bf16[128,2048]{1,0:T(8,128)(2,1)}, bf16[128,2048]{1,0:T(8,128)(2,1)S(1)}, u32[]{:S(2)}, u32[]{:S(2)}) collective-permute-start(bf16[128,2048]{1,0:T(8,128)(2,1)} %copy-done.67), channel_id=1, source_target_pairs={{0,1},{1,0},{2,3},{3,2},{4,5},{5,4},{6,7},{7,6},{8,9},{9,8},{10,11... | collective-permute-start | bytes 1572872 | tf_op jit(solution)/shard_map/ppermute | solution.py:446
  435.7 52.8 %collective-permute-start.47 = (bf16[128,2048]{1,0:T(8,128)(2,1)S(1)}, bf16[128,2048]{1,0:T(8,128)(2,1)S(1)}, u32[]{:S(2)}, u32[]{:S(2)}) collective-permute-start(bf16[128,2048]{1,0:T(8,128)(2,1)S(1)} %add_convert_fusion.9.refs_15_), channel_id=1, source_target_pairs={{0,4},{2,6},{4,0},{6,2},{8,12},{10,14},{12,8},{14,10},{16,20},{18,... | collective-permute-start | bytes 1572872 | tf_op jit(solution)/shard_map/ppermute | solution.py:438
  438.5 53.4 %collective-permute-start.46 = (bf16[128,2048]{1,0:T(8,128)(2,1)S(1)}, bf16[128,2048]{1,0:T(8,128)(2,1)S(1)}, u32[]{:S(2)}, u32[]{:S(2)}) collective-permute-start(bf16[128,2048]{1,0:T(8,128)(2,1)S(1)} %add_convert_fusion.10.refs_16_), channel_id=1, source_target_pairs={{0,1},{1,0},{2,3},{3,2},{4,5},{5,4},{6,7},{7,6},{8,9},{9,8},{10,11... | collective-permute-start | bytes 1572872 | tf_op jit(solution)/shard_map/ppermute | solution.py:446
  486.4 36.9 %collective-permute-start.51 = (bf16[128,2048]{1,0:T(8,128)(2,1)S(1)}, bf16[128,2048]{1,0:T(8,128)(2,1)S(1)}, u32[]{:S(2)}, u32[]{:S(2)}) collective-permute-start(bf16[128,2048]{1,0:T(8,128)(2,1)S(1)} %get-tuple-element.126), channel_id=1, source_target_pairs={{0,4},{2,6},{4,0},{6,2},{8,12},{10,14},{12,8},{14,10},{16,20},{18,... | collective-permute-start | bytes 1572872 | tf_op jit(solution)/shard_map/ppermute | solution.py:438
  487.9 53.1 %collective-permute-start.50 = (bf16[128,2048]{1,0:T(8,128)(2,1)}, bf16[128,2048]{1,0:T(8,128)(2,1)}, u32[]{:S(2)}, u32[]{:S(2)}) collective-permute-start(bf16[128,2048]{1,0:T(8,128)(2,1)} %get-tuple-element.124), channel_id=1, source_target_pairs={{0,4},{2,6},{4,0},{6,2},{8,12},{10,14},{12,8},{14,10},{16,20},{18,... | collective-permute-start | bytes 1572872 | tf_op jit(solution)/shard_map/ppermute | solution.py:438
  489.5 52.9 %collective-permute-start.49 = (bf16[128,2048]{1,0:T(8,128)(2,1)}, bf16[128,2048]{1,0:T(8,128)(2,1)}, u32[]{:S(2)}, u32[]{:S(2)}) collective-permute-start(bf16[128,2048]{1,0:T(8,128)(2,1)} %add_convert_fusion.8), channel_id=1, source_target_pairs={{0,8},{2,10},{4,12},{6,14},{8,16},{10,18},{12,20},{14,22},{16,24},... | collective-permute-start | bytes 1572872 | tf_op jit(solution)/shard_map/ppermute | solution.py:434
  556.3 62.3 %collective-permute-start.60 = (bf16[1,1,704,2048]{3,2,1,0:T(8,128)(2,1)}, bf16[1,1,704,2048]{3,2,1,0:T(8,128)(2,1)}, u32[]{:S(2)}, u32[]{:S(2)}) collective-permute-start(bf16[1,1,704,2048]{3,2,1,0:T(8,128)(2,1)} %shard_map.299.refs_1_), channel_id=1, source_target_pairs={{0,2},{2,0},{4,6},{6,4},{8,10},{10,8},{12,14},{14,12},{16,18},{18,... | collective-permute-start | bytes 8650760 | tf_op jit(solution)/shard_map/ppermute | solution.py:442
  559.6 59.1 %all-to-all-start.1 = ((bf16[16,288,128]{2,1,0:T(8,128)(2,1)}), bf16[16,288,128]{2,1,0:T(8,128)(2,1)}, u32[]{:S(2)}, u32[]{:S(2)}) async-start(bf16[16,288,128]{2,1,0:T(8,128)(2,1)} %add_convert_fusion.1), calls=%async_computation.1 | async-start | bytes 2359296 | tf_op jit(solution)/shard_map/all_to_all | solution.py:1802
  675.4 56.3 %collective-permute-start.75 = (bf16[1024,1536]{1,0:T(8,128)(2,1)}, bf16[1024,1536]{1,0:T(8,128)(2,1)}, u32[]{:S(2)}, u32[]{:S(2)}) collective-permute-start(bf16[1024,1536]{1,0:T(8,128)(2,1)} %shard_map.315), channel_id=1, source_target_pairs={{0,2},{2,0},{4,6},{6,4},{8,10},{10,8},{12,14},{14,12},{16,18},{18,... | collective-permute-start | bytes 9437192 | tf_op jit(solution)/shard_map/ppermute | solution.py:442
  675.9 48.8 %collective-permute-start.62 = (bf16[512,2048]{1,0:T(8,128)(2,1)}, bf16[512,2048]{1,0:T(8,128)(2,1)}, u32[]{:S(2)}, u32[]{:S(2)}) collective-permute-start(bf16[512,2048]{1,0:T(8,128)(2,1)} %shard_map.309), channel_id=1, source_target_pairs={{0,1},{1,0},{2,3},{3,2},{4,5},{5,4},{6,7},{7,6},{8,9},{9,8},{10,11... | collective-permute-start | bytes 6291464 | tf_op jit(solution)/shard_map/ppermute | solution.py:446
  702.4 115.0 %collective-permute-start.69 = (bf16[1,2,704,2048]{3,2,1,0:T(8,128)(2,1)}, bf16[1,2,704,2048]{3,2,1,0:T(8,128)(2,1)}, u32[]{:S(2)}, u32[]{:S(2)}) collective-permute-start(bf16[1,2,704,2048]{3,2,1,0:T(8,128)(2,1)} %shard_map.312), channel_id=1, source_target_pairs={{0,2},{2,0},{4,6},{6,4},{8,10},{10,8},{12,14},{14,12},{16,18},{18,... | collective-permute-start | bytes 17301512 | tf_op jit(solution)/shard_map/ppermute | solution.py:442
  702.4 85.8 %collective-permute-start.64 = (bf16[512,2048]{1,0:T(8,128)(2,1)}, bf16[512,2048]{1,0:T(8,128)(2,1)}, u32[]{:S(2)}, u32[]{:S(2)}) collective-permute-start(bf16[512,2048]{1,0:T(8,128)(2,1)} %shard_map.310), channel_id=1, source_target_pairs={{0,1},{1,0},{2,3},{3,2},{4,5},{5,4},{6,7},{7,6},{8,9},{9,8},{10,11... | collective-permute-start | bytes 6291464 | tf_op jit(solution)/shard_map/ppermute | solution.py:446
  729.4 58.8 %collective-permute-start.63 = (bf16[512,2048]{1,0:T(8,128)(2,1)}, bf16[512,2048]{1,0:T(8,128)(2,1)}, u32[]{:S(2)}, u32[]{:S(2)}) collective-permute-start(bf16[512,2048]{1,0:T(8,128)(2,1)} %add_convert_fusion), channel_id=1, source_target_pairs={{0,4},{2,6},{4,0},{6,2},{8,12},{10,14},{12,8},{14,10},{16,20},{18,... | collective-permute-start | bytes 6291464 | tf_op jit(solution)/shard_map/ppermute | solution.py:438
  730.9 48.9 %collective-permute-start.68 = (bf16[128,2048]{1,0:T(8,128)(2,1)S(1)}, bf16[128,2048]{1,0:T(8,128)(2,1)S(1)}, u32[]{:S(2)}, u32[]{:S(2)}) collective-permute-start(bf16[128,2048]{1,0:T(8,128)(2,1)S(1)} %copy-done.90), channel_id=1, source_target_pairs={{0,1},{1,0},{2,3},{3,2},{4,5},{5,4},{6,7},{7,6},{8,9},{9,8},{10,11... | collective-permute-start | bytes 1572872 | tf_op jit(solution)/shard_map/ppermute | solution.py:446
  738.7 41.6 %collective-permute-start.76 = (bf16[256,1536]{1,0:T(8,128)(2,1)S(1)}, bf16[256,1536]{1,0:T(8,128)(2,1)S(1)}, u32[]{:S(2)}, u32[]{:S(2)}) collective-permute-start(bf16[256,1536]{1,0:T(8,128)(2,1)S(1)} %slice.159), channel_id=1, source_target_pairs={{0,8},{2,10},{4,12},{6,14},{8,16},{10,18},{12,20},{14,22},{16,24},... | collective-permute-start | bytes 2359304 | tf_op jit(solution)/shard_map/ppermute | solution.py:434
  785.3 53.2 %collective-permute-start.70 = (bf16[512,2176]{1,0:T(8,128)(2,1)}, bf16[512,2176]{1,0:T(8,128)(2,1)}, u32[]{:S(2)}, u32[]{:S(2)}) collective-permute-start(bf16[512,2176]{1,0:T(8,128)(2,1)} %shard_map.307.refs_1_.refs_2_), channel_id=1, source_target_pairs={{0,4},{2,6},{4,0},{6,2},{8,12},{10,14},{12,8},{14,10},{16,20},{18,... | collective-permute-start | bytes 6684680 | tf_op jit(solution)/shard_map/ppermute | solution.py:438
  806.4 37.6 %collective-permute-start.78 = (bf16[256,1536]{1,0:T(8,128)(2,1)}, bf16[256,1536]{1,0:T(8,128)(2,1)S(1)}, u32[]{:S(2)}, u32[]{:S(2)}) collective-permute-start(bf16[256,1536]{1,0:T(8,128)(2,1)} %add_convert_fusion.2), channel_id=1, source_target_pairs={{0,8},{2,10},{4,12},{6,14},{8,16},{10,18},{12,20},{14,22},{16,24},... | collective-permute-start | bytes 2359304 | tf_op jit(solution)/shard_map/ppermute | solution.py:434
  (167 other events, 2521.1 us)

commit v10 on v9

--- a/solution.py
+++ b/solution.py
@@ -422,14 +422,6 @@
 RINGS = 4
 
 
-def cost(flops, bytes_accessed, transcendentals):
-    return pl.CostEstimate(
-        flops=flops // 16,
-        bytes_accessed=bytes_accessed // 16,
-        transcendentals=transcendentals // 16,
-    )
-
-
 def ring_step(values):
     return lax.ppermute(values, "dp", [(i, (i + RINGS) % 16) for i in range(16)])
 
@@ -471,7 +463,7 @@
         held = jnp.concatenate(ring[k : k + 2], axis=0)
         across = jnp.concatenate(over_x[k : k + 2], axis=0)
         beside = other_y(held)
-        groups.append((held, beside, across, other_x(beside) if k else other_y(across)))
+        groups.append((held, beside, across, other_y(across) if k else other_x(beside)))
     return groups, ring, over_x
 
 
@@ -818,7 +810,7 @@
             pltpu.SemaphoreType.DMA((len(chunks) * (2 + depth // latent_depth),))
         ],
         compiler_params=pltpu.CompilerParams(vmem_limit_bytes=48 * 1024 * 1024),
-        cost_estimate=cost(
+        cost_estimate=pl.CostEstimate(
             flops=2 * tokens * D * (first_width + heads * VD + 1024),
             bytes_accessed=4 * D * (first_width + 1536),
             transcendentals=2 * heads * tokens * tokens,
@@ -965,7 +957,7 @@
             pltpu.VMEM((tokens, 2 * span), f32),
         ],
         compiler_params=pltpu.CompilerParams(vmem_limit_bytes=48 * 1024 * 1024),
-        cost_estimate=cost(
+        cost_estimate=pl.CostEstimate(
             flops=2 * tokens * D * 3000,
             bytes_accessed=2 * D * 1536,
             transcendentals=heads * tokens * tokens,
@@ -1042,7 +1034,7 @@
         ),
         out_shape=jax.ShapeDtypeStruct((count * size, width), jnp.bfloat16),
         compiler_params=pltpu.CompilerParams(vmem_limit_bytes=32 * 1024 * 1024),
-        cost_estimate=cost(
+        cost_estimate=pl.CostEstimate(
             flops=1024 * count * size * width,
             bytes_accessed=4 * count * size * width,
             transcendentals=0,
@@ -1125,7 +1117,7 @@
         in_specs=[pl.BlockSpec(memory_space=pltpu.SMEM)] + in_vmem(4),
         out_specs=in_vmem(3),
         compiler_params=pltpu.CompilerParams(vmem_limit_bytes=32 * 1024 * 1024),
-        cost_estimate=cost(
+        cost_estimate=pl.CostEstimate(
             flops=4 * own.shape[0] * weight.shape[0] * weight.shape[1],
             bytes_accessed=2 * weight.shape[0] * weight.shape[1],
             transcendentals=0,
@@ -1286,7 +1278,7 @@
         out_specs=[pl.BlockSpec((height, columns), lambda i: (0, i))] * 3,
         out_shape=[jax.ShapeDtypeStruct((height, depth), jnp.bfloat16)] * 3,
         compiler_params=pltpu.CompilerParams(vmem_limit_bytes=32 * 1024 * 1024),
-        cost_estimate=cost(
+        cost_estimate=pl.CostEstimate(
             flops=0, bytes_accessed=12 * height * depth, transcendentals=0
         ),
     )(own_in, other_in, own_down, other_down, near, far, *others)
@@ -1320,7 +1312,7 @@
         out_specs=out,
         out_shape=jax.ShapeDtypeStruct((1, len(lefts), units, depth), kind),
         compiler_params=pltpu.CompilerParams(vmem_limit_bytes=48 * 1024 * 1024),
-        cost_estimate=cost(
+        cost_estimate=pl.CostEstimate(
             flops=2 * len(lefts) * total * depth * wide,
             bytes_accessed=2 * len(lefts) * total * (depth + wide) + 8 * depth * units,
             transcendentals=0,
@@ -1364,7 +1356,7 @@
             jax.ShapeDtypeStruct((logits.shape[1], depth), jnp.float32),
         ],
         compiler_params=pltpu.CompilerParams(vmem_limit_bytes=48 * 1024 * 1024),
-        cost_estimate=cost(
+        cost_estimate=pl.CostEstimate(
             flops=8 * total * depth * TILE,
             bytes_accessed=4 * total * depth,
             transcendentals=0,
@@ -1409,7 +1401,7 @@
         scratch_shapes=[pltpu.SemaphoreType.DMA((count,))],
         input_output_aliases={count + 1 + k: k for k in range(len(kept))},
         compiler_params=pltpu.CompilerParams(vmem_limit_bytes=48 * 1024 * 1024),
-        cost_estimate=cost(
+        cost_estimate=pl.CostEstimate(
             flops=2 * rows * depth * width,
             bytes_accessed=2 * (2 * rows * depth + depth * width + rows * width),
             transcendentals=0,
@@ -1438,7 +1430,7 @@
         out_specs=[pl.BlockSpec((rows // pieces, TILE), lambda i: (0, i))] * pieces,
         out_shape=[jax.ShapeDtypeStruct((rows // pieces, depth), jnp.bfloat16)] * pieces,
         compiler_params=pltpu.CompilerParams(vmem_limit_bytes=48 * 1024 * 1024),
-        cost_estimate=cost(
+        cost_estimate=pl.CostEstimate(
             flops=2 * rows * depth * width,
             bytes_accessed=2 * (rows * depth + depth * width + rows * width),
             transcendentals=0,
@@ -1574,7 +1566,7 @@
         ],
         input_output_aliases={first_kept + k: pieces + k for k in range(len(kept))},
         compiler_params=pltpu.CompilerParams(vmem_limit_bytes=48 * 1024 * 1024),
-        cost_estimate=cost(
+        cost_estimate=pl.CostEstimate(
             flops=2 * total * depth * width * 4,
             bytes_accessed=2 * (4 * depth * width + 3 * total * depth + 4 * total * width),
             transcendentals=total * width,
@@ -1641,6 +1633,15 @@
     chunks, held, besides = gather_weight(
         shards, (expert_in_other, expert_down_other, other_input)
     )
+    shared_near = lax.all_to_all(
+        pack_shared(shared_gate_up, shared_down, blocks, (held[3],)),
+        "dp",
+        split_axis=0,
+        concat_axis=0,
+        tiled=True,
+    )
+    shared_far = other_core(shared_near)
+
     grad_groups, grad_ring, grad_across = gather_whole(
         after(cotangent, held[3], besides[2]), besides[3]
     )
@@ -1675,7 +1676,7 @@
         chunks,
         heads,
         sizes,
-        (grad_ring[3], grad_across[2], grad_groups[0][1]),
+        (grad_ring[3], grad_across[1], grad_across[2], grad_groups[0][1]),
     )
     attn_gain_wide, ffn_gain_wide = gains[0], gains[1]
     mixed = block_input.astype(f32) + own_part + other_x(sent_part).astype(f32)
@@ -1713,15 +1714,6 @@
         [(array, local_rows) for array in row_groups[2]],
     ]
 
-    shared_near = lax.all_to_all(
-        after(pack_shared(shared_gate_up, shared_down, blocks, (held[1],)), sent_part),
-        "dp",
-        split_axis=0,
-        concat_axis=0,
-        tiled=True,
-    )
-    shared_far = other_core(shared_near)
-
     gate_weight, up_weight, down_weight = pack_units(
         expert_in,
         expert_in_other,
@@ -1752,13 +1744,14 @@
         [chip_experts, jnp.array([experts, used + 3 - query_width - KVR], jnp.int32)]
     )
     kept = []
-    turned, closed = [], []
+    planes = []
+    turned, closed = [None] * RINGS, [None] * RINGS
     for distance in range(RINGS):
-        others = [row_ring[3]] if distance == 0 else list(row_groups[2][1:3])
-        if distance == 2:
+        others = [row_ring[3]] if distance == 0 else []
+        if distance == 1:
+            others = list(row_groups[2][1:3])
+        elif distance == 3:
             others = list(turned[0][1:])
-        elif distance == 3:
-            others = list(turned[1][1:]) + list(closed[0][1:])
         grads, kept = mlp_plane(
             distance,
             expert_ids,
@@ -1770,9 +1763,16 @@
             kept,
             others,
         )
-        turned.append(turn_corner(grads, corners[distance]))
-        if distance < RINGS - 1:
-            closed.append(close_plane(turned[distance]))
+        planes.append(list(grads))
+        if distance:
+            before = planes[distance - 1]
+            k = 1 if corners[distance - 1] == "x" else 2
+            before[k] = after(before[k], grads[3])
+            turned[distance - 1] = turn_corner(before, corners[distance - 1])
+            closed[distance - 1] = close_plane(turned[distance - 1])
+    turned[3] = turn_corner(planes[3], corners[3])
+    first_part = closed[1]
+    closed[1] = (after(first_part[0], planes[3][3]),) + tuple(first_part[1:])
     every_row, every_hidden, every_gate_grad, every_up_grad, logit_grads = kept
     shared_kept, shared_sent, logit_rows = side_grads(
         every_row,
@@ -1784,18 +1784,22 @@
         shared,
         blocks,
     )
-    outs = list(out_rows(4, every_hidden, down_weight))
+    first_total = wide_sum(*closed[1]).astype(bf16)
+    sent_in = expert_grads(
+        (every_gate_grad, every_up_grad), every_row, units, 1, None, bf16, (first_total,)
+    )
     sent_down = expert_grads((every_hidden,), every_grad, units, 1, None, bf16)
-    moving = ring_step(wide_sum(*closed[1]).astype(bf16))
+    moving = ring_step(first_total)
     moving = ring_step(wide_sum(moving, *closed[2]).astype(bf16))
     own, beside, across = turned[3]
     own = after(own, sent_down)
     grad_close = close_plane((own, after(beside, shared_sent), across))
     grad_second = wide_sum(
         ring_step(wide_sum(moving, *grad_close).astype(bf16)),
-        after(closed[0][0], outs[0]),
+        after(closed[0][0], sent_in),
         *closed[0][1:],
     )
+    arrived_in = other_core(sent_in)
     arrived_down = other_core(sent_down)
     router_at = used + 3 - query_width - KVR
     grad_router = logit_rows[router_at : router_at + experts]
@@ -1809,6 +1813,7 @@
     )
     grad_mixed_low = grad_mixed.astype(bf16)
     other_grad = other_x(grad_mixed_low)
+    outs = list(out_rows(4, every_hidden, down_weight))
     outs[3] = after(outs[3], grad_close[2])
     outs[2] = after(outs[2], other_grad)
     out_own, out_beside, out_across = close_plane(turn_corner(outs, "x"))
@@ -1825,7 +1830,7 @@
         (keyval_weight, output_turned, nope, turned_query, latent, key, keyval, total, latent_gain_row),
         heads,
         first_width,
-        (shared_grads, arrived_down),
+        (shared_grads, arrived_in, arrived_down),
     )
     grad_attn = jnp.concatenate(
         [
@@ -1860,9 +1865,6 @@
     other_kept = other_grads(*other_parts, 0, 8, other_arrived)
     far = first_grads(*first_parts, 4, 4, first_arrived)
     from_y = other_y(far)
-    arrived_in = other_core(
-        expert_grads((every_gate_grad, every_up_grad), every_row, units, 1, None, bf16, (far,))
-    )
     out_total = wide_sum(after(out_own, far), out_beside, out_across)
     block_output = mixed + ring_sum(
         [out_total[r * local_rows : (r + 1) * local_rows] for r in range(RINGS)], bf16
@@ -1875,10 +1877,10 @@
     grad_expert_down = expert_grads(
         (every_hidden,), every_grad, units, 0, arrived_down, f32, (from_y,)
     )
+    first_closed = close_ring(near, from_y)
     grad_expert_in = expert_grads(
         (every_gate_grad, every_up_grad), every_row, units, 0, arrived_in, f32, (near,)
     )
-    first_closed = close_ring(after(near, grad_expert_in), from_y)
     grad_shared_in, grad_shared_down = unpack_shared(shared_grads, shared, (from_y,))
     grad_expert_gate_up = grad_expert_in.swapaxes(2, 3)
     grad_expert_down = grad_expert_down[0]

time: 924 us -> 767 us (0.83)
  waiting for transfers between devices: 314 us -> 216 us
  starting transfers between devices: 96 us -> 69.9 us
  local copies, waits for them, and re-layouts: 104 us -> 79.8 us
    ppermute x22, waiting for transfers between devices: 123 us -> 34.5 us  [other_x(): return lax.ppermute(values, 'tensor', [(0, 1), (1, 0)])]
    ppermute x21, starting transfers between devices: 34.5 us -> 10 us  [ring_step(): lax.ppermute(values, 'dp', [(i, (i + RINGS) % 16) for i in range(16)])]
    ppermute x21, waiting for transfers between devices: 140 us -> 129 us  [ring_step(): lax.ppermute(values, 'dp', [(i, (i + RINGS) % 16) for i in range(16)])]
    unnamed x253 -> x241, local copies, waits for them, and re-layouts: 70.8 us -> 61.8 us
  transfers between devices with their start and end apart: 82 -> 82, of which waited for: 25 -> 28; matrix products, arithmetic and copies ran while one was open for 12% -> 11% of each run, Pallas kernels for 28% -> 44%
where the time goes in v10:
time: 767 us; the launch traced here: 758 us
  Pallas kernels  337 us (44%)
  waiting for transfers between devices  216 us (28%)
  local copies, waits for them, and re-layouts  79.8 us (10%)
  starting transfers between devices  69.9 us (9%)
  other arithmetic  53.1 us (7%)
    ppermute x21, waiting for transfers between devices, ring_step(): lax.ppermute(values, 'dp', [(i, (i + RINGS) % 16) for i in range(16)])  129 us
    pallas_call x4, Pallas kernels, mlp_plane(): pl.pallas_call(functools.partial(mlp_kernel, tiles, tuple((start for _, s...  117 us
    pallas_call x4, Pallas kernels, expert_grads(): pl.pallas_call(functools.partial(expert_grads_kernel, units, len(lefts),...  63.2 us
    unnamed x241, local copies, waits for them, and re-layouts  61.8 us
    ppermute x21, waiting for transfers between devices, other_y(): return lax.ppermute(values, 'dp', [(i, i ^ 2) for i in range(16)])  51.9 us
    ppermute x22, waiting for transfers between devices, other_x(): return lax.ppermute(values, 'tensor', [(0, 1), (1, 0)])  34.5 us
    pallas_call x2, Pallas kernels, down_grads(): pl.pallas_call(functools.partial(down_kernel, tuple((start for _, start i...  29.4 us
    pallas_call x5, Pallas kernels, grads_call(): pl.pallas_call(functools.partial(kernel, len(extra)), grid_spec=pltpu.Pre...  29.3 us
  transfers between devices with their start and end apart: 82, of which 28 were waited for; matrix products, arithmetic and copies ran while one was open for 11% of the time, Pallas kernels for 44%

profile of v10, /device:TPU:0, one launch (start us, length us, event | category | flops | bytes accessed | tf_op | source)
XLA Modules:
  0.0 758.3 jit_solution(6185918658027986705)
XLA Ops:
  18.5 20.5 %collective-permute-done.4.refs_4_ = bf16[128,3712]{1,0:T(8,128)(2,1)S(1)} collective-permute-done((bf16[128,3712]{1,0:T(8,128)(2,1)}, bf16[128,3712]{1,0:T(8,128)(2,1)S(1)}, u32[]{:S(2)}, u32[]{:S(2)}) %collective-permute-start.4) | collective-permute-done | bytes 950304 | tf_op jit(solution)/shard_map/ppermute | solution.py:426
  46.2 19.3 %collective-permute-done.10.refs_8_ = bf16[128,3712]{1,0:T(8,128)(2,1)} collective-permute-done((bf16[128,3712]{1,0:T(8,128)(2,1)}, bf16[128,3712]{1,0:T(8,128)(2,1)}, u32[]{:S(2)}, u32[]{:S(2)}) %collective-permute-start.10) | collective-permute-done | bytes 950304 | tf_op jit(solution)/shard_map/ppermute | solution.py:426
  71.3 18.4 %collective-permute-done.12.refs_2_.refs_10_ = bf16[128,3712]{1,0:T(8,128)(2,1)} collective-permute-done((bf16[128,3712]{1,0:T(8,128)(2,1)}, bf16[128,3712]{1,0:T(8,128)(2,1)}, u32[]{:S(2)}, u32[]{:S(2)}) %collective-permute-start.12) | collective-permute-done | bytes 950304 | tf_op jit(solution)/shard_map/ppermute | solution.py:430
  94.0 13.0 %collective-permute-done.18 = bf16[128,2048]{1,0:T(8,128)(2,1)S(1)} collective-permute-done((bf16[128,2048]{1,0:T(8,128)(2,1)}, bf16[128,2048]{1,0:T(8,128)(2,1)S(1)}, u32[]{:S(2)}, u32[]{:S(2)}) %collective-permute-start.18) | collective-permute-done | bytes 524320 | tf_op jit(solution)/shard_map/ppermute | solution.py:426
  109.5 9.5 %collective-permute-done.19.refs_0_ = bf16[128,2048]{1,0:T(8,128)(2,1)S(1)} collective-permute-done((bf16[128,2048]{1,0:T(8,128)(2,1)S(1)}, bf16[128,2048]{1,0:T(8,128)(2,1)S(1)}, u32[]{:S(2)}, u32[]{:S(2)}) %collective-permute-start.19) | collective-permute-done | bytes 524320 | tf_op jit(solution)/shard_map/ppermute | solution.py:426
  124.1 8.0 %collective-permute-done.16.refs_1_.refs_14_ = bf16[128,3712]{1,0:T(8,128)(2,1)} collective-permute-done((bf16[128,3712]{1,0:T(8,128)(2,1)}, bf16[128,3712]{1,0:T(8,128)(2,1)}, u32[]{:S(2)}, u32[]{:S(2)}) %collective-permute-start.16) | collective-permute-done | bytes 950304 | tf_op jit(solution)/shard_map/ppermute | solution.py:430
  135.8 9.1 %collective-permute-done.21.refs_17_ = bf16[128,2048]{1,0:T(8,128)(2,1)S(1)} collective-permute-done((bf16[128,2048]{1,0:T(8,128)(2,1)S(1)}, bf16[128,2048]{1,0:T(8,128)(2,1)S(1)}, u32[]{:S(2)}, u32[]{:S(2)}) %collective-permute-start.21) | collective-permute-done | bytes 524320 | tf_op jit(solution)/shard_map/ppermute | solution.py:438
  148.8 6.8 all-to-all-start
  160.0 22.8 %shard_map.287 = (f32[128,2048]{1,0:T(8,128)}, bf16[128,2048]{1,0:T(8,128)(2,1)S(1)}, bf16[2048,2176]{1,0:T(8,128)(2,1)}, bf16[512,2048]{1,0:T(8,128)(2,1)}, bf1...) custom-call(s32[5]{0:T(128)S(1)} %concatenate.39.place_ref.refs_0_, ...), custom_call_target="tpu_custom_call" | custom-call | flops 4429185024 | bytes 30408704 | tf_op jit(solution)/shard_map/pallas_call | solution.py:802
  192.3 9.9 %collective-permute-done.24 = bf16[128,2048]{1,0:T(8,128)(2,1)} collective-permute-done((bf16[128,2048]{1,0:T(8,128)(2,1)S(1)}, bf16[128,2048]{1,0:T(8,128)(2,1)}, u32[]{:S(2)}, u32[]{:S(2)}) %collective-permute-start.24) | collective-permute-done | bytes 524320 | tf_op jit(solution)/shard_map/ppermute | solution.py:438
  232.4 11.8 %shard_map.290 = (bf16[1792,2048]{1,0:T(8,128)(2,1)}, bf16[1792,2048]{1,0:T(8,128)(2,1)}, bf16[1792,2048]{1,0:T(8,128)(2,1)}) custom-call(bf16[1,2,704,2048]{3,2,1,0:T(8,128)(2,1)S(1)} %bitcast.79, bf16[1,2,704,2048]{3,2,1,0:T(8,128)(2,1)} %collective-permute-done.6.refs_1_.other_in, bf16[1,704,2048]{2,1,0:T(8,128)(2,1)S(1)} %copy-done.30, ...), custom_call_target="tpu_custom_call" | custom-call | bytes 44040192 | tf_op jit(solution)/shard_map/pallas_call | solution.py:1273
  244.8 14.5 %shard_map.291 = (bf16[2048,1792]{1,0:T(8,128)(2,1)}, bf16[2048,2048]{1,0:T(8,128)(2,1)}) custom-call(bf16[256,2048]{1,0:T(8,128)(2,1)} %pad_maximum_fusion.refs_0_.refs_4_, bf16[256,2048]{1,0:T(8,128)(2,1)} %collective-permute-done.23.refs_19_.refs_1_.refs_5_, bf16[256,2048]{1,0:T(8,128)(2,1)S(1)} %copy-done.55, ...), custom_call_target="tpu_custom_call" | custom-call | flops 7516192768 | bytes 19398656 | tf_op jit(solution)/shard_map/pallas_call | solution.py:1387
  267.5 14.9 %shard_map.292 = (bf16[2048,1792]{1,0:T(8,128)(2,1)}, bf16[2048,2048]{1,0:T(8,128)(2,1)}) custom-call(bf16[256,2048]{1,0:T(8,128)(2,1)} %constant_dynamic-update-slice_fusion.4.refs_0_.refs_4_, bf16[256,2048]{1,0:T(8,128)(2,1)} %collective-permute-done.34.refs_1_.refs_5_, ...), custom_call_target="tpu_custom_call", output_to_operand_aliasing={{0}: (9, {}), {1}: (10, {})} | custom-call | flops 7516192768 | bytes 19398656 | tf_op jit(solution)/shard_map/pallas_call | solution.py:1387
  284.5 29.6 %shard_map.293 = (bf16[128,2048]{1,0:T(8,128)(2,1)S(1)}, bf16[128,2048]{1,0:T(8,128)(2,1)}, bf16[128,2048]{1,0:T(8,128)(2,1)S(1)}, bf16[128,2048]{1,0:T(8,128)(2...) custom-call(s32[4]{0:T(128)S(1)} %pad_add_fusion.experts_ref, ...), custom_call_target="tpu_custom_call" | custom-call | flops 15032385536 | bytes 42991616 | tf_op jit(solution)/shard_map/pallas_call | solution.py:1531
  315.3 8.3 %collective-permute-done.30.refs_15_.refs_1_ = bf16[256,2048]{1,0:T(8,128)(2,1)S(1)} collective-permute-done((bf16[256,2048]{1,0:T(8,128)(2,1)S(1)}, bf16[256,2048]{1,0:T(8,128)(2,1)S(1)}, u32[]{:S(2)}, u32[]{:S(2)}) %collective-permute-start.30) | collective-permute-done | bytes 1048608 | tf_op jit(solution)/shard_map/ppermute | solution.py:430
  324.9 28.3 %shard_map.294 = (bf16[128,2048]{1,0:T(8,128)(2,1)S(1)}, bf16[128,2048]{1,0:T(8,128)(2,1)S(1)}, bf16[128,2048]{1,0:T(8,128)(2,1)S(1)}, bf16[128,2048]{1,0:T(8,12...) custom-call(s32[4]{0:T(128)S(1)} %pad_add_fusion.experts_ref, ...), custom_call_target="tpu_custom_call", output_to_operand_aliasing={{4}: (12, {}), {5}: (13, {}), {6}: (14, {}), {7}: (15, {}),... | custom-call | flops 15032385536 | bytes 42991616 | tf_op jit(solution)/shard_map/pallas_call | solution.py:1531
  360.2 29.9 %shard_map.295 = (bf16[128,2048]{1,0:T(8,128)(2,1)S(1)}, bf16[128,2048]{1,0:T(8,128)(2,1)S(1)}, bf16[128,2048]{1,0:T(8,128)(2,1)S(1)}, bf16[128,2048]{1,0:T(8,12...) custom-call(s32[4]{0:T(128)S(1)} %pad_add_fusion.experts_ref, ...), custom_call_target="tpu_custom_call", output_to_operand_aliasing={{4}: (12, {}), {5}: (13, {}), {6}: (14, {}), {7}: (15, {}),... | custom-call | flops 15032385536 | bytes 42991616 | tf_op jit(solution)/shard_map/pallas_call | solution.py:1531
  396.7 29.5 %shard_map.297 = (bf16[128,2048]{1,0:T(8,128)(2,1)S(1)}, bf16[128,2048]{1,0:T(8,128)(2,1)S(1)}, bf16[128,2048]{1,0:T(8,128)(2,1)S(1)}, bf16[128,2048]{1,0:T(8,12...) custom-call(s32[4]{0:T(128)S(1)} %pad_add_fusion.experts_ref, ...), custom_call_target="tpu_custom_call", output_to_operand_aliasing={{4}: (12, {}), {5}: (13, {}), {6}: (14, {}), {7}: (15, {}),... | custom-call | flops 15032385536 | bytes 42991616 | tf_op jit(solution)/shard_map/pallas_call | solution.py:1531
  428.7 12.4 %shard_map.304 = (f32[16,288,128]{2,1,0:T(8,128)S(1)}, bf16[16,288,128]{2,1,0:T(8,128)(2,1)}, f32[128,2048]{1,0:T(8,128)S(1)}) custom-call(bf16[2048,2048]{1,0:T(8,128)(2,1)} %get-tuple-element.131.rows_ref.right_ref, bf16[2048,2048]{1,0:T(8,128)(2,1)} %get-tuple-element.129.right_ref.cots_ref, bf16[2048,1792]{1,0:T(8,128)(2,1)} %get-tuple-element.132.gate_ref.refs_0_, ...), custom_call_target="tpu_custom_call" | custom-call | flops 8589934592 | bytes 16777216 | tf_op jit(solution)/shard_map/pallas_call | solution.py:1348
  451.4 19.4 %shard_map.306.refs_1_ = bf16[1,2,704,2048]{3,2,1,0:T(8,128)(2,1)} custom-call(bf16[2048,2048]{1,0:T(8,128)(2,1)} %get-tuple-element.131.rows_ref.right_ref, bf16[2048,1792]{1,0:T(8,128)(2,1)} %get-tuple-element.132.gate_ref.refs_0_, bf16[2048,1792]{1,0:T(8,128)(2,1)} %get-tuple-element.133.up_ref.refs_1_, bf16[128,2048]{1,0:T(8,128)(2,1)S(1)} %add_convert_fusion.8.refs_2_), custom_call_target="tpu_custom_call" | custom-call | flops 12884901888 | bytes 34603008 | tf_op jit(solution)/shard_map/pallas_call | solution.py:1305
  477.7 10.8 %shard_map.302.refs_1_ = bf16[1,1,704,2048]{3,2,1,0:T(8,128)(2,1)} custom-call(bf16[2048,2048]{1,0:T(8,128)(2,1)} %get-tuple-element.129.right_ref.cots_ref, bf16[2048,1792]{1,0:T(8,128)(2,1)} %get-tuple-element.117.refs_0_.hidden_ref), custom_call_target="tpu_custom_call" | custom-call | flops 6442450944 | bytes 23068672 | tf_op jit(solution)/shard_map/pallas_call | solution.py:1305
  499.3 5.8 all-to-all-start.1
  515.4 21.3 %shard_map.298 = (bf16[512,2048]{1,0:T(8,128)(2,1)S(1)}, bf16[512,2048]{1,0:T(8,128)(2,1)S(1)}, bf16[512,2048]{1,0:T(8,128)(2,1)}, bf16[512,2048]{1,0:T(8,128)(2,1)}) custom-call(bf16[2048,1792]{1,0:T(8,128)(2,1)} %get-tuple-element.117.refs_0_.hidden_ref, bf16[1792,2048]{1,0:T(8,128)(2,1)} %get-tuple-element.94.refs_8_.refs_1_), custom_call_target="tpu_custom_call" | custom-call | flops 15032385536 | bytes 23068672 | tf_op jit(solution)/shard_map/pallas_call | solution.py:1426
  547.4 13.3 %shard_map.308 = (bf16[256,2176]{1,0:T(8,128)(2,1)}, bf16[256,2048]{1,0:T(8,128)(2,1)S(1)}, bf16[256,512]{1,0:T(8,128)(2,1)S(1)}, f32[1,512]{1,0:T(1,128)S(1)}) custom-call(s32[5]{0:T(128)S(1)} %copy-done.75, s32[1,256]{1,0:T(1,128)S(1)} %copy-done.72, s32[256,1]{1,0:T(8,128)S(1)} %copy-done.48, f32[256,256]{1,0:T(8,128)S(1)} %copy-done.32, ...), custom_call_target="tpu_custom_call" | custom-call | flops 3145728000 | bytes 6291456 | tf_op jit(solution)/shard_map/pallas_call | solution.py:944
  568.2 7.6 %shard_map.309 = (f32[128,2048]{1,0:T(8,128)S(1)}, bf16[128,2048]{1,0:T(8,128)(2,1)}, f32[1,2048]{1,0:T(1,128)S(1)}) custom-call(s32[5]{0:T(128)S(1)} %copy-done.75, bf16[128,2048]{1,0:T(8,128)(2,1)S(1)} %copy-done.3, bf16[128,2048]{1,0:T(8,128)(2,1)} %collective-permute-done.refs_3_.other_ref, bf16[256,2176]{1,0:T(8,128)(2,1)S(1)} %copy-done.8, ...), custom_call_target="tpu_custom_call" | custom-call | flops 2281701376 | bytes 8912896 | tf_op jit(solution)/shard_map/pallas_call | solution.py:1110
  599.2 7.1 shard_map.317
  611.5 15.5 %collective-permute-done.76 = bf16[256,1536]{1,0:T(8,128)(2,1)S(1)} collective-permute-done((bf16[256,1536]{1,0:T(8,128)(2,1)S(1)}, bf16[256,1536]{1,0:T(8,128)(2,1)S(1)}, u32[]{:S(2)}, u32[]{:S(2)}) %collective-permute-start.76) | collective-permute-done | bytes 786464 | tf_op jit(solution)/shard_map/ppermute | solution.py:426
  633.8 8.2 %collective-permute-done.64 = bf16[512,2048]{1,0:T(8,128)(2,1)} collective-permute-done((bf16[512,2048]{1,0:T(8,128)(2,1)}, bf16[512,2048]{1,0:T(8,128)(2,1)}, u32[]{:S(2)}, u32[]{:S(2)}) %collective-permute-start.64) | collective-permute-done | bytes 2097184 | tf_op jit(solution)/shard_map/ppermute | solution.py:430
  658.9 21.2 %shard_map.319 = f32[1,2,704,2048]{3,2,1,0:T(8,128)} custom-call(bf16[2048,2048]{1,0:T(8,128)(2,1)} %get-tuple-element.131.rows_ref.right_ref, bf16[2048,1792]{1,0:T(8,128)(2,1)} %get-tuple-element.132.gate_ref.refs_0_, bf16[2048,1792]{1,0:T(8,128)(2,1)} %get-tuple-element.133.up_ref.refs_1_, ...), custom_call_target="tpu_custom_call" | custom-call | flops 12884901888 | bytes 34603008 | tf_op jit(solution)/shard_map/pallas_call | solution.py:1305
  697.7 10.9 %collective-permute-done.71 = bf16[128,2176]{1,0:T(8,128)(2,1)S(1)} collective-permute-done((bf16[128,2176]{1,0:T(8,128)(2,1)S(1)}, bf16[128,2176]{1,0:T(8,128)(2,1)S(1)}, u32[]{:S(2)}, u32[]{:S(2)}) %collective-permute-start.71) | collective-permute-done | bytes 557088 | tf_op jit(solution)/shard_map/ppermute | solution.py:426
  710.6 9.4 %collective-permute-done.68 = bf16[128,2048]{1,0:T(8,128)(2,1)} collective-permute-done((bf16[128,2048]{1,0:T(8,128)(2,1)}, bf16[128,2048]{1,0:T(8,128)(2,1)}, u32[]{:S(2)}, u32[]{:S(2)}) %collective-permute-start.68) | collective-permute-done | bytes 524320 | tf_op jit(solution)/shard_map/ppermute | solution.py:426
  731.5 11.8 %shard_map.320 = f32[1,1,704,2048]{3,2,1,0:T(8,128)} custom-call(bf16[2048,2048]{1,0:T(8,128)(2,1)} %get-tuple-element.129.right_ref.cots_ref, bf16[2048,1792]{1,0:T(8,128)(2,1)} %get-tuple-element.117.refs_0_.hidden_ref, bf16[1,1,704,2048]{3,2,1,0:T(8,128)(2,1)} %collective-permute-done.61.refs_18_.refs_1_, bf16[512,2176]{1,0:T(8,128)(2,1)S(1)} %copy-done.1), custom_call_target="tpu_custom_call" | custom-call | flops 6442450944 | bytes 23068672 | tf_op jit(solution)/shard_map/pallas_call | solution.py:1305
  (518 shorter events, 276.6 us)
Async XLA Ops:
  0.7 42.5 %collective-permute-start.6 = (bf16[1,2,704,2048]{3,2,1,0:T(8,128)(2,1)}, bf16[1,2,704,2048]{3,2,1,0:T(8,128)(2,1)}, u32[]{:S(2)}, u32[]{:S(2)}) collective-permute-start(bf16[1,2,704,2048]{3,2,1,0:T(8,128)(2,1)} %bitcast.78), channel_id=1, source_target_pairs={{0,2},{2,0},{4,6},{6,4},{8,10},{10,8},{12,14},{14,12},{16,18},{18,... | collective-permute-start | bytes 17301512 | tf_op jit(solution)/shard_map/ppermute | solution.py:434
  1.2 42.0 %collective-permute-start.7 = (bf16[1,704,2048]{2,1,0:T(8,128)(2,1)}, bf16[1,704,2048]{2,1,0:T(8,128)(2,1)S(1)}, u32[]{:S(2)}, u32[]{:S(2)}) collective-permute-start(bf16[1,704,2048]{2,1,0:T(8,128)(2,1)} %own_down.1), channel_id=1, source_target_pairs={{0,2},{2,0},{4,6},{6,4},{8,10},{10,8},{12,14},{14,12},{16,18},{18,... | collective-permute-start | bytes 8650760 | tf_op jit(solution)/shard_map/ppermute | solution.py:434
  70.0 37.1 %collective-permute-start.1 = (bf16[128,3712]{1,0:T(8,128)(2,1)}, bf16[128,3712]{1,0:T(8,128)(2,1)}, u32[]{:S(2)}, u32[]{:S(2)}) collective-permute-start(bf16[128,3712]{1,0:T(8,128)(2,1)} %shard_map.281.refs_0_), channel_id=1, source_target_pairs={{0,2},{2,0},{4,6},{6,4},{8,10},{10,8},{12,14},{14,12},{16,18},{18,... | collective-permute-start | bytes 2850824 | tf_op jit(solution)/shard_map/ppermute | solution.py:434
  70.0 37.8 %collective-permute-start.5 = (bf16[128,3712]{1,0:T(8,128)(2,1)S(1)}, bf16[128,3712]{1,0:T(8,128)(2,1)}, u32[]{:S(2)}, u32[]{:S(2)}) collective-permute-start(bf16[128,3712]{1,0:T(8,128)(2,1)S(1)} %copy-done.88), channel_id=1, source_target_pairs={{0,2},{2,0},{4,6},{6,4},{8,10},{10,8},{12,14},{14,12},{16,18},{18,... | collective-permute-start | bytes 2850824 | tf_op jit(solution)/shard_map/ppermute | solution.py:434
  123.2 34.3 %collective-permute-start.23 = (bf16[256,2048]{1,0:T(8,128)(2,1)}, bf16[256,2048]{1,0:T(8,128)(2,1)}, u32[]{:S(2)}, u32[]{:S(2)}) collective-permute-start(bf16[256,2048]{1,0:T(8,128)(2,1)} %pad_maximum_fusion.refs_0_.refs_4_), channel_id=1, source_target_pairs={{0,4},{2,6},{4,0},{6,2},{8,12},{10,14},{12,8},{14,10},{16,20},{18,... | collective-permute-start | bytes 3145736 | tf_op jit(solution)/shard_map/ppermute | solution.py:430
  124.0 35.0 %collective-permute-start.9 = (bf16[128,3712]{1,0:T(8,128)(2,1)}, bf16[128,3712]{1,0:T(8,128)(2,1)}, u32[]{:S(2)}, u32[]{:S(2)}) collective-permute-start(bf16[128,3712]{1,0:T(8,128)(2,1)} %copy-done.90), channel_id=1, source_target_pairs={{0,2},{2,0},{4,6},{6,4},{8,10},{10,8},{12,14},{14,12},{16,18},{18,... | collective-permute-start | bytes 2850824 | tf_op jit(solution)/shard_map/ppermute | solution.py:434
  148.8 43.5 %all-to-all-start = ((bf16[16,288,128]{2,1,0:T(8,128)(2,1)}), bf16[16,288,128]{2,1,0:T(8,128)(2,1)}, u32[]{:S(2)}, u32[]{:S(2)}) async-start(bf16[16,288,128]{2,1,0:T(8,128)(2,1)} %shard_map.289), calls=%async_computation | async-start | bytes 2359296 | tf_op jit(solution)/shard_map/all_to_all | solution.py:1636
  157.5 86.7 %collective-permute-start.38 = (bf16[256,2048]{1,0:T(8,128)(2,1)}, bf16[256,2048]{1,0:T(8,128)(2,1)}, u32[]{:S(2)}, u32[]{:S(2)}) collective-permute-start(bf16[256,2048]{1,0:T(8,128)(2,1)} %collective-permute-done.23.refs_19_.refs_1_.refs_5_), channel_id=1, source_target_pairs={{0,1},{1,0},{2,3},{3,2},{4,5},{5,4},{6,7},{7,6},{8,9},{9,8},{10,11... | collective-permute-start | bytes 3145736 | tf_op jit(solution)/shard_map/ppermute | solution.py:438
  192.3 34.5 %collective-permute-start.33 = (bf16[16,288,128]{2,1,0:T(8,128)(2,1)}, bf16[16,288,128]{2,1,0:T(8,128)(2,1)}, u32[]{:S(2)}, u32[]{:S(2)}) collective-permute-start(bf16[16,288,128]{2,1,0:T(8,128)(2,1)} %all-to-all-done.near), channel_id=1, source_target_pairs={{0,2},{2,0},{4,6},{6,4},{8,10},{10,8},{12,14},{14,12},{16,18},{18,... | collective-permute-start | bytes 3538952 | tf_op jit(solution)/shard_map/ppermute | solution.py:434
  218.6 40.7 %collective-permute-start.34 = (bf16[256,2048]{1,0:T(8,128)(2,1)}, bf16[256,2048]{1,0:T(8,128)(2,1)}, u32[]{:S(2)}, u32[]{:S(2)}) collective-permute-start(bf16[256,2048]{1,0:T(8,128)(2,1)} %constant_dynamic-update-slice_fusion.4.refs_0_.refs_4_), channel_id=1, source_target_pairs={{0,4},{2,6},{4,0},{6,2},{8,12},{10,14},{12,8},{14,10},{16,20},{18,... | collective-permute-start | bytes 3145736 | tf_op jit(solution)/shard_map/ppermute | solution.py:430
  220.1 47.4 %collective-permute-start.36 = (bf16[256,2048]{1,0:T(8,128)(2,1)}, bf16[256,2048]{1,0:T(8,128)(2,1)}, u32[]{:S(2)}, u32[]{:S(2)}) collective-permute-start(bf16[256,2048]{1,0:T(8,128)(2,1)} %constant_dynamic-update-slice_fusion.6.refs_2_.refs_6_), channel_id=1, source_target_pairs={{0,4},{2,6},{4,0},{6,2},{8,12},{10,14},{12,8},{14,10},{16,20},{18,... | collective-permute-start | bytes 3145736 | tf_op jit(solution)/shard_map/ppermute | solution.py:430
  224.9 35.3 %collective-permute-start.28 = (bf16[128,2048]{1,0:T(8,128)(2,1)}, bf16[128,2048]{1,0:T(8,128)(2,1)S(1)}, u32[]{:S(2)}, u32[]{:S(2)}) collective-permute-start(bf16[128,2048]{1,0:T(8,128)(2,1)} %shard_map.288), channel_id=1, source_target_pairs={{0,8},{2,10},{4,12},{6,14},{8,16},{10,18},{12,20},{14,22},{16,24},... | collective-permute-start | bytes 1572872 | tf_op jit(solution)/shard_map/ppermute | solution.py:426
  226.8 57.7 %collective-permute-start.42 = (bf16[128,2048]{1,0:T(8,128)(2,1)}, bf16[128,2048]{1,0:T(8,128)(2,1)S(1)}, u32[]{:S(2)}, u32[]{:S(2)}) collective-permute-start(bf16[128,2048]{1,0:T(8,128)(2,1)} %collective-permute-done.27.refs_2_), channel_id=1, source_target_pairs={{0,4},{2,6},{4,0},{6,2},{8,12},{10,14},{12,8},{14,10},{16,20},{18,... | collective-permute-start | bytes 1572872 | tf_op jit(solution)/shard_map/ppermute | solution.py:430
  259.3 64.6 %collective-permute-start.39 = (bf16[128,2048]{1,0:T(8,128)(2,1)S(1)}, bf16[128,2048]{1,0:T(8,128)(2,1)S(1)}, u32[]{:S(2)}, u32[]{:S(2)}) collective-permute-start(bf16[128,2048]{1,0:T(8,128)(2,1)S(1)} %collective-permute-done.25.refs_9_.refs_0_), channel_id=1, source_target_pairs={{0,4},{2,6},{4,0},{6,2},{8,12},{10,14},{12,8},{14,10},{16,20},{18,... | collective-permute-start | bytes 1572872 | tf_op jit(solution)/shard_map/ppermute | solution.py:430
  261.7 62.1 %collective-permute-start.41 = (bf16[128,2048]{1,0:T(8,128)(2,1)S(1)}, bf16[128,2048]{1,0:T(8,128)(2,1)S(1)}, u32[]{:S(2)}, u32[]{:S(2)}) collective-permute-start(bf16[128,2048]{1,0:T(8,128)(2,1)S(1)} %collective-permute-done.40.refs_2_), channel_id=1, source_target_pairs={{0,4},{2,6},{4,0},{6,2},{8,12},{10,14},{12,8},{14,10},{16,20},{18,... | collective-permute-start | bytes 1572872 | tf_op jit(solution)/shard_map/ppermute | solution.py:430
  282.5 41.0 %collective-permute-start.30 = (bf16[256,2048]{1,0:T(8,128)(2,1)S(1)}, bf16[256,2048]{1,0:T(8,128)(2,1)S(1)}, u32[]{:S(2)}, u32[]{:S(2)}) collective-permute-start(bf16[256,2048]{1,0:T(8,128)(2,1)S(1)} %constant_dynamic-update-slice_fusion.2.refs_0_), channel_id=1, source_target_pairs={{0,4},{2,6},{4,0},{6,2},{8,12},{10,14},{12,8},{14,10},{16,20},{18,... | collective-permute-start | bytes 3145736 | tf_op jit(solution)/shard_map/ppermute | solution.py:430
  284.0 39.8 %collective-permute-start.31 = (bf16[256,2048]{1,0:T(8,128)(2,1)S(1)}, bf16[256,2048]{1,0:T(8,128)(2,1)S(1)}, u32[]{:S(2)}, u32[]{:S(2)}) collective-permute-start(bf16[256,2048]{1,0:T(8,128)(2,1)S(1)} %constant_dynamic-update-slice_fusion.2.refs_0_), channel_id=1, source_target_pairs={{0,1},{1,0},{2,3},{3,2},{4,5},{5,4},{6,7},{7,6},{8,9},{9,8},{10,11... | collective-permute-start | bytes 3145736 | tf_op jit(solution)/shard_map/ppermute | solution.py:438
  314.9 42.7 %collective-permute-start.43 = (bf16[128,2048]{1,0:T(8,128)(2,1)}, bf16[128,2048]{1,0:T(8,128)(2,1)}, u32[]{:S(2)}, u32[]{:S(2)}) collective-permute-start(bf16[128,2048]{1,0:T(8,128)(2,1)} %get-tuple-element.116), channel_id=1, source_target_pairs={{0,4},{2,6},{4,0},{6,2},{8,12},{10,14},{12,8},{14,10},{16,20},{18,... | collective-permute-start | bytes 1572872 | tf_op jit(solution)/shard_map/ppermute | solution.py:430
  323.6 35.4 %collective-permute-start.32 = (bf16[256,2048]{1,0:T(8,128)(2,1)S(1)}, bf16[256,2048]{1,0:T(8,128)(2,1)}, u32[]{:S(2)}, u32[]{:S(2)}) collective-permute-start(bf16[256,2048]{1,0:T(8,128)(2,1)S(1)} %collective-permute-done.30.refs_15_.refs_1_), channel_id=1, source_target_pairs={{0,1},{1,0},{2,3},{3,2},{4,5},{5,4},{6,7},{7,6},{8,9},{9,8},{10,11... | collective-permute-start | bytes 3145736 | tf_op jit(solution)/shard_map/ppermute | solution.py:438
  355.6 38.6 %collective-permute-start.44 = (bf16[128,2048]{1,0:T(8,128)(2,1)}, bf16[128,2048]{1,0:T(8,128)(2,1)}, u32[]{:S(2)}, u32[]{:S(2)}) collective-permute-start(bf16[128,2048]{1,0:T(8,128)(2,1)} %get-tuple-element.115.refs_1_), channel_id=1, source_target_pairs={{0,1},{1,0},{2,3},{3,2},{4,5},{5,4},{6,7},{7,6},{8,9},{9,8},{10,11... | collective-permute-start | bytes 1572872 | tf_op jit(solution)/shard_map/ppermute | solution.py:438
  357.3 91.4 %collective-permute-start.46 = (bf16[128,2048]{1,0:T(8,128)(2,1)}, bf16[128,2048]{1,0:T(8,128)(2,1)}, u32[]{:S(2)}, u32[]{:S(2)}) collective-permute-start(bf16[128,2048]{1,0:T(8,128)(2,1)} %copy-done.76), channel_id=1, source_target_pairs={{0,1},{1,0},{2,3},{3,2},{4,5},{5,4},{6,7},{7,6},{8,9},{9,8},{10,11... | collective-permute-start | bytes 1572872 | tf_op jit(solution)/shard_map/ppermute | solution.py:438
  392.6 52.6 %collective-permute-start.49 = (bf16[128,2048]{1,0:T(8,128)(2,1)}, bf16[128,2048]{1,0:T(8,128)(2,1)}, u32[]{:S(2)}, u32[]{:S(2)}) collective-permute-start(bf16[128,2048]{1,0:T(8,128)(2,1)} %get-tuple-element.123.refs_1_), channel_id=1, source_target_pairs={{0,4},{2,6},{4,0},{6,2},{8,12},{10,14},{12,8},{14,10},{16,20},{18,... | collective-permute-start | bytes 1572872 | tf_op jit(solution)/shard_map/ppermute | solution.py:430
  396.3 53.4 %collective-permute-start.45 = (bf16[128,2048]{1,0:T(8,128)(2,1)}, bf16[128,2048]{1,0:T(8,128)(2,1)}, u32[]{:S(2)}, u32[]{:S(2)}) collective-permute-start(bf16[128,2048]{1,0:T(8,128)(2,1)} %add_convert_fusion.9), channel_id=1, source_target_pairs={{0,4},{2,6},{4,0},{6,2},{8,12},{10,14},{12,8},{14,10},{16,20},{18,... | collective-permute-start | bytes 1572872 | tf_op jit(solution)/shard_map/ppermute | solution.py:430
  443.4 51.7 %collective-permute-start.59 = (bf16[16,288,128]{2,1,0:T(8,128)(2,1)}, bf16[16,288,128]{2,1,0:T(8,128)(2,1)}, u32[]{:S(2)}, u32[]{:S(2)}) collective-permute-start(bf16[16,288,128]{2,1,0:T(8,128)(2,1)} %get-tuple-element.135.refs_1_), channel_id=1, source_target_pairs={{0,2},{2,0},{4,6},{6,4},{8,10},{10,8},{12,14},{14,12},{16,18},{18,... | collective-permute-start | bytes 3538952 | tf_op jit(solution)/shard_map/ppermute | solution.py:434
  470.8 71.3 %collective-permute-start.60 = (bf16[1,2,704,2048]{3,2,1,0:T(8,128)(2,1)}, bf16[1,2,704,2048]{3,2,1,0:T(8,128)(2,1)}, u32[]{:S(2)}, u32[]{:S(2)}) collective-permute-start(bf16[1,2,704,2048]{3,2,1,0:T(8,128)(2,1)} %shard_map.306.refs_1_), channel_id=1, source_target_pairs={{0,2},{2,0},{4,6},{6,4},{8,10},{10,8},{12,14},{14,12},{16,18},{18,... | collective-permute-start | bytes 17301512 | tf_op jit(solution)/shard_map/ppermute | solution.py:434
  495.1 47.0 %collective-permute-start.61 = (bf16[1,1,704,2048]{3,2,1,0:T(8,128)(2,1)}, bf16[1,1,704,2048]{3,2,1,0:T(8,128)(2,1)}, u32[]{:S(2)}, u32[]{:S(2)}) collective-permute-start(bf16[1,1,704,2048]{3,2,1,0:T(8,128)(2,1)} %shard_map.302.refs_1_), channel_id=1, source_target_pairs={{0,2},{2,0},{4,6},{6,4},{8,10},{10,8},{12,14},{14,12},{16,18},{18,... | collective-permute-start | bytes 8650760 | tf_op jit(solution)/shard_map/ppermute | solution.py:434
  499.3 42.8 %all-to-all-start.1 = ((bf16[16,288,128]{2,1,0:T(8,128)(2,1)}), bf16[16,288,128]{2,1,0:T(8,128)(2,1)}, u32[]{:S(2)}, u32[]{:S(2)}) async-start(bf16[16,288,128]{2,1,0:T(8,128)(2,1)} %add_convert_fusion.1), calls=%async_computation.1 | async-start | bytes 2359296 | tf_op jit(solution)/shard_map/all_to_all | solution.py:1806
  539.8 49.6 %collective-permute-start.63 = (bf16[512,2048]{1,0:T(8,128)(2,1)}, bf16[512,2048]{1,0:T(8,128)(2,1)}, u32[]{:S(2)}, u32[]{:S(2)}) collective-permute-start(bf16[512,2048]{1,0:T(8,128)(2,1)} %shard_map.313), channel_id=1, source_target_pairs={{0,1},{1,0},{2,3},{3,2},{4,5},{5,4},{6,7},{7,6},{8,9},{9,8},{10,11... | collective-permute-start | bytes 6291464 | tf_op jit(solution)/shard_map/ppermute | solution.py:438
  587.9 40.2 %collective-permute-start.62 = (bf16[1024,2176]{1,0:T(8,128)(2,1)}, bf16[1024,2176]{1,0:T(8,128)(2,1)}, u32[]{:S(2)}, u32[]{:S(2)}) collective-permute-start(bf16[1024,2176]{1,0:T(8,128)(2,1)} %shard_map.310), channel_id=1, source_target_pairs={{0,2},{2,0},{4,6},{6,4},{8,10},{10,8},{12,14},{14,12},{16,18},{18,... | collective-permute-start | bytes 13369352 | tf_op jit(solution)/shard_map/ppermute | solution.py:434
  593.2 48.8 %collective-permute-start.64 = (bf16[512,2048]{1,0:T(8,128)(2,1)}, bf16[512,2048]{1,0:T(8,128)(2,1)}, u32[]{:S(2)}, u32[]{:S(2)}) collective-permute-start(bf16[512,2048]{1,0:T(8,128)(2,1)} %add_convert_fusion), channel_id=1, source_target_pairs={{0,4},{2,6},{4,0},{6,2},{8,12},{10,14},{12,8},{14,10},{16,20},{18,... | collective-permute-start | bytes 6291464 | tf_op jit(solution)/shard_map/ppermute | solution.py:430
  594.6 52.9 %collective-permute-start.65 = (bf16[512,2048]{1,0:T(8,128)(2,1)}, bf16[512,2048]{1,0:T(8,128)(2,1)}, u32[]{:S(2)}, u32[]{:S(2)}) collective-permute-start(bf16[512,2048]{1,0:T(8,128)(2,1)} %shard_map.314), channel_id=1, source_target_pairs={{0,1},{1,0},{2,3},{3,2},{4,5},{5,4},{6,7},{7,6},{8,9},{9,8},{10,11... | collective-permute-start | bytes 6291464 | tf_op jit(solution)/shard_map/ppermute | solution.py:438
  633.3 56.4 %collective-permute-start.70 = (bf16[512,2176]{1,0:T(8,128)(2,1)}, bf16[512,2176]{1,0:T(8,128)(2,1)S(1)}, u32[]{:S(2)}, u32[]{:S(2)}) collective-permute-start(bf16[512,2176]{1,0:T(8,128)(2,1)} %shard_map.311.refs_1_), channel_id=1, source_target_pairs={{0,4},{2,6},{4,0},{6,2},{8,12},{10,14},{12,8},{14,10},{16,20},{18,... | collective-permute-start | bytes 6684680 | tf_op jit(solution)/shard_map/ppermute | solution.py:430
  (161 other events, 1969.6 us)

commit v11 on v10

--- a/solution.py
+++ b/solution.py
@@ -1020,15 +1020,22 @@
     return pl.BlockSpec(array.shape, lambda i, where: (0, 0))
 
 
-def grads_call(kernel, specs, operands, scratch, size, width, places, first, count, arrived):
+def grads_call(
+    kernel, specs, operands, scratch, size, width, places, first, count, arrived, others
+):
     extra = [] if arrived is None else [arrived]
     return pl.pallas_call(
-        functools.partial(kernel, len(extra)),
+        lambda *refs: kernel(
+            len(extra),
+            *refs[: 1 + len(operands) + len(extra)],
+            *refs[1 + len(operands) + len(extra) + len(others) :],
+        ),
         grid_spec=pltpu.PrefetchScalarGridSpec(
             num_scalar_prefetch=1,
             grid=(count,),
             in_specs=specs
-            + [pl.BlockSpec((size, width), lambda i, where: (first + i, 0))] * len(extra),
+            + [pl.BlockSpec((size, width), lambda i, where: (first + i, 0))] * len(extra)
+            + in_place(len(others)),
             out_specs=pl.BlockSpec((size, width), lambda i, where: (i, 0)),
             scratch_shapes=scratch,
         ),
@@ -1039,10 +1046,10 @@
             bytes_accessed=4 * count * size * width,
             transcendentals=0,
         ),
-    )(places, *operands, *extra)
-
-
-def first_grads(left, right, small, places, first, count, arrived=None):
+    )(places, *operands, *extra, *others)
+
+
+def first_grads(left, right, small, places, first, count, arrived=None, others=()):
     rows, width = right.shape
     size = left.shape[1] // places.shape[0]
     specs = [
@@ -1051,11 +1058,21 @@
         pl.BlockSpec((small.shape[0], size), lambda i, where: (0, where[first + i])),
     ]
     return grads_call(
-        first_grads_kernel, specs, (left, right, small), [], size, width, places, first, count, arrived
-    )
-
-
-def other_grads(latent, keyval, grad, attended, places, first, count, arrived=None):
+        first_grads_kernel,
+        specs,
+        (left, right, small),
+        [],
+        size,
+        width,
+        places,
+        first,
+        count,
+        arrived,
+        others,
+    )
+
+
+def other_grads(latent, keyval, grad, attended, places, first, count, arrived=None, others=()):
     rows = grad.shape[0]
     blocks = places.shape[0]
     size = grad.shape[1] // blocks
@@ -1079,6 +1096,7 @@
         first,
         count,
         arrived,
+        others,
     )
 
 
@@ -1337,7 +1355,7 @@
     router_ref[...] = dot_rows(logit_ref[...], rows_ref[...])
 
 
-def side_grads(rows, cots, gate, up, hidden, logits, shared, blocks):
+def side_grads(rows, cots, gate, up, hidden, logits, shared, blocks, others):
     total, depth = rows.shape
     column = gate.shape[1] // TILE - 1
     size = depth // blocks
@@ -1346,9 +1364,9 @@
     side = pl.BlockSpec((total, TILE), lambda i: (0, column))
     packed = pl.BlockSpec((2 * TILE // size, 3 * stride, size), lambda i: (i, 0, 0))
     return pl.pallas_call(
-        functools.partial(side_grads_kernel, shared),
+        lambda *refs: side_grads_kernel(shared, *refs[:6], *refs[6 + len(others) :]),
         grid=(depth // (2 * TILE),),
-        in_specs=[wide, wide, side, side, side, whole(logits)],
+        in_specs=[wide, wide, side, side, side, whole(logits)] + in_place(len(others)),
         out_specs=[packed, packed, pl.BlockSpec((logits.shape[1], 2 * TILE), lambda i: (0, i))],
         out_shape=[
             jax.ShapeDtypeStruct((blocks, 3 * stride, size), jnp.float32),
@@ -1361,7 +1379,7 @@
             bytes_accessed=4 * total * depth,
             transcendentals=0,
         ),
-    )(rows, cots, gate, up, hidden, logits)
+    )(rows, cots, gate, up, hidden, logits, *others)
 
 
 def down_kernel(starts, *refs):
@@ -1409,10 +1427,10 @@
     )(*[array for array, _ in pieces], down, *kept, *others)
 
 
-def out_kernel(pieces, *refs):
-    hidden_ref, weight_ref = refs[:2]
-    outs = refs[2 : 2 + pieces]
+def out_kernel(pieces, hidden_ref, weight_ref, *refs):
+    outs, done_ref = refs[-1 - pieces : -1], refs[-1]
     size = hidden_ref.shape[0] // (RINGS * pieces)
+    done_ref[...] = jnp.zeros_like(done_ref)
     for r in range(RINGS):
         part = hidden_ref[r * pieces * size : (r + 1) * pieces * size, :]
         result = wide_dot(part, weight_ref[...]).astype(jnp.bfloat16)
@@ -1420,22 +1438,28 @@
             outs[k][r * size : (r + 1) * size, :] = result[k * size : (k + 1) * size]
 
 
-def out_rows(pieces, hidden, down):
+def out_rows(pieces, half, hidden, down, kept, others):
     rows, width = hidden.shape
     depth = down.shape[1]
-    return pl.pallas_call(
+    steps = depth // (2 * TILE)
+    results = pl.pallas_call(
         functools.partial(out_kernel, pieces),
-        grid=(depth // TILE,),
-        in_specs=[whole(hidden), pl.BlockSpec((width, TILE), lambda i: (0, i))],
-        out_specs=[pl.BlockSpec((rows // pieces, TILE), lambda i: (0, i))] * pieces,
-        out_shape=[jax.ShapeDtypeStruct((rows // pieces, depth), jnp.bfloat16)] * pieces,
+        grid=(steps,),
+        in_specs=[whole(hidden), pl.BlockSpec((width, TILE), lambda i: (0, half * steps + i))]
+        + in_place(len(kept) + len(others)),
+        out_specs=[pl.BlockSpec((rows // pieces, TILE), lambda i: (0, half * steps + i))] * pieces
+        + [pl.BlockSpec((8, 128), lambda i: (0, 0))],
+        out_shape=[jax.ShapeDtypeStruct((rows // pieces, depth), jnp.bfloat16)] * pieces
+        + [jax.ShapeDtypeStruct((8, 128), jnp.float32)],
+        input_output_aliases={2 + k: k for k in range(len(kept))},
         compiler_params=pltpu.CompilerParams(vmem_limit_bytes=48 * 1024 * 1024),
         cost_estimate=pl.CostEstimate(
-            flops=2 * rows * depth * width,
-            bytes_accessed=2 * (rows * depth + depth * width + rows * width),
+            flops=rows * depth * width,
+            bytes_accessed=rows * depth + depth * width + 2 * rows * width,
             transcendentals=0,
         ),
-    )(hidden, down)
+    )(hidden, down, *kept, *others)
+    return results[:-1], results[-1]
 
 
 def mlp_kernel(tiles, starts, others, experts_ref, routed_ref, *refs):
@@ -1676,7 +1700,7 @@
         chunks,
         heads,
         sizes,
-        (grad_ring[3], grad_across[1], grad_across[2], grad_groups[0][1]),
+        (grad_ring[2], grad_across[0], grad_across[1]),
     )
     attn_gain_wide, ffn_gain_wide = gains[0], gains[1]
     mixed = block_input.astype(f32) + own_part + other_x(sent_part).astype(f32)
@@ -1774,6 +1798,7 @@
     first_part = closed[1]
     closed[1] = (after(first_part[0], planes[3][3]),) + tuple(first_part[1:])
     every_row, every_hidden, every_gate_grad, every_up_grad, logit_grads = kept
+    first_total = wide_sum(*closed[1]).astype(bf16)
     shared_kept, shared_sent, logit_rows = side_grads(
         every_row,
         every_grad,
@@ -1783,12 +1808,10 @@
         logit_grads,
         shared,
         blocks,
-    )
-    first_total = wide_sum(*closed[1]).astype(bf16)
-    sent_in = expert_grads(
-        (every_gate_grad, every_up_grad), every_row, units, 1, None, bf16, (first_total,)
-    )
-    sent_down = expert_grads((every_hidden,), every_grad, units, 1, None, bf16)
+        (first_total,),
+    )
+    sent_down = expert_grads((every_hidden,), every_grad, units, 1, None, bf16, (shared_sent,))
+    half_outs, half_done = out_rows(4, 0, every_hidden, down_weight, (), (sent_down,))
     moving = ring_step(first_total)
     moving = ring_step(wide_sum(moving, *closed[2]).astype(bf16))
     own, beside, across = turned[3]
@@ -1796,16 +1819,14 @@
     grad_close = close_plane((own, after(beside, shared_sent), across))
     grad_second = wide_sum(
         ring_step(wide_sum(moving, *grad_close).astype(bf16)),
-        after(closed[0][0], sent_in),
+        after(closed[0][0], half_done),
         *closed[0][1:],
     )
-    arrived_in = other_core(sent_in)
+
     arrived_down = other_core(sent_down)
     router_at = used + 3 - query_width - KVR
     grad_router = logit_rows[router_at : router_at + experts]
-    shared_grads = lax.all_to_all(
-        add_low(shared_kept, other_core(shared_sent)), "dp", split_axis=0, concat_axis=0, tiled=True
-    )
+    shared_came = other_core(shared_sent)
 
     gain_ffn_part = jnp.sum(grad_second * second_unit, axis=0)
     grad_mixed = cotangent.astype(f32) + rms_back(
@@ -1813,10 +1834,10 @@
     )
     grad_mixed_low = grad_mixed.astype(bf16)
     other_grad = other_x(grad_mixed_low)
-    outs = list(out_rows(4, every_hidden, down_weight))
-    outs[3] = after(outs[3], grad_close[2])
+    outs, outs_done = out_rows(4, 1, every_hidden, down_weight, half_outs, (grad_mixed_low,))
+    outs = list(outs)
     outs[2] = after(outs[2], other_grad)
-    out_own, out_beside, out_across = close_plane(turn_corner(outs, "x"))
+    outs[3] = after(outs[3], other_grad)
 
 
     places = jnp.stack([place_of(coords, key_of) for key_of in weight_keys()]).astype(jnp.int32)
@@ -1830,7 +1851,7 @@
         (keyval_weight, output_turned, nope, turned_query, latent, key, keyval, total, latent_gain_row),
         heads,
         first_width,
-        (shared_grads, arrived_in, arrived_down),
+        (arrived_down, shared_came, outs_done),
     )
     grad_attn = jnp.concatenate(
         [
@@ -1841,7 +1862,6 @@
     )
     ring_places = places.reshape(2, 2, RINGS).swapaxes(1, 2).reshape(-1)
     other_parts = (latent_normed, keyval_grad, grad_attn, attended, ring_places)
-    other_arrived = other_core(other_grads(*other_parts, 8, 8))
     own_first, sent_first, gain_attn_part = first_back(
         place, block_input, other_input, projected_grad, first_weight
     )
@@ -1861,11 +1881,20 @@
         axis=0,
     )
     first_parts = (first_normed, projected_grad, small_rows, places)
-    first_arrived = other_core(first_grads(*first_parts, 8, 8))
-    other_kept = other_grads(*other_parts, 0, 8, other_arrived)
+    first_sent = first_grads(*first_parts, 8, 8, None)
+    first_arrived = other_core(first_sent)
+    other_arrived = other_core(other_grads(*other_parts, 8, 8, None, (first_sent,)))
     far = first_grads(*first_parts, 4, 4, first_arrived)
+    other_kept = other_grads(*other_parts, 0, 8, other_arrived, (far,))
+    shared_grads = lax.all_to_all(
+        add_low(after(shared_kept, far), shared_came), "dp", split_axis=0, concat_axis=0, tiled=True
+    )
     from_y = other_y(far)
-    out_total = wide_sum(after(out_own, far), out_beside, out_across)
+    arrived_in = other_core(
+        expert_grads((every_gate_grad, every_up_grad), every_row, units, 1, None, bf16, (far,))
+    )
+    outs[1] = after(outs[1], from_y)
+    out_total = wide_sum(*close_plane(turn_corner(outs, "x")))
     block_output = mixed + ring_sum(
         [out_total[r * local_rows : (r + 1) * local_rows] for r in range(RINGS)], bf16
     )
@@ -1873,7 +1902,6 @@
     other_summed = ring_sum(
         [other_kept[2 * r * depth : 2 * (r + 1) * depth] for r in range(RINGS)], bf16
     )
-    other_closed = other_summed[:depth] + other_y(other_summed[depth:].astype(bf16)).astype(f32)
     grad_expert_down = expert_grads(
         (every_hidden,), every_grad, units, 0, arrived_down, f32, (from_y,)
     )
@@ -1881,6 +1909,9 @@
     grad_expert_in = expert_grads(
         (every_gate_grad, every_up_grad), every_row, units, 0, arrived_in, f32, (near,)
     )
+    other_closed = after(other_summed[:depth], grad_expert_in) + other_y(
+        other_summed[depth:].astype(bf16)
+    ).astype(f32)
     grad_shared_in, grad_shared_down = unpack_shared(shared_grads, shared, (from_y,))
     grad_expert_gate_up = grad_expert_in.swapaxes(2, 3)
     grad_expert_down = grad_expert_down[0]

time: 767 us -> 818 us (1.066)
  local copies, waits for them, and re-layouts: 79.8 us -> 103 us
  starting transfers between devices: 69.9 us -> 85.7 us
  other arithmetic: 53.1 us -> 62.4 us
    ppermute x21, starting transfers between devices: 10 us -> 28 us  [ring_step(): lax.ppermute(values, 'dp', [(i, (i + RINGS) % 16) for i in range(16)])]
    unnamed x241 -> x261, local copies, waits for them, and re-layouts: 61.8 us -> 78.3 us
    ppermute x21, waiting for transfers between devices: 51.9 us -> 36.7 us  [other_y(): return lax.ppermute(values, 'dp', [(i, i ^ 2) for i in range(16)])]
    pallas_call x7 -> x8, Pallas kernels: 62.9 us -> 65.6 us  [the longest x5 27.8 us: grads_call(): pl.pallas_call(lambda *refs: kernel(len(extra), *refs[:1 + len(operands)...]
  transfers between devices with their start and end apart: 82 -> 82, of which waited for: 28 -> 22; matrix products, arithmetic and copies ran while one was open for 11% -> 13% of each run, Pallas kernels for 44% -> 39%
where the time goes in v11:
time: 818 us; the launch traced here: 805 us
  Pallas kernels  338 us (41%)
  waiting for transfers between devices  213 us (26%)
  local copies, waits for them, and re-layouts  103 us (13%)
  starting transfers between devices  85.7 us (10%)
  other arithmetic  62.4 us (8%)
    ppermute x21, waiting for transfers between devices, ring_step(): lax.ppermute(values, 'dp', [(i, (i + RINGS) % 16) for i in range(16)])  135 us
    pallas_call x4, Pallas kernels, mlp_plane(): pl.pallas_call(functools.partial(mlp_kernel, tiles, tuple((start for _, s...  118 us
    unnamed x261, local copies, waits for them, and re-layouts  78.3 us
    pallas_call x4, Pallas kernels, expert_grads(): pl.pallas_call(functools.partial(expert_grads_kernel, units, len(lefts),...  62.8 us
    ppermute x22, waiting for transfers between devices, other_x(): return lax.ppermute(values, 'tensor', [(0, 1), (1, 0)])  41.1 us
    ppermute x21, waiting for transfers between devices, other_y(): return lax.ppermute(values, 'dp', [(i, i ^ 2) for i in range(16)])  36.7 us
    pallas_call x2, Pallas kernels, down_grads(): pl.pallas_call(functools.partial(down_kernel, tuple((start for _, start i...  29.4 us
    ppermute x21, starting transfers between devices, ring_step(): lax.ppermute(values, 'dp', [(i, (i + RINGS) % 16) for i in range(16)])  28 us
  transfers between devices with their start and end apart: 82, of which 22 were waited for; matrix products, arithmetic and copies ran while one was open for 13% of the time, Pallas kernels for 39%

profile of v11, /device:TPU:0, one launch (start us, length us, event | category | flops | bytes accessed | tf_op | source)
XLA Modules:
  0.0 805.2 jit_solution(2862940266881179874)
XLA Ops:
  18.5 20.5 %collective-permute-done.4.refs_4_ = bf16[128,3712]{1,0:T(8,128)(2,1)S(1)} collective-permute-done((bf16[128,3712]{1,0:T(8,128)(2,1)}, bf16[128,3712]{1,0:T(8,128)(2,1)S(1)}, u32[]{:S(2)}, u32[]{:S(2)}) %collective-permute-start.4) | collective-permute-done | bytes 950304 | tf_op jit(solution)/shard_map/ppermute | solution.py:426
  46.3 19.3 %collective-permute-done.10.refs_8_ = bf16[128,3712]{1,0:T(8,128)(2,1)} collective-permute-done((bf16[128,3712]{1,0:T(8,128)(2,1)}, bf16[128,3712]{1,0:T(8,128)(2,1)}, u32[]{:S(2)}, u32[]{:S(2)}) %collective-permute-start.10) | collective-permute-done | bytes 950304 | tf_op jit(solution)/shard_map/ppermute | solution.py:426
  70.8 18.9 %collective-permute-done.12.refs_2_.refs_10_ = bf16[128,3712]{1,0:T(8,128)(2,1)} collective-permute-done((bf16[128,3712]{1,0:T(8,128)(2,1)}, bf16[128,3712]{1,0:T(8,128)(2,1)}, u32[]{:S(2)}, u32[]{:S(2)}) %collective-permute-start.12) | collective-permute-done | bytes 950304 | tf_op jit(solution)/shard_map/ppermute | solution.py:430
  94.6 12.6 %collective-permute-done.18 = bf16[128,2048]{1,0:T(8,128)(2,1)} collective-permute-done((bf16[128,2048]{1,0:T(8,128)(2,1)}, bf16[128,2048]{1,0:T(8,128)(2,1)}, u32[]{:S(2)}, u32[]{:S(2)}) %collective-permute-start.18) | collective-permute-done | bytes 524320 | tf_op jit(solution)/shard_map/ppermute | solution.py:426
  110.2 9.1 %collective-permute-done.19.refs_16_.refs_0_ = bf16[128,2048]{1,0:T(8,128)(2,1)S(1)} collective-permute-done((bf16[128,2048]{1,0:T(8,128)(2,1)}, bf16[128,2048]{1,0:T(8,128)(2,1)S(1)}, u32[]{:S(2)}, u32[]{:S(2)}) %collective-permute-start.19) | collective-permute-done | bytes 524320 | tf_op jit(solution)/shard_map/ppermute | solution.py:426
  124.8 6.8 collective-permute-done.16.refs_14_.refs_1_
  134.3 10.6 %collective-permute-done.34 = bf16[128,2048]{1,0:T(8,128)(2,1)} collective-permute-done((bf16[128,2048]{1,0:T(8,128)(2,1)S(1)}, bf16[128,2048]{1,0:T(8,128)(2,1)}, u32[]{:S(2)}, u32[]{:S(2)}) %collective-permute-start.34) | collective-permute-done | bytes 524320 | tf_op jit(solution)/shard_map/ppermute | solution.py:438
  159.3 22.8 %shard_map.286 = (f32[128,2048]{1,0:T(8,128)}, bf16[128,2048]{1,0:T(8,128)(2,1)S(1)}, bf16[2048,2176]{1,0:T(8,128)(2,1)}, bf16[512,2048]{1,0:T(8,128)(2,1)}, bf1...) custom-call(s32[5]{0:T(128)S(1)} %concatenate.39.place_ref.refs_0_, ...), custom_call_target="tpu_custom_call" | custom-call | flops 4429185024 | bytes 30408704 | tf_op jit(solution)/shard_map/pallas_call | solution.py:802
  192.0 8.0 collective-permute-done.22
  206.9 8.4 %collective-permute-done.35 = bf16[128,2048]{1,0:T(8,128)(2,1)S(1)} collective-permute-done((bf16[128,2048]{1,0:T(8,128)(2,1)S(1)}, bf16[128,2048]{1,0:T(8,128)(2,1)S(1)}, u32[]{:S(2)}, u32[]{:S(2)}) %collective-permute-start.35) | collective-permute-done | bytes 524320 | tf_op jit(solution)/shard_map/ppermute | solution.py:438
  236.4 12.0 %shard_map.289 = (bf16[1792,2048]{1,0:T(8,128)(2,1)}, bf16[1792,2048]{1,0:T(8,128)(2,1)}, bf16[1792,2048]{1,0:T(8,128)(2,1)}) custom-call(bf16[1,2,704,2048]{3,2,1,0:T(8,128)(2,1)S(1)} %bitcast.77, bf16[1,2,704,2048]{3,2,1,0:T(8,128)(2,1)} %collective-permute-done.6.refs_1_.other_in, bf16[1,704,2048]{2,1,0:T(8,128)(2,1)S(1)} %copy-done.44, ...), custom_call_target="tpu_custom_call" | custom-call | bytes 44040192 | tf_op jit(solution)/shard_map/pallas_call | solution.py:1291
  249.3 14.6 %shard_map.291 = (bf16[2048,1792]{1,0:T(8,128)(2,1)}, bf16[2048,2048]{1,0:T(8,128)(2,1)}) custom-call(bf16[256,2048]{1,0:T(8,128)(2,1)} %pad_maximum_fusion.refs_0_.refs_4_, bf16[256,2048]{1,0:T(8,128)(2,1)} %collective-permute-done.37.refs_1_.refs_5_, bf16[256,2048]{1,0:T(8,128)(2,1)S(1)} %copy-done.70, ...), custom_call_target="tpu_custom_call" | custom-call | flops 7516192768 | bytes 19398656 | tf_op jit(solution)/shard_map/pallas_call | solution.py:1405
  268.5 14.8 %shard_map.292 = (bf16[2048,1792]{1,0:T(8,128)(2,1)}, bf16[2048,2048]{1,0:T(8,128)(2,1)}) custom-call(bf16[256,2048]{1,0:T(8,128)(2,1)} %constant_dynamic-update-slice_fusion.4.refs_0_.refs_4_, bf16[256,2048]{1,0:T(8,128)(2,1)} %collective-permute-done.33.refs_1_.refs_5_, ...), custom_call_target="tpu_custom_call", output_to_operand_aliasing={{0}: (9, {}), {1}: (10, {})} | custom-call | flops 7516192768 | bytes 19398656 | tf_op jit(solution)/shard_map/pallas_call | solution.py:1405
  285.4 29.5 %shard_map.293 = (bf16[128,2048]{1,0:T(8,128)(2,1)S(1)}, bf16[128,2048]{1,0:T(8,128)(2,1)}, bf16[128,2048]{1,0:T(8,128)(2,1)S(1)}, bf16[128,2048]{1,0:T(8,128)(2...) custom-call(s32[4]{0:T(128)S(1)} %pad_add_fusion.experts_ref, ...), custom_call_target="tpu_custom_call" | custom-call | flops 15032385536 | bytes 42991616 | tf_op jit(solution)/shard_map/pallas_call | solution.py:1555
  326.1 29.2 %shard_map.294 = (bf16[128,2048]{1,0:T(8,128)(2,1)S(1)}, bf16[128,2048]{1,0:T(8,128)(2,1)S(1)}, bf16[128,2048]{1,0:T(8,128)(2,1)S(1)}, bf16[128,2048]{1,0:T(8,12...) custom-call(s32[4]{0:T(128)S(1)} %pad_add_fusion.experts_ref, ...), custom_call_target="tpu_custom_call", output_to_operand_aliasing={{4}: (12, {}), {5}: (13, {}), {6}: (14, {}), {7}: (15, {}),... | custom-call | flops 15032385536 | bytes 42991616 | tf_op jit(solution)/shard_map/pallas_call | solution.py:1555
  361.9 29.6 %shard_map.295 = (bf16[128,2048]{1,0:T(8,128)(2,1)S(1)}, bf16[128,2048]{1,0:T(8,128)(2,1)}, bf16[128,2048]{1,0:T(8,128)(2,1)S(1)}, bf16[128,2048]{1,0:T(8,128)(2...) custom-call(s32[4]{0:T(128)S(1)} %pad_add_fusion.experts_ref, ...), custom_call_target="tpu_custom_call", output_to_operand_aliasing={{4}: (12, {}), {5}: (13, {}), {6}: (14, {}), {7}: (15, {}),... | custom-call | flops 15032385536 | bytes 42991616 | tf_op jit(solution)/shard_map/pallas_call | solution.py:1555
  397.2 29.4 %shard_map.297 = (bf16[128,2048]{1,0:T(8,128)(2,1)S(1)}, bf16[128,2048]{1,0:T(8,128)(2,1)S(1)}, bf16[128,2048]{1,0:T(8,128)(2,1)S(1)}, bf16[128,2048]{1,0:T(8,12...) custom-call(s32[4]{0:T(128)S(1)} %pad_add_fusion.experts_ref, ...), custom_call_target="tpu_custom_call", output_to_operand_aliasing={{4}: (12, {}), {5}: (13, {}), {6}: (14, {}), {7}: (15, {}),... | custom-call | flops 15032385536 | bytes 42991616 | tf_op jit(solution)/shard_map/pallas_call | solution.py:1555
  436.7 11.9 %shard_map.300 = (f32[16,288,128]{2,1,0:T(8,128)S(1)}, bf16[16,288,128]{2,1,0:T(8,128)(2,1)S(1)}, f32[128,2048]{1,0:T(8,128)S(1)}) custom-call(bf16[2048,2048]{1,0:T(8,128)(2,1)} %get-tuple-element.125.refs_0_.right_ref, bf16[2048,2048]{1,0:T(8,128)(2,1)} %get-tuple-element.124.refs_1_.right_ref, bf16[2048,1792]{1,0:T(8,128)(2,1)} %get-tuple-element.126.refs_2_.refs_0_, ...), custom_call_target="tpu_custom_call" | custom-call | flops 8589934592 | bytes 16777216 | tf_op jit(solution)/shard_map/pallas_call | solution.py:1366
  459.3 10.0 %shard_map.301.refs_0_.refs_1_ = bf16[1,1,704,2048]{3,2,1,0:T(8,128)(2,1)S(1)} custom-call(bf16[2048,2048]{1,0:T(8,128)(2,1)} %get-tuple-element.124.refs_1_.right_ref, bf16[2048,1792]{1,0:T(8,128)(2,1)} %get-tuple-element.123.refs_4_.refs_0_.hidden_ref, bf16[16,288,128]{2,1,0:T(8,128)(2,1)S(1)} %copy-done.65), custom_call_target="tpu_custom_call" | custom-call | flops 6442450944 | bytes 23068672 | tf_op jit(solution)/shard_map/pallas_call | solution.py:1323
  475.6 13.0 %shard_map.302 = (bf16[512,2048]{1,0:T(8,128)(2,1)S(1)}, bf16[512,2048]{1,0:T(8,128)(2,1)S(1)}, bf16[512,2048]{1,0:T(8,128)(2,1)}, bf16[512,2048]{1,0:T(8,128)(2,1)}, f32[8,128]{1,0:T(8,128)S(1)}) custom-call(bf16[2048,1792]{1,0:T(8,128)(2,1)} %get-tuple-element.123.refs_4_.refs_0_.hidden_ref, bf16[1792,2048]{1,0:T(8,128)(2,1)} %get-tuple-element.100.refs_8_.weight_ref, ...), custom_call_target="tpu_custom_call" | custom-call | flops 7516192768 | bytes 15204352 | tf_op jit(solution)/shard_map/pallas_call | solution.py:1445
  498.6 12.9 %shard_map.307 = (bf16[512,2048]{1,0:T(8,128)(2,1)S(1)}, bf16[512,2048]{1,0:T(8,128)(2,1)S(1)}, bf16[512,2048]{1,0:T(8,128)(2,1)}, bf16[512,2048]{1,0:T(8,128)(2,1)}, f32[8,128]{1,0:T(8,128)S(1)}) custom-call(bf16[2048,1792]{1,0:T(8,128)(2,1)} %get-tuple-element.123.refs_4_.refs_0_.hidden_ref, ...), custom_call_target="tpu_custom_call", output_to_operand_aliasing={{0}: (2, {}), {1}: (3, {}), {2}: (4, {}), {3}: (5, {})} | custom-call | flops 7516192768 | bytes 15204352 | tf_op jit(solution)/shard_map/pallas_call | solution.py:1445
  515.8 13.3 %shard_map.308 = (bf16[256,2176]{1,0:T(8,128)(2,1)}, bf16[256,2048]{1,0:T(8,128)(2,1)S(1)}, bf16[256,512]{1,0:T(8,128)(2,1)S(1)}, f32[1,512]{1,0:T(1,128)S(1)}) custom-call(s32[5]{0:T(128)S(1)} %copy-done.90, s32[1,256]{1,0:T(1,128)S(1)} %copy-done.88, s32[256,1]{1,0:T(8,128)S(1)} %copy-done.63, f32[256,256]{1,0:T(8,128)S(1)} %copy-done.47, ...), custom_call_target="tpu_custom_call" | custom-call | flops 3145728000 | bytes 6291456 | tf_op jit(solution)/shard_map/pallas_call | solution.py:944
  537.7 6.9 shard_map.309
  569.9 11.3 %collective-permute-done.69 = bf16[128,2048]{1,0:T(8,128)(2,1)} collective-permute-done((bf16[128,2048]{1,0:T(8,128)(2,1)S(1)}, bf16[128,2048]{1,0:T(8,128)(2,1)}, u32[]{:S(2)}, u32[]{:S(2)}) %collective-permute-start.69) | collective-permute-done | bytes 524320 | tf_op jit(solution)/shard_map/ppermute | solution.py:438
  596.6 6.9 shard_map.317
  610.1 20.0 %shard_map.318 = bf16[1,2,704,2048]{3,2,1,0:T(8,128)(2,1)} custom-call(bf16[2048,2048]{1,0:T(8,128)(2,1)} %get-tuple-element.125.refs_0_.right_ref, bf16[2048,1792]{1,0:T(8,128)(2,1)} %get-tuple-element.126.refs_2_.refs_0_, bf16[2048,1792]{1,0:T(8,128)(2,1)} %get-tuple-element.127.refs_3_.refs_1_, bf16[512,2176]{1,0:T(8,128)(2,1)} %shard_map.311.refs_6_.refs_2_.refs_1_), custom_call_target="tpu_custom_call" | custom-call | flops 12884901888 | bytes 34603008 | tf_op jit(solution)/shard_map/pallas_call | solution.py:1323
  656.3 9.4 %collective-permute-done.70 = bf16[128,2176]{1,0:T(8,128)(2,1)S(1)} collective-permute-done((bf16[128,2176]{1,0:T(8,128)(2,1)}, bf16[128,2176]{1,0:T(8,128)(2,1)S(1)}, u32[]{:S(2)}, u32[]{:S(2)}) %collective-permute-start.70) | collective-permute-done | bytes 557088 | tf_op jit(solution)/shard_map/ppermute | solution.py:426
  671.7 38.6 %collective-permute-done.71 = bf16[128,2176]{1,0:T(8,128)(2,1)S(1)} collective-permute-done((bf16[128,2176]{1,0:T(8,128)(2,1)S(1)}, bf16[128,2176]{1,0:T(8,128)(2,1)S(1)}, u32[]{:S(2)}, u32[]{:S(2)}) %collective-permute-start.71) | collective-permute-done | bytes 557088 | tf_op jit(solution)/shard_map/ppermute | solution.py:426
  716.8 11.5 %shard_map.323 = f32[1,1,704,2048]{3,2,1,0:T(8,128)} custom-call(bf16[2048,2048]{1,0:T(8,128)(2,1)} %get-tuple-element.124.refs_1_.right_ref, bf16[2048,1792]{1,0:T(8,128)(2,1)} %get-tuple-element.123.refs_4_.refs_0_.hidden_ref, bf16[1,1,704,2048]{3,2,1,0:T(8,128)(2,1)S(1)} %copy-done.9, bf16[512,2176]{1,0:T(8,128)(2,1)S(1)} %copy-done.2), custom_call_target="tpu_custom_call" | custom-call | flops 6442450944 | bytes 23068672 | tf_op jit(solution)/shard_map/pallas_call | solution.py:1323
  752.6 8.2 %collective-permute-done.66 = bf16[128,2048]{1,0:T(8,128)(2,1)} collective-permute-done((bf16[128,2048]{1,0:T(8,128)(2,1)}, bf16[128,2048]{1,0:T(8,128)(2,1)}, u32[]{:S(2)}, u32[]{:S(2)}) %collective-permute-start.66) | collective-permute-done | bytes 524320 | tf_op jit(solution)/shard_map/ppermute | solution.py:426
  767.8 8.2 %collective-permute-done.67 = bf16[128,2048]{1,0:T(8,128)(2,1)} collective-permute-done((bf16[128,2048]{1,0:T(8,128)(2,1)S(1)}, bf16[128,2048]{1,0:T(8,128)(2,1)}, u32[]{:S(2)}, u32[]{:S(2)}) %collective-permute-start.67) | collective-permute-done | bytes 524320 | tf_op jit(solution)/shard_map/ppermute | solution.py:426
  778.3 21.2 %shard_map.319.refs_1_ = f32[1,2,704,2048]{3,2,1,0:T(8,128)} custom-call(bf16[2048,2048]{1,0:T(8,128)(2,1)} %get-tuple-element.125.refs_0_.right_ref, bf16[2048,1792]{1,0:T(8,128)(2,1)} %get-tuple-element.126.refs_2_.refs_0_, bf16[2048,1792]{1,0:T(8,128)(2,1)} %get-tuple-element.127.refs_3_.refs_1_, ...), custom_call_target="tpu_custom_call" | custom-call | flops 12884901888 | bytes 34603008 | tf_op jit(solution)/shard_map/pallas_call | solution.py:1323
  (541 shorter events, 303.0 us)
Async XLA Ops:
  0.7 42.5 %collective-permute-start.6 = (bf16[1,2,704,2048]{3,2,1,0:T(8,128)(2,1)}, bf16[1,2,704,2048]{3,2,1,0:T(8,128)(2,1)}, u32[]{:S(2)}, u32[]{:S(2)}) collective-permute-start(bf16[1,2,704,2048]{3,2,1,0:T(8,128)(2,1)} %bitcast.76), channel_id=1, source_target_pairs={{0,2},{2,0},{4,6},{6,4},{8,10},{10,8},{12,14},{14,12},{16,18},{18,... | collective-permute-start | bytes 17301512 | tf_op jit(solution)/shard_map/ppermute | solution.py:434
  1.2 41.9 %collective-permute-start.7 = (bf16[1,704,2048]{2,1,0:T(8,128)(2,1)}, bf16[1,704,2048]{2,1,0:T(8,128)(2,1)S(1)}, u32[]{:S(2)}, u32[]{:S(2)}) collective-permute-start(bf16[1,704,2048]{2,1,0:T(8,128)(2,1)} %own_down.1), channel_id=1, source_target_pairs={{0,2},{2,0},{4,6},{6,4},{8,10},{10,8},{12,14},{14,12},{16,18},{18,... | collective-permute-start | bytes 8650760 | tf_op jit(solution)/shard_map/ppermute | solution.py:434
  70.0 37.4 %collective-permute-start.1 = (bf16[128,3712]{1,0:T(8,128)(2,1)}, bf16[128,3712]{1,0:T(8,128)(2,1)}, u32[]{:S(2)}, u32[]{:S(2)}) collective-permute-start(bf16[128,3712]{1,0:T(8,128)(2,1)} %shard_map.281.refs_0_), channel_id=1, source_target_pairs={{0,2},{2,0},{4,6},{6,4},{8,10},{10,8},{12,14},{14,12},{16,18},{18,... | collective-permute-start | bytes 2850824 | tf_op jit(solution)/shard_map/ppermute | solution.py:434
  147.8 44.2 %all-to-all-start = ((bf16[16,288,128]{2,1,0:T(8,128)(2,1)}), bf16[16,288,128]{2,1,0:T(8,128)(2,1)}, u32[]{:S(2)}, u32[]{:S(2)}) async-start(bf16[16,288,128]{2,1,0:T(8,128)(2,1)} %shard_map.288), calls=%async_computation | async-start | bytes 2359296 | tf_op jit(solution)/shard_map/all_to_all | solution.py:1660
  157.8 90.6 %collective-permute-start.38 = (bf16[256,2048]{1,0:T(8,128)(2,1)}, bf16[256,2048]{1,0:T(8,128)(2,1)}, u32[]{:S(2)}, u32[]{:S(2)}) collective-permute-start(bf16[256,2048]{1,0:T(8,128)(2,1)} %collective-permute-done.37.refs_1_.refs_5_), channel_id=1, source_target_pairs={{0,1},{1,0},{2,3},{3,2},{4,5},{5,4},{6,7},{7,6},{8,9},{9,8},{10,11... | collective-permute-start | bytes 3145736 | tf_op jit(solution)/shard_map/ppermute | solution.py:438
  192.0 38.5 %collective-permute-start.31 = (bf16[16,288,128]{2,1,0:T(8,128)(2,1)}, bf16[16,288,128]{2,1,0:T(8,128)(2,1)}, u32[]{:S(2)}, u32[]{:S(2)}) collective-permute-start(bf16[16,288,128]{2,1,0:T(8,128)(2,1)} %all-to-all-done.near), channel_id=1, source_target_pairs={{0,2},{2,0},{4,6},{6,4},{8,10},{10,8},{12,14},{14,12},{16,18},{18,... | collective-permute-start | bytes 3538952 | tf_op jit(solution)/shard_map/ppermute | solution.py:434
  219.6 45.0 %collective-permute-start.33 = (bf16[256,2048]{1,0:T(8,128)(2,1)}, bf16[256,2048]{1,0:T(8,128)(2,1)}, u32[]{:S(2)}, u32[]{:S(2)}) collective-permute-start(bf16[256,2048]{1,0:T(8,128)(2,1)} %constant_dynamic-update-slice_fusion.4.refs_0_.refs_4_), channel_id=1, source_target_pairs={{0,4},{2,6},{4,0},{6,2},{8,12},{10,14},{12,8},{14,10},{16,20},{18,... | collective-permute-start | bytes 3145736 | tf_op jit(solution)/shard_map/ppermute | solution.py:430
  221.0 47.4 %collective-permute-start.36 = (bf16[256,2048]{1,0:T(8,128)(2,1)}, bf16[256,2048]{1,0:T(8,128)(2,1)}, u32[]{:S(2)}, u32[]{:S(2)}) collective-permute-start(bf16[256,2048]{1,0:T(8,128)(2,1)} %constant_dynamic-update-slice_fusion.6.refs_2_.refs_6_), channel_id=1, source_target_pairs={{0,4},{2,6},{4,0},{6,2},{8,12},{10,14},{12,8},{14,10},{16,20},{18,... | collective-permute-start | bytes 3145736 | tf_op jit(solution)/shard_map/ppermute | solution.py:430
  230.5 55.0 %collective-permute-start.42 = (bf16[128,2048]{1,0:T(8,128)(2,1)}, bf16[128,2048]{1,0:T(8,128)(2,1)S(1)}, u32[]{:S(2)}, u32[]{:S(2)}) collective-permute-start(bf16[128,2048]{1,0:T(8,128)(2,1)} %collective-permute-done.25.refs_2_), channel_id=1, source_target_pairs={{0,4},{2,6},{4,0},{6,2},{8,12},{10,14},{12,8},{14,10},{16,20},{18,... | collective-permute-start | bytes 1572872 | tf_op jit(solution)/shard_map/ppermute | solution.py:430
  263.9 53.2 %collective-permute-start.39 = (bf16[128,2048]{1,0:T(8,128)(2,1)}, bf16[128,2048]{1,0:T(8,128)(2,1)S(1)}, u32[]{:S(2)}, u32[]{:S(2)}) collective-permute-start(bf16[128,2048]{1,0:T(8,128)(2,1)} %collective-permute-done.23.refs_9_.refs_0_), channel_id=1, source_target_pairs={{0,4},{2,6},{4,0},{6,2},{8,12},{10,14},{12,8},{14,10},{16,20},{18,... | collective-permute-start | bytes 1572872 | tf_op jit(solution)/shard_map/ppermute | solution.py:430
  266.1 59.0 %collective-permute-start.41 = (bf16[128,2048]{1,0:T(8,128)(2,1)S(1)}, bf16[128,2048]{1,0:T(8,128)(2,1)S(1)}, u32[]{:S(2)}, u32[]{:S(2)}) collective-permute-start(bf16[128,2048]{1,0:T(8,128)(2,1)S(1)} %collective-permute-done.40.refs_2_), channel_id=1, source_target_pairs={{0,4},{2,6},{4,0},{6,2},{8,12},{10,14},{12,8},{14,10},{16,20},{18,... | collective-permute-start | bytes 1572872 | tf_op jit(solution)/shard_map/ppermute | solution.py:430
  283.3 41.2 %collective-permute-start.28 = (bf16[256,2048]{1,0:T(8,128)(2,1)S(1)}, bf16[256,2048]{1,0:T(8,128)(2,1)S(1)}, u32[]{:S(2)}, u32[]{:S(2)}) collective-permute-start(bf16[256,2048]{1,0:T(8,128)(2,1)S(1)} %constant_dynamic-update-slice_fusion.2.refs_0_), channel_id=1, source_target_pairs={{0,4},{2,6},{4,0},{6,2},{8,12},{10,14},{12,8},{14,10},{16,20},{18,... | collective-permute-start | bytes 3145736 | tf_op jit(solution)/shard_map/ppermute | solution.py:430
  284.8 40.3 %collective-permute-start.29 = (bf16[256,2048]{1,0:T(8,128)(2,1)S(1)}, bf16[256,2048]{1,0:T(8,128)(2,1)S(1)}, u32[]{:S(2)}, u32[]{:S(2)}) collective-permute-start(bf16[256,2048]{1,0:T(8,128)(2,1)S(1)} %constant_dynamic-update-slice_fusion.2.refs_0_), channel_id=1, source_target_pairs={{0,1},{1,0},{2,3},{3,2},{4,5},{5,4},{6,7},{7,6},{8,9},{9,8},{10,11... | collective-permute-start | bytes 3145736 | tf_op jit(solution)/shard_map/ppermute | solution.py:438
  316.5 43.2 %collective-permute-start.43 = (bf16[128,2048]{1,0:T(8,128)(2,1)}, bf16[128,2048]{1,0:T(8,128)(2,1)}, u32[]{:S(2)}, u32[]{:S(2)}) collective-permute-start(bf16[128,2048]{1,0:T(8,128)(2,1)} %get-tuple-element.122), channel_id=1, source_target_pairs={{0,4},{2,6},{4,0},{6,2},{8,12},{10,14},{12,8},{14,10},{16,20},{18,... | collective-permute-start | bytes 1572872 | tf_op jit(solution)/shard_map/ppermute | solution.py:430
  317.1 174.7 %collective-permute-start.56 = (bf16[128,2048]{1,0:T(8,128)(2,1)}, bf16[128,2048]{1,0:T(8,128)(2,1)}, u32[]{:S(2)}, u32[]{:S(2)}) collective-permute-start(bf16[128,2048]{1,0:T(8,128)(2,1)} %get-tuple-element.119.refs_15_), channel_id=1, source_target_pairs={{0,4},{2,6},{4,0},{6,2},{8,12},{10,14},{12,8},{14,10},{16,20},{18,... | collective-permute-start | bytes 1572872 | tf_op jit(solution)/shard_map/ppermute | solution.py:430
  324.5 37.3 %collective-permute-start.30 = (bf16[256,2048]{1,0:T(8,128)(2,1)S(1)}, bf16[256,2048]{1,0:T(8,128)(2,1)}, u32[]{:S(2)}, u32[]{:S(2)}) collective-permute-start(bf16[256,2048]{1,0:T(8,128)(2,1)S(1)} %collective-permute-done.28.refs_15_.refs_1_), channel_id=1, source_target_pairs={{0,1},{1,0},{2,3},{3,2},{4,5},{5,4},{6,7},{7,6},{8,9},{9,8},{10,11... | collective-permute-start | bytes 3145736 | tf_op jit(solution)/shard_map/ppermute | solution.py:438
  357.7 36.8 %collective-permute-start.44 = (bf16[128,2048]{1,0:T(8,128)(2,1)}, bf16[128,2048]{1,0:T(8,128)(2,1)}, u32[]{:S(2)}, u32[]{:S(2)}) collective-permute-start(bf16[128,2048]{1,0:T(8,128)(2,1)} %get-tuple-element.121.refs_1_), channel_id=1, source_target_pairs={{0,1},{1,0},{2,3},{3,2},{4,5},{5,4},{6,7},{7,6},{8,9},{9,8},{10,11... | collective-permute-start | bytes 1572872 | tf_op jit(solution)/shard_map/ppermute | solution.py:438
  359.1 75.0 %collective-permute-start.46 = (bf16[128,2048]{1,0:T(8,128)(2,1)}, bf16[128,2048]{1,0:T(8,128)(2,1)}, u32[]{:S(2)}, u32[]{:S(2)}) collective-permute-start(bf16[128,2048]{1,0:T(8,128)(2,1)} %copy-done.94), channel_id=1, source_target_pairs={{0,1},{1,0},{2,3},{3,2},{4,5},{5,4},{6,7},{7,6},{8,9},{9,8},{10,11... | collective-permute-start | bytes 1572872 | tf_op jit(solution)/shard_map/ppermute | solution.py:438
  393.1 37.5 %collective-permute-start.49 = (bf16[128,2048]{1,0:T(8,128)(2,1)}, bf16[128,2048]{1,0:T(8,128)(2,1)}, u32[]{:S(2)}, u32[]{:S(2)}) collective-permute-start(bf16[128,2048]{1,0:T(8,128)(2,1)} %get-tuple-element.132.refs_1_), channel_id=1, source_target_pairs={{0,4},{2,6},{4,0},{6,2},{8,12},{10,14},{12,8},{14,10},{16,20},{18,... | collective-permute-start | bytes 1572872 | tf_op jit(solution)/shard_map/ppermute | solution.py:430
  396.6 38.0 %collective-permute-start.45 = (bf16[128,2048]{1,0:T(8,128)(2,1)}, bf16[128,2048]{1,0:T(8,128)(2,1)}, u32[]{:S(2)}, u32[]{:S(2)}) collective-permute-start(bf16[128,2048]{1,0:T(8,128)(2,1)} %add_convert_fusion.9), channel_id=1, source_target_pairs={{0,4},{2,6},{4,0},{6,2},{8,12},{10,14},{12,8},{14,10},{16,20},{18,... | collective-permute-start | bytes 1572872 | tf_op jit(solution)/shard_map/ppermute | solution.py:430
  451.8 40.1 %collective-permute-start.57 = (bf16[128,2048]{1,0:T(8,128)(2,1)}, bf16[128,2048]{1,0:T(8,128)(2,1)}, u32[]{:S(2)}, u32[]{:S(2)}) collective-permute-start(bf16[128,2048]{1,0:T(8,128)(2,1)} %add_convert_fusion.10.refs_16_), channel_id=1, source_target_pairs={{0,1},{1,0},{2,3},{3,2},{4,5},{5,4},{6,7},{7,6},{8,9},{9,8},{10,11... | collective-permute-start | bytes 1572872 | tf_op jit(solution)/shard_map/ppermute | solution.py:438
  471.0 43.2 %collective-permute-start.59 = (bf16[1,1,704,2048]{3,2,1,0:T(8,128)(2,1)}, bf16[1,1,704,2048]{3,2,1,0:T(8,128)(2,1)S(1)}, u32[]{:S(2)}, u32[]{:S(2)}) collective-permute-start(bf16[1,1,704,2048]{3,2,1,0:T(8,128)(2,1)} %copy-done.45), channel_id=1, source_target_pairs={{0,2},{2,0},{4,6},{6,4},{8,10},{10,8},{12,14},{14,12},{16,18},{18,... | collective-permute-start | bytes 8650760 | tf_op jit(solution)/shard_map/ppermute | solution.py:434
  471.0 43.2 %collective-permute-start.60 = (bf16[16,288,128]{2,1,0:T(8,128)(2,1)}, bf16[16,288,128]{2,1,0:T(8,128)(2,1)}, u32[]{:S(2)}, u32[]{:S(2)}) collective-permute-start(bf16[16,288,128]{2,1,0:T(8,128)(2,1)} %copy-done.64), channel_id=1, source_target_pairs={{0,2},{2,0},{4,6},{6,4},{8,10},{10,8},{12,14},{14,12},{16,18},{18,... | collective-permute-start | bytes 3538952 | tf_op jit(solution)/shard_map/ppermute | solution.py:434
  567.9 99.3 %collective-permute-start.63 = (bf16[512,2048]{1,0:T(8,128)(2,1)}, bf16[512,2048]{1,0:T(8,128)(2,1)}, u32[]{:S(2)}, u32[]{:S(2)}) collective-permute-start(bf16[512,2048]{1,0:T(8,128)(2,1)} %shard_map.313), channel_id=1, source_target_pairs={{0,1},{1,0},{2,3},{3,2},{4,5},{5,4},{6,7},{7,6},{8,9},{9,8},{10,11... | collective-permute-start | bytes 6291464 | tf_op jit(solution)/shard_map/ppermute | solution.py:438
  568.5 172.9 %collective-permute-start.65 = (bf16[512,2048]{1,0:T(8,128)(2,1)}, bf16[512,2048]{1,0:T(8,128)(2,1)}, u32[]{:S(2)}, u32[]{:S(2)}) collective-permute-start(bf16[512,2048]{1,0:T(8,128)(2,1)} %shard_map.314), channel_id=1, source_target_pairs={{0,1},{1,0},{2,3},{3,2},{4,5},{5,4},{6,7},{7,6},{8,9},{9,8},{10,11... | collective-permute-start | bytes 6291464 | tf_op jit(solution)/shard_map/ppermute | solution.py:438
  588.2 48.9 %collective-permute-start.62 = (bf16[512,2176]{1,0:T(8,128)(2,1)}, bf16[512,2176]{1,0:T(8,128)(2,1)S(1)}, u32[]{:S(2)}, u32[]{:S(2)}) collective-permute-start(bf16[512,2176]{1,0:T(8,128)(2,1)} %shard_map.311.refs_6_.refs_2_.refs_1_), channel_id=1, source_target_pairs={{0,4},{2,6},{4,0},{6,2},{8,12},{10,14},{12,8},{14,10},{16,20},{18,... | collective-permute-start | bytes 6684680 | tf_op jit(solution)/shard_map/ppermute | solution.py:430
  645.9 82.4 %all-to-all-start.1 = ((bf16[16,288,128]{2,1,0:T(8,128)(2,1)}), bf16[16,288,128]{2,1,0:T(8,128)(2,1)S(1)}, u32[]{:S(2)}, u32[]{:S(2)}) async-start(bf16[16,288,128]{2,1,0:T(8,128)(2,1)} %add_convert_fusion.1), calls=%async_computation.1 | async-start | bytes 2359296 | tf_op jit(solution)/shard_map/all_to_all | solution.py:1889
  649.7 128.6 %collective-permute-start.78 = (bf16[1,2,704,2048]{3,2,1,0:T(8,128)(2,1)}, bf16[1,2,704,2048]{3,2,1,0:T(8,128)(2,1)}, u32[]{:S(2)}, u32[]{:S(2)}) collective-permute-start(bf16[1,2,704,2048]{3,2,1,0:T(8,128)(2,1)} %shard_map.318), channel_id=1, source_target_pairs={{0,2},{2,0},{4,6},{6,4},{8,10},{10,8},{12,14},{14,12},{16,18},{18,... | collective-permute-start | bytes 17301512 | tf_op jit(solution)/shard_map/ppermute | solution.py:434
  656.3 76.0 %collective-permute-start.77 = (bf16[256,1536]{1,0:T(8,128)(2,1)}, bf16[256,1536]{1,0:T(8,128)(2,1)}, u32[]{:S(2)}, u32[]{:S(2)}) collective-permute-start(bf16[256,1536]{1,0:T(8,128)(2,1)} %add_convert_fusion.2), channel_id=1, source_target_pairs={{0,8},{2,10},{4,12},{6,14},{8,16},{10,18},{12,20},{14,22},{16,24},... | collective-permute-start | bytes 2359304 | tf_op jit(solution)/shard_map/ppermute | solution.py:426
  667.1 43.2 %collective-permute-start.71 = (bf16[128,2176]{1,0:T(8,128)(2,1)S(1)}, bf16[128,2176]{1,0:T(8,128)(2,1)S(1)}, u32[]{:S(2)}, u32[]{:S(2)}) collective-permute-start(bf16[128,2176]{1,0:T(8,128)(2,1)S(1)} %fusion.3), channel_id=1, source_target_pairs={{0,8},{2,10},{4,12},{6,14},{8,16},{10,18},{12,20},{14,22},{16,24},... | collective-permute-start | bytes 1671176 | tf_op jit(solution)/shard_map/ppermute | solution.py:426
  671.0 70.3 %collective-permute-start.64 = (bf16[512,2048]{1,0:T(8,128)(2,1)}, bf16[512,2048]{1,0:T(8,128)(2,1)}, u32[]{:S(2)}, u32[]{:S(2)}) collective-permute-start(bf16[512,2048]{1,0:T(8,128)(2,1)} %add_convert_fusion), channel_id=1, source_target_pairs={{0,4},{2,6},{4,0},{6,2},{8,12},{10,14},{12,8},{14,10},{16,20},{18,... | collective-permute-start | bytes 6291464 | tf_op jit(solution)/shard_map/ppermute | solution.py:430
  735.6 63.8 %collective-permute-start.79 = (bf16[128,1536]{1,0:T(8,128)(2,1)}, bf16[128,1536]{1,0:T(8,128)(2,1)}, u32[]{:S(2)}, u32[]{:S(2)}) collective-permute-start(bf16[128,1536]{1,0:T(8,128)(2,1)} %slice.200), channel_id=1, source_target_pairs={{0,4},{2,6},{4,0},{6,2},{8,12},{10,14},{12,8},{14,10},{16,20},{18,... | collective-permute-start | bytes 1179656 | tf_op jit(solution)/shard_map/ppermute | solution.py:430
  (171 other events, 2233.6 us)

commit v12 on v11

--- a/solution.py
+++ b/solution.py
@@ -1143,10 +1143,12 @@
     )(place, own, other, grads, weight)
 
 
-def close_ring(near, arrived):
+def close_ring(near, arrived, last):
     size = near.shape[0] // RINGS
     total = near.astype(jnp.float32) + arrived.astype(jnp.float32)
-    return ring_sum([total[r * size : (r + 1) * size] for r in range(RINGS)], jnp.bfloat16)
+    parts = [total[r * size : (r + 1) * size] for r in range(RINGS)]
+    parts[0] = after(parts[0], last)
+    return ring_sum(parts, jnp.bfloat16)
 
 
 def pack_kernel(heads, query_ref, latent_ref, small_ref, keyval_ref, output_ref, out_ref):
@@ -1799,6 +1801,9 @@
     closed[1] = (after(first_part[0], planes[3][3]),) + tuple(first_part[1:])
     every_row, every_hidden, every_gate_grad, every_up_grad, logit_grads = kept
     first_total = wide_sum(*closed[1]).astype(bf16)
+    half_outs, half_done = out_rows(4, 0, every_hidden, down_weight, (), (first_total,))
+    outs, outs_done = out_rows(4, 1, every_hidden, down_weight, half_outs, (half_done,))
+    outs = list(outs)
     shared_kept, shared_sent, logit_rows = side_grads(
         every_row,
         every_grad,
@@ -1808,22 +1813,19 @@
         logit_grads,
         shared,
         blocks,
-        (first_total,),
-    )
-    sent_down = expert_grads((every_hidden,), every_grad, units, 1, None, bf16, (shared_sent,))
-    half_outs, half_done = out_rows(4, 0, every_hidden, down_weight, (), (sent_down,))
+        (outs_done,),
+    )
     moving = ring_step(first_total)
     moving = ring_step(wide_sum(moving, *closed[2]).astype(bf16))
     own, beside, across = turned[3]
-    own = after(own, sent_down)
-    grad_close = close_plane((own, after(beside, shared_sent), across))
+    grad_close = close_plane((after(own, outs_done), after(beside, half_done), across))
     grad_second = wide_sum(
         ring_step(wide_sum(moving, *grad_close).astype(bf16)),
-        after(closed[0][0], half_done),
+        after(closed[0][0], shared_sent),
         *closed[0][1:],
     )
-
-    arrived_down = other_core(sent_down)
+    outs[3] = after(outs[3], grad_close[2])
+
     router_at = used + 3 - query_width - KVR
     grad_router = logit_rows[router_at : router_at + experts]
     shared_came = other_core(shared_sent)
@@ -1834,11 +1836,11 @@
     )
     grad_mixed_low = grad_mixed.astype(bf16)
     other_grad = other_x(grad_mixed_low)
-    outs, outs_done = out_rows(4, 1, every_hidden, down_weight, half_outs, (grad_mixed_low,))
-    outs = list(outs)
     outs[2] = after(outs[2], other_grad)
-    outs[3] = after(outs[3], other_grad)
-
+    sent_down = expert_grads(
+        (every_hidden,), every_grad, units, 1, None, bf16, (grad_mixed_low,)
+    )
+    arrived_down = other_core(sent_down)
 
     places = jnp.stack([place_of(coords, key_of) for key_of in weight_keys()]).astype(jnp.int32)
     projected_grad, keyval_grad, latent_normed, gain_latent_part = attend_back(
@@ -1851,7 +1853,7 @@
         (keyval_weight, output_turned, nope, turned_query, latent, key, keyval, total, latent_gain_row),
         heads,
         first_width,
-        (arrived_down, shared_came, outs_done),
+        (sent_down,),
     )
     grad_attn = jnp.concatenate(
         [
@@ -1881,20 +1883,27 @@
         axis=0,
     )
     first_parts = (first_normed, projected_grad, small_rows, places)
-    first_sent = first_grads(*first_parts, 8, 8, None)
+    outs[1] = after(outs[1], projected_grad)
+    out_turned = turn_corner(outs, "x")
+    first_sent = first_grads(*first_parts, 8, 8, None, (out_turned[1],))
     first_arrived = other_core(first_sent)
     other_arrived = other_core(other_grads(*other_parts, 8, 8, None, (first_sent,)))
-    far = first_grads(*first_parts, 4, 4, first_arrived)
+    shared_grads = lax.all_to_all(
+        add_low(after(shared_kept, projected_grad), shared_came),
+        "dp",
+        split_axis=0,
+        concat_axis=0,
+        tiled=True,
+    )
+    far = first_grads(*first_parts, 4, 4, first_arrived, (shared_grads,))
     other_kept = other_grads(*other_parts, 0, 8, other_arrived, (far,))
-    shared_grads = lax.all_to_all(
-        add_low(after(shared_kept, far), shared_came), "dp", split_axis=0, concat_axis=0, tiled=True
-    )
     from_y = other_y(far)
-    arrived_in = other_core(
-        expert_grads((every_gate_grad, every_up_grad), every_row, units, 1, None, bf16, (far,))
-    )
-    outs[1] = after(outs[1], from_y)
-    out_total = wide_sum(*close_plane(turn_corner(outs, "x")))
+    sent_in = expert_grads(
+        (every_gate_grad, every_up_grad), every_row, units, 1, None, bf16, (far,)
+    )
+    arrived_in = other_core(sent_in)
+    out_own, out_beside, out_across = close_plane(out_turned)
+    out_total = wide_sum(after(out_own, sent_in), out_beside, out_across)
     block_output = mixed + ring_sum(
         [out_total[r * local_rows : (r + 1) * local_rows] for r in range(RINGS)], bf16
     )
@@ -1905,11 +1914,11 @@
     grad_expert_down = expert_grads(
         (every_hidden,), every_grad, units, 0, arrived_down, f32, (from_y,)
     )
-    first_closed = close_ring(near, from_y)
     grad_expert_in = expert_grads(
         (every_gate_grad, every_up_grad), every_row, units, 0, arrived_in, f32, (near,)
     )
-    other_closed = after(other_summed[:depth], grad_expert_in) + other_y(
+    first_closed = close_ring(near, from_y, grad_expert_in)
+    other_closed = other_summed[:depth] + other_y(
         other_summed[depth:].astype(bf16)
     ).astype(f32)
     grad_shared_in, grad_shared_down = unpack_shared(shared_grads, shared, (from_y,))

time: 818 us -> 841 us (1.028)
  waiting for transfers between devices: 213 us -> 263 us
  local copies, waits for them, and re-layouts: 103 us -> 83.8 us
    ppermute x22, waiting for transfers between devices: 41.1 us -> 68 us  [other_x(): return lax.ppermute(values, 'tensor', [(0, 1), (1, 0)])]
    unnamed x261 -> x241, local copies, waits for them, and re-layouts: 78.3 us -> 63.4 us
    all_to_all x1, waiting for transfers between devices: 0.01 us -> 13.5 us  [gather_body(): lax.all_to_all(add_low(after(shared_kept, projected_grad), shared_came),...]
    ppermute x21, waiting for transfers between devices: 36.7 us -> 46.7 us  [other_y(): return lax.ppermute(values, 'dp', [(i, i ^ 2) for i in range(16)])]
    ppermute x21, waiting for transfers between devices: 135 us -> 125 us  [ring_step(): lax.ppermute(values, 'dp', [(i, (i + RINGS) % 16) for i in range(16)])]
    ppermute x16, waiting for transfers between devices: 0.04 us -> 9.09 us  [other_core(): return lax.ppermute(values, 'dp', [(i, i ^ 1) for i in range(16)])]
  transfers between devices with their start and end apart: 82 -> 82, of which waited for: 22 -> 27; matrix products, arithmetic and copies ran while one was open for 13% -> 10% of each run, Pallas kernels for 39% -> 40%
where the time goes in v12:
time: 841 us; the launch traced here: 828 us
  Pallas kernels  336 us (40%)
  waiting for transfers between devices  263 us (31%)
  starting transfers between devices  86.3 us (10%)
  local copies, waits for them, and re-layouts  83.8 us (10%)
  other arithmetic  56.2 us (7%)
    ppermute x21, waiting for transfers between devices, ring_step(): lax.ppermute(values, 'dp', [(i, (i + RINGS) % 16) for i in range(16)])  125 us
    pallas_call x4, Pallas kernels, mlp_plane(): pl.pallas_call(functools.partial(mlp_kernel, tiles, tuple((start for _, s...  117 us
    ppermute x22, waiting for transfers between devices, other_x(): return lax.ppermute(values, 'tensor', [(0, 1), (1, 0)])  68 us
    unnamed x241, local copies, waits for them, and re-layouts  63.4 us
    pallas_call x4, Pallas kernels, expert_grads(): pl.pallas_call(functools.partial(expert_grads_kernel, units, len(lefts),...  63.3 us
    ppermute x21, waiting for transfers between devices, other_y(): return lax.ppermute(values, 'dp', [(i, i ^ 2) for i in range(16)])  46.7 us
    ppermute x21, starting transfers between devices, ring_step(): lax.ppermute(values, 'dp', [(i, (i + RINGS) % 16) for i in range(16)])  29.1 us
    pallas_call x2, Pallas kernels, down_grads(): pl.pallas_call(functools.partial(down_kernel, tuple((start for _, start i...  28.3 us
  transfers between devices with their start and end apart: 82, of which 27 were waited for; matrix products, arithmetic and copies ran while one was open for 10% of the time, Pallas kernels for 40%

profile of v12, /device:TPU:0, one launch (start us, length us, event | category | flops | bytes accessed | tf_op | source)
XLA Modules:
  0.0 828.1 jit_solution(2893493045788984813)
XLA Ops:
  18.5 20.5 %collective-permute-done.4.refs_4_ = bf16[128,3712]{1,0:T(8,128)(2,1)S(1)} collective-permute-done((bf16[128,3712]{1,0:T(8,128)(2,1)}, bf16[128,3712]{1,0:T(8,128)(2,1)S(1)}, u32[]{:S(2)}, u32[]{:S(2)}) %collective-permute-start.4) | collective-permute-done | bytes 950304 | tf_op jit(solution)/shard_map/ppermute | solution.py:426
  46.1 19.3 %collective-permute-done.10.refs_8_ = bf16[128,3712]{1,0:T(8,128)(2,1)} collective-permute-done((bf16[128,3712]{1,0:T(8,128)(2,1)}, bf16[128,3712]{1,0:T(8,128)(2,1)}, u32[]{:S(2)}, u32[]{:S(2)}) %collective-permute-start.10) | collective-permute-done | bytes 950304 | tf_op jit(solution)/shard_map/ppermute | solution.py:426
  70.8 18.8 %collective-permute-done.12.refs_2_.refs_10_ = bf16[128,3712]{1,0:T(8,128)(2,1)} collective-permute-done((bf16[128,3712]{1,0:T(8,128)(2,1)}, bf16[128,3712]{1,0:T(8,128)(2,1)}, u32[]{:S(2)}, u32[]{:S(2)}) %collective-permute-start.12) | collective-permute-done | bytes 950304 | tf_op jit(solution)/shard_map/ppermute | solution.py:430
  94.6 12.5 %collective-permute-done.18 = bf16[128,2048]{1,0:T(8,128)(2,1)} collective-permute-done((bf16[128,2048]{1,0:T(8,128)(2,1)}, bf16[128,2048]{1,0:T(8,128)(2,1)}, u32[]{:S(2)}, u32[]{:S(2)}) %collective-permute-start.18) | collective-permute-done | bytes 524320 | tf_op jit(solution)/shard_map/ppermute | solution.py:426
  110.1 9.1 %collective-permute-done.19.refs_16_.refs_0_ = bf16[128,2048]{1,0:T(8,128)(2,1)S(1)} collective-permute-done((bf16[128,2048]{1,0:T(8,128)(2,1)}, bf16[128,2048]{1,0:T(8,128)(2,1)S(1)}, u32[]{:S(2)}, u32[]{:S(2)}) %collective-permute-start.19) | collective-permute-done | bytes 524320 | tf_op jit(solution)/shard_map/ppermute | solution.py:426
  134.3 10.6 %collective-permute-done.34 = bf16[128,2048]{1,0:T(8,128)(2,1)} collective-permute-done((bf16[128,2048]{1,0:T(8,128)(2,1)S(1)}, bf16[128,2048]{1,0:T(8,128)(2,1)}, u32[]{:S(2)}, u32[]{:S(2)}) %collective-permute-start.34) | collective-permute-done | bytes 524320 | tf_op jit(solution)/shard_map/ppermute | solution.py:438
  159.7 23.2 %shard_map.286 = (f32[128,2048]{1,0:T(8,128)}, bf16[128,2048]{1,0:T(8,128)(2,1)}, bf16[2048,2176]{1,0:T(8,128)(2,1)}, bf16[512,2048]{1,0:T(8,128)(2,1)}, bf16[20...) custom-call(s32[5]{0:T(128)S(1)} %concatenate.39.place_ref.refs_0_, ...), custom_call_target="tpu_custom_call" | custom-call | flops 4429185024 | bytes 30408704 | tf_op jit(solution)/shard_map/pallas_call | solution.py:802
  193.4 8.2 collective-permute-done.22
  208.5 8.6 %collective-permute-done.35 = bf16[128,2048]{1,0:T(8,128)(2,1)S(1)} collective-permute-done((bf16[128,2048]{1,0:T(8,128)(2,1)}, bf16[128,2048]{1,0:T(8,128)(2,1)S(1)}, u32[]{:S(2)}, u32[]{:S(2)}) %collective-permute-start.35) | collective-permute-done | bytes 524320 | tf_op jit(solution)/shard_map/ppermute | solution.py:438
  236.9 11.8 %shard_map.289 = (bf16[1792,2048]{1,0:T(8,128)(2,1)}, bf16[1792,2048]{1,0:T(8,128)(2,1)}, bf16[1792,2048]{1,0:T(8,128)(2,1)}) custom-call(bf16[1,2,704,2048]{3,2,1,0:T(8,128)(2,1)S(1)} %bitcast.77, bf16[1,2,704,2048]{3,2,1,0:T(8,128)(2,1)} %collective-permute-done.6.refs_1_.other_in, bf16[1,704,2048]{2,1,0:T(8,128)(2,1)S(1)} %copy-done.45, ...), custom_call_target="tpu_custom_call" | custom-call | bytes 44040192 | tf_op jit(solution)/shard_map/pallas_call | solution.py:1293
  249.2 14.5 %shard_map.291 = (bf16[2048,1792]{1,0:T(8,128)(2,1)}, bf16[2048,2048]{1,0:T(8,128)(2,1)}) custom-call(bf16[256,2048]{1,0:T(8,128)(2,1)} %pad_maximum_fusion.refs_0_.refs_4_, bf16[256,2048]{1,0:T(8,128)(2,1)} %collective-permute-done.37.refs_1_.refs_5_, bf16[256,2048]{1,0:T(8,128)(2,1)S(1)} %copy-done.67, ...), custom_call_target="tpu_custom_call" | custom-call | flops 7516192768 | bytes 19398656 | tf_op jit(solution)/shard_map/pallas_call | solution.py:1407
  270.3 13.8 %shard_map.292 = (bf16[2048,1792]{1,0:T(8,128)(2,1)}, bf16[2048,2048]{1,0:T(8,128)(2,1)}) custom-call(bf16[256,2048]{1,0:T(8,128)(2,1)S(1)} %copy-done.32, bf16[256,2048]{1,0:T(8,128)(2,1)} %collective-permute-done.33.refs_1_.refs_5_, ...), custom_call_target="tpu_custom_call", output_to_operand_aliasing={{0}: (9, {}), {1}: (10, {})} | custom-call | flops 7516192768 | bytes 19398656 | tf_op jit(solution)/shard_map/pallas_call | solution.py:1407
  286.3 29.5 %shard_map.293 = (bf16[128,2048]{1,0:T(8,128)(2,1)S(1)}, bf16[128,2048]{1,0:T(8,128)(2,1)}, bf16[128,2048]{1,0:T(8,128)(2,1)S(1)}, bf16[128,2048]{1,0:T(8,128)(2...) custom-call(s32[4]{0:T(128)S(1)} %pad_add_fusion.experts_ref, ...), custom_call_target="tpu_custom_call" | custom-call | flops 15032385536 | bytes 42991616 | tf_op jit(solution)/shard_map/pallas_call | solution.py:1557
  328.0 28.2 %shard_map.294 = (bf16[128,2048]{1,0:T(8,128)(2,1)S(1)}, bf16[128,2048]{1,0:T(8,128)(2,1)S(1)}, bf16[128,2048]{1,0:T(8,128)(2,1)S(1)}, bf16[128,2048]{1,0:T(8,12...) custom-call(s32[4]{0:T(128)S(1)} %pad_add_fusion.experts_ref, ...), custom_call_target="tpu_custom_call", output_to_operand_aliasing={{4}: (12, {}), {5}: (13, {}), {6}: (14, {}), {7}: (15, {}),... | custom-call | flops 15032385536 | bytes 42991616 | tf_op jit(solution)/shard_map/pallas_call | solution.py:1557
  362.1 29.6 %shard_map.295 = (bf16[128,2048]{1,0:T(8,128)(2,1)S(1)}, bf16[128,2048]{1,0:T(8,128)(2,1)}, bf16[128,2048]{1,0:T(8,128)(2,1)S(1)}, bf16[128,2048]{1,0:T(8,128)(2...) custom-call(s32[4]{0:T(128)S(1)} %pad_add_fusion.experts_ref, ...), custom_call_target="tpu_custom_call", output_to_operand_aliasing={{4}: (12, {}), {5}: (13, {}), {6}: (14, {}), {7}: (15, {}),... | custom-call | flops 15032385536 | bytes 42991616 | tf_op jit(solution)/shard_map/pallas_call | solution.py:1557
  397.5 29.4 %shard_map.297 = (bf16[128,2048]{1,0:T(8,128)(2,1)S(1)}, bf16[128,2048]{1,0:T(8,128)(2,1)S(1)}, bf16[128,2048]{1,0:T(8,128)(2,1)S(1)}, bf16[128,2048]{1,0:T(8,12...) custom-call(s32[4]{0:T(128)S(1)} %pad_add_fusion.experts_ref, ...), custom_call_target="tpu_custom_call", output_to_operand_aliasing={{4}: (12, {}), {5}: (13, {}), {6}: (14, {}), {7}: (15, {}),... | custom-call | flops 15032385536 | bytes 42991616 | tf_op jit(solution)/shard_map/pallas_call | solution.py:1557
  438.8 12.8 %shard_map.300 = (bf16[512,2048]{1,0:T(8,128)(2,1)S(1)}, bf16[512,2048]{1,0:T(8,128)(2,1)S(1)}, bf16[512,2048]{1,0:T(8,128)(2,1)}, bf16[512,2048]{1,0:T(8,128)(2,1)}, f32[8,128]{1,0:T(8,128)S(1)}) custom-call(bf16[2048,1792]{1,0:T(8,128)(2,1)} %get-tuple-element.123.hidden_ref.refs_4_.refs_0_, bf16[1792,2048]{1,0:T(8,128)(2,1)} %get-tuple-element.100.refs_8_.weight_ref, ...), custom_call_target="tpu_custom_call" | custom-call | flops 7516192768 | bytes 15204352 | tf_op jit(solution)/shard_map/pallas_call | solution.py:1447
  461.6 12.8 %shard_map.301 = (bf16[512,2048]{1,0:T(8,128)(2,1)S(1)}, bf16[512,2048]{1,0:T(8,128)(2,1)S(1)}, bf16[512,2048]{1,0:T(8,128)(2,1)}, bf16[512,2048]{1,0:T(8,128)(2,1)}, f32[8,128]{1,0:T(8,128)S(1)}) custom-call(bf16[2048,1792]{1,0:T(8,128)(2,1)} %get-tuple-element.123.hidden_ref.refs_4_.refs_0_, ...), custom_call_target="tpu_custom_call", output_to_operand_aliasing={{0}: (2, {}), {1}: (3, {}), {2}: (4, {}), {3}: (5, {})} | custom-call | flops 7516192768 | bytes 15204352 | tf_op jit(solution)/shard_map/pallas_call | solution.py:1447
  481.2 12.6 %shard_map.305 = (f32[16,288,128]{2,1,0:T(8,128)S(1)}, bf16[16,288,128]{2,1,0:T(8,128)(2,1)}, f32[128,2048]{1,0:T(8,128)S(1)}) custom-call(bf16[2048,2048]{1,0:T(8,128)(2,1)} %get-tuple-element.135.refs_0_.right_ref, bf16[2048,2048]{1,0:T(8,128)(2,1)} %get-tuple-element.147.refs_1_.right_ref, bf16[2048,1792]{1,0:T(8,128)(2,1)} %get-tuple-element.136.refs_2_.refs_0_, ...), custom_call_target="tpu_custom_call" | custom-call | flops 8589934592 | bytes 16777216 | tf_op jit(solution)/shard_map/pallas_call | solution.py:1368
  503.2 10.1 %shard_map.307.refs_16_ = bf16[1,1,704,2048]{3,2,1,0:T(8,128)(2,1)S(1)} custom-call(bf16[2048,2048]{1,0:T(8,128)(2,1)} %get-tuple-element.147.refs_1_.right_ref, bf16[2048,1792]{1,0:T(8,128)(2,1)} %get-tuple-element.123.hidden_ref.refs_4_.refs_0_, bf16[128,2048]{1,0:T(8,128)(2,1)S(1)} %get-tuple-element.236.refs_1_.refs_5_), custom_call_target="tpu_custom_call" | custom-call | flops 6442450944 | bytes 23068672 | tf_op jit(solution)/shard_map/pallas_call | solution.py:1325
  514.9 29.9 %collective-permute-done.58.refs_6_.refs_1_ = bf16[128,2048]{1,0:T(8,128)(2,1)S(1)} collective-permute-done((bf16[128,2048]{1,0:T(8,128)(2,1)S(1)}, bf16[128,2048]{1,0:T(8,128)(2,1)S(1)}, u32[]{:S(2)}, u32[]{:S(2)}) %collective-permute-start.58) | collective-permute-done | bytes 524320 | tf_op jit(solution)/shard_map/ppermute | solution.py:438
  545.0 13.2 %shard_map.308 = (bf16[256,2176]{1,0:T(8,128)(2,1)}, bf16[256,2048]{1,0:T(8,128)(2,1)S(1)}, bf16[256,512]{1,0:T(8,128)(2,1)S(1)}, f32[1,512]{1,0:T(1,128)S(1)}) custom-call(s32[5]{0:T(128)S(1)} %copy-done.87, s32[1,256]{1,0:T(1,128)S(1)} %copy-done.83, s32[256,1]{1,0:T(8,128)S(1)} %copy-done.62, f32[256,256]{1,0:T(8,128)S(1)} %copy-done.48, ...), custom_call_target="tpu_custom_call" | custom-call | flops 3145728000 | bytes 6291456 | tf_op jit(solution)/shard_map/pallas_call | solution.py:944
  590.6 9.1 %collective-permute-done.61 = bf16[16,288,128]{2,1,0:T(8,128)(2,1)} collective-permute-done((bf16[16,288,128]{2,1,0:T(8,128)(2,1)}, bf16[16,288,128]{2,1,0:T(8,128)(2,1)}, u32[]{:S(2)}, u32[]{:S(2)}) %collective-permute-start.61) | collective-permute-done | bytes 1179680 | tf_op jit(solution)/shard_map/ppermute | solution.py:434
  619.3 13.5 %all-to-all-done.1.refs_5_.packed_ref = bf16[16,288,128]{2,1,0:T(8,128)(2,1)} async-done(((bf16[16,288,128]{2,1,0:T(8,128)(2,1)}), bf16[16,288,128]{2,1,0:T(8,128)(2,1)}, u32[]{:S(2)}, u32[]{:S(2)}) %all-to-all-start.1) | async-done | bytes 1179680 | tf_op jit(solution)/shard_map/all_to_all | solution.py:1891
  638.1 20.0 %shard_map.315.refs_1_ = bf16[1,2,704,2048]{3,2,1,0:T(8,128)(2,1)} custom-call(bf16[2048,2048]{1,0:T(8,128)(2,1)} %get-tuple-element.135.refs_0_.right_ref, bf16[2048,1792]{1,0:T(8,128)(2,1)} %get-tuple-element.136.refs_2_.refs_0_, bf16[2048,1792]{1,0:T(8,128)(2,1)} %get-tuple-element.137.refs_3_.refs_1_, bf16[512,2176]{1,0:T(8,128)(2,1)S(1)} %shard_map.314.refs_2_.refs_6_), custom_call_target="tpu_custom_call" | custom-call | flops 12884901888 | bytes 34603008 | tf_op jit(solution)/shard_map/pallas_call | solution.py:1325
  658.1 11.3 %collective-permute-done.62 = bf16[512,2048]{1,0:T(8,128)(2,1)} collective-permute-done((bf16[512,2048]{1,0:T(8,128)(2,1)}, bf16[512,2048]{1,0:T(8,128)(2,1)}, u32[]{:S(2)}, u32[]{:S(2)}) %collective-permute-start.62) | collective-permute-done | bytes 2097184 | tf_op jit(solution)/shard_map/ppermute | solution.py:430
  692.3 14.7 %collective-permute-done.75 = bf16[256,1536]{1,0:T(8,128)(2,1)S(1)} collective-permute-done((bf16[256,1536]{1,0:T(8,128)(2,1)S(1)}, bf16[256,1536]{1,0:T(8,128)(2,1)S(1)}, u32[]{:S(2)}, u32[]{:S(2)}) %collective-permute-start.75) | collective-permute-done | bytes 786464 | tf_op jit(solution)/shard_map/ppermute | solution.py:426
  720.4 14.7 %collective-permute-done.76 = bf16[256,1536]{1,0:T(8,128)(2,1)S(1)} collective-permute-done((bf16[256,1536]{1,0:T(8,128)(2,1)S(1)}, bf16[256,1536]{1,0:T(8,128)(2,1)S(1)}, u32[]{:S(2)}, u32[]{:S(2)}) %collective-permute-start.76) | collective-permute-done | bytes 786464 | tf_op jit(solution)/shard_map/ppermute | solution.py:426
  737.3 9.0 %collective-permute-done.66 = bf16[128,2048]{1,0:T(8,128)(2,1)S(1)} collective-permute-done((bf16[128,2048]{1,0:T(8,128)(2,1)S(1)}, bf16[128,2048]{1,0:T(8,128)(2,1)S(1)}, u32[]{:S(2)}, u32[]{:S(2)}) %collective-permute-start.66) | collective-permute-done | bytes 524320 | tf_op jit(solution)/shard_map/ppermute | solution.py:426
  752.3 11.9 %shard_map.324 = f32[1,1,704,2048]{3,2,1,0:T(8,128)} custom-call(bf16[2048,2048]{1,0:T(8,128)(2,1)} %get-tuple-element.147.refs_1_.right_ref, bf16[2048,1792]{1,0:T(8,128)(2,1)} %get-tuple-element.123.hidden_ref.refs_4_.refs_0_, bf16[1,1,704,2048]{3,2,1,0:T(8,128)(2,1)} %collective-permute-done.79.refs_1_, ...), custom_call_target="tpu_custom_call" | custom-call | flops 6442450944 | bytes 23068672 | tf_op jit(solution)/shard_map/pallas_call | solution.py:1325
  779.3 12.0 %collective-permute-done.70 = bf16[128,2176]{1,0:T(8,128)(2,1)S(1)} collective-permute-done((bf16[128,2176]{1,0:T(8,128)(2,1)S(1)}, bf16[128,2176]{1,0:T(8,128)(2,1)S(1)}, u32[]{:S(2)}, u32[]{:S(2)}) %collective-permute-start.70) | collective-permute-done | bytes 557088 | tf_op jit(solution)/shard_map/ppermute | solution.py:426
  794.0 21.2 %shard_map.319.refs_1_ = f32[1,2,704,2048]{3,2,1,0:T(8,128)} custom-call(bf16[2048,2048]{1,0:T(8,128)(2,1)} %get-tuple-element.135.refs_0_.right_ref, bf16[2048,1792]{1,0:T(8,128)(2,1)} %get-tuple-element.136.refs_2_.refs_0_, bf16[2048,1792]{1,0:T(8,128)(2,1)} %get-tuple-element.137.refs_3_.refs_1_, ...), custom_call_target="tpu_custom_call" | custom-call | flops 12884901888 | bytes 34603008 | tf_op jit(solution)/shard_map/pallas_call | solution.py:1325
  (521 shorter events, 308.6 us)
Async XLA Ops:
  0.7 42.4 %collective-permute-start.6 = (bf16[1,2,704,2048]{3,2,1,0:T(8,128)(2,1)}, bf16[1,2,704,2048]{3,2,1,0:T(8,128)(2,1)}, u32[]{:S(2)}, u32[]{:S(2)}) collective-permute-start(bf16[1,2,704,2048]{3,2,1,0:T(8,128)(2,1)} %bitcast.76), channel_id=1, source_target_pairs={{0,2},{2,0},{4,6},{6,4},{8,10},{10,8},{12,14},{14,12},{16,18},{18,... | collective-permute-start | bytes 17301512 | tf_op jit(solution)/shard_map/ppermute | solution.py:434
  1.2 41.9 %collective-permute-start.7 = (bf16[1,704,2048]{2,1,0:T(8,128)(2,1)}, bf16[1,704,2048]{2,1,0:T(8,128)(2,1)S(1)}, u32[]{:S(2)}, u32[]{:S(2)}) collective-permute-start(bf16[1,704,2048]{2,1,0:T(8,128)(2,1)} %own_down.1), channel_id=1, source_target_pairs={{0,2},{2,0},{4,6},{6,4},{8,10},{10,8},{12,14},{14,12},{16,18},{18,... | collective-permute-start | bytes 8650760 | tf_op jit(solution)/shard_map/ppermute | solution.py:434
  69.9 37.4 %collective-permute-start.1 = (bf16[128,3712]{1,0:T(8,128)(2,1)}, bf16[128,3712]{1,0:T(8,128)(2,1)}, u32[]{:S(2)}, u32[]{:S(2)}) collective-permute-start(bf16[128,3712]{1,0:T(8,128)(2,1)} %shard_map.281.refs_0_), channel_id=1, source_target_pairs={{0,2},{2,0},{4,6},{6,4},{8,10},{10,8},{12,14},{14,12},{16,18},{18,... | collective-permute-start | bytes 2850824 | tf_op jit(solution)/shard_map/ppermute | solution.py:434
  124.7 34.9 %collective-permute-start.13 = (bf16[128,3712]{1,0:T(8,128)(2,1)}, bf16[128,3712]{1,0:T(8,128)(2,1)}, u32[]{:S(2)}, u32[]{:S(2)}) collective-permute-start(bf16[128,3712]{1,0:T(8,128)(2,1)} %collective-permute-done.12.refs_2_.refs_10_), channel_id=1, source_target_pairs={{0,2},{2,0},{4,6},{6,4},{8,10},{10,8},{12,14},{14,12},{16,18},{18,... | collective-permute-start | bytes 2850824 | tf_op jit(solution)/shard_map/ppermute | solution.py:434
  147.7 45.7 %all-to-all-start = ((bf16[16,288,128]{2,1,0:T(8,128)(2,1)}), bf16[16,288,128]{2,1,0:T(8,128)(2,1)}, u32[]{:S(2)}, u32[]{:S(2)}) async-start(bf16[16,288,128]{2,1,0:T(8,128)(2,1)} %shard_map.288), calls=%async_computation | async-start | bytes 2359296 | tf_op jit(solution)/shard_map/all_to_all | solution.py:1662
  158.1 90.6 %collective-permute-start.38 = (bf16[256,2048]{1,0:T(8,128)(2,1)}, bf16[256,2048]{1,0:T(8,128)(2,1)}, u32[]{:S(2)}, u32[]{:S(2)}) collective-permute-start(bf16[256,2048]{1,0:T(8,128)(2,1)} %collective-permute-done.37.refs_1_.refs_5_), channel_id=1, source_target_pairs={{0,1},{1,0},{2,3},{3,2},{4,5},{5,4},{6,7},{7,6},{8,9},{9,8},{10,11... | collective-permute-start | bytes 3145736 | tf_op jit(solution)/shard_map/ppermute | solution.py:438
  193.4 37.6 %collective-permute-start.31 = (bf16[16,288,128]{2,1,0:T(8,128)(2,1)}, bf16[16,288,128]{2,1,0:T(8,128)(2,1)}, u32[]{:S(2)}, u32[]{:S(2)}) collective-permute-start(bf16[16,288,128]{2,1,0:T(8,128)(2,1)} %all-to-all-done.near), channel_id=1, source_target_pairs={{0,2},{2,0},{4,6},{6,4},{8,10},{10,8},{12,14},{14,12},{16,18},{18,... | collective-permute-start | bytes 3538952 | tf_op jit(solution)/shard_map/ppermute | solution.py:434
  221.4 43.0 %collective-permute-start.33 = (bf16[256,2048]{1,0:T(8,128)(2,1)}, bf16[256,2048]{1,0:T(8,128)(2,1)}, u32[]{:S(2)}, u32[]{:S(2)}) collective-permute-start(bf16[256,2048]{1,0:T(8,128)(2,1)} %copy-done.31), channel_id=1, source_target_pairs={{0,4},{2,6},{4,0},{6,2},{8,12},{10,14},{12,8},{14,10},{16,20},{18,... | collective-permute-start | bytes 3145736 | tf_op jit(solution)/shard_map/ppermute | solution.py:430
  222.8 47.4 %collective-permute-start.36 = (bf16[256,2048]{1,0:T(8,128)(2,1)}, bf16[256,2048]{1,0:T(8,128)(2,1)}, u32[]{:S(2)}, u32[]{:S(2)}) collective-permute-start(bf16[256,2048]{1,0:T(8,128)(2,1)} %constant_dynamic-update-slice_fusion.6.refs_2_.refs_6_), channel_id=1, source_target_pairs={{0,4},{2,6},{4,0},{6,2},{8,12},{10,14},{12,8},{14,10},{16,20},{18,... | collective-permute-start | bytes 3145736 | tf_op jit(solution)/shard_map/ppermute | solution.py:430
  229.5 34.2 %collective-permute-start.26 = (bf16[128,2048]{1,0:T(8,128)(2,1)}, bf16[128,2048]{1,0:T(8,128)(2,1)S(1)}, u32[]{:S(2)}, u32[]{:S(2)}) collective-permute-start(bf16[128,2048]{1,0:T(8,128)(2,1)} %shard_map.287), channel_id=1, source_target_pairs={{0,8},{2,10},{4,12},{6,14},{8,16},{10,18},{12,20},{14,22},{16,24},... | collective-permute-start | bytes 1572872 | tf_op jit(solution)/shard_map/ppermute | solution.py:426
  230.9 55.4 %collective-permute-start.42 = (bf16[128,2048]{1,0:T(8,128)(2,1)}, bf16[128,2048]{1,0:T(8,128)(2,1)S(1)}, u32[]{:S(2)}, u32[]{:S(2)}) collective-permute-start(bf16[128,2048]{1,0:T(8,128)(2,1)} %collective-permute-done.25.refs_2_), channel_id=1, source_target_pairs={{0,4},{2,6},{4,0},{6,2},{8,12},{10,14},{12,8},{14,10},{16,20},{18,... | collective-permute-start | bytes 1572872 | tf_op jit(solution)/shard_map/ppermute | solution.py:430
  263.7 54.4 %collective-permute-start.39 = (bf16[128,2048]{1,0:T(8,128)(2,1)S(1)}, bf16[128,2048]{1,0:T(8,128)(2,1)S(1)}, u32[]{:S(2)}, u32[]{:S(2)}) collective-permute-start(bf16[128,2048]{1,0:T(8,128)(2,1)S(1)} %collective-permute-done.23.refs_9_.refs_0_), channel_id=1, source_target_pairs={{0,4},{2,6},{4,0},{6,2},{8,12},{10,14},{12,8},{14,10},{16,20},{18,... | collective-permute-start | bytes 1572872 | tf_op jit(solution)/shard_map/ppermute | solution.py:430
  265.9 61.1 %collective-permute-start.41 = (bf16[128,2048]{1,0:T(8,128)(2,1)S(1)}, bf16[128,2048]{1,0:T(8,128)(2,1)S(1)}, u32[]{:S(2)}, u32[]{:S(2)}) collective-permute-start(bf16[128,2048]{1,0:T(8,128)(2,1)S(1)} %collective-permute-done.40.refs_2_), channel_id=1, source_target_pairs={{0,4},{2,6},{4,0},{6,2},{8,12},{10,14},{12,8},{14,10},{16,20},{18,... | collective-permute-start | bytes 1572872 | tf_op jit(solution)/shard_map/ppermute | solution.py:430
  284.1 42.2 %collective-permute-start.28 = (bf16[256,2048]{1,0:T(8,128)(2,1)S(1)}, bf16[256,2048]{1,0:T(8,128)(2,1)S(1)}, u32[]{:S(2)}, u32[]{:S(2)}) collective-permute-start(bf16[256,2048]{1,0:T(8,128)(2,1)S(1)} %constant_dynamic-update-slice_fusion.2.refs_0_), channel_id=1, source_target_pairs={{0,4},{2,6},{4,0},{6,2},{8,12},{10,14},{12,8},{14,10},{16,20},{18,... | collective-permute-start | bytes 3145736 | tf_op jit(solution)/shard_map/ppermute | solution.py:430
  285.6 41.4 %collective-permute-start.29 = (bf16[256,2048]{1,0:T(8,128)(2,1)S(1)}, bf16[256,2048]{1,0:T(8,128)(2,1)S(1)}, u32[]{:S(2)}, u32[]{:S(2)}) collective-permute-start(bf16[256,2048]{1,0:T(8,128)(2,1)S(1)} %constant_dynamic-update-slice_fusion.2.refs_0_), channel_id=1, source_target_pairs={{0,1},{1,0},{2,3},{3,2},{4,5},{5,4},{6,7},{7,6},{8,9},{9,8},{10,11... | collective-permute-start | bytes 3145736 | tf_op jit(solution)/shard_map/ppermute | solution.py:438
  317.5 43.3 %collective-permute-start.43 = (bf16[128,2048]{1,0:T(8,128)(2,1)}, bf16[128,2048]{1,0:T(8,128)(2,1)}, u32[]{:S(2)}, u32[]{:S(2)}) collective-permute-start(bf16[128,2048]{1,0:T(8,128)(2,1)} %get-tuple-element.122), channel_id=1, source_target_pairs={{0,4},{2,6},{4,0},{6,2},{8,12},{10,14},{12,8},{14,10},{16,20},{18,... | collective-permute-start | bytes 1572872 | tf_op jit(solution)/shard_map/ppermute | solution.py:430
  318.1 178.3 %collective-permute-start.56 = (bf16[128,2048]{1,0:T(8,128)(2,1)}, bf16[128,2048]{1,0:T(8,128)(2,1)}, u32[]{:S(2)}, u32[]{:S(2)}) collective-permute-start(bf16[128,2048]{1,0:T(8,128)(2,1)} %get-tuple-element.119.refs_15_), channel_id=1, source_target_pairs={{0,4},{2,6},{4,0},{6,2},{8,12},{10,14},{12,8},{14,10},{16,20},{18,... | collective-permute-start | bytes 1572872 | tf_op jit(solution)/shard_map/ppermute | solution.py:430
  326.4 35.7 %collective-permute-start.30 = (bf16[256,2048]{1,0:T(8,128)(2,1)S(1)}, bf16[256,2048]{1,0:T(8,128)(2,1)}, u32[]{:S(2)}, u32[]{:S(2)}) collective-permute-start(bf16[256,2048]{1,0:T(8,128)(2,1)S(1)} %collective-permute-done.28.refs_15_.refs_1_), channel_id=1, source_target_pairs={{0,1},{1,0},{2,3},{3,2},{4,5},{5,4},{6,7},{7,6},{8,9},{9,8},{10,11... | collective-permute-start | bytes 3145736 | tf_op jit(solution)/shard_map/ppermute | solution.py:438
  358.7 36.0 %collective-permute-start.44 = (bf16[128,2048]{1,0:T(8,128)(2,1)}, bf16[128,2048]{1,0:T(8,128)(2,1)}, u32[]{:S(2)}, u32[]{:S(2)}) collective-permute-start(bf16[128,2048]{1,0:T(8,128)(2,1)} %get-tuple-element.121.refs_1_), channel_id=1, source_target_pairs={{0,1},{1,0},{2,3},{3,2},{4,5},{5,4},{6,7},{7,6},{8,9},{9,8},{10,11... | collective-permute-start | bytes 1572872 | tf_op jit(solution)/shard_map/ppermute | solution.py:438
  360.0 74.2 %collective-permute-start.46 = (bf16[128,2048]{1,0:T(8,128)(2,1)}, bf16[128,2048]{1,0:T(8,128)(2,1)}, u32[]{:S(2)}, u32[]{:S(2)}) collective-permute-start(bf16[128,2048]{1,0:T(8,128)(2,1)} %copy-done.93), channel_id=1, source_target_pairs={{0,1},{1,0},{2,3},{3,2},{4,5},{5,4},{6,7},{7,6},{8,9},{9,8},{10,11... | collective-permute-start | bytes 1572872 | tf_op jit(solution)/shard_map/ppermute | solution.py:438
  393.3 37.3 %collective-permute-start.49 = (bf16[128,2048]{1,0:T(8,128)(2,1)}, bf16[128,2048]{1,0:T(8,128)(2,1)}, u32[]{:S(2)}, u32[]{:S(2)}) collective-permute-start(bf16[128,2048]{1,0:T(8,128)(2,1)} %get-tuple-element.127.refs_1_), channel_id=1, source_target_pairs={{0,4},{2,6},{4,0},{6,2},{8,12},{10,14},{12,8},{14,10},{16,20},{18,... | collective-permute-start | bytes 1572872 | tf_op jit(solution)/shard_map/ppermute | solution.py:430
  396.9 38.0 %collective-permute-start.45 = (bf16[128,2048]{1,0:T(8,128)(2,1)}, bf16[128,2048]{1,0:T(8,128)(2,1)}, u32[]{:S(2)}, u32[]{:S(2)}) collective-permute-start(bf16[128,2048]{1,0:T(8,128)(2,1)} %add_convert_fusion.9), channel_id=1, source_target_pairs={{0,4},{2,6},{4,0},{6,2},{8,12},{10,14},{12,8},{14,10},{16,20},{18,... | collective-permute-start | bytes 1572872 | tf_op jit(solution)/shard_map/ppermute | solution.py:430
  452.9 43.6 %collective-permute-start.57 = (bf16[128,2048]{1,0:T(8,128)(2,1)S(1)}, bf16[128,2048]{1,0:T(8,128)(2,1)}, u32[]{:S(2)}, u32[]{:S(2)}) collective-permute-start(bf16[128,2048]{1,0:T(8,128)(2,1)S(1)} %add_convert_fusion.10.refs_16_), channel_id=1, source_target_pairs={{0,1},{1,0},{2,3},{3,2},{4,5},{5,4},{6,7},{7,6},{8,9},{9,8},{10,11... | collective-permute-start | bytes 1572872 | tf_op jit(solution)/shard_map/ppermute | solution.py:438
  495.9 83.1 %collective-permute-start.59 = (bf16[512,2048]{1,0:T(8,128)(2,1)}, bf16[512,2048]{1,0:T(8,128)(2,1)}, u32[]{:S(2)}, u32[]{:S(2)}) collective-permute-start(bf16[512,2048]{1,0:T(8,128)(2,1)} %shard_map.311), channel_id=1, source_target_pairs={{0,1},{1,0},{2,3},{3,2},{4,5},{5,4},{6,7},{7,6},{8,9},{9,8},{10,11... | collective-permute-start | bytes 6291464 | tf_op jit(solution)/shard_map/ppermute | solution.py:438
  502.2 42.7 %collective-permute-start.58 = (bf16[128,2048]{1,0:T(8,128)(2,1)S(1)}, bf16[128,2048]{1,0:T(8,128)(2,1)S(1)}, u32[]{:S(2)}, u32[]{:S(2)}) collective-permute-start(bf16[128,2048]{1,0:T(8,128)(2,1)S(1)} %get-tuple-element.236.refs_1_.refs_5_), channel_id=1, source_target_pairs={{0,1},{1,0},{2,3},{3,2},{4,5},{5,4},{6,7},{7,6},{8,9},{9,8},{10,11... | collective-permute-start | bytes 1572872 | tf_op jit(solution)/shard_map/ppermute | solution.py:438
  615.2 62.1 %collective-permute-start.74 = (bf16[1024,1536]{1,0:T(8,128)(2,1)}, bf16[1024,1536]{1,0:T(8,128)(2,1)}, u32[]{:S(2)}, u32[]{:S(2)}) collective-permute-start(bf16[1024,1536]{1,0:T(8,128)(2,1)} %shard_map.321), channel_id=1, source_target_pairs={{0,2},{2,0},{4,6},{6,4},{8,10},{10,8},{12,14},{14,12},{16,18},{18,... | collective-permute-start | bytes 9437192 | tf_op jit(solution)/shard_map/ppermute | solution.py:434
  615.5 53.9 %collective-permute-start.62 = (bf16[512,2048]{1,0:T(8,128)(2,1)}, bf16[512,2048]{1,0:T(8,128)(2,1)}, u32[]{:S(2)}, u32[]{:S(2)}) collective-permute-start(bf16[512,2048]{1,0:T(8,128)(2,1)} %add_convert_fusion.refs_4_), channel_id=1, source_target_pairs={{0,4},{2,6},{4,0},{6,2},{8,12},{10,14},{12,8},{14,10},{16,20},{18,... | collective-permute-start | bytes 6291464 | tf_op jit(solution)/shard_map/ppermute | solution.py:430
  617.2 52.2 %collective-permute-start.63 = (bf16[512,2048]{1,0:T(8,128)(2,1)}, bf16[512,2048]{1,0:T(8,128)(2,1)}, u32[]{:S(2)}, u32[]{:S(2)}) collective-permute-start(bf16[512,2048]{1,0:T(8,128)(2,1)} %shard_map.317), channel_id=1, source_target_pairs={{0,1},{1,0},{2,3},{3,2},{4,5},{5,4},{6,7},{7,6},{8,9},{9,8},{10,11... | collective-permute-start | bytes 6291464 | tf_op jit(solution)/shard_map/ppermute | solution.py:438
  617.9 134.4 %collective-permute-start.79 = (bf16[1,1,704,2048]{3,2,1,0:T(8,128)(2,1)}, bf16[1,1,704,2048]{3,2,1,0:T(8,128)(2,1)}, u32[]{:S(2)}, u32[]{:S(2)}) collective-permute-start(bf16[1,1,704,2048]{3,2,1,0:T(8,128)(2,1)} %copy-done.46), channel_id=1, source_target_pairs={{0,2},{2,0},{4,6},{6,4},{8,10},{10,8},{12,14},{14,12},{16,18},{18,... | collective-permute-start | bytes 8650760 | tf_op jit(solution)/shard_map/ppermute | solution.py:434
  618.3 66.3 %collective-permute-start.67 = (bf16[128,2048]{1,0:T(8,128)(2,1)S(1)}, bf16[128,2048]{1,0:T(8,128)(2,1)}, u32[]{:S(2)}, u32[]{:S(2)}) collective-permute-start(bf16[128,2048]{1,0:T(8,128)(2,1)S(1)} %copy-done.91), channel_id=1, source_target_pairs={{0,1},{1,0},{2,3},{3,2},{4,5},{5,4},{6,7},{7,6},{8,9},{9,8},{10,11... | collective-permute-start | bytes 1572872 | tf_op jit(solution)/shard_map/ppermute | solution.py:438
  687.7 59.8 %collective-permute-start.68 = (bf16[512,2176]{1,0:T(8,128)(2,1)S(1)}, bf16[512,2176]{1,0:T(8,128)(2,1)S(1)}, u32[]{:S(2)}, u32[]{:S(2)}) collective-permute-start(bf16[512,2176]{1,0:T(8,128)(2,1)S(1)} %copy-done.23), channel_id=1, source_target_pairs={{0,4},{2,6},{4,0},{6,2},{8,12},{10,14},{12,8},{14,10},{16,20},{18,... | collective-permute-start | bytes 6684680 | tf_op jit(solution)/shard_map/ppermute | solution.py:430
  711.7 82.3 %collective-permute-start.72 = (bf16[1,2,704,2048]{3,2,1,0:T(8,128)(2,1)}, bf16[1,2,704,2048]{3,2,1,0:T(8,128)(2,1)}, u32[]{:S(2)}, u32[]{:S(2)}) collective-permute-start(bf16[1,2,704,2048]{3,2,1,0:T(8,128)(2,1)} %shard_map.315.refs_1_), channel_id=1, source_target_pairs={{0,2},{2,0},{4,6},{6,4},{8,10},{10,8},{12,14},{14,12},{16,18},{18,... | collective-permute-start | bytes 17301512 | tf_op jit(solution)/shard_map/ppermute | solution.py:434
  (161 other events, 2659.8 us)

commit v13 on v11

--- a/solution.py
+++ b/solution.py
@@ -1143,10 +1143,12 @@
     )(place, own, other, grads, weight)
 
 
-def close_ring(near, arrived):
+def close_ring(near, arrived, last):
     size = near.shape[0] // RINGS
     total = near.astype(jnp.float32) + arrived.astype(jnp.float32)
-    return ring_sum([total[r * size : (r + 1) * size] for r in range(RINGS)], jnp.bfloat16)
+    parts = [total[r * size : (r + 1) * size] for r in range(RINGS)]
+    parts[0] = after(parts[0], last)
+    return ring_sum(parts, jnp.bfloat16)
 
 
 def pack_kernel(heads, query_ref, latent_ref, small_ref, keyval_ref, output_ref, out_ref):
@@ -1887,29 +1889,34 @@
     far = first_grads(*first_parts, 4, 4, first_arrived)
     other_kept = other_grads(*other_parts, 0, 8, other_arrived, (far,))
     shared_grads = lax.all_to_all(
-        add_low(after(shared_kept, far), shared_came), "dp", split_axis=0, concat_axis=0, tiled=True
+        add_low(after(shared_kept, projected_grad), shared_came),
+        "dp",
+        split_axis=0,
+        concat_axis=0,
+        tiled=True,
     )
     from_y = other_y(far)
     arrived_in = other_core(
         expert_grads((every_gate_grad, every_up_grad), every_row, units, 1, None, bf16, (far,))
     )
     outs[1] = after(outs[1], from_y)
-    out_total = wide_sum(*close_plane(turn_corner(outs, "x")))
+    near = first_grads(*first_parts, 0, 4, first_arrived, (shared_grads,))
+    other_summed = ring_sum(
+        [other_kept[2 * r * depth : 2 * (r + 1) * depth] for r in range(RINGS)], bf16
+    )
+    grad_expert_down = expert_grads(
+        (every_hidden,), every_grad, units, 0, arrived_down, f32, (from_y,)
+    )
+    grad_expert_in = expert_grads(
+        (every_gate_grad, every_up_grad), every_row, units, 0, arrived_in, f32, (near,)
+    )
+    first_closed = close_ring(near, from_y, grad_expert_in)
+    out_own, out_beside, out_across = close_plane(turn_corner(outs, "x"))
+    out_total = wide_sum(after(out_own, first_closed), out_beside, out_across)
     block_output = mixed + ring_sum(
         [out_total[r * local_rows : (r + 1) * local_rows] for r in range(RINGS)], bf16
     )
-    near = first_grads(*first_parts, 0, 4, first_arrived)
-    other_summed = ring_sum(
-        [other_kept[2 * r * depth : 2 * (r + 1) * depth] for r in range(RINGS)], bf16
-    )
-    grad_expert_down = expert_grads(
-        (every_hidden,), every_grad, units, 0, arrived_down, f32, (from_y,)
-    )
-    first_closed = close_ring(near, from_y)
-    grad_expert_in = expert_grads(
-        (every_gate_grad, every_up_grad), every_row, units, 0, arrived_in, f32, (near,)
-    )
-    other_closed = after(other_summed[:depth], grad_expert_in) + other_y(
+    other_closed = other_summed[:depth] + other_y(
         other_summed[depth:].astype(bf16)
     ).astype(f32)
     grad_shared_in, grad_shared_down = unpack_shared(shared_grads, shared, (from_y,))

time: 818 us -> 785 us (0.960)
  waiting for transfers between devices: 213 us -> 188 us
  local copies, waits for them, and re-layouts: 103 us -> 94.4 us
    ppermute x21, waiting for transfers between devices: 135 us -> 123 us  [ring_step(): lax.ppermute(values, 'dp', [(i, (i + RINGS) % 16) for i in range(16)])]
    ppermute x22, waiting for transfers between devices: 41.1 us -> 32.9 us  [other_x(): return lax.ppermute(values, 'tensor', [(0, 1), (1, 0)])]
    unnamed x261 -> x255, local copies, waits for them, and re-layouts: 78.3 us -> 73.8 us
  transfers between devices with their start and end apart: 82 -> 82, of which waited for: 22 -> 22; matrix products, arithmetic and copies ran while one was open for 13% -> 13% of each run, Pallas kernels for 39% -> 40%
where the time goes in v13:
time: 785 us; the launch traced here: 773 us
  Pallas kernels  337 us (43%)
  waiting for transfers between devices  188 us (24%)
  local copies, waits for them, and re-layouts  94.4 us (12%)
  starting transfers between devices  83.4 us (11%)
  other arithmetic  66.4 us (8%)
    ppermute x21, waiting for transfers between devices, ring_step(): lax.ppermute(values, 'dp', [(i, (i + RINGS) % 16) for i in range(16)])  123 us
    pallas_call x4, Pallas kernels, mlp_plane(): pl.pallas_call(functools.partial(mlp_kernel, tiles, tuple((start for _, s...  118 us
    unnamed x255, local copies, waits for them, and re-layouts  73.8 us
    pallas_call x4, Pallas kernels, expert_grads(): pl.pallas_call(functools.partial(expert_grads_kernel, units, len(lefts),...  61.9 us
    ppermute x22, waiting for transfers between devices, other_x(): return lax.ppermute(values, 'tensor', [(0, 1), (1, 0)])  32.9 us
    ppermute x21, waiting for transfers between devices, other_y(): return lax.ppermute(values, 'dp', [(i, i ^ 2) for i in range(16)])  32.6 us
    pallas_call x2, Pallas kernels, down_grads(): pl.pallas_call(functools.partial(down_kernel, tuple((start for _, start i...  29.4 us
    pallas_call x5, Pallas kernels, grads_call(): pl.pallas_call(lambda *refs: kernel(len(extra), *refs[:1 + len(operands)...  27.5 us
  transfers between devices with their start and end apart: 82, of which 22 were waited for; matrix products, arithmetic and copies ran while one was open for 13% of the time, Pallas kernels for 40%

profile of v13, /device:TPU:0, one launch (start us, length us, event | category | flops | bytes accessed | tf_op | source)
XLA Modules:
  0.0 772.6 jit_solution(9119666406862695138)
XLA Ops:
  18.5 20.5 %collective-permute-done.4.refs_4_ = bf16[128,3712]{1,0:T(8,128)(2,1)S(1)} collective-permute-done((bf16[128,3712]{1,0:T(8,128)(2,1)}, bf16[128,3712]{1,0:T(8,128)(2,1)S(1)}, u32[]{:S(2)}, u32[]{:S(2)}) %collective-permute-start.4) | collective-permute-done | bytes 950304 | tf_op jit(solution)/shard_map/ppermute | solution.py:426
  46.3 19.3 %collective-permute-done.10.refs_8_ = bf16[128,3712]{1,0:T(8,128)(2,1)} collective-permute-done((bf16[128,3712]{1,0:T(8,128)(2,1)}, bf16[128,3712]{1,0:T(8,128)(2,1)}, u32[]{:S(2)}, u32[]{:S(2)}) %collective-permute-start.10) | collective-permute-done | bytes 950304 | tf_op jit(solution)/shard_map/ppermute | solution.py:426
  70.8 18.9 %collective-permute-done.12.refs_2_.refs_10_ = bf16[128,3712]{1,0:T(8,128)(2,1)} collective-permute-done((bf16[128,3712]{1,0:T(8,128)(2,1)}, bf16[128,3712]{1,0:T(8,128)(2,1)}, u32[]{:S(2)}, u32[]{:S(2)}) %collective-permute-start.12) | collective-permute-done | bytes 950304 | tf_op jit(solution)/shard_map/ppermute | solution.py:430
  94.6 12.6 %collective-permute-done.18 = bf16[128,2048]{1,0:T(8,128)(2,1)} collective-permute-done((bf16[128,2048]{1,0:T(8,128)(2,1)}, bf16[128,2048]{1,0:T(8,128)(2,1)}, u32[]{:S(2)}, u32[]{:S(2)}) %collective-permute-start.18) | collective-permute-done | bytes 524320 | tf_op jit(solution)/shard_map/ppermute | solution.py:426
  110.2 9.1 %collective-permute-done.19.refs_16_.refs_0_ = bf16[128,2048]{1,0:T(8,128)(2,1)S(1)} collective-permute-done((bf16[128,2048]{1,0:T(8,128)(2,1)}, bf16[128,2048]{1,0:T(8,128)(2,1)S(1)}, u32[]{:S(2)}, u32[]{:S(2)}) %collective-permute-start.19) | collective-permute-done | bytes 524320 | tf_op jit(solution)/shard_map/ppermute | solution.py:426
  124.8 6.8 collective-permute-done.16.refs_14_.refs_1_
  134.3 10.6 %collective-permute-done.34 = bf16[128,2048]{1,0:T(8,128)(2,1)} collective-permute-done((bf16[128,2048]{1,0:T(8,128)(2,1)S(1)}, bf16[128,2048]{1,0:T(8,128)(2,1)}, u32[]{:S(2)}, u32[]{:S(2)}) %collective-permute-start.34) | collective-permute-done | bytes 524320 | tf_op jit(solution)/shard_map/ppermute | solution.py:438
  159.3 22.8 %shard_map.286 = (f32[128,2048]{1,0:T(8,128)}, bf16[128,2048]{1,0:T(8,128)(2,1)S(1)}, bf16[2048,2176]{1,0:T(8,128)(2,1)}, bf16[512,2048]{1,0:T(8,128)(2,1)}, bf1...) custom-call(s32[5]{0:T(128)S(1)} %concatenate.39.place_ref.refs_0_, ...), custom_call_target="tpu_custom_call" | custom-call | flops 4429185024 | bytes 30408704 | tf_op jit(solution)/shard_map/pallas_call | solution.py:802
  192.0 8.0 %collective-permute-done.22 = bf16[128,2048]{1,0:T(8,128)(2,1)} collective-permute-done((bf16[128,2048]{1,0:T(8,128)(2,1)S(1)}, bf16[128,2048]{1,0:T(8,128)(2,1)}, u32[]{:S(2)}, u32[]{:S(2)}) %collective-permute-start.22) | collective-permute-done | bytes 524320 | tf_op jit(solution)/shard_map/ppermute | solution.py:438
  207.0 8.4 %collective-permute-done.35 = bf16[128,2048]{1,0:T(8,128)(2,1)S(1)} collective-permute-done((bf16[128,2048]{1,0:T(8,128)(2,1)S(1)}, bf16[128,2048]{1,0:T(8,128)(2,1)S(1)}, u32[]{:S(2)}, u32[]{:S(2)}) %collective-permute-start.35) | collective-permute-done | bytes 524320 | tf_op jit(solution)/shard_map/ppermute | solution.py:438
  236.5 12.0 %shard_map.289 = (bf16[1792,2048]{1,0:T(8,128)(2,1)}, bf16[1792,2048]{1,0:T(8,128)(2,1)}, bf16[1792,2048]{1,0:T(8,128)(2,1)}) custom-call(bf16[1,2,704,2048]{3,2,1,0:T(8,128)(2,1)S(1)} %bitcast.77, bf16[1,2,704,2048]{3,2,1,0:T(8,128)(2,1)} %collective-permute-done.6.refs_1_.other_in, bf16[1,704,2048]{2,1,0:T(8,128)(2,1)S(1)} %copy-done.46, ...), custom_call_target="tpu_custom_call" | custom-call | bytes 44040192 | tf_op jit(solution)/shard_map/pallas_call | solution.py:1293
  249.3 14.6 %shard_map.291 = (bf16[2048,1792]{1,0:T(8,128)(2,1)}, bf16[2048,2048]{1,0:T(8,128)(2,1)}) custom-call(bf16[256,2048]{1,0:T(8,128)(2,1)} %pad_maximum_fusion.refs_0_.refs_4_, bf16[256,2048]{1,0:T(8,128)(2,1)} %collective-permute-done.37.refs_1_.refs_5_, bf16[256,2048]{1,0:T(8,128)(2,1)S(1)} %copy-done.68, ...), custom_call_target="tpu_custom_call" | custom-call | flops 7516192768 | bytes 19398656 | tf_op jit(solution)/shard_map/pallas_call | solution.py:1407
  268.5 14.8 %shard_map.292 = (bf16[2048,1792]{1,0:T(8,128)(2,1)}, bf16[2048,2048]{1,0:T(8,128)(2,1)}) custom-call(bf16[256,2048]{1,0:T(8,128)(2,1)} %constant_dynamic-update-slice_fusion.4.refs_0_.refs_4_, bf16[256,2048]{1,0:T(8,128)(2,1)} %collective-permute-done.33.refs_1_.refs_5_, ...), custom_call_target="tpu_custom_call", output_to_operand_aliasing={{0}: (9, {}), {1}: (10, {})} | custom-call | flops 7516192768 | bytes 19398656 | tf_op jit(solution)/shard_map/pallas_call | solution.py:1407
  285.5 29.5 %shard_map.293 = (bf16[128,2048]{1,0:T(8,128)(2,1)S(1)}, bf16[128,2048]{1,0:T(8,128)(2,1)}, bf16[128,2048]{1,0:T(8,128)(2,1)S(1)}, bf16[128,2048]{1,0:T(8,128)(2...) custom-call(s32[4]{0:T(128)S(1)} %pad_add_fusion.experts_ref, ...), custom_call_target="tpu_custom_call" | custom-call | flops 15032385536 | bytes 42991616 | tf_op jit(solution)/shard_map/pallas_call | solution.py:1557
  326.2 29.2 %shard_map.294 = (bf16[128,2048]{1,0:T(8,128)(2,1)S(1)}, bf16[128,2048]{1,0:T(8,128)(2,1)S(1)}, bf16[128,2048]{1,0:T(8,128)(2,1)S(1)}, bf16[128,2048]{1,0:T(8,12...) custom-call(s32[4]{0:T(128)S(1)} %pad_add_fusion.experts_ref, ...), custom_call_target="tpu_custom_call", output_to_operand_aliasing={{4}: (12, {}), {5}: (13, {}), {6}: (14, {}), {7}: (15, {}),... | custom-call | flops 15032385536 | bytes 42991616 | tf_op jit(solution)/shard_map/pallas_call | solution.py:1557
  361.9 29.6 %shard_map.295 = (bf16[128,2048]{1,0:T(8,128)(2,1)S(1)}, bf16[128,2048]{1,0:T(8,128)(2,1)}, bf16[128,2048]{1,0:T(8,128)(2,1)S(1)}, bf16[128,2048]{1,0:T(8,128)(2...) custom-call(s32[4]{0:T(128)S(1)} %pad_add_fusion.experts_ref, ...), custom_call_target="tpu_custom_call", output_to_operand_aliasing={{4}: (12, {}), {5}: (13, {}), {6}: (14, {}), {7}: (15, {}),... | custom-call | flops 15032385536 | bytes 42991616 | tf_op jit(solution)/shard_map/pallas_call | solution.py:1557
  397.3 29.4 %shard_map.297 = (bf16[128,2048]{1,0:T(8,128)(2,1)S(1)}, bf16[128,2048]{1,0:T(8,128)(2,1)S(1)}, bf16[128,2048]{1,0:T(8,128)(2,1)S(1)}, bf16[128,2048]{1,0:T(8,12...) custom-call(s32[4]{0:T(128)S(1)} %pad_add_fusion.experts_ref, ...), custom_call_target="tpu_custom_call", output_to_operand_aliasing={{4}: (12, {}), {5}: (13, {}), {6}: (14, {}), {7}: (15, {}),... | custom-call | flops 15032385536 | bytes 42991616 | tf_op jit(solution)/shard_map/pallas_call | solution.py:1557
  436.8 11.9 %shard_map.300 = (f32[16,288,128]{2,1,0:T(8,128)S(1)}, bf16[16,288,128]{2,1,0:T(8,128)(2,1)S(1)}, f32[128,2048]{1,0:T(8,128)S(1)}) custom-call(bf16[2048,2048]{1,0:T(8,128)(2,1)} %get-tuple-element.125.refs_0_.right_ref, bf16[2048,2048]{1,0:T(8,128)(2,1)} %get-tuple-element.124.refs_1_.right_ref, bf16[2048,1792]{1,0:T(8,128)(2,1)} %get-tuple-element.126.refs_2_.refs_0_, ...), custom_call_target="tpu_custom_call" | custom-call | flops 8589934592 | bytes 16777216 | tf_op jit(solution)/shard_map/pallas_call | solution.py:1368
  459.3 10.0 %shard_map.301.refs_0_.refs_1_ = bf16[1,1,704,2048]{3,2,1,0:T(8,128)(2,1)S(1)} custom-call(bf16[2048,2048]{1,0:T(8,128)(2,1)} %get-tuple-element.124.refs_1_.right_ref, bf16[2048,1792]{1,0:T(8,128)(2,1)} %get-tuple-element.123.refs_4_.refs_0_.hidden_ref, bf16[16,288,128]{2,1,0:T(8,128)(2,1)S(1)} %copy-done.63), custom_call_target="tpu_custom_call" | custom-call | flops 6442450944 | bytes 23068672 | tf_op jit(solution)/shard_map/pallas_call | solution.py:1325
  475.6 13.0 %shard_map.302 = (bf16[512,2048]{1,0:T(8,128)(2,1)S(1)}, bf16[512,2048]{1,0:T(8,128)(2,1)S(1)}, bf16[512,2048]{1,0:T(8,128)(2,1)}, bf16[512,2048]{1,0:T(8,128)(2,1)}, f32[8,128]{1,0:T(8,128)S(1)}) custom-call(bf16[2048,1792]{1,0:T(8,128)(2,1)} %get-tuple-element.123.refs_4_.refs_0_.hidden_ref, bf16[1792,2048]{1,0:T(8,128)(2,1)} %get-tuple-element.100.refs_8_.weight_ref, ...), custom_call_target="tpu_custom_call" | custom-call | flops 7516192768 | bytes 15204352 | tf_op jit(solution)/shard_map/pallas_call | solution.py:1447
  498.6 12.9 %shard_map.307 = (bf16[512,2048]{1,0:T(8,128)(2,1)S(1)}, bf16[512,2048]{1,0:T(8,128)(2,1)S(1)}, bf16[512,2048]{1,0:T(8,128)(2,1)}, bf16[512,2048]{1,0:T(8,128)(2,1)}, f32[8,128]{1,0:T(8,128)S(1)}) custom-call(bf16[2048,1792]{1,0:T(8,128)(2,1)} %get-tuple-element.123.refs_4_.refs_0_.hidden_ref, ...), custom_call_target="tpu_custom_call", output_to_operand_aliasing={{0}: (2, {}), {1}: (3, {}), {2}: (4, {}), {3}: (5, {})} | custom-call | flops 7516192768 | bytes 15204352 | tf_op jit(solution)/shard_map/pallas_call | solution.py:1447
  515.9 13.3 %shard_map.308 = (bf16[256,2176]{1,0:T(8,128)(2,1)}, bf16[256,2048]{1,0:T(8,128)(2,1)S(1)}, bf16[256,512]{1,0:T(8,128)(2,1)S(1)}, f32[1,512]{1,0:T(1,128)S(1)}) custom-call(s32[5]{0:T(128)S(1)} %copy-done.88, s32[1,256]{1,0:T(1,128)S(1)} %copy-done.86, s32[256,1]{1,0:T(8,128)S(1)} %copy-done.61, f32[256,256]{1,0:T(8,128)S(1)} %copy-done.49, ...), custom_call_target="tpu_custom_call" | custom-call | flops 3145728000 | bytes 6291456 | tf_op jit(solution)/shard_map/pallas_call | solution.py:944
  537.7 6.9 shard_map.309
  588.0 6.9 shard_map.322
  597.6 19.3 %shard_map.314 = bf16[1,2,704,2048]{3,2,1,0:T(8,128)(2,1)} custom-call(bf16[2048,2048]{1,0:T(8,128)(2,1)} %get-tuple-element.125.refs_0_.right_ref, bf16[2048,1792]{1,0:T(8,128)(2,1)} %get-tuple-element.126.refs_2_.refs_0_, bf16[2048,1792]{1,0:T(8,128)(2,1)} %get-tuple-element.127.refs_3_.refs_1_, bf16[512,2176]{1,0:T(8,128)(2,1)} %shard_map.313.refs_2_.refs_6_), custom_call_target="tpu_custom_call" | custom-call | flops 12884901888 | bytes 34603008 | tf_op jit(solution)/shard_map/pallas_call | solution.py:1325
  631.0 9.1 %collective-permute-done.77 = bf16[256,1536]{1,0:T(8,128)(2,1)} collective-permute-done((bf16[256,1536]{1,0:T(8,128)(2,1)}, bf16[256,1536]{1,0:T(8,128)(2,1)}, u32[]{:S(2)}, u32[]{:S(2)}) %collective-permute-start.77) | collective-permute-done | bytes 786464 | tf_op jit(solution)/shard_map/ppermute | solution.py:426
  656.4 19.2 %collective-permute-done.63 = bf16[128,2176]{1,0:T(8,128)(2,1)} collective-permute-done((bf16[128,2176]{1,0:T(8,128)(2,1)}, bf16[128,2176]{1,0:T(8,128)(2,1)}, u32[]{:S(2)}, u32[]{:S(2)}) %collective-permute-start.63) | collective-permute-done | bytes 557088 | tf_op jit(solution)/shard_map/ppermute | solution.py:426
  677.9 11.4 %shard_map.324 = f32[1,1,704,2048]{3,2,1,0:T(8,128)} custom-call(bf16[2048,2048]{1,0:T(8,128)(2,1)} %get-tuple-element.124.refs_1_.right_ref, bf16[2048,1792]{1,0:T(8,128)(2,1)} %get-tuple-element.123.refs_4_.refs_0_.hidden_ref, bf16[1,1,704,2048]{3,2,1,0:T(8,128)(2,1)S(1)} %copy-done.12, bf16[512,2176]{1,0:T(8,128)(2,1)S(1)} %copy-done.2), custom_call_target="tpu_custom_call" | custom-call | flops 6442450944 | bytes 23068672 | tf_op jit(solution)/shard_map/pallas_call | solution.py:1325
  699.7 21.2 %shard_map.315.refs_1_ = f32[1,2,704,2048]{3,2,1,0:T(8,128)} custom-call(bf16[2048,2048]{1,0:T(8,128)(2,1)} %get-tuple-element.125.refs_0_.right_ref, bf16[2048,1792]{1,0:T(8,128)(2,1)} %get-tuple-element.126.refs_2_.refs_0_, bf16[2048,1792]{1,0:T(8,128)(2,1)} %get-tuple-element.127.refs_3_.refs_1_, ...), custom_call_target="tpu_custom_call" | custom-call | flops 12884901888 | bytes 34603008 | tf_op jit(solution)/shard_map/pallas_call | solution.py:1325
  733.0 10.2 %collective-permute-done.70 = bf16[128,2048]{1,0:T(8,128)(2,1)} collective-permute-done((bf16[128,2048]{1,0:T(8,128)(2,1)}, bf16[128,2048]{1,0:T(8,128)(2,1)}, u32[]{:S(2)}, u32[]{:S(2)}) %collective-permute-start.70) | collective-permute-done | bytes 524320 | tf_op jit(solution)/shard_map/ppermute | solution.py:426
  748.0 9.6 %collective-permute-done.71 = bf16[128,2048]{1,0:T(8,128)(2,1)} collective-permute-done((bf16[128,2048]{1,0:T(8,128)(2,1)}, bf16[128,2048]{1,0:T(8,128)(2,1)}, u32[]{:S(2)}, u32[]{:S(2)}) %collective-permute-start.71) | collective-permute-done | bytes 524320 | tf_op jit(solution)/shard_map/ppermute | solution.py:426
  762.2 7.9 %collective-permute-done.72 = bf16[128,2048]{1,0:T(8,128)(2,1)S(1)} collective-permute-done((bf16[128,2048]{1,0:T(8,128)(2,1)S(1)}, bf16[128,2048]{1,0:T(8,128)(2,1)S(1)}, u32[]{:S(2)}, u32[]{:S(2)}) %collective-permute-start.72) | collective-permute-done | bytes 524320 | tf_op jit(solution)/shard_map/ppermute | solution.py:426
  (536 shorter events, 290.9 us)
Async XLA Ops:
  0.7 42.5 %collective-permute-start.6 = (bf16[1,2,704,2048]{3,2,1,0:T(8,128)(2,1)}, bf16[1,2,704,2048]{3,2,1,0:T(8,128)(2,1)}, u32[]{:S(2)}, u32[]{:S(2)}) collective-permute-start(bf16[1,2,704,2048]{3,2,1,0:T(8,128)(2,1)} %bitcast.76), channel_id=1, source_target_pairs={{0,2},{2,0},{4,6},{6,4},{8,10},{10,8},{12,14},{14,12},{16,18},{18,... | collective-permute-start | bytes 17301512 | tf_op jit(solution)/shard_map/ppermute | solution.py:434
  1.2 41.9 %collective-permute-start.7 = (bf16[1,704,2048]{2,1,0:T(8,128)(2,1)}, bf16[1,704,2048]{2,1,0:T(8,128)(2,1)S(1)}, u32[]{:S(2)}, u32[]{:S(2)}) collective-permute-start(bf16[1,704,2048]{2,1,0:T(8,128)(2,1)} %own_down.1), channel_id=1, source_target_pairs={{0,2},{2,0},{4,6},{6,4},{8,10},{10,8},{12,14},{14,12},{16,18},{18,... | collective-permute-start | bytes 8650760 | tf_op jit(solution)/shard_map/ppermute | solution.py:434
  70.0 37.4 %collective-permute-start.1 = (bf16[128,3712]{1,0:T(8,128)(2,1)}, bf16[128,3712]{1,0:T(8,128)(2,1)}, u32[]{:S(2)}, u32[]{:S(2)}) collective-permute-start(bf16[128,3712]{1,0:T(8,128)(2,1)} %shard_map.281.refs_0_), channel_id=1, source_target_pairs={{0,2},{2,0},{4,6},{6,4},{8,10},{10,8},{12,14},{14,12},{16,18},{18,... | collective-permute-start | bytes 2850824 | tf_op jit(solution)/shard_map/ppermute | solution.py:434
  124.8 34.5 %collective-permute-start.13 = (bf16[128,3712]{1,0:T(8,128)(2,1)}, bf16[128,3712]{1,0:T(8,128)(2,1)}, u32[]{:S(2)}, u32[]{:S(2)}) collective-permute-start(bf16[128,3712]{1,0:T(8,128)(2,1)} %collective-permute-done.12.refs_2_.refs_10_), channel_id=1, source_target_pairs={{0,2},{2,0},{4,6},{6,4},{8,10},{10,8},{12,14},{14,12},{16,18},{18,... | collective-permute-start | bytes 2850824 | tf_op jit(solution)/shard_map/ppermute | solution.py:434
  147.8 44.3 %all-to-all-start = ((bf16[16,288,128]{2,1,0:T(8,128)(2,1)}), bf16[16,288,128]{2,1,0:T(8,128)(2,1)}, u32[]{:S(2)}, u32[]{:S(2)}) async-start(bf16[16,288,128]{2,1,0:T(8,128)(2,1)} %shard_map.288), calls=%async_computation | async-start | bytes 2359296 | tf_op jit(solution)/shard_map/all_to_all | solution.py:1662
  157.8 90.7 %collective-permute-start.38 = (bf16[256,2048]{1,0:T(8,128)(2,1)}, bf16[256,2048]{1,0:T(8,128)(2,1)}, u32[]{:S(2)}, u32[]{:S(2)}) collective-permute-start(bf16[256,2048]{1,0:T(8,128)(2,1)} %collective-permute-done.37.refs_1_.refs_5_), channel_id=1, source_target_pairs={{0,1},{1,0},{2,3},{3,2},{4,5},{5,4},{6,7},{7,6},{8,9},{9,8},{10,11... | collective-permute-start | bytes 3145736 | tf_op jit(solution)/shard_map/ppermute | solution.py:438
  192.0 38.5 %collective-permute-start.31 = (bf16[16,288,128]{2,1,0:T(8,128)(2,1)}, bf16[16,288,128]{2,1,0:T(8,128)(2,1)}, u32[]{:S(2)}, u32[]{:S(2)}) collective-permute-start(bf16[16,288,128]{2,1,0:T(8,128)(2,1)} %all-to-all-done.near), channel_id=1, source_target_pairs={{0,2},{2,0},{4,6},{6,4},{8,10},{10,8},{12,14},{14,12},{16,18},{18,... | collective-permute-start | bytes 3538952 | tf_op jit(solution)/shard_map/ppermute | solution.py:434
  219.6 45.0 %collective-permute-start.33 = (bf16[256,2048]{1,0:T(8,128)(2,1)}, bf16[256,2048]{1,0:T(8,128)(2,1)}, u32[]{:S(2)}, u32[]{:S(2)}) collective-permute-start(bf16[256,2048]{1,0:T(8,128)(2,1)} %constant_dynamic-update-slice_fusion.4.refs_0_.refs_4_), channel_id=1, source_target_pairs={{0,4},{2,6},{4,0},{6,2},{8,12},{10,14},{12,8},{14,10},{16,20},{18,... | collective-permute-start | bytes 3145736 | tf_op jit(solution)/shard_map/ppermute | solution.py:430
  221.1 47.4 %collective-permute-start.36 = (bf16[256,2048]{1,0:T(8,128)(2,1)}, bf16[256,2048]{1,0:T(8,128)(2,1)}, u32[]{:S(2)}, u32[]{:S(2)}) collective-permute-start(bf16[256,2048]{1,0:T(8,128)(2,1)} %constant_dynamic-update-slice_fusion.6.refs_2_.refs_6_), channel_id=1, source_target_pairs={{0,4},{2,6},{4,0},{6,2},{8,12},{10,14},{12,8},{14,10},{16,20},{18,... | collective-permute-start | bytes 3145736 | tf_op jit(solution)/shard_map/ppermute | solution.py:430
  230.5 55.0 %collective-permute-start.42 = (bf16[128,2048]{1,0:T(8,128)(2,1)}, bf16[128,2048]{1,0:T(8,128)(2,1)S(1)}, u32[]{:S(2)}, u32[]{:S(2)}) collective-permute-start(bf16[128,2048]{1,0:T(8,128)(2,1)} %collective-permute-done.25.refs_2_), channel_id=1, source_target_pairs={{0,4},{2,6},{4,0},{6,2},{8,12},{10,14},{12,8},{14,10},{16,20},{18,... | collective-permute-start | bytes 1572872 | tf_op jit(solution)/shard_map/ppermute | solution.py:430
  263.9 53.3 %collective-permute-start.39 = (bf16[128,2048]{1,0:T(8,128)(2,1)}, bf16[128,2048]{1,0:T(8,128)(2,1)S(1)}, u32[]{:S(2)}, u32[]{:S(2)}) collective-permute-start(bf16[128,2048]{1,0:T(8,128)(2,1)} %collective-permute-done.23.refs_9_.refs_0_), channel_id=1, source_target_pairs={{0,4},{2,6},{4,0},{6,2},{8,12},{10,14},{12,8},{14,10},{16,20},{18,... | collective-permute-start | bytes 1572872 | tf_op jit(solution)/shard_map/ppermute | solution.py:430
  266.1 59.1 %collective-permute-start.41 = (bf16[128,2048]{1,0:T(8,128)(2,1)S(1)}, bf16[128,2048]{1,0:T(8,128)(2,1)S(1)}, u32[]{:S(2)}, u32[]{:S(2)}) collective-permute-start(bf16[128,2048]{1,0:T(8,128)(2,1)S(1)} %collective-permute-done.40.refs_2_), channel_id=1, source_target_pairs={{0,4},{2,6},{4,0},{6,2},{8,12},{10,14},{12,8},{14,10},{16,20},{18,... | collective-permute-start | bytes 1572872 | tf_op jit(solution)/shard_map/ppermute | solution.py:430
  283.4 41.2 %collective-permute-start.28 = (bf16[256,2048]{1,0:T(8,128)(2,1)S(1)}, bf16[256,2048]{1,0:T(8,128)(2,1)S(1)}, u32[]{:S(2)}, u32[]{:S(2)}) collective-permute-start(bf16[256,2048]{1,0:T(8,128)(2,1)S(1)} %constant_dynamic-update-slice_fusion.2.refs_0_), channel_id=1, source_target_pairs={{0,4},{2,6},{4,0},{6,2},{8,12},{10,14},{12,8},{14,10},{16,20},{18,... | collective-permute-start | bytes 3145736 | tf_op jit(solution)/shard_map/ppermute | solution.py:430
  284.9 40.3 %collective-permute-start.29 = (bf16[256,2048]{1,0:T(8,128)(2,1)S(1)}, bf16[256,2048]{1,0:T(8,128)(2,1)S(1)}, u32[]{:S(2)}, u32[]{:S(2)}) collective-permute-start(bf16[256,2048]{1,0:T(8,128)(2,1)S(1)} %constant_dynamic-update-slice_fusion.2.refs_0_), channel_id=1, source_target_pairs={{0,1},{1,0},{2,3},{3,2},{4,5},{5,4},{6,7},{7,6},{8,9},{9,8},{10,11... | collective-permute-start | bytes 3145736 | tf_op jit(solution)/shard_map/ppermute | solution.py:438
  316.6 43.2 %collective-permute-start.43 = (bf16[128,2048]{1,0:T(8,128)(2,1)}, bf16[128,2048]{1,0:T(8,128)(2,1)}, u32[]{:S(2)}, u32[]{:S(2)}) collective-permute-start(bf16[128,2048]{1,0:T(8,128)(2,1)} %get-tuple-element.122), channel_id=1, source_target_pairs={{0,4},{2,6},{4,0},{6,2},{8,12},{10,14},{12,8},{14,10},{16,20},{18,... | collective-permute-start | bytes 1572872 | tf_op jit(solution)/shard_map/ppermute | solution.py:430
  317.2 174.6 %collective-permute-start.56 = (bf16[128,2048]{1,0:T(8,128)(2,1)}, bf16[128,2048]{1,0:T(8,128)(2,1)}, u32[]{:S(2)}, u32[]{:S(2)}) collective-permute-start(bf16[128,2048]{1,0:T(8,128)(2,1)} %get-tuple-element.119.refs_15_), channel_id=1, source_target_pairs={{0,4},{2,6},{4,0},{6,2},{8,12},{10,14},{12,8},{14,10},{16,20},{18,... | collective-permute-start | bytes 1572872 | tf_op jit(solution)/shard_map/ppermute | solution.py:430
  324.6 37.3 %collective-permute-start.30 = (bf16[256,2048]{1,0:T(8,128)(2,1)S(1)}, bf16[256,2048]{1,0:T(8,128)(2,1)}, u32[]{:S(2)}, u32[]{:S(2)}) collective-permute-start(bf16[256,2048]{1,0:T(8,128)(2,1)S(1)} %collective-permute-done.28.refs_15_.refs_1_), channel_id=1, source_target_pairs={{0,1},{1,0},{2,3},{3,2},{4,5},{5,4},{6,7},{7,6},{8,9},{9,8},{10,11... | collective-permute-start | bytes 3145736 | tf_op jit(solution)/shard_map/ppermute | solution.py:438
  357.8 36.8 %collective-permute-start.44 = (bf16[128,2048]{1,0:T(8,128)(2,1)}, bf16[128,2048]{1,0:T(8,128)(2,1)}, u32[]{:S(2)}, u32[]{:S(2)}) collective-permute-start(bf16[128,2048]{1,0:T(8,128)(2,1)} %get-tuple-element.121.refs_1_), channel_id=1, source_target_pairs={{0,1},{1,0},{2,3},{3,2},{4,5},{5,4},{6,7},{7,6},{8,9},{9,8},{10,11... | collective-permute-start | bytes 1572872 | tf_op jit(solution)/shard_map/ppermute | solution.py:438
  359.2 75.0 %collective-permute-start.46 = (bf16[128,2048]{1,0:T(8,128)(2,1)}, bf16[128,2048]{1,0:T(8,128)(2,1)}, u32[]{:S(2)}, u32[]{:S(2)}) collective-permute-start(bf16[128,2048]{1,0:T(8,128)(2,1)} %copy-done.92), channel_id=1, source_target_pairs={{0,1},{1,0},{2,3},{3,2},{4,5},{5,4},{6,7},{7,6},{8,9},{9,8},{10,11... | collective-permute-start | bytes 1572872 | tf_op jit(solution)/shard_map/ppermute | solution.py:438
  393.1 37.4 %collective-permute-start.49 = (bf16[128,2048]{1,0:T(8,128)(2,1)}, bf16[128,2048]{1,0:T(8,128)(2,1)}, u32[]{:S(2)}, u32[]{:S(2)}) collective-permute-start(bf16[128,2048]{1,0:T(8,128)(2,1)} %get-tuple-element.132.refs_1_), channel_id=1, source_target_pairs={{0,4},{2,6},{4,0},{6,2},{8,12},{10,14},{12,8},{14,10},{16,20},{18,... | collective-permute-start | bytes 1572872 | tf_op jit(solution)/shard_map/ppermute | solution.py:430
  396.7 38.0 %collective-permute-start.45 = (bf16[128,2048]{1,0:T(8,128)(2,1)}, bf16[128,2048]{1,0:T(8,128)(2,1)}, u32[]{:S(2)}, u32[]{:S(2)}) collective-permute-start(bf16[128,2048]{1,0:T(8,128)(2,1)} %add_convert_fusion.9), channel_id=1, source_target_pairs={{0,4},{2,6},{4,0},{6,2},{8,12},{10,14},{12,8},{14,10},{16,20},{18,... | collective-permute-start | bytes 1572872 | tf_op jit(solution)/shard_map/ppermute | solution.py:430
  451.8 40.1 %collective-permute-start.57 = (bf16[128,2048]{1,0:T(8,128)(2,1)}, bf16[128,2048]{1,0:T(8,128)(2,1)}, u32[]{:S(2)}, u32[]{:S(2)}) collective-permute-start(bf16[128,2048]{1,0:T(8,128)(2,1)} %add_convert_fusion.10.refs_16_), channel_id=1, source_target_pairs={{0,1},{1,0},{2,3},{3,2},{4,5},{5,4},{6,7},{7,6},{8,9},{9,8},{10,11... | collective-permute-start | bytes 1572872 | tf_op jit(solution)/shard_map/ppermute | solution.py:438
  471.0 43.3 %collective-permute-start.59 = (bf16[1,1,704,2048]{3,2,1,0:T(8,128)(2,1)}, bf16[1,1,704,2048]{3,2,1,0:T(8,128)(2,1)S(1)}, u32[]{:S(2)}, u32[]{:S(2)}) collective-permute-start(bf16[1,1,704,2048]{3,2,1,0:T(8,128)(2,1)} %copy-done.47), channel_id=1, source_target_pairs={{0,2},{2,0},{4,6},{6,4},{8,10},{10,8},{12,14},{14,12},{16,18},{18,... | collective-permute-start | bytes 8650760 | tf_op jit(solution)/shard_map/ppermute | solution.py:434
  471.0 43.2 %collective-permute-start.60 = (bf16[16,288,128]{2,1,0:T(8,128)(2,1)}, bf16[16,288,128]{2,1,0:T(8,128)(2,1)}, u32[]{:S(2)}, u32[]{:S(2)}) collective-permute-start(bf16[16,288,128]{2,1,0:T(8,128)(2,1)} %copy-done.62), channel_id=1, source_target_pairs={{0,2},{2,0},{4,6},{6,4},{8,10},{10,8},{12,14},{14,12},{16,18},{18,... | collective-permute-start | bytes 3538952 | tf_op jit(solution)/shard_map/ppermute | solution.py:434
  566.1 84.2 %collective-permute-start.67 = (bf16[512,2048]{1,0:T(8,128)(2,1)}, bf16[512,2048]{1,0:T(8,128)(2,1)}, u32[]{:S(2)}, u32[]{:S(2)}) collective-permute-start(bf16[512,2048]{1,0:T(8,128)(2,1)} %shard_map.319), channel_id=1, source_target_pairs={{0,1},{1,0},{2,3},{3,2},{4,5},{5,4},{6,7},{7,6},{8,9},{9,8},{10,11... | collective-permute-start | bytes 6291464 | tf_op jit(solution)/shard_map/ppermute | solution.py:438
  566.7 156.5 %collective-permute-start.69 = (bf16[512,2048]{1,0:T(8,128)(2,1)}, bf16[512,2048]{1,0:T(8,128)(2,1)}, u32[]{:S(2)}, u32[]{:S(2)}) collective-permute-start(bf16[512,2048]{1,0:T(8,128)(2,1)} %shard_map.320), channel_id=1, source_target_pairs={{0,1},{1,0},{2,3},{3,2},{4,5},{5,4},{6,7},{7,6},{8,9},{9,8},{10,11... | collective-permute-start | bytes 6291464 | tf_op jit(solution)/shard_map/ppermute | solution.py:438
  571.4 53.2 %all-to-all-start.1 = ((bf16[16,288,128]{2,1,0:T(8,128)(2,1)}), bf16[16,288,128]{2,1,0:T(8,128)(2,1)}, u32[]{:S(2)}, u32[]{:S(2)}) async-start(bf16[16,288,128]{2,1,0:T(8,128)(2,1)} %add_convert_fusion.1), calls=%async_computation.1 | async-start | bytes 2359296 | tf_op jit(solution)/shard_map/all_to_all | solution.py:1891
  586.5 57.6 %collective-permute-start.62 = (bf16[512,2176]{1,0:T(8,128)(2,1)}, bf16[512,2176]{1,0:T(8,128)(2,1)S(1)}, u32[]{:S(2)}, u32[]{:S(2)}) collective-permute-start(bf16[512,2176]{1,0:T(8,128)(2,1)} %shard_map.313.refs_2_.refs_6_), channel_id=1, source_target_pairs={{0,4},{2,6},{4,0},{6,2},{8,12},{10,14},{12,8},{14,10},{16,20},{18,... | collective-permute-start | bytes 6684680 | tf_op jit(solution)/shard_map/ppermute | solution.py:430
  616.9 82.8 %collective-permute-start.66 = (bf16[1,2,704,2048]{3,2,1,0:T(8,128)(2,1)}, bf16[1,2,704,2048]{3,2,1,0:T(8,128)(2,1)}, u32[]{:S(2)}, u32[]{:S(2)}) collective-permute-start(bf16[1,2,704,2048]{3,2,1,0:T(8,128)(2,1)} %shard_map.314), channel_id=1, source_target_pairs={{0,2},{2,0},{4,6},{6,4},{8,10},{10,8},{12,14},{14,12},{16,18},{18,... | collective-permute-start | bytes 17301512 | tf_op jit(solution)/shard_map/ppermute | solution.py:434
  642.6 49.5 %collective-permute-start.78 = (bf16[256,1536]{1,0:T(8,128)(2,1)}, bf16[256,1536]{1,0:T(8,128)(2,1)S(1)}, u32[]{:S(2)}, u32[]{:S(2)}) collective-permute-start(bf16[256,1536]{1,0:T(8,128)(2,1)} %add_convert_fusion.2), channel_id=1, source_target_pairs={{0,8},{2,10},{4,12},{6,14},{8,16},{10,18},{12,20},{14,22},{16,24},... | collective-permute-start | bytes 2359304 | tf_op jit(solution)/shard_map/ppermute | solution.py:426
  654.9 68.3 %collective-permute-start.68 = (bf16[512,2048]{1,0:T(8,128)(2,1)}, bf16[512,2048]{1,0:T(8,128)(2,1)}, u32[]{:S(2)}, u32[]{:S(2)}) collective-permute-start(bf16[512,2048]{1,0:T(8,128)(2,1)} %add_convert_fusion), channel_id=1, source_target_pairs={{0,4},{2,6},{4,0},{6,2},{8,12},{10,14},{12,8},{14,10},{16,20},{18,... | collective-permute-start | bytes 6291464 | tf_op jit(solution)/shard_map/ppermute | solution.py:430
  693.5 37.2 %collective-permute-start.79 = (bf16[128,1536]{1,0:T(8,128)(2,1)S(1)}, bf16[128,1536]{1,0:T(8,128)(2,1)S(1)}, u32[]{:S(2)}, u32[]{:S(2)}) collective-permute-start(bf16[128,1536]{1,0:T(8,128)(2,1)S(1)} %slice.200), channel_id=1, source_target_pairs={{0,4},{2,6},{4,0},{6,2},{8,12},{10,14},{12,8},{14,10},{16,20},{18,... | collective-permute-start | bytes 1179656 | tf_op jit(solution)/shard_map/ppermute | solution.py:430
  (169 other events, 2129.4 us)

commit v14 on v13

--- a/solution.py
+++ b/solution.py
@@ -1910,12 +1910,12 @@
     grad_expert_in = expert_grads(
         (every_gate_grad, every_up_grad), every_row, units, 0, arrived_in, f32, (near,)
     )
-    first_closed = close_ring(near, from_y, grad_expert_in)
+    first_closed = close_ring(near, from_y, from_y)
     out_own, out_beside, out_across = close_plane(turn_corner(outs, "x"))
     out_total = wide_sum(after(out_own, first_closed), out_beside, out_across)
-    block_output = mixed + ring_sum(
-        [out_total[r * local_rows : (r + 1) * local_rows] for r in range(RINGS)], bf16
-    )
+    out_parts = [out_total[r * local_rows : (r + 1) * local_rows] for r in range(RINGS)]
+    out_parts[2] = after(out_parts[2], grad_expert_in)
+    block_output = mixed + ring_sum(out_parts, bf16)
     other_closed = other_summed[:depth] + other_y(
         other_summed[depth:].astype(bf16)
     ).astype(f32)

time: 785 us -> 867 us (1.10)
  waiting for transfers between devices: 188 us -> 268 us
  Pallas kernels: 337 us -> 347 us
    ppermute x22, waiting for transfers between devices: 32.9 us -> 107 us  [other_x(): return lax.ppermute(values, 'tensor', [(0, 1), (1, 0)])]
    ppermute x21, waiting for transfers between devices: 32.6 us -> 71.3 us  [other_y(): return lax.ppermute(values, 'dp', [(i, i ^ 2) for i in range(16)])]
    ppermute x21, waiting for transfers between devices: 123 us -> 89.9 us  [ring_step(): lax.ppermute(values, 'dp', [(i, (i + RINGS) % 16) for i in range(16)])]
    pallas_call x4, Pallas kernels: 118 us -> 127 us  [mlp_plane(): pl.pallas_call(functools.partial(mlp_kernel, tiles, tuple((start for _, s...]
    unnamed x255 -> x251, local copies, waits for them, and re-layouts: 73.8 us -> 73.8 us
  transfers between devices with their start and end apart: 82 -> 82, of which waited for: 22 -> 21; matrix products, arithmetic and copies ran while one was open for 13% -> 12% of each run, Pallas kernels for 40% -> 37%
where the time goes in v14:
time: 867 us; the launch traced here: 859 us
  Pallas kernels  347 us (40%)
  waiting for transfers between devices  268 us (31%)
  local copies, waits for them, and re-layouts  94.7 us (11%)
  starting transfers between devices  81.1 us (9%)
  other arithmetic  65 us (7%)
    pallas_call x4, Pallas kernels, mlp_plane(): pl.pallas_call(functools.partial(mlp_kernel, tiles, tuple((start for _, s...  127 us
    ppermute x22, waiting for transfers between devices, other_x(): return lax.ppermute(values, 'tensor', [(0, 1), (1, 0)])  107 us
    ppermute x21, waiting for transfers between devices, ring_step(): lax.ppermute(values, 'dp', [(i, (i + RINGS) % 16) for i in range(16)])  89.9 us
    unnamed x251, local copies, waits for them, and re-layouts  73.8 us
    ppermute x21, waiting for transfers between devices, other_y(): return lax.ppermute(values, 'dp', [(i, i ^ 2) for i in range(16)])  71.3 us
    pallas_call x4, Pallas kernels, expert_grads(): pl.pallas_call(functools.partial(expert_grads_kernel, units, len(lefts),...  61.8 us
    pallas_call x2, Pallas kernels, down_grads(): pl.pallas_call(functools.partial(down_kernel, tuple((start for _, start i...  29.2 us
    pallas_call x5, Pallas kernels, grads_call(): pl.pallas_call(lambda *refs: kernel(len(extra), *refs[:1 + len(operands)...  27.3 us
  transfers between devices with their start and end apart: 82, of which 21 were waited for; matrix products, arithmetic and copies ran while one was open for 12% of the time, Pallas kernels for 37%

profile of v14, /device:TPU:0, one launch (start us, length us, event | category | flops | bytes accessed | tf_op | source)
XLA Modules:
  0.0 859.1 jit_solution(15745576793757971108)
XLA Ops:
  18.5 20.5 %collective-permute-done.4.refs_4_ = bf16[128,3712]{1,0:T(8,128)(2,1)S(1)} collective-permute-done((bf16[128,3712]{1,0:T(8,128)(2,1)}, bf16[128,3712]{1,0:T(8,128)(2,1)S(1)}, u32[]{:S(2)}, u32[]{:S(2)}) %collective-permute-start.4) | collective-permute-done | bytes 950304 | tf_op jit(solution)/shard_map/ppermute | solution.py:426
  46.2 19.3 %collective-permute-done.10.refs_8_ = bf16[128,3712]{1,0:T(8,128)(2,1)} collective-permute-done((bf16[128,3712]{1,0:T(8,128)(2,1)}, bf16[128,3712]{1,0:T(8,128)(2,1)}, u32[]{:S(2)}, u32[]{:S(2)}) %collective-permute-start.10) | collective-permute-done | bytes 950304 | tf_op jit(solution)/shard_map/ppermute | solution.py:426
  70.8 18.9 %collective-permute-done.12.refs_2_.refs_10_ = bf16[128,3712]{1,0:T(8,128)(2,1)} collective-permute-done((bf16[128,3712]{1,0:T(8,128)(2,1)}, bf16[128,3712]{1,0:T(8,128)(2,1)}, u32[]{:S(2)}, u32[]{:S(2)}) %collective-permute-start.12) | collective-permute-done | bytes 950304 | tf_op jit(solution)/shard_map/ppermute | solution.py:430
  94.5 12.6 %collective-permute-done.18 = bf16[128,2048]{1,0:T(8,128)(2,1)} collective-permute-done((bf16[128,2048]{1,0:T(8,128)(2,1)}, bf16[128,2048]{1,0:T(8,128)(2,1)}, u32[]{:S(2)}, u32[]{:S(2)}) %collective-permute-start.18) | collective-permute-done | bytes 524320 | tf_op jit(solution)/shard_map/ppermute | solution.py:426
  110.1 9.1 %collective-permute-done.19.refs_16_.refs_0_ = bf16[128,2048]{1,0:T(8,128)(2,1)S(1)} collective-permute-done((bf16[128,2048]{1,0:T(8,128)(2,1)}, bf16[128,2048]{1,0:T(8,128)(2,1)S(1)}, u32[]{:S(2)}, u32[]{:S(2)}) %collective-permute-start.19) | collective-permute-done | bytes 524320 | tf_op jit(solution)/shard_map/ppermute | solution.py:426
  124.8 6.8 collective-permute-done.16.refs_14_.refs_1_
  134.3 10.6 %collective-permute-done.34 = bf16[128,2048]{1,0:T(8,128)(2,1)} collective-permute-done((bf16[128,2048]{1,0:T(8,128)(2,1)S(1)}, bf16[128,2048]{1,0:T(8,128)(2,1)}, u32[]{:S(2)}, u32[]{:S(2)}) %collective-permute-start.34) | collective-permute-done | bytes 524320 | tf_op jit(solution)/shard_map/ppermute | solution.py:438
  159.3 22.8 %shard_map.286 = (f32[128,2048]{1,0:T(8,128)}, bf16[128,2048]{1,0:T(8,128)(2,1)S(1)}, bf16[2048,2176]{1,0:T(8,128)(2,1)}, bf16[512,2048]{1,0:T(8,128)(2,1)}, bf1...) custom-call(s32[5]{0:T(128)S(1)} %concatenate.39.place_ref.refs_0_, ...), custom_call_target="tpu_custom_call" | custom-call | flops 4429185024 | bytes 30408704 | tf_op jit(solution)/shard_map/pallas_call | solution.py:802
  191.8 8.2 collective-permute-done.22
  206.9 8.4 collective-permute-done.35
  236.3 12.0 %shard_map.289 = (bf16[1792,2048]{1,0:T(8,128)(2,1)}, bf16[1792,2048]{1,0:T(8,128)(2,1)}, bf16[1792,2048]{1,0:T(8,128)(2,1)}) custom-call(bf16[1,2,704,2048]{3,2,1,0:T(8,128)(2,1)S(1)} %bitcast.77, bf16[1,2,704,2048]{3,2,1,0:T(8,128)(2,1)} %collective-permute-done.6.refs_1_.other_in, bf16[1,704,2048]{2,1,0:T(8,128)(2,1)S(1)} %copy-done.45, ...), custom_call_target="tpu_custom_call" | custom-call | bytes 44040192 | tf_op jit(solution)/shard_map/pallas_call | solution.py:1293
  249.3 14.5 %shard_map.291 = (bf16[2048,1792]{1,0:T(8,128)(2,1)}, bf16[2048,2048]{1,0:T(8,128)(2,1)}) custom-call(bf16[256,2048]{1,0:T(8,128)(2,1)} %pad_maximum_fusion.refs_0_.refs_4_, bf16[256,2048]{1,0:T(8,128)(2,1)} %collective-permute-done.37.refs_1_.refs_5_, bf16[256,2048]{1,0:T(8,128)(2,1)S(1)} %copy-done.67, ...), custom_call_target="tpu_custom_call" | custom-call | flops 7516192768 | bytes 19398656 | tf_op jit(solution)/shard_map/pallas_call | solution.py:1407
  268.3 14.8 %shard_map.292 = (bf16[2048,1792]{1,0:T(8,128)(2,1)}, bf16[2048,2048]{1,0:T(8,128)(2,1)}) custom-call(bf16[256,2048]{1,0:T(8,128)(2,1)} %constant_dynamic-update-slice_fusion.4.refs_0_.refs_4_, bf16[256,2048]{1,0:T(8,128)(2,1)} %collective-permute-done.33.refs_1_.refs_5_, ...), custom_call_target="tpu_custom_call", output_to_operand_aliasing={{0}: (9, {}), {1}: (10, {})} | custom-call | flops 7516192768 | bytes 19398656 | tf_op jit(solution)/shard_map/pallas_call | solution.py:1407
  285.4 29.5 %shard_map.293 = (bf16[128,2048]{1,0:T(8,128)(2,1)S(1)}, bf16[128,2048]{1,0:T(8,128)(2,1)}, bf16[128,2048]{1,0:T(8,128)(2,1)S(1)}, bf16[128,2048]{1,0:T(8,128)(2...) custom-call(s32[4]{0:T(128)S(1)} %pad_add_fusion.experts_ref, ...), custom_call_target="tpu_custom_call" | custom-call | flops 15032385536 | bytes 42991616 | tf_op jit(solution)/shard_map/pallas_call | solution.py:1557
  326.1 29.2 %shard_map.294 = (bf16[128,2048]{1,0:T(8,128)(2,1)S(1)}, bf16[128,2048]{1,0:T(8,128)(2,1)S(1)}, bf16[128,2048]{1,0:T(8,128)(2,1)S(1)}, bf16[128,2048]{1,0:T(8,12...) custom-call(s32[4]{0:T(128)S(1)} %pad_add_fusion.experts_ref, ...), custom_call_target="tpu_custom_call", output_to_operand_aliasing={{4}: (12, {}), {5}: (13, {}), {6}: (14, {}), {7}: (15, {}),... | custom-call | flops 15032385536 | bytes 42991616 | tf_op jit(solution)/shard_map/pallas_call | solution.py:1557
  362.0 38.6 %shard_map.295 = (bf16[128,2048]{1,0:T(8,128)(2,1)S(1)}, bf16[128,2048]{1,0:T(8,128)(2,1)}, bf16[128,2048]{1,0:T(8,128)(2,1)S(1)}, bf16[128,2048]{1,0:T(8,128)(2...) custom-call(s32[4]{0:T(128)S(1)} %pad_add_fusion.experts_ref, ...), custom_call_target="tpu_custom_call", output_to_operand_aliasing={{4}: (12, {}), {5}: (13, {}), {6}: (14, {}), {7}: (15, {}),... | custom-call | flops 15032385536 | bytes 42991616 | tf_op jit(solution)/shard_map/pallas_call | solution.py:1557
  406.3 29.4 %shard_map.297 = (bf16[128,2048]{1,0:T(8,128)(2,1)S(1)}, bf16[128,2048]{1,0:T(8,128)(2,1)S(1)}, bf16[128,2048]{1,0:T(8,128)(2,1)S(1)}, bf16[128,2048]{1,0:T(8,12...) custom-call(s32[4]{0:T(128)S(1)} %pad_add_fusion.experts_ref, ...), custom_call_target="tpu_custom_call", output_to_operand_aliasing={{4}: (12, {}), {5}: (13, {}), {6}: (14, {}), {7}: (15, {}),... | custom-call | flops 15032385536 | bytes 42991616 | tf_op jit(solution)/shard_map/pallas_call | solution.py:1557
  445.8 11.9 %shard_map.300 = (f32[16,288,128]{2,1,0:T(8,128)S(1)}, bf16[16,288,128]{2,1,0:T(8,128)(2,1)S(1)}, f32[128,2048]{1,0:T(8,128)S(1)}) custom-call(bf16[2048,2048]{1,0:T(8,128)(2,1)} %get-tuple-element.125.refs_0_.right_ref, bf16[2048,2048]{1,0:T(8,128)(2,1)} %get-tuple-element.124.refs_1_.right_ref, bf16[2048,1792]{1,0:T(8,128)(2,1)} %get-tuple-element.126.refs_2_.refs_0_, ...), custom_call_target="tpu_custom_call" | custom-call | flops 8589934592 | bytes 16777216 | tf_op jit(solution)/shard_map/pallas_call | solution.py:1368
  468.3 10.0 %shard_map.301.refs_0_.refs_1_ = bf16[1,1,704,2048]{3,2,1,0:T(8,128)(2,1)S(1)} custom-call(bf16[2048,2048]{1,0:T(8,128)(2,1)} %get-tuple-element.124.refs_1_.right_ref, bf16[2048,1792]{1,0:T(8,128)(2,1)} %get-tuple-element.123.refs_4_.refs_0_.hidden_ref, bf16[16,288,128]{2,1,0:T(8,128)(2,1)S(1)} %copy-done.62), custom_call_target="tpu_custom_call" | custom-call | flops 6442450944 | bytes 23068672 | tf_op jit(solution)/shard_map/pallas_call | solution.py:1325
  484.6 13.2 %shard_map.302 = (bf16[512,2048]{1,0:T(8,128)(2,1)S(1)}, bf16[512,2048]{1,0:T(8,128)(2,1)S(1)}, bf16[512,2048]{1,0:T(8,128)(2,1)}, bf16[512,2048]{1,0:T(8,128)(2,1)}, f32[8,128]{1,0:T(8,128)S(1)}) custom-call(bf16[2048,1792]{1,0:T(8,128)(2,1)} %get-tuple-element.123.refs_4_.refs_0_.hidden_ref, bf16[1792,2048]{1,0:T(8,128)(2,1)} %get-tuple-element.100.refs_8_.weight_ref, ...), custom_call_target="tpu_custom_call" | custom-call | flops 7516192768 | bytes 15204352 | tf_op jit(solution)/shard_map/pallas_call | solution.py:1447
  507.8 12.9 %shard_map.307 = (bf16[512,2048]{1,0:T(8,128)(2,1)S(1)}, bf16[512,2048]{1,0:T(8,128)(2,1)S(1)}, bf16[512,2048]{1,0:T(8,128)(2,1)}, bf16[512,2048]{1,0:T(8,128)(2,1)}, f32[8,128]{1,0:T(8,128)S(1)}) custom-call(bf16[2048,1792]{1,0:T(8,128)(2,1)} %get-tuple-element.123.refs_4_.refs_0_.hidden_ref, ...), custom_call_target="tpu_custom_call", output_to_operand_aliasing={{0}: (2, {}), {1}: (3, {}), {2}: (4, {}), {3}: (5, {})} | custom-call | flops 7516192768 | bytes 15204352 | tf_op jit(solution)/shard_map/pallas_call | solution.py:1447
  525.0 13.3 %shard_map.308 = (bf16[256,2176]{1,0:T(8,128)(2,1)}, bf16[256,2048]{1,0:T(8,128)(2,1)S(1)}, bf16[256,512]{1,0:T(8,128)(2,1)S(1)}, f32[1,512]{1,0:T(1,128)S(1)}) custom-call(s32[5]{0:T(128)S(1)} %copy-done.87, s32[1,256]{1,0:T(1,128)S(1)} %copy-done.85, s32[256,1]{1,0:T(8,128)S(1)} %copy-done.60, f32[256,256]{1,0:T(8,128)S(1)} %copy-done.48, ...), custom_call_target="tpu_custom_call" | custom-call | flops 3145728000 | bytes 6291456 | tf_op jit(solution)/shard_map/pallas_call | solution.py:944
  546.9 7.6 shard_map.309
  591.9 6.9 shard_map.323
  600.8 77.1 %collective-permute-done.73 = bf16[128,2048]{1,0:T(8,128)(2,1)} collective-permute-done((bf16[128,2048]{1,0:T(8,128)(2,1)}, bf16[128,2048]{1,0:T(8,128)(2,1)}, u32[]{:S(2)}, u32[]{:S(2)}) %collective-permute-start.73) | collective-permute-done | bytes 524320 | tf_op jit(solution)/shard_map/ppermute | solution.py:438
  686.6 19.2 %shard_map.319 = bf16[1,2,704,2048]{3,2,1,0:T(8,128)(2,1)} custom-call(bf16[2048,2048]{1,0:T(8,128)(2,1)} %get-tuple-element.125.refs_0_.right_ref, bf16[2048,1792]{1,0:T(8,128)(2,1)} %get-tuple-element.126.refs_2_.refs_0_, bf16[2048,1792]{1,0:T(8,128)(2,1)} %get-tuple-element.127.refs_3_.refs_1_, bf16[512,2176]{1,0:T(8,128)(2,1)} %shard_map.313.refs_2_.refs_6_), custom_call_target="tpu_custom_call" | custom-call | flops 12884901888 | bytes 34603008 | tf_op jit(solution)/shard_map/pallas_call | solution.py:1325
  715.5 16.0 %collective-permute-done.62.refs_1_.refs_0_.refs_2_ = bf16[512,2176]{1,0:T(8,128)(2,1)S(1)} collective-permute-done((bf16[512,2176]{1,0:T(8,128)(2,1)}, bf16[512,2176]{1,0:T(8,128)(2,1)S(1)}, u32[]{:S(2)}, u32[]{:S(2)}) %collective-permute-start.62) | collective-permute-done | bytes 2228256 | tf_op jit(solution)/shard_map/ppermute | solution.py:430
  752.9 11.4 %shard_map.325 = f32[1,1,704,2048]{3,2,1,0:T(8,128)} custom-call(bf16[2048,2048]{1,0:T(8,128)(2,1)} %get-tuple-element.124.refs_1_.right_ref, bf16[2048,1792]{1,0:T(8,128)(2,1)} %get-tuple-element.123.refs_4_.refs_0_.hidden_ref, bf16[1,1,704,2048]{3,2,1,0:T(8,128)(2,1)S(1)} %copy-done.11, bf16[512,2176]{1,0:T(8,128)(2,1)S(1)} %copy-done.2), custom_call_target="tpu_custom_call" | custom-call | flops 6442450944 | bytes 23068672 | tf_op jit(solution)/shard_map/pallas_call | solution.py:1325
  773.2 23.1 %collective-permute-done.79 = bf16[128,1536]{1,0:T(8,128)(2,1)S(1)} collective-permute-done((bf16[128,1536]{1,0:T(8,128)(2,1)S(1)}, bf16[128,1536]{1,0:T(8,128)(2,1)S(1)}, u32[]{:S(2)}, u32[]{:S(2)}) %collective-permute-start.79) | collective-permute-done | bytes 393248 | tf_op jit(solution)/shard_map/ppermute | solution.py:430
  808.0 21.1 %shard_map.320.refs_1_ = f32[1,2,704,2048]{3,2,1,0:T(8,128)} custom-call(bf16[2048,2048]{1,0:T(8,128)(2,1)} %get-tuple-element.125.refs_0_.right_ref, bf16[2048,1792]{1,0:T(8,128)(2,1)} %get-tuple-element.126.refs_2_.refs_0_, bf16[2048,1792]{1,0:T(8,128)(2,1)} %get-tuple-element.127.refs_3_.refs_1_, ...), custom_call_target="tpu_custom_call" | custom-call | flops 12884901888 | bytes 34603008 | tf_op jit(solution)/shard_map/pallas_call | solution.py:1325
  834.6 8.7 %collective-permute-done.71 = bf16[128,2048]{1,0:T(8,128)(2,1)} collective-permute-done((bf16[128,2048]{1,0:T(8,128)(2,1)S(1)}, bf16[128,2048]{1,0:T(8,128)(2,1)}, u32[]{:S(2)}, u32[]{:S(2)}) %collective-permute-start.71) | collective-permute-done | bytes 524320 | tf_op jit(solution)/shard_map/ppermute | solution.py:426
  848.0 8.5 collective-permute-done.72
  (533 shorter events, 289.8 us)
Async XLA Ops:
  0.7 42.4 %collective-permute-start.6 = (bf16[1,2,704,2048]{3,2,1,0:T(8,128)(2,1)}, bf16[1,2,704,2048]{3,2,1,0:T(8,128)(2,1)}, u32[]{:S(2)}, u32[]{:S(2)}) collective-permute-start(bf16[1,2,704,2048]{3,2,1,0:T(8,128)(2,1)} %bitcast.76), channel_id=1, source_target_pairs={{0,2},{2,0},{4,6},{6,4},{8,10},{10,8},{12,14},{14,12},{16,18},{18,... | collective-permute-start | bytes 17301512 | tf_op jit(solution)/shard_map/ppermute | solution.py:434
  1.2 41.9 %collective-permute-start.7 = (bf16[1,704,2048]{2,1,0:T(8,128)(2,1)}, bf16[1,704,2048]{2,1,0:T(8,128)(2,1)S(1)}, u32[]{:S(2)}, u32[]{:S(2)}) collective-permute-start(bf16[1,704,2048]{2,1,0:T(8,128)(2,1)} %own_down.1), channel_id=1, source_target_pairs={{0,2},{2,0},{4,6},{6,4},{8,10},{10,8},{12,14},{14,12},{16,18},{18,... | collective-permute-start | bytes 8650760 | tf_op jit(solution)/shard_map/ppermute | solution.py:434
  70.0 37.4 %collective-permute-start.1 = (bf16[128,3712]{1,0:T(8,128)(2,1)}, bf16[128,3712]{1,0:T(8,128)(2,1)}, u32[]{:S(2)}, u32[]{:S(2)}) collective-permute-start(bf16[128,3712]{1,0:T(8,128)(2,1)} %shard_map.281.refs_0_), channel_id=1, source_target_pairs={{0,2},{2,0},{4,6},{6,4},{8,10},{10,8},{12,14},{14,12},{16,18},{18,... | collective-permute-start | bytes 2850824 | tf_op jit(solution)/shard_map/ppermute | solution.py:434
  147.7 44.1 %all-to-all-start = ((bf16[16,288,128]{2,1,0:T(8,128)(2,1)}), bf16[16,288,128]{2,1,0:T(8,128)(2,1)}, u32[]{:S(2)}, u32[]{:S(2)}) async-start(bf16[16,288,128]{2,1,0:T(8,128)(2,1)} %shard_map.288), calls=%async_computation | async-start | bytes 2359296 | tf_op jit(solution)/shard_map/all_to_all | solution.py:1662
  157.7 90.5 %collective-permute-start.38 = (bf16[256,2048]{1,0:T(8,128)(2,1)}, bf16[256,2048]{1,0:T(8,128)(2,1)}, u32[]{:S(2)}, u32[]{:S(2)}) collective-permute-start(bf16[256,2048]{1,0:T(8,128)(2,1)} %collective-permute-done.37.refs_1_.refs_5_), channel_id=1, source_target_pairs={{0,1},{1,0},{2,3},{3,2},{4,5},{5,4},{6,7},{7,6},{8,9},{9,8},{10,11... | collective-permute-start | bytes 3145736 | tf_op jit(solution)/shard_map/ppermute | solution.py:438
  191.8 38.5 %collective-permute-start.31 = (bf16[16,288,128]{2,1,0:T(8,128)(2,1)}, bf16[16,288,128]{2,1,0:T(8,128)(2,1)}, u32[]{:S(2)}, u32[]{:S(2)}) collective-permute-start(bf16[16,288,128]{2,1,0:T(8,128)(2,1)} %all-to-all-done.near), channel_id=1, source_target_pairs={{0,2},{2,0},{4,6},{6,4},{8,10},{10,8},{12,14},{14,12},{16,18},{18,... | collective-permute-start | bytes 3538952 | tf_op jit(solution)/shard_map/ppermute | solution.py:434
  219.4 45.1 %collective-permute-start.33 = (bf16[256,2048]{1,0:T(8,128)(2,1)}, bf16[256,2048]{1,0:T(8,128)(2,1)}, u32[]{:S(2)}, u32[]{:S(2)}) collective-permute-start(bf16[256,2048]{1,0:T(8,128)(2,1)} %constant_dynamic-update-slice_fusion.4.refs_0_.refs_4_), channel_id=1, source_target_pairs={{0,4},{2,6},{4,0},{6,2},{8,12},{10,14},{12,8},{14,10},{16,20},{18,... | collective-permute-start | bytes 3145736 | tf_op jit(solution)/shard_map/ppermute | solution.py:430
  220.8 47.4 %collective-permute-start.36 = (bf16[256,2048]{1,0:T(8,128)(2,1)}, bf16[256,2048]{1,0:T(8,128)(2,1)}, u32[]{:S(2)}, u32[]{:S(2)}) collective-permute-start(bf16[256,2048]{1,0:T(8,128)(2,1)} %constant_dynamic-update-slice_fusion.6.refs_2_.refs_6_), channel_id=1, source_target_pairs={{0,4},{2,6},{4,0},{6,2},{8,12},{10,14},{12,8},{14,10},{16,20},{18,... | collective-permute-start | bytes 3145736 | tf_op jit(solution)/shard_map/ppermute | solution.py:430
  230.3 55.1 %collective-permute-start.42 = (bf16[128,2048]{1,0:T(8,128)(2,1)}, bf16[128,2048]{1,0:T(8,128)(2,1)S(1)}, u32[]{:S(2)}, u32[]{:S(2)}) collective-permute-start(bf16[128,2048]{1,0:T(8,128)(2,1)} %collective-permute-done.25.refs_2_), channel_id=1, source_target_pairs={{0,4},{2,6},{4,0},{6,2},{8,12},{10,14},{12,8},{14,10},{16,20},{18,... | collective-permute-start | bytes 1572872 | tf_op jit(solution)/shard_map/ppermute | solution.py:430
  263.8 53.4 %collective-permute-start.39 = (bf16[128,2048]{1,0:T(8,128)(2,1)}, bf16[128,2048]{1,0:T(8,128)(2,1)S(1)}, u32[]{:S(2)}, u32[]{:S(2)}) collective-permute-start(bf16[128,2048]{1,0:T(8,128)(2,1)} %collective-permute-done.23.refs_9_.refs_0_), channel_id=1, source_target_pairs={{0,4},{2,6},{4,0},{6,2},{8,12},{10,14},{12,8},{14,10},{16,20},{18,... | collective-permute-start | bytes 1572872 | tf_op jit(solution)/shard_map/ppermute | solution.py:430
  266.0 59.1 %collective-permute-start.41 = (bf16[128,2048]{1,0:T(8,128)(2,1)S(1)}, bf16[128,2048]{1,0:T(8,128)(2,1)S(1)}, u32[]{:S(2)}, u32[]{:S(2)}) collective-permute-start(bf16[128,2048]{1,0:T(8,128)(2,1)S(1)} %collective-permute-done.40.refs_2_), channel_id=1, source_target_pairs={{0,4},{2,6},{4,0},{6,2},{8,12},{10,14},{12,8},{14,10},{16,20},{18,... | collective-permute-start | bytes 1572872 | tf_op jit(solution)/shard_map/ppermute | solution.py:430
  283.1 41.2 %collective-permute-start.28 = (bf16[256,2048]{1,0:T(8,128)(2,1)S(1)}, bf16[256,2048]{1,0:T(8,128)(2,1)S(1)}, u32[]{:S(2)}, u32[]{:S(2)}) collective-permute-start(bf16[256,2048]{1,0:T(8,128)(2,1)S(1)} %constant_dynamic-update-slice_fusion.2.refs_0_), channel_id=1, source_target_pairs={{0,4},{2,6},{4,0},{6,2},{8,12},{10,14},{12,8},{14,10},{16,20},{18,... | collective-permute-start | bytes 3145736 | tf_op jit(solution)/shard_map/ppermute | solution.py:430
  284.6 40.5 %collective-permute-start.29 = (bf16[256,2048]{1,0:T(8,128)(2,1)S(1)}, bf16[256,2048]{1,0:T(8,128)(2,1)S(1)}, u32[]{:S(2)}, u32[]{:S(2)}) collective-permute-start(bf16[256,2048]{1,0:T(8,128)(2,1)S(1)} %constant_dynamic-update-slice_fusion.2.refs_0_), channel_id=1, source_target_pairs={{0,1},{1,0},{2,3},{3,2},{4,5},{5,4},{6,7},{7,6},{8,9},{9,8},{10,11... | collective-permute-start | bytes 3145736 | tf_op jit(solution)/shard_map/ppermute | solution.py:438
  316.6 43.2 %collective-permute-start.43 = (bf16[128,2048]{1,0:T(8,128)(2,1)}, bf16[128,2048]{1,0:T(8,128)(2,1)}, u32[]{:S(2)}, u32[]{:S(2)}) collective-permute-start(bf16[128,2048]{1,0:T(8,128)(2,1)} %get-tuple-element.122), channel_id=1, source_target_pairs={{0,4},{2,6},{4,0},{6,2},{8,12},{10,14},{12,8},{14,10},{16,20},{18,... | collective-permute-start | bytes 1572872 | tf_op jit(solution)/shard_map/ppermute | solution.py:430
  317.2 183.8 %collective-permute-start.56 = (bf16[128,2048]{1,0:T(8,128)(2,1)}, bf16[128,2048]{1,0:T(8,128)(2,1)}, u32[]{:S(2)}, u32[]{:S(2)}) collective-permute-start(bf16[128,2048]{1,0:T(8,128)(2,1)} %get-tuple-element.119.refs_15_), channel_id=1, source_target_pairs={{0,4},{2,6},{4,0},{6,2},{8,12},{10,14},{12,8},{14,10},{16,20},{18,... | collective-permute-start | bytes 1572872 | tf_op jit(solution)/shard_map/ppermute | solution.py:430
  324.3 37.6 %collective-permute-start.30 = (bf16[256,2048]{1,0:T(8,128)(2,1)S(1)}, bf16[256,2048]{1,0:T(8,128)(2,1)}, u32[]{:S(2)}, u32[]{:S(2)}) collective-permute-start(bf16[256,2048]{1,0:T(8,128)(2,1)S(1)} %collective-permute-done.28.refs_15_.refs_1_), channel_id=1, source_target_pairs={{0,1},{1,0},{2,3},{3,2},{4,5},{5,4},{6,7},{7,6},{8,9},{9,8},{10,11... | collective-permute-start | bytes 3145736 | tf_op jit(solution)/shard_map/ppermute | solution.py:438
  357.8 45.8 %collective-permute-start.44 = (bf16[128,2048]{1,0:T(8,128)(2,1)}, bf16[128,2048]{1,0:T(8,128)(2,1)}, u32[]{:S(2)}, u32[]{:S(2)}) collective-permute-start(bf16[128,2048]{1,0:T(8,128)(2,1)} %get-tuple-element.121.refs_1_), channel_id=1, source_target_pairs={{0,1},{1,0},{2,3},{3,2},{4,5},{5,4},{6,7},{7,6},{8,9},{9,8},{10,11... | collective-permute-start | bytes 1572872 | tf_op jit(solution)/shard_map/ppermute | solution.py:438
  359.1 83.9 %collective-permute-start.46 = (bf16[128,2048]{1,0:T(8,128)(2,1)}, bf16[128,2048]{1,0:T(8,128)(2,1)}, u32[]{:S(2)}, u32[]{:S(2)}) collective-permute-start(bf16[128,2048]{1,0:T(8,128)(2,1)} %copy-done.91), channel_id=1, source_target_pairs={{0,1},{1,0},{2,3},{3,2},{4,5},{5,4},{6,7},{7,6},{8,9},{9,8},{10,11... | collective-permute-start | bytes 1572872 | tf_op jit(solution)/shard_map/ppermute | solution.py:438
  402.2 37.2 %collective-permute-start.49 = (bf16[128,2048]{1,0:T(8,128)(2,1)}, bf16[128,2048]{1,0:T(8,128)(2,1)}, u32[]{:S(2)}, u32[]{:S(2)}) collective-permute-start(bf16[128,2048]{1,0:T(8,128)(2,1)} %get-tuple-element.132.refs_1_), channel_id=1, source_target_pairs={{0,4},{2,6},{4,0},{6,2},{8,12},{10,14},{12,8},{14,10},{16,20},{18,... | collective-permute-start | bytes 1572872 | tf_op jit(solution)/shard_map/ppermute | solution.py:430
  405.7 38.0 %collective-permute-start.45 = (bf16[128,2048]{1,0:T(8,128)(2,1)}, bf16[128,2048]{1,0:T(8,128)(2,1)}, u32[]{:S(2)}, u32[]{:S(2)}) collective-permute-start(bf16[128,2048]{1,0:T(8,128)(2,1)} %add_convert_fusion.10), channel_id=1, source_target_pairs={{0,4},{2,6},{4,0},{6,2},{8,12},{10,14},{12,8},{14,10},{16,20},{18,... | collective-permute-start | bytes 1572872 | tf_op jit(solution)/shard_map/ppermute | solution.py:430
  460.8 40.3 %collective-permute-start.57 = (bf16[128,2048]{1,0:T(8,128)(2,1)}, bf16[128,2048]{1,0:T(8,128)(2,1)}, u32[]{:S(2)}, u32[]{:S(2)}) collective-permute-start(bf16[128,2048]{1,0:T(8,128)(2,1)} %add_convert_fusion.11.refs_16_), channel_id=1, source_target_pairs={{0,1},{1,0},{2,3},{3,2},{4,5},{5,4},{6,7},{7,6},{8,9},{9,8},{10,11... | collective-permute-start | bytes 1572872 | tf_op jit(solution)/shard_map/ppermute | solution.py:438
  480.0 43.4 %collective-permute-start.59 = (bf16[1,1,704,2048]{3,2,1,0:T(8,128)(2,1)}, bf16[1,1,704,2048]{3,2,1,0:T(8,128)(2,1)S(1)}, u32[]{:S(2)}, u32[]{:S(2)}) collective-permute-start(bf16[1,1,704,2048]{3,2,1,0:T(8,128)(2,1)} %copy-done.46), channel_id=1, source_target_pairs={{0,2},{2,0},{4,6},{6,4},{8,10},{10,8},{12,14},{14,12},{16,18},{18,... | collective-permute-start | bytes 8650760 | tf_op jit(solution)/shard_map/ppermute | solution.py:434
  480.0 43.4 %collective-permute-start.60 = (bf16[16,288,128]{2,1,0:T(8,128)(2,1)}, bf16[16,288,128]{2,1,0:T(8,128)(2,1)}, u32[]{:S(2)}, u32[]{:S(2)}) collective-permute-start(bf16[16,288,128]{2,1,0:T(8,128)(2,1)} %copy-done.61), channel_id=1, source_target_pairs={{0,2},{2,0},{4,6},{6,4},{8,10},{10,8},{12,14},{14,12},{16,18},{18,... | collective-permute-start | bytes 3538952 | tf_op jit(solution)/shard_map/ppermute | solution.py:434
  573.8 163.7 %collective-permute-start.66 = (bf16[512,2048]{1,0:T(8,128)(2,1)}, bf16[512,2048]{1,0:T(8,128)(2,1)}, u32[]{:S(2)}, u32[]{:S(2)}) collective-permute-start(bf16[512,2048]{1,0:T(8,128)(2,1)} %shard_map.317), channel_id=1, source_target_pairs={{0,1},{1,0},{2,3},{3,2},{4,5},{5,4},{6,7},{7,6},{8,9},{9,8},{10,11... | collective-permute-start | bytes 6291464 | tf_op jit(solution)/shard_map/ppermute | solution.py:438
  575.3 225.4 %collective-permute-start.68 = (bf16[512,2048]{1,0:T(8,128)(2,1)}, bf16[512,2048]{1,0:T(8,128)(2,1)}, u32[]{:S(2)}, u32[]{:S(2)}) collective-permute-start(bf16[512,2048]{1,0:T(8,128)(2,1)} %shard_map.318), channel_id=1, source_target_pairs={{0,1},{1,0},{2,3},{3,2},{4,5},{5,4},{6,7},{7,6},{8,9},{9,8},{10,11... | collective-permute-start | bytes 6291464 | tf_op jit(solution)/shard_map/ppermute | solution.py:438
  575.9 102.0 %collective-permute-start.73 = (bf16[128,2048]{1,0:T(8,128)(2,1)}, bf16[128,2048]{1,0:T(8,128)(2,1)}, u32[]{:S(2)}, u32[]{:S(2)}) collective-permute-start(bf16[128,2048]{1,0:T(8,128)(2,1)} %get-tuple-element.168), channel_id=1, source_target_pairs={{0,1},{1,0},{2,3},{3,2},{4,5},{5,4},{6,7},{7,6},{8,9},{9,8},{10,11... | collective-permute-start | bytes 1572872 | tf_op jit(solution)/shard_map/ppermute | solution.py:438
  580.6 125.3 %all-to-all-start.1 = ((bf16[16,288,128]{2,1,0:T(8,128)(2,1)}), bf16[16,288,128]{2,1,0:T(8,128)(2,1)}, u32[]{:S(2)}, u32[]{:S(2)}) async-start(bf16[16,288,128]{2,1,0:T(8,128)(2,1)} %add_convert_fusion.1), calls=%async_computation.1 | async-start | bytes 2359296 | tf_op jit(solution)/shard_map/all_to_all | solution.py:1891
  598.9 84.4 %collective-permute-start.76 = (bf16[256,1536]{1,0:T(8,128)(2,1)S(1)}, bf16[256,1536]{1,0:T(8,128)(2,1)S(1)}, u32[]{:S(2)}, u32[]{:S(2)}) collective-permute-start(bf16[256,1536]{1,0:T(8,128)(2,1)S(1)} %slice.159), channel_id=1, source_target_pairs={{0,8},{2,10},{4,12},{6,14},{8,16},{10,18},{12,20},{14,22},{16,24},... | collective-permute-start | bytes 2359304 | tf_op jit(solution)/shard_map/ppermute | solution.py:426
  681.7 49.8 %collective-permute-start.62 = (bf16[512,2176]{1,0:T(8,128)(2,1)}, bf16[512,2176]{1,0:T(8,128)(2,1)S(1)}, u32[]{:S(2)}, u32[]{:S(2)}) collective-permute-start(bf16[512,2176]{1,0:T(8,128)(2,1)} %shard_map.313.refs_2_.refs_6_), channel_id=1, source_target_pairs={{0,4},{2,6},{4,0},{6,2},{8,12},{10,14},{12,8},{14,10},{16,20},{18,... | collective-permute-start | bytes 6684680 | tf_op jit(solution)/shard_map/ppermute | solution.py:430
  705.9 102.1 %collective-permute-start.70 = (bf16[1,2,704,2048]{3,2,1,0:T(8,128)(2,1)}, bf16[1,2,704,2048]{3,2,1,0:T(8,128)(2,1)}, u32[]{:S(2)}, u32[]{:S(2)}) collective-permute-start(bf16[1,2,704,2048]{3,2,1,0:T(8,128)(2,1)} %shard_map.319), channel_id=1, source_target_pairs={{0,2},{2,0},{4,6},{6,4},{8,10},{10,8},{12,14},{14,12},{16,18},{18,... | collective-permute-start | bytes 17301512 | tf_op jit(solution)/shard_map/ppermute | solution.py:434
  715.5 51.6 %collective-permute-start.78 = (bf16[256,1536]{1,0:T(8,128)(2,1)}, bf16[256,1536]{1,0:T(8,128)(2,1)S(1)}, u32[]{:S(2)}, u32[]{:S(2)}) collective-permute-start(bf16[256,1536]{1,0:T(8,128)(2,1)} %add_convert_fusion.2), channel_id=1, source_target_pairs={{0,8},{2,10},{4,12},{6,14},{8,16},{10,18},{12,20},{14,22},{16,24},... | collective-permute-start | bytes 2359304 | tf_op jit(solution)/shard_map/ppermute | solution.py:426
  742.1 58.6 %collective-permute-start.67 = (bf16[512,2048]{1,0:T(8,128)(2,1)}, bf16[512,2048]{1,0:T(8,128)(2,1)}, u32[]{:S(2)}, u32[]{:S(2)}) collective-permute-start(bf16[512,2048]{1,0:T(8,128)(2,1)} %add_convert_fusion), channel_id=1, source_target_pairs={{0,4},{2,6},{4,0},{6,2},{8,12},{10,14},{12,8},{14,10},{16,20},{18,... | collective-permute-start | bytes 6291464 | tf_op jit(solution)/shard_map/ppermute | solution.py:430
  (166 other events, 2385.7 us)
